TPU v7x, 32 devices: a whole 2x2x4 slice. The times are simulated.
32 devices in a mesh: grp: 2 (over x), head: 16 (over z, y, core).
Axes of the slice: x: 2, y: 2, z: 4, core: 2. Of those that a mesh axis runs over, the one named last changes fastest.
Arguments:
- queries: bfloat16 [2048, 2, 16, 256], P('head', 'grp'), parts along dimension 1, may hold values from -12 to 12
- new_kv: bfloat16 [2048, 2, 2, 512], P('head', 'grp'), parts along dimension 1, may hold values from -4 to 4
- cache: bfloat16 [32, 256, 512], P(('grp', 'head')), parts along dimension 0, may hold values from -12 to 12
- resid: bfloat16 [2048, 2, 2048], P('head', 'grp'), parts along dimension 1, may hold values from -6 to 6
- w_out: bfloat16 [16, 256, 2048], P(None, 'head'), may hold values from -0.375 to 0.375
- norm_gain: float32 [2048], replicated, may hold values from 0.1 to 1.9
- expert_ids: int32 [2048, 2, 2], P('head', 'grp'), parts along dimension 1, may hold values from 0 to 15, all different within a row; in each aligned block of 128 rows (0 to 127, 128 to 255, ..., all dimensions but the last counted through in order) at most 32 rows name the same one
- expert_gates: float32 [2048, 2, 2], P('head', 'grp'), parts along dimension 1, may hold values from 0.2 to 1
- w_in: bfloat16 [16, 2048, 1024], P('head'), may hold values from -0.125 to 0.125
- w_down: bfloat16 [16, 512, 2048], P('head'), may hold values from -0.25 to 0.25
Outputs:
- layer_out: bfloat16 [2048, 2, 2048], P('head', 'grp'), parts along dimension 1
There are 2 independent parts, one for each index of `grp`. A program takes and returns all parts, laid end to end along the dimension named above; an argument that names none is the same for every part. Nothing has to cross between parts.
Inputs may be any that keep to these rules, and one draw needn't show every extreme that they name: `expert_ids`: rows are taken in order over positions and then sequences; in each aligned block of 128 such rows (the rows of one device) no expert is named by more than 32 rows, a bound that some block reaches. A row names 2 different experts.
All inputs are finite; a program needn't handle non-finite values.
Results may differ from a plain program's by a relative error of at most 0.009.
Values may be sent and summed in bfloat16 or wider, within the bound.
No kernel may reach another device: no remote copies, remote signals or barrier semaphores. Data moves between devices by JAX's collectives and lax.ppermute only.
A program may use at most 128 MiB of HBM per device.

v0:
```python
import jax
import jax.numpy as jnp
from jax import lax
from jax.sharding import PartitionSpec as P

eps_norm = 1e-06


def partner_2(value, axis, stride):
    mask = 2**stride
    pairs = [(source, source ^ mask) for source in range(lax.axis_size(axis))]
    return lax.ppermute(value, axis, pairs)


def attend(query_rows_all, new_keys, new_values, cached):
    length = query_rows_all.shape[0]
    head_width = query_rows_all.shape[1]
    block_rows = min(512, length)
    score_scale = head_width ** (-0.5)
    old_keys = cached[:, :head_width]
    old_values = cached[:, head_width:]
    key_positions = jnp.arange(length, dtype=jnp.int32)

    def one_block(first_row):
        query_rows = lax.dynamic_slice_in_dim(query_rows_all, first_row, block_rows, 0)
        old_scores = (
            jnp.dot(query_rows, old_keys.T, preferred_element_type=jnp.float32) * score_scale
        )
        new_scores = (
            jnp.dot(query_rows, new_keys.T, preferred_element_type=jnp.float32) * score_scale
        )
        row_positions = first_row + jnp.arange(block_rows, dtype=jnp.int32)
        allowed = key_positions[None, :] <= row_positions[:, None]
        new_scores = jnp.where(allowed, new_scores, -jnp.inf)
        row_max = jnp.maximum(jnp.max(old_scores, 1), jnp.max(new_scores, 1))[:, None]
        old_exp = jnp.exp(old_scores - row_max)
        new_exp = jnp.exp(new_scores - row_max)
        denominator = jnp.sum(old_exp, 1) + jnp.sum(new_exp, 1)
        weighted_sum = jnp.dot(
            old_exp.astype(jnp.bfloat16), old_values, preferred_element_type=jnp.float32
        )
        weighted_sum = weighted_sum + jnp.dot(
            new_exp.astype(jnp.bfloat16), new_values, preferred_element_type=jnp.float32
        )
        return (weighted_sum / denominator[:, None]).astype(jnp.bfloat16)

    starts = jnp.arange(length // block_rows) * block_rows
    return lax.map(one_block, starts).reshape(length, head_width)


def local(queries, new_kv, cache, resid, w_out, norm_gain, expert_ids, expert_gates, w_in, w_down):
    axis_count = lax.axis_size("head")
    local_rows = queries.shape[0]
    seq_count = queries.shape[1]
    head_count = queries.shape[2]
    head_width = queries.shape[3]
    pair_heads = new_kv.shape[2]
    group_size = head_count // pair_heads
    model_width = resid.shape[2]
    row_count = local_rows * seq_count
    query_slots = queries.reshape(local_rows, axis_count, head_width)
    pair_slots = jnp.broadcast_to(
        new_kv[:, :, :, None, :], (local_rows, seq_count, pair_heads, group_size, 2 * head_width)
    )
    pair_slots = pair_slots.reshape(local_rows, axis_count, 2 * head_width)
    head_queries = lax.all_to_all(query_slots, "head", split_axis=1, concat_axis=0, tiled=True)[
        :, 0
    ]
    head_pairs = lax.all_to_all(pair_slots, "head", split_axis=1, concat_axis=0, tiled=True)[:, 0]
    cache_rows = cache[0]
    for bit_number in range(group_size.bit_length() - 1):
        partner = partner_2(cache_rows, "head", bit_number)
        cache_rows = jnp.concatenate([cache_rows, partner], 0)
    attended = attend(
        head_queries, head_pairs[:, :head_width], head_pairs[:, head_width:], cache_rows
    )
    returned = lax.all_to_all(
        attended.reshape(attended.shape[0], 1, head_width),
        "head",
        split_axis=0,
        concat_axis=1,
        tiled=True,
    )
    attn_rows = returned.reshape(row_count, head_count * head_width)
    attn_heads = attn_rows.reshape(row_count, head_count, head_width)
    projected = jnp.einsum(
        "rhi,hid->rd",
        attn_heads,
        lax.all_gather(w_out, "head", axis=1, tiled=True),
        preferred_element_type=jnp.float32,
    )
    stream = resid.reshape(row_count, model_width).astype(jnp.float32) + projected
    normed = stream * lax.rsqrt(jnp.mean(stream * stream, 1, keepdims=True) + eps_norm) * norm_gain
    normed = normed.astype(jnp.bfloat16)
    top_count = expert_ids.shape[2]
    flat_ids = expert_ids.reshape(-1)
    local_experts = w_in.shape[0]
    experts = local_experts * axis_count
    capacity = max(2, 2 * row_count * top_count // experts)
    onehot = (flat_ids[:, None] == jnp.arange(experts, dtype=jnp.int32)[None, :]).astype(jnp.int32)
    earlier = jnp.cumsum(onehot, 0) - onehot
    slot_rank = jnp.sum(earlier * onehot, 1)
    target = flat_ids * capacity + slot_rank
    repeated = jnp.repeat(normed, top_count, axis=0)
    outgoing = jnp.zeros((experts * capacity, model_width), jnp.bfloat16).at[target].set(repeated)
    outgoing = outgoing.reshape(experts, 1, capacity, model_width)
    hidden_width = w_down.shape[1]
    inner_act = jnp.einsum(
        "esmd,edf->esmf",
        lax.all_to_all(outgoing, "head", split_axis=0, concat_axis=1, tiled=True),
        w_in,
        preferred_element_type=jnp.float32,
    )
    hidden = (jax.nn.silu(inner_act[..., :hidden_width]) * inner_act[..., hidden_width:]).astype(
        jnp.bfloat16
    )
    answered = jnp.einsum(
        "esmf,efd->esmd", hidden, w_down, preferred_element_type=jnp.float32
    ).astype(jnp.bfloat16)
    returned_rows = lax.all_to_all(answered, "head", split_axis=1, concat_axis=0, tiled=True)
    picked = returned_rows.reshape(experts * capacity, model_width)[target].astype(jnp.float32)
    weighted = picked * expert_gates.reshape(-1)[:, None]
    expert_sum = weighted.reshape(row_count, top_count, model_width).sum(1)
    return (stream + expert_sum).astype(jnp.bfloat16).reshape(local_rows, seq_count, model_width)


def solution(mesh):
    return jax.shard_map(
        local,
        mesh=mesh,
        in_specs=(
            P("head", "grp", None, None),
            P("head", "grp", None, None),
            P(("grp", "head"), None, None),
            P("head", "grp", None),
            P(None, "head", None),
            P(),
            P("head", "grp", None),
            P("head", "grp", None),
            P("head", None, None),
            P("head", None, None),
        ),
        out_specs=P("head", "grp", None),
        check_vma=False,
    )
```

profile of v0, /device:TPU:13, one launch (start us, length us, event | category | flops | bytes accessed | tf_op | source)
XLA Modules:
  0.0 386.4 jit_solution(4581564289091582553)
XLA Ops:
  8.2 1.5 broadcast_in_dim.38
  9.7 6.6 %all-to-all-start.1 = ((bf16[128,16,512]{2,0,1:T(8,128)(2,1)}), bf16[128,16,512]{2,0,1:T(8,128)(2,1)}, u32[]{:S(2)}, u32[]{:S(2)}) async-start(bf16[128,16,512]{2,0,1:T(8,128)(2,1)} %bitcast.108), calls=%async_computation.1 | async-start | bytes 4194304 | tf_op jit(solution)/shard_map/all_to_all | solution.py:69
  16.7 1.2 collective-permute-done
  18.3 33.6 %collective-permute-done.1 = bf16[512,512]{1,0:T(8,128)(2,1)S(1)} collective-permute-done((bf16[512,512]{1,0:T(8,128)(2,1)S(1)}, bf16[512,512]{1,0:T(8,128)(2,1)S(1)}, u32[]{:S(2)}, u32[]{:S(2)}) %collective-permute-start.1) | collective-permute-done | bytes 524320 | tf_op jit(solution)/shard_map/ppermute | solution.py:12
  53.0 4.2 %collective-permute-start.2 = (bf16[1024,512]{1,0:T(8,128)(2,1)}, bf16[1024,512]{1,0:T(8,128)(2,1)}, u32[]{:S(2)}, u32[]{:S(2)}) collective-permute-start(bf16[1024,512]{1,0:T(8,128)(2,1)} %pad_maximum_fusion.1), channel_id=1, source_target_pairs={{0,4},{1,5},{2,6},{3,7},{4,0},{5,1},{6,2},{7,3},{8,12},{9,13},{10,... | collective-permute-start | bytes 3145736 | tf_op jit(solution)/shard_map/ppermute | solution.py:12
  57.2 2.6 copy.42
  59.8 38.0 %all-to-all-done.1 = bf16[128,16,512]{2,0,1:T(8,128)(2,1)} async-done(((bf16[128,16,512]{2,0,1:T(8,128)(2,1)}), bf16[128,16,512]{2,0,1:T(8,128)(2,1)}, u32[]{:S(2)}, u32[]{:S(2)}) %all-to-all-start.1) | async-done | bytes 2097184 | tf_op jit(solution)/shard_map/all_to_all | solution.py:69
  97.8 4.6 %all-to-all-start = ((bf16[128,16,256]{2,0,1:T(8,128)(2,1)}), bf16[128,16,256]{2,0,1:T(8,128)(2,1)}, u32[]{:S(2)}, u32[]{:S(2)}) async-start(bf16[128,16,256]{2,0,1:T(8,128)(2,1)} %bitcast.95), calls=%async_computation | async-start | bytes 2097152 | tf_op jit(solution)/shard_map/all_to_all | solution.py:66
  102.4 19.2 %collective-permute-done.2 = bf16[1024,512]{1,0:T(8,128)(2,1)} collective-permute-done((bf16[1024,512]{1,0:T(8,128)(2,1)}, bf16[1024,512]{1,0:T(8,128)(2,1)}, u32[]{:S(2)}, u32[]{:S(2)}) %collective-permute-start.2) | collective-permute-done | bytes 1048608 | tf_op jit(solution)/shard_map/ppermute | solution.py:12
  121.7 1.4 pad_maximum_fusion
  123.0 1.1 fusion.58
  124.2 3.0 fusion.57
  127.2 25.3 %all-to-all-done = bf16[128,16,256]{2,0,1:T(8,128)(2,1)} async-done(((bf16[128,16,256]{2,0,1:T(8,128)(2,1)}), bf16[128,16,256]{2,0,1:T(8,128)(2,1)}, u32[]{:S(2)}, u32[]{:S(2)}) %all-to-all-start) | async-done | bytes 1048608 | tf_op jit(solution)/shard_map/all_to_all | solution.py:66
  152.5 45.5 %while.11 = (s32[]{:T(128)}, bf16[4,512,256]{2,1,0:T(8,128)(2,1)}, s32[4]{0:T(128)S(1)}, bf16[2048,256]{1,0:T(8,128)(2,1)}, bf16[2048,256]{1,0:T(8,128)(2,1)S(1)...) while((s32[]{:T(128)}, bf16[4,512,256]{2,1,0:T(8,128)(2,1)}, ...), condition=%wide.region_5.6_spmd.clone, body=%wide.region_0.5_spmd.clone.sunk | while | flops 2164653568 | bytes 39617248 | solution.py:48
  155.7 2.3 fusion.81
  158.0 1.8 multiply_reduce_fusion.4
  159.8 1.4 fusion.83
  162.4 1.5 fusion.84
  167.0 2.3 fusion.81
  169.3 1.8 multiply_reduce_fusion.4
  171.2 1.4 fusion.83
  173.8 1.5 fusion.84
  178.4 2.3 fusion.81
  180.7 1.8 multiply_reduce_fusion.4
  182.6 1.4 fusion.83
  185.2 1.5 fusion.84
  189.8 2.3 fusion.81
  192.1 1.8 multiply_reduce_fusion.4
  193.9 1.4 fusion.83
  196.5 1.5 fusion.84
  198.5 2.7 reduce.2
  201.2 1.1 reshape.162
  202.3 4.4 %all-to-all-start.2 = ((bf16[16,2,16384]{2,1,0:T(2,128)(2,1)}), bf16[16,2,16384]{2,1,0:T(2,128)(2,1)S(1)}, u32[]{:S(2)}, u32[]{:S(2)}) async-start(bf16[16,2,16384]{2,1,0:T(2,128)(2,1)} %reshape.162), calls=%async_computation.2 | async-start | bytes 2097152 | tf_op jit(solution)/shard_map/all_to_all | solution.py:77
  208.4 23.3 %all-to-all-done.2 = bf16[16,2,16384]{2,1,0:T(2,128)(2,1)S(1)} async-done(((bf16[16,2,16384]{2,1,0:T(2,128)(2,1)}), bf16[16,2,16384]{2,1,0:T(2,128)(2,1)S(1)}, u32[]{:S(2)}, u32[]{:S(2)}) %all-to-all-start.2) | async-done | bytes 1048608 | tf_op jit(solution)/shard_map/all_to_all | solution.py:77
  231.7 3.5 reshape.163
  235.1 2.8 copy.38
  237.9 8.6 %multiply_reduce_fusion.2 = (f32[128]{0:T(128)S(1)}, f32[128,2048]{1,0:T(8,128)S(1)}) fusion(bf16[128,16,256]{2,0,1:T(8,128)(2,1)} %bitcast.110, bf16[16,256,2048]{2,1,0:T(8,128)(2,1)} %all-gather.2.cloned.1.call-done, bf16[128,1,2048]{2,0,1:T(8,128)(2,1)} %param.15), kind=kOutput, calls=%fused_computation.46 | convolution fusion | flops 2148532224 | bytes 19399168 | tf_op jit(solution)/shard_map/rhi,hid->rd/dot_general | solution.py:86
  246.7 1.6 broadcast_in_dim.41
  248.3 2.3 reshape.152
  250.5 4.4 %scatter_custom_fusion = bf16[512,2048]{1,0:T(8,128)(2,1)} fusion(s32[256]{0:T(256)S(1)} %bitcast.116, bf16[256,2048]{1,0:T(8,128)(2,1)} %reshape.152, bf16[]{:T(256)} %constant.7.clone.1), kind=kCustom, calls=%fused_computation.47 | custom fusion | bytes 2097664 | tf_op jit(solution)/shard_map/scatter | solution.py:105
  255.0 52.5 %all_to_all.66 = bf16[16,1,32,2048]{3,2,1,0:T(8,128)(2,1)S(1)} all-to-all(bf16[16,1,32,2048]{3,2,1,0:T(8,128)(2,1)} %bitcast.109), channel_id=1, replica_groups=mesh['grp'=2,'head'=16] {'head'}, dimensions={0} | all-to-all | bytes 4194304 | tf_op jit(solution)/shard_map/all_to_all | solution.py:110
  307.5 2.3 fusion.40
  309.8 2.6 fusion.36
  312.4 5.3 %all-to-all-start.4 = ((bf16[1,16,32,2048]{3,2,0,1:T(8,128)(2,1)}), bf16[1,16,32,2048]{3,2,0,1:T(8,128)(2,1)}, u32[]{:S(2)}, u32[]{:S(2)}) async-start(bf16[1,16,32,2048]{3,2,0,1:T(8,128)(2,1)} %fusion.36), calls=%async_computation.4 | async-start | bytes 4194304 | tf_op jit(solution)/shard_map/all_to_all | solution.py:120
  317.8 47.4 %all-to-all-done.4 = bf16[1,16,32,2048]{3,2,0,1:T(8,128)(2,1)} async-done(((bf16[1,16,32,2048]{3,2,0,1:T(8,128)(2,1)}), bf16[1,16,32,2048]{3,2,0,1:T(8,128)(2,1)}, u32[]{:S(2)}, u32[]{:S(2)}) %all-to-all-start.4) | async-done | bytes 2097184 | tf_op jit(solution)/shard_map/all_to_all | solution.py:120
  365.2 5.2 %gather_fusion = bf16[256,2048]{1,0:T(8,128)(2,1)} fusion(bf16[512,2048]{1,0:T(8,128)(2,1)} %bitcast.30, s32[1024]{0:T(1024)S(1)} %pad_clamp_fusion), kind=kCustom, calls=%fused_computation | custom fusion | bytes 2098176 | tf_op jit(solution)/shard_map/gather | solution.py:121
  370.4 3.4 reshape.139
  373.8 4.8 %multiply_reduce_fusion.1 = f32[128,2048]{1,0:T(8,128)S(1)} fusion(f32[128,2,2048]{2,1,0:T(2,128)} %reshape.139, f32[128,2]{1,0:T(8,128)S(1)} %copy.37), kind=kLoop, calls=%fused_computation.38 | loop fusion | flops 786432 | bytes 3146752 | tf_op jit(solution)/shard_map/reduce_sum | solution.py:123
  (77 shorter events, 16.7 us)
Async XLA Ops:
  6.5 303.3 %copy-start = (bf16[1,512,2048]{2,1,0:T(8,128)(2,1)S(1)}, bf16[1,512,2048]{2,1,0:T(8,128)(2,1)}, u32[]{:S(2)}) copy-start(bf16[1,512,2048]{2,1,0:T(8,128)(2,1)} %param.21) | copy-start | bytes 6291460
  6.5 9.8 %copy-start.1 = (bf16[1,256,512]{2,1,0:T(8,128)(2,1)S(1)}, bf16[1,256,512]{2,1,0:T(8,128)(2,1)}, u32[]{:S(2)}) copy-start(bf16[1,256,512]{2,1,0:T(8,128)(2,1)} %param.14) | copy-start | bytes 786436
  6.5 231.3 %all-gather.2.cloned.1.call-start = ((), (), s32[]{:S(2)}) async-start(), calls=%async_computation.5 | async-start | bytes 17825792 | tf_op jit(solution)/shard_map/all_gather | solution.py:89
  9.7 88.0 %all-to-all-start.1 = ((bf16[128,16,512]{2,0,1:T(8,128)(2,1)}), bf16[128,16,512]{2,0,1:T(8,128)(2,1)}, u32[]{:S(2)}, u32[]{:S(2)}) async-start(bf16[128,16,512]{2,0,1:T(8,128)(2,1)} %bitcast.108), calls=%async_computation.1 | async-start | bytes 4194304 | tf_op jit(solution)/shard_map/all_to_all | solution.py:69
  16.3 1.6 collective-permute-start
  17.9 34.0 %collective-permute-start.1 = (bf16[512,512]{1,0:T(8,128)(2,1)S(1)}, bf16[512,512]{1,0:T(8,128)(2,1)S(1)}, u32[]{:S(2)}, u32[]{:S(2)}) collective-permute-start(bf16[512,512]{1,0:T(8,128)(2,1)S(1)} %pad_maximum_fusion.2), channel_id=1, source_target_pairs={{0,2},{1,3},{2,0},{3,1},{4,6},{5,7},{6,4},{7,5},{8,10},{9,11},{10,... | collective-permute-start | bytes 1572872 | tf_op jit(solution)/shard_map/ppermute | solution.py:12
  53.0 68.7 %collective-permute-start.2 = (bf16[1024,512]{1,0:T(8,128)(2,1)}, bf16[1024,512]{1,0:T(8,128)(2,1)}, u32[]{:S(2)}, u32[]{:S(2)}) collective-permute-start(bf16[1024,512]{1,0:T(8,128)(2,1)} %pad_maximum_fusion.1), channel_id=1, source_target_pairs={{0,4},{1,5},{2,6},{3,7},{4,0},{5,1},{6,2},{7,3},{8,12},{9,13},{10,... | collective-permute-start | bytes 3145736 | tf_op jit(solution)/shard_map/ppermute | solution.py:12
  97.8 54.7 %all-to-all-start = ((bf16[128,16,256]{2,0,1:T(8,128)(2,1)}), bf16[128,16,256]{2,0,1:T(8,128)(2,1)}, u32[]{:S(2)}, u32[]{:S(2)}) async-start(bf16[128,16,256]{2,0,1:T(8,128)(2,1)} %bitcast.95), calls=%async_computation | async-start | bytes 2097152 | tf_op jit(solution)/shard_map/all_to_all | solution.py:66
  159.8 1.4 copy-start.2
  161.2 1.2 copy-start.3
  171.2 1.4 copy-start.2
  172.6 1.2 copy-start.3
  182.5 1.4 copy-start.2
  183.9 1.2 copy-start.3
  193.9 1.4 copy-start.2
  195.3 1.2 copy-start.3
  198.0 8.8 %copy-start.5 = (s32[128,1,2]{0,2,1:T(2,128)S(1)}, s32[128,1,2]{0,2,1:T(2,128)}, u32[]{:S(2)}) copy-start(s32[128,1,2]{0,2,1:T(2,128)} %param.18) | copy-start | bytes 3076
  202.3 29.3 %all-to-all-start.2 = ((bf16[16,2,16384]{2,1,0:T(2,128)(2,1)}), bf16[16,2,16384]{2,1,0:T(2,128)(2,1)S(1)}, u32[]{:S(2)}, u32[]{:S(2)}) async-start(bf16[16,2,16384]{2,1,0:T(2,128)(2,1)} %reshape.162), calls=%async_computation.2 | async-start | bytes 2097152 | tf_op jit(solution)/shard_map/all_to_all | solution.py:77
  237.9 8.6 %copy-start.4 = (f32[2048]{0:T(1024)S(1)}, f32[2048]{0:T(1024)}, u32[]{:S(2)}) copy-start(f32[2048]{0:T(1024)} %param.17) | copy-start | bytes 24580
  255.0 52.5 %copy-start.7 = (bf16[1,2048,1024]{2,1,0:T(8,128)(2,1)S(1)}, bf16[1,2048,1024]{2,1,0:T(8,128)(2,1)}, u32[]{:S(2)}) copy-start(bf16[1,2048,1024]{2,1,0:T(8,128)(2,1)} %param.20) | copy-start | bytes 12582916
  312.4 5.3 %copy-start.6 = (f32[128,1,2]{0,2,1:T(2,128)S(1)}, f32[128,1,2]{0,2,1:T(2,128)}, u32[]{:S(2)}) copy-start(f32[128,1,2]{0,2,1:T(2,128)} %param.19) | copy-start | bytes 3076
  312.4 52.8 %all-to-all-start.4 = ((bf16[1,16,32,2048]{3,2,0,1:T(8,128)(2,1)}), bf16[1,16,32,2048]{3,2,0,1:T(8,128)(2,1)}, u32[]{:S(2)}, u32[]{:S(2)}) async-start(bf16[1,16,32,2048]{3,2,0,1:T(8,128)(2,1)} %fusion.36), calls=%async_computation.4 | async-start | bytes 4194304 | tf_op jit(solution)/shard_map/all_to_all | solution.py:120
Sparse Core Ops, SparseCore 0:
  9.6 185.5 all-gather.1
where the time goes:
time: 388 us; the launch traced here: 386 us
  waiting for transfers between devices  189 us (49%)
  blocking collectives  52.5 us (14%)
  matrix products  39.2 us (10%)
  local copies, waits for them, and re-layouts  38.8 us (10%)
  starting transfers between devices  25.9 us (7%)
  other arithmetic  19.9 us (5%)
  between operations  13.5 us (3%)
  loops' own time  7.86 us (2%)
    ppermute x3, waiting for transfers between devices, partner_2(): return lax.ppermute(value, axis, pairs)  54 us
    all_to_all x1, blocking collectives, local(): lax.all_to_all(outgoing, 'head', split_axis=0, concat_axis=1, tiled=True)  52.5 us
    all_to_all x1, waiting for transfers between devices, local(): lax.all_to_all(answered, 'head', split_axis=1, concat_axis=0, tiled=True)  47.4 us
    all_to_all x1, waiting for transfers between devices, local(): lax.all_to_all(pair_slots, 'head', split_axis=1, concat_axis=0, tiled=True)  38 us
    all_to_all x1, waiting for transfers between devices, local(): lax.all_to_all(query_slots, 'head', split_axis=1, concat_axis=0, tiled=True)  25.3 us
    all_to_all x1, waiting for transfers between devices, local(): lax.all_to_all(attended.reshape(attended.shape[0], 1, head_width), 'head'...  23.3 us
    unnamed x17, local copies, waits for them, and re-layouts  10 us
    dot_general x4, matrix products, one_block(): jnp.dot(query_rows, new_keys.T, preferred_element_type=jnp.float32)  9.17 us
  transfers between devices with their start and end apart: 8, of which 7 were waited for; matrix products, arithmetic and copies ran while one was open for 16% of the time, Pallas kernels for 0%

commit v1 on v0

v1 whole, which is shorter than its diff:
```python
import functools

import jax
import jax.numpy as jnp
from jax import lax
from jax.experimental import pallas as pl
from jax.experimental.pallas import tpu as pltpu
from jax.sharding import PartitionSpec as P

eps_norm = 1e-06
F32 = jnp.float32
BF16 = jnp.bfloat16
HIGH_VMEM = 48 * 2**20


def anywhere():
    return pl.BlockSpec(memory_space=pl.ANY)


def in_vmem():
    return pl.BlockSpec(memory_space=pltpu.VMEM)


def attend_kernel(
    block, chunk, width, q_hbm, cache_hbm, kv_hbm, o_ref, q_ref, cache_ref, kv_ref, s0, s1, sems
):
    members, groups, piece, _ = kv_hbm.shape
    length = members * groups * piece
    old = cache_hbm.shape[0]
    scale = width**-0.5
    in_q = pltpu.make_async_copy(q_hbm, q_ref, sems.at[0])
    in_cache = pltpu.make_async_copy(cache_hbm, cache_ref, sems.at[1])
    in_q.start()
    in_cache.start()
    in_kv = []
    for group in range(groups):
        for member in range(members):
            place = (group * members + member) * piece
            copy = pltpu.make_async_copy(
                kv_hbm.at[member, group], kv_ref.at[pl.ds(place, piece)], sems.at[2]
            )
            copy.start()
            in_kv.append(copy)
    in_q.wait()
    in_cache.wait()
    for copy in in_kv:
        copy.wait()
    scores = [s0, s1]

    def pieces(b):
        out = [(True, k, chunk, k) for k in range(0, old, chunk)]
        last = b * block
        for k in range(0, last, chunk):
            out.append((False, k, min(chunk, last - k), old + k))
        out.append((False, last, block, old + last))
        return out

    def make_scores(b, part, running):
        of_cache, first, count, column = part
        keys = (cache_ref if of_cache else kv_ref)[pl.ds(first, count), :width]
        s = lax.dot_general(
            q_ref[pl.ds(b * block, block), :],
            keys,
            (((1,), (1,)), ((), ())),
            preferred_element_type=F32,
        )
        if not of_cache and first == b * block:
            row = lax.broadcasted_iota(jnp.int32, s.shape, 0)
            col = lax.broadcasted_iota(jnp.int32, s.shape, 1)
            s = jnp.where(col <= row, s, -jnp.inf)
        scores[b % 2][:, pl.ds(column, count)] = s
        for k in range(0, count, 128):
            piece_max = s[:, k : k + 128]
            running = piece_max if running is None else jnp.maximum(running, piece_max)
        return running

    def use_scores(b, part, top, total, acc):
        of_cache, first, count, column = part
        values = (cache_ref if of_cache else kv_ref)[pl.ds(first, count), width:]
        e = jnp.exp((scores[b % 2][:, pl.ds(column, count)] - top) * scale)
        for k in range(0, count, 128):
            total = e[:, k : k + 128] if total is None else total + e[:, k : k + 128]
        product = jnp.dot(e.astype(BF16), values, preferred_element_type=F32)
        return total, product if acc is None else acc + product

    blocks = length // block
    running = None
    for part in pieces(0):
        running = make_scores(0, part, running)
    for b in range(blocks):
        top = jnp.max(running, 1, keepdims=True)
        now, later = pieces(b), pieces(b + 1) if b + 1 < blocks else []
        running, total, acc = None, None, None
        for k in range(max(len(now), len(later))):
            if k < len(now):
                total, acc = use_scores(b, now[k], top, total, acc)
            if k < len(later):
                running = make_scores(b + 1, later[k], running)
        o_ref[pl.ds(b * block, block), :] = (acc / jnp.sum(total, 1, keepdims=True)).astype(BF16)


def attend(q, cache, kv):
    length, width = q.shape
    old = cache.shape[0]
    block = min(256, length)
    chunk = min(512, old)
    return pl.pallas_call(
        functools.partial(attend_kernel, block, chunk, width),
        out_shape=jax.ShapeDtypeStruct((length, width), BF16),
        in_specs=[anywhere()] * 3,
        out_specs=in_vmem(),
        scratch_shapes=[
            pltpu.VMEM((length, width), BF16),
            pltpu.VMEM((old, 2 * width), BF16),
            pltpu.VMEM((length, 2 * width), BF16),
            pltpu.VMEM((block, old + length), F32),
            pltpu.VMEM((block, old + length), F32),
            pltpu.SemaphoreType.DMA((3,)),
        ],
        compiler_params=pltpu.CompilerParams(vmem_limit_bytes=HIGH_VMEM),
        cost_estimate=pl.CostEstimate(
            flops=4 * length * (old + length // 2) * width,
            bytes_accessed=4 * (2 * length + 2 * old) * width,
            transcendentals=length * (old + length // 2),
        ),
        name="attend",
    )(q, cache, kv)


def project_kernel(a_ref, w_ref, o_ref):
    members = a_ref.shape[0]
    planes, share = w_ref.shape[1], w_ref.shape[3]
    acc = None
    for head in range(members):
        w = jnp.concatenate(
            [w_ref[m, p, head] for p in range(planes) for m in range(members)], 0
        )
        part = jnp.dot(a_ref[head], w, preferred_element_type=F32)
        acc = part if acc is None else acc + part
    o_ref[...] = acc.astype(BF16)


def project(a, w):
    members, rows, width = a.shape
    planes, share, model = w.shape[1], w.shape[3], w.shape[4]
    tile = min(512, model)
    return pl.pallas_call(
        project_kernel,
        grid=(model // tile,),
        out_shape=jax.ShapeDtypeStruct((rows, model), BF16),
        in_specs=[
            pl.BlockSpec((members, rows, width), lambda t: (0, 0, 0)),
            pl.BlockSpec((members, planes, members, share, tile), lambda t: (0, 0, 0, 0, t)),
        ],
        out_specs=pl.BlockSpec((rows, tile), lambda t: (0, t)),
        compiler_params=pltpu.CompilerParams(vmem_limit_bytes=HIGH_VMEM),
        cost_estimate=pl.CostEstimate(
            flops=2 * members * rows * width * model,
            bytes_accessed=2 * (members * width * model + members * rows * width + rows * model),
            transcendentals=0,
        ),
        name="project",
    )(a, w)


def route_kernel(parts_ref, resid_ref, gain_ref, slots_ref, stream_ref, out_ref):
    seqs, planes = parts_ref.shape[0], parts_ref.shape[1]
    streams = []
    for seq in range(seqs):
        stream = resid_ref[seq].astype(F32)
        projected = parts_ref[seq, 0].astype(F32)
        for p in range(1, planes):
            projected = projected + parts_ref[seq, p].astype(F32)
        streams.append(stream + projected)
    stream = jnp.concatenate(streams, 0) if seqs > 1 else streams[0]
    stream_ref[...] = stream
    normed = stream * lax.rsqrt(jnp.mean(stream * stream, 1, keepdims=True) + eps_norm)
    normed = (normed * gain_ref[...]).astype(BF16)
    slots, rows = out_ref.shape[0], stream.shape[0]
    place = lax.broadcasted_iota(jnp.int32, (slots, rows), 0)
    hit = place == slots_ref[0:1, :]
    for k in range(1, slots_ref.shape[0]):
        hit = hit | (place == slots_ref[k : k + 1, :])
    out_ref[...] = jnp.dot(hit.astype(BF16), normed, preferred_element_type=F32).astype(BF16)


def route(parts, resid, gain, slots_of, slots):
    seqs, planes, local_rows, model = parts.shape
    rows = seqs * local_rows
    return pl.pallas_call(
        route_kernel,
        out_shape=(
            jax.ShapeDtypeStruct((rows, model), F32),
            jax.ShapeDtypeStruct((slots, model), BF16),
        ),
        in_specs=[in_vmem()] * 4,
        out_specs=(in_vmem(), in_vmem()),
        compiler_params=pltpu.CompilerParams(vmem_limit_bytes=HIGH_VMEM),
        cost_estimate=pl.CostEstimate(
            flops=2 * slots * rows * model,
            bytes_accessed=2 * (planes + 3 + slots // rows) * rows * model,
            transcendentals=0,
        ),
        name="route",
    )(parts, resid, gain, slots_of)


def expert_kernel(x_ref, w_in_ref, w_down_ref, o_ref):
    hidden_width = w_down_ref.shape[0]
    inner = jnp.dot(x_ref[...], w_in_ref[...], preferred_element_type=F32)
    gate = inner[:, :hidden_width]
    hidden = (gate / (1.0 + jnp.exp(-gate)) * inner[:, hidden_width:]).astype(BF16)
    o_ref[...] = jnp.dot(hidden, w_down_ref[...], preferred_element_type=F32).astype(BF16)


def expert(x, w_in, w_down):
    rows, model = x.shape
    hidden_width = w_down.shape[0]
    return pl.pallas_call(
        expert_kernel,
        out_shape=jax.ShapeDtypeStruct((rows, model), BF16),
        in_specs=[in_vmem()] * 3,
        out_specs=in_vmem(),
        compiler_params=pltpu.CompilerParams(vmem_limit_bytes=HIGH_VMEM),
        cost_estimate=pl.CostEstimate(
            flops=6 * rows * model * hidden_width,
            bytes_accessed=2 * (2 * rows * model + 3 * model * hidden_width),
            transcendentals=rows * hidden_width,
        ),
        name="expert",
    )(x, w_in, w_down)


def combine_kernel(seqs, back_ref, stream_ref, slots_ref, gates_ref, o_ref):
    slots = back_ref.shape[0]
    rows = stream_ref.shape[0]
    place = lax.broadcasted_iota(jnp.int32, (rows, slots), 1)
    total = stream_ref[...]
    gathered = None
    for k in range(slots_ref.shape[1]):
        pick = (place == slots_ref[:, k : k + 1]).astype(BF16)
        picked = jnp.dot(pick, back_ref[...], preferred_element_type=F32)
        part = picked * gates_ref[:, k : k + 1]
        gathered = part if gathered is None else gathered + part
    out = (total + gathered).astype(BF16)
    local_rows = rows // seqs
    for seq in range(seqs):
        o_ref[seq] = out[seq * local_rows : (seq + 1) * local_rows]


def combine(back, stream, slots_of, gates, seqs):
    slots, model = back.shape
    rows = stream.shape[0]
    top = slots_of.shape[1]
    return pl.pallas_call(
        functools.partial(combine_kernel, seqs),
        out_shape=jax.ShapeDtypeStruct((seqs, rows // seqs, model), BF16),
        in_specs=[in_vmem()] * 4,
        out_specs=in_vmem(),
        compiler_params=pltpu.CompilerParams(vmem_limit_bytes=HIGH_VMEM),
        cost_estimate=pl.CostEstimate(
            flops=2 * top * slots * rows * model,
            bytes_accessed=2 * slots * model + 6 * rows * model,
            transcendentals=0,
        ),
        name="combine",
    )(back, stream, slots_of, gates)


def local(queries, new_kv, cache, resid, w_out, norm_gain, expert_ids, expert_gates, w_in, w_down):
    n = lax.axis_size("head")
    local_rows, seqs, heads, width = queries.shape
    pair_heads = new_kv.shape[2]
    members = heads // pair_heads
    groups = n // members
    model = resid.shape[2]
    rows = local_rows * seqs
    side = 1 << ((n.bit_length() - 1) // 2)
    side = min(side, heads)
    planes = n // side
    planes_of_seq = heads // side
    pair_groups = [[g * members + m for m in range(members)] for g in range(groups)]
    cross_groups = [[g * members + m for g in range(groups)] for m in range(members)]
    plane_groups = [[p * side + m for m in range(side)] for p in range(planes)]
    column_groups = [[p * side + m for p in range(planes)] for m in range(side)]

    query_slots = queries.reshape(local_rows, n, width).transpose(1, 0, 2)
    q = lax.all_to_all(query_slots, "head", split_axis=0, concat_axis=0, tiled=True)
    q = q.reshape(n * local_rows, width)

    kv_slots = new_kv.reshape(local_rows, groups, 2 * width).transpose(1, 0, 2)
    kv = lax.all_to_all(
        kv_slots, "head", split_axis=0, concat_axis=0, tiled=True, axis_index_groups=cross_groups
    )
    kv = lax.all_gather(kv, "head", axis=0, axis_index_groups=pair_groups)
    pages = lax.all_gather(cache, "head", axis=0, tiled=True, axis_index_groups=pair_groups)

    share = w_out.shape[1]
    w_planes = w_out.reshape(planes_of_seq, side, share, model)
    if planes > planes_of_seq:
        w_planes = jnp.tile(w_planes, (planes // planes_of_seq, 1, 1, 1))
    w = lax.all_to_all(
        w_planes, "head", split_axis=0, concat_axis=0, tiled=True, axis_index_groups=column_groups
    )
    w = lax.all_gather(w, "head", axis=0, axis_index_groups=plane_groups)
    if share % 16:
        w = w.transpose(2, 1, 0, 3, 4).reshape(1, 1, side, width, model)
        w = w.reshape(side, width, model)

    top = expert_ids.shape[2]
    experts = w_in.shape[0] * n
    capacity = max(2, 2 * rows * top // experts)
    ids = expert_ids.transpose(1, 0, 2).reshape(rows, top)
    gates = expert_gates.transpose(1, 0, 2).reshape(rows, top)
    onehot = (ids[:, :, None] == jnp.arange(experts, dtype=jnp.int32)).astype(jnp.int32)
    named = onehot.sum(1)
    before = jnp.cumsum(named, 0) - named
    slots_of = ids * capacity + jnp.sum(onehot * before[:, None, :], 2)
    slots = experts * capacity

    attended = attend(q, pages.reshape(-1, 2 * width), kv)
    a = attended.reshape(planes, side, local_rows, width).transpose(1, 0, 2, 3)
    a = a.reshape(side, planes * local_rows, width)
    a = lax.all_to_all(
        a, "head", split_axis=0, concat_axis=0, tiled=True, axis_index_groups=plane_groups
    )
    if share % 16:
        partial = jnp.einsum("hri,hid->rd", a, w, preferred_element_type=F32).astype(BF16)
    else:
        partial = project(a, w)
    parts = lax.all_to_all(
        partial.reshape(planes, local_rows, model),
        "head",
        split_axis=0,
        concat_axis=0,
        tiled=True,
        axis_index_groups=column_groups,
    )
    parts = parts.reshape(seqs, planes_of_seq, local_rows, model)
    stream, outgoing = route(
        parts, resid.transpose(1, 0, 2), norm_gain[None, :], slots_of.T, slots
    )
    arrived = lax.all_to_all(
        outgoing.reshape(n, slots // n, model), "head", split_axis=0, concat_axis=0, tiled=True
    )
    local_experts = w_in.shape[0]
    if local_experts == 1:
        answered = expert(arrived.reshape(slots, model), w_in[0], w_down[0])
        answered = answered.reshape(n, slots // n, model)
    else:
        arrived = arrived.reshape(n, local_experts, capacity, model).transpose(1, 0, 2, 3)
        arrived = arrived.reshape(local_experts, n * capacity, model)
        answered = jnp.stack([expert(arrived[e], w_in[e], w_down[e]) for e in range(local_experts)])
        answered = answered.reshape(local_experts, n, capacity, model).transpose(1, 0, 2, 3)
        answered = answered.reshape(n, slots // n, model)
    back = lax.all_to_all(answered, "head", split_axis=0, concat_axis=0, tiled=True)
    out = combine(back.reshape(slots, model), stream, slots_of, gates, seqs)
    return out.transpose(1, 0, 2)


def solution(mesh):
    return jax.shard_map(
        local,
        mesh=mesh,
        in_specs=(
            P("head", "grp", None, None),
            P("head", "grp", None, None),
            P(("grp", "head"), None, None),
            P("head", "grp", None),
            P(None, "head", None),
            P(),
            P("head", "grp", None),
            P("head", "grp", None),
            P("head", None, None),
            P("head", None, None),
        ),
        out_specs=P("head", "grp", None),
        check_vma=False,
    )
```

time: 388 us -> 310 us (0.80)
  blocking collectives: 52.5 us -> 153 us
  waiting for transfers between devices: 189 us -> 99.5 us
  matrix products: 39.2 us -> 0 us
  local copies, waits for them, and re-layouts: 38.8 us -> 7.34 us
  Pallas kernels: 0 us -> 25.8 us
  other arithmetic: 19.9 us -> 0.23 us
  starting transfers between devices: 25.9 us -> 10 us
  loops' own time: 7.86 us -> 0 us
    all_to_all x1 -> x5, blocking collectives: 52.5 us -> 153 us  [the longest x1 55.1 us: local(): lax.all_to_all(outgoing.reshape(n, slots // n, model), 'head', split_axis...]
    ppermute x3 -> x0, waiting for transfers between devices: 54 us -> none  [partner_2(): return lax.ppermute(value, axis, pairs)]
    all_to_all x4 -> x2, waiting for transfers between devices: 134 us -> 91.3 us  [the longest x1 47.3 us: local(): lax.all_to_all(answered, 'head', split_axis=0, concat_axis=0, tiled=True)]
    dot_general x19 -> x0, matrix products: 39.2 us -> none  [the longest x4 9.17 us: one_block(): jnp.dot(query_rows, new_keys.T, preferred_element_type=jnp.float32)]
    pallas_call x0 -> x5, Pallas kernels: none -> 25.8 us  [the longest x1 12 us: attend(): pl.pallas_call(functools.partial(attend_kernel, block, chunk, width), out...]
    all_to_all x4 -> x2, starting transfers between devices: 20.9 us -> 9.96 us  [the longest x1 5.25 us: local(): lax.all_to_all(answered, 'head', split_axis=0, concat_axis=0, tiled=True)]
    reduce_sum x6 -> x2, other arithmetic: 10.4 us -> 0.04 us  [the longest x1 0.03 us: local(): slots_of = ids * capacity + jnp.sum(onehot * before[:, None, :], 2)]
    another operation x1 -> x0, loops' own time: 7.86 us -> none  [attend(): return lax.map(one_block, starts).reshape(length, head_width)]
  transfers between devices with their start and end apart: 8 -> 5, of which waited for: 7 -> 3; matrix products, arithmetic and copies ran while one was open for 16% -> 1% of each run, Pallas kernels for 0% -> 4%
where the time goes in v1:
time: 310 us; the launch traced here: 309 us
  blocking collectives  153 us (49%)
  waiting for transfers between devices  99.5 us (32%)
  Pallas kernels  25.8 us (8%)
  between operations  13.2 us (4%)
  starting transfers between devices  10 us (3%)
  local copies, waits for them, and re-layouts  7.34 us (2%)
    all_to_all x1, blocking collectives, local(): lax.all_to_all(outgoing.reshape(n, slots // n, model), 'head', split_axis...  55.1 us
    all_to_all x1, waiting for transfers between devices, local(): lax.all_to_all(answered, 'head', split_axis=0, concat_axis=0, tiled=True)  47.3 us
    all_to_all x1, waiting for transfers between devices, local(): lax.all_to_all(partial.reshape(planes, local_rows, model), 'head', split_...  44 us
    all_to_all x1, blocking collectives, local(): lax.all_to_all(query_slots, 'head', split_axis=0, concat_axis=0, tiled=True)  32.9 us
    all_to_all x1, blocking collectives, local(): lax.all_to_all(w_planes, 'head', split_axis=0, concat_axis=0, tiled=True,...  28.1 us
    all_to_all x1, blocking collectives, local(): lax.all_to_all(a, 'head', split_axis=0, concat_axis=0, tiled=True, axis_i...  27.5 us
    pallas_call x1, Pallas kernels, attend(): pl.pallas_call(functools.partial(attend_kernel, block, chunk, width), out...  12 us
    all_to_all x1, blocking collectives, local(): lax.all_to_all(kv_slots, 'head', split_axis=0, concat_axis=0, tiled=True,...  9.63 us
  transfers between devices with their start and end apart: 5, of which 3 were waited for; matrix products, arithmetic and copies ran while one was open for 1% of the time, Pallas kernels for 4%

profile of v1, /device:TPU:13, one launch (start us, length us, event | category | flops | bytes accessed | tf_op | source)
XLA Modules:
  0.0 309.3 jit_solution(10444520638626514389)
XLA Ops:
  6.5 0.0 copy-start.5
  6.5 0.0 all-gather.6.cloned.1.call-start
  6.5 0.7 all-gather.6.cloned.1.call-update
  7.3 0.0 all-gather.8.cloned.1.call-start
  7.3 1.0 copy.37
  8.3 0.0 copy-start.6
  8.3 9.6 %all_to_all.35 = bf16[2,128,512]{2,1,0:T(8,128)(2,1)} all-to-all(bf16[2,128,512]{2,1,0:T(8,128)(2,1)S(1)} %bitcast.50), channel_id=1, replica_groups={{0,8},{1,9},{2,10},{3,11},{4,12},{5,13},{6,14},{7,15},{16,24},{17,25},{..., dimensions={0} | all-to-all | bytes 524288 | tf_op jit(solution)/shard_map/all_to_all | solution.py:292
  17.9 0.0 all-gather.8.cloned.1.call-update
  18.0 0.0 all-gather.10.cloned.1.call-start
  18.0 0.0 copy-done.5
  18.0 28.1 %all_to_all.36 = bf16[4,4,16,2048]{3,2,1,0:T(8,128)(2,1)} all-to-all(bf16[4,4,16,2048]{3,2,1,0:T(8,128)(2,1)S(1)} %bitcast.49), channel_id=1, replica_groups={{0,4,8,12},{1,5,9,13},{2,6,10,14},{3,7,11,15},{16,20,24,28},{17,21,25,2..., dimensions={0} | all-to-all | bytes 2097152 | tf_op jit(solution)/shard_map/all_to_all | solution.py:302
  46.1 0.0 all-gather.10.cloned.1.call-update
  46.1 0.0 copy-done.6
  46.1 0.3 copy.36
  46.5 32.9 %all_to_all.37 = bf16[16,128,256]{2,1,0:T(8,128)(2,1)S(1)} all-to-all(bf16[16,128,256]{2,1,0:T(8,128)(2,1)S(1)} %bitcast.48), channel_id=1, replica_groups=mesh['grp'=2,'head'=16] {'head'}, dimensions={0} | all-to-all | bytes 2097152 | tf_op jit(solution)/shard_map/all_to_all | solution.py:288
  79.3 0.0 all-gather.6.cloned.1.call-done
  79.3 0.0 all-gather.8.cloned.1.call-done
  79.3 0.0 copy-start.4
  79.3 1.6 copy-done.4
  80.9 12.0 %attend.1 = bf16[2048,256]{1,0:T(8,128)(2,1)S(1)} custom-call(bf16[2048,256]{1,0:T(8,128)(2,1)S(1)} %bitcast.40, bf16[2048,512]{1,0:T(8,128)(2,1)S(1)} %bitcast.46, bf16[8,2,128,512]{3,2,1,0:T(8,128)(2,1)} %bitcast.55), custom_call_target="tpu_custom_call" | custom-call | flops 6442450944 | bytes 8388608 | tf_op jit(solution)/shard_map/attend/pallas_call | solution.py:107
  92.9 0.1 copy.25
  93.0 27.5 %all_to_all.38.a_ref = bf16[4,512,256]{2,1,0:T(8,128)(2,1)S(1)} all-to-all(bf16[4,512,256]{2,1,0:T(8,128)(2,1)S(1)} %bitcast.47), channel_id=1, replica_groups={{0,1,2,3},{4,5,6,7},{8,9,10,11},{12,13,14,15},{16,17,18,19},{20,21,22,2..., dimensions={0} | all-to-all | bytes 2097152 | tf_op jit(solution)/shard_map/all_to_all | solution.py:324
  120.6 7.5 %all-gather.10.cloned.1.call-done = bf16[16,4,16,2048]{3,2,1,0:T(8,128)(2,1)} async-done(((bf16[4,4,16,2048]{3,2,1,0:T(8,128)(2,1)}), bf16[16,4,16,2048]{3,2,1,0:T(8,128)(2,1)}) %all-gather.10.cloned.1.call-update) | async-done | bytes 4194320 | tf_op jit(solution)/shard_map/all_gather | solution.py:305
  128.0 4.7 %project.1 = bf16[512,2048]{1,0:T(8,128)(2,1)S(1)} custom-call(bf16[4,512,256]{2,1,0:T(8,128)(2,1)S(1)} %all_to_all.38.a_ref, bf16[4,4,4,16,2048]{4,3,2,1,0:T(8,128)(2,1)} %bitcast.53), custom_call_target="tpu_custom_call" | custom-call | flops 2147483648 | bytes 7340032 | tf_op jit(solution)/shard_map/project/pallas_call | solution.py:147
  132.8 0.0 copy-start
  132.8 1.3 copy-done
  134.1 4.7 %all-to-all-start.4 = ((bf16[4,128,2048]{2,1,0:T(8,128)(2,1)}), bf16[4,128,2048]{2,1,0:T(8,128)(2,1)S(1)}, u32[]{:S(2)}, u32[]{:S(2)}) async-start(bf16[4,128,2048]{2,1,0:T(8,128)(2,1)} %bitcast.36), calls=%async_computation.4 | async-start | bytes 4194304 | tf_op jit(solution)/shard_map/all_to_all | solution.py:331
  138.8 0.0 copy-done.7
  138.8 0.1 copy.26
  138.9 0.1 copy.27
  139.0 0.1 copy.28
  139.1 0.2 reduce_window_sum.11
  139.3 0.1 copy.30
  139.4 0.1 copy.31
  139.5 0.1 copy.32.slots_ref
  139.6 44.0 %all-to-all-done.4 = bf16[4,128,2048]{2,1,0:T(8,128)(2,1)S(1)} async-done(((bf16[4,128,2048]{2,1,0:T(8,128)(2,1)}), bf16[4,128,2048]{2,1,0:T(8,128)(2,1)S(1)}, u32[]{:S(2)}, u32[]{:S(2)}) %all-to-all-start.4) | async-done | bytes 2097184 | tf_op jit(solution)/shard_map/all_to_all | solution.py:331
  183.6 0.0 copy-done.3
  183.6 1.0 copy-done.2
  184.6 1.2 route.1
  185.8 55.1 %all_to_all.39 = bf16[16,32,2048]{2,1,0:T(8,128)(2,1)S(1)} all-to-all(bf16[16,32,2048]{2,1,0:T(8,128)(2,1)S(1)} %bitcast.38), channel_id=1, replica_groups=mesh['grp'=2,'head'=16] {'head'}, dimensions={0} | all-to-all | bytes 4194304 | tf_op jit(solution)/shard_map/all_to_all | solution.py:343
  240.9 6.3 %expert.1 = bf16[512,2048]{1,0:T(8,128)(2,1)S(1)} custom-call(bf16[512,2048]{1,0:T(8,128)(2,1)S(1)} %bitcast.39, bf16[2048,1024]{1,0:T(8,128)(2,1)} %bitcast.52, bf16[512,2048]{1,0:T(8,128)(2,1)} %bitcast.54), custom_call_target="tpu_custom_call" | custom-call | flops 3221225472 | bytes 10485760 | tf_op jit(solution)/shard_map/expert/pallas_call | solution.py:219
  247.2 0.0 copy-start.1
  247.2 1.3 copy-done.1
  248.5 5.3 %all-to-all-start.6 = ((bf16[16,32,2048]{2,1,0:T(8,128)(2,1)}), bf16[16,32,2048]{2,1,0:T(8,128)(2,1)S(1)}, u32[]{:S(2)}, u32[]{:S(2)}) async-start(bf16[16,32,2048]{2,1,0:T(8,128)(2,1)} %bitcast.37), calls=%async_computation.6 | async-start | bytes 4194304 | tf_op jit(solution)/shard_map/all_to_all | solution.py:356
  253.8 0.0 copy-done.8
  253.8 0.1 copy.33
  253.9 47.3 %all-to-all-done.6 = bf16[16,32,2048]{2,1,0:T(8,128)(2,1)S(1)} async-done(((bf16[16,32,2048]{2,1,0:T(8,128)(2,1)}), bf16[16,32,2048]{2,1,0:T(8,128)(2,1)S(1)}, u32[]{:S(2)}, u32[]{:S(2)}) %all-to-all-start.6) | async-done | bytes 2097184 | tf_op jit(solution)/shard_map/all_to_all | solution.py:356
  301.2 1.6 combine.1
  (8 shorter events, 0.1 us)
Async XLA Ops:
  6.5 11.5 %copy-start.5 = (bf16[16,16,2048]{2,1,0:T(8,128)(2,1)S(1)}, bf16[16,16,2048]{2,1,0:T(8,128)(2,1)}, u32[]{:S(2)}) copy-start(bf16[16,16,2048]{2,1,0:T(8,128)(2,1)} %param.14) | copy-start | bytes 3145732
  6.5 72.8 %all-gather.6.cloned.1.call-start = ((), (), s32[]{:S(2)}) async-start(), calls=%async_computation.7 | async-start | bytes 2359296 | tf_op jit(solution)/shard_map/all_gather | solution.py:296
  7.3 72.1 %all-gather.8.cloned.1.call-start = ((), (), s32[]{:S(2)}) async-start(), calls=%async_computation.8 | async-start | bytes 2359296 | tf_op jit(solution)/shard_map/all_gather | solution.py:295
  8.3 37.8 %copy-start.6 = (bf16[128,1,16,256]{3,2,1,0:T(8,128)(2,1)S(1)}, bf16[128,1,16,256]{3,2,1,0:T(8,128)(2,1)}, u32[]{:S(2)}) copy-start(bf16[128,1,16,256]{3,2,1,0:T(8,128)(2,1)} %param.10) | copy-start | bytes 3145732
  18.0 110.1 %all-gather.10.cloned.1.call-start = ((), (), s32[]{:S(2)}) async-start(), calls=%async_computation.9 | async-start | bytes 5242880 | tf_op jit(solution)/shard_map/all_gather | solution.py:305
  79.3 1.6 copy-start.4
  132.8 1.3 copy-start
  134.1 4.7 %copy-start.7 = (s32[128,1,2]{0,2,1:T(2,128)S(1)}, s32[128,1,2]{0,2,1:T(2,128)}, u32[]{:S(2)}) copy-start(s32[128,1,2]{0,2,1:T(2,128)} %param.16) | copy-start | bytes 3076
  134.1 49.5 %copy-start.3 = (f32[2048]{0:T(1024)S(1)}, f32[2048]{0:T(1024)}, u32[]{:S(2)}) copy-start(f32[2048]{0:T(1024)} %param.15) | copy-start | bytes 24580
  134.1 49.5 %all-to-all-start.4 = ((bf16[4,128,2048]{2,1,0:T(8,128)(2,1)}), bf16[4,128,2048]{2,1,0:T(8,128)(2,1)S(1)}, u32[]{:S(2)}, u32[]{:S(2)}) async-start(bf16[4,128,2048]{2,1,0:T(8,128)(2,1)} %bitcast.36), calls=%async_computation.4 | async-start | bytes 4194304 | tf_op jit(solution)/shard_map/all_to_all | solution.py:331
  183.6 1.0 copy-start.2
  247.2 1.3 copy-start.1
  248.5 5.3 %copy-start.8 = (f32[128,1,2]{0,2,1:T(2,128)S(1)}, f32[128,1,2]{0,2,1:T(2,128)}, u32[]{:S(2)}) copy-start(f32[128,1,2]{0,2,1:T(2,128)} %param.17) | copy-start | bytes 3076
  248.5 52.7 %all-to-all-start.6 = ((bf16[16,32,2048]{2,1,0:T(8,128)(2,1)}), bf16[16,32,2048]{2,1,0:T(8,128)(2,1)S(1)}, u32[]{:S(2)}, u32[]{:S(2)}) async-start(bf16[16,32,2048]{2,1,0:T(8,128)(2,1)} %bitcast.37), calls=%async_computation.6 | async-start | bytes 4194304 | tf_op jit(solution)/shard_map/all_to_all | solution.py:356
Sparse Core Ops, SparseCore 0:
  9.0 26.7 all-gather.5
  37.3 39.8 all-gather.7
  78.8 49.1 all-gather.9

commit v2 on v1

--- a/solution.py
+++ b/solution.py
@@ -127,6 +127,215 @@
     )(q, cache, kv)
 
 
+def attend_pair_kernel(
+    block,
+    chunk,
+    width,
+    q_hbm,
+    page_a,
+    page_b,
+    page_y,
+    page_c,
+    page_cy,
+    kv_own,
+    kv_y,
+    kv_c,
+    kv_cy,
+    o_ref,
+    q_ref,
+    old_ref,
+    kv_ref,
+    s0,
+    s1,
+    sems,
+):
+    me = lax.axis_index("head")
+    members, heads, piece, _ = q_hbm.shape
+    length = members * piece
+    planes = kv_own.shape[0]
+    old = old_ref.shape[0]
+    earlier_group = me // members > 0
+    core = lax.rem(me, 2)
+    copies = []
+
+    def bring(source, target, sem):
+        copy = pltpu.make_async_copy(source, target, sems.at[sem])
+        copy.start()
+        copies.append(copy)
+
+    for member in range(members):
+        for head in range(heads):
+            bring(q_hbm.at[member, head], q_ref.at[head, pl.ds(member * piece, piece)], 0)
+    place = 0
+    for page in (page_a, page_b, page_y, page_c, page_cy):
+        count = page.shape[0]
+        bring(page, old_ref.at[pl.ds(place, count)], 1)
+        place += count
+    for flip, pieces_of in ((0, kv_own), (2, kv_y), (1, kv_c), (3, kv_cy)):
+        for t in range(planes):
+            number = jnp.bitwise_and(
+                jnp.bitwise_xor(me, flip ^ (t * (members // 2))), members - 1
+            )
+            start = pl.multiple_of(number * piece, piece)
+            area = 0 if t * (members // 2) >= members else length
+            bring(pieces_of.at[t], kv_ref.at[pl.ds(area + start, piece)], 2)
+    for copy in copies:
+        copy.wait()
+    scale = width**-0.5
+    scores = [s0, s1]
+    blocks = length // block
+    units = [(head, b) for head in range(heads) for b in range(blocks)]
+
+    def pieces(unit):
+        _, b = units[unit]
+        out = [("old", k, chunk, k) for k in range(0, old, chunk)]
+        out += [("past", k, chunk, old + k) for k in range(0, length, chunk)]
+        last = b * block
+        for k in range(0, last, chunk):
+            out.append(("new", length + k, min(chunk, last - k), old + length + k))
+        out.append(("edge", length + last, block, old + length + last))
+        return out
+
+    def make_scores(unit, part, running):
+        kind, first, count, column = part
+        head, b = units[unit]
+        keys = (old_ref if kind == "old" else kv_ref)[pl.ds(first, count), :width]
+        s = lax.dot_general(
+            q_ref[head, pl.ds(b * block, block), :],
+            keys,
+            (((1,), (1,)), ((), ())),
+            preferred_element_type=F32,
+        )
+        if kind == "past":
+            s = jnp.where(earlier_group, s, -jnp.inf)
+        if kind == "edge":
+            row = lax.broadcasted_iota(jnp.int32, s.shape, 0)
+            col = lax.broadcasted_iota(jnp.int32, s.shape, 1)
+            s = jnp.where(col <= row, s, -jnp.inf)
+        scores[unit % 2][:, pl.ds(column, count)] = s
+        for k in range(0, count, 128):
+            piece_max = s[:, k : k + 128]
+            running = piece_max if running is None else jnp.maximum(running, piece_max)
+        return running
+
+    def use_scores(unit, part, top, total, acc):
+        kind, first, count, column = part
+        values = (old_ref if kind == "old" else kv_ref)[pl.ds(first, count), width:]
+        e = jnp.exp((scores[unit % 2][:, pl.ds(column, count)] - top) * scale)
+        for k in range(0, count, 128):
+            total = e[:, k : k + 128] if total is None else total + e[:, k : k + 128]
+        product = jnp.dot(e.astype(BF16), values, preferred_element_type=F32)
+        return total, product if acc is None else acc + product
+
+    running = None
+    for part in pieces(0):
+        running = make_scores(0, part, running)
+    for unit, (head, b) in enumerate(units):
+        top = jnp.max(running, 1, keepdims=True)
+        now = pieces(unit)
+        later = pieces(unit + 1) if unit + 1 < len(units) else []
+        running, total, acc = None, None, None
+        for k in range(max(len(now), len(later))):
+            if k < len(now):
+                total, acc = use_scores(unit, now[k], top, total, acc)
+            if k < len(later):
+                running = make_scores(unit + 1, later[k], running)
+        done = (acc / jnp.sum(total, 1, keepdims=True)).astype(BF16)
+        for k in range(0, block, piece):
+            member = (b * block + k) // piece
+            side = jnp.bitwise_xor(core, member % 2)
+            o_ref[side, pl.ds((member // 2) * piece, piece), pl.ds(head * width, width)] = done[
+                k : k + piece
+            ]
+
+
+def attend_pair(q, pages, kvs):
+    members, heads, piece, width = q.shape
+    length = members * piece
+    old = sum(page.shape[0] for page in pages)
+    block = 2 * piece
+    chunk = min(512, old, length)
+    keys = old + 2 * length
+    return pl.pallas_call(
+        functools.partial(attend_pair_kernel, block, chunk, width),
+        out_shape=jax.ShapeDtypeStruct((2, length // 2, heads * width), BF16),
+        in_specs=[anywhere()] * (1 + len(pages) + len(kvs)),
+        out_specs=in_vmem(),
+        scratch_shapes=[
+            pltpu.VMEM((heads, length, width), BF16),
+            pltpu.VMEM((old, 2 * width), BF16),
+            pltpu.VMEM((2 * length, 2 * width), BF16),
+            pltpu.VMEM((block, keys), F32),
+            pltpu.VMEM((block, keys), F32),
+            pltpu.SemaphoreType.DMA((3,)),
+        ],
+        compiler_params=pltpu.CompilerParams(vmem_limit_bytes=HIGH_VMEM),
+        cost_estimate=pl.CostEstimate(
+            flops=4 * heads * length * (keys - length // 2) * width,
+            bytes_accessed=4 * (heads * length + keys) * width,
+            transcendentals=heads * length * (keys - length // 2),
+        ),
+        name="attend",
+    )(q, *pages, *kvs)
+
+
+def project_pair_kernel(a_ref, got_ref, w_own, w_c, w_x, w_cx, o_ref, w_ref, sems):
+    me = lax.axis_index("head")
+    half = lax.axis_index("grp")
+    core = lax.rem(me, 2)
+    planes, sides, heads, share, columns = w_own.shape
+    width = w_ref.shape[1]
+    copies = []
+    for flip, x, pieces_of in ((0, 0, w_own), (1, 0, w_c), (0, 1, w_x), (1, 1, w_cx)):
+        column = pl.multiple_of(jnp.bitwise_xor(half, x) * columns, columns)
+        for t in range(planes):
+            for u in range(sides):
+                number = jnp.bitwise_xor(me, flip ^ (2 * u) ^ (4 * t))
+                row = pl.multiple_of(number * share, share)
+                copy = pltpu.make_async_copy(
+                    pieces_of.at[t, u],
+                    w_ref.at[:, pl.ds(row, share), pl.ds(column, columns)],
+                    sems.at[0],
+                )
+                copy.start()
+                copies.append(copy)
+    for copy in copies:
+        copy.wait()
+    acc = None
+    for k in range(heads):
+        mine = k < heads // 2
+        column = (k % (heads // 2)) * width
+        a = a_ref[0, :, pl.ds(column, width)] if mine else got_ref[:, pl.ds(column, width)]
+        head = jnp.bitwise_xor(core, 0 if mine else 1) * (heads // 2) + k % (heads // 2)
+        part = jnp.dot(a, w_ref[head], preferred_element_type=F32)
+        acc = part if acc is None else acc + part
+    o_ref[...] = acc.astype(BF16)
+
+
+def project_pair(a, got, w_own, w_c, w_x, w_cx):
+    planes, sides, heads, share, columns = w_own.shape
+    rows = got.shape[0]
+    width = 2 * got.shape[1] // heads
+    model = 2 * columns
+    return pl.pallas_call(
+        project_pair_kernel,
+        out_shape=jax.ShapeDtypeStruct((rows, model), BF16),
+        in_specs=[in_vmem(), in_vmem()] + [anywhere()] * 4,
+        out_specs=in_vmem(),
+        scratch_shapes=[
+            pltpu.VMEM((heads, width, model), BF16),
+            pltpu.SemaphoreType.DMA((1,)),
+        ],
+        compiler_params=pltpu.CompilerParams(vmem_limit_bytes=HIGH_VMEM),
+        cost_estimate=pl.CostEstimate(
+            flops=2 * heads * rows * width * model,
+            bytes_accessed=2 * (heads * width * model + heads * rows * width + rows * model),
+            transcendentals=0,
+        ),
+        name="project",
+    )(a, got, w_own, w_c, w_x, w_cx)
+
+
 def project_kernel(a_ref, w_ref, o_ref):
     members = a_ref.shape[0]
     planes, share = w_ref.shape[1], w_ref.shape[3]
@@ -267,14 +476,99 @@
     )(back, stream, slots_of, gates)
 
 
-def local(queries, new_kv, cache, resid, w_out, norm_gain, expert_ids, expert_gates, w_in, w_down):
+def flipped(value, axis, mask):
+    pairs = [(source, source ^ mask) for source in range(lax.axis_size(axis))]
+    return lax.ppermute(value, axis, pairs)
+
+
+def parts_in_pairs(queries, new_kv, cache, w_out):
+    n = lax.axis_size("head")
+    local_rows, _, heads, width = queries.shape
+    pair_heads = new_kv.shape[2]
+    members = heads // pair_heads
+    model = w_out.shape[2]
+    share = w_out.shape[1]
+    me = lax.axis_index("head")
+    plane_bit = members // 2
+    planes = n // plane_bit
+    b = (me // plane_bit) % 2
+    y = (me // 2) % 2
+    group_sets = [[g * members + m for m in range(members)] for g in range(n // members)]
+
+    query_slots = queries.reshape(local_rows, heads, width).transpose(1, 0, 2)
+    query_slots = query_slots.reshape(members, heads // members, local_rows, width)
+    q = lax.all_to_all(
+        query_slots, "head", split_axis=0, concat_axis=0, tiled=True, axis_index_groups=group_sets
+    )
+
+    def page_target(source, other):
+        p, plane, rest = source // members, (source // plane_bit) % 2, source % plane_bit
+        return (plane ^ other) * members + p * plane_bit + rest
+
+    page_a, page_b = (
+        lax.ppermute(cache[0], "head", [(d, page_target(d, other)) for d in range(n)])
+        for other in range(2)
+    )
+    own_pages = jnp.concatenate([page_a, page_b], 0)
+    pages_y = flipped(own_pages, "head", 2)
+    pages_c = flipped(own_pages, "head", 1)
+    pages_cy = flipped(pages_y, "head", 1)
+
+    kv_heads = new_kv.reshape(local_rows, pair_heads, 2 * width).transpose(1, 0, 2)
+    kv_same = lax.dynamic_index_in_dim(kv_heads, b, 0, keepdims=False)
+    kv_other = lax.dynamic_index_in_dim(kv_heads, 1 - b, 0, keepdims=False)
+    kv_own = [kv_same]
+    for t in range(1, planes):
+        kv_own.append(flipped(kv_other if t % 2 else kv_same, "head", t * plane_bit))
+    kv_own = jnp.stack(kv_own, 0)
+    kv_y = flipped(kv_own, "head", 2)
+    kv_c = flipped(kv_own, "head", 1)
+    kv_cy = flipped(kv_y, "head", 1)
+
+    columns = model // 2
+    w = lax.dynamic_slice_in_dim(w_out, lax.axis_index("grp") * columns, columns, 2)
+    w = w.reshape(2, 2, heads // 4, share, columns)
+    w_keep = lax.dynamic_index_in_dim(w, y, 1, keepdims=False)
+    w_give = lax.dynamic_index_in_dim(w, 1 - y, 1, keepdims=False)
+    w_both = jnp.stack([w_keep, flipped(w_give, "head", 2)], 1)
+    w_same = lax.dynamic_index_in_dim(w_both, b, 0, keepdims=False)
+    w_other = lax.dynamic_index_in_dim(w_both, 1 - b, 0, keepdims=False)
+    w_own = [w_same]
+    for t in range(1, planes):
+        w_own.append(flipped(w_other if t % 2 else w_same, "head", t * plane_bit))
+    w_own = jnp.stack(w_own, 0)
+    w_x = flipped(w_own, "grp", 1)
+    w_c = flipped(w_own, "head", 1)
+    w_cx = flipped(w_x, "head", 1)
+
+    a = attend_pair(
+        q, (page_a, page_b, pages_y, pages_c, pages_cy), (kv_own, kv_y, kv_c, kv_cy)
+    )
+    got = flipped(a[1], "head", 1)
+    partial = project_pair(a, got, w_own, w_c, w_x, w_cx)
+    quads = [
+        [g * members + 2 * k + core for k in range(members // 2)]
+        for g in range(n // members)
+        for core in range(2)
+    ]
+    parts = lax.all_to_all(
+        partial.reshape(members // 2, local_rows, model),
+        "head",
+        split_axis=0,
+        concat_axis=0,
+        tiled=True,
+        axis_index_groups=quads,
+    )
+    return parts[None]
+
+
+def parts_in_planes(queries, new_kv, cache, w_out):
     n = lax.axis_size("head")
     local_rows, seqs, heads, width = queries.shape
     pair_heads = new_kv.shape[2]
     members = heads // pair_heads
     groups = n // members
-    model = resid.shape[2]
-    rows = local_rows * seqs
+    model = w_out.shape[2]
     side = 1 << ((n.bit_length() - 1) // 2)
     side = min(side, heads)
     planes = n // side
@@ -306,17 +600,6 @@
     if share % 16:
         w = w.transpose(2, 1, 0, 3, 4).reshape(1, 1, side, width, model)
         w = w.reshape(side, width, model)
-
-    top = expert_ids.shape[2]
-    experts = w_in.shape[0] * n
-    capacity = max(2, 2 * rows * top // experts)
-    ids = expert_ids.transpose(1, 0, 2).reshape(rows, top)
-    gates = expert_gates.transpose(1, 0, 2).reshape(rows, top)
-    onehot = (ids[:, :, None] == jnp.arange(experts, dtype=jnp.int32)).astype(jnp.int32)
-    named = onehot.sum(1)
-    before = jnp.cumsum(named, 0) - named
-    slots_of = ids * capacity + jnp.sum(onehot * before[:, None, :], 2)
-    slots = experts * capacity
 
     attended = attend(q, pages.reshape(-1, 2 * width), kv)
     a = attended.reshape(planes, side, local_rows, width).transpose(1, 0, 2, 3)
@@ -336,7 +619,38 @@
         tiled=True,
         axis_index_groups=column_groups,
     )
-    parts = parts.reshape(seqs, planes_of_seq, local_rows, model)
+    return parts.reshape(seqs, planes_of_seq, local_rows, model)
+
+
+def local(queries, new_kv, cache, resid, w_out, norm_gain, expert_ids, expert_gates, w_in, w_down):
+    n = lax.axis_size("head")
+    local_rows, seqs, heads, width = queries.shape
+    model = resid.shape[2]
+    rows = local_rows * seqs
+    members = heads // new_kv.shape[2]
+    in_pairs = (
+        lax.axis_size("grp") == 2
+        and seqs == 1
+        and new_kv.shape[2] == 2
+        and n == heads == 2 * members
+        and members == 8
+        and cache.shape[0] == 1
+        and w_out.shape[1] % 16 == 0
+    )
+    plan = parts_in_pairs if in_pairs else parts_in_planes
+    parts = plan(queries, new_kv, cache, w_out)
+
+    top = expert_ids.shape[2]
+    experts = w_in.shape[0] * n
+    capacity = max(2, 2 * rows * top // experts)
+    ids = expert_ids.transpose(1, 0, 2).reshape(rows, top)
+    gates = expert_gates.transpose(1, 0, 2).reshape(rows, top)
+    onehot = (ids[:, :, None] == jnp.arange(experts, dtype=jnp.int32)).astype(jnp.int32)
+    named = onehot.sum(1)
+    before = jnp.cumsum(named, 0) - named
+    slots_of = ids * capacity + jnp.sum(onehot * before[:, None, :], 2)
+    slots = experts * capacity
+
     stream, outgoing = route(
         parts, resid.transpose(1, 0, 2), norm_gain[None, :], slots_of.T, slots
     )

time: 310 us -> 261 us (0.84)
  blocking collectives: 153 us -> 51.9 us
  starting transfers between devices: 10 us -> 45.7 us
  waiting for transfers between devices: 99.5 us -> 113 us
  between operations: 13.2 us -> 0.27 us
  local copies, waits for them, and re-layouts: 7.34 us -> 18.7 us
  Pallas kernels: 25.8 us -> 30.1 us
    all_to_all x4 -> x0, blocking collectives: 98.1 us -> none  [the longest x1 32.9 us: local(): lax.all_to_all(query_slots, 'head', split_axis=0, concat_axis=0, tiled=True)]
    ppermute x0 -> x19, waiting for transfers between devices: none -> 43 us  [the longest x17 43 us: flipped(): return lax.ppermute(value, axis, pairs)]
    ppermute x0 -> x19, starting transfers between devices: none -> 28 us  [the longest x17 23.8 us: flipped(): return lax.ppermute(value, axis, pairs)]
    all_to_all x1 -> x2, waiting for transfers between devices: 44 us -> 23.1 us  [the longest x1 23.1 us: parts_in_pairs(): lax.all_to_all(partial.reshape(members // 2, local_rows, model), 'head',...]
    unnamed x22 -> x49, local copies, waits for them, and re-layouts: 6.86 us -> 16.3 us
    all_to_all x1 -> x2, starting transfers between devices: 4.71 us -> 12.5 us  [the longest x1 6.32 us: parts_in_pairs(): lax.all_to_all(partial.reshape(members // 2, local_rows, model), 'head',...]
    all_gather x3 -> x0, waiting for transfers between devices: 7.46 us -> none  [the longest x1 7.46 us: local(): w = lax.all_gather(w, 'head', axis=0, axis_index_groups=plane_groups)]
    pallas_call x2, Pallas kernels: 16.8 us -> 21.1 us  [the longest x1 15.2 us: attend_pair(): pl.pallas_call(functools.partial(attend_pair_kernel, block, chunk, width)...]
  transfers between devices with their start and end apart: 5 -> 22, of which waited for: 3 -> 9; matrix products, arithmetic and copies ran while one was open for 1% -> 1% of each run, Pallas kernels for 4% -> 6%
where the time goes in v2:
time: 261 us
  waiting for transfers between devices  113 us (43%)
  blocking collectives  51.9 us (20%)
  starting transfers between devices  45.7 us (18%)
  Pallas kernels  30.1 us (12%)
  local copies, waits for them, and re-layouts  18.7 us (7%)
    all_to_all x1, blocking collectives, local(): lax.all_to_all(outgoing.reshape(n, slots // n, model), 'head', split_axis...  51.9 us
    all_to_all x1, waiting for transfers between devices, local(): lax.all_to_all(answered, 'head', split_axis=0, concat_axis=0, tiled=True)  47.3 us
    ppermute x17, waiting for transfers between devices, flipped(): return lax.ppermute(value, axis, pairs)  43 us
    ppermute x17, starting transfers between devices, flipped(): return lax.ppermute(value, axis, pairs)  23.8 us
    all_to_all x1, waiting for transfers between devices, parts_in_pairs(): lax.all_to_all(partial.reshape(members // 2, local_rows, model), 'head',...  23.1 us
    unnamed x49, local copies, waits for them, and re-layouts  16.3 us
    pallas_call x1, Pallas kernels, attend_pair(): pl.pallas_call(functools.partial(attend_pair_kernel, block, chunk, width)...  15.2 us
    pallas_call x1, Pallas kernels, expert(): pl.pallas_call(expert_kernel, out_shape=jax.ShapeDtypeStruct((rows, model...  6.34 us
  transfers between devices with their start and end apart: 22, of which 9 were waited for; matrix products, arithmetic and copies ran while one was open for 1% of the time, Pallas kernels for 6%

profile of v2, /device:TPU:13, one launch (start us, length us, event | category | flops | bytes accessed | tf_op | source)
XLA Modules:
  0.0 260.6 jit_solution(3356489342881383569)
XLA Ops:
  0.0 1.2 copy-done
  1.6 1.3 copy.21
  3.0 6.1 %all-to-all-start = ((bf16[8,2,128,256]{3,2,1,0:T(8,128)(2,1)}), bf16[8,2,128,256]{3,2,1,0:T(8,128)(2,1)}, u32[]{:S(2)}, u32[]{:S(2)}) async-start(bf16[8,2,128,256]{3,2,1,0:T(8,128)(2,1)} %bitcast.2), calls=%async_computation | async-start | bytes 2097152 | tf_op jit(solution)/shard_map/all_to_all | solution.py:500
  9.1 0.5 constant_dynamic-slice_fusion.3
  9.7 1.4 collective-permute-start.7
  11.1 1.0 collective-permute-start.6
  12.2 1.2 collective-permute-start.5
  13.4 3.0 %collective-permute-start = (bf16[256,512]{1,0:T(8,128)(2,1)}, bf16[256,512]{1,0:T(8,128)(2,1)S(1)}, u32[]{:S(2)}, u32[]{:S(2)}) collective-permute-start(bf16[256,512]{1,0:T(8,128)(2,1)} %bitcast.3), channel_id=1, source_target_pairs={{0,0},{1,1},{2,2},{3,3},{4,8},{5,9},{6,10},{7,11},{8,4},{9,5},{10,... | collective-permute-start | bytes 786440 | tf_op jit(solution)/shard_map/ppermute | solution.py:509
  16.5 0.4 collective-permute-start.15
  16.9 9.6 %collective-permute-start.14 = (bf16[2,4,16,1024]{3,2,1,0:T(8,128)(2,1)S(1)}, bf16[2,4,16,1024]{3,2,1,0:T(8,128)(2,1)S(1)}, u32[]{:S(2)}, u32[]{:S(2)}) collective-permute-start(bf16[2,4,16,1024]{3,2,1,0:T(8,128)(2,1)S(1)} %bitcast.55), channel_id=1, source_target_pairs={{0,8},{1,9},{2,10},{3,11},{4,12},{5,13},{6,14},{7,15},{8,0},{9,1},... | collective-permute-start | bytes 786440 | tf_op jit(solution)/shard_map/ppermute | solution.py:481
  26.5 2.8 %collective-permute-done.6 = bf16[128,512]{1,0:T(8,128)(2,1)S(1)} collective-permute-done((bf16[128,512]{1,0:T(8,128)(2,1)S(1)}, bf16[128,512]{1,0:T(8,128)(2,1)S(1)}, u32[]{:S(2)}, u32[]{:S(2)}) %collective-permute-start.6) | collective-permute-done | bytes 131104 | tf_op jit(solution)/shard_map/ppermute | solution.py:481
  29.3 0.7 collective-permute-done.5
  30.0 1.2 collective-permute-start.1
  31.6 14.0 %collective-permute-done.15 = bf16[2,4,16,1024]{3,2,1,0:T(8,128)(2,1)S(1)} collective-permute-done((bf16[2,4,16,1024]{3,2,1,0:T(8,128)(2,1)S(1)}, bf16[2,4,16,1024]{3,2,1,0:T(8,128)(2,1)S(1)}, u32[]{:S(2)}, u32[]{:S(2)}) %collective-permute-start.15) | collective-permute-done | bytes 262176 | tf_op jit(solution)/shard_map/ppermute | solution.py:481
  45.7 9.7 %collective-permute-done.14 = bf16[2,4,16,1024]{3,2,1,0:T(8,128)(2,1)S(1)} collective-permute-done((bf16[2,4,16,1024]{3,2,1,0:T(8,128)(2,1)S(1)}, bf16[2,4,16,1024]{3,2,1,0:T(8,128)(2,1)S(1)}, u32[]{:S(2)}, u32[]{:S(2)}) %collective-permute-start.14) | collective-permute-done | bytes 262176 | tf_op jit(solution)/shard_map/ppermute | solution.py:481
  55.5 1.3 collective-permute-start.17
  56.9 2.3 collective-permute-start.9
  59.2 0.5 collective-permute-start.10
  59.7 0.8 copy-done.6
  60.5 8.0 %collective-permute-done.2.page_y = bf16[512,512]{1,0:T(8,128)(2,1)S(1)} collective-permute-done((bf16[512,512]{1,0:T(8,128)(2,1)S(1)}, bf16[512,512]{1,0:T(8,128)(2,1)S(1)}, u32[]{:S(2)}, u32[]{:S(2)}) %collective-permute-start.2) | collective-permute-done | bytes 524320 | tf_op jit(solution)/shard_map/ppermute | solution.py:481
  68.5 2.7 %collective-permute-start.4 = (bf16[512,512]{1,0:T(8,128)(2,1)S(1)}, bf16[512,512]{1,0:T(8,128)(2,1)S(1)}, u32[]{:S(2)}, u32[]{:S(2)}) collective-permute-start(bf16[512,512]{1,0:T(8,128)(2,1)S(1)} %collective-permute-done.2.page_y), channel_id=1, source_target_pairs={{0,1},{1,0},{2,3},{3,2},{4,5},{5,4},{6,7},{7,6},{8,9},{9,8},{10,11... | collective-permute-start | bytes 1572872 | tf_op jit(solution)/shard_map/ppermute | solution.py:481
  71.2 0.8 copy-done.8
  72.0 0.8 copy-done.10
  72.8 5.8 %collective-permute-done.17.w_x = bf16[4,2,4,16,1024]{4,3,2,1,0:T(8,128)(2,1)} collective-permute-done((bf16[4,2,4,16,1024]{4,3,2,1,0:T(8,128)(2,1)S(1)}, bf16[4,2,4,16,1024]{4,3,2,1,0:T(8,128)(2,1)}, u32[]{:S(2)}, u32[]{:S(2)}) %collective-permute-start.17) | collective-permute-done | bytes 1048608 | tf_op jit(solution)/shard_map/ppermute | solution.py:481
  78.7 2.6 collective-permute-start.18
  81.3 0.8 copy-done.12
  82.1 0.9 copy-done.14
  82.9 0.8 copy-done.16
  83.7 1.0 copy-done.7
  84.8 1.0 copy-done.9
  85.8 1.0 copy-done.11
  86.9 1.0 copy-done.13
  87.9 1.0 copy-done.15
  88.9 1.0 copy-done.17
  90.0 15.2 %attend.1.a_ref = bf16[2,512,512]{2,1,0:T(8,128)(2,1)S(1)} custom-call(bf16[8,2,128,256]{3,2,1,0:T(8,128)(2,1)} %all-to-all-done.q_hbm, bf16[256,512]{1,0:T(8,128)(2,1)S(1)} %collective-permute-done.page_a, bf16[256,512]{1,0:T(8,128)(2,1)S(1)} %collective-permute-done.1.page_b, bf16[512,512]{1,0:T(8,128)(2,1)S(1)} %copy-done.9, ...), custom_call_target="tpu_custom_call" | custom-call | flops 7516192768 | bytes 6291456 | tf_op jit(solution)/shard_map/attend/pallas_call | solution.py:259
  105.3 1.9 collective-permute-done.11.got_ref
  107.2 5.9 %project.1 = bf16[512,2048]{1,0:T(8,128)(2,1)} custom-call(bf16[2,512,512]{2,1,0:T(8,128)(2,1)S(1)} %attend.1.a_ref, bf16[512,512]{1,0:T(8,128)(2,1)S(1)} %collective-permute-done.11.got_ref, bf16[4,2,4,16,1024]{4,3,2,1,0:T(8,128)(2,1)S(1)} %pad_maximum_fusion.w_own, bf16[4,2,4,16,1024]{4,3,2,1,0:T(8,128)(2,1)} %collective-permute-done.16.w_c, ...), custom_call_target="tpu_custom_call" | custom-call | flops 2147483648 | bytes 7340032 | tf_op jit(solution)/shard_map/project/pallas_call | solution.py:320
  113.1 6.3 %all-to-all-start.1 = ((bf16[4,128,2048]{2,1,0:T(8,128)(2,1)}), bf16[4,128,2048]{2,1,0:T(8,128)(2,1)S(1)}, u32[]{:S(2)}, u32[]{:S(2)}) async-start(bf16[4,128,2048]{2,1,0:T(8,128)(2,1)} %bitcast.52), calls=%async_computation.1 | async-start | bytes 4194304 | tf_op jit(solution)/shard_map/all_to_all | solution.py:554
  120.2 23.1 %all-to-all-done.1 = bf16[4,128,2048]{2,1,0:T(8,128)(2,1)S(1)} async-done(((bf16[4,128,2048]{2,1,0:T(8,128)(2,1)}), bf16[4,128,2048]{2,1,0:T(8,128)(2,1)S(1)}, u32[]{:S(2)}, u32[]{:S(2)}) %all-to-all-start.1) | async-done | bytes 2097184 | tf_op jit(solution)/shard_map/all_to_all | solution.py:554
  143.3 1.0 copy-done.4
  144.3 1.2 route.1
  145.5 51.9 %all_to_all.20 = bf16[16,32,2048]{2,1,0:T(8,128)(2,1)S(1)} all-to-all(bf16[16,32,2048]{2,1,0:T(8,128)(2,1)S(1)} %bitcast.46), channel_id=1, replica_groups=mesh['grp'=2,'head'=16] {'head'}, dimensions={0} | all-to-all | bytes 4194304 | tf_op jit(solution)/shard_map/all_to_all | solution.py:657
  197.4 6.3 %expert.1 = bf16[512,2048]{1,0:T(8,128)(2,1)S(1)} custom-call(bf16[512,2048]{1,0:T(8,128)(2,1)S(1)} %bitcast.47, bf16[2048,1024]{1,0:T(8,128)(2,1)} %bitcast.68, bf16[512,2048]{1,0:T(8,128)(2,1)} %bitcast.69), custom_call_target="tpu_custom_call" | custom-call | flops 3221225472 | bytes 10485760 | tf_op jit(solution)/shard_map/expert/pallas_call | solution.py:428
  203.7 1.4 copy-done.1
  205.1 5.3 %all-to-all-start.3 = ((bf16[16,32,2048]{2,1,0:T(8,128)(2,1)}), bf16[16,32,2048]{2,1,0:T(8,128)(2,1)S(1)}, u32[]{:S(2)}, u32[]{:S(2)}) async-start(bf16[16,32,2048]{2,1,0:T(8,128)(2,1)} %bitcast.45), calls=%async_computation.3 | async-start | bytes 4194304 | tf_op jit(solution)/shard_map/all_to_all | solution.py:670
  210.5 47.3 %all-to-all-done.3 = bf16[16,32,2048]{2,1,0:T(8,128)(2,1)S(1)} async-done(((bf16[16,32,2048]{2,1,0:T(8,128)(2,1)}), bf16[16,32,2048]{2,1,0:T(8,128)(2,1)S(1)}, u32[]{:S(2)}, u32[]{:S(2)}) %all-to-all-start.3) | async-done | bytes 2097184 | tf_op jit(solution)/shard_map/all_to_all | solution.py:670
  257.8 1.2 copy-done.3
  259.0 1.6 combine.1
  (70 shorter events, 2.2 us)
Async XLA Ops:
  0.0 1.2 copy-start
  0.0 1.6 copy-start.19
  1.3 15.1 %collective-permute-start.12 = (bf16[2,4,16,1024]{3,2,1,0:T(8,128)(2,1)S(1)}, bf16[2,4,16,1024]{3,2,1,0:T(8,128)(2,1)S(1)}, u32[]{:S(2)}, u32[]{:S(2)}) collective-permute-start(bf16[2,4,16,1024]{3,2,1,0:T(8,128)(2,1)S(1)} %get-tuple-element.11), channel_id=1, source_target_pairs={{0,2},{1,3},{2,0},{3,1},{4,6},{5,7},{6,4},{7,5},{8,10},{9,11},{10,... | collective-permute-start | bytes 786440 | tf_op jit(solution)/shard_map/ppermute | solution.py:481
  1.6 7.5 %copy-start.18 = (bf16[128,1,2,512]{3,2,1,0:T(2,128)(2,1)S(1)}, bf16[128,1,2,512]{3,2,1,0:T(2,128)(2,1)}, u32[]{:S(2)}) copy-start(bf16[128,1,2,512]{3,2,1,0:T(2,128)(2,1)} %param.11) | copy-start | bytes 786436
  3.0 80.8 %all-to-all-start = ((bf16[8,2,128,256]{3,2,1,0:T(8,128)(2,1)}), bf16[8,2,128,256]{3,2,1,0:T(8,128)(2,1)}, u32[]{:S(2)}, u32[]{:S(2)}) async-start(bf16[8,2,128,256]{3,2,1,0:T(8,128)(2,1)} %bitcast.2), calls=%async_computation | async-start | bytes 2097152 | tf_op jit(solution)/shard_map/all_to_all | solution.py:500
  9.7 7.2 %collective-permute-start.7 = (bf16[128,512]{1,0:T(8,128)(2,1)S(1)}, bf16[128,512]{1,0:T(8,128)(2,1)S(1)}, u32[]{:S(2)}, u32[]{:S(2)}) collective-permute-start(bf16[128,512]{1,0:T(8,128)(2,1)S(1)} %bitcast.63), channel_id=1, source_target_pairs={{0,12},{1,13},{2,14},{3,15},{4,8},{5,9},{6,10},{7,11},{8,4},{9,5},... | collective-permute-start | bytes 393224 | tf_op jit(solution)/shard_map/ppermute | solution.py:481
  11.1 18.1 %collective-permute-start.6 = (bf16[128,512]{1,0:T(8,128)(2,1)S(1)}, bf16[128,512]{1,0:T(8,128)(2,1)S(1)}, u32[]{:S(2)}, u32[]{:S(2)}) collective-permute-start(bf16[128,512]{1,0:T(8,128)(2,1)S(1)} %bitcast.57), channel_id=1, source_target_pairs={{0,8},{1,9},{2,10},{3,11},{4,12},{5,13},{6,14},{7,15},{8,0},{9,1},... | collective-permute-start | bytes 393224 | tf_op jit(solution)/shard_map/ppermute | solution.py:481
  12.2 17.9 %collective-permute-start.5 = (bf16[128,512]{1,0:T(8,128)(2,1)S(1)}, bf16[128,512]{1,0:T(8,128)(2,1)S(1)}, u32[]{:S(2)}, u32[]{:S(2)}) collective-permute-start(bf16[128,512]{1,0:T(8,128)(2,1)S(1)} %bitcast.64), channel_id=1, source_target_pairs={{0,4},{1,5},{2,6},{3,7},{4,0},{5,1},{6,2},{7,3},{8,12},{9,13},{10,... | collective-permute-start | bytes 393224 | tf_op jit(solution)/shard_map/ppermute | solution.py:481
  13.4 17.9 %collective-permute-start = (bf16[256,512]{1,0:T(8,128)(2,1)}, bf16[256,512]{1,0:T(8,128)(2,1)S(1)}, u32[]{:S(2)}, u32[]{:S(2)}) collective-permute-start(bf16[256,512]{1,0:T(8,128)(2,1)} %bitcast.3), channel_id=1, source_target_pairs={{0,0},{1,1},{2,2},{3,3},{4,8},{5,9},{6,10},{7,11},{8,4},{9,5},{10,... | collective-permute-start | bytes 786440 | tf_op jit(solution)/shard_map/ppermute | solution.py:509
  16.5 29.2 %collective-permute-start.15 = (bf16[2,4,16,1024]{3,2,1,0:T(8,128)(2,1)S(1)}, bf16[2,4,16,1024]{3,2,1,0:T(8,128)(2,1)S(1)}, u32[]{:S(2)}, u32[]{:S(2)}) collective-permute-start(bf16[2,4,16,1024]{3,2,1,0:T(8,128)(2,1)S(1)} %get-tuple-element.10), channel_id=1, source_target_pairs={{0,12},{1,13},{2,14},{3,15},{4,8},{5,9},{6,10},{7,11},{8,4},{9,5},... | collective-permute-start | bytes 786440 | tf_op jit(solution)/shard_map/ppermute | solution.py:481
  16.9 38.5 %collective-permute-start.14 = (bf16[2,4,16,1024]{3,2,1,0:T(8,128)(2,1)S(1)}, bf16[2,4,16,1024]{3,2,1,0:T(8,128)(2,1)S(1)}, u32[]{:S(2)}, u32[]{:S(2)}) collective-permute-start(bf16[2,4,16,1024]{3,2,1,0:T(8,128)(2,1)S(1)} %bitcast.55), channel_id=1, source_target_pairs={{0,8},{1,9},{2,10},{3,11},{4,12},{5,13},{6,14},{7,15},{8,0},{9,1},... | collective-permute-start | bytes 786440 | tf_op jit(solution)/shard_map/ppermute | solution.py:481
  29.3 26.1 %collective-permute-start.13 = (bf16[2,4,16,1024]{3,2,1,0:T(8,128)(2,1)S(1)}, bf16[2,4,16,1024]{3,2,1,0:T(8,128)(2,1)S(1)}, u32[]{:S(2)}, u32[]{:S(2)}) collective-permute-start(bf16[2,4,16,1024]{3,2,1,0:T(8,128)(2,1)S(1)} %get-tuple-element.10), channel_id=1, source_target_pairs={{0,4},{1,5},{2,6},{3,7},{4,0},{5,1},{6,2},{7,3},{8,12},{9,13},{10,... | collective-permute-start | bytes 786440 | tf_op jit(solution)/shard_map/ppermute | solution.py:481
  30.0 26.8 %collective-permute-start.1 = (bf16[256,512]{1,0:T(8,128)(2,1)}, bf16[256,512]{1,0:T(8,128)(2,1)S(1)}, u32[]{:S(2)}, u32[]{:S(2)}) collective-permute-start(bf16[256,512]{1,0:T(8,128)(2,1)} %bitcast.3), channel_id=1, source_target_pairs={{0,8},{1,9},{2,10},{3,11},{4,0},{5,1},{6,2},{7,3},{8,12},{9,13},{1... | collective-permute-start | bytes 786440 | tf_op jit(solution)/shard_map/ppermute | solution.py:509
  31.3 27.9 %collective-permute-start.8 = (bf16[4,128,512]{2,1,0:T(8,128)(2,1)S(1)}, bf16[4,128,512]{2,1,0:T(8,128)(2,1)S(1)}, u32[]{:S(2)}, u32[]{:S(2)}) collective-permute-start(bf16[4,128,512]{2,1,0:T(8,128)(2,1)S(1)} %pad_maximum_fusion.1.kv_own), channel_id=1, source_target_pairs={{0,2},{1,3},{2,0},{3,1},{4,6},{5,7},{6,4},{7,5},{8,10},{9,11},{10,... | collective-permute-start | bytes 1572872 | tf_op jit(solution)/shard_map/ppermute | solution.py:481
  55.5 23.2 %collective-permute-start.17 = (bf16[4,2,4,16,1024]{4,3,2,1,0:T(8,128)(2,1)S(1)}, bf16[4,2,4,16,1024]{4,3,2,1,0:T(8,128)(2,1)}, u32[]{:S(2)}, u32[]{:S(2)}) collective-permute-start(bf16[4,2,4,16,1024]{4,3,2,1,0:T(8,128)(2,1)S(1)} %pad_maximum_fusion.w_own), channel_id=1, source_target_pairs={{0,16},{16,0},{1,17},{17,1},{2,18},{18,2},{3,19},{19,3},{4,20},{20... | collective-permute-start | bytes 3145736 | tf_op jit(solution)/shard_map/ppermute | solution.py:481
  56.8 11.7 %collective-permute-start.2 = (bf16[512,512]{1,0:T(8,128)(2,1)S(1)}, bf16[512,512]{1,0:T(8,128)(2,1)S(1)}, u32[]{:S(2)}, u32[]{:S(2)}) collective-permute-start(bf16[512,512]{1,0:T(8,128)(2,1)S(1)} %constant_dynamic-update-slice_fusion), channel_id=1, source_target_pairs={{0,2},{1,3},{2,0},{3,1},{4,6},{5,7},{6,4},{7,5},{8,10},{9,11},{10,... | collective-permute-start | bytes 1572872 | tf_op jit(solution)/shard_map/ppermute | solution.py:481
  56.9 15.1 %collective-permute-start.9 = (bf16[4,128,512]{2,1,0:T(8,128)(2,1)S(1)}, bf16[4,128,512]{2,1,0:T(8,128)(2,1)S(1)}, u32[]{:S(2)}, u32[]{:S(2)}) collective-permute-start(bf16[4,128,512]{2,1,0:T(8,128)(2,1)S(1)} %pad_maximum_fusion.1.kv_own), channel_id=1, source_target_pairs={{0,1},{1,0},{2,3},{3,2},{4,5},{5,4},{6,7},{7,6},{8,9},{9,8},{10,11... | collective-permute-start | bytes 1572872 | tf_op jit(solution)/shard_map/ppermute | solution.py:481
  59.2 22.1 %collective-permute-start.3 = (bf16[512,512]{1,0:T(8,128)(2,1)S(1)}, bf16[512,512]{1,0:T(8,128)(2,1)S(1)}, u32[]{:S(2)}, u32[]{:S(2)}) collective-permute-start(bf16[512,512]{1,0:T(8,128)(2,1)S(1)} %constant_dynamic-update-slice_fusion), channel_id=1, source_target_pairs={{0,1},{1,0},{2,3},{3,2},{4,5},{5,4},{6,7},{7,6},{8,9},{9,8},{10,11... | collective-permute-start | bytes 1572872 | tf_op jit(solution)/shard_map/ppermute | solution.py:481
  59.2 22.9 %collective-permute-start.10 = (bf16[4,128,512]{2,1,0:T(8,128)(2,1)S(1)}, bf16[4,128,512]{2,1,0:T(8,128)(2,1)S(1)}, u32[]{:S(2)}, u32[]{:S(2)}) collective-permute-start(bf16[4,128,512]{2,1,0:T(8,128)(2,1)S(1)} %collective-permute-done.8.kv_y), channel_id=1, source_target_pairs={{0,1},{1,0},{2,3},{3,2},{4,5},{5,4},{6,7},{7,6},{8,9},{9,8},{10,11... | collective-permute-start | bytes 1572872 | tf_op jit(solution)/shard_map/ppermute | solution.py:481
  59.7 0.8 copy-start.6
  68.5 14.4 %collective-permute-start.4 = (bf16[512,512]{1,0:T(8,128)(2,1)S(1)}, bf16[512,512]{1,0:T(8,128)(2,1)S(1)}, u32[]{:S(2)}, u32[]{:S(2)}) collective-permute-start(bf16[512,512]{1,0:T(8,128)(2,1)S(1)} %collective-permute-done.2.page_y), channel_id=1, source_target_pairs={{0,1},{1,0},{2,3},{3,2},{4,5},{5,4},{6,7},{7,6},{8,9},{9,8},{10,11... | collective-permute-start | bytes 1572872 | tf_op jit(solution)/shard_map/ppermute | solution.py:481
  71.2 0.8 copy-start.8
  72.0 0.8 copy-start.10
  72.8 32.5 %collective-permute-start.16 = (bf16[4,2,4,16,1024]{4,3,2,1,0:T(8,128)(2,1)S(1)}, bf16[4,2,4,16,1024]{4,3,2,1,0:T(8,128)(2,1)}, u32[]{:S(2)}, u32[]{:S(2)}) collective-permute-start(bf16[4,2,4,16,1024]{4,3,2,1,0:T(8,128)(2,1)S(1)} %pad_maximum_fusion.w_own), channel_id=1, source_target_pairs={{0,1},{1,0},{2,3},{3,2},{4,5},{5,4},{6,7},{7,6},{8,9},{9,8},{10,11... | collective-permute-start | bytes 3145736 | tf_op jit(solution)/shard_map/ppermute | solution.py:481
  78.7 28.5 %collective-permute-start.18 = (bf16[4,2,4,16,1024]{4,3,2,1,0:T(8,128)(2,1)}, bf16[4,2,4,16,1024]{4,3,2,1,0:T(8,128)(2,1)}, u32[]{:S(2)}, u32[]{:S(2)}) collective-permute-start(bf16[4,2,4,16,1024]{4,3,2,1,0:T(8,128)(2,1)} %collective-permute-done.17.w_x), channel_id=1, source_target_pairs={{0,1},{1,0},{2,3},{3,2},{4,5},{5,4},{6,7},{7,6},{8,9},{9,8},{10,11... | collective-permute-start | bytes 3145736 | tf_op jit(solution)/shard_map/ppermute | solution.py:481
  81.3 0.8 copy-start.12
  82.1 0.9 copy-start.14
  82.9 0.8 copy-start.16
  83.7 1.0 copy-start.7
  84.8 1.0 copy-start.9
  85.8 1.0 copy-start.11
  86.9 1.0 copy-start.13
  87.9 1.0 copy-start.15
  88.9 1.0 copy-start.17
  105.2 2.0 collective-permute-start.11
  113.1 6.3 %copy-start.20 = (s32[128,1,2]{0,2,1:T(2,128)S(1)}, s32[128,1,2]{0,2,1:T(2,128)}, u32[]{:S(2)}) copy-start(s32[128,1,2]{0,2,1:T(2,128)} %param.16) | copy-start | bytes 3076
  113.1 30.2 %copy-start.5 = (f32[2048]{0:T(1024)S(1)}, f32[2048]{0:T(1024)}, u32[]{:S(2)}) copy-start(f32[2048]{0:T(1024)} %param.15) | copy-start | bytes 24580
  113.1 30.2 %all-to-all-start.1 = ((bf16[4,128,2048]{2,1,0:T(8,128)(2,1)}), bf16[4,128,2048]{2,1,0:T(8,128)(2,1)S(1)}, u32[]{:S(2)}, u32[]{:S(2)}) async-start(bf16[4,128,2048]{2,1,0:T(8,128)(2,1)} %bitcast.52), calls=%async_computation.1 | async-start | bytes 4194304 | tf_op jit(solution)/shard_map/all_to_all | solution.py:554
  143.3 1.0 copy-start.4
  145.5 51.9 %copy-start.2 = (f32[128,2048]{1,0:T(8,128)}, f32[128,2048]{1,0:T(8,128)S(1)}, u32[]{:S(2)}) copy-start(f32[128,2048]{1,0:T(8,128)S(1)} %get-tuple-element.8.stream_ref) | copy-start | bytes 3145732
  203.7 1.4 copy-start.1
  205.1 5.3 %copy-start.21 = (f32[128,1,2]{0,2,1:T(2,128)S(1)}, f32[128,1,2]{0,2,1:T(2,128)}, u32[]{:S(2)}) copy-start(f32[128,1,2]{0,2,1:T(2,128)} %param.17) | copy-start | bytes 3076
  205.1 52.7 %all-to-all-start.3 = ((bf16[16,32,2048]{2,1,0:T(8,128)(2,1)}), bf16[16,32,2048]{2,1,0:T(8,128)(2,1)S(1)}, u32[]{:S(2)}, u32[]{:S(2)}) async-start(bf16[16,32,2048]{2,1,0:T(8,128)(2,1)} %bitcast.45), calls=%async_computation.3 | async-start | bytes 4194304 | tf_op jit(solution)/shard_map/all_to_all | solution.py:670
  257.8 1.2 copy-start.3

commit v3 on v2

--- a/solution.py
+++ b/solution.py
@@ -13,8 +13,8 @@
 HIGH_VMEM = 48 * 2**20
 
 
-def anywhere():
-    return pl.BlockSpec(memory_space=pl.ANY)
+def in_hbm():
+    return pl.BlockSpec(memory_space=pltpu.HBM)
 
 
 def in_vmem():
@@ -107,7 +107,7 @@
     return pl.pallas_call(
         functools.partial(attend_kernel, block, chunk, width),
         out_shape=jax.ShapeDtypeStruct((length, width), BF16),
-        in_specs=[anywhere()] * 3,
+        in_specs=[in_hbm()] * 3,
         out_specs=in_vmem(),
         scratch_shapes=[
             pltpu.VMEM((length, width), BF16),
@@ -259,7 +259,7 @@
     return pl.pallas_call(
         functools.partial(attend_pair_kernel, block, chunk, width),
         out_shape=jax.ShapeDtypeStruct((2, length // 2, heads * width), BF16),
-        in_specs=[anywhere()] * (1 + len(pages) + len(kvs)),
+        in_specs=[in_hbm()] * (1 + len(pages) + len(kvs)),
         out_specs=in_vmem(),
         scratch_shapes=[
             pltpu.VMEM((heads, length, width), BF16),
@@ -320,7 +320,7 @@
     return pl.pallas_call(
         project_pair_kernel,
         out_shape=jax.ShapeDtypeStruct((rows, model), BF16),
-        in_specs=[in_vmem(), in_vmem()] + [anywhere()] * 4,
+        in_specs=[in_vmem(), in_vmem()] + [in_hbm()] * 4,
         out_specs=in_vmem(),
         scratch_shapes=[
             pltpu.VMEM((heads, width, model), BF16),
@@ -509,41 +509,47 @@
         lax.ppermute(cache[0], "head", [(d, page_target(d, other)) for d in range(n)])
         for other in range(2)
     )
-    own_pages = jnp.concatenate([page_a, page_b], 0)
-    pages_y = flipped(own_pages, "head", 2)
-    pages_c = flipped(own_pages, "head", 1)
-    pages_cy = flipped(pages_y, "head", 1)
-
     kv_heads = new_kv.reshape(local_rows, pair_heads, 2 * width).transpose(1, 0, 2)
     kv_same = lax.dynamic_index_in_dim(kv_heads, b, 0, keepdims=False)
     kv_other = lax.dynamic_index_in_dim(kv_heads, 1 - b, 0, keepdims=False)
     kv_own = [kv_same]
     for t in range(1, planes):
         kv_own.append(flipped(kv_other if t % 2 else kv_same, "head", t * plane_bit))
-    kv_own = jnp.stack(kv_own, 0)
-    kv_y = flipped(kv_own, "head", 2)
-    kv_c = flipped(kv_own, "head", 1)
-    kv_cy = flipped(kv_y, "head", 1)
 
     columns = model // 2
     w = lax.dynamic_slice_in_dim(w_out, lax.axis_index("grp") * columns, columns, 2)
     w = w.reshape(2, 2, heads // 4, share, columns)
     w_keep = lax.dynamic_index_in_dim(w, y, 1, keepdims=False)
     w_give = lax.dynamic_index_in_dim(w, 1 - y, 1, keepdims=False)
-    w_both = jnp.stack([w_keep, flipped(w_give, "head", 2)], 1)
+    w_got = flipped(w_give, "head", 2)
+
+    (page_a, page_b, kv_own, q), w_got = lax.optimization_barrier(
+        ((page_a, page_b, kv_own, q), w_got)
+    )
+    own_pages = jnp.concatenate([page_a, page_b], 0)
+    kv_own = jnp.stack(kv_own, 0)
+    pages_y = flipped(own_pages, "head", 2)
+    kv_y = flipped(kv_own, "head", 2)
+    w_both = jnp.stack([w_keep, w_got], 1)
     w_same = lax.dynamic_index_in_dim(w_both, b, 0, keepdims=False)
     w_other = lax.dynamic_index_in_dim(w_both, 1 - b, 0, keepdims=False)
     w_own = [w_same]
     for t in range(1, planes):
         w_own.append(flipped(w_other if t % 2 else w_same, "head", t * plane_bit))
+    pages_c = flipped(own_pages, "head", 1)
+    kv_c = flipped(kv_own, "head", 1)
+    (pages_y, kv_y), w_own = lax.optimization_barrier(((pages_y, kv_y), w_own))
+    pages_cy = flipped(pages_y, "head", 1)
+    kv_cy = flipped(kv_y, "head", 1)
     w_own = jnp.stack(w_own, 0)
+    q, w_own = lax.optimization_barrier((q, w_own))
     w_x = flipped(w_own, "grp", 1)
     w_c = flipped(w_own, "head", 1)
-    w_cx = flipped(w_x, "head", 1)
-
     a = attend_pair(
         q, (page_a, page_b, pages_y, pages_c, pages_cy), (kv_own, kv_y, kv_c, kv_cy)
     )
+    a, w_x, w_c = lax.optimization_barrier((a, w_x, w_c))
+    w_cx = flipped(w_x, "head", 1)
     got = flipped(a[1], "head", 1)
     partial = project_pair(a, got, w_own, w_c, w_x, w_cx)
     quads = [

time: 261 us -> 247 us (0.946)
  starting transfers between devices: 45.7 us -> 30.4 us
  waiting for transfers between devices: 113 us -> 124 us
  local copies, waits for them, and re-layouts: 18.7 us -> 8.28 us
    unnamed x49 -> x27, local copies, waits for them, and re-layouts: 16.3 us -> 4.57 us
    ppermute x17, starting transfers between devices: 23.8 us -> 12.4 us  [flipped(): return lax.ppermute(value, axis, pairs)]
    ppermute x17, waiting for transfers between devices: 43 us -> 53.3 us  [flipped(): return lax.ppermute(value, axis, pairs)]
    all_to_all x1, starting transfers between devices: 6.32 us -> 3.64 us  [parts_in_pairs(): lax.all_to_all(partial.reshape(members // 2, local_rows, model), 'head',...]
  transfers between devices with their start and end apart: 22 -> 22, of which waited for: 9 -> 11; matrix products, arithmetic and copies ran while one was open for 1% -> 1% of each run, Pallas kernels for 6% -> 6%
where the time goes in v3:
time: 247 us
  waiting for transfers between devices  124 us (50%)
  blocking collectives  53.8 us (22%)
  starting transfers between devices  30.4 us (12%)
  Pallas kernels  28.8 us (12%)
  local copies, waits for them, and re-layouts  8.28 us (3%)
    all_to_all x1, blocking collectives, local(): lax.all_to_all(outgoing.reshape(n, slots // n, model), 'head', split_axis...  53.8 us
    ppermute x17, waiting for transfers between devices, flipped(): return lax.ppermute(value, axis, pairs)  53.3 us
    all_to_all x1, waiting for transfers between devices, local(): lax.all_to_all(answered, 'head', split_axis=0, concat_axis=0, tiled=True)  47.3 us
    all_to_all x1, waiting for transfers between devices, parts_in_pairs(): lax.all_to_all(partial.reshape(members // 2, local_rows, model), 'head',...  23 us
    pallas_call x1, Pallas kernels, attend_pair(): pl.pallas_call(functools.partial(attend_pair_kernel, block, chunk, width)...  15.2 us
    ppermute x17, starting transfers between devices, flipped(): return lax.ppermute(value, axis, pairs)  12.4 us
    pallas_call x1, Pallas kernels, expert(): pl.pallas_call(expert_kernel, out_shape=jax.ShapeDtypeStruct((rows, model...  6.34 us
    all_to_all x1, starting transfers between devices, local(): lax.all_to_all(answered, 'head', split_axis=0, concat_axis=0, tiled=True)  5.25 us
  transfers between devices with their start and end apart: 22, of which 11 were waited for; matrix products, arithmetic and copies ran while one was open for 1% of the time, Pallas kernels for 6%

profile of v3, /device:TPU:13, one launch (start us, length us, event | category | flops | bytes accessed | tf_op | source)
XLA Modules:
  0.0 246.9 jit_solution(9548122113821266726)
XLA Ops:
  0.0 2.6 %copy.23 = bf16[16,128,256]{2,1,0:T(8,128)(2,1)} copy(bf16[16,128,256]{2,0,1:T(8,128)(2,1)} %bitcast.55) | data formatting | bytes 2097152 | tf_op jit(solution)/shard_map/transpose | solution.py:498
  2.6 4.6 %all-to-all-start = ((bf16[8,2,128,256]{3,2,1,0:T(8,128)(2,1)}), bf16[8,2,128,256]{3,2,1,0:T(8,128)(2,1)S(1)}, u32[]{:S(2)}, u32[]{:S(2)}) async-start(bf16[8,2,128,256]{3,2,1,0:T(8,128)(2,1)} %bitcast.5), calls=%async_computation | async-start | bytes 2097152 | tf_op jit(solution)/shard_map/all_to_all | solution.py:500
  7.4 0.3 collective-permute-start.5
  7.7 0.5 constant_dynamic-slice_fusion.2
  8.3 0.1 collective-permute-start.2
  8.5 4.4 %collective-permute-start = (bf16[256,512]{1,0:T(8,128)(2,1)}, bf16[256,512]{1,0:T(8,128)(2,1)S(1)}, u32[]{:S(2)}, u32[]{:S(2)}) collective-permute-start(bf16[256,512]{1,0:T(8,128)(2,1)} %bitcast.69), channel_id=1, source_target_pairs={{0,0},{1,1},{2,2},{3,3},{4,8},{5,9},{6,10},{7,11},{8,4},{9,5},{10,... | collective-permute-start | bytes 786440 | tf_op jit(solution)/shard_map/ppermute | solution.py:509
  13.0 2.4 collective-permute-start.3
  15.4 9.0 %collective-permute-done.2 = bf16[128,512]{1,0:T(8,128)(2,1)} collective-permute-done((bf16[128,512]{1,0:T(8,128)(2,1)S(1)}, bf16[128,512]{1,0:T(8,128)(2,1)}, u32[]{:S(2)}, u32[]{:S(2)}) %collective-permute-start.2) | collective-permute-done | bytes 131104 | tf_op jit(solution)/shard_map/ppermute | solution.py:481
  24.4 1.4 collective-permute-start.4
  25.8 7.4 %collective-permute-done.3 = bf16[128,512]{1,0:T(8,128)(2,1)} collective-permute-done((bf16[128,512]{1,0:T(8,128)(2,1)S(1)}, bf16[128,512]{1,0:T(8,128)(2,1)}, u32[]{:S(2)}, u32[]{:S(2)}) %collective-permute-start.3) | collective-permute-done | bytes 131104 | tf_op jit(solution)/shard_map/ppermute | solution.py:481
  33.2 5.8 %collective-permute-done.4 = bf16[128,512]{1,0:T(8,128)(2,1)S(1)} collective-permute-done((bf16[128,512]{1,0:T(8,128)(2,1)S(1)}, bf16[128,512]{1,0:T(8,128)(2,1)S(1)}, u32[]{:S(2)}, u32[]{:S(2)}) %collective-permute-start.4) | collective-permute-done | bytes 131104 | tf_op jit(solution)/shard_map/ppermute | solution.py:481
  39.0 0.6 copy-done.8
  39.8 0.1 collective-permute-start.10
  39.8 1.3 pad_maximum_fusion.1.kv_own
  41.2 0.3 collective-permute-start.7
  41.6 1.2 collective-permute-start.6
  42.8 1.1 collective-permute-start.13
  43.9 8.4 %collective-permute-done.10 = bf16[2,4,16,1024]{3,2,1,0:T(8,128)(2,1)S(1)} collective-permute-done((bf16[2,4,16,1024]{3,2,1,0:T(8,128)(2,1)S(1)}, bf16[2,4,16,1024]{3,2,1,0:T(8,128)(2,1)S(1)}, u32[]{:S(2)}, u32[]{:S(2)}) %collective-permute-start.10) | collective-permute-done | bytes 262176 | tf_op jit(solution)/shard_map/ppermute | solution.py:481
  52.3 0.5 collective-permute-start.11
  52.8 11.0 %collective-permute-done.9 = bf16[2,4,16,1024]{3,2,1,0:T(8,128)(2,1)S(1)} collective-permute-done((bf16[2,4,16,1024]{3,2,1,0:T(8,128)(2,1)S(1)}, bf16[2,4,16,1024]{3,2,1,0:T(8,128)(2,1)S(1)}, u32[]{:S(2)}, u32[]{:S(2)}) %collective-permute-start.9) | collective-permute-done | bytes 262176 | tf_op jit(solution)/shard_map/ppermute | solution.py:481
  63.8 1.7 collective-permute-done.6.page_y
  65.5 1.3 collective-permute-start.12
  66.8 0.1 pad_maximum_fusion.w_own
  67.0 1.3 collective-permute-start.15
  68.3 0.8 collective-permute-start.16
  69.0 0.1 collective-permute-done.14.kv_cy
  69.1 15.2 %attend.1.a_ref = bf16[2,512,512]{2,1,0:T(8,128)(2,1)S(1)} custom-call(bf16[8,2,128,256]{3,2,1,0:T(8,128)(2,1)} %copy-done.7, bf16[256,512]{1,0:T(8,128)(2,1)S(1)} %collective-permute-done.page_a, bf16[256,512]{1,0:T(8,128)(2,1)S(1)} %collective-permute-done.1.page_b, bf16[512,512]{1,0:T(8,128)(2,1)S(1)} %collective-permute-done.6.page_y, ...), custom_call_target="tpu_custom_call" | custom-call | flops 7516192768 | bytes 6291456 | tf_op jit(solution)/shard_map/attend/pallas_call | solution.py:259
  84.3 6.9 %collective-permute-done.15.w_x = bf16[4,2,4,16,1024]{4,3,2,1,0:T(8,128)(2,1)S(1)} collective-permute-done((bf16[4,2,4,16,1024]{4,3,2,1,0:T(8,128)(2,1)S(1)}, bf16[4,2,4,16,1024]{4,3,2,1,0:T(8,128)(2,1)S(1)}, u32[]{:S(2)}, u32[]{:S(2)}) %collective-permute-start.15) | collective-permute-done | bytes 1048608 | tf_op jit(solution)/shard_map/ppermute | solution.py:481
  91.3 1.4 collective-permute-start.18
  92.7 0.1 collective-permute-start.17
  92.7 2.9 %collective-permute-done.17.got_ref = bf16[512,512]{1,0:T(8,128)(2,1)S(1)} collective-permute-done((bf16[512,512]{1,0:T(8,128)(2,1)S(1)}, bf16[512,512]{1,0:T(8,128)(2,1)S(1)}, u32[]{:S(2)}, u32[]{:S(2)}) %collective-permute-start.17) | collective-permute-done | bytes 524320 | tf_op jit(solution)/shard_map/ppermute | solution.py:481
  95.7 4.5 %project.1 = bf16[512,2048]{1,0:T(8,128)(2,1)} custom-call(bf16[2,512,512]{2,1,0:T(8,128)(2,1)S(1)} %attend.1.a_ref, bf16[512,512]{1,0:T(8,128)(2,1)S(1)} %collective-permute-done.17.got_ref, bf16[4,2,4,16,1024]{4,3,2,1,0:T(8,128)(2,1)S(1)} %pad_maximum_fusion.w_own, bf16[4,2,4,16,1024]{4,3,2,1,0:T(8,128)(2,1)S(1)} %collective-permute-done.16.w_c, ...), custom_call_target="tpu_custom_call" | custom-call | flops 2147483648 | bytes 7340032 | tf_op jit(solution)/shard_map/project/pallas_call | solution.py:320
  100.2 3.6 %all-to-all-start.1 = ((bf16[4,128,2048]{2,1,0:T(8,128)(2,1)}), bf16[4,128,2048]{2,1,0:T(8,128)(2,1)S(1)}, u32[]{:S(2)}, u32[]{:S(2)}) async-start(bf16[4,128,2048]{2,1,0:T(8,128)(2,1)} %bitcast.53), calls=%async_computation.1 | async-start | bytes 4194304 | tf_op jit(solution)/shard_map/all_to_all | solution.py:560
  103.8 0.1 copy.24
  104.0 0.1 copy.26
  104.1 0.2 reduce_window_sum.11
  104.4 0.1 copy.29
  104.6 23.0 %all-to-all-done.1 = bf16[4,128,2048]{2,1,0:T(8,128)(2,1)S(1)} async-done(((bf16[4,128,2048]{2,1,0:T(8,128)(2,1)}), bf16[4,128,2048]{2,1,0:T(8,128)(2,1)S(1)}, u32[]{:S(2)}, u32[]{:S(2)}) %all-to-all-start.1) | async-done | bytes 2097184 | tf_op jit(solution)/shard_map/all_to_all | solution.py:560
  127.7 1.0 copy-done.4
  128.7 1.2 route.1
  129.9 53.8 %all_to_all.20 = bf16[16,32,2048]{2,1,0:T(8,128)(2,1)S(1)} all-to-all(bf16[16,32,2048]{2,1,0:T(8,128)(2,1)S(1)} %bitcast.47), channel_id=1, replica_groups=mesh['grp'=2,'head'=16] {'head'}, dimensions={0} | all-to-all | bytes 4194304 | tf_op jit(solution)/shard_map/all_to_all | solution.py:663
  183.7 6.3 %expert.1 = bf16[512,2048]{1,0:T(8,128)(2,1)S(1)} custom-call(bf16[512,2048]{1,0:T(8,128)(2,1)S(1)} %bitcast.48, bf16[2048,1024]{1,0:T(8,128)(2,1)} %bitcast.67, bf16[512,2048]{1,0:T(8,128)(2,1)} %bitcast.68), custom_call_target="tpu_custom_call" | custom-call | flops 3221225472 | bytes 10485760 | tf_op jit(solution)/shard_map/expert/pallas_call | solution.py:428
  190.1 1.3 copy-done.1
  191.4 5.3 %all-to-all-start.3 = ((bf16[16,32,2048]{2,1,0:T(8,128)(2,1)}), bf16[16,32,2048]{2,1,0:T(8,128)(2,1)S(1)}, u32[]{:S(2)}, u32[]{:S(2)}) async-start(bf16[16,32,2048]{2,1,0:T(8,128)(2,1)} %bitcast.46), calls=%async_computation.3 | async-start | bytes 4194304 | tf_op jit(solution)/shard_map/all_to_all | solution.py:676
  196.7 0.1 copy.31
  196.8 47.3 %all-to-all-done.3 = bf16[16,32,2048]{2,1,0:T(8,128)(2,1)S(1)} async-done(((bf16[16,32,2048]{2,1,0:T(8,128)(2,1)}), bf16[16,32,2048]{2,1,0:T(8,128)(2,1)S(1)}, u32[]{:S(2)}, u32[]{:S(2)}) %all-to-all-start.3) | async-done | bytes 2097184 | tf_op jit(solution)/shard_map/all_to_all | solution.py:676
  244.1 1.2 copy-done.3
  245.3 1.6 combine.1
  (48 shorter events, 0.6 us)
Async XLA Ops:
  0.0 7.3 %copy-start = (bf16[16,16,2048]{2,1,0:T(8,128)(2,1)S(1)}, bf16[16,16,2048]{2,1,0:T(8,128)(2,1)}, u32[]{:S(2)}) copy-start(bf16[16,16,2048]{2,1,0:T(8,128)(2,1)} %param.14) | copy-start | bytes 3145732
  2.6 5.1 %copy-start.6 = (bf16[128,1,2,512]{3,2,1,0:T(2,128)(2,1)S(1)}, bf16[128,1,2,512]{3,2,1,0:T(2,128)(2,1)}, u32[]{:S(2)}) copy-start(bf16[128,1,2,512]{3,2,1,0:T(2,128)(2,1)} %param.11) | copy-start | bytes 786436
  2.6 37.1 %all-to-all-start = ((bf16[8,2,128,256]{3,2,1,0:T(8,128)(2,1)}), bf16[8,2,128,256]{3,2,1,0:T(8,128)(2,1)S(1)}, u32[]{:S(2)}, u32[]{:S(2)}) async-start(bf16[8,2,128,256]{3,2,1,0:T(8,128)(2,1)} %bitcast.5), calls=%async_computation | async-start | bytes 2097152 | tf_op jit(solution)/shard_map/all_to_all | solution.py:500
  7.4 31.7 %collective-permute-start.5 = (bf16[2,4,16,1024]{3,2,1,0:T(8,128)(2,1)S(1)}, bf16[2,4,16,1024]{3,2,1,0:T(8,128)(2,1)S(1)}, u32[]{:S(2)}, u32[]{:S(2)}) collective-permute-start(bf16[2,4,16,1024]{3,2,1,0:T(8,128)(2,1)S(1)} %get-tuple-element.50), channel_id=1, source_target_pairs={{0,2},{1,3},{2,0},{3,1},{4,6},{5,7},{6,4},{7,5},{8,10},{9,11},{10,... | collective-permute-start | bytes 786440 | tf_op jit(solution)/shard_map/ppermute | solution.py:481
  8.3 16.1 %collective-permute-start.2 = (bf16[128,512]{1,0:T(8,128)(2,1)S(1)}, bf16[128,512]{1,0:T(8,128)(2,1)}, u32[]{:S(2)}, u32[]{:S(2)}) collective-permute-start(bf16[128,512]{1,0:T(8,128)(2,1)S(1)} %bitcast.64), channel_id=1, source_target_pairs={{0,4},{1,5},{2,6},{3,7},{4,0},{5,1},{6,2},{7,3},{8,12},{9,13},{10,... | collective-permute-start | bytes 393224 | tf_op jit(solution)/shard_map/ppermute | solution.py:481
  8.5 30.6 %collective-permute-start = (bf16[256,512]{1,0:T(8,128)(2,1)}, bf16[256,512]{1,0:T(8,128)(2,1)S(1)}, u32[]{:S(2)}, u32[]{:S(2)}) collective-permute-start(bf16[256,512]{1,0:T(8,128)(2,1)} %bitcast.69), channel_id=1, source_target_pairs={{0,0},{1,1},{2,2},{3,3},{4,8},{5,9},{6,10},{7,11},{8,4},{9,5},{10,... | collective-permute-start | bytes 786440 | tf_op jit(solution)/shard_map/ppermute | solution.py:509
  12.9 26.8 %collective-permute-start.1 = (bf16[256,512]{1,0:T(8,128)(2,1)}, bf16[256,512]{1,0:T(8,128)(2,1)S(1)}, u32[]{:S(2)}, u32[]{:S(2)}) collective-permute-start(bf16[256,512]{1,0:T(8,128)(2,1)} %bitcast.70), channel_id=1, source_target_pairs={{0,8},{1,9},{2,10},{3,11},{4,0},{5,1},{6,2},{7,3},{8,12},{9,13},{1... | collective-permute-start | bytes 786440 | tf_op jit(solution)/shard_map/ppermute | solution.py:509
  13.0 20.2 %collective-permute-start.3 = (bf16[128,512]{1,0:T(8,128)(2,1)S(1)}, bf16[128,512]{1,0:T(8,128)(2,1)}, u32[]{:S(2)}, u32[]{:S(2)}) collective-permute-start(bf16[128,512]{1,0:T(8,128)(2,1)S(1)} %bitcast.58), channel_id=1, source_target_pairs={{0,8},{1,9},{2,10},{3,11},{4,12},{5,13},{6,14},{7,15},{8,0},{9,1},... | collective-permute-start | bytes 393224 | tf_op jit(solution)/shard_map/ppermute | solution.py:481
  24.4 14.7 %collective-permute-start.4 = (bf16[128,512]{1,0:T(8,128)(2,1)S(1)}, bf16[128,512]{1,0:T(8,128)(2,1)S(1)}, u32[]{:S(2)}, u32[]{:S(2)}) collective-permute-start(bf16[128,512]{1,0:T(8,128)(2,1)S(1)} %bitcast.65), channel_id=1, source_target_pairs={{0,12},{1,13},{2,14},{3,15},{4,8},{5,9},{6,10},{7,11},{8,4},{9,5},... | collective-permute-start | bytes 393224 | tf_op jit(solution)/shard_map/ppermute | solution.py:481
  39.0 0.7 copy-start.8
  39.7 27.3 %copy-start.7 = (bf16[8,2,128,256]{3,2,1,0:T(8,128)(2,1)}, bf16[8,2,128,256]{3,2,1,0:T(8,128)(2,1)S(1)}, u32[]{:S(2)}) copy-start(bf16[8,2,128,256]{3,2,1,0:T(8,128)(2,1)S(1)} %all-to-all-done.q_hbm) | copy-start | bytes 3145732
  39.8 12.6 %collective-permute-start.10 = (bf16[2,4,16,1024]{3,2,1,0:T(8,128)(2,1)S(1)}, bf16[2,4,16,1024]{3,2,1,0:T(8,128)(2,1)S(1)}, u32[]{:S(2)}, u32[]{:S(2)}) collective-permute-start(bf16[2,4,16,1024]{3,2,1,0:T(8,128)(2,1)S(1)} %get-tuple-element.47), channel_id=1, source_target_pairs={{0,12},{1,13},{2,14},{3,15},{4,8},{5,9},{6,10},{7,11},{8,4},{9,5},... | collective-permute-start | bytes 786440 | tf_op jit(solution)/shard_map/ppermute | solution.py:481
  41.2 22.6 %collective-permute-start.7 = (bf16[4,128,512]{2,1,0:T(8,128)(2,1)S(1)}, bf16[4,128,512]{2,1,0:T(8,128)(2,1)S(1)}, u32[]{:S(2)}, u32[]{:S(2)}) collective-permute-start(bf16[4,128,512]{2,1,0:T(8,128)(2,1)S(1)} %pad_maximum_fusion.1.kv_own), channel_id=1, source_target_pairs={{0,2},{1,3},{2,0},{3,1},{4,6},{5,7},{6,4},{7,5},{8,10},{9,11},{10,... | collective-permute-start | bytes 1572872 | tf_op jit(solution)/shard_map/ppermute | solution.py:481
  41.6 23.9 %collective-permute-start.6 = (bf16[512,512]{1,0:T(8,128)(2,1)S(1)}, bf16[512,512]{1,0:T(8,128)(2,1)S(1)}, u32[]{:S(2)}, u32[]{:S(2)}) collective-permute-start(bf16[512,512]{1,0:T(8,128)(2,1)S(1)} %constant_dynamic-update-slice_fusion), channel_id=1, source_target_pairs={{0,2},{1,3},{2,0},{3,1},{4,6},{5,7},{6,4},{7,5},{8,10},{9,11},{10,... | collective-permute-start | bytes 1572872 | tf_op jit(solution)/shard_map/ppermute | solution.py:481
  42.8 25.4 %collective-permute-start.13 = (bf16[4,128,512]{2,1,0:T(8,128)(2,1)S(1)}, bf16[4,128,512]{2,1,0:T(8,128)(2,1)S(1)}, u32[]{:S(2)}, u32[]{:S(2)}) collective-permute-start(bf16[4,128,512]{2,1,0:T(8,128)(2,1)S(1)} %pad_maximum_fusion.1.kv_own), channel_id=1, source_target_pairs={{0,1},{1,0},{2,3},{3,2},{4,5},{5,4},{6,7},{7,6},{8,9},{9,8},{10,11... | collective-permute-start | bytes 1572872 | tf_op jit(solution)/shard_map/ppermute | solution.py:481
  43.9 8.5 %collective-permute-start.8 = (bf16[2,4,16,1024]{3,2,1,0:T(8,128)(2,1)S(1)}, bf16[2,4,16,1024]{3,2,1,0:T(8,128)(2,1)S(1)}, u32[]{:S(2)}, u32[]{:S(2)}) collective-permute-start(bf16[2,4,16,1024]{3,2,1,0:T(8,128)(2,1)S(1)} %get-tuple-element.47), channel_id=1, source_target_pairs={{0,4},{1,5},{2,6},{3,7},{4,0},{5,1},{6,2},{7,3},{8,12},{9,13},{10,... | collective-permute-start | bytes 786440 | tf_op jit(solution)/shard_map/ppermute | solution.py:481
  52.3 11.5 %collective-permute-start.9 = (bf16[2,4,16,1024]{3,2,1,0:T(8,128)(2,1)S(1)}, bf16[2,4,16,1024]{3,2,1,0:T(8,128)(2,1)S(1)}, u32[]{:S(2)}, u32[]{:S(2)}) collective-permute-start(bf16[2,4,16,1024]{3,2,1,0:T(8,128)(2,1)S(1)} %get-tuple-element.34), channel_id=1, source_target_pairs={{0,8},{1,9},{2,10},{3,11},{4,12},{5,13},{6,14},{7,15},{8,0},{9,1},... | collective-permute-start | bytes 786440 | tf_op jit(solution)/shard_map/ppermute | solution.py:481
  52.3 16.7 %collective-permute-start.11 = (bf16[512,512]{1,0:T(8,128)(2,1)S(1)}, bf16[512,512]{1,0:T(8,128)(2,1)S(1)}, u32[]{:S(2)}, u32[]{:S(2)}) collective-permute-start(bf16[512,512]{1,0:T(8,128)(2,1)S(1)} %constant_dynamic-update-slice_fusion), channel_id=1, source_target_pairs={{0,1},{1,0},{2,3},{3,2},{4,5},{5,4},{6,7},{7,6},{8,9},{9,8},{10,11... | collective-permute-start | bytes 1572872 | tf_op jit(solution)/shard_map/ppermute | solution.py:481
  65.5 3.6 %collective-permute-start.12 = (bf16[512,512]{1,0:T(8,128)(2,1)S(1)}, bf16[512,512]{1,0:T(8,128)(2,1)S(1)}, u32[]{:S(2)}, u32[]{:S(2)}) collective-permute-start(bf16[512,512]{1,0:T(8,128)(2,1)S(1)} %collective-permute-done.6.page_y), channel_id=1, source_target_pairs={{0,1},{1,0},{2,3},{3,2},{4,5},{5,4},{6,7},{7,6},{8,9},{9,8},{10,11... | collective-permute-start | bytes 1572872 | tf_op jit(solution)/shard_map/ppermute | solution.py:481
  66.8 2.3 collective-permute-start.14
  67.0 24.3 %collective-permute-start.15 = (bf16[4,2,4,16,1024]{4,3,2,1,0:T(8,128)(2,1)S(1)}, bf16[4,2,4,16,1024]{4,3,2,1,0:T(8,128)(2,1)S(1)}, u32[]{:S(2)}, u32[]{:S(2)}) collective-permute-start(bf16[4,2,4,16,1024]{4,3,2,1,0:T(8,128)(2,1)S(1)} %pad_maximum_fusion.w_own), channel_id=1, source_target_pairs={{0,16},{16,0},{1,17},{17,1},{2,18},{18,2},{3,19},{19,3},{4,20},{20... | collective-permute-start | bytes 3145736 | tf_op jit(solution)/shard_map/ppermute | solution.py:481
  68.3 23.0 %collective-permute-start.16 = (bf16[4,2,4,16,1024]{4,3,2,1,0:T(8,128)(2,1)S(1)}, bf16[4,2,4,16,1024]{4,3,2,1,0:T(8,128)(2,1)S(1)}, u32[]{:S(2)}, u32[]{:S(2)}) collective-permute-start(bf16[4,2,4,16,1024]{4,3,2,1,0:T(8,128)(2,1)S(1)} %pad_maximum_fusion.w_own), channel_id=1, source_target_pairs={{0,1},{1,0},{2,3},{3,2},{4,5},{5,4},{6,7},{7,6},{8,9},{9,8},{10,11... | collective-permute-start | bytes 3145736 | tf_op jit(solution)/shard_map/ppermute | solution.py:481
  91.3 4.4 %collective-permute-start.18 = (bf16[4,2,4,16,1024]{4,3,2,1,0:T(8,128)(2,1)S(1)}, bf16[4,2,4,16,1024]{4,3,2,1,0:T(8,128)(2,1)S(1)}, u32[]{:S(2)}, u32[]{:S(2)}) collective-permute-start(bf16[4,2,4,16,1024]{4,3,2,1,0:T(8,128)(2,1)S(1)} %collective-permute-done.15.w_x), channel_id=1, source_target_pairs={{0,1},{1,0},{2,3},{3,2},{4,5},{5,4},{6,7},{7,6},{8,9},{9,8},{10,11... | collective-permute-start | bytes 3145736 | tf_op jit(solution)/shard_map/ppermute | solution.py:481
  92.7 3.0 %collective-permute-start.17 = (bf16[512,512]{1,0:T(8,128)(2,1)S(1)}, bf16[512,512]{1,0:T(8,128)(2,1)S(1)}, u32[]{:S(2)}, u32[]{:S(2)}) collective-permute-start(bf16[512,512]{1,0:T(8,128)(2,1)S(1)} %slice_bitcast_fusion), channel_id=1, source_target_pairs={{0,1},{1,0},{2,3},{3,2},{4,5},{5,4},{6,7},{7,6},{8,9},{9,8},{10,11... | collective-permute-start | bytes 1572872 | tf_op jit(solution)/shard_map/ppermute | solution.py:481
  100.2 3.7 %copy-start.9 = (s32[128,1,2]{0,2,1:T(2,128)S(1)}, s32[128,1,2]{0,2,1:T(2,128)}, u32[]{:S(2)}) copy-start(s32[128,1,2]{0,2,1:T(2,128)} %param.16) | copy-start | bytes 3076
  100.2 27.5 %copy-start.5 = (f32[2048]{0:T(1024)S(1)}, f32[2048]{0:T(1024)}, u32[]{:S(2)}) copy-start(f32[2048]{0:T(1024)} %param.15) | copy-start | bytes 24580
  100.2 27.5 %all-to-all-start.1 = ((bf16[4,128,2048]{2,1,0:T(8,128)(2,1)}), bf16[4,128,2048]{2,1,0:T(8,128)(2,1)S(1)}, u32[]{:S(2)}, u32[]{:S(2)}) async-start(bf16[4,128,2048]{2,1,0:T(8,128)(2,1)} %bitcast.53), calls=%async_computation.1 | async-start | bytes 4194304 | tf_op jit(solution)/shard_map/all_to_all | solution.py:560
  127.7 1.0 copy-start.4
  129.9 53.8 %copy-start.2 = (f32[128,2048]{1,0:T(8,128)}, f32[128,2048]{1,0:T(8,128)S(1)}, u32[]{:S(2)}) copy-start(f32[128,2048]{1,0:T(8,128)S(1)} %get-tuple-element.46.stream_ref) | copy-start | bytes 3145732
  190.1 1.3 copy-start.1
  191.4 5.3 %copy-start.10 = (f32[128,1,2]{0,2,1:T(2,128)S(1)}, f32[128,1,2]{0,2,1:T(2,128)}, u32[]{:S(2)}) copy-start(f32[128,1,2]{0,2,1:T(2,128)} %param.17) | copy-start | bytes 3076
  191.4 52.7 %all-to-all-start.3 = ((bf16[16,32,2048]{2,1,0:T(8,128)(2,1)}), bf16[16,32,2048]{2,1,0:T(8,128)(2,1)S(1)}, u32[]{:S(2)}, u32[]{:S(2)}) async-start(bf16[16,32,2048]{2,1,0:T(8,128)(2,1)} %bitcast.46), calls=%async_computation.3 | async-start | bytes 4194304 | tf_op jit(solution)/shard_map/all_to_all | solution.py:676
  244.1 1.2 copy-start.3

commit v4 on v3

--- a/solution.py
+++ b/solution.py
@@ -279,26 +279,28 @@
     )(q, *pages, *kvs)
 
 
-def project_pair_kernel(a_ref, got_ref, w_own, w_c, w_x, w_cx, o_ref, w_ref, sems):
+def project_pair_kernel(a_ref, got_ref, *refs):
+    near, far, (o_ref, w_ref, sems) = refs[:4], refs[4:8], refs[8:]
     me = lax.axis_index("head")
     half = lax.axis_index("grp")
     core = lax.rem(me, 2)
-    planes, sides, heads, share, columns = w_own.shape
+    steps, sides, heads, share, columns = near[0].shape
     width = w_ref.shape[1]
     copies = []
-    for flip, x, pieces_of in ((0, 0, w_own), (1, 0, w_c), (0, 1, w_x), (1, 1, w_cx)):
-        column = pl.multiple_of(jnp.bitwise_xor(half, x) * columns, columns)
-        for t in range(planes):
-            for u in range(sides):
-                number = jnp.bitwise_xor(me, flip ^ (2 * u) ^ (4 * t))
-                row = pl.multiple_of(number * share, share)
-                copy = pltpu.make_async_copy(
-                    pieces_of.at[t, u],
-                    w_ref.at[:, pl.ds(row, share), pl.ds(column, columns)],
-                    sems.at[0],
-                )
-                copy.start()
-                copies.append(copy)
+    for first, given in ((0, near), (steps, far)):
+        for flip, x, pieces_of in zip((0, 1, 0, 1), (0, 0, 1, 1), given):
+            column = pl.multiple_of(jnp.bitwise_xor(half, x) * columns, columns)
+            for t in range(steps):
+                for u in range(sides):
+                    number = jnp.bitwise_xor(me, flip ^ (2 * u) ^ (4 * (first + t)))
+                    row = pl.multiple_of(number * share, share)
+                    copy = pltpu.make_async_copy(
+                        pieces_of.at[t, u],
+                        w_ref.at[:, pl.ds(row, share), pl.ds(column, columns)],
+                        sems.at[0],
+                    )
+                    copy.start()
+                    copies.append(copy)
     for copy in copies:
         copy.wait()
     acc = None
@@ -312,15 +314,15 @@
     o_ref[...] = acc.astype(BF16)
 
 
-def project_pair(a, got, w_own, w_c, w_x, w_cx):
-    planes, sides, heads, share, columns = w_own.shape
+def project_pair(a, got, near, far):
+    _, _, heads, share, columns = near[0].shape
     rows = got.shape[0]
     width = 2 * got.shape[1] // heads
     model = 2 * columns
     return pl.pallas_call(
         project_pair_kernel,
         out_shape=jax.ShapeDtypeStruct((rows, model), BF16),
-        in_specs=[in_vmem(), in_vmem()] + [in_hbm()] * 4,
+        in_specs=[in_vmem(), in_vmem()] + [in_hbm()] * 8,
         out_specs=in_vmem(),
         scratch_shapes=[
             pltpu.VMEM((heads, width, model), BF16),
@@ -333,7 +335,7 @@
             transcendentals=0,
         ),
         name="project",
-    )(a, got, w_own, w_c, w_x, w_cx)
+    )(a, got, *near, *far)
 
 
 def project_kernel(a_ref, w_ref, o_ref):
@@ -476,6 +478,104 @@
     )(back, stream, slots_of, gates)
 
 
+def slot_matrix(slots_ref, slots, rows):
+    place = lax.broadcasted_iota(jnp.int32, (slots, rows), 0).astype(F32)
+    hit = place == slots_ref[0:1, :]
+    for k in range(1, slots_ref.shape[0]):
+        hit = hit | (place == slots_ref[k : k + 1, :])
+    return hit.astype(BF16)
+
+
+def route_pair_kernel(parts_ref, resid_ref, gain_ref, slots_ref, stream_ref, normed_ref, out_ref):
+    projected = parts_ref[0].astype(F32)
+    for p in range(1, parts_ref.shape[0]):
+        projected = projected + parts_ref[p].astype(F32)
+    stream = resid_ref[...].astype(F32) + projected
+    stream_ref[...] = stream
+    normed = stream * lax.rsqrt(jnp.mean(stream * stream, 1, keepdims=True) + eps_norm)
+    normed = (normed * gain_ref[...]).astype(BF16)
+    normed_ref[...] = normed
+    matrix = slot_matrix(slots_ref, out_ref.shape[0], stream.shape[0])
+    out_ref[...] = jnp.dot(matrix, normed, preferred_element_type=F32).astype(BF16)
+
+
+def route_pair(parts, resid, gain, slots_of, slots):
+    planes, rows, model = parts.shape
+    return pl.pallas_call(
+        route_pair_kernel,
+        out_shape=(
+            jax.ShapeDtypeStruct((rows, model), F32),
+            jax.ShapeDtypeStruct((rows, model), BF16),
+            jax.ShapeDtypeStruct((slots, model), BF16),
+        ),
+        in_specs=[in_vmem()] * 4,
+        out_specs=(in_vmem(), in_vmem(), in_vmem()),
+        compiler_params=pltpu.CompilerParams(vmem_limit_bytes=HIGH_VMEM),
+        cost_estimate=pl.CostEstimate(
+            flops=2 * slots * rows * model,
+            bytes_accessed=2 * ((planes + 4) * rows + slots) * model,
+            transcendentals=0,
+        ),
+        name="route",
+    )(parts, resid, gain, slots_of)
+
+
+def spread_kernel(rows_ref, slots_ref, out_ref):
+    matrix = slot_matrix(slots_ref, out_ref.shape[0], rows_ref.shape[0])
+    out_ref[...] = jnp.dot(matrix, rows_ref[...], preferred_element_type=F32).astype(BF16)
+
+
+def spread(rows, slots_of, slots):
+    count, model = rows.shape
+    return pl.pallas_call(
+        spread_kernel,
+        out_shape=jax.ShapeDtypeStruct((slots, model), BF16),
+        in_specs=[in_vmem()] * 2,
+        out_specs=in_vmem(),
+        compiler_params=pltpu.CompilerParams(vmem_limit_bytes=HIGH_VMEM),
+        cost_estimate=pl.CostEstimate(
+            flops=2 * slots * count * model,
+            bytes_accessed=2 * (count + slots) * model,
+            transcendentals=0,
+        ),
+        name="spread",
+    )(rows, slots_of)
+
+
+def gather_kernel(back_ref, slots_ref, gates_ref, *refs):
+    o_ref = refs[-1]
+    shape = (slots_ref.shape[0], back_ref.shape[0])
+    place = lax.broadcasted_iota(jnp.int32, shape, 1).astype(F32)
+    total = None
+    for k in range(slots_ref.shape[1]):
+        pick = (place == slots_ref[:, k : k + 1]).astype(BF16)
+        picked = jnp.dot(pick, back_ref[...], preferred_element_type=F32)
+        part = picked * gates_ref[:, k : k + 1]
+        total = part if total is None else total + part
+    if len(refs) > 1:
+        total = refs[0][...] + (total + refs[1][...].astype(F32))
+    o_ref[...] = total.astype(BF16)
+
+
+def gather(back, slots_of, gates, stream, partial):
+    slots, model = back.shape
+    rows, top = slots_of.shape
+    more = [] if stream is None else [stream, partial]
+    return pl.pallas_call(
+        gather_kernel,
+        out_shape=jax.ShapeDtypeStruct((rows, model), BF16),
+        in_specs=[in_vmem()] * (3 + len(more)),
+        out_specs=in_vmem(),
+        compiler_params=pltpu.CompilerParams(vmem_limit_bytes=HIGH_VMEM),
+        cost_estimate=pl.CostEstimate(
+            flops=2 * top * slots * rows * model,
+            bytes_accessed=2 * (slots + 4 * rows) * model,
+            transcendentals=0,
+        ),
+        name="gather",
+    )(back, slots_of, gates, *more)
+
+
 def flipped(value, axis, mask):
     pairs = [(source, source ^ mask) for source in range(lax.axis_size(axis))]
     return lax.ppermute(value, axis, pairs)
@@ -521,37 +621,47 @@
     w = w.reshape(2, 2, heads // 4, share, columns)
     w_keep = lax.dynamic_index_in_dim(w, y, 1, keepdims=False)
     w_give = lax.dynamic_index_in_dim(w, 1 - y, 1, keepdims=False)
+
+    (page_a, page_b), w_give = lax.optimization_barrier(((page_a, page_b), w_give))
+    own_pages = jnp.concatenate([page_a, page_b], 0)
+    pages_y = flipped(own_pages, "head", 2)
     w_got = flipped(w_give, "head", 2)
-
-    (page_a, page_b, kv_own, q), w_got = lax.optimization_barrier(
-        ((page_a, page_b, kv_own, q), w_got)
-    )
-    own_pages = jnp.concatenate([page_a, page_b], 0)
+    kv_own, w_got = lax.optimization_barrier((kv_own, w_got))
     kv_own = jnp.stack(kv_own, 0)
-    pages_y = flipped(own_pages, "head", 2)
     kv_y = flipped(kv_own, "head", 2)
     w_both = jnp.stack([w_keep, w_got], 1)
     w_same = lax.dynamic_index_in_dim(w_both, b, 0, keepdims=False)
     w_other = lax.dynamic_index_in_dim(w_both, 1 - b, 0, keepdims=False)
-    w_own = [w_same]
-    for t in range(1, planes):
-        w_own.append(flipped(w_other if t % 2 else w_same, "head", t * plane_bit))
+    w_far = [
+        flipped(w_other if t % 2 else w_same, "head", t * plane_bit) for t in range(1, planes)
+    ]
+    w_near = jnp.stack([w_same, w_far[0]], 0)
+    w_near_x = flipped(w_near, "grp", 1)
+    pages_y, kv_y, w_far = lax.optimization_barrier((pages_y, kv_y, w_far[1:]))
     pages_c = flipped(own_pages, "head", 1)
     kv_c = flipped(kv_own, "head", 1)
-    (pages_y, kv_y), w_own = lax.optimization_barrier(((pages_y, kv_y), w_own))
     pages_cy = flipped(pages_y, "head", 1)
     kv_cy = flipped(kv_y, "head", 1)
-    w_own = jnp.stack(w_own, 0)
-    q, w_own = lax.optimization_barrier((q, w_own))
-    w_x = flipped(w_own, "grp", 1)
-    w_c = flipped(w_own, "head", 1)
+    w_far = jnp.stack(w_far, 0)
+    q, w_far = lax.optimization_barrier((q, w_far))
+    w_far_x = flipped(w_far, "grp", 1)
+    w_near_c = flipped(w_near, "head", 1)
+    w_far_c = flipped(w_far, "head", 1)
     a = attend_pair(
         q, (page_a, page_b, pages_y, pages_c, pages_cy), (kv_own, kv_y, kv_c, kv_cy)
     )
-    a, w_x, w_c = lax.optimization_barrier((a, w_x, w_c))
-    w_cx = flipped(w_x, "head", 1)
+    a, w_near_x, w_far_x, w_near_c, w_far_c = lax.optimization_barrier(
+        (a, w_near_x, w_far_x, w_near_c, w_far_c)
+    )
+    w_near_cx = flipped(w_near_x, "head", 1)
+    w_far_cx = flipped(w_far_x, "head", 1)
     got = flipped(a[1], "head", 1)
-    partial = project_pair(a, got, w_own, w_c, w_x, w_cx)
+    partial = project_pair(
+        a,
+        got,
+        (w_near, w_near_c, w_near_x, w_near_cx),
+        (w_far, w_far_c, w_far_x, w_far_cx),
+    )
     quads = [
         [g * members + 2 * k + core for k in range(members // 2)]
         for g in range(n // members)
@@ -628,6 +738,41 @@
     return parts.reshape(seqs, planes_of_seq, local_rows, model)
 
 
+def route_in_pairs(parts, resid, norm_gain, slots_of, gates, w_in, w_down, capacity, members):
+    n = lax.axis_size("head")
+    local_rows, seqs, model = resid.shape
+    top = slots_of.shape[1]
+    me = lax.axis_index("head")
+    group_sets = [[g * members + m for m in range(members)] for g in range(n // members)]
+    group_slots = members * capacity
+
+    def around(value):
+        value = value.reshape(members, capacity, model)
+        value = lax.all_to_all(
+            value, "head", split_axis=0, concat_axis=0, tiled=True, axis_index_groups=group_sets
+        )
+        return value.reshape(group_slots, model)
+
+    own = jnp.concatenate([slots_of.astype(F32), gates], 1)
+    other = flipped(own, "head", members)
+    first = ((me // members) * group_slots).astype(F32)
+    slots_own, gates_own = own[:, :top] - first, own[:, top:]
+    slots_other, gates_other = other[:, :top] - first, other[:, top:]
+
+    stream, normed, out_own = route_pair(
+        parts, resid.reshape(local_rows, model), norm_gain[None, :], slots_own.T, group_slots
+    )
+    normed_other = flipped(normed, "head", members)
+    answer_own = expert(around(out_own), w_in, w_down)
+    out_other = spread(normed_other, slots_other.T, group_slots)
+    answer_other = expert(around(out_other), w_in, w_down)
+    partial = gather(around(answer_other), slots_other, gates_other, None, None)
+    partial, answer_own = lax.optimization_barrier((partial, answer_own))
+    partial = flipped(partial, "head", members)
+    out = gather(around(answer_own), slots_own, gates_own, stream, partial)
+    return out.reshape(local_rows, seqs, model)
+
+
 def local(queries, new_kv, cache, resid, w_out, norm_gain, expert_ids, expert_gates, w_in, w_down):
     n = lax.axis_size("head")
     local_rows, seqs, heads, width = queries.shape
@@ -656,7 +801,10 @@
     before = jnp.cumsum(named, 0) - named
     slots_of = ids * capacity + jnp.sum(onehot * before[:, None, :], 2)
     slots = experts * capacity
-
+    if in_pairs and w_in.shape[0] == 1:
+        return route_in_pairs(
+            parts[0], resid, norm_gain, slots_of, gates, w_in[0], w_down[0], capacity, members
+        )
     stream, outgoing = route(
         parts, resid.transpose(1, 0, 2), norm_gain[None, :], slots_of.T, slots
     )

time: 247 us -> 266 us (1.077); the launches traced: 247 us -> 262 us
  blocking collectives: 53.8 us -> 19.9 us
  starting transfers between devices: 30.4 us -> 56.1 us
  waiting for transfers between devices: 124 us -> 138 us
  local copies, waits for them, and re-layouts: 8.28 us -> 14.3 us
  Pallas kernels: 28.8 us -> 32.8 us
    all_to_all x1, blocking collectives: 53.8 us -> 19.9 us  [around(): lax.all_to_all(value, 'head', split_axis=0, concat_axis=0, tiled=True, ax...]
    all_to_all x1 -> x3, waiting for transfers between devices: 47.3 us -> 13.5 us  [around(): lax.all_to_all(value, 'head', split_axis=0, concat_axis=0, tiled=True, ax...]
    ppermute x17 -> x23, waiting for transfers between devices: 53.3 us -> 84.6 us  [flipped(): return lax.ppermute(value, axis, pairs)]
    ppermute x2, waiting for transfers between devices: 0.01 us -> 16.6 us  [parts_in_pairs(): lax.ppermute(cache[0], 'head', [(d, page_target(d, other)) for d in range...]
    ppermute x17 -> x23, starting transfers between devices: 12.4 us -> 26.3 us  [flipped(): return lax.ppermute(value, axis, pairs)]
    all_to_all x1 -> x3, starting transfers between devices: 5.25 us -> 17.6 us  [around(): lax.all_to_all(value, 'head', split_axis=0, concat_axis=0, tiled=True, ax...]
    unnamed x27 -> x39, local copies, waits for them, and re-layouts: 4.57 us -> 9.83 us
    pallas_call x1 -> x2, Pallas kernels: 6.34 us -> 8.43 us  [expert(): pl.pallas_call(expert_kernel, out_shape=jax.ShapeDtypeStruct((rows, model...]
  transfers between devices with their start and end apart: 22 -> 30, of which waited for: 11 -> 14; matrix products, arithmetic and copies ran while one was open for 1% -> 1% of each run, Pallas kernels for 6% -> 9%
where the time goes in v4:
time: 266 us; the launch traced here: 262 us
  waiting for transfers between devices  138 us (52%)
  starting transfers between devices  56.1 us (21%)
  Pallas kernels  32.8 us (12%)
  blocking collectives  19.9 us (7%)
  local copies, waits for them, and re-layouts  14.3 us (5%)
    ppermute x23, waiting for transfers between devices, flipped(): return lax.ppermute(value, axis, pairs)  84.6 us
    ppermute x23, starting transfers between devices, flipped(): return lax.ppermute(value, axis, pairs)  26.3 us
    all_to_all x1, waiting for transfers between devices, parts_in_pairs(): lax.all_to_all(partial.reshape(members // 2, local_rows, model), 'head',...  23.1 us
    all_to_all x1, blocking collectives, around(): lax.all_to_all(value, 'head', split_axis=0, concat_axis=0, tiled=True, ax...  19.9 us
    all_to_all x3, starting transfers between devices, around(): lax.all_to_all(value, 'head', split_axis=0, concat_axis=0, tiled=True, ax...  17.6 us
    ppermute x2, waiting for transfers between devices, parts_in_pairs(): lax.ppermute(cache[0], 'head', [(d, page_target(d, other)) for d in range...  16.6 us
    pallas_call x1, Pallas kernels, attend_pair(): pl.pallas_call(functools.partial(attend_pair_kernel, block, chunk, width)...  14.6 us
    all_to_all x3, waiting for transfers between devices, around(): lax.all_to_all(value, 'head', split_axis=0, concat_axis=0, tiled=True, ax...  13.5 us
  transfers between devices with their start and end apart: 30, of which 14 were waited for; matrix products, arithmetic and copies ran while one was open for 1% of the time, Pallas kernels for 9%

profile of v4, /device:TPU:13, one launch (start us, length us, event | category | flops | bytes accessed | tf_op | source)
XLA Modules:
  0.0 261.8 jit_solution(17057198440801040890)
XLA Ops:
  0.0 2.7 %copy.33 = bf16[16,128,256]{2,1,0:T(8,128)(2,1)} copy(bf16[16,128,256]{2,0,1:T(8,128)(2,1)} %bitcast.65) | data formatting | bytes 2097152 | tf_op jit(solution)/shard_map/transpose | solution.py:598
  2.7 4.6 %all-to-all-start = ((bf16[8,2,128,256]{3,2,1,0:T(8,128)(2,1)}), bf16[8,2,128,256]{3,2,1,0:T(8,128)(2,1)}, u32[]{:S(2)}, u32[]{:S(2)}) async-start(bf16[8,2,128,256]{3,2,1,0:T(8,128)(2,1)} %bitcast.2), calls=%async_computation | async-start | bytes 2097152 | tf_op jit(solution)/shard_map/all_to_all | solution.py:600
  7.3 3.6 %collective-permute-start = (bf16[256,512]{1,0:T(8,128)(2,1)S(1)}, bf16[256,512]{1,0:T(8,128)(2,1)S(1)}, u32[]{:S(2)}, u32[]{:S(2)}) collective-permute-start(bf16[256,512]{1,0:T(8,128)(2,1)S(1)} %bitcast.79), channel_id=1, source_target_pairs={{0,0},{1,1},{2,2},{3,3},{4,8},{5,9},{6,10},{7,11},{8,4},{9,5},{10,... | collective-permute-start | bytes 786440 | tf_op jit(solution)/shard_map/ppermute | solution.py:609
  11.2 6.2 %collective-permute-done.page_a = bf16[256,512]{1,0:T(8,128)(2,1)S(1)} collective-permute-done((bf16[256,512]{1,0:T(8,128)(2,1)S(1)}, bf16[256,512]{1,0:T(8,128)(2,1)S(1)}, u32[]{:S(2)}, u32[]{:S(2)}) %collective-permute-start) | collective-permute-done | bytes 262176 | tf_op jit(solution)/shard_map/ppermute | solution.py:609
  17.4 10.4 %collective-permute-done.1.page_b = bf16[256,512]{1,0:T(8,128)(2,1)S(1)} collective-permute-done((bf16[256,512]{1,0:T(8,128)(2,1)S(1)}, bf16[256,512]{1,0:T(8,128)(2,1)S(1)}, u32[]{:S(2)}, u32[]{:S(2)}) %collective-permute-start.1) | collective-permute-done | bytes 262176 | tf_op jit(solution)/shard_map/ppermute | solution.py:609
  29.4 3.0 %collective-permute-start.4 = (bf16[128,512]{1,0:T(8,128)(2,1)S(1)}, bf16[128,512]{1,0:T(8,128)(2,1)S(1)}, u32[]{:S(2)}, u32[]{:S(2)}) collective-permute-start(bf16[128,512]{1,0:T(8,128)(2,1)S(1)} %bitcast.68), channel_id=1, source_target_pairs={{0,8},{1,9},{2,10},{3,11},{4,12},{5,13},{6,14},{7,15},{8,0},{9,1},... | collective-permute-start | bytes 393224 | tf_op jit(solution)/shard_map/ppermute | solution.py:581
  33.8 1.2 collective-permute-start.2
  35.0 5.7 %collective-permute-done.4 = bf16[128,512]{1,0:T(8,128)(2,1)S(1)} collective-permute-done((bf16[128,512]{1,0:T(8,128)(2,1)S(1)}, bf16[128,512]{1,0:T(8,128)(2,1)S(1)}, u32[]{:S(2)}, u32[]{:S(2)}) %collective-permute-start.4) | collective-permute-done | bytes 131104 | tf_op jit(solution)/shard_map/ppermute | solution.py:581
  40.8 1.2 collective-permute-start.7
  42.0 3.2 %collective-permute-start.8 = (bf16[2,4,16,1024]{3,2,1,0:T(8,128)(2,1)S(1)}, bf16[2,4,16,1024]{3,2,1,0:T(8,128)(2,1)S(1)}, u32[]{:S(2)}, u32[]{:S(2)}) collective-permute-start(bf16[2,4,16,1024]{3,2,1,0:T(8,128)(2,1)S(1)} %bitcast.66), channel_id=1, source_target_pairs={{0,8},{1,9},{2,10},{3,11},{4,12},{5,13},{6,14},{7,15},{8,0},{9,1},... | collective-permute-start | bytes 786440 | tf_op jit(solution)/shard_map/ppermute | solution.py:581
  45.2 2.6 collective-permute-start.10
  47.8 3.2 %collective-permute-start.12 = (bf16[4,128,512]{2,1,0:T(8,128)(2,1)S(1)}, bf16[4,128,512]{2,1,0:T(8,128)(2,1)}, u32[]{:S(2)}, u32[]{:S(2)}) collective-permute-start(bf16[4,128,512]{2,1,0:T(8,128)(2,1)S(1)} %pad_maximum_fusion.kv_own), channel_id=1, source_target_pairs={{0,1},{1,0},{2,3},{3,2},{4,5},{5,4},{6,7},{7,6},{8,9},{9,8},{10,11... | collective-permute-start | bytes 1572872 | tf_op jit(solution)/shard_map/ppermute | solution.py:581
  51.0 9.4 %collective-permute-done.8 = bf16[2,4,16,1024]{3,2,1,0:T(8,128)(2,1)S(1)} collective-permute-done((bf16[2,4,16,1024]{3,2,1,0:T(8,128)(2,1)S(1)}, bf16[2,4,16,1024]{3,2,1,0:T(8,128)(2,1)S(1)}, u32[]{:S(2)}, u32[]{:S(2)}) %collective-permute-start.8) | collective-permute-done | bytes 262176 | tf_op jit(solution)/shard_map/ppermute | solution.py:581
  60.4 7.1 %collective-permute-done.9 = bf16[2,4,16,1024]{3,2,1,0:T(8,128)(2,1)S(1)} collective-permute-done((bf16[2,4,16,1024]{3,2,1,0:T(8,128)(2,1)S(1)}, bf16[2,4,16,1024]{3,2,1,0:T(8,128)(2,1)S(1)}, u32[]{:S(2)}, u32[]{:S(2)}) %collective-permute-start.9) | collective-permute-done | bytes 262176 | tf_op jit(solution)/shard_map/ppermute | solution.py:581
  67.5 1.2 collective-permute-start.11
  68.7 7.4 %collective-permute-done.14 = bf16[2,4,16,1024]{3,2,1,0:T(8,128)(2,1)S(1)} collective-permute-done((bf16[2,4,16,1024]{3,2,1,0:T(8,128)(2,1)S(1)}, bf16[2,4,16,1024]{3,2,1,0:T(8,128)(2,1)S(1)}, u32[]{:S(2)}, u32[]{:S(2)}) %collective-permute-start.14) | collective-permute-done | bytes 262176 | tf_op jit(solution)/shard_map/ppermute | solution.py:581
  76.1 1.3 collective-permute-start.15
  77.5 1.7 collective-permute-start.17
  79.8 14.6 %attend.1.a_ref = bf16[2,512,512]{2,1,0:T(8,128)(2,1)S(1)} custom-call(bf16[8,2,128,256]{3,2,1,0:T(8,128)(2,1)} %all-to-all-done.q_hbm, bf16[256,512]{1,0:T(8,128)(2,1)S(1)} %collective-permute-done.page_a, bf16[256,512]{1,0:T(8,128)(2,1)S(1)} %collective-permute-done.1.page_b, bf16[512,512]{1,0:T(8,128)(2,1)} %collective-permute-done.2.page_y, ...), custom_call_target="tpu_custom_call" | custom-call | flops 7516192768 | bytes 6291456 | tf_op jit(solution)/shard_map/attend/pallas_call | solution.py:259
  94.4 5.1 %collective-permute-done.16.refs_6_ = bf16[2,2,4,16,1024]{4,3,2,1,0:T(8,128)(2,1)S(1)} collective-permute-done((bf16[2,2,4,16,1024]{4,3,2,1,0:T(8,128)(2,1)S(1)}, bf16[2,2,4,16,1024]{4,3,2,1,0:T(8,128)(2,1)S(1)}, u32[]{:S(2)}, u32[]{:S(2)}) %collective-permute-start.16) | collective-permute-done | bytes 524320 | tf_op jit(solution)/shard_map/ppermute | solution.py:581
  99.5 2.3 collective-permute-start.19
  102.4 1.0 collective-permute-done.19.got_ref
  103.4 1.7 collective-permute-done.20.refs_3_
  105.1 5.0 %project.1 = bf16[512,2048]{1,0:T(8,128)(2,1)} custom-call(bf16[2,512,512]{2,1,0:T(8,128)(2,1)S(1)} %attend.1.a_ref, bf16[512,512]{1,0:T(8,128)(2,1)S(1)} %collective-permute-done.19.got_ref, bf16[2,2,4,16,1024]{4,3,2,1,0:T(8,128)(2,1)S(1)} %pad_maximum_fusion.2.refs_0_, bf16[2,2,4,16,1024]{4,3,2,1,0:T(8,128)(2,1)S(1)} %collective-permute-done.17.refs_1_, ...), custom_call_target="tpu_custom_call" | custom-call | flops 2147483648 | bytes 7340032 | tf_op jit(solution)/shard_map/project/pallas_call | solution.py:322
  110.1 3.9 %all-to-all-start.1 = ((bf16[4,128,2048]{2,1,0:T(8,128)(2,1)}), bf16[4,128,2048]{2,1,0:T(8,128)(2,1)S(1)}, u32[]{:S(2)}, u32[]{:S(2)}) async-start(bf16[4,128,2048]{2,1,0:T(8,128)(2,1)} %bitcast.63), calls=%async_computation.1 | async-start | bytes 4194304 | tf_op jit(solution)/shard_map/all_to_all | solution.py:670
  114.8 23.1 %all-to-all-done.1.parts_ref = bf16[4,128,2048]{2,1,0:T(8,128)(2,1)S(1)} async-done(((bf16[4,128,2048]{2,1,0:T(8,128)(2,1)}), bf16[4,128,2048]{2,1,0:T(8,128)(2,1)S(1)}, u32[]{:S(2)}, u32[]{:S(2)}) %all-to-all-start.1) | async-done | bytes 2097184 | tf_op jit(solution)/shard_map/all_to_all | solution.py:670
  137.9 1.0 copy-done.8
  138.9 1.3 route.1
  140.3 1.0 copy-done.5
  141.3 1.0 copy-done.7
  142.2 0.9 collective-permute-start.22
  143.3 1.5 collective-permute-start.23
  144.9 23.6 %collective-permute-done.23 = f32[128,4]{1,0:T(8,128)S(1)} collective-permute-done((f32[128,4]{1,0:T(8,128)S(1)}, f32[128,4]{1,0:T(8,128)S(1)}, u32[]{:S(2)}, u32[]{:S(2)}) %collective-permute-start.23) | collective-permute-done | bytes 2080 | tf_op jit(solution)/shard_map/ppermute | solution.py:581
  169.1 19.9 %all_to_all.30 = bf16[8,32,2048]{2,1,0:T(8,128)(2,1)} all-to-all(bf16[8,32,2048]{2,1,0:T(8,128)(2,1)S(1)} %bitcast.50), channel_id=1, replica_groups={{0,1,2,3,4,5,6,7},{8,9,10,11,12,13,14,15},{16,17,18,19,20,21,22,23},{24..., dimensions={0} | all-to-all | bytes 2097152 | tf_op jit(solution)/shard_map/all_to_all | solution.py:751
  189.0 6.0 %all-to-all-start.4 = ((bf16[8,32,2048]{2,1,0:T(8,128)(2,1)}), bf16[8,32,2048]{2,1,0:T(8,128)(2,1)}, u32[]{:S(2)}, u32[]{:S(2)}) async-start(bf16[8,32,2048]{2,1,0:T(8,128)(2,1)} %bitcast.54), calls=%async_computation.4 | async-start | bytes 2097152 | tf_op jit(solution)/shard_map/all_to_all | solution.py:751
  195.0 1.2 copy-done.4
  196.2 4.1 %expert.2 = bf16[256,2048]{1,0:T(8,128)(2,1)S(1)} custom-call(bf16[256,2048]{1,0:T(8,128)(2,1)S(1)} %bitcast.53, bf16[2048,1024]{1,0:T(8,128)(2,1)} %bitcast.61, bf16[512,2048]{1,0:T(8,128)(2,1)S(1)} %bitcast.47), custom_call_target="tpu_custom_call" | custom-call | flops 1610612736 | bytes 8388608 | tf_op jit(solution)/shard_map/expert/pallas_call | solution.py:430
  200.2 1.0 copy-done.3
  201.2 6.3 %all-to-all-done.4 = bf16[8,32,2048]{2,1,0:T(8,128)(2,1)} async-done(((bf16[8,32,2048]{2,1,0:T(8,128)(2,1)}), bf16[8,32,2048]{2,1,0:T(8,128)(2,1)}, u32[]{:S(2)}, u32[]{:S(2)}) %all-to-all-start.4) | async-done | bytes 1048608 | tf_op jit(solution)/shard_map/all_to_all | solution.py:751
  207.5 6.1 %all-to-all-start.3 = ((bf16[8,32,2048]{2,1,0:T(8,128)(2,1)}), bf16[8,32,2048]{2,1,0:T(8,128)(2,1)}, u32[]{:S(2)}, u32[]{:S(2)}) async-start(bf16[8,32,2048]{2,1,0:T(8,128)(2,1)} %bitcast.52), calls=%async_computation.3 | async-start | bytes 2097152 | tf_op jit(solution)/shard_map/all_to_all | solution.py:751
  213.7 4.4 %expert.3 = bf16[256,2048]{1,0:T(8,128)(2,1)S(1)} custom-call(bf16[256,2048]{1,0:T(8,128)(2,1)} %bitcast.33.x_ref, bf16[2048,1024]{1,0:T(8,128)(2,1)} %bitcast.62, bf16[512,2048]{1,0:T(8,128)(2,1)S(1)} %bitcast.48), custom_call_target="tpu_custom_call" | custom-call | flops 1610612736 | bytes 8388608 | tf_op jit(solution)/shard_map/expert/pallas_call | solution.py:430
  218.1 1.0 copy-done.2
  219.0 7.2 %all-to-all-done.3 = bf16[8,32,2048]{2,1,0:T(8,128)(2,1)} async-done(((bf16[8,32,2048]{2,1,0:T(8,128)(2,1)}), bf16[8,32,2048]{2,1,0:T(8,128)(2,1)}, u32[]{:S(2)}, u32[]{:S(2)}) %all-to-all-start.3) | async-done | bytes 1048608 | tf_op jit(solution)/shard_map/all_to_all | solution.py:751
  226.2 1.7 gather.2
  228.7 5.5 %all-to-all-start.5 = ((bf16[8,32,2048]{2,1,0:T(8,128)(2,1)}), bf16[8,32,2048]{2,1,0:T(8,128)(2,1)S(1)}, u32[]{:S(2)}, u32[]{:S(2)}) async-start(bf16[8,32,2048]{2,1,0:T(8,128)(2,1)} %bitcast.51), calls=%async_computation.5 | async-start | bytes 2097152 | tf_op jit(solution)/shard_map/all_to_all | solution.py:751
  235.1 23.5 %collective-permute-done.24.refs_1_ = bf16[128,2048]{1,0:T(8,128)(2,1)S(1)} collective-permute-done((bf16[128,2048]{1,0:T(8,128)(2,1)}, bf16[128,2048]{1,0:T(8,128)(2,1)S(1)}, u32[]{:S(2)}, u32[]{:S(2)}) %collective-permute-start.24) | collective-permute-done | bytes 524320 | tf_op jit(solution)/shard_map/ppermute | solution.py:581
  259.4 1.0 copy-done.10
  260.4 1.4 gather.3
  (83 shorter events, 8.6 us)
Async XLA Ops:
  0.0 11.1 %copy-start = (bf16[16,16,2048]{2,1,0:T(8,128)(2,1)S(1)}, bf16[16,16,2048]{2,1,0:T(8,128)(2,1)}, u32[]{:S(2)}) copy-start(bf16[16,16,2048]{2,1,0:T(8,128)(2,1)} %param.14) | copy-start | bytes 3145732
  0.0 7.3 %copy-start.16 = (bf16[1,256,512]{2,1,0:T(8,128)(2,1)S(1)}, bf16[1,256,512]{2,1,0:T(8,128)(2,1)}, u32[]{:S(2)}) copy-start(bf16[1,256,512]{2,1,0:T(8,128)(2,1)} %param.12) | copy-start | bytes 786436
  2.7 25.4 %copy-start.13 = (bf16[128,1,2,512]{3,2,1,0:T(2,128)(2,1)S(1)}, bf16[128,1,2,512]{3,2,1,0:T(2,128)(2,1)}, u32[]{:S(2)}) copy-start(bf16[128,1,2,512]{3,2,1,0:T(2,128)(2,1)} %param.11) | copy-start | bytes 786436
  2.7 74.8 %all-to-all-start = ((bf16[8,2,128,256]{3,2,1,0:T(8,128)(2,1)}), bf16[8,2,128,256]{3,2,1,0:T(8,128)(2,1)}, u32[]{:S(2)}, u32[]{:S(2)}) async-start(bf16[8,2,128,256]{3,2,1,0:T(8,128)(2,1)} %bitcast.2), calls=%async_computation | async-start | bytes 2097152 | tf_op jit(solution)/shard_map/all_to_all | solution.py:600
  7.3 10.1 %collective-permute-start = (bf16[256,512]{1,0:T(8,128)(2,1)S(1)}, bf16[256,512]{1,0:T(8,128)(2,1)S(1)}, u32[]{:S(2)}, u32[]{:S(2)}) collective-permute-start(bf16[256,512]{1,0:T(8,128)(2,1)S(1)} %bitcast.79), channel_id=1, source_target_pairs={{0,0},{1,1},{2,2},{3,3},{4,8},{5,9},{6,10},{7,11},{8,4},{9,5},{10,... | collective-permute-start | bytes 786440 | tf_op jit(solution)/shard_map/ppermute | solution.py:609
  10.9 16.8 %collective-permute-start.1 = (bf16[256,512]{1,0:T(8,128)(2,1)S(1)}, bf16[256,512]{1,0:T(8,128)(2,1)S(1)}, u32[]{:S(2)}, u32[]{:S(2)}) collective-permute-start(bf16[256,512]{1,0:T(8,128)(2,1)S(1)} %bitcast.80), channel_id=1, source_target_pairs={{0,8},{1,9},{2,10},{3,11},{4,0},{5,1},{6,2},{7,3},{8,12},{9,13},{1... | collective-permute-start | bytes 786440 | tf_op jit(solution)/shard_map/ppermute | solution.py:609
  27.8 12.9 %collective-permute-start.6 = (bf16[2,4,16,1024]{3,2,1,0:T(8,128)(2,1)S(1)}, bf16[2,4,16,1024]{3,2,1,0:T(8,128)(2,1)S(1)}, u32[]{:S(2)}, u32[]{:S(2)}) collective-permute-start(bf16[2,4,16,1024]{3,2,1,0:T(8,128)(2,1)S(1)} %get-tuple-element.31), channel_id=1, source_target_pairs={{0,2},{1,3},{2,0},{3,1},{4,6},{5,7},{6,4},{7,5},{8,10},{9,11},{10,... | collective-permute-start | bytes 786440 | tf_op jit(solution)/shard_map/ppermute | solution.py:581
  28.6 6.3 %collective-permute-start.3 = (bf16[128,512]{1,0:T(8,128)(2,1)S(1)}, bf16[128,512]{1,0:T(8,128)(2,1)S(1)}, u32[]{:S(2)}, u32[]{:S(2)}) collective-permute-start(bf16[128,512]{1,0:T(8,128)(2,1)S(1)} %bitcast.74), channel_id=1, source_target_pairs={{0,4},{1,5},{2,6},{3,7},{4,0},{5,1},{6,2},{7,3},{8,12},{9,13},{10,... | collective-permute-start | bytes 393224 | tf_op jit(solution)/shard_map/ppermute | solution.py:581
  28.7 11.9 %collective-permute-start.5 = (bf16[128,512]{1,0:T(8,128)(2,1)S(1)}, bf16[128,512]{1,0:T(8,128)(2,1)S(1)}, u32[]{:S(2)}, u32[]{:S(2)}) collective-permute-start(bf16[128,512]{1,0:T(8,128)(2,1)S(1)} %bitcast.75), channel_id=1, source_target_pairs={{0,12},{1,13},{2,14},{3,15},{4,8},{5,9},{6,10},{7,11},{8,4},{9,5},... | collective-permute-start | bytes 393224 | tf_op jit(solution)/shard_map/ppermute | solution.py:581
  29.4 11.3 %collective-permute-start.4 = (bf16[128,512]{1,0:T(8,128)(2,1)S(1)}, bf16[128,512]{1,0:T(8,128)(2,1)S(1)}, u32[]{:S(2)}, u32[]{:S(2)}) collective-permute-start(bf16[128,512]{1,0:T(8,128)(2,1)S(1)} %bitcast.68), channel_id=1, source_target_pairs={{0,8},{1,9},{2,10},{3,11},{4,12},{5,13},{6,14},{7,15},{8,0},{9,1},... | collective-permute-start | bytes 393224 | tf_op jit(solution)/shard_map/ppermute | solution.py:581
  33.8 14.0 %collective-permute-start.2 = (bf16[512,512]{1,0:T(8,128)(2,1)}, bf16[512,512]{1,0:T(8,128)(2,1)}, u32[]{:S(2)}, u32[]{:S(2)}) collective-permute-start(bf16[512,512]{1,0:T(8,128)(2,1)} %constant_dynamic-update-slice_fusion), channel_id=1, source_target_pairs={{0,2},{1,3},{2,0},{3,1},{4,6},{5,7},{6,4},{7,5},{8,10},{9,11},{10,... | collective-permute-start | bytes 1572872 | tf_op jit(solution)/shard_map/ppermute | solution.py:581
  40.8 26.8 %collective-permute-start.7 = (bf16[4,128,512]{2,1,0:T(8,128)(2,1)S(1)}, bf16[4,128,512]{2,1,0:T(8,128)(2,1)}, u32[]{:S(2)}, u32[]{:S(2)}) collective-permute-start(bf16[4,128,512]{2,1,0:T(8,128)(2,1)S(1)} %pad_maximum_fusion.kv_own), channel_id=1, source_target_pairs={{0,2},{1,3},{2,0},{3,1},{4,6},{5,7},{6,4},{7,5},{8,10},{9,11},{10,... | collective-permute-start | bytes 1572872 | tf_op jit(solution)/shard_map/ppermute | solution.py:581
  42.0 18.3 %collective-permute-start.8 = (bf16[2,4,16,1024]{3,2,1,0:T(8,128)(2,1)S(1)}, bf16[2,4,16,1024]{3,2,1,0:T(8,128)(2,1)S(1)}, u32[]{:S(2)}, u32[]{:S(2)}) collective-permute-start(bf16[2,4,16,1024]{3,2,1,0:T(8,128)(2,1)S(1)} %bitcast.66), channel_id=1, source_target_pairs={{0,8},{1,9},{2,10},{3,11},{4,12},{5,13},{6,14},{7,15},{8,0},{9,1},... | collective-permute-start | bytes 786440 | tf_op jit(solution)/shard_map/ppermute | solution.py:581
  45.2 22.3 %collective-permute-start.9 = (bf16[2,4,16,1024]{3,2,1,0:T(8,128)(2,1)S(1)}, bf16[2,4,16,1024]{3,2,1,0:T(8,128)(2,1)S(1)}, u32[]{:S(2)}, u32[]{:S(2)}) collective-permute-start(bf16[2,4,16,1024]{3,2,1,0:T(8,128)(2,1)S(1)} %get-tuple-element.55), channel_id=1, source_target_pairs={{0,12},{1,13},{2,14},{3,15},{4,8},{5,9},{6,10},{7,11},{8,4},{9,5},... | collective-permute-start | bytes 786440 | tf_op jit(solution)/shard_map/ppermute | solution.py:581
  45.2 32.2 %collective-permute-start.10 = (bf16[512,512]{1,0:T(8,128)(2,1)}, bf16[512,512]{1,0:T(8,128)(2,1)}, u32[]{:S(2)}, u32[]{:S(2)}) collective-permute-start(bf16[512,512]{1,0:T(8,128)(2,1)} %constant_dynamic-update-slice_fusion), channel_id=1, source_target_pairs={{0,1},{1,0},{2,3},{3,2},{4,5},{5,4},{6,7},{7,6},{8,9},{9,8},{10,11... | collective-permute-start | bytes 1572872 | tf_op jit(solution)/shard_map/ppermute | solution.py:581
  47.8 31.4 %collective-permute-start.12 = (bf16[4,128,512]{2,1,0:T(8,128)(2,1)S(1)}, bf16[4,128,512]{2,1,0:T(8,128)(2,1)}, u32[]{:S(2)}, u32[]{:S(2)}) collective-permute-start(bf16[4,128,512]{2,1,0:T(8,128)(2,1)S(1)} %pad_maximum_fusion.kv_own), channel_id=1, source_target_pairs={{0,1},{1,0},{2,3},{3,2},{4,5},{5,4},{6,7},{7,6},{8,9},{9,8},{10,11... | collective-permute-start | bytes 1572872 | tf_op jit(solution)/shard_map/ppermute | solution.py:581
  67.5 11.9 %collective-permute-start.11 = (bf16[512,512]{1,0:T(8,128)(2,1)}, bf16[512,512]{1,0:T(8,128)(2,1)}, u32[]{:S(2)}, u32[]{:S(2)}) collective-permute-start(bf16[512,512]{1,0:T(8,128)(2,1)} %collective-permute-done.2.page_y), channel_id=1, source_target_pairs={{0,1},{1,0},{2,3},{3,2},{4,5},{5,4},{6,7},{7,6},{8,9},{9,8},{10,11... | collective-permute-start | bytes 1572872 | tf_op jit(solution)/shard_map/ppermute | solution.py:581
  68.7 11.1 %collective-permute-start.13 = (bf16[4,128,512]{2,1,0:T(8,128)(2,1)}, bf16[4,128,512]{2,1,0:T(8,128)(2,1)}, u32[]{:S(2)}, u32[]{:S(2)}) collective-permute-start(bf16[4,128,512]{2,1,0:T(8,128)(2,1)} %collective-permute-done.7.kv_y), channel_id=1, source_target_pairs={{0,1},{1,0},{2,3},{3,2},{4,5},{5,4},{6,7},{7,6},{8,9},{9,8},{10,11... | collective-permute-start | bytes 1572872 | tf_op jit(solution)/shard_map/ppermute | solution.py:581
  68.7 7.4 %collective-permute-start.14 = (bf16[2,4,16,1024]{3,2,1,0:T(8,128)(2,1)S(1)}, bf16[2,4,16,1024]{3,2,1,0:T(8,128)(2,1)S(1)}, u32[]{:S(2)}, u32[]{:S(2)}) collective-permute-start(bf16[2,4,16,1024]{3,2,1,0:T(8,128)(2,1)S(1)} %get-tuple-element.55), channel_id=1, source_target_pairs={{0,4},{1,5},{2,6},{3,7},{4,0},{5,1},{6,2},{7,3},{8,12},{9,13},{10,... | collective-permute-start | bytes 786440 | tf_op jit(solution)/shard_map/ppermute | solution.py:581
  76.1 18.3 %collective-permute-start.15 = (bf16[2,2,4,16,1024]{4,3,2,1,0:T(8,128)(2,1)S(1)}, bf16[2,2,4,16,1024]{4,3,2,1,0:T(8,128)(2,1)}, u32[]{:S(2)}, u32[]{:S(2)}) collective-permute-start(bf16[2,2,4,16,1024]{4,3,2,1,0:T(8,128)(2,1)S(1)} %pad_maximum_fusion.2.refs_0_), channel_id=1, source_target_pairs={{0,16},{16,0},{1,17},{17,1},{2,18},{18,2},{3,19},{19,3},{4,20},{20... | collective-permute-start | bytes 1572872 | tf_op jit(solution)/shard_map/ppermute | solution.py:581
  77.5 16.9 %collective-permute-start.17 = (bf16[2,2,4,16,1024]{4,3,2,1,0:T(8,128)(2,1)S(1)}, bf16[2,2,4,16,1024]{4,3,2,1,0:T(8,128)(2,1)S(1)}, u32[]{:S(2)}, u32[]{:S(2)}) collective-permute-start(bf16[2,2,4,16,1024]{4,3,2,1,0:T(8,128)(2,1)S(1)} %pad_maximum_fusion.2.refs_0_), channel_id=1, source_target_pairs={{0,1},{1,0},{2,3},{3,2},{4,5},{5,4},{6,7},{7,6},{8,9},{9,8},{10,11... | collective-permute-start | bytes 1572872 | tf_op jit(solution)/shard_map/ppermute | solution.py:581
  79.2 20.3 %collective-permute-start.16 = (bf16[2,2,4,16,1024]{4,3,2,1,0:T(8,128)(2,1)S(1)}, bf16[2,2,4,16,1024]{4,3,2,1,0:T(8,128)(2,1)S(1)}, u32[]{:S(2)}, u32[]{:S(2)}) collective-permute-start(bf16[2,2,4,16,1024]{4,3,2,1,0:T(8,128)(2,1)S(1)} %pad_maximum_fusion.1.refs_4_), channel_id=1, source_target_pairs={{0,16},{16,0},{1,17},{17,1},{2,18},{18,2},{3,19},{19,3},{4,20},{20... | collective-permute-start | bytes 1572872 | tf_op jit(solution)/shard_map/ppermute | solution.py:581
  79.4 20.0 %collective-permute-start.18 = (bf16[2,2,4,16,1024]{4,3,2,1,0:T(8,128)(2,1)S(1)}, bf16[2,2,4,16,1024]{4,3,2,1,0:T(8,128)(2,1)S(1)}, u32[]{:S(2)}, u32[]{:S(2)}) collective-permute-start(bf16[2,2,4,16,1024]{4,3,2,1,0:T(8,128)(2,1)S(1)} %pad_maximum_fusion.1.refs_4_), channel_id=1, source_target_pairs={{0,1},{1,0},{2,3},{3,2},{4,5},{5,4},{6,7},{7,6},{8,9},{9,8},{10,11... | collective-permute-start | bytes 1572872 | tf_op jit(solution)/shard_map/ppermute | solution.py:581
  99.5 3.9 %collective-permute-start.19 = (bf16[512,512]{1,0:T(8,128)(2,1)S(1)}, bf16[512,512]{1,0:T(8,128)(2,1)S(1)}, u32[]{:S(2)}, u32[]{:S(2)}) collective-permute-start(bf16[512,512]{1,0:T(8,128)(2,1)S(1)} %slice_bitcast_fusion), channel_id=1, source_target_pairs={{0,1},{1,0},{2,3},{3,2},{4,5},{5,4},{6,7},{7,6},{8,9},{9,8},{10,11... | collective-permute-start | bytes 1572872 | tf_op jit(solution)/shard_map/ppermute | solution.py:581
  101.9 3.2 %collective-permute-start.20 = (bf16[2,2,4,16,1024]{4,3,2,1,0:T(8,128)(2,1)}, bf16[2,2,4,16,1024]{4,3,2,1,0:T(8,128)(2,1)S(1)}, u32[]{:S(2)}, u32[]{:S(2)}) collective-permute-start(bf16[2,2,4,16,1024]{4,3,2,1,0:T(8,128)(2,1)} %collective-permute-done.15.refs_2_), channel_id=1, source_target_pairs={{0,1},{1,0},{2,3},{3,2},{4,5},{5,4},{6,7},{7,6},{8,9},{9,8},{10,11... | collective-permute-start | bytes 1572872 | tf_op jit(solution)/shard_map/ppermute | solution.py:581
  101.9 3.2 %collective-permute-start.21 = (bf16[2,2,4,16,1024]{4,3,2,1,0:T(8,128)(2,1)S(1)}, bf16[2,2,4,16,1024]{4,3,2,1,0:T(8,128)(2,1)S(1)}, u32[]{:S(2)}, u32[]{:S(2)}) collective-permute-start(bf16[2,2,4,16,1024]{4,3,2,1,0:T(8,128)(2,1)S(1)} %collective-permute-done.16.refs_6_), channel_id=1, source_target_pairs={{0,1},{1,0},{2,3},{3,2},{4,5},{5,4},{6,7},{7,6},{8,9},{9,8},{10,11... | collective-permute-start | bytes 1572872 | tf_op jit(solution)/shard_map/ppermute | solution.py:581
  110.1 3.9 %copy-start.14 = (s32[128,1,2]{0,2,1:T(2,128)S(1)}, s32[128,1,2]{0,2,1:T(2,128)}, u32[]{:S(2)}) copy-start(s32[128,1,2]{0,2,1:T(2,128)} %param.16) | copy-start | bytes 3076
  110.1 27.8 %copy-start.12 = (f32[2048]{0:T(1024)S(1)}, f32[2048]{0:T(1024)}, u32[]{:S(2)}) copy-start(f32[2048]{0:T(1024)} %param.15) | copy-start | bytes 24580
  110.1 27.8 %all-to-all-start.1 = ((bf16[4,128,2048]{2,1,0:T(8,128)(2,1)}), bf16[4,128,2048]{2,1,0:T(8,128)(2,1)S(1)}, u32[]{:S(2)}, u32[]{:S(2)}) async-start(bf16[4,128,2048]{2,1,0:T(8,128)(2,1)} %bitcast.63), calls=%async_computation.1 | async-start | bytes 4194304 | tf_op jit(solution)/shard_map/all_to_all | solution.py:670
  114.0 29.1 %copy-start.15 = (f32[128,1,2]{0,2,1:T(2,128)S(1)}, f32[128,1,2]{0,2,1:T(2,128)}, u32[]{:S(2)}) copy-start(f32[128,1,2]{0,2,1:T(2,128)} %param.17) | copy-start | bytes 3076
  137.9 1.0 copy-start.8
  140.3 1.0 copy-start.5
  141.3 1.0 copy-start.7
  142.2 26.4 %collective-permute-start.22 = (bf16[128,2048]{1,0:T(8,128)(2,1)}, bf16[128,2048]{1,0:T(8,128)(2,1)S(1)}, u32[]{:S(2)}, u32[]{:S(2)}) collective-permute-start(bf16[128,2048]{1,0:T(8,128)(2,1)} %get-tuple-element.48), channel_id=1, source_target_pairs={{0,8},{1,9},{2,10},{3,11},{4,12},{5,13},{6,14},{7,15},{8,0},{9,1},... | collective-permute-start | bytes 1572872 | tf_op jit(solution)/shard_map/ppermute | solution.py:581
  143.3 25.2 %collective-permute-start.23 = (f32[128,4]{1,0:T(8,128)S(1)}, f32[128,4]{1,0:T(8,128)S(1)}, u32[]{:S(2)}, u32[]{:S(2)}) collective-permute-start(f32[128,4]{1,0:T(8,128)S(1)} %pad_maximum_fusion.3), channel_id=1, source_target_pairs={{0,8},{1,9},{2,10},{3,11},{4,12},{5,13},{6,14},{7,15},{8,0},{9,1},... | collective-permute-start | bytes 6152 | tf_op jit(solution)/shard_map/ppermute | solution.py:581
  169.1 25.8 %copy-start.1 = (bf16[1,512,2048]{2,1,0:T(8,128)(2,1)S(1)}, bf16[1,512,2048]{2,1,0:T(8,128)(2,1)}, u32[]{:S(2)}) copy-start(bf16[1,512,2048]{2,1,0:T(8,128)(2,1)} %param.19) | copy-start | bytes 6291460
  189.0 18.5 %all-to-all-start.4 = ((bf16[8,32,2048]{2,1,0:T(8,128)(2,1)}), bf16[8,32,2048]{2,1,0:T(8,128)(2,1)}, u32[]{:S(2)}, u32[]{:S(2)}) async-start(bf16[8,32,2048]{2,1,0:T(8,128)(2,1)} %bitcast.54), calls=%async_computation.4 | async-start | bytes 2097152 | tf_op jit(solution)/shard_map/all_to_all | solution.py:751
  195.0 1.2 copy-start.4
  200.2 1.0 copy-start.3
  207.5 18.7 %all-to-all-start.3 = ((bf16[8,32,2048]{2,1,0:T(8,128)(2,1)}), bf16[8,32,2048]{2,1,0:T(8,128)(2,1)}, u32[]{:S(2)}, u32[]{:S(2)}) async-start(bf16[8,32,2048]{2,1,0:T(8,128)(2,1)} %bitcast.52), calls=%async_computation.3 | async-start | bytes 2097152 | tf_op jit(solution)/shard_map/all_to_all | solution.py:751
  218.0 1.0 copy-start.2
  219.0 40.4 %copy-start.6 = (f32[128,2048]{1,0:T(8,128)S(1)}, f32[128,2048]{1,0:T(8,128)}, u32[]{:S(2)}) copy-start(f32[128,2048]{1,0:T(8,128)} %copy-done.5) | copy-start | bytes 3145732
  227.9 0.8 copy-start.11
  228.7 30.7 %all-to-all-start.5 = ((bf16[8,32,2048]{2,1,0:T(8,128)(2,1)}), bf16[8,32,2048]{2,1,0:T(8,128)(2,1)S(1)}, u32[]{:S(2)}, u32[]{:S(2)}) async-start(bf16[8,32,2048]{2,1,0:T(8,128)(2,1)} %bitcast.51), calls=%async_computation.5 | async-start | bytes 2097152 | tf_op jit(solution)/shard_map/all_to_all | solution.py:751
  234.2 24.4 %collective-permute-start.24 = (bf16[128,2048]{1,0:T(8,128)(2,1)}, bf16[128,2048]{1,0:T(8,128)(2,1)S(1)}, u32[]{:S(2)}, u32[]{:S(2)}) collective-permute-start(bf16[128,2048]{1,0:T(8,128)(2,1)} %copy-done.11), channel_id=1, source_target_pairs={{0,8},{1,9},{2,10},{3,11},{4,12},{5,13},{6,14},{7,15},{8,0},{9,1},... | collective-permute-start | bytes 1572872 | tf_op jit(solution)/shard_map/ppermute | solution.py:581
  258.6 0.8 copy-start.9
  259.4 1.0 copy-start.10

commit v5 on v4

--- a/solution.py
+++ b/solution.py
@@ -11,6 +11,7 @@
 F32 = jnp.float32
 BF16 = jnp.bfloat16
 HIGH_VMEM = 48 * 2**20
+ATTEND_VMEM = 32 * 2**20
 
 
 def in_hbm():
@@ -127,23 +128,144 @@
     )(q, cache, kv)
 
 
-def attend_pair_kernel(
+def attend_units(q_ref, units, pieces, arrays, scores, width, prior, finish):
+    scale = width**-0.5
+
+    def make_scores(unit, part, running):
+        name, first, count, column, mask = part
+        head, row, rows = units[unit]
+        s = lax.dot_general(
+            q_ref[head, pl.ds(row, rows), :],
+            arrays[name][pl.ds(first, count), :width],
+            (((1,), (1,)), ((), ())),
+            preferred_element_type=F32,
+        )
+        if mask is not None:
+            s = jnp.where(mask(s.shape), s, -jnp.inf)
+        scores[unit % 2][:, pl.ds(column, count)] = s
+        for k in range(0, count, 128):
+            piece_max = s[:, k : k + 128]
+            running = piece_max if running is None else jnp.maximum(running, piece_max)
+        return running
+
+    def use_scores(unit, part, top, total, acc):
+        name, first, count, column, _ = part
+        e = jnp.exp((scores[unit % 2][:, pl.ds(column, count)] - top) * scale)
+        for k in range(0, count, 128):
+            total = e[:, k : k + 128] if total is None else total + e[:, k : k + 128]
+        values = arrays[name][pl.ds(first, count), width:]
+        product = jnp.dot(e.astype(BF16), values, preferred_element_type=F32)
+        return total, product if acc is None else acc + product
+
+    running = None
+    for part in pieces(0):
+        running = make_scores(0, part, running)
+    for unit in range(len(units)):
+        top = jnp.max(running, 1, keepdims=True)
+        before = prior(unit)
+        if before is not None:
+            top = jnp.maximum(top, before[0])
+        now = pieces(unit)
+        later = pieces(unit + 1) if unit + 1 < len(units) else []
+        running, total, acc = None, None, None
+        for k in range(max(len(now), len(later))):
+            if k < len(now):
+                total, acc = use_scores(unit, now[k], top, total, acc)
+            if k < len(later):
+                running = make_scores(unit + 1, later[k], running)
+        if before is not None:
+            shrink = jnp.exp((before[0] - top) * scale)
+            total = total + before[1] * shrink
+            acc = acc + before[2] * shrink
+        finish(unit, top, total, acc)
+
+
+def bring_queries(q_hbm, q_ref, sem):
+    members, heads, piece, _ = q_hbm.shape
+    copies = []
+    for member in range(members):
+        for head in range(heads):
+            copies.append(
+                pltpu.make_async_copy(
+                    q_hbm.at[member, head], q_ref.at[head, pl.ds(member * piece, piece)], sem
+                )
+            )
+    return copies
+
+
+def attend_old_kernel(block, chunk, width, count, q_hbm, *refs):
+    pages, (top_ref, total_ref, acc_ref, q_ref, old_ref, s0, s1, sems) = refs[:count], refs[count:]
+    copies = bring_queries(q_hbm, q_ref, sems.at[0])
+    place = 0
+    for page in pages:
+        copies.append(
+            pltpu.make_async_copy(page, old_ref.at[pl.ds(place, page.shape[0])], sems.at[1])
+        )
+        place += page.shape[0]
+    for copy in copies:
+        copy.start()
+    for copy in copies:
+        copy.wait()
+    heads, length, _ = q_ref.shape
+    units = [(head, row, block) for head in range(heads) for row in range(0, length, block)]
+
+    def pieces(unit):
+        return [("old", k, chunk, k, None) for k in range(0, old_ref.shape[0], chunk)]
+
+    def finish(unit, top, total, acc):
+        head, row, rows = units[unit]
+        top_ref[head, pl.ds(row, rows), :] = jnp.broadcast_to(top, total.shape)
+        total_ref[head, pl.ds(row, rows), :] = total
+        acc_ref[head, pl.ds(row, rows), :] = acc
+
+    attend_units(
+        q_ref, units, pieces, {"old": old_ref}, [s0, s1], width, lambda unit: None, finish
+    )
+
+
+def attend_old(q, pages):
+    members, heads, piece, width = q.shape
+    length = members * piece
+    old = sum(page.shape[0] for page in pages)
+    block = 2 * piece
+    chunk = min(512, old)
+    lanes = jax.ShapeDtypeStruct((heads, length, 128), F32)
+    return pl.pallas_call(
+        functools.partial(attend_old_kernel, block, chunk, width, len(pages)),
+        out_shape=(lanes, lanes, jax.ShapeDtypeStruct((heads, length, width), F32)),
+        in_specs=[in_hbm()] * (1 + len(pages)),
+        out_specs=(in_vmem(),) * 3,
+        scratch_shapes=[
+            pltpu.VMEM((heads, length, width), BF16),
+            pltpu.VMEM((old, 2 * width), BF16),
+            pltpu.VMEM((block, old), F32),
+            pltpu.VMEM((block, old), F32),
+            pltpu.SemaphoreType.DMA((2,)),
+        ],
+        compiler_params=pltpu.CompilerParams(vmem_limit_bytes=ATTEND_VMEM),
+        cost_estimate=pl.CostEstimate(
+            flops=4 * heads * length * old * width,
+            bytes_accessed=4 * (heads * length + old) * width,
+            transcendentals=heads * length * old,
+        ),
+        name="attend_old",
+    )(q, *pages)
+
+
+def attend_new_kernel(
     block,
     chunk,
     width,
     q_hbm,
-    page_a,
-    page_b,
-    page_y,
-    page_c,
-    page_cy,
     kv_own,
     kv_y,
     kv_c,
     kv_cy,
+    top_ref,
+    total_ref,
+    acc_ref,
     o_ref,
     q_ref,
-    old_ref,
     kv_ref,
     s0,
     s1,
@@ -153,24 +275,9 @@
     members, heads, piece, _ = q_hbm.shape
     length = members * piece
     planes = kv_own.shape[0]
-    old = old_ref.shape[0]
     earlier_group = me // members > 0
     core = lax.rem(me, 2)
-    copies = []
-
-    def bring(source, target, sem):
-        copy = pltpu.make_async_copy(source, target, sems.at[sem])
-        copy.start()
-        copies.append(copy)
-
-    for member in range(members):
-        for head in range(heads):
-            bring(q_hbm.at[member, head], q_ref.at[head, pl.ds(member * piece, piece)], 0)
-    place = 0
-    for page in (page_a, page_b, page_y, page_c, page_cy):
-        count = page.shape[0]
-        bring(page, old_ref.at[pl.ds(place, count)], 1)
-        place += count
+    copies = bring_queries(q_hbm, q_ref, sems.at[0])
     for flip, pieces_of in ((0, kv_own), (2, kv_y), (1, kv_c), (3, kv_cy)):
         for t in range(planes):
             number = jnp.bitwise_and(
@@ -178,105 +285,74 @@
             )
             start = pl.multiple_of(number * piece, piece)
             area = 0 if t * (members // 2) >= members else length
-            bring(pieces_of.at[t], kv_ref.at[pl.ds(area + start, piece)], 2)
+            copies.append(
+                pltpu.make_async_copy(
+                    pieces_of.at[t], kv_ref.at[pl.ds(area + start, piece)], sems.at[1]
+                )
+            )
+    for copy in copies:
+        copy.start()
     for copy in copies:
         copy.wait()
-    scale = width**-0.5
-    scores = [s0, s1]
-    blocks = length // block
-    units = [(head, b) for head in range(heads) for b in range(blocks)]
+    units = [(head, row, block) for head in range(heads) for row in range(0, length, block)]
+
+    def earlier(shape):
+        return jnp.broadcast_to(earlier_group, shape)
+
+    def causal(shape):
+        row = lax.broadcasted_iota(jnp.int32, shape, 0)
+        return lax.broadcasted_iota(jnp.int32, shape, 1) <= row
 
     def pieces(unit):
-        _, b = units[unit]
-        out = [("old", k, chunk, k) for k in range(0, old, chunk)]
-        out += [("past", k, chunk, old + k) for k in range(0, length, chunk)]
-        last = b * block
-        for k in range(0, last, chunk):
-            out.append(("new", length + k, min(chunk, last - k), old + length + k))
-        out.append(("edge", length + last, block, old + length + last))
-        return out
-
-    def make_scores(unit, part, running):
-        kind, first, count, column = part
-        head, b = units[unit]
-        keys = (old_ref if kind == "old" else kv_ref)[pl.ds(first, count), :width]
-        s = lax.dot_general(
-            q_ref[head, pl.ds(b * block, block), :],
-            keys,
-            (((1,), (1,)), ((), ())),
-            preferred_element_type=F32,
-        )
-        if kind == "past":
-            s = jnp.where(earlier_group, s, -jnp.inf)
-        if kind == "edge":
-            row = lax.broadcasted_iota(jnp.int32, s.shape, 0)
-            col = lax.broadcasted_iota(jnp.int32, s.shape, 1)
-            s = jnp.where(col <= row, s, -jnp.inf)
-        scores[unit % 2][:, pl.ds(column, count)] = s
-        for k in range(0, count, 128):
-            piece_max = s[:, k : k + 128]
-            running = piece_max if running is None else jnp.maximum(running, piece_max)
-        return running
-
-    def use_scores(unit, part, top, total, acc):
-        kind, first, count, column = part
-        values = (old_ref if kind == "old" else kv_ref)[pl.ds(first, count), width:]
-        e = jnp.exp((scores[unit % 2][:, pl.ds(column, count)] - top) * scale)
-        for k in range(0, count, 128):
-            total = e[:, k : k + 128] if total is None else total + e[:, k : k + 128]
-        product = jnp.dot(e.astype(BF16), values, preferred_element_type=F32)
-        return total, product if acc is None else acc + product
-
-    running = None
-    for part in pieces(0):
-        running = make_scores(0, part, running)
-    for unit, (head, b) in enumerate(units):
-        top = jnp.max(running, 1, keepdims=True)
-        now = pieces(unit)
-        later = pieces(unit + 1) if unit + 1 < len(units) else []
-        running, total, acc = None, None, None
-        for k in range(max(len(now), len(later))):
-            if k < len(now):
-                total, acc = use_scores(unit, now[k], top, total, acc)
-            if k < len(later):
-                running = make_scores(unit + 1, later[k], running)
+        _, row, rows = units[unit]
+        out = [("new", k, chunk, k, earlier) for k in range(0, length, chunk)]
+        for k in range(0, row, chunk):
+            out.append(("new", length + k, min(chunk, row - k), length + k, None))
+        return out + [("new", length + row, rows, length + row, causal)]
+
+    def prior(unit):
+        head, row, rows = units[unit]
+        at = pl.ds(row, rows)
+        return top_ref[head, at, :1], total_ref[head, at, :], acc_ref[head, at, :]
+
+    def finish(unit, top, total, acc):
+        head, row, rows = units[unit]
         done = (acc / jnp.sum(total, 1, keepdims=True)).astype(BF16)
-        for k in range(0, block, piece):
-            member = (b * block + k) // piece
+        for k in range(0, rows, piece):
+            member = (row + k) // piece
             side = jnp.bitwise_xor(core, member % 2)
             o_ref[side, pl.ds((member // 2) * piece, piece), pl.ds(head * width, width)] = done[
                 k : k + piece
             ]
 
-
-def attend_pair(q, pages, kvs):
+    attend_units(q_ref, units, pieces, {"new": kv_ref}, [s0, s1], width, prior, finish)
+
+
+def attend_new(q, kvs, old):
     members, heads, piece, width = q.shape
     length = members * piece
-    old = sum(page.shape[0] for page in pages)
     block = 2 * piece
-    chunk = min(512, old, length)
-    keys = old + 2 * length
-    return pl.pallas_call(
-        functools.partial(attend_pair_kernel, block, chunk, width),
+    chunk = min(512, length)
+    return pl.pallas_call(
+        functools.partial(attend_new_kernel, block, chunk, width),
         out_shape=jax.ShapeDtypeStruct((2, length // 2, heads * width), BF16),
-        in_specs=[in_hbm()] * (1 + len(pages) + len(kvs)),
+        in_specs=[in_hbm()] * (1 + len(kvs)) + [in_vmem()] * 3,
         out_specs=in_vmem(),
         scratch_shapes=[
             pltpu.VMEM((heads, length, width), BF16),
-            pltpu.VMEM((old, 2 * width), BF16),
             pltpu.VMEM((2 * length, 2 * width), BF16),
-            pltpu.VMEM((block, keys), F32),
-            pltpu.VMEM((block, keys), F32),
-            pltpu.SemaphoreType.DMA((3,)),
+            pltpu.VMEM((block, 2 * length), F32),
+            pltpu.VMEM((block, 2 * length), F32),
+            pltpu.SemaphoreType.DMA((2,)),
         ],
-        compiler_params=pltpu.CompilerParams(vmem_limit_bytes=HIGH_VMEM),
-        cost_estimate=pl.CostEstimate(
-            flops=4 * heads * length * (keys - length // 2) * width,
-            bytes_accessed=4 * (heads * length + keys) * width,
-            transcendentals=heads * length * (keys - length // 2),
-        ),
-        name="attend",
-    )(q, *pages, *kvs)
+        compiler_params=pltpu.CompilerParams(vmem_limit_bytes=ATTEND_VMEM),
+        cost_estimate=pl.CostEstimate(
+            flops=6 * heads * length * length * width,
+            bytes_accessed=4 * (2 * heads * length + 2 * length) * width,
+            transcendentals=3 * heads * length * length // 2,
+        ),
+        name="attend_new",
+    )(q, *kvs, *old)
 
 
 def project_pair_kernel(a_ref, got_ref, *refs):
@@ -595,12 +671,6 @@
     y = (me // 2) % 2
     group_sets = [[g * members + m for m in range(members)] for g in range(n // members)]
 
-    query_slots = queries.reshape(local_rows, heads, width).transpose(1, 0, 2)
-    query_slots = query_slots.reshape(members, heads // members, local_rows, width)
-    q = lax.all_to_all(
-        query_slots, "head", split_axis=0, concat_axis=0, tiled=True, axis_index_groups=group_sets
-    )
-
     def page_target(source, other):
         p, plane, rest = source // members, (source // plane_bit) % 2, source % plane_bit
         return (plane ^ other) * members + p * plane_bit + rest
@@ -609,26 +679,36 @@
         lax.ppermute(cache[0], "head", [(d, page_target(d, other)) for d in range(n)])
         for other in range(2)
     )
-    kv_heads = new_kv.reshape(local_rows, pair_heads, 2 * width).transpose(1, 0, 2)
-    kv_same = lax.dynamic_index_in_dim(kv_heads, b, 0, keepdims=False)
-    kv_other = lax.dynamic_index_in_dim(kv_heads, 1 - b, 0, keepdims=False)
-    kv_own = [kv_same]
-    for t in range(1, planes):
-        kv_own.append(flipped(kv_other if t % 2 else kv_same, "head", t * plane_bit))
 
     columns = model // 2
     w = lax.dynamic_slice_in_dim(w_out, lax.axis_index("grp") * columns, columns, 2)
     w = w.reshape(2, 2, heads // 4, share, columns)
     w_keep = lax.dynamic_index_in_dim(w, y, 1, keepdims=False)
     w_give = lax.dynamic_index_in_dim(w, 1 - y, 1, keepdims=False)
-
-    (page_a, page_b), w_give = lax.optimization_barrier(((page_a, page_b), w_give))
-    own_pages = jnp.concatenate([page_a, page_b], 0)
-    pages_y = flipped(own_pages, "head", 2)
     w_got = flipped(w_give, "head", 2)
+
+    query_slots = queries.reshape(local_rows, heads, width).transpose(1, 0, 2)
+    query_slots = query_slots.reshape(members, heads // members, local_rows, width)
+    kv_heads = new_kv.reshape(local_rows, pair_heads, 2 * width).transpose(1, 0, 2)
+    kv_same = lax.dynamic_index_in_dim(kv_heads, b, 0, keepdims=False)
+    kv_other = lax.dynamic_index_in_dim(kv_heads, 1 - b, 0, keepdims=False)
+    (page_a, page_b), kv_same, kv_other, query_slots = lax.optimization_barrier(
+        ((page_a, page_b), kv_same, kv_other, query_slots)
+    )
+    page_ya = flipped(page_a, "head", 2)
+    page_yb = flipped(page_b, "head", 2)
+    kv_own = [kv_same]
+    for t in range(1, planes):
+        kv_own.append(flipped(kv_other if t % 2 else kv_same, "head", t * plane_bit))
+    q = lax.all_to_all(
+        query_slots, "head", split_axis=0, concat_axis=0, tiled=True, axis_index_groups=group_sets
+    )
+
+    page_c = flipped(jnp.concatenate([page_a, page_b], 0), "head", 1)
     kv_own, w_got = lax.optimization_barrier((kv_own, w_got))
     kv_own = jnp.stack(kv_own, 0)
     kv_y = flipped(kv_own, "head", 2)
+    kv_c = flipped(kv_own, "head", 1)
     w_both = jnp.stack([w_keep, w_got], 1)
     w_same = lax.dynamic_index_in_dim(w_both, b, 0, keepdims=False)
     w_other = lax.dynamic_index_in_dim(w_both, 1 - b, 0, keepdims=False)
@@ -636,20 +716,19 @@
         flipped(w_other if t % 2 else w_same, "head", t * plane_bit) for t in range(1, planes)
     ]
     w_near = jnp.stack([w_same, w_far[0]], 0)
+    page_cya = flipped(page_ya, "head", 1)
+    page_cyb = flipped(page_yb, "head", 1)
+    q, w_near = lax.optimization_barrier((q, w_near))
     w_near_x = flipped(w_near, "grp", 1)
-    pages_y, kv_y, w_far = lax.optimization_barrier((pages_y, kv_y, w_far[1:]))
-    pages_c = flipped(own_pages, "head", 1)
-    kv_c = flipped(kv_own, "head", 1)
-    pages_cy = flipped(pages_y, "head", 1)
+    old = attend_old(q, (page_a, page_b, page_ya, page_yb, page_c, page_cya, page_cyb))
+    old, kv_y, kv_c, w_far = lax.optimization_barrier((old, kv_y, kv_c, w_far[1:]))
     kv_cy = flipped(kv_y, "head", 1)
     w_far = jnp.stack(w_far, 0)
     q, w_far = lax.optimization_barrier((q, w_far))
     w_far_x = flipped(w_far, "grp", 1)
     w_near_c = flipped(w_near, "head", 1)
     w_far_c = flipped(w_far, "head", 1)
-    a = attend_pair(
-        q, (page_a, page_b, pages_y, pages_c, pages_cy), (kv_own, kv_y, kv_c, kv_cy)
-    )
+    a = attend_new(q, (kv_own, kv_y, kv_c, kv_cy), old)
     a, w_near_x, w_far_x, w_near_c, w_far_c = lax.optimization_barrier(
         (a, w_near_x, w_far_x, w_near_c, w_far_c)
     )
@@ -764,6 +843,7 @@
     )
     normed_other = flipped(normed, "head", members)
     answer_own = expert(around(out_own), w_in, w_down)
+    normed_other, answer_own = lax.optimization_barrier((normed_other, answer_own))
     out_other = spread(normed_other, slots_other.T, group_slots)
     answer_other = expert(around(out_other), w_in, w_down)
     partial = gather(around(answer_other), slots_other, gates_other, None, None)

time: 266 us -> 263 us (0.989); the launches traced: 262 us -> 262 us
  blocking collectives: 19.9 us -> 36.3 us
  waiting for transfers between devices: 138 us -> 125 us
  starting transfers between devices: 56.1 us -> 49.5 us
  Pallas kernels: 32.8 us -> 36.2 us
    all_to_all x1 -> x2, blocking collectives: 19.9 us -> 36.3 us  [around(): lax.all_to_all(value, 'head', split_axis=0, concat_axis=0, tiled=True, ax...]
    all_to_all x3 -> x2, waiting for transfers between devices: 13.5 us -> 0.01 us  [around(): lax.all_to_all(value, 'head', split_axis=0, concat_axis=0, tiled=True, ax...]
    ppermute x23 -> x25, waiting for transfers between devices: 84.6 us -> 95.1 us  [flipped(): return lax.ppermute(value, axis, pairs)]
    ppermute x2, waiting for transfers between devices: 16.6 us -> 6.77 us  [parts_in_pairs(): lax.ppermute(cache[0], 'head', [(d, page_target(d, other)) for d in range...]
    all_to_all x3 -> x2, starting transfers between devices: 17.6 us -> 11.5 us  [around(): lax.all_to_all(value, 'head', split_axis=0, concat_axis=0, tiled=True, ax...]
    pallas_call x1 -> x2, Pallas kernels: 14.6 us -> 18 us  [the longest x1 9.65 us: attend_new(): pl.pallas_call(functools.partial(attend_new_kernel, block, chunk, width),...]
    ppermute x23 -> x25, starting transfers between devices: 26.3 us -> 23.3 us  [flipped(): return lax.ppermute(value, axis, pairs)]
    unnamed x39 -> x36, local copies, waits for them, and re-layouts: 9.83 us -> 7.61 us
  transfers between devices with their start and end apart: 30 -> 31, of which waited for: 14 -> 15; matrix products, arithmetic and copies ran while one was open for 1% -> 3% of each run, Pallas kernels for 9% -> 9%
where the time goes in v5:
time: 263 us; the launch traced here: 262 us
  waiting for transfers between devices  125 us (48%)
  starting transfers between devices  49.5 us (19%)
  blocking collectives  36.3 us (14%)
  Pallas kernels  36.2 us (14%)
  local copies, waits for them, and re-layouts  13 us (5%)
    ppermute x25, waiting for transfers between devices, flipped(): return lax.ppermute(value, axis, pairs)  95.1 us
    all_to_all x2, blocking collectives, around(): lax.all_to_all(value, 'head', split_axis=0, concat_axis=0, tiled=True, ax...  36.3 us
    ppermute x25, starting transfers between devices, flipped(): return lax.ppermute(value, axis, pairs)  23.3 us
    all_to_all x1, waiting for transfers between devices, parts_in_pairs(): lax.all_to_all(partial.reshape(members // 2, local_rows, model), 'head',...  23.1 us
    all_to_all x2, starting transfers between devices, around(): lax.all_to_all(value, 'head', split_axis=0, concat_axis=0, tiled=True, ax...  11.5 us
    pallas_call x1, Pallas kernels, attend_new(): pl.pallas_call(functools.partial(attend_new_kernel, block, chunk, width),...  9.65 us
    pallas_call x2, Pallas kernels, expert(): pl.pallas_call(expert_kernel, out_shape=jax.ShapeDtypeStruct((rows, model...  9.42 us
    pallas_call x1, Pallas kernels, attend_old(): pl.pallas_call(functools.partial(attend_old_kernel, block, chunk, width,...  8.34 us
  transfers between devices with their start and end apart: 31, of which 15 were waited for; matrix products, arithmetic and copies ran while one was open for 3% of the time, Pallas kernels for 9%

profile of v5, /device:TPU:13, one launch (start us, length us, event | category | flops | bytes accessed | tf_op | source)
XLA Modules:
  0.0 261.8 jit_solution(18347224517882948837)
XLA Ops:
  0.0 3.3 %collective-permute-start = (bf16[256,512]{1,0:T(8,128)(2,1)}, bf16[256,512]{1,0:T(8,128)(2,1)S(1)}, u32[]{:S(2)}, u32[]{:S(2)}) collective-permute-start(bf16[256,512]{1,0:T(8,128)(2,1)} %bitcast.75), channel_id=1, source_target_pairs={{0,0},{1,1},{2,2},{3,3},{4,8},{5,9},{6,10},{7,11},{8,4},{9,5},{10,... | collective-permute-start | bytes 786440 | tf_op jit(solution)/shard_map/ppermute | solution.py:679
  3.4 1.6 constant_dynamic-slice_fusion.2
  5.0 2.6 copy.35
  8.3 6.8 %collective-permute-done.refs_0_ = bf16[256,512]{1,0:T(8,128)(2,1)S(1)} collective-permute-done((bf16[256,512]{1,0:T(8,128)(2,1)}, bf16[256,512]{1,0:T(8,128)(2,1)S(1)}, u32[]{:S(2)}, u32[]{:S(2)}) %collective-permute-start) | collective-permute-done | bytes 262176 | tf_op jit(solution)/shard_map/ppermute | solution.py:679
  15.0 5.4 %all-to-all-start = ((bf16[8,2,128,256]{3,2,1,0:T(8,128)(2,1)}), bf16[8,2,128,256]{3,2,1,0:T(8,128)(2,1)S(1)}, u32[]{:S(2)}, u32[]{:S(2)}) async-start(bf16[8,2,128,256]{3,2,1,0:T(8,128)(2,1)} %bitcast.61), calls=%async_computation | async-start | bytes 2097152 | tf_op jit(solution)/shard_map/all_to_all | solution.py:703
  20.9 2.2 collective-permute-start.4
  23.1 1.3 collective-permute-start.3
  25.2 1.5 collective-permute-start.9
  26.7 12.0 %collective-permute-done.5 = bf16[2,4,16,1024]{3,2,1,0:T(8,128)(2,1)S(1)} collective-permute-done((bf16[2,4,16,1024]{3,2,1,0:T(8,128)(2,1)S(1)}, bf16[2,4,16,1024]{3,2,1,0:T(8,128)(2,1)S(1)}, u32[]{:S(2)}, u32[]{:S(2)}) %collective-permute-start.5) | collective-permute-done | bytes 262176 | tf_op jit(solution)/shard_map/ppermute | solution.py:657
  38.7 1.0 collective-permute-start.7
  40.3 2.7 %collective-permute-done.3 = bf16[128,512]{1,0:T(8,128)(2,1)S(1)} collective-permute-done((bf16[128,512]{1,0:T(8,128)(2,1)S(1)}, bf16[128,512]{1,0:T(8,128)(2,1)S(1)}, u32[]{:S(2)}, u32[]{:S(2)}) %collective-permute-start.3) | collective-permute-done | bytes 131104 | tf_op jit(solution)/shard_map/ppermute | solution.py:657
  43.2 2.8 %collective-permute-done.7.refs_2_ = bf16[256,512]{1,0:T(8,128)(2,1)} collective-permute-done((bf16[256,512]{1,0:T(8,128)(2,1)S(1)}, bf16[256,512]{1,0:T(8,128)(2,1)}, u32[]{:S(2)}, u32[]{:S(2)}) %collective-permute-start.7) | collective-permute-done | bytes 262176 | tf_op jit(solution)/shard_map/ppermute | solution.py:657
  46.0 2.7 %collective-permute-start.10 = (bf16[256,512]{1,0:T(8,128)(2,1)}, bf16[256,512]{1,0:T(8,128)(2,1)}, u32[]{:S(2)}, u32[]{:S(2)}) collective-permute-start(bf16[256,512]{1,0:T(8,128)(2,1)} %collective-permute-done.7.refs_2_), channel_id=1, source_target_pairs={{0,1},{1,0},{2,3},{3,2},{4,5},{5,4},{6,7},{7,6},{8,9},{9,8},{10,11... | collective-permute-start | bytes 786440 | tf_op jit(solution)/shard_map/ppermute | solution.py:657
  48.7 2.9 %collective-permute-done.8.refs_3_ = bf16[256,512]{1,0:T(8,128)(2,1)} collective-permute-done((bf16[256,512]{1,0:T(8,128)(2,1)S(1)}, bf16[256,512]{1,0:T(8,128)(2,1)}, u32[]{:S(2)}, u32[]{:S(2)}) %collective-permute-start.8) | collective-permute-done | bytes 262176 | tf_op jit(solution)/shard_map/ppermute | solution.py:657
  51.6 1.5 collective-permute-start.11
  53.2 1.1 collective-permute-start.12
  54.7 1.1 collective-permute-start.15
  55.8 1.3 collective-permute-start.14
  57.1 0.9 copy-done.10
  58.0 8.3 %attend_old.1 = (f32[2,1024,128]{2,1,0:T(8,128)S(1)}, f32[2,1024,128]{2,1,0:T(8,128)S(1)}, f32[2,1024,256]{2,1,0:T(8,128)S(1)}) custom-call(bf16[8,2,128,256]{3,2,1,0:T(8,128)(2,1)S(1)} %all-to-all-done.q_hbm, bf16[256,512]{1,0:T(8,128)(2,1)S(1)} %collective-permute-done.refs_0_, bf16[256,512]{1,0:T(8,128)(2,1)S(1)} %copy-done.10, ...), custom_call_target="tpu_custom_call" | custom-call | flops 4294967296 | bytes 4194304 | tf_op jit(solution)/shard_map/attend_old/pallas_call | solution.py:233
  66.4 12.0 %collective-permute-done.14 = bf16[2,4,16,1024]{3,2,1,0:T(8,128)(2,1)S(1)} collective-permute-done((bf16[2,4,16,1024]{3,2,1,0:T(8,128)(2,1)}, bf16[2,4,16,1024]{3,2,1,0:T(8,128)(2,1)S(1)}, u32[]{:S(2)}, u32[]{:S(2)}) %collective-permute-start.14) | collective-permute-done | bytes 262176 | tf_op jit(solution)/shard_map/ppermute | solution.py:657
  78.4 1.1 collective-permute-start.16
  79.6 1.3 collective-permute-start.17
  81.7 9.7 %attend_new.1.a_ref = bf16[2,512,512]{2,1,0:T(8,128)(2,1)S(1)} custom-call(bf16[8,2,128,256]{3,2,1,0:T(8,128)(2,1)S(1)} %all-to-all-done.q_hbm, bf16[4,128,512]{2,1,0:T(8,128)(2,1)S(1)} %pad_maximum_fusion.2.kv_own, bf16[4,128,512]{2,1,0:T(8,128)(2,1)} %collective-permute-done.12.kv_y, bf16[4,128,512]{2,1,0:T(8,128)(2,1)} %collective-permute-done.13.kv_c, ...), custom_call_target="tpu_custom_call" | custom-call | flops 3221225472 | bytes 6291456 | tf_op jit(solution)/shard_map/attend_new/pallas_call | solution.py:336
  91.4 1.8 collective-permute-done.17.refs_2_
  93.2 11.2 %collective-permute-done.18.refs_6_ = bf16[2,2,4,16,1024]{4,3,2,1,0:T(8,128)(2,1)S(1)} collective-permute-done((bf16[2,2,4,16,1024]{4,3,2,1,0:T(8,128)(2,1)S(1)}, bf16[2,2,4,16,1024]{4,3,2,1,0:T(8,128)(2,1)S(1)}, u32[]{:S(2)}, u32[]{:S(2)}) %collective-permute-start.18) | collective-permute-done | bytes 524320 | tf_op jit(solution)/shard_map/ppermute | solution.py:657
  104.5 0.9 collective-permute-start.21
  105.9 1.0 collective-permute-done.21.got_ref
  108.4 4.5 %project.1 = bf16[512,2048]{1,0:T(8,128)(2,1)} custom-call(bf16[2,512,512]{2,1,0:T(8,128)(2,1)S(1)} %attend_new.1.a_ref, bf16[512,512]{1,0:T(8,128)(2,1)S(1)} %collective-permute-done.21.got_ref, bf16[2,2,4,16,1024]{4,3,2,1,0:T(8,128)(2,1)S(1)} %pad_maximum_fusion.refs_0_, bf16[2,2,4,16,1024]{4,3,2,1,0:T(8,128)(2,1)S(1)} %collective-permute-done.19.refs_1_, ...), custom_call_target="tpu_custom_call" | custom-call | flops 2147483648 | bytes 7340032 | tf_op jit(solution)/shard_map/project/pallas_call | solution.py:398
  112.9 6.0 %all-to-all-start.1 = ((bf16[4,128,2048]{2,1,0:T(8,128)(2,1)}), bf16[4,128,2048]{2,1,0:T(8,128)(2,1)S(1)}, u32[]{:S(2)}, u32[]{:S(2)}) async-start(bf16[4,128,2048]{2,1,0:T(8,128)(2,1)} %bitcast.62), calls=%async_computation.1 | async-start | bytes 4194304 | tf_op jit(solution)/shard_map/all_to_all | solution.py:749
  119.7 23.1 %all-to-all-done.1.parts_ref = bf16[4,128,2048]{2,1,0:T(8,128)(2,1)S(1)} async-done(((bf16[4,128,2048]{2,1,0:T(8,128)(2,1)}), bf16[4,128,2048]{2,1,0:T(8,128)(2,1)S(1)}, u32[]{:S(2)}, u32[]{:S(2)}) %all-to-all-start.1) | async-done | bytes 2097184 | tf_op jit(solution)/shard_map/all_to_all | solution.py:749
  142.8 1.0 copy-done.5
  143.9 0.9 route.1
  144.8 1.0 copy-done.2
  145.7 1.0 copy-done.4
  147.5 6.2 %all-to-all-start.2 = ((bf16[8,32,2048]{2,1,0:T(8,128)(2,1)}), bf16[8,32,2048]{2,1,0:T(8,128)(2,1)}, u32[]{:S(2)}, u32[]{:S(2)}) async-start(bf16[8,32,2048]{2,1,0:T(8,128)(2,1)} %bitcast.52), calls=%async_computation.2 | async-start | bytes 2097152 | tf_op jit(solution)/shard_map/all_to_all | solution.py:830
  154.5 1.8 collective-permute-start.25
  156.3 23.3 %collective-permute-done.25 = f32[128,4]{1,0:T(8,128)S(1)} collective-permute-done((f32[128,4]{1,0:T(8,128)S(1)}, f32[128,4]{1,0:T(8,128)S(1)}, u32[]{:S(2)}, u32[]{:S(2)}) %collective-permute-start.25) | collective-permute-done | bytes 2080 | tf_op jit(solution)/shard_map/ppermute | solution.py:657
  179.7 5.4 %expert.2 = bf16[256,2048]{1,0:T(8,128)(2,1)} custom-call(bf16[256,2048]{1,0:T(8,128)(2,1)} %bitcast.25.x_ref, bf16[2048,1024]{1,0:T(8,128)(2,1)} %bitcast.59, bf16[512,2048]{1,0:T(8,128)(2,1)S(1)} %bitcast.45), custom_call_target="tpu_custom_call" | custom-call | flops 1610612736 | bytes 8388608 | tf_op jit(solution)/shard_map/expert/pallas_call | solution.py:506
  185.1 1.5 spread.1
  186.5 19.1 %all_to_all.30 = bf16[8,32,2048]{2,1,0:T(8,128)(2,1)S(1)} all-to-all(bf16[8,32,2048]{2,1,0:T(8,128)(2,1)S(1)} %bitcast.48), channel_id=1, replica_groups={{0,1,2,3,4,5,6,7},{8,9,10,11,12,13,14,15},{16,17,18,19,20,21,22,23},{24..., dimensions={0} | all-to-all | bytes 2097152 | tf_op jit(solution)/shard_map/all_to_all | solution.py:830
  205.7 4.1 %expert.3 = bf16[256,2048]{1,0:T(8,128)(2,1)S(1)} custom-call(bf16[256,2048]{1,0:T(8,128)(2,1)S(1)} %bitcast.50, bf16[2048,1024]{1,0:T(8,128)(2,1)} %bitcast.60, bf16[512,2048]{1,0:T(8,128)(2,1)S(1)} %bitcast.46), custom_call_target="tpu_custom_call" | custom-call | flops 1610612736 | bytes 8388608 | tf_op jit(solution)/shard_map/expert/pallas_call | solution.py:506
  209.7 17.2 %all_to_all.31 = bf16[8,32,2048]{2,1,0:T(8,128)(2,1)S(1)} all-to-all(bf16[8,32,2048]{2,1,0:T(8,128)(2,1)S(1)} %bitcast.51), channel_id=1, replica_groups={{0,1,2,3,4,5,6,7},{8,9,10,11,12,13,14,15},{16,17,18,19,20,21,22,23},{24..., dimensions={0} | all-to-all | bytes 2097152 | tf_op jit(solution)/shard_map/all_to_all | solution.py:830
  228.2 5.3 %all-to-all-start.5 = ((bf16[8,32,2048]{2,1,0:T(8,128)(2,1)}), bf16[8,32,2048]{2,1,0:T(8,128)(2,1)S(1)}, u32[]{:S(2)}, u32[]{:S(2)}) async-start(bf16[8,32,2048]{2,1,0:T(8,128)(2,1)} %bitcast.34), calls=%async_computation.5 | async-start | bytes 2097152 | tf_op jit(solution)/shard_map/all_to_all | solution.py:830
  233.5 1.6 collective-permute-start.26
  235.1 23.4 %collective-permute-done.26.refs_1_ = bf16[128,2048]{1,0:T(8,128)(2,1)S(1)} collective-permute-done((bf16[128,2048]{1,0:T(8,128)(2,1)}, bf16[128,2048]{1,0:T(8,128)(2,1)S(1)}, u32[]{:S(2)}, u32[]{:S(2)}) %collective-permute-start.26) | collective-permute-done | bytes 524320 | tf_op jit(solution)/shard_map/ppermute | solution.py:657
  259.3 1.0 copy-done.7
  260.4 1.4 gather.3
  (85 shorter events, 10.8 us)
Async XLA Ops:
  0.0 20.4 %copy-start = (bf16[16,16,2048]{2,1,0:T(8,128)(2,1)S(1)}, bf16[16,16,2048]{2,1,0:T(8,128)(2,1)}, u32[]{:S(2)}) copy-start(bf16[16,16,2048]{2,1,0:T(8,128)(2,1)} %param.14) | copy-start | bytes 3145732
  0.0 15.0 %collective-permute-start = (bf16[256,512]{1,0:T(8,128)(2,1)}, bf16[256,512]{1,0:T(8,128)(2,1)S(1)}, u32[]{:S(2)}, u32[]{:S(2)}) collective-permute-start(bf16[256,512]{1,0:T(8,128)(2,1)} %bitcast.75), channel_id=1, source_target_pairs={{0,0},{1,1},{2,2},{3,3},{4,8},{5,9},{6,10},{7,11},{8,4},{9,5},{10,... | collective-permute-start | bytes 786440 | tf_op jit(solution)/shard_map/ppermute | solution.py:679
  3.3 11.7 %collective-permute-start.1 = (bf16[256,512]{1,0:T(8,128)(2,1)}, bf16[256,512]{1,0:T(8,128)(2,1)S(1)}, u32[]{:S(2)}, u32[]{:S(2)}) collective-permute-start(bf16[256,512]{1,0:T(8,128)(2,1)} %bitcast.76), channel_id=1, source_target_pairs={{0,8},{1,9},{2,10},{3,11},{4,0},{5,1},{6,2},{7,3},{8,12},{9,13},{1... | collective-permute-start | bytes 786440 | tf_op jit(solution)/shard_map/ppermute | solution.py:679
  15.0 25.0 %copy-start.9 = (bf16[256,512]{1,0:T(8,128)(2,1)}, bf16[256,512]{1,0:T(8,128)(2,1)S(1)}, u32[]{:S(2)}) copy-start(bf16[256,512]{1,0:T(8,128)(2,1)S(1)} %collective-permute-done.1.refs_1_) | copy-start | bytes 786436
  15.0 39.6 %all-to-all-start = ((bf16[8,2,128,256]{3,2,1,0:T(8,128)(2,1)}), bf16[8,2,128,256]{3,2,1,0:T(8,128)(2,1)S(1)}, u32[]{:S(2)}, u32[]{:S(2)}) async-start(bf16[8,2,128,256]{3,2,1,0:T(8,128)(2,1)} %bitcast.61), calls=%async_computation | async-start | bytes 2097152 | tf_op jit(solution)/shard_map/all_to_all | solution.py:703
  20.5 18.2 %collective-permute-start.5 = (bf16[2,4,16,1024]{3,2,1,0:T(8,128)(2,1)S(1)}, bf16[2,4,16,1024]{3,2,1,0:T(8,128)(2,1)S(1)}, u32[]{:S(2)}, u32[]{:S(2)}) collective-permute-start(bf16[2,4,16,1024]{3,2,1,0:T(8,128)(2,1)S(1)} %get-tuple-element.81), channel_id=1, source_target_pairs={{0,2},{1,3},{2,0},{3,1},{4,6},{5,7},{6,4},{7,5},{8,10},{9,11},{10,... | collective-permute-start | bytes 786440 | tf_op jit(solution)/shard_map/ppermute | solution.py:657
  20.9 19.2 %collective-permute-start.2 = (bf16[128,512]{1,0:T(8,128)(2,1)}, bf16[128,512]{1,0:T(8,128)(2,1)S(1)}, u32[]{:S(2)}, u32[]{:S(2)}) collective-permute-start(bf16[128,512]{1,0:T(8,128)(2,1)} %get-tuple-element.43), channel_id=1, source_target_pairs={{0,4},{1,5},{2,6},{3,7},{4,0},{5,1},{6,2},{7,3},{8,12},{9,13},{10,... | collective-permute-start | bytes 393224 | tf_op jit(solution)/shard_map/ppermute | solution.py:657
  20.9 22.1 %collective-permute-start.4 = (bf16[128,512]{1,0:T(8,128)(2,1)}, bf16[128,512]{1,0:T(8,128)(2,1)S(1)}, u32[]{:S(2)}, u32[]{:S(2)}) collective-permute-start(bf16[128,512]{1,0:T(8,128)(2,1)} %get-tuple-element.43), channel_id=1, source_target_pairs={{0,12},{1,13},{2,14},{3,15},{4,8},{5,9},{6,10},{7,11},{8,4},{9,5},... | collective-permute-start | bytes 393224 | tf_op jit(solution)/shard_map/ppermute | solution.py:657
  23.1 19.9 %collective-permute-start.3 = (bf16[128,512]{1,0:T(8,128)(2,1)S(1)}, bf16[128,512]{1,0:T(8,128)(2,1)S(1)}, u32[]{:S(2)}, u32[]{:S(2)}) collective-permute-start(bf16[128,512]{1,0:T(8,128)(2,1)S(1)} %get-tuple-element.51), channel_id=1, source_target_pairs={{0,8},{1,9},{2,10},{3,11},{4,12},{5,13},{6,14},{7,15},{8,0},{9,1},... | collective-permute-start | bytes 393224 | tf_op jit(solution)/shard_map/ppermute | solution.py:657
  25.2 29.4 %collective-permute-start.9 = (bf16[512,512]{1,0:T(8,128)(2,1)}, bf16[512,512]{1,0:T(8,128)(2,1)}, u32[]{:S(2)}, u32[]{:S(2)}) collective-permute-start(bf16[512,512]{1,0:T(8,128)(2,1)} %pad_maximum_fusion.1), channel_id=1, source_target_pairs={{0,1},{1,0},{2,3},{3,2},{4,5},{5,4},{6,7},{7,6},{8,9},{9,8},{10,11... | collective-permute-start | bytes 1572872 | tf_op jit(solution)/shard_map/ppermute | solution.py:657
  38.7 7.3 %collective-permute-start.7 = (bf16[256,512]{1,0:T(8,128)(2,1)S(1)}, bf16[256,512]{1,0:T(8,128)(2,1)}, u32[]{:S(2)}, u32[]{:S(2)}) collective-permute-start(bf16[256,512]{1,0:T(8,128)(2,1)S(1)} %collective-permute-done.refs_0_), channel_id=1, source_target_pairs={{0,2},{1,3},{2,0},{3,1},{4,6},{5,7},{6,4},{7,5},{8,10},{9,11},{10,... | collective-permute-start | bytes 786440 | tf_op jit(solution)/shard_map/ppermute | solution.py:657
  40.0 11.6 %collective-permute-start.8 = (bf16[256,512]{1,0:T(8,128)(2,1)S(1)}, bf16[256,512]{1,0:T(8,128)(2,1)}, u32[]{:S(2)}, u32[]{:S(2)}) collective-permute-start(bf16[256,512]{1,0:T(8,128)(2,1)S(1)} %collective-permute-done.1.refs_1_), channel_id=1, source_target_pairs={{0,2},{1,3},{2,0},{3,1},{4,6},{5,7},{6,4},{7,5},{8,10},{9,11},{10,... | collective-permute-start | bytes 786440 | tf_op jit(solution)/shard_map/ppermute | solution.py:657
  43.1 11.5 %copy-start.14 = (bf16[2,4,16,1024]{3,2,1,0:T(8,128)(2,1)}, bf16[2,4,16,1024]{3,2,1,0:T(8,128)(2,1)S(1)}, u32[]{:S(2)}) copy-start(bf16[2,4,16,1024]{3,2,1,0:T(8,128)(2,1)S(1)} %get-tuple-element.80) | copy-start | bytes 786436
  43.1 11.5 %copy-start.13 = (bf16[1,2,4,16,1024]{4,3,2,1,0:T(8,128)(2,1)}, bf16[1,2,4,16,1024]{4,3,2,1,0:T(8,128)(2,1)S(1)}, u32[]{:S(2)}) copy-start(bf16[1,2,4,16,1024]{4,3,2,1,0:T(8,128)(2,1)S(1)} %get-tuple-element.79) | copy-start | bytes 786436
  43.1 11.2 %collective-permute-start.6 = (bf16[2,4,16,1024]{3,2,1,0:T(8,128)(2,1)S(1)}, bf16[2,4,16,1024]{3,2,1,0:T(8,128)(2,1)S(1)}, u32[]{:S(2)}, u32[]{:S(2)}) collective-permute-start(bf16[2,4,16,1024]{3,2,1,0:T(8,128)(2,1)S(1)} %get-tuple-element.80), channel_id=1, source_target_pairs={{0,4},{1,5},{2,6},{3,7},{4,0},{5,1},{6,2},{7,3},{8,12},{9,13},{10,... | collective-permute-start | bytes 786440 | tf_op jit(solution)/shard_map/ppermute | solution.py:657
  46.0 9.8 %collective-permute-start.10 = (bf16[256,512]{1,0:T(8,128)(2,1)}, bf16[256,512]{1,0:T(8,128)(2,1)}, u32[]{:S(2)}, u32[]{:S(2)}) collective-permute-start(bf16[256,512]{1,0:T(8,128)(2,1)} %collective-permute-done.7.refs_2_), channel_id=1, source_target_pairs={{0,1},{1,0},{2,3},{3,2},{4,5},{5,4},{6,7},{7,6},{8,9},{9,8},{10,11... | collective-permute-start | bytes 786440 | tf_op jit(solution)/shard_map/ppermute | solution.py:657
  51.6 5.5 %collective-permute-start.11 = (bf16[256,512]{1,0:T(8,128)(2,1)}, bf16[256,512]{1,0:T(8,128)(2,1)}, u32[]{:S(2)}, u32[]{:S(2)}) collective-permute-start(bf16[256,512]{1,0:T(8,128)(2,1)} %collective-permute-done.8.refs_3_), channel_id=1, source_target_pairs={{0,1},{1,0},{2,3},{3,2},{4,5},{5,4},{6,7},{7,6},{8,9},{9,8},{10,11... | collective-permute-start | bytes 786440 | tf_op jit(solution)/shard_map/ppermute | solution.py:657
  53.2 25.2 %collective-permute-start.12 = (bf16[4,128,512]{2,1,0:T(8,128)(2,1)S(1)}, bf16[4,128,512]{2,1,0:T(8,128)(2,1)}, u32[]{:S(2)}, u32[]{:S(2)}) collective-permute-start(bf16[4,128,512]{2,1,0:T(8,128)(2,1)S(1)} %pad_maximum_fusion.2.kv_own), channel_id=1, source_target_pairs={{0,2},{1,3},{2,0},{3,1},{4,6},{5,7},{6,4},{7,5},{8,10},{9,11},{10,... | collective-permute-start | bytes 1572872 | tf_op jit(solution)/shard_map/ppermute | solution.py:657
  54.3 24.2 %collective-permute-start.13 = (bf16[4,128,512]{2,1,0:T(8,128)(2,1)S(1)}, bf16[4,128,512]{2,1,0:T(8,128)(2,1)}, u32[]{:S(2)}, u32[]{:S(2)}) collective-permute-start(bf16[4,128,512]{2,1,0:T(8,128)(2,1)S(1)} %pad_maximum_fusion.2.kv_own), channel_id=1, source_target_pairs={{0,1},{1,0},{2,3},{3,2},{4,5},{5,4},{6,7},{7,6},{8,9},{9,8},{10,11... | collective-permute-start | bytes 1572872 | tf_op jit(solution)/shard_map/ppermute | solution.py:657
  54.7 23.8 %collective-permute-start.15 = (bf16[2,4,16,1024]{3,2,1,0:T(8,128)(2,1)}, bf16[2,4,16,1024]{3,2,1,0:T(8,128)(2,1)S(1)}, u32[]{:S(2)}, u32[]{:S(2)}) collective-permute-start(bf16[2,4,16,1024]{3,2,1,0:T(8,128)(2,1)} %copy-done.14), channel_id=1, source_target_pairs={{0,12},{1,13},{2,14},{3,15},{4,8},{5,9},{6,10},{7,11},{8,4},{9,5},... | collective-permute-start | bytes 786440 | tf_op jit(solution)/shard_map/ppermute | solution.py:657
  55.8 22.6 %collective-permute-start.14 = (bf16[2,4,16,1024]{3,2,1,0:T(8,128)(2,1)}, bf16[2,4,16,1024]{3,2,1,0:T(8,128)(2,1)S(1)}, u32[]{:S(2)}, u32[]{:S(2)}) collective-permute-start(bf16[2,4,16,1024]{3,2,1,0:T(8,128)(2,1)} %bitcast.65), channel_id=1, source_target_pairs={{0,8},{1,9},{2,10},{3,11},{4,12},{5,13},{6,14},{7,15},{8,0},{9,1},... | collective-permute-start | bytes 786440 | tf_op jit(solution)/shard_map/ppermute | solution.py:657
  57.1 1.0 copy-start.10
  78.4 3.3 %collective-permute-start.16 = (bf16[4,128,512]{2,1,0:T(8,128)(2,1)}, bf16[4,128,512]{2,1,0:T(8,128)(2,1)S(1)}, u32[]{:S(2)}, u32[]{:S(2)}) collective-permute-start(bf16[4,128,512]{2,1,0:T(8,128)(2,1)} %collective-permute-done.12.kv_y), channel_id=1, source_target_pairs={{0,1},{1,0},{2,3},{3,2},{4,5},{5,4},{6,7},{7,6},{8,9},{9,8},{10,11... | collective-permute-start | bytes 1572872 | tf_op jit(solution)/shard_map/ppermute | solution.py:657
  79.6 13.6 %collective-permute-start.17 = (bf16[2,2,4,16,1024]{4,3,2,1,0:T(8,128)(2,1)S(1)}, bf16[2,2,4,16,1024]{4,3,2,1,0:T(8,128)(2,1)S(1)}, u32[]{:S(2)}, u32[]{:S(2)}) collective-permute-start(bf16[2,2,4,16,1024]{4,3,2,1,0:T(8,128)(2,1)S(1)} %pad_maximum_fusion.refs_0_), channel_id=1, source_target_pairs={{0,16},{16,0},{1,17},{17,1},{2,18},{18,2},{3,19},{19,3},{4,20},{20... | collective-permute-start | bytes 1572872 | tf_op jit(solution)/shard_map/ppermute | solution.py:657
  80.9 23.6 %collective-permute-start.18 = (bf16[2,2,4,16,1024]{4,3,2,1,0:T(8,128)(2,1)S(1)}, bf16[2,2,4,16,1024]{4,3,2,1,0:T(8,128)(2,1)S(1)}, u32[]{:S(2)}, u32[]{:S(2)}) collective-permute-start(bf16[2,2,4,16,1024]{4,3,2,1,0:T(8,128)(2,1)S(1)} %pad_maximum_fusion.3.refs_4_), channel_id=1, source_target_pairs={{0,16},{16,0},{1,17},{17,1},{2,18},{18,2},{3,19},{19,3},{4,20},{20... | collective-permute-start | bytes 1572872 | tf_op jit(solution)/shard_map/ppermute | solution.py:657
  81.1 23.3 %collective-permute-start.19 = (bf16[2,2,4,16,1024]{4,3,2,1,0:T(8,128)(2,1)S(1)}, bf16[2,2,4,16,1024]{4,3,2,1,0:T(8,128)(2,1)S(1)}, u32[]{:S(2)}, u32[]{:S(2)}) collective-permute-start(bf16[2,2,4,16,1024]{4,3,2,1,0:T(8,128)(2,1)S(1)} %pad_maximum_fusion.refs_0_), channel_id=1, source_target_pairs={{0,1},{1,0},{2,3},{3,2},{4,5},{5,4},{6,7},{7,6},{8,9},{9,8},{10,11... | collective-permute-start | bytes 1572872 | tf_op jit(solution)/shard_map/ppermute | solution.py:657
  81.7 22.7 %collective-permute-start.20 = (bf16[2,2,4,16,1024]{4,3,2,1,0:T(8,128)(2,1)S(1)}, bf16[2,2,4,16,1024]{4,3,2,1,0:T(8,128)(2,1)S(1)}, u32[]{:S(2)}, u32[]{:S(2)}) collective-permute-start(bf16[2,2,4,16,1024]{4,3,2,1,0:T(8,128)(2,1)S(1)} %pad_maximum_fusion.3.refs_4_), channel_id=1, source_target_pairs={{0,1},{1,0},{2,3},{3,2},{4,5},{5,4},{6,7},{7,6},{8,9},{9,8},{10,11... | collective-permute-start | bytes 1572872 | tf_op jit(solution)/shard_map/ppermute | solution.py:657
  104.5 2.4 collective-permute-start.21
  105.4 2.3 collective-permute-start.22
  105.4 3.0 %collective-permute-start.23 = (bf16[2,2,4,16,1024]{4,3,2,1,0:T(8,128)(2,1)S(1)}, bf16[2,2,4,16,1024]{4,3,2,1,0:T(8,128)(2,1)S(1)}, u32[]{:S(2)}, u32[]{:S(2)}) collective-permute-start(bf16[2,2,4,16,1024]{4,3,2,1,0:T(8,128)(2,1)S(1)} %collective-permute-done.18.refs_6_), channel_id=1, source_target_pairs={{0,1},{1,0},{2,3},{3,2},{4,5},{5,4},{6,7},{7,6},{8,9},{9,8},{10,11... | collective-permute-start | bytes 1572872 | tf_op jit(solution)/shard_map/ppermute | solution.py:657
  112.9 6.0 %copy-start.15 = (s32[128,1,2]{0,2,1:T(2,128)S(1)}, s32[128,1,2]{0,2,1:T(2,128)}, u32[]{:S(2)}) copy-start(s32[128,1,2]{0,2,1:T(2,128)} %param.16) | copy-start | bytes 3076
  112.9 29.9 %copy-start.11 = (f32[2048]{0:T(1024)S(1)}, f32[2048]{0:T(1024)}, u32[]{:S(2)}) copy-start(f32[2048]{0:T(1024)} %param.15) | copy-start | bytes 24580
  112.9 29.9 %all-to-all-start.1 = ((bf16[4,128,2048]{2,1,0:T(8,128)(2,1)}), bf16[4,128,2048]{2,1,0:T(8,128)(2,1)S(1)}, u32[]{:S(2)}, u32[]{:S(2)}) async-start(bf16[4,128,2048]{2,1,0:T(8,128)(2,1)} %bitcast.62), calls=%async_computation.1 | async-start | bytes 4194304 | tf_op jit(solution)/shard_map/all_to_all | solution.py:749
  142.8 1.0 copy-start.5
  143.8 10.5 %copy-start.16 = (f32[128,1,2]{0,2,1:T(2,128)S(1)}, f32[128,1,2]{0,2,1:T(2,128)}, u32[]{:S(2)}) copy-start(f32[128,1,2]{0,2,1:T(2,128)} %param.17) | copy-start | bytes 3076
  144.7 1.0 copy-start.2
  145.7 1.0 copy-start.4
  146.7 0.8 copy-start.12
  147.5 32.2 %copy-start.1 = (bf16[1,512,2048]{2,1,0:T(8,128)(2,1)S(1)}, bf16[1,512,2048]{2,1,0:T(8,128)(2,1)}, u32[]{:S(2)}) copy-start(bf16[1,512,2048]{2,1,0:T(8,128)(2,1)} %param.19) | copy-start | bytes 6291460
  147.5 32.2 %all-to-all-start.2 = ((bf16[8,32,2048]{2,1,0:T(8,128)(2,1)}), bf16[8,32,2048]{2,1,0:T(8,128)(2,1)}, u32[]{:S(2)}, u32[]{:S(2)}) async-start(bf16[8,32,2048]{2,1,0:T(8,128)(2,1)} %bitcast.52), calls=%async_computation.2 | async-start | bytes 2097152 | tf_op jit(solution)/shard_map/all_to_all | solution.py:830
  153.7 31.4 %collective-permute-start.24 = (bf16[128,2048]{1,0:T(8,128)(2,1)}, bf16[128,2048]{1,0:T(8,128)(2,1)}, u32[]{:S(2)}, u32[]{:S(2)}) collective-permute-start(bf16[128,2048]{1,0:T(8,128)(2,1)} %copy-done.12), channel_id=1, source_target_pairs={{0,8},{1,9},{2,10},{3,11},{4,12},{5,13},{6,14},{7,15},{8,0},{9,1},... | collective-permute-start | bytes 1572872 | tf_op jit(solution)/shard_map/ppermute | solution.py:657
  154.5 25.0 %collective-permute-start.25 = (f32[128,4]{1,0:T(8,128)S(1)}, f32[128,4]{1,0:T(8,128)S(1)}, u32[]{:S(2)}, u32[]{:S(2)}) collective-permute-start(f32[128,4]{1,0:T(8,128)S(1)} %pad_maximum_fusion.4), channel_id=1, source_target_pairs={{0,8},{1,9},{2,10},{3,11},{4,12},{5,13},{6,14},{7,15},{8,0},{9,1},... | collective-permute-start | bytes 6152 | tf_op jit(solution)/shard_map/ppermute | solution.py:657
  226.9 32.4 %copy-start.3 = (f32[128,2048]{1,0:T(8,128)S(1)}, f32[128,2048]{1,0:T(8,128)}, u32[]{:S(2)}) copy-start(f32[128,2048]{1,0:T(8,128)} %copy-done.2) | copy-start | bytes 3145732
  227.4 0.8 copy-start.8
  228.2 31.1 %all-to-all-start.5 = ((bf16[8,32,2048]{2,1,0:T(8,128)(2,1)}), bf16[8,32,2048]{2,1,0:T(8,128)(2,1)S(1)}, u32[]{:S(2)}, u32[]{:S(2)}) async-start(bf16[8,32,2048]{2,1,0:T(8,128)(2,1)} %bitcast.34), calls=%async_computation.5 | async-start | bytes 2097152 | tf_op jit(solution)/shard_map/all_to_all | solution.py:830
  233.5 25.0 %collective-permute-start.26 = (bf16[128,2048]{1,0:T(8,128)(2,1)}, bf16[128,2048]{1,0:T(8,128)(2,1)S(1)}, u32[]{:S(2)}, u32[]{:S(2)}) collective-permute-start(bf16[128,2048]{1,0:T(8,128)(2,1)} %copy-done.8), channel_id=1, source_target_pairs={{0,8},{1,9},{2,10},{3,11},{4,12},{5,13},{6,14},{7,15},{8,0},{9,1},... | collective-permute-start | bytes 1572872 | tf_op jit(solution)/shard_map/ppermute | solution.py:657
  258.5 0.8 copy-start.6
  259.3 1.0 copy-start.7

commit v6 on v4

--- a/solution.py
+++ b/solution.py
@@ -11,6 +11,7 @@
 F32 = jnp.float32
 BF16 = jnp.bfloat16
 HIGH_VMEM = 48 * 2**20
+ATTEND_VMEM = 32 * 2**20
 
 
 def in_hbm():
@@ -132,15 +133,18 @@
     chunk,
     width,
     q_hbm,
-    page_a,
-    page_b,
-    page_y,
-    page_c,
-    page_cy,
-    kv_own,
-    kv_y,
-    kv_c,
-    kv_cy,
+    own_pages,
+    y_pages,
+    c_pages,
+    cy_pages,
+    near,
+    far,
+    near_y,
+    far_y,
+    near_c,
+    far_c,
+    near_cy,
+    far_cy,
     o_ref,
     q_ref,
     old_ref,
@@ -152,7 +156,7 @@
     me = lax.axis_index("head")
     members, heads, piece, _ = q_hbm.shape
     length = members * piece
-    planes = kv_own.shape[0]
+    steps = near.shape[0]
     old = old_ref.shape[0]
     earlier_group = me // members > 0
     core = lax.rem(me, 2)
@@ -167,18 +171,24 @@
         for head in range(heads):
             bring(q_hbm.at[member, head], q_ref.at[head, pl.ds(member * piece, piece)], 0)
     place = 0
-    for page in (page_a, page_b, page_y, page_c, page_cy):
+    for page in (own_pages, y_pages, c_pages, cy_pages):
         count = page.shape[0]
         bring(page, old_ref.at[pl.ds(place, count)], 1)
         place += count
-    for flip, pieces_of in ((0, kv_own), (2, kv_y), (1, kv_c), (3, kv_cy)):
-        for t in range(planes):
-            number = jnp.bitwise_and(
-                jnp.bitwise_xor(me, flip ^ (t * (members // 2))), members - 1
-            )
-            start = pl.multiple_of(number * piece, piece)
-            area = 0 if t * (members // 2) >= members else length
-            bring(pieces_of.at[t], kv_ref.at[pl.ds(area + start, piece)], 2)
+    for flip, group in (
+        (0, (near, far)),
+        (2, (near_y, far_y)),
+        (1, (near_c, far_c)),
+        (3, (near_cy, far_cy)),
+    ):
+        for other, pieces_of in enumerate(group):
+            for t in range(steps):
+                number = jnp.bitwise_and(
+                    jnp.bitwise_xor(me, flip ^ (t * (members // 2))), members - 1
+                )
+                start = pl.multiple_of(number * piece, piece)
+                area = 0 if other else length
+                bring(pieces_of.at[t], kv_ref.at[pl.ds(area + start, piece)], 2)
     for copy in copies:
         copy.wait()
     scale = width**-0.5
@@ -269,7 +279,7 @@
             pltpu.VMEM((block, keys), F32),
             pltpu.SemaphoreType.DMA((3,)),
         ],
-        compiler_params=pltpu.CompilerParams(vmem_limit_bytes=HIGH_VMEM),
+        compiler_params=pltpu.CompilerParams(vmem_limit_bytes=ATTEND_VMEM),
         cost_estimate=pl.CostEstimate(
             flops=4 * heads * length * (keys - length // 2) * width,
             bytes_accessed=4 * (heads * length + keys) * width,
@@ -486,94 +496,179 @@
     return hit.astype(BF16)
 
 
-def route_pair_kernel(parts_ref, resid_ref, gain_ref, slots_ref, stream_ref, normed_ref, out_ref):
-    projected = parts_ref[0].astype(F32)
-    for p in range(1, parts_ref.shape[0]):
-        projected = projected + parts_ref[p].astype(F32)
-    stream = resid_ref[...].astype(F32) + projected
-    stream_ref[...] = stream
-    normed = stream * lax.rsqrt(jnp.mean(stream * stream, 1, keepdims=True) + eps_norm)
-    normed = (normed * gain_ref[...]).astype(BF16)
-    normed_ref[...] = normed
-    matrix = slot_matrix(slots_ref, out_ref.shape[0], stream.shape[0])
-    out_ref[...] = jnp.dot(matrix, normed, preferred_element_type=F32).astype(BF16)
+def by_copies(body, name, inputs, outputs, flops, bytes_accessed, transcendentals=0):
+    count = len(inputs)
+
+    def kernel(*refs):
+        ins, outs = refs[:count], refs[count : count + len(outputs)]
+        rest = refs[count + len(outputs) :]
+        in_vm, out_vm, sems = rest[:count], rest[count:-1], rest[-1]
+        copies = [
+            pltpu.make_async_copy(ins[k], in_vm[k], sems.at[k]) for k in range(count)
+        ]
+        for copy in copies:
+            copy.start()
+        body(lambda k: copies[k].wait(), in_vm, out_vm)
+        back = [
+            pltpu.make_async_copy(out_vm[k], outs[k], sems.at[count + k])
+            for k in range(len(outputs))
+        ]
+        for copy in back:
+            copy.start()
+        for copy in back:
+            copy.wait()
+
+    shapes = [jax.ShapeDtypeStruct(shape, dtype) for shape, dtype in outputs]
+    return pl.pallas_call(
+        kernel,
+        out_shape=shapes,
+        in_specs=[in_hbm()] * count,
+        out_specs=[in_hbm()] * len(outputs),
+        scratch_shapes=[pltpu.VMEM(x.shape, x.dtype) for x in inputs]
+        + [pltpu.VMEM(shape, dtype) for shape, dtype in outputs]
+        + [pltpu.SemaphoreType.DMA((count + len(outputs),))],
+        compiler_params=pltpu.CompilerParams(vmem_limit_bytes=HIGH_VMEM),
+        cost_estimate=pl.CostEstimate(
+            flops=flops, bytes_accessed=bytes_accessed, transcendentals=transcendentals
+        ),
+        name=name,
+    )(*inputs)
 
 
 def route_pair(parts, resid, gain, slots_of, slots):
     planes, rows, model = parts.shape
+
+    def body(wait, ins, outs):
+        parts_ref, resid_ref, gain_ref, slots_ref = ins
+        stream_ref, normed_ref, out_ref = outs
+        wait(0)
+        projected = parts_ref[0].astype(F32)
+        for p in range(1, planes):
+            projected = projected + parts_ref[p].astype(F32)
+        wait(1)
+        stream = resid_ref[...].astype(F32) + projected
+        stream_ref[...] = stream
+        normed = stream * lax.rsqrt(jnp.mean(stream * stream, 1, keepdims=True) + eps_norm)
+        wait(2)
+        normed = (normed * gain_ref[...]).astype(BF16)
+        normed_ref[...] = normed
+        wait(3)
+        matrix = slot_matrix(slots_ref, slots, rows)
+        out_ref[...] = jnp.dot(matrix, normed, preferred_element_type=F32).astype(BF16)
+
+    return by_copies(
+        body,
+        "route",
+        [parts, resid, gain, slots_of],
+        [((rows, model), F32), ((rows, model), BF16), ((slots, model), BF16)],
+        2 * slots * rows * model,
+        2 * ((planes + 4) * rows + slots) * model,
+    )
+
+
+def spread(given, slots_of, slots):
+    rows, model = given.shape
+
+    def body(wait, ins, outs):
+        wait(1)
+        matrix = slot_matrix(ins[1], slots, rows)
+        wait(0)
+        product = jnp.dot(matrix, ins[0][...], preferred_element_type=F32)
+        outs[0][...] = product.astype(BF16)
+
+    return by_copies(
+        body,
+        "spread",
+        [given, slots_of],
+        [((slots, model), BF16)],
+        2 * slots * rows * model,
+        2 * (rows + slots) * model,
+    )[0]
+
+
+def expert_pair(x, w_in, w_down):
+    rows, model = x.shape
+    hidden_width = w_down.shape[0]
+    parts = 4
+    depth = model // parts
+
+    def kernel(x_hbm, in_hbm_ref, down_hbm, o_hbm, x_ref, in_ref, down_ref, o_ref, sems):
+        bring_x = pltpu.make_async_copy(x_hbm, x_ref, sems.at[parts])
+        bring_x.start()
+        bring_in = []
+        for k in range(parts):
+            at = pl.ds(k * depth, depth)
+            bring_in.append(pltpu.make_async_copy(in_hbm_ref.at[at], in_ref.at[at], sems.at[k]))
+            bring_in[k].start()
+        bring_down = pltpu.make_async_copy(down_hbm, down_ref, sems.at[parts + 1])
+        bring_down.start()
+        bring_x.wait()
+        inner = None
+        for k in range(parts):
+            bring_in[k].wait()
+            at = pl.ds(k * depth, depth)
+            part = jnp.dot(x_ref[:, at], in_ref[at, :], preferred_element_type=F32)
+            inner = part if inner is None else inner + part
+        gate = inner[:, :hidden_width]
+        hidden = (gate / (1.0 + jnp.exp(-gate)) * inner[:, hidden_width:]).astype(BF16)
+        bring_down.wait()
+        o_ref[...] = jnp.dot(hidden, down_ref[...], preferred_element_type=F32).astype(BF16)
+        back = pltpu.make_async_copy(o_ref, o_hbm, sems.at[parts + 2])
+        back.start()
+        back.wait()
+
     return pl.pallas_call(
-        route_pair_kernel,
-        out_shape=(
-            jax.ShapeDtypeStruct((rows, model), F32),
-            jax.ShapeDtypeStruct((rows, model), BF16),
-            jax.ShapeDtypeStruct((slots, model), BF16),
-        ),
-        in_specs=[in_vmem()] * 4,
-        out_specs=(in_vmem(), in_vmem(), in_vmem()),
+        kernel,
+        out_shape=jax.ShapeDtypeStruct((rows, model), BF16),
+        in_specs=[in_hbm()] * 3,
+        out_specs=in_hbm(),
+        scratch_shapes=[
+            pltpu.VMEM((rows, model), BF16),
+            pltpu.VMEM(w_in.shape, BF16),
+            pltpu.VMEM(w_down.shape, BF16),
+            pltpu.VMEM((rows, model), BF16),
+            pltpu.SemaphoreType.DMA((parts + 3,)),
+        ],
         compiler_params=pltpu.CompilerParams(vmem_limit_bytes=HIGH_VMEM),
         cost_estimate=pl.CostEstimate(
-            flops=2 * slots * rows * model,
-            bytes_accessed=2 * ((planes + 4) * rows + slots) * model,
-            transcendentals=0,
-        ),
-        name="route",
-    )(parts, resid, gain, slots_of)
-
-
-def spread_kernel(rows_ref, slots_ref, out_ref):
-    matrix = slot_matrix(slots_ref, out_ref.shape[0], rows_ref.shape[0])
-    out_ref[...] = jnp.dot(matrix, rows_ref[...], preferred_element_type=F32).astype(BF16)
-
-
-def spread(rows, slots_of, slots):
-    count, model = rows.shape
-    return pl.pallas_call(
-        spread_kernel,
-        out_shape=jax.ShapeDtypeStruct((slots, model), BF16),
-        in_specs=[in_vmem()] * 2,
-        out_specs=in_vmem(),
-        compiler_params=pltpu.CompilerParams(vmem_limit_bytes=HIGH_VMEM),
-        cost_estimate=pl.CostEstimate(
-            flops=2 * slots * count * model,
-            bytes_accessed=2 * (count + slots) * model,
-            transcendentals=0,
-        ),
-        name="spread",
-    )(rows, slots_of)
-
-
-def gather_kernel(back_ref, slots_ref, gates_ref, *refs):
-    o_ref = refs[-1]
-    shape = (slots_ref.shape[0], back_ref.shape[0])
-    place = lax.broadcasted_iota(jnp.int32, shape, 1).astype(F32)
-    total = None
-    for k in range(slots_ref.shape[1]):
-        pick = (place == slots_ref[:, k : k + 1]).astype(BF16)
-        picked = jnp.dot(pick, back_ref[...], preferred_element_type=F32)
-        part = picked * gates_ref[:, k : k + 1]
-        total = part if total is None else total + part
-    if len(refs) > 1:
-        total = refs[0][...] + (total + refs[1][...].astype(F32))
-    o_ref[...] = total.astype(BF16)
+            flops=6 * rows * model * hidden_width,
+            bytes_accessed=2 * (2 * rows * model + 3 * model * hidden_width),
+            transcendentals=rows * hidden_width,
+        ),
+        name="expert",
+    )(x, w_in, w_down)
 
 
 def gather(back, slots_of, gates, stream, partial):
     slots, model = back.shape
     rows, top = slots_of.shape
     more = [] if stream is None else [stream, partial]
-    return pl.pallas_call(
-        gather_kernel,
-        out_shape=jax.ShapeDtypeStruct((rows, model), BF16),
-        in_specs=[in_vmem()] * (3 + len(more)),
-        out_specs=in_vmem(),
-        compiler_params=pltpu.CompilerParams(vmem_limit_bytes=HIGH_VMEM),
-        cost_estimate=pl.CostEstimate(
-            flops=2 * top * slots * rows * model,
-            bytes_accessed=2 * (slots + 4 * rows) * model,
-            transcendentals=0,
-        ),
-        name="gather",
-    )(back, slots_of, gates, *more)
+
+    def body(wait, ins, outs):
+        back_ref, slots_ref, gates_ref = ins[:3]
+        for k in (1, 2, 0):
+            wait(k)
+        place = lax.broadcasted_iota(jnp.int32, (rows, slots), 1).astype(F32)
+        total = None
+        for k in range(top):
+            pick = (place == slots_ref[:, k : k + 1]).astype(BF16)
+            picked = jnp.dot(pick, back_ref[...], preferred_element_type=F32)
+            part = picked * gates_ref[:, k : k + 1]
+            total = part if total is None else total + part
+        if more:
+            wait(3)
+            wait(4)
+            total = ins[3][...] + (total + ins[4][...].astype(F32))
+        outs[0][...] = total.astype(BF16)
+
+    return by_copies(
+        body,
+        "gather",
+        [back, slots_of, gates] + more,
+        [((rows, model), BF16)],
+        2 * top * slots * rows * model,
+        2 * (slots + 4 * rows) * model,
+    )[0]
 
 
 def flipped(value, axis, mask):
@@ -581,7 +676,7 @@
     return lax.ppermute(value, axis, pairs)
 
 
-def parts_in_pairs(queries, new_kv, cache, w_out):
+def parts_in_pairs(queries, new_kv, cache, w_out, other):
     n = lax.axis_size("head")
     local_rows, _, heads, width = queries.shape
     pair_heads = new_kv.shape[2]
@@ -595,63 +690,59 @@
     y = (me // 2) % 2
     group_sets = [[g * members + m for m in range(members)] for g in range(n // members)]
 
-    query_slots = queries.reshape(local_rows, heads, width).transpose(1, 0, 2)
-    query_slots = query_slots.reshape(members, heads // members, local_rows, width)
-    q = lax.all_to_all(
-        query_slots, "head", split_axis=0, concat_axis=0, tiled=True, axis_index_groups=group_sets
-    )
-
-    def page_target(source, other):
-        p, plane, rest = source // members, (source // plane_bit) % 2, source % plane_bit
-        return (plane ^ other) * members + p * plane_bit + rest
-
-    page_a, page_b = (
-        lax.ppermute(cache[0], "head", [(d, page_target(d, other)) for d in range(n)])
-        for other in range(2)
-    )
     kv_heads = new_kv.reshape(local_rows, pair_heads, 2 * width).transpose(1, 0, 2)
     kv_same = lax.dynamic_index_in_dim(kv_heads, b, 0, keepdims=False)
     kv_other = lax.dynamic_index_in_dim(kv_heads, 1 - b, 0, keepdims=False)
-    kv_own = [kv_same]
-    for t in range(1, planes):
-        kv_own.append(flipped(kv_other if t % 2 else kv_same, "head", t * plane_bit))
+    page = cache[0]
+    first = flipped(jnp.concatenate([kv_other, page], 0), "head", plane_bit)
 
     columns = model // 2
     w = lax.dynamic_slice_in_dim(w_out, lax.axis_index("grp") * columns, columns, 2)
     w = w.reshape(2, 2, heads // 4, share, columns)
     w_keep = lax.dynamic_index_in_dim(w, y, 1, keepdims=False)
     w_give = lax.dynamic_index_in_dim(w, 1 - y, 1, keepdims=False)
-
-    (page_a, page_b), w_give = lax.optimization_barrier(((page_a, page_b), w_give))
-    own_pages = jnp.concatenate([page_a, page_b], 0)
-    pages_y = flipped(own_pages, "head", 2)
+    query_slots = queries.reshape(local_rows, heads, width).transpose(1, 0, 2)
+    query_slots = query_slots.reshape(members, heads // members, local_rows, width)
+    first, query_slots, w_give = lax.optimization_barrier((first, query_slots, w_give))
+
+    near = jnp.stack([kv_same, first[:local_rows]], 0)
+    near_pages = jnp.concatenate([page, first[local_rows:]], 0)
+    far = flipped(near, "head", members)
+    has_pages = [d for d in range(n) if d // members == (d // plane_bit) % 2]
+    far_pages = lax.ppermute(near_pages, "head", [(d, d ^ members) for d in has_pages])
+    near_y = flipped(near, "head", 2)
     w_got = flipped(w_give, "head", 2)
-    kv_own, w_got = lax.optimization_barrier((kv_own, w_got))
-    kv_own = jnp.stack(kv_own, 0)
-    kv_y = flipped(kv_own, "head", 2)
+    q = lax.all_to_all(
+        query_slots, "head", split_axis=0, concat_axis=0, tiled=True, axis_index_groups=group_sets
+    )
+    far, far_pages, w_got = lax.optimization_barrier((far, far_pages, w_got))
+    own_pages = jnp.where(me // members == b, near_pages, far_pages)
+    y_pages = flipped(own_pages, "head", 2)
+    far_y = flipped(far, "head", 2)
     w_both = jnp.stack([w_keep, w_got], 1)
     w_same = lax.dynamic_index_in_dim(w_both, b, 0, keepdims=False)
     w_other = lax.dynamic_index_in_dim(w_both, 1 - b, 0, keepdims=False)
-    w_far = [
-        flipped(w_other if t % 2 else w_same, "head", t * plane_bit) for t in range(1, planes)
-    ]
-    w_near = jnp.stack([w_same, w_far[0]], 0)
+    w_near = jnp.stack([w_same, flipped(w_other, "head", plane_bit)], 0)
+    w_far = flipped(w_near, "head", members)
+    near_c = flipped(near, "head", 1)
+    far_c = flipped(far, "head", 1)
+    c_pages = flipped(own_pages, "head", 1)
+    y_pages, far_y, w_near = lax.optimization_barrier((y_pages, far_y, w_near))
+    near_cy = flipped(near_y, "head", 1)
+    far_cy = flipped(far_y, "head", 1)
+    cy_pages = flipped(y_pages, "head", 1)
     w_near_x = flipped(w_near, "grp", 1)
-    pages_y, kv_y, w_far = lax.optimization_barrier((pages_y, kv_y, w_far[1:]))
-    pages_c = flipped(own_pages, "head", 1)
-    kv_c = flipped(kv_own, "head", 1)
-    pages_cy = flipped(pages_y, "head", 1)
-    kv_cy = flipped(kv_y, "head", 1)
-    w_far = jnp.stack(w_far, 0)
     q, w_far = lax.optimization_barrier((q, w_far))
     w_far_x = flipped(w_far, "grp", 1)
     w_near_c = flipped(w_near, "head", 1)
     w_far_c = flipped(w_far, "head", 1)
     a = attend_pair(
-        q, (page_a, page_b, pages_y, pages_c, pages_cy), (kv_own, kv_y, kv_c, kv_cy)
-    )
-    a, w_near_x, w_far_x, w_near_c, w_far_c = lax.optimization_barrier(
-        (a, w_near_x, w_far_x, w_near_c, w_far_c)
+        q,
+        (own_pages, y_pages, c_pages, cy_pages),
+        (near, far, near_y, far_y, near_c, far_c, near_cy, far_cy),
+    )
+    a, w_near_x, w_far_x, w_near_c, w_far_c, other = lax.optimization_barrier(
+        (a, w_near_x, w_far_x, w_near_c, w_far_c, other)
     )
     w_near_cx = flipped(w_near_x, "head", 1)
     w_far_cx = flipped(w_far_x, "head", 1)
@@ -675,7 +766,7 @@
         tiled=True,
         axis_index_groups=quads,
     )
-    return parts[None]
+    return parts, other
 
 
 def parts_in_planes(queries, new_kv, cache, w_out):
@@ -738,10 +829,9 @@
     return parts.reshape(seqs, planes_of_seq, local_rows, model)
 
 
-def route_in_pairs(parts, resid, norm_gain, slots_of, gates, w_in, w_down, capacity, members):
+def route_in_pairs(parts, resid, norm_gain, own, other, top, w_in, w_down, capacity, members):
     n = lax.axis_size("head")
     local_rows, seqs, model = resid.shape
-    top = slots_of.shape[1]
     me = lax.axis_index("head")
     group_sets = [[g * members + m for m in range(members)] for g in range(n // members)]
     group_slots = members * capacity
@@ -753,8 +843,6 @@
         )
         return value.reshape(group_slots, model)
 
-    own = jnp.concatenate([slots_of.astype(F32), gates], 1)
-    other = flipped(own, "head", members)
     first = ((me // members) * group_slots).astype(F32)
     slots_own, gates_own = own[:, :top] - first, own[:, top:]
     slots_other, gates_other = other[:, :top] - first, other[:, top:]
@@ -763,9 +851,11 @@
         parts, resid.reshape(local_rows, model), norm_gain[None, :], slots_own.T, group_slots
     )
     normed_other = flipped(normed, "head", members)
-    answer_own = expert(around(out_own), w_in, w_down)
+    arrived_own = around(out_own)
+    normed_other, arrived_own = lax.optimization_barrier((normed_other, arrived_own))
+    answer_own = expert_pair(arrived_own, w_in, w_down)
     out_other = spread(normed_other, slots_other.T, group_slots)
-    answer_other = expert(around(out_other), w_in, w_down)
+    answer_other = expert_pair(around(out_other), w_in, w_down)
     partial = gather(around(answer_other), slots_other, gates_other, None, None)
     partial, answer_own = lax.optimization_barrier((partial, answer_own))
     partial = flipped(partial, "head", members)
@@ -786,10 +876,9 @@
         and n == heads == 2 * members
         and members == 8
         and cache.shape[0] == 1
+        and w_in.shape[0] == 1
         and w_out.shape[1] % 16 == 0
     )
-    plan = parts_in_pairs if in_pairs else parts_in_planes
-    parts = plan(queries, new_kv, cache, w_out)
 
     top = expert_ids.shape[2]
     experts = w_in.shape[0] * n
@@ -801,10 +890,14 @@
     before = jnp.cumsum(named, 0) - named
     slots_of = ids * capacity + jnp.sum(onehot * before[:, None, :], 2)
     slots = experts * capacity
-    if in_pairs and w_in.shape[0] == 1:
+    if in_pairs:
+        own = jnp.concatenate([slots_of.astype(F32), gates], 1)
+        other = flipped(own, "head", members)
+        parts, other = parts_in_pairs(queries, new_kv, cache, w_out, other)
         return route_in_pairs(
-            parts[0], resid, norm_gain, slots_of, gates, w_in[0], w_down[0], capacity, members
+            parts, resid, norm_gain, own, other, top, w_in[0], w_down[0], capacity, members
         )
+    parts = parts_in_planes(queries, new_kv, cache, w_out)
     stream, outgoing = route(
         parts, resid.transpose(1, 0, 2), norm_gain[None, :], slots_of.T, slots
     )

time: 266 us -> 263 us (0.989)
  waiting for transfers between devices: 138 us -> 124 us
  other arithmetic: 0.61 us -> 6.78 us
  local copies, waits for them, and re-layouts: 14.3 us -> 18.1 us
  Pallas kernels: 32.8 us -> 35.8 us
    ppermute x2 -> x1, waiting for transfers between devices: 16.6 us -> 0.01 us  [parts_in_pairs(): lax.ppermute(near_pages, 'head', [(d, d ^ members) for d in has_pages])]
    ppermute x23 -> x24, waiting for transfers between devices: 84.6 us -> 92.6 us  [flipped(): return lax.ppermute(value, axis, pairs)]
    all_to_all x3, waiting for transfers between devices: 13.5 us -> 7.51 us  [around(): lax.all_to_all(value, 'head', split_axis=0, concat_axis=0, tiled=True, ax...]
    all_to_all x1, starting transfers between devices: 4.64 us -> 9.08 us  [parts_in_pairs(): lax.all_to_all(query_slots, 'head', split_axis=0, concat_axis=0, tiled=Tr...]
    ppermute x23 -> x24, starting transfers between devices: 26.3 us -> 27 us  [flipped(): return lax.ppermute(value, axis, pairs)]
    unnamed x39 -> x52, local copies, waits for them, and re-layouts: 9.83 us -> 10.4 us
  transfers between devices with their start and end apart: 30 -> 30, of which waited for: 14 -> 13; matrix products, arithmetic and copies ran while one was open for 1% -> 4% of each run, Pallas kernels for 9% -> 8%
where the time goes in v6:
time: 263 us; the launch traced here: 261 us
  waiting for transfers between devices  124 us (47%)
  starting transfers between devices  58.6 us (22%)
  Pallas kernels  35.8 us (14%)
  local copies, waits for them, and re-layouts  18.1 us (7%)
  blocking collectives  17.5 us (7%)
  other arithmetic  6.78 us (3%)
    ppermute x24, waiting for transfers between devices, flipped(): return lax.ppermute(value, axis, pairs)  92.6 us
    ppermute x24, starting transfers between devices, flipped(): return lax.ppermute(value, axis, pairs)  27 us
    all_to_all x1, waiting for transfers between devices, parts_in_pairs(): lax.all_to_all(partial.reshape(members // 2, local_rows, model), 'head',...  23.8 us
    all_to_all x1, blocking collectives, around(): lax.all_to_all(value, 'head', split_axis=0, concat_axis=0, tiled=True, ax...  17.5 us
    all_to_all x3, starting transfers between devices, around(): lax.all_to_all(value, 'head', split_axis=0, concat_axis=0, tiled=True, ax...  17.5 us
    pallas_call x1, Pallas kernels, attend_pair(): pl.pallas_call(functools.partial(attend_pair_kernel, block, chunk, width)...  15.8 us
    unnamed x52, local copies, waits for them, and re-layouts  10.4 us
    all_to_all x1, starting transfers between devices, parts_in_pairs(): lax.all_to_all(query_slots, 'head', split_axis=0, concat_axis=0, tiled=Tr...  9.08 us
  transfers between devices with their start and end apart: 30, of which 13 were waited for; matrix products, arithmetic and copies ran while one was open for 4% of the time, Pallas kernels for 8%

profile of v6, /device:TPU:13, one launch (start us, length us, event | category | flops | bytes accessed | tf_op | source)
XLA Modules:
  0.0 261.2 jit_solution(15823126467442250688)
XLA Ops:
  0.0 1.7 constant_dynamic-slice_fusion
  1.8 1.0 pad_maximum_fusion.2
  3.0 1.3 copy.34
  5.2 7.7 %collective-permute-done = bf16[384,512]{1,0:T(8,128)(2,1)} collective-permute-done((bf16[384,512]{1,0:T(8,128)(2,1)S(1)}, bf16[384,512]{1,0:T(8,128)(2,1)}, u32[]{:S(2)}, u32[]{:S(2)}) %collective-permute-start) | collective-permute-done | bytes 393248 | tf_op jit(solution)/shard_map/ppermute | solution.py:676
  12.9 1.0 slice.16
  15.4 1.3 collective-permute-start.2
  16.7 9.1 %all-to-all-start = ((bf16[8,2,128,256]{3,2,1,0:T(8,128)(2,1)}), bf16[8,2,128,256]{3,2,1,0:T(8,128)(2,1)S(1)}, u32[]{:S(2)}, u32[]{:S(2)}) async-start(bf16[8,2,128,256]{3,2,1,0:T(8,128)(2,1)} %bitcast.4), calls=%async_computation | async-start | bytes 2097152 | tf_op jit(solution)/shard_map/all_to_all | solution.py:715
  27.5 19.7 %collective-permute-done.1.far = bf16[2,128,512]{2,1,0:T(8,128)(2,1)S(1)} collective-permute-done((bf16[2,128,512]{2,1,0:T(8,128)(2,1)S(1)}, bf16[2,128,512]{2,1,0:T(8,128)(2,1)S(1)}, u32[]{:S(2)}, u32[]{:S(2)}) %collective-permute-start.1) | collective-permute-done | bytes 262176 | tf_op jit(solution)/shard_map/ppermute | solution.py:676
  47.2 1.1 fusion.2
  48.4 1.3 broadcast_select_fusion.own_pages
  50.0 3.7 %collective-permute-done.4 = bf16[2,4,16,1024]{3,2,1,0:T(8,128)(2,1)S(1)} collective-permute-done((bf16[2,4,16,1024]{3,2,1,0:T(8,128)(2,1)S(1)}, bf16[2,4,16,1024]{3,2,1,0:T(8,128)(2,1)S(1)}, u32[]{:S(2)}, u32[]{:S(2)}) %collective-permute-start.4) | collective-permute-done | bytes 262176 | tf_op jit(solution)/shard_map/ppermute | solution.py:676
  53.7 1.5 collective-permute-start.5
  55.4 1.2 collective-permute-start.10
  56.6 4.0 %collective-permute-start.11 = (bf16[2,128,512]{2,1,0:T(8,128)(2,1)S(1)}, bf16[2,128,512]{2,1,0:T(8,128)(2,1)}, u32[]{:S(2)}, u32[]{:S(2)}) collective-permute-start(bf16[2,128,512]{2,1,0:T(8,128)(2,1)S(1)} %pad_maximum_fusion.3.near), channel_id=1, source_target_pairs={{0,1},{1,0},{2,3},{3,2},{4,5},{5,4},{6,7},{7,6},{8,9},{9,8},{10,11... | collective-permute-start | bytes 786440 | tf_op jit(solution)/shard_map/ppermute | solution.py:676
  60.8 5.6 %collective-permute-done.7.far_y = bf16[2,128,512]{2,1,0:T(8,128)(2,1)} collective-permute-done((bf16[2,128,512]{2,1,0:T(8,128)(2,1)}, bf16[2,128,512]{2,1,0:T(8,128)(2,1)}, u32[]{:S(2)}, u32[]{:S(2)}) %collective-permute-start.7) | collective-permute-done | bytes 262176 | tf_op jit(solution)/shard_map/ppermute | solution.py:676
  66.4 6.2 %collective-permute-start.8 = (bf16[512,512]{1,0:T(8,128)(2,1)S(1)}, bf16[512,512]{1,0:T(8,128)(2,1)}, u32[]{:S(2)}, u32[]{:S(2)}) collective-permute-start(bf16[512,512]{1,0:T(8,128)(2,1)S(1)} %broadcast_select_fusion.own_pages), channel_id=1, source_target_pairs={{0,1},{1,0},{2,3},{3,2},{4,5},{5,4},{6,7},{7,6},{8,9},{9,8},{10,11... | collective-permute-start | bytes 1572872 | tf_op jit(solution)/shard_map/ppermute | solution.py:676
  76.0 1.2 collective-permute-done.5.refs_4_
  77.2 1.3 collective-permute-start.14
  80.2 3.2 %collective-permute-start.19 = (f32[128,4]{1,0:T(8,128)}, f32[128,4]{1,0:T(8,128)S(1)}, u32[]{:S(2)}, u32[]{:S(2)}) collective-permute-start(f32[128,4]{1,0:T(8,128)} %pad_maximum_fusion.4), channel_id=1, source_target_pairs={{0,8},{1,9},{2,10},{3,11},{4,12},{5,13},{6,14},{7,15},{8,0},{9,1},... | collective-permute-start | bytes 6152 | tf_op jit(solution)/shard_map/ppermute | solution.py:676
  83.4 1.2 collective-permute-start.15
  86.7 15.8 %attend.1.a_ref = bf16[2,512,512]{2,1,0:T(8,128)(2,1)S(1)} custom-call(bf16[8,2,128,256]{3,2,1,0:T(8,128)(2,1)S(1)} %all-to-all-done.q_hbm, bf16[512,512]{1,0:T(8,128)(2,1)S(1)} %broadcast_select_fusion.own_pages, bf16[512,512]{1,0:T(8,128)(2,1)} %collective-permute-done.6.y_pages, bf16[512,512]{1,0:T(8,128)(2,1)} %collective-permute-done.8.c_pages, ...), custom_call_target="tpu_custom_call" | custom-call | flops 7516192768 | bytes 6291456 | tf_op jit(solution)/shard_map/attend/pallas_call | solution.py:269
  102.6 5.3 %collective-permute-done.16.refs_6_ = bf16[2,2,4,16,1024]{4,3,2,1,0:T(8,128)(2,1)S(1)} collective-permute-done((bf16[2,2,4,16,1024]{4,3,2,1,0:T(8,128)(2,1)}, bf16[2,2,4,16,1024]{4,3,2,1,0:T(8,128)(2,1)S(1)}, u32[]{:S(2)}, u32[]{:S(2)}) %collective-permute-start.16) | collective-permute-done | bytes 524320 | tf_op jit(solution)/shard_map/ppermute | solution.py:676
  107.9 1.2 collective-permute-start.20
  109.6 1.0 collective-permute-done.20.got_ref
  112.1 5.2 %project.1 = bf16[512,2048]{1,0:T(8,128)(2,1)} custom-call(bf16[2,512,512]{2,1,0:T(8,128)(2,1)S(1)} %attend.1.a_ref, bf16[512,512]{1,0:T(8,128)(2,1)S(1)} %collective-permute-done.20.got_ref, bf16[2,2,4,16,1024]{4,3,2,1,0:T(8,128)(2,1)S(1)} %pad_maximum_fusion.1.refs_0_, bf16[2,2,4,16,1024]{4,3,2,1,0:T(8,128)(2,1)S(1)} %collective-permute-done.17.refs_1_, ...), custom_call_target="tpu_custom_call" | custom-call | flops 2147483648 | bytes 7340032 | tf_op jit(solution)/shard_map/project/pallas_call | solution.py:332
  117.3 3.6 %all-to-all-start.1 = ((bf16[4,128,2048]{2,1,0:T(8,128)(2,1)}), bf16[4,128,2048]{2,1,0:T(8,128)(2,1)S(1)}, u32[]{:S(2)}, u32[]{:S(2)}) async-start(bf16[4,128,2048]{2,1,0:T(8,128)(2,1)} %bitcast.61), calls=%async_computation.1 | async-start | bytes 4194304 | tf_op jit(solution)/shard_map/all_to_all | solution.py:761
  121.0 23.8 %all-to-all-done.1.refs_0_ = bf16[4,128,2048]{2,1,0:T(8,128)(2,1)S(1)} async-done(((bf16[4,128,2048]{2,1,0:T(8,128)(2,1)}), bf16[4,128,2048]{2,1,0:T(8,128)(2,1)S(1)}, u32[]{:S(2)}, u32[]{:S(2)}) %all-to-all-start.1) | async-done | bytes 2097184 | tf_op jit(solution)/shard_map/all_to_all | solution.py:761
  144.8 1.0 copy-done.7
  145.8 1.7 route.1
  147.6 1.0 copy-done.4
  148.6 1.0 copy-done.6
  150.3 6.1 %all-to-all-start.2 = ((bf16[8,32,2048]{2,1,0:T(8,128)(2,1)}), bf16[8,32,2048]{2,1,0:T(8,128)(2,1)}, u32[]{:S(2)}, u32[]{:S(2)}) async-start(bf16[8,32,2048]{2,1,0:T(8,128)(2,1)} %bitcast.49), calls=%async_computation.2 | async-start | bytes 2097152 | tf_op jit(solution)/shard_map/all_to_all | solution.py:841
  156.4 1.2 collective-permute-start.23
  157.8 23.4 %collective-permute-done.23.refs_0_ = bf16[128,2048]{1,0:T(8,128)(2,1)} collective-permute-done((bf16[128,2048]{1,0:T(8,128)(2,1)}, bf16[128,2048]{1,0:T(8,128)(2,1)}, u32[]{:S(2)}, u32[]{:S(2)}) %collective-permute-start.23) | collective-permute-done | bytes 524320 | tf_op jit(solution)/shard_map/ppermute | solution.py:676
  181.2 1.6 spread.1
  182.8 17.5 %all_to_all.30 = bf16[8,32,2048]{2,1,0:T(8,128)(2,1)S(1)} all-to-all(bf16[8,32,2048]{2,1,0:T(8,128)(2,1)S(1)} %bitcast.45), channel_id=1, replica_groups={{0,1,2,3,4,5,6,7},{8,9,10,11,12,13,14,15},{16,17,18,19,20,21,22,23},{24..., dimensions={0} | all-to-all | bytes 2097152 | tf_op jit(solution)/shard_map/all_to_all | solution.py:841
  200.3 3.8 %expert.2 = bf16[256,2048]{1,0:T(8,128)(2,1)S(1)} custom-call(bf16[256,2048]{1,0:T(8,128)(2,1)S(1)} %bitcast.48, bf16[2048,1024]{1,0:T(8,128)(2,1)} %bitcast.56, bf16[512,2048]{1,0:T(8,128)(2,1)S(1)} %bitcast.42), custom_call_target="tpu_custom_call" | custom-call | flops 1610612736 | bytes 8388608 | tf_op jit(solution)/shard_map/expert/pallas_call | solution.py:620
  204.2 1.0 copy-done.3
  205.2 6.0 %all-to-all-start.4 = ((bf16[8,32,2048]{2,1,0:T(8,128)(2,1)}), bf16[8,32,2048]{2,1,0:T(8,128)(2,1)}, u32[]{:S(2)}, u32[]{:S(2)}) async-start(bf16[8,32,2048]{2,1,0:T(8,128)(2,1)} %bitcast.47), calls=%async_computation.4 | async-start | bytes 2097152 | tf_op jit(solution)/shard_map/all_to_all | solution.py:841
  211.1 4.1 %expert.3 = bf16[256,2048]{1,0:T(8,128)(2,1)S(1)} custom-call(bf16[256,2048]{1,0:T(8,128)(2,1)} %bitcast.20.x_hbm, bf16[2048,1024]{1,0:T(8,128)(2,1)} %bitcast.57, bf16[512,2048]{1,0:T(8,128)(2,1)S(1)} %bitcast.43), custom_call_target="tpu_custom_call" | custom-call | flops 1610612736 | bytes 8388608 | tf_op jit(solution)/shard_map/expert/pallas_call | solution.py:620
  215.2 1.0 copy-done.2
  216.2 7.5 %all-to-all-done.4 = bf16[8,32,2048]{2,1,0:T(8,128)(2,1)} async-done(((bf16[8,32,2048]{2,1,0:T(8,128)(2,1)}), bf16[8,32,2048]{2,1,0:T(8,128)(2,1)}, u32[]{:S(2)}, u32[]{:S(2)}) %all-to-all-start.4) | async-done | bytes 1048608 | tf_op jit(solution)/shard_map/all_to_all | solution.py:841
  223.7 1.8 gather.2
  226.3 5.5 %all-to-all-start.5 = ((bf16[8,32,2048]{2,1,0:T(8,128)(2,1)}), bf16[8,32,2048]{2,1,0:T(8,128)(2,1)S(1)}, u32[]{:S(2)}, u32[]{:S(2)}) async-start(bf16[8,32,2048]{2,1,0:T(8,128)(2,1)} %bitcast.46), calls=%async_computation.5 | async-start | bytes 2097152 | tf_op jit(solution)/shard_map/all_to_all | solution.py:841
  231.8 2.1 collective-permute-start.24
  233.9 23.4 %collective-permute-done.24.refs_4_ = bf16[128,2048]{1,0:T(8,128)(2,1)S(1)} collective-permute-done((bf16[128,2048]{1,0:T(8,128)(2,1)}, bf16[128,2048]{1,0:T(8,128)(2,1)S(1)}, u32[]{:S(2)}, u32[]{:S(2)}) %collective-permute-start.24) | collective-permute-done | bytes 524320 | tf_op jit(solution)/shard_map/ppermute | solution.py:676
  258.2 1.0 copy-done.9
  259.2 1.8 gather.3
  (99 shorter events, 16.9 us)
Async XLA Ops:
  0.0 4.4 %copy-start = (bf16[16,16,2048]{2,1,0:T(8,128)(2,1)S(1)}, bf16[16,16,2048]{2,1,0:T(8,128)(2,1)}, u32[]{:S(2)}) copy-start(bf16[16,16,2048]{2,1,0:T(8,128)(2,1)} %param.14) | copy-start | bytes 3145732
  0.0 3.0 %copy-start.17 = (bf16[128,1,16,256]{3,2,1,0:T(8,128)(2,1)S(1)}, bf16[128,1,16,256]{3,2,1,0:T(8,128)(2,1)}, u32[]{:S(2)}) copy-start(bf16[128,1,16,256]{3,2,1,0:T(8,128)(2,1)} %param.10) | copy-start | bytes 3145732
  2.7 10.2 %collective-permute-start = (bf16[384,512]{1,0:T(8,128)(2,1)S(1)}, bf16[384,512]{1,0:T(8,128)(2,1)}, u32[]{:S(2)}, u32[]{:S(2)}) collective-permute-start(bf16[384,512]{1,0:T(8,128)(2,1)S(1)} %pad_maximum_fusion.2), channel_id=1, source_target_pairs={{0,4},{1,5},{2,6},{3,7},{4,0},{5,1},{6,2},{7,3},{8,12},{9,13},{10,... | collective-permute-start | bytes 1179656 | tf_op jit(solution)/shard_map/ppermute | solution.py:676
  3.0 11.6 %copy-start.15 = (bf16[1,256,512]{2,1,0:T(8,128)(2,1)S(1)}, bf16[1,256,512]{2,1,0:T(8,128)(2,1)}, u32[]{:S(2)}) copy-start(bf16[1,256,512]{2,1,0:T(8,128)(2,1)} %param.12) | copy-start | bytes 786436
  14.6 12.6 %copy-start.19 = (bf16[2,4,16,1024]{3,2,1,0:T(8,128)(2,1)S(1)}, bf16[2,4,16,1024]{3,2,1,0:T(8,128)(2,1)}, u32[]{:S(2)}) copy-start(bf16[2,4,16,1024]{3,2,1,0:T(8,128)(2,1)} %get-tuple-element.31) | copy-start | bytes 786436
  15.4 31.8 %collective-permute-start.2 = (bf16[512,512]{1,0:T(8,128)(2,1)}, bf16[512,512]{1,0:T(8,128)(2,1)}, u32[]{:S(2)}, u32[]{:S(2)}) collective-permute-start(bf16[512,512]{1,0:T(8,128)(2,1)} %pad_maximum_fusion), channel_id=1, source_target_pairs={{0,8},{1,9},{2,10},{3,11},{12,4},{13,5},{14,6},{15,7},{16,24},{17,... | collective-permute-start | bytes 1572872 | tf_op jit(solution)/shard_map/ppermute | solution.py:712
  16.7 63.4 %all-to-all-start = ((bf16[8,2,128,256]{3,2,1,0:T(8,128)(2,1)}), bf16[8,2,128,256]{3,2,1,0:T(8,128)(2,1)S(1)}, u32[]{:S(2)}, u32[]{:S(2)}) async-start(bf16[8,2,128,256]{3,2,1,0:T(8,128)(2,1)} %bitcast.4), calls=%async_computation | async-start | bytes 2097152 | tf_op jit(solution)/shard_map/all_to_all | solution.py:715
  26.7 33.9 %copy-start.22 = (s32[128,1,2]{0,2,1:T(2,128)S(1)}, s32[128,1,2]{0,2,1:T(2,128)}, u32[]{:S(2)}) copy-start(s32[128,1,2]{0,2,1:T(2,128)} %param.16) | copy-start | bytes 3076
  26.8 20.4 %collective-permute-start.1 = (bf16[2,128,512]{2,1,0:T(8,128)(2,1)S(1)}, bf16[2,128,512]{2,1,0:T(8,128)(2,1)S(1)}, u32[]{:S(2)}, u32[]{:S(2)}) collective-permute-start(bf16[2,128,512]{2,1,0:T(8,128)(2,1)S(1)} %pad_maximum_fusion.3.near), channel_id=1, source_target_pairs={{0,8},{1,9},{2,10},{3,11},{4,12},{5,13},{6,14},{7,15},{8,0},{9,1},... | collective-permute-start | bytes 786440 | tf_op jit(solution)/shard_map/ppermute | solution.py:676
  27.2 20.0 %collective-permute-start.3 = (bf16[2,4,16,1024]{3,2,1,0:T(8,128)(2,1)S(1)}, bf16[2,4,16,1024]{3,2,1,0:T(8,128)(2,1)}, u32[]{:S(2)}, u32[]{:S(2)}) collective-permute-start(bf16[2,4,16,1024]{3,2,1,0:T(8,128)(2,1)S(1)} %copy-done.19), channel_id=1, source_target_pairs={{0,2},{1,3},{2,0},{3,1},{4,6},{5,7},{6,4},{7,5},{8,10},{9,11},{10,... | collective-permute-start | bytes 786440 | tf_op jit(solution)/shard_map/ppermute | solution.py:676
  47.2 6.4 %copy-start.13 = (bf16[2,128,512]{2,1,0:T(8,128)(2,1)}, bf16[2,128,512]{2,1,0:T(8,128)(2,1)S(1)}, u32[]{:S(2)}) copy-start(bf16[2,128,512]{2,1,0:T(8,128)(2,1)S(1)} %collective-permute-done.1.far) | copy-start | bytes 786436
  47.2 28.0 %copy-start.23 = (f32[128,1,2]{0,2,1:T(2,128)S(1)}, f32[128,1,2]{0,2,1:T(2,128)}, u32[]{:S(2)}) copy-start(f32[128,1,2]{0,2,1:T(2,128)} %param.17) | copy-start | bytes 3076
  48.3 5.3 %collective-permute-start.4 = (bf16[2,4,16,1024]{3,2,1,0:T(8,128)(2,1)S(1)}, bf16[2,4,16,1024]{3,2,1,0:T(8,128)(2,1)S(1)}, u32[]{:S(2)}, u32[]{:S(2)}) collective-permute-start(bf16[2,4,16,1024]{3,2,1,0:T(8,128)(2,1)S(1)} %get-tuple-element.56), channel_id=1, source_target_pairs={{0,4},{1,5},{2,6},{3,7},{4,0},{5,1},{6,2},{7,3},{8,12},{9,13},{10,... | collective-permute-start | bytes 786440 | tf_op jit(solution)/shard_map/ppermute | solution.py:676
  49.7 22.9 %collective-permute-start.6 = (bf16[512,512]{1,0:T(8,128)(2,1)S(1)}, bf16[512,512]{1,0:T(8,128)(2,1)}, u32[]{:S(2)}, u32[]{:S(2)}) collective-permute-start(bf16[512,512]{1,0:T(8,128)(2,1)S(1)} %broadcast_select_fusion.own_pages), channel_id=1, source_target_pairs={{0,2},{1,3},{2,0},{3,1},{4,6},{5,7},{6,4},{7,5},{8,10},{9,11},{10,... | collective-permute-start | bytes 1572872 | tf_op jit(solution)/shard_map/ppermute | solution.py:676
  53.7 23.5 %collective-permute-start.5 = (bf16[2,2,4,16,1024]{4,3,2,1,0:T(8,128)(2,1)S(1)}, bf16[2,2,4,16,1024]{4,3,2,1,0:T(8,128)(2,1)}, u32[]{:S(2)}, u32[]{:S(2)}) collective-permute-start(bf16[2,2,4,16,1024]{4,3,2,1,0:T(8,128)(2,1)S(1)} %pad_maximum_fusion.1.refs_0_), channel_id=1, source_target_pairs={{0,8},{1,9},{2,10},{3,11},{4,12},{5,13},{6,14},{7,15},{8,0},{9,1},... | collective-permute-start | bytes 1572872 | tf_op jit(solution)/shard_map/ppermute | solution.py:676
  55.2 11.2 %collective-permute-start.7 = (bf16[2,128,512]{2,1,0:T(8,128)(2,1)}, bf16[2,128,512]{2,1,0:T(8,128)(2,1)}, u32[]{:S(2)}, u32[]{:S(2)}) collective-permute-start(bf16[2,128,512]{2,1,0:T(8,128)(2,1)} %copy-done.13), channel_id=1, source_target_pairs={{0,2},{1,3},{2,0},{3,1},{4,6},{5,7},{6,4},{7,5},{8,10},{9,11},{10,... | collective-permute-start | bytes 786440 | tf_op jit(solution)/shard_map/ppermute | solution.py:676
  55.4 19.9 %collective-permute-start.10 = (bf16[2,128,512]{2,1,0:T(8,128)(2,1)S(1)}, bf16[2,128,512]{2,1,0:T(8,128)(2,1)}, u32[]{:S(2)}, u32[]{:S(2)}) collective-permute-start(bf16[2,128,512]{2,1,0:T(8,128)(2,1)S(1)} %pad_maximum_fusion.3.near), channel_id=1, source_target_pairs={{0,2},{1,3},{2,0},{3,1},{4,6},{5,7},{6,4},{7,5},{8,10},{9,11},{10,... | collective-permute-start | bytes 786440 | tf_op jit(solution)/shard_map/ppermute | solution.py:676
  56.6 19.3 %collective-permute-start.11 = (bf16[2,128,512]{2,1,0:T(8,128)(2,1)S(1)}, bf16[2,128,512]{2,1,0:T(8,128)(2,1)}, u32[]{:S(2)}, u32[]{:S(2)}) collective-permute-start(bf16[2,128,512]{2,1,0:T(8,128)(2,1)S(1)} %pad_maximum_fusion.3.near), channel_id=1, source_target_pairs={{0,1},{1,0},{2,3},{3,2},{4,5},{5,4},{6,7},{7,6},{8,9},{9,8},{10,11... | collective-permute-start | bytes 786440 | tf_op jit(solution)/shard_map/ppermute | solution.py:676
  60.7 11.9 %copy-start.18 = (s32[128,1,2]{2,0,1:T(8,128)}, s32[128,1,2]{2,0,1:T(8,128)S(1)}, u32[]{:S(2)}) copy-start(s32[128,1,2]{2,0,1:T(8,128)S(1)} %copy.36) | copy-start | bytes 3076
  66.4 18.2 %collective-permute-start.8 = (bf16[512,512]{1,0:T(8,128)(2,1)S(1)}, bf16[512,512]{1,0:T(8,128)(2,1)}, u32[]{:S(2)}, u32[]{:S(2)}) collective-permute-start(bf16[512,512]{1,0:T(8,128)(2,1)S(1)} %broadcast_select_fusion.own_pages), channel_id=1, source_target_pairs={{0,1},{1,0},{2,3},{3,2},{4,5},{5,4},{6,7},{7,6},{8,9},{9,8},{10,11... | collective-permute-start | bytes 1572872 | tf_op jit(solution)/shard_map/ppermute | solution.py:676
  72.6 12.8 %collective-permute-start.9 = (bf16[512,512]{1,0:T(8,128)(2,1)}, bf16[512,512]{1,0:T(8,128)(2,1)}, u32[]{:S(2)}, u32[]{:S(2)}) collective-permute-start(bf16[512,512]{1,0:T(8,128)(2,1)} %collective-permute-done.6.y_pages), channel_id=1, source_target_pairs={{0,1},{1,0},{2,3},{3,2},{4,5},{5,4},{6,7},{7,6},{8,9},{9,8},{10,11... | collective-permute-start | bytes 1572872 | tf_op jit(solution)/shard_map/ppermute | solution.py:676
  75.3 4.8 %collective-permute-start.13 = (bf16[2,128,512]{2,1,0:T(8,128)(2,1)}, bf16[2,128,512]{2,1,0:T(8,128)(2,1)}, u32[]{:S(2)}, u32[]{:S(2)}) collective-permute-start(bf16[2,128,512]{2,1,0:T(8,128)(2,1)} %collective-permute-done.10.near_y), channel_id=1, source_target_pairs={{0,1},{1,0},{2,3},{3,2},{4,5},{5,4},{6,7},{7,6},{8,9},{9,8},{10,11... | collective-permute-start | bytes 786440 | tf_op jit(solution)/shard_map/ppermute | solution.py:676
  75.9 7.5 %collective-permute-start.12 = (bf16[2,128,512]{2,1,0:T(8,128)(2,1)}, bf16[2,128,512]{2,1,0:T(8,128)(2,1)}, u32[]{:S(2)}, u32[]{:S(2)}) collective-permute-start(bf16[2,128,512]{2,1,0:T(8,128)(2,1)} %copy-done.13), channel_id=1, source_target_pairs={{0,1},{1,0},{2,3},{3,2},{4,5},{5,4},{6,7},{7,6},{8,9},{9,8},{10,11... | collective-permute-start | bytes 786440 | tf_op jit(solution)/shard_map/ppermute | solution.py:676
  77.2 8.0 %collective-permute-start.14 = (bf16[2,128,512]{2,1,0:T(8,128)(2,1)}, bf16[2,128,512]{2,1,0:T(8,128)(2,1)}, u32[]{:S(2)}, u32[]{:S(2)}) collective-permute-start(bf16[2,128,512]{2,1,0:T(8,128)(2,1)} %collective-permute-done.7.far_y), channel_id=1, source_target_pairs={{0,1},{1,0},{2,3},{3,2},{4,5},{5,4},{6,7},{7,6},{8,9},{9,8},{10,11... | collective-permute-start | bytes 786440 | tf_op jit(solution)/shard_map/ppermute | solution.py:676
  80.2 22.4 %collective-permute-start.19 = (f32[128,4]{1,0:T(8,128)}, f32[128,4]{1,0:T(8,128)S(1)}, u32[]{:S(2)}, u32[]{:S(2)}) collective-permute-start(f32[128,4]{1,0:T(8,128)} %pad_maximum_fusion.4), channel_id=1, source_target_pairs={{0,8},{1,9},{2,10},{3,11},{4,12},{5,13},{6,14},{7,15},{8,0},{9,1},... | collective-permute-start | bytes 6152 | tf_op jit(solution)/shard_map/ppermute | solution.py:676
  83.4 19.2 %collective-permute-start.15 = (bf16[2,2,4,16,1024]{4,3,2,1,0:T(8,128)(2,1)S(1)}, bf16[2,2,4,16,1024]{4,3,2,1,0:T(8,128)(2,1)S(1)}, u32[]{:S(2)}, u32[]{:S(2)}) collective-permute-start(bf16[2,2,4,16,1024]{4,3,2,1,0:T(8,128)(2,1)S(1)} %pad_maximum_fusion.1.refs_0_), channel_id=1, source_target_pairs={{0,16},{16,0},{1,17},{17,1},{2,18},{18,2},{3,19},{19,3},{4,20},{20... | collective-permute-start | bytes 1572872 | tf_op jit(solution)/shard_map/ppermute | solution.py:676
  84.6 18.0 %collective-permute-start.17 = (bf16[2,2,4,16,1024]{4,3,2,1,0:T(8,128)(2,1)S(1)}, bf16[2,2,4,16,1024]{4,3,2,1,0:T(8,128)(2,1)S(1)}, u32[]{:S(2)}, u32[]{:S(2)}) collective-permute-start(bf16[2,2,4,16,1024]{4,3,2,1,0:T(8,128)(2,1)S(1)} %pad_maximum_fusion.1.refs_0_), channel_id=1, source_target_pairs={{0,1},{1,0},{2,3},{3,2},{4,5},{5,4},{6,7},{7,6},{8,9},{9,8},{10,11... | collective-permute-start | bytes 1572872 | tf_op jit(solution)/shard_map/ppermute | solution.py:676
  85.2 22.7 %collective-permute-start.16 = (bf16[2,2,4,16,1024]{4,3,2,1,0:T(8,128)(2,1)}, bf16[2,2,4,16,1024]{4,3,2,1,0:T(8,128)(2,1)S(1)}, u32[]{:S(2)}, u32[]{:S(2)}) collective-permute-start(bf16[2,2,4,16,1024]{4,3,2,1,0:T(8,128)(2,1)} %collective-permute-done.5.refs_4_), channel_id=1, source_target_pairs={{0,16},{16,0},{1,17},{17,1},{2,18},{18,2},{3,19},{19,3},{4,20},{20... | collective-permute-start | bytes 1572872 | tf_op jit(solution)/shard_map/ppermute | solution.py:676
  85.4 22.4 %collective-permute-start.18 = (bf16[2,2,4,16,1024]{4,3,2,1,0:T(8,128)(2,1)}, bf16[2,2,4,16,1024]{4,3,2,1,0:T(8,128)(2,1)S(1)}, u32[]{:S(2)}, u32[]{:S(2)}) collective-permute-start(bf16[2,2,4,16,1024]{4,3,2,1,0:T(8,128)(2,1)} %collective-permute-done.5.refs_4_), channel_id=1, source_target_pairs={{0,1},{1,0},{2,3},{3,2},{4,5},{5,4},{6,7},{7,6},{8,9},{9,8},{10,11... | collective-permute-start | bytes 1572872 | tf_op jit(solution)/shard_map/ppermute | solution.py:676
  102.5 8.8 %copy-start.20 = (f32[128,4]{1,0:T(8,128)}, f32[128,4]{1,0:T(8,128)S(1)}, u32[]{:S(2)}) copy-start(f32[128,4]{1,0:T(8,128)S(1)} %collective-permute-done.19) | copy-start | bytes 6148
  107.9 2.7 %collective-permute-start.20 = (bf16[512,512]{1,0:T(8,128)(2,1)S(1)}, bf16[512,512]{1,0:T(8,128)(2,1)S(1)}, u32[]{:S(2)}, u32[]{:S(2)}) collective-permute-start(bf16[512,512]{1,0:T(8,128)(2,1)S(1)} %slice_bitcast_fusion), channel_id=1, source_target_pairs={{0,1},{1,0},{2,3},{3,2},{4,5},{5,4},{6,7},{7,6},{8,9},{9,8},{10,11... | collective-permute-start | bytes 1572872 | tf_op jit(solution)/shard_map/ppermute | solution.py:676
  109.1 2.3 collective-permute-start.21
  109.1 3.0 %collective-permute-start.22 = (bf16[2,2,4,16,1024]{4,3,2,1,0:T(8,128)(2,1)S(1)}, bf16[2,2,4,16,1024]{4,3,2,1,0:T(8,128)(2,1)S(1)}, u32[]{:S(2)}, u32[]{:S(2)}) collective-permute-start(bf16[2,2,4,16,1024]{4,3,2,1,0:T(8,128)(2,1)S(1)} %collective-permute-done.16.refs_6_), channel_id=1, source_target_pairs={{0,1},{1,0},{2,3},{3,2},{4,5},{5,4},{6,7},{7,6},{8,9},{9,8},{10,11... | collective-permute-start | bytes 1572872 | tf_op jit(solution)/shard_map/ppermute | solution.py:676
  117.3 27.5 %copy-start.11 = (f32[2048]{0:T(1024)S(1)}, f32[2048]{0:T(1024)}, u32[]{:S(2)}) copy-start(f32[2048]{0:T(1024)} %param.15) | copy-start | bytes 24580
  117.3 27.5 %all-to-all-start.1 = ((bf16[4,128,2048]{2,1,0:T(8,128)(2,1)}), bf16[4,128,2048]{2,1,0:T(8,128)(2,1)S(1)}, u32[]{:S(2)}, u32[]{:S(2)}) async-start(bf16[4,128,2048]{2,1,0:T(8,128)(2,1)} %bitcast.61), calls=%async_computation.1 | async-start | bytes 4194304 | tf_op jit(solution)/shard_map/all_to_all | solution.py:761
  144.8 1.0 copy-start.7
  145.8 11.8 %copy-start.21 = (f32[128,4]{1,0:T(8,128)S(1)}, f32[128,4]{1,0:T(8,128)}, u32[]{:S(2)}) copy-start(f32[128,4]{1,0:T(8,128)} %copy-done.20) | copy-start | bytes 6148
  147.5 1.0 copy-start.4
  148.6 1.0 copy-start.6
  150.3 30.9 %all-to-all-start.2 = ((bf16[8,32,2048]{2,1,0:T(8,128)(2,1)}), bf16[8,32,2048]{2,1,0:T(8,128)(2,1)}, u32[]{:S(2)}, u32[]{:S(2)}) async-start(bf16[8,32,2048]{2,1,0:T(8,128)(2,1)} %bitcast.49), calls=%async_computation.2 | async-start | bytes 2097152 | tf_op jit(solution)/shard_map/all_to_all | solution.py:841
  156.4 43.9 %copy-start.1 = (bf16[1,512,2048]{2,1,0:T(8,128)(2,1)S(1)}, bf16[1,512,2048]{2,1,0:T(8,128)(2,1)}, u32[]{:S(2)}) copy-start(bf16[1,512,2048]{2,1,0:T(8,128)(2,1)} %param.19) | copy-start | bytes 6291460
  156.4 24.8 %collective-permute-start.23 = (bf16[128,2048]{1,0:T(8,128)(2,1)}, bf16[128,2048]{1,0:T(8,128)(2,1)}, u32[]{:S(2)}, u32[]{:S(2)}) collective-permute-start(bf16[128,2048]{1,0:T(8,128)(2,1)} %copy-done.12), channel_id=1, source_target_pairs={{0,8},{1,9},{2,10},{3,11},{4,12},{5,13},{6,14},{7,15},{8,0},{9,1},... | collective-permute-start | bytes 1572872 | tf_op jit(solution)/shard_map/ppermute | solution.py:676
  204.2 1.0 copy-start.3
  205.2 18.5 %all-to-all-start.4 = ((bf16[8,32,2048]{2,1,0:T(8,128)(2,1)}), bf16[8,32,2048]{2,1,0:T(8,128)(2,1)}, u32[]{:S(2)}, u32[]{:S(2)}) async-start(bf16[8,32,2048]{2,1,0:T(8,128)(2,1)} %bitcast.47), calls=%async_computation.4 | async-start | bytes 2097152 | tf_op jit(solution)/shard_map/all_to_all | solution.py:841
  216.2 42.0 %copy-start.5 = (f32[128,2048]{1,0:T(8,128)S(1)}, f32[128,2048]{1,0:T(8,128)}, u32[]{:S(2)}) copy-start(f32[128,2048]{1,0:T(8,128)} %copy-done.4) | copy-start | bytes 3145732
  226.3 31.9 %all-to-all-start.5 = ((bf16[8,32,2048]{2,1,0:T(8,128)(2,1)}), bf16[8,32,2048]{2,1,0:T(8,128)(2,1)S(1)}, u32[]{:S(2)}, u32[]{:S(2)}) async-start(bf16[8,32,2048]{2,1,0:T(8,128)(2,1)} %bitcast.46), calls=%async_computation.5 | async-start | bytes 2097152 | tf_op jit(solution)/shard_map/all_to_all | solution.py:841
  231.8 25.6 %collective-permute-start.24 = (bf16[128,2048]{1,0:T(8,128)(2,1)}, bf16[128,2048]{1,0:T(8,128)(2,1)S(1)}, u32[]{:S(2)}, u32[]{:S(2)}) collective-permute-start(bf16[128,2048]{1,0:T(8,128)(2,1)} %copy-done.10), channel_id=1, source_target_pairs={{0,8},{1,9},{2,10},{3,11},{4,12},{5,13},{6,14},{7,15},{8,0},{9,1},... | collective-permute-start | bytes 1572872 | tf_op jit(solution)/shard_map/ppermute | solution.py:676
  258.2 1.0 copy-start.9
  (6 other events, 5.0 us)

commit v7 on v3

--- a/solution.py
+++ b/solution.py
@@ -11,6 +11,7 @@
 F32 = jnp.float32
 BF16 = jnp.bfloat16
 HIGH_VMEM = 48 * 2**20
+LOG2_E = 1.4426950408889634
 
 
 def in_hbm():
@@ -181,7 +182,7 @@
             bring(pieces_of.at[t], kv_ref.at[pl.ds(area + start, piece)], 2)
     for copy in copies:
         copy.wait()
-    scale = width**-0.5
+    scale = width**-0.5 * LOG2_E
     scores = [s0, s1]
     blocks = length // block
     units = [(head, b) for head in range(heads) for b in range(blocks)]
@@ -221,7 +222,7 @@
     def use_scores(unit, part, top, total, acc):
         kind, first, count, column = part
         values = (old_ref if kind == "old" else kv_ref)[pl.ds(first, count), width:]
-        e = jnp.exp((scores[unit % 2][:, pl.ds(column, count)] - top) * scale)
+        e = jnp.exp2((scores[unit % 2][:, pl.ds(column, count)] - top) * scale)
         for k in range(0, count, 128):
             total = e[:, k : k + 128] if total is None else total + e[:, k : k + 128]
         product = jnp.dot(e.astype(BF16), values, preferred_element_type=F32)
@@ -253,7 +254,7 @@
     members, heads, piece, width = q.shape
     length = members * piece
     old = sum(page.shape[0] for page in pages)
-    block = 2 * piece
+    block = min(4 * piece, length)
     chunk = min(512, old, length)
     keys = old + 2 * length
     return pl.pallas_call(
@@ -279,49 +280,68 @@
     )(q, *pages, *kvs)
 
 
-def project_pair_kernel(a_ref, got_ref, w_own, w_c, w_x, w_cx, o_ref, w_ref, sems):
+def project_pair_kernel(a_ref, got_ref, *refs):
+    near, far, outs, (w_ref, sems) = refs[:4], refs[4:8], refs[8:-2], refs[-2:]
     me = lax.axis_index("head")
     half = lax.axis_index("grp")
     core = lax.rem(me, 2)
-    planes, sides, heads, share, columns = w_own.shape
+    chip = jnp.bitwise_and(me // 2, len(outs) - 1)
+    steps, sides, heads, share, columns = near[0].shape
     width = w_ref.shape[1]
     copies = []
-    for flip, x, pieces_of in ((0, 0, w_own), (1, 0, w_c), (0, 1, w_x), (1, 1, w_cx)):
-        column = pl.multiple_of(jnp.bitwise_xor(half, x) * columns, columns)
-        for t in range(planes):
-            for u in range(sides):
-                number = jnp.bitwise_xor(me, flip ^ (2 * u) ^ (4 * t))
-                row = pl.multiple_of(number * share, share)
-                copy = pltpu.make_async_copy(
-                    pieces_of.at[t, u],
-                    w_ref.at[:, pl.ds(row, share), pl.ds(column, columns)],
-                    sems.at[0],
-                )
-                copy.start()
-                copies.append(copy)
+    for first, given in ((0, near), (steps, far)):
+        for flip, x, pieces_of in zip((0, 1, 0, 1), (0, 0, 1, 1), given):
+            column = pl.multiple_of(jnp.bitwise_xor(half, x) * columns, columns)
+            for t in range(steps):
+                for u in range(sides):
+                    number = jnp.bitwise_xor(me, flip ^ (2 * u) ^ (4 * (first + t)))
+                    row = pl.multiple_of(number * share, share)
+                    copy = pltpu.make_async_copy(
+                        pieces_of.at[t, u],
+                        w_ref.at[:, pl.ds(row, share), pl.ds(column, columns)],
+                        sems.at[0],
+                    )
+                    copy.start()
+                    copies.append(copy)
+    rows = outs[0].shape[0]
+    starts = [
+        pl.multiple_of(jnp.bitwise_xor(chip, k) * rows, rows) for k in range(len(outs))
+    ]
+    blocks = []
+    for k in range(heads):
+        mine = k < heads // 2
+        column = (k % (heads // 2)) * width
+        at = pl.ds(column, width)
+        blocks.append(
+            jnp.concatenate(
+                [
+                    a_ref[0, pl.ds(start, rows), at] if mine else got_ref[pl.ds(start, rows), at]
+                    for start in starts
+                ],
+                0,
+            )
+        )
     for copy in copies:
         copy.wait()
     acc = None
     for k in range(heads):
-        mine = k < heads // 2
-        column = (k % (heads // 2)) * width
-        a = a_ref[0, :, pl.ds(column, width)] if mine else got_ref[:, pl.ds(column, width)]
-        head = jnp.bitwise_xor(core, 0 if mine else 1) * (heads // 2) + k % (heads // 2)
-        part = jnp.dot(a, w_ref[head], preferred_element_type=F32)
+        head = jnp.bitwise_xor(core, 0 if k < heads // 2 else 1) * (heads // 2) + k % (heads // 2)
+        part = jnp.dot(blocks[k], w_ref[head], preferred_element_type=F32)
         acc = part if acc is None else acc + part
-    o_ref[...] = acc.astype(BF16)
-
-
-def project_pair(a, got, w_own, w_c, w_x, w_cx):
-    planes, sides, heads, share, columns = w_own.shape
+    for k, out in enumerate(outs):
+        out[...] = acc[k * rows : (k + 1) * rows].astype(BF16)
+
+
+def project_pair(a, got, near, far, parts):
+    _, _, heads, share, columns = near[0].shape
     rows = got.shape[0]
     width = 2 * got.shape[1] // heads
     model = 2 * columns
     return pl.pallas_call(
         project_pair_kernel,
-        out_shape=jax.ShapeDtypeStruct((rows, model), BF16),
-        in_specs=[in_vmem(), in_vmem()] + [in_hbm()] * 4,
-        out_specs=in_vmem(),
+        out_shape=[jax.ShapeDtypeStruct((rows // parts, model), BF16)] * parts,
+        in_specs=[in_vmem(), in_vmem()] + [in_hbm()] * 8,
+        out_specs=[in_vmem()] * parts,
         scratch_shapes=[
             pltpu.VMEM((heads, width, model), BF16),
             pltpu.SemaphoreType.DMA((1,)),
@@ -333,7 +353,7 @@
             transcendentals=0,
         ),
         name="project",
-    )(a, got, w_own, w_c, w_x, w_cx)
+    )(a, got, *near, *far)
 
 
 def project_kernel(a_ref, w_ref, o_ref):
@@ -372,14 +392,15 @@
     )(a, w)
 
 
-def route_kernel(parts_ref, resid_ref, gain_ref, slots_ref, stream_ref, out_ref):
-    seqs, planes = parts_ref.shape[0], parts_ref.shape[1]
+def route_kernel(resid_ref, gain_ref, slots_ref, *refs):
+    parts_refs, (stream_ref, out_ref) = refs[:-2], refs[-2:]
+    seqs = resid_ref.shape[0]
     streams = []
     for seq in range(seqs):
         stream = resid_ref[seq].astype(F32)
-        projected = parts_ref[seq, 0].astype(F32)
-        for p in range(1, planes):
-            projected = projected + parts_ref[seq, p].astype(F32)
+        projected = parts_refs[0][seq].astype(F32)
+        for part in parts_refs[1:]:
+            projected = projected + part[seq].astype(F32)
         streams.append(stream + projected)
     stream = jnp.concatenate(streams, 0) if seqs > 1 else streams[0]
     stream_ref[...] = stream
@@ -394,7 +415,7 @@
 
 
 def route(parts, resid, gain, slots_of, slots):
-    seqs, planes, local_rows, model = parts.shape
+    seqs, local_rows, model = resid.shape
     rows = seqs * local_rows
     return pl.pallas_call(
         route_kernel,
@@ -402,16 +423,16 @@
             jax.ShapeDtypeStruct((rows, model), F32),
             jax.ShapeDtypeStruct((slots, model), BF16),
         ),
-        in_specs=[in_vmem()] * 4,
+        in_specs=[in_vmem()] * (3 + len(parts)),
         out_specs=(in_vmem(), in_vmem()),
         compiler_params=pltpu.CompilerParams(vmem_limit_bytes=HIGH_VMEM),
         cost_estimate=pl.CostEstimate(
             flops=2 * slots * rows * model,
-            bytes_accessed=2 * (planes + 3 + slots // rows) * rows * model,
+            bytes_accessed=2 * (len(parts) + 3 + slots // rows) * rows * model,
             transcendentals=0,
         ),
         name="route",
-    )(parts, resid, gain, slots_of)
+    )(resid, gain, slots_of, *parts)
 
 
 def expert_kernel(x_ref, w_in_ref, w_down_ref, o_ref):
@@ -430,6 +451,59 @@
         out_shape=jax.ShapeDtypeStruct((rows, model), BF16),
         in_specs=[in_vmem()] * 3,
         out_specs=in_vmem(),
+        compiler_params=pltpu.CompilerParams(vmem_limit_bytes=HIGH_VMEM),
+        cost_estimate=pl.CostEstimate(
+            flops=6 * rows * model * hidden_width,
+            bytes_accessed=2 * (2 * rows * model + 3 * model * hidden_width),
+            transcendentals=rows * hidden_width,
+        ),
+        name="expert",
+    )(x, w_in, w_down)
+
+
+def expert_pair(x, w_in, w_down):
+    rows, model = x.shape
+    hidden_width = w_down.shape[0]
+    parts = 4
+    depth = model // parts
+
+    def kernel(x_hbm, in_hbm_ref, down_hbm, o_hbm, x_ref, in_ref, down_ref, o_ref, sems):
+        bring_x = pltpu.make_async_copy(x_hbm, x_ref, sems.at[parts])
+        bring_x.start()
+        bring_in = []
+        for k in range(parts):
+            at = pl.ds(k * depth, depth)
+            bring_in.append(pltpu.make_async_copy(in_hbm_ref.at[at], in_ref.at[at], sems.at[k]))
+            bring_in[k].start()
+        bring_down = pltpu.make_async_copy(down_hbm, down_ref, sems.at[parts + 1])
+        bring_down.start()
+        bring_x.wait()
+        inner = None
+        for k in range(parts):
+            bring_in[k].wait()
+            at = pl.ds(k * depth, depth)
+            part = jnp.dot(x_ref[:, at], in_ref[at, :], preferred_element_type=F32)
+            inner = part if inner is None else inner + part
+        gate = inner[:, :hidden_width]
+        hidden = (gate / (1.0 + jnp.exp(-gate)) * inner[:, hidden_width:]).astype(BF16)
+        bring_down.wait()
+        o_ref[...] = jnp.dot(hidden, down_ref[...], preferred_element_type=F32).astype(BF16)
+        back = pltpu.make_async_copy(o_ref, o_hbm, sems.at[parts + 2])
+        back.start()
+        back.wait()
+
+    return pl.pallas_call(
+        kernel,
+        out_shape=jax.ShapeDtypeStruct((rows, model), BF16),
+        in_specs=[in_hbm()] * 3,
+        out_specs=in_hbm(),
+        scratch_shapes=[
+            pltpu.VMEM((rows, model), BF16),
+            pltpu.VMEM(w_in.shape, BF16),
+            pltpu.VMEM(w_down.shape, BF16),
+            pltpu.VMEM((rows, model), BF16),
+            pltpu.SemaphoreType.DMA((parts + 3,)),
+        ],
         compiler_params=pltpu.CompilerParams(vmem_limit_bytes=HIGH_VMEM),
         cost_estimate=pl.CostEstimate(
             flops=6 * rows * model * hidden_width,
@@ -512,16 +586,19 @@
     kv_heads = new_kv.reshape(local_rows, pair_heads, 2 * width).transpose(1, 0, 2)
     kv_same = lax.dynamic_index_in_dim(kv_heads, b, 0, keepdims=False)
     kv_other = lax.dynamic_index_in_dim(kv_heads, 1 - b, 0, keepdims=False)
-    kv_own = [kv_same]
-    for t in range(1, planes):
-        kv_own.append(flipped(kv_other if t % 2 else kv_same, "head", t * plane_bit))
-
     columns = model // 2
     w = lax.dynamic_slice_in_dim(w_out, lax.axis_index("grp") * columns, columns, 2)
     w = w.reshape(2, 2, heads // 4, share, columns)
     w_keep = lax.dynamic_index_in_dim(w, y, 1, keepdims=False)
     w_give = lax.dynamic_index_in_dim(w, 1 - y, 1, keepdims=False)
     w_got = flipped(w_give, "head", 2)
+    kv_last, w_got = lax.optimization_barrier((kv_other, w_got))
+    kv_own = [
+        kv_same,
+        flipped(kv_other, "head", plane_bit),
+        flipped(kv_same, "head", 2 * plane_bit),
+        flipped(kv_last, "head", 3 * plane_bit),
+    ]
 
     (page_a, page_b, kv_own, q), w_got = lax.optimization_barrier(
         ((page_a, page_b, kv_own, q), w_got)
@@ -533,39 +610,35 @@
     w_both = jnp.stack([w_keep, w_got], 1)
     w_same = lax.dynamic_index_in_dim(w_both, b, 0, keepdims=False)
     w_other = lax.dynamic_index_in_dim(w_both, 1 - b, 0, keepdims=False)
-    w_own = [w_same]
-    for t in range(1, planes):
-        w_own.append(flipped(w_other if t % 2 else w_same, "head", t * plane_bit))
+    w_near = jnp.stack([w_same, flipped(w_other, "head", plane_bit)], 0)
+    w_near_x = flipped(w_near, "grp", 1)
+    w_far = [flipped(w_same, "head", 2 * plane_bit), flipped(w_other, "head", 3 * plane_bit)]
     pages_c = flipped(own_pages, "head", 1)
     kv_c = flipped(kv_own, "head", 1)
-    (pages_y, kv_y), w_own = lax.optimization_barrier(((pages_y, kv_y), w_own))
+    (pages_y, kv_y), w_far = lax.optimization_barrier(((pages_y, kv_y), w_far))
     pages_cy = flipped(pages_y, "head", 1)
     kv_cy = flipped(kv_y, "head", 1)
-    w_own = jnp.stack(w_own, 0)
-    q, w_own = lax.optimization_barrier((q, w_own))
-    w_x = flipped(w_own, "grp", 1)
-    w_c = flipped(w_own, "head", 1)
+    w_far = jnp.stack(w_far, 0)
+    q, w_far = lax.optimization_barrier((q, w_far))
+    w_far_x = flipped(w_far, "grp", 1)
+    w_near_c = flipped(w_near, "head", 1)
     a = attend_pair(
         q, (page_a, page_b, pages_y, pages_c, pages_cy), (kv_own, kv_y, kv_c, kv_cy)
     )
-    a, w_x, w_c = lax.optimization_barrier((a, w_x, w_c))
-    w_cx = flipped(w_x, "head", 1)
     got = flipped(a[1], "head", 1)
-    partial = project_pair(a, got, w_own, w_c, w_x, w_cx)
-    quads = [
-        [g * members + 2 * k + core for k in range(members // 2)]
-        for g in range(n // members)
-        for core in range(2)
-    ]
-    parts = lax.all_to_all(
-        partial.reshape(members // 2, local_rows, model),
-        "head",
-        split_axis=0,
-        concat_axis=0,
-        tiled=True,
-        axis_index_groups=quads,
-    )
-    return parts[None]
+    a, w_near_x, w_far_x, w_near_c = lax.optimization_barrier((a, w_near_x, w_far_x, w_near_c))
+    w_far_c = flipped(w_far, "head", 1)
+    w_near_cx = flipped(w_near_x, "head", 1)
+    w_far_cx = flipped(w_far_x, "head", 1)
+    partial = project_pair(
+        a,
+        got,
+        (w_near, w_near_c, w_near_x, w_near_cx),
+        (w_far, w_far_c, w_far_x, w_far_cx),
+        members // 2,
+    )
+    parts = [partial[0]] + [flipped(partial[k], "head", 2 * k) for k in (3, 2, 1)]
+    return [part[None] for part in parts]
 
 
 def parts_in_planes(queries, new_kv, cache, w_out):
@@ -625,7 +698,8 @@
         tiled=True,
         axis_index_groups=column_groups,
     )
-    return parts.reshape(seqs, planes_of_seq, local_rows, model)
+    parts = parts.reshape(seqs, planes_of_seq, local_rows, model)
+    return [parts[:, k] for k in range(planes_of_seq)]
 
 
 def local(queries, new_kv, cache, resid, w_out, norm_gain, expert_ids, expert_gates, w_in, w_down):
@@ -641,6 +715,7 @@
         and n == heads == 2 * members
         and members == 8
         and cache.shape[0] == 1
+        and w_in.shape[0] == 1
         and w_out.shape[1] % 16 == 0
     )
     plan = parts_in_pairs if in_pairs else parts_in_planes
@@ -665,7 +740,7 @@
     )
     local_experts = w_in.shape[0]
     if local_experts == 1:
-        answered = expert(arrived.reshape(slots, model), w_in[0], w_down[0])
+        answered = expert_pair(arrived.reshape(slots, model), w_in[0], w_down[0])
         answered = answered.reshape(n, slots // n, model)
     else:
         arrived = arrived.reshape(n, local_experts, capacity, model).transpose(1, 0, 2, 3)

time: 247 us -> 251 us (1.016)
  starting transfers between devices: 30.4 us -> 38 us
  waiting for transfers between devices: 124 us -> 120 us
  Pallas kernels: 28.8 us -> 31.6 us
    all_to_all x1 -> x0, waiting for transfers between devices: 23 us -> none  [parts_in_pairs(): lax.all_to_all(partial.reshape(members // 2, local_rows, model), 'head',...]
    ppermute x17 -> x23, waiting for transfers between devices: 53.3 us -> 72.5 us  [flipped(): return lax.ppermute(value, axis, pairs)]
    ppermute x17 -> x23, starting transfers between devices: 12.4 us -> 25 us  [flipped(): return lax.ppermute(value, axis, pairs)]
    all_to_all x1 -> x0, starting transfers between devices: 3.64 us -> none  [parts_in_pairs(): lax.all_to_all(partial.reshape(members // 2, local_rows, model), 'head',...]
  transfers between devices with their start and end apart: 22 -> 27, of which waited for: 11 -> 15; matrix products, arithmetic and copies ran while one was open for 1% -> 1% of each run, Pallas kernels for 6% -> 6%
where the time goes in v7:
time: 251 us
  waiting for transfers between devices  120 us (48%)
  blocking collectives  51.4 us (20%)
  starting transfers between devices  38 us (15%)
  Pallas kernels  31.6 us (13%)
  local copies, waits for them, and re-layouts  8.11 us (3%)
    ppermute x23, waiting for transfers between devices, flipped(): return lax.ppermute(value, axis, pairs)  72.5 us
    all_to_all x1, blocking collectives, local(): lax.all_to_all(outgoing.reshape(n, slots // n, model), 'head', split_axis...  51.4 us
    all_to_all x1, waiting for transfers between devices, local(): lax.all_to_all(answered, 'head', split_axis=0, concat_axis=0, tiled=True)  47.3 us
    ppermute x23, starting transfers between devices, flipped(): return lax.ppermute(value, axis, pairs)  25 us
    pallas_call x1, Pallas kernels, attend_pair(): pl.pallas_call(functools.partial(attend_pair_kernel, block, chunk, width)...  15.6 us
    pallas_call x1, Pallas kernels, project_pair(): pl.pallas_call(project_pair_kernel, out_shape=[jax.ShapeDtypeStruct((rows...  6.56 us
    pallas_call x1, Pallas kernels, expert_pair(): pl.pallas_call(kernel, out_shape=jax.ShapeDtypeStruct((rows, model), BF16...  5.69 us
    all_to_all x1, starting transfers between devices, local(): lax.all_to_all(answered, 'head', split_axis=0, concat_axis=0, tiled=True)  5.25 us
  transfers between devices with their start and end apart: 27, of which 15 were waited for; matrix products, arithmetic and copies ran while one was open for 1% of the time, Pallas kernels for 6%

profile of v7, /device:TPU:13, one launch (start us, length us, event | category | flops | bytes accessed | tf_op | source)
XLA Modules:
  0.0 250.7 jit_solution(7036105060583857248)
XLA Ops:
  0.0 2.6 %copy.29 = bf16[16,128,256]{2,1,0:T(8,128)(2,1)} copy(bf16[16,128,256]{2,0,1:T(8,128)(2,1)} %bitcast.56) | data formatting | bytes 2097152 | tf_op jit(solution)/shard_map/transpose | solution.py:572
  2.6 4.6 %all-to-all-start = ((bf16[8,2,128,256]{3,2,1,0:T(8,128)(2,1)}), bf16[8,2,128,256]{3,2,1,0:T(8,128)(2,1)S(1)}, u32[]{:S(2)}, u32[]{:S(2)}) async-start(bf16[8,2,128,256]{3,2,1,0:T(8,128)(2,1)} %bitcast.11), calls=%async_computation | async-start | bytes 2097152 | tf_op jit(solution)/shard_map/all_to_all | solution.py:574
  7.3 0.8 constant_dynamic-slice_fusion
  8.4 3.1 %collective-permute-start = (bf16[256,512]{1,0:T(8,128)(2,1)}, bf16[256,512]{1,0:T(8,128)(2,1)S(1)}, u32[]{:S(2)}, u32[]{:S(2)}) collective-permute-start(bf16[256,512]{1,0:T(8,128)(2,1)} %bitcast.4), channel_id=1, source_target_pairs={{0,0},{1,1},{2,2},{3,3},{4,8},{5,9},{6,10},{7,11},{8,4},{9,5},{10,... | collective-permute-start | bytes 786440 | tf_op jit(solution)/shard_map/ppermute | solution.py:583
  11.6 0.5 constant_dynamic-slice_fusion.2
  12.2 1.4 collective-permute-start.2
  13.6 1.0 collective-permute-start.3
  14.6 10.9 %collective-permute-done.4 = bf16[2,4,16,1024]{3,2,1,0:T(8,128)(2,1)S(1)} collective-permute-done((bf16[2,4,16,1024]{3,2,1,0:T(8,128)(2,1)}, bf16[2,4,16,1024]{3,2,1,0:T(8,128)(2,1)S(1)}, u32[]{:S(2)}, u32[]{:S(2)}) %collective-permute-start.4) | collective-permute-done | bytes 262176 | tf_op jit(solution)/shard_map/ppermute | solution.py:555
  25.6 1.3 collective-permute-start.5
  26.9 3.1 %collective-permute-done.2 = bf16[128,512]{1,0:T(8,128)(2,1)S(1)} collective-permute-done((bf16[128,512]{1,0:T(8,128)(2,1)S(1)}, bf16[128,512]{1,0:T(8,128)(2,1)S(1)}, u32[]{:S(2)}, u32[]{:S(2)}) %collective-permute-start.2) | collective-permute-done | bytes 131104 | tf_op jit(solution)/shard_map/ppermute | solution.py:555
  30.0 3.2 %collective-permute-done.3 = bf16[128,512]{1,0:T(8,128)(2,1)} collective-permute-done((bf16[128,512]{1,0:T(8,128)(2,1)S(1)}, bf16[128,512]{1,0:T(8,128)(2,1)}, u32[]{:S(2)}, u32[]{:S(2)}) %collective-permute-start.3) | collective-permute-done | bytes 131104 | tf_op jit(solution)/shard_map/ppermute | solution.py:555
  33.2 2.1 collective-permute-done.5
  35.3 1.0 collective-permute-start.6
  36.3 1.0 pad_maximum_fusion.kv_own
  37.3 0.6 collective-permute-start.7
  38.0 0.9 collective-permute-start.8
  38.9 2.3 collective-permute-start.9
  41.2 2.1 collective-permute-start.10
  43.2 10.9 %collective-permute-done.8 = bf16[2,4,16,1024]{3,2,1,0:T(8,128)(2,1)S(1)} collective-permute-done((bf16[2,4,16,1024]{3,2,1,0:T(8,128)(2,1)S(1)}, bf16[2,4,16,1024]{3,2,1,0:T(8,128)(2,1)S(1)}, u32[]{:S(2)}, u32[]{:S(2)}) %collective-permute-start.8) | collective-permute-done | bytes 262176 | tf_op jit(solution)/shard_map/ppermute | solution.py:555
  54.1 4.6 %collective-permute-start.12 = (bf16[4,128,512]{2,1,0:T(8,128)(2,1)S(1)}, bf16[4,128,512]{2,1,0:T(8,128)(2,1)S(1)}, u32[]{:S(2)}, u32[]{:S(2)}) collective-permute-start(bf16[4,128,512]{2,1,0:T(8,128)(2,1)S(1)} %pad_maximum_fusion.kv_own), channel_id=1, source_target_pairs={{0,1},{1,0},{2,3},{3,2},{4,5},{5,4},{6,7},{7,6},{8,9},{9,8},{10,11... | collective-permute-start | bytes 1572872 | tf_op jit(solution)/shard_map/ppermute | solution.py:555
  58.7 5.3 %collective-permute-done.9 = bf16[2,4,16,1024]{3,2,1,0:T(8,128)(2,1)S(1)} collective-permute-done((bf16[2,4,16,1024]{3,2,1,0:T(8,128)(2,1)S(1)}, bf16[2,4,16,1024]{3,2,1,0:T(8,128)(2,1)S(1)}, u32[]{:S(2)}, u32[]{:S(2)}) %collective-permute-start.9) | collective-permute-done | bytes 262176 | tf_op jit(solution)/shard_map/ppermute | solution.py:555
  64.0 0.5 collective-permute-start.11
  64.6 7.4 %collective-permute-done.14 = bf16[2,4,16,1024]{3,2,1,0:T(8,128)(2,1)S(1)} collective-permute-done((bf16[2,4,16,1024]{3,2,1,0:T(8,128)(2,1)S(1)}, bf16[2,4,16,1024]{3,2,1,0:T(8,128)(2,1)S(1)}, u32[]{:S(2)}, u32[]{:S(2)}) %collective-permute-start.14) | collective-permute-done | bytes 262176 | tf_op jit(solution)/shard_map/ppermute | solution.py:555
  72.1 1.3 collective-permute-start.15
  73.4 1.6 collective-permute-start.17
  75.7 15.6 %attend.1.a_ref = bf16[2,512,512]{2,1,0:T(8,128)(2,1)S(1)} custom-call(bf16[8,2,128,256]{3,2,1,0:T(8,128)(2,1)} %copy-done.8, bf16[256,512]{1,0:T(8,128)(2,1)S(1)} %collective-permute-done.page_a, bf16[256,512]{1,0:T(8,128)(2,1)S(1)} %collective-permute-done.1.page_b, bf16[512,512]{1,0:T(8,128)(2,1)S(1)} %collective-permute-done.6.page_y, ...), custom_call_target="tpu_custom_call" | custom-call | flops 7516192768 | bytes 6291456 | tf_op jit(solution)/shard_map/attend/pallas_call | solution.py:260
  91.4 4.2 %collective-permute-done.16.refs_6_ = bf16[2,2,4,16,1024]{4,3,2,1,0:T(8,128)(2,1)S(1)} collective-permute-done((bf16[2,2,4,16,1024]{4,3,2,1,0:T(8,128)(2,1)S(1)}, bf16[2,2,4,16,1024]{4,3,2,1,0:T(8,128)(2,1)S(1)}, u32[]{:S(2)}, u32[]{:S(2)}) %collective-permute-start.16) | collective-permute-done | bytes 524320 | tf_op jit(solution)/shard_map/ppermute | solution.py:555
  95.5 2.2 collective-permute-start.18
  97.7 0.5 collective-permute-start.21
  98.3 1.0 collective-permute-done.18.got_ref
  99.3 0.7 collective-permute-done.19.refs_3_
  100.0 0.7 collective-permute-done.21.refs_7_
  100.8 0.8 copy-done.12
  101.6 6.6 %project.1 = (bf16[128,2048]{1,0:T(8,128)(2,1)S(1)}, bf16[128,2048]{1,0:T(8,128)(2,1)}, bf16[128,2048]{1,0:T(8,128)(2,1)}, bf16[128,2048]{1,0:T(8,128)(2,1)}) custom-call(bf16[2,512,512]{2,1,0:T(8,128)(2,1)} %copy-done.5, bf16[512,512]{1,0:T(8,128)(2,1)S(1)} %collective-permute-done.18.got_ref, bf16[2,2,4,16,1024]{4,3,2,1,0:T(8,128)(2,1)S(1)} %pad_maximum_fusion.2.refs_0_, ...), custom_call_target="tpu_custom_call" | custom-call | flops 2147483648 | bytes 7340032 | tf_op jit(solution)/shard_map/project/pallas_call | solution.py:340
  108.1 1.0 collective-permute-start.22
  109.2 1.1 collective-permute-start.23
  110.3 0.6 collective-permute-start.24
  111.6 10.9 %collective-permute-done.22 = bf16[128,2048]{1,0:T(8,128)(2,1)S(1)} collective-permute-done((bf16[128,2048]{1,0:T(8,128)(2,1)}, bf16[128,2048]{1,0:T(8,128)(2,1)S(1)}, u32[]{:S(2)}, u32[]{:S(2)}) %collective-permute-start.22) | collective-permute-done | bytes 524320 | tf_op jit(solution)/shard_map/ppermute | solution.py:555
  122.5 11.1 %collective-permute-done.23 = bf16[128,2048]{1,0:T(8,128)(2,1)S(1)} collective-permute-done((bf16[128,2048]{1,0:T(8,128)(2,1)}, bf16[128,2048]{1,0:T(8,128)(2,1)S(1)}, u32[]{:S(2)}, u32[]{:S(2)}) %collective-permute-start.23) | collective-permute-done | bytes 524320 | tf_op jit(solution)/shard_map/ppermute | solution.py:555
  133.6 0.9 collective-permute-done.24
  134.5 2.2 route.1
  136.7 51.4 %all_to_all.15 = bf16[16,32,2048]{2,1,0:T(8,128)(2,1)S(1)} all-to-all(bf16[16,32,2048]{2,1,0:T(8,128)(2,1)S(1)} %bitcast.45), channel_id=1, replica_groups=mesh['grp'=2,'head'=16] {'head'}, dimensions={0} | all-to-all | bytes 4194304 | tf_op jit(solution)/shard_map/all_to_all | solution.py:738
  188.2 5.7 %expert.1 = bf16[512,2048]{1,0:T(8,128)(2,1)S(1)} custom-call(bf16[512,2048]{1,0:T(8,128)(2,1)S(1)} %bitcast.47, bf16[2048,1024]{1,0:T(8,128)(2,1)} %bitcast.68, bf16[512,2048]{1,0:T(8,128)(2,1)} %bitcast.69), custom_call_target="tpu_custom_call" | custom-call | flops 3221225472 | bytes 10485760 | tf_op jit(solution)/shard_map/expert/pallas_call | solution.py:495
  193.9 1.4 copy-done.1
  195.2 5.3 %all-to-all-start.2 = ((bf16[16,32,2048]{2,1,0:T(8,128)(2,1)}), bf16[16,32,2048]{2,1,0:T(8,128)(2,1)S(1)}, u32[]{:S(2)}, u32[]{:S(2)}) async-start(bf16[16,32,2048]{2,1,0:T(8,128)(2,1)} %bitcast.46), calls=%async_computation.2 | async-start | bytes 4194304 | tf_op jit(solution)/shard_map/all_to_all | solution.py:751
  200.6 47.3 %all-to-all-done.2 = bf16[16,32,2048]{2,1,0:T(8,128)(2,1)S(1)} async-done(((bf16[16,32,2048]{2,1,0:T(8,128)(2,1)}), bf16[16,32,2048]{2,1,0:T(8,128)(2,1)S(1)}, u32[]{:S(2)}, u32[]{:S(2)}) %all-to-all-start.2) | async-done | bytes 2097184 | tf_op jit(solution)/shard_map/all_to_all | solution.py:751
  247.9 1.2 copy-done.3
  249.1 1.6 combine.1
  (63 shorter events, 2.3 us)
Async XLA Ops:
  0.0 7.3 %copy-start = (bf16[16,16,2048]{2,1,0:T(8,128)(2,1)S(1)}, bf16[16,16,2048]{2,1,0:T(8,128)(2,1)}, u32[]{:S(2)}) copy-start(bf16[16,16,2048]{2,1,0:T(8,128)(2,1)} %param.14) | copy-start | bytes 3145732
  2.6 9.0 %copy-start.7 = (bf16[128,1,2,512]{3,2,1,0:T(2,128)(2,1)S(1)}, bf16[128,1,2,512]{3,2,1,0:T(2,128)(2,1)}, u32[]{:S(2)}) copy-start(bf16[128,1,2,512]{3,2,1,0:T(2,128)(2,1)} %param.11) | copy-start | bytes 786436
  2.6 32.6 %all-to-all-start = ((bf16[8,2,128,256]{3,2,1,0:T(8,128)(2,1)}), bf16[8,2,128,256]{3,2,1,0:T(8,128)(2,1)S(1)}, u32[]{:S(2)}, u32[]{:S(2)}) async-start(bf16[8,2,128,256]{3,2,1,0:T(8,128)(2,1)} %bitcast.11), calls=%async_computation | async-start | bytes 2097152 | tf_op jit(solution)/shard_map/all_to_all | solution.py:574
  8.1 17.5 %collective-permute-start.4 = (bf16[2,4,16,1024]{3,2,1,0:T(8,128)(2,1)}, bf16[2,4,16,1024]{3,2,1,0:T(8,128)(2,1)S(1)}, u32[]{:S(2)}, u32[]{:S(2)}) collective-permute-start(bf16[2,4,16,1024]{3,2,1,0:T(8,128)(2,1)} %get-tuple-element.60), channel_id=1, source_target_pairs={{0,2},{1,3},{2,0},{3,1},{4,6},{5,7},{6,4},{7,5},{8,10},{9,11},{10,... | collective-permute-start | bytes 786440 | tf_op jit(solution)/shard_map/ppermute | solution.py:555
  8.4 24.8 %collective-permute-start = (bf16[256,512]{1,0:T(8,128)(2,1)}, bf16[256,512]{1,0:T(8,128)(2,1)S(1)}, u32[]{:S(2)}, u32[]{:S(2)}) collective-permute-start(bf16[256,512]{1,0:T(8,128)(2,1)} %bitcast.4), channel_id=1, source_target_pairs={{0,0},{1,1},{2,2},{3,3},{4,8},{5,9},{6,10},{7,11},{8,4},{9,5},{10,... | collective-permute-start | bytes 786440 | tf_op jit(solution)/shard_map/ppermute | solution.py:583
  11.5 21.7 %collective-permute-start.1 = (bf16[256,512]{1,0:T(8,128)(2,1)}, bf16[256,512]{1,0:T(8,128)(2,1)S(1)}, u32[]{:S(2)}, u32[]{:S(2)}) collective-permute-start(bf16[256,512]{1,0:T(8,128)(2,1)} %bitcast.4), channel_id=1, source_target_pairs={{0,8},{1,9},{2,10},{3,11},{4,0},{5,1},{6,2},{7,3},{8,12},{9,13},{1... | collective-permute-start | bytes 786440 | tf_op jit(solution)/shard_map/ppermute | solution.py:583
  12.2 17.8 %collective-permute-start.2 = (bf16[128,512]{1,0:T(8,128)(2,1)S(1)}, bf16[128,512]{1,0:T(8,128)(2,1)S(1)}, u32[]{:S(2)}, u32[]{:S(2)}) collective-permute-start(bf16[128,512]{1,0:T(8,128)(2,1)S(1)} %bitcast.65), channel_id=1, source_target_pairs={{0,4},{1,5},{2,6},{3,7},{4,0},{5,1},{6,2},{7,3},{8,12},{9,13},{10,... | collective-permute-start | bytes 393224 | tf_op jit(solution)/shard_map/ppermute | solution.py:555
  13.6 19.5 %collective-permute-start.3 = (bf16[128,512]{1,0:T(8,128)(2,1)S(1)}, bf16[128,512]{1,0:T(8,128)(2,1)}, u32[]{:S(2)}, u32[]{:S(2)}) collective-permute-start(bf16[128,512]{1,0:T(8,128)(2,1)S(1)} %bitcast.59), channel_id=1, source_target_pairs={{0,8},{1,9},{2,10},{3,11},{4,12},{5,13},{6,14},{7,15},{8,0},{9,1},... | collective-permute-start | bytes 393224 | tf_op jit(solution)/shard_map/ppermute | solution.py:555
  25.6 9.7 %collective-permute-start.5 = (bf16[128,512]{1,0:T(8,128)(2,1)S(1)}, bf16[128,512]{1,0:T(8,128)(2,1)}, u32[]{:S(2)}, u32[]{:S(2)}) collective-permute-start(bf16[128,512]{1,0:T(8,128)(2,1)S(1)} %bitcast.66), channel_id=1, source_target_pairs={{0,12},{1,13},{2,14},{3,15},{4,8},{5,9},{6,10},{7,11},{8,4},{9,5},... | collective-permute-start | bytes 393224 | tf_op jit(solution)/shard_map/ppermute | solution.py:555
  35.2 36.9 %copy-start.8 = (bf16[8,2,128,256]{3,2,1,0:T(8,128)(2,1)}, bf16[8,2,128,256]{3,2,1,0:T(8,128)(2,1)S(1)}, u32[]{:S(2)}) copy-start(bf16[8,2,128,256]{3,2,1,0:T(8,128)(2,1)S(1)} %all-to-all-done.q_hbm) | copy-start | bytes 3145732
  35.3 28.7 %collective-permute-start.6 = (bf16[512,512]{1,0:T(8,128)(2,1)S(1)}, bf16[512,512]{1,0:T(8,128)(2,1)S(1)}, u32[]{:S(2)}, u32[]{:S(2)}) collective-permute-start(bf16[512,512]{1,0:T(8,128)(2,1)S(1)} %constant_dynamic-update-slice_fusion), channel_id=1, source_target_pairs={{0,2},{1,3},{2,0},{3,1},{4,6},{5,7},{6,4},{7,5},{8,10},{9,11},{10,... | collective-permute-start | bytes 1572872 | tf_op jit(solution)/shard_map/ppermute | solution.py:555
  37.3 26.7 %collective-permute-start.7 = (bf16[4,128,512]{2,1,0:T(8,128)(2,1)S(1)}, bf16[4,128,512]{2,1,0:T(8,128)(2,1)S(1)}, u32[]{:S(2)}, u32[]{:S(2)}) collective-permute-start(bf16[4,128,512]{2,1,0:T(8,128)(2,1)S(1)} %pad_maximum_fusion.kv_own), channel_id=1, source_target_pairs={{0,2},{1,3},{2,0},{3,1},{4,6},{5,7},{6,4},{7,5},{8,10},{9,11},{10,... | collective-permute-start | bytes 1572872 | tf_op jit(solution)/shard_map/ppermute | solution.py:555
  38.0 16.2 %collective-permute-start.8 = (bf16[2,4,16,1024]{3,2,1,0:T(8,128)(2,1)S(1)}, bf16[2,4,16,1024]{3,2,1,0:T(8,128)(2,1)S(1)}, u32[]{:S(2)}, u32[]{:S(2)}) collective-permute-start(bf16[2,4,16,1024]{3,2,1,0:T(8,128)(2,1)S(1)} %bitcast.57), channel_id=1, source_target_pairs={{0,8},{1,9},{2,10},{3,11},{4,12},{5,13},{6,14},{7,15},{8,0},{9,1},... | collective-permute-start | bytes 786440 | tf_op jit(solution)/shard_map/ppermute | solution.py:555
  38.9 25.1 %collective-permute-start.9 = (bf16[2,4,16,1024]{3,2,1,0:T(8,128)(2,1)S(1)}, bf16[2,4,16,1024]{3,2,1,0:T(8,128)(2,1)S(1)}, u32[]{:S(2)}, u32[]{:S(2)}) collective-permute-start(bf16[2,4,16,1024]{3,2,1,0:T(8,128)(2,1)S(1)} %get-tuple-element.57), channel_id=1, source_target_pairs={{0,12},{1,13},{2,14},{3,15},{4,8},{5,9},{6,10},{7,11},{8,4},{9,5},... | collective-permute-start | bytes 786440 | tf_op jit(solution)/shard_map/ppermute | solution.py:555
  41.2 32.3 %collective-permute-start.10 = (bf16[512,512]{1,0:T(8,128)(2,1)S(1)}, bf16[512,512]{1,0:T(8,128)(2,1)S(1)}, u32[]{:S(2)}, u32[]{:S(2)}) collective-permute-start(bf16[512,512]{1,0:T(8,128)(2,1)S(1)} %constant_dynamic-update-slice_fusion), channel_id=1, source_target_pairs={{0,1},{1,0},{2,3},{3,2},{4,5},{5,4},{6,7},{7,6},{8,9},{9,8},{10,11... | collective-permute-start | bytes 1572872 | tf_op jit(solution)/shard_map/ppermute | solution.py:555
  54.1 20.9 %collective-permute-start.12 = (bf16[4,128,512]{2,1,0:T(8,128)(2,1)S(1)}, bf16[4,128,512]{2,1,0:T(8,128)(2,1)S(1)}, u32[]{:S(2)}, u32[]{:S(2)}) collective-permute-start(bf16[4,128,512]{2,1,0:T(8,128)(2,1)S(1)} %pad_maximum_fusion.kv_own), channel_id=1, source_target_pairs={{0,1},{1,0},{2,3},{3,2},{4,5},{5,4},{6,7},{7,6},{8,9},{9,8},{10,11... | collective-permute-start | bytes 1572872 | tf_op jit(solution)/shard_map/ppermute | solution.py:555
  64.0 11.3 %collective-permute-start.11 = (bf16[512,512]{1,0:T(8,128)(2,1)S(1)}, bf16[512,512]{1,0:T(8,128)(2,1)S(1)}, u32[]{:S(2)}, u32[]{:S(2)}) collective-permute-start(bf16[512,512]{1,0:T(8,128)(2,1)S(1)} %collective-permute-done.6.page_y), channel_id=1, source_target_pairs={{0,1},{1,0},{2,3},{3,2},{4,5},{5,4},{6,7},{7,6},{8,9},{9,8},{10,11... | collective-permute-start | bytes 1572872 | tf_op jit(solution)/shard_map/ppermute | solution.py:555
  64.5 11.2 %collective-permute-start.13 = (bf16[4,128,512]{2,1,0:T(8,128)(2,1)S(1)}, bf16[4,128,512]{2,1,0:T(8,128)(2,1)S(1)}, u32[]{:S(2)}, u32[]{:S(2)}) collective-permute-start(bf16[4,128,512]{2,1,0:T(8,128)(2,1)S(1)} %collective-permute-done.7.kv_y), channel_id=1, source_target_pairs={{0,1},{1,0},{2,3},{3,2},{4,5},{5,4},{6,7},{7,6},{8,9},{9,8},{10,11... | collective-permute-start | bytes 1572872 | tf_op jit(solution)/shard_map/ppermute | solution.py:555
  64.6 7.4 %collective-permute-start.14 = (bf16[2,4,16,1024]{3,2,1,0:T(8,128)(2,1)S(1)}, bf16[2,4,16,1024]{3,2,1,0:T(8,128)(2,1)S(1)}, u32[]{:S(2)}, u32[]{:S(2)}) collective-permute-start(bf16[2,4,16,1024]{3,2,1,0:T(8,128)(2,1)S(1)} %get-tuple-element.57), channel_id=1, source_target_pairs={{0,4},{1,5},{2,6},{3,7},{4,0},{5,1},{6,2},{7,3},{8,12},{9,13},{10,... | collective-permute-start | bytes 786440 | tf_op jit(solution)/shard_map/ppermute | solution.py:555
  72.1 19.3 %collective-permute-start.15 = (bf16[2,2,4,16,1024]{4,3,2,1,0:T(8,128)(2,1)S(1)}, bf16[2,2,4,16,1024]{4,3,2,1,0:T(8,128)(2,1)S(1)}, u32[]{:S(2)}, u32[]{:S(2)}) collective-permute-start(bf16[2,2,4,16,1024]{4,3,2,1,0:T(8,128)(2,1)S(1)} %pad_maximum_fusion.2.refs_0_), channel_id=1, source_target_pairs={{0,16},{16,0},{1,17},{17,1},{2,18},{18,2},{3,19},{19,3},{4,20},{20... | collective-permute-start | bytes 1572872 | tf_op jit(solution)/shard_map/ppermute | solution.py:555
  73.4 17.9 %collective-permute-start.17 = (bf16[2,2,4,16,1024]{4,3,2,1,0:T(8,128)(2,1)S(1)}, bf16[2,2,4,16,1024]{4,3,2,1,0:T(8,128)(2,1)S(1)}, u32[]{:S(2)}, u32[]{:S(2)}) collective-permute-start(bf16[2,2,4,16,1024]{4,3,2,1,0:T(8,128)(2,1)S(1)} %pad_maximum_fusion.2.refs_0_), channel_id=1, source_target_pairs={{0,1},{1,0},{2,3},{3,2},{4,5},{5,4},{6,7},{7,6},{8,9},{9,8},{10,11... | collective-permute-start | bytes 1572872 | tf_op jit(solution)/shard_map/ppermute | solution.py:555
  75.1 20.5 %collective-permute-start.16 = (bf16[2,2,4,16,1024]{4,3,2,1,0:T(8,128)(2,1)S(1)}, bf16[2,2,4,16,1024]{4,3,2,1,0:T(8,128)(2,1)S(1)}, u32[]{:S(2)}, u32[]{:S(2)}) collective-permute-start(bf16[2,2,4,16,1024]{4,3,2,1,0:T(8,128)(2,1)S(1)} %pad_maximum_fusion.1.refs_4_), channel_id=1, source_target_pairs={{0,16},{16,0},{1,17},{17,1},{2,18},{18,2},{3,19},{19,3},{4,20},{20... | collective-permute-start | bytes 1572872 | tf_op jit(solution)/shard_map/ppermute | solution.py:555
  75.3 22.9 %collective-permute-start.20 = (bf16[2,2,4,16,1024]{4,3,2,1,0:T(8,128)(2,1)S(1)}, bf16[2,2,4,16,1024]{4,3,2,1,0:T(8,128)(2,1)S(1)}, u32[]{:S(2)}, u32[]{:S(2)}) collective-permute-start(bf16[2,2,4,16,1024]{4,3,2,1,0:T(8,128)(2,1)S(1)} %pad_maximum_fusion.1.refs_4_), channel_id=1, source_target_pairs={{0,1},{1,0},{2,3},{3,2},{4,5},{5,4},{6,7},{7,6},{8,9},{9,8},{10,11... | collective-permute-start | bytes 1572872 | tf_op jit(solution)/shard_map/ppermute | solution.py:555
  91.3 9.5 %copy-start.5 = (bf16[2,512,512]{2,1,0:T(8,128)(2,1)}, bf16[2,512,512]{2,1,0:T(8,128)(2,1)S(1)}, u32[]{:S(2)}) copy-start(bf16[2,512,512]{2,1,0:T(8,128)(2,1)S(1)} %attend.1.a_ref) | copy-start | bytes 3145732
  91.3 19.5 %copy-start.9 = (s32[128,1,2]{0,2,1:T(2,128)S(1)}, s32[128,1,2]{0,2,1:T(2,128)}, u32[]{:S(2)}) copy-start(s32[128,1,2]{0,2,1:T(2,128)} %param.16) | copy-start | bytes 3076
  91.3 43.2 %copy-start.4 = (bf16[128,1,2048]{2,0,1:T(8,128)(2,1)S(1)}, bf16[128,1,2048]{2,0,1:T(8,128)(2,1)}, u32[]{:S(2)}) copy-start(bf16[128,1,2048]{2,0,1:T(8,128)(2,1)} %param.13) | copy-start | bytes 1572868
  91.3 43.2 %copy-start.6 = (f32[2048]{0:T(1024)S(1)}, f32[2048]{0:T(1024)}, u32[]{:S(2)}) copy-start(f32[2048]{0:T(1024)} %param.15) | copy-start | bytes 24580
  95.5 5.2 %copy-start.11 = (bf16[2,2,4,16,1024]{4,3,2,1,0:T(8,128)(2,1)}, bf16[2,2,4,16,1024]{4,3,2,1,0:T(8,128)(2,1)S(1)}, u32[]{:S(2)}) copy-start(bf16[2,2,4,16,1024]{4,3,2,1,0:T(8,128)(2,1)S(1)} %collective-permute-done.16.refs_6_) | copy-start | bytes 1572868
  95.5 3.7 %collective-permute-start.18 = (bf16[512,512]{1,0:T(8,128)(2,1)S(1)}, bf16[512,512]{1,0:T(8,128)(2,1)S(1)}, u32[]{:S(2)}, u32[]{:S(2)}) collective-permute-start(bf16[512,512]{1,0:T(8,128)(2,1)S(1)} %slice_bitcast_fusion), channel_id=1, source_target_pairs={{0,1},{1,0},{2,3},{3,2},{4,5},{5,4},{6,7},{7,6},{8,9},{9,8},{10,11... | collective-permute-start | bytes 1572872 | tf_op jit(solution)/shard_map/ppermute | solution.py:555
  97.7 2.3 collective-permute-start.19
  97.7 3.0 %collective-permute-start.21 = (bf16[2,2,4,16,1024]{4,3,2,1,0:T(8,128)(2,1)S(1)}, bf16[2,2,4,16,1024]{4,3,2,1,0:T(8,128)(2,1)S(1)}, u32[]{:S(2)}, u32[]{:S(2)}) collective-permute-start(bf16[2,2,4,16,1024]{4,3,2,1,0:T(8,128)(2,1)S(1)} %collective-permute-done.16.refs_6_), channel_id=1, source_target_pairs={{0,1},{1,0},{2,3},{3,2},{4,5},{5,4},{6,7},{7,6},{8,9},{9,8},{10,11... | collective-permute-start | bytes 1572872 | tf_op jit(solution)/shard_map/ppermute | solution.py:555
  100.8 0.8 copy-start.12
  108.1 14.3 %collective-permute-start.22 = (bf16[128,2048]{1,0:T(8,128)(2,1)}, bf16[128,2048]{1,0:T(8,128)(2,1)S(1)}, u32[]{:S(2)}, u32[]{:S(2)}) collective-permute-start(bf16[128,2048]{1,0:T(8,128)(2,1)} %get-tuple-element.52), channel_id=1, source_target_pairs={{0,6},{1,7},{2,4},{3,5},{4,2},{5,3},{6,0},{7,1},{8,14},{9,15},{10,... | collective-permute-start | bytes 1572872 | tf_op jit(solution)/shard_map/ppermute | solution.py:555
  109.2 24.4 %collective-permute-start.23 = (bf16[128,2048]{1,0:T(8,128)(2,1)}, bf16[128,2048]{1,0:T(8,128)(2,1)S(1)}, u32[]{:S(2)}, u32[]{:S(2)}) collective-permute-start(bf16[128,2048]{1,0:T(8,128)(2,1)} %get-tuple-element.53), channel_id=1, source_target_pairs={{0,4},{1,5},{2,6},{3,7},{4,0},{5,1},{6,2},{7,3},{8,12},{9,13},{10,... | collective-permute-start | bytes 1572872 | tf_op jit(solution)/shard_map/ppermute | solution.py:555
  110.3 24.2 %collective-permute-start.24 = (bf16[128,2048]{1,0:T(8,128)(2,1)}, bf16[128,2048]{1,0:T(8,128)(2,1)}, u32[]{:S(2)}, u32[]{:S(2)}) collective-permute-start(bf16[128,2048]{1,0:T(8,128)(2,1)} %get-tuple-element.54), channel_id=1, source_target_pairs={{0,2},{1,3},{2,0},{3,1},{4,6},{5,7},{6,4},{7,5},{8,10},{9,11},{10,... | collective-permute-start | bytes 1572872 | tf_op jit(solution)/shard_map/ppermute | solution.py:555
  136.7 51.5 %copy-start.2 = (f32[128,2048]{1,0:T(8,128)}, f32[128,2048]{1,0:T(8,128)S(1)}, u32[]{:S(2)}) copy-start(f32[128,2048]{1,0:T(8,128)S(1)} %get-tuple-element.56.stream_ref) | copy-start | bytes 3145732
  193.9 1.4 copy-start.1
  195.2 5.3 %copy-start.10 = (f32[128,1,2]{0,2,1:T(2,128)S(1)}, f32[128,1,2]{0,2,1:T(2,128)}, u32[]{:S(2)}) copy-start(f32[128,1,2]{0,2,1:T(2,128)} %param.17) | copy-start | bytes 3076
  195.2 52.7 %all-to-all-start.2 = ((bf16[16,32,2048]{2,1,0:T(8,128)(2,1)}), bf16[16,32,2048]{2,1,0:T(8,128)(2,1)S(1)}, u32[]{:S(2)}, u32[]{:S(2)}) async-start(bf16[16,32,2048]{2,1,0:T(8,128)(2,1)} %bitcast.46), calls=%async_computation.2 | async-start | bytes 4194304 | tf_op jit(solution)/shard_map/all_to_all | solution.py:751
  247.9 1.2 copy-start.3

commit v8 on v7

--- a/solution.py
+++ b/solution.py
@@ -139,9 +139,7 @@
     page_c,
     page_cy,
     kv_own,
-    kv_y,
     kv_c,
-    kv_cy,
     o_ref,
     q_ref,
     old_ref,
@@ -153,7 +151,7 @@
     me = lax.axis_index("head")
     members, heads, piece, _ = q_hbm.shape
     length = members * piece
-    planes = kv_own.shape[0]
+    planes, sides = kv_own.shape[:2]
     old = old_ref.shape[0]
     earlier_group = me // members > 0
     core = lax.rem(me, 2)
@@ -172,14 +170,15 @@
         count = page.shape[0]
         bring(page, old_ref.at[pl.ds(place, count)], 1)
         place += count
-    for flip, pieces_of in ((0, kv_own), (2, kv_y), (1, kv_c), (3, kv_cy)):
+    for flip, pieces_of in ((0, kv_own), (1, kv_c)):
         for t in range(planes):
-            number = jnp.bitwise_and(
-                jnp.bitwise_xor(me, flip ^ (t * (members // 2))), members - 1
-            )
-            start = pl.multiple_of(number * piece, piece)
-            area = 0 if t * (members // 2) >= members else length
-            bring(pieces_of.at[t], kv_ref.at[pl.ds(area + start, piece)], 2)
+            for u in range(sides):
+                number = jnp.bitwise_and(
+                    jnp.bitwise_xor(me, flip ^ (2 * u) ^ (t * (members // 2))), members - 1
+                )
+                start = pl.multiple_of(number * piece, piece)
+                area = 0 if t * (members // 2) >= members else length
+                bring(pieces_of.at[t, u], kv_ref.at[pl.ds(area + start, piece)], 2)
     for copy in copies:
         copy.wait()
     scale = width**-0.5 * LOG2_E
@@ -254,7 +253,7 @@
     members, heads, piece, width = q.shape
     length = members * piece
     old = sum(page.shape[0] for page in pages)
-    block = min(4 * piece, length)
+    block = 2 * piece
     chunk = min(512, old, length)
     keys = old + 2 * length
     return pl.pallas_call(
@@ -281,7 +280,7 @@
 
 
 def project_pair_kernel(a_ref, got_ref, *refs):
-    near, far, outs, (w_ref, sems) = refs[:4], refs[4:8], refs[8:-2], refs[-2:]
+    near, far, outs, (w_ref, all_ref, sems) = refs[:4], refs[4:8], refs[8:-3], refs[-3:]
     me = lax.axis_index("head")
     half = lax.axis_index("grp")
     core = lax.rem(me, 2)
@@ -303,33 +302,21 @@
                     )
                     copy.start()
                     copies.append(copy)
-    rows = outs[0].shape[0]
-    starts = [
-        pl.multiple_of(jnp.bitwise_xor(chip, k) * rows, rows) for k in range(len(outs))
-    ]
-    blocks = []
-    for k in range(heads):
-        mine = k < heads // 2
-        column = (k % (heads // 2)) * width
-        at = pl.ds(column, width)
-        blocks.append(
-            jnp.concatenate(
-                [
-                    a_ref[0, pl.ds(start, rows), at] if mine else got_ref[pl.ds(start, rows), at]
-                    for start in starts
-                ],
-                0,
-            )
-        )
     for copy in copies:
         copy.wait()
     acc = None
     for k in range(heads):
-        head = jnp.bitwise_xor(core, 0 if k < heads // 2 else 1) * (heads // 2) + k % (heads // 2)
-        part = jnp.dot(blocks[k], w_ref[head], preferred_element_type=F32)
+        mine = k < heads // 2
+        at = pl.ds((k % (heads // 2)) * width, width)
+        rows_of = a_ref[0, :, at] if mine else got_ref[:, at]
+        head = jnp.bitwise_xor(core, 0 if mine else 1) * (heads // 2) + k % (heads // 2)
+        part = jnp.dot(rows_of, w_ref[head], preferred_element_type=F32)
         acc = part if acc is None else acc + part
+    all_ref[...] = acc.astype(BF16)
+    rows = outs[0].shape[0]
     for k, out in enumerate(outs):
-        out[...] = acc[k * rows : (k + 1) * rows].astype(BF16)
+        start = pl.multiple_of(jnp.bitwise_xor(chip, k) * rows, rows)
+        out[...] = all_ref[pl.ds(start, rows), :]
 
 
 def project_pair(a, got, near, far, parts):
@@ -344,6 +331,7 @@
         out_specs=[in_vmem()] * parts,
         scratch_shapes=[
             pltpu.VMEM((heads, width, model), BF16),
+            pltpu.VMEM((rows, model), BF16),
             pltpu.SemaphoreType.DMA((1,)),
         ],
         compiler_params=pltpu.CompilerParams(vmem_limit_bytes=HIGH_VMEM),
@@ -584,49 +572,44 @@
         for other in range(2)
     )
     kv_heads = new_kv.reshape(local_rows, pair_heads, 2 * width).transpose(1, 0, 2)
-    kv_same = lax.dynamic_index_in_dim(kv_heads, b, 0, keepdims=False)
-    kv_other = lax.dynamic_index_in_dim(kv_heads, 1 - b, 0, keepdims=False)
+    kv_beside = flipped(kv_heads, "head", 2)
+
     columns = model // 2
     w = lax.dynamic_slice_in_dim(w_out, lax.axis_index("grp") * columns, columns, 2)
     w = w.reshape(2, 2, heads // 4, share, columns)
     w_keep = lax.dynamic_index_in_dim(w, y, 1, keepdims=False)
     w_give = lax.dynamic_index_in_dim(w, 1 - y, 1, keepdims=False)
     w_got = flipped(w_give, "head", 2)
-    kv_last, w_got = lax.optimization_barrier((kv_other, w_got))
-    kv_own = [
-        kv_same,
-        flipped(kv_other, "head", plane_bit),
-        flipped(kv_same, "head", 2 * plane_bit),
-        flipped(kv_last, "head", 3 * plane_bit),
-    ]
-
-    (page_a, page_b, kv_own, q), w_got = lax.optimization_barrier(
-        ((page_a, page_b, kv_own, q), w_got)
-    )
+
+    page_a, page_b, kv_beside, w_got = lax.optimization_barrier(
+        (page_a, page_b, kv_beside, w_got)
+    )
+    kv_both = jnp.stack([kv_heads, kv_beside], 1)
+    kv_same = lax.dynamic_index_in_dim(kv_both, b, 0, keepdims=False)
+    kv_other = lax.dynamic_index_in_dim(kv_both, 1 - b, 0, keepdims=False)
+    kv_own = [kv_same]
+    for t in range(1, planes):
+        kv_own.append(flipped(kv_other if t % 2 else kv_same, "head", t * plane_bit))
     own_pages = jnp.concatenate([page_a, page_b], 0)
-    kv_own = jnp.stack(kv_own, 0)
     pages_y = flipped(own_pages, "head", 2)
-    kv_y = flipped(kv_own, "head", 2)
     w_both = jnp.stack([w_keep, w_got], 1)
     w_same = lax.dynamic_index_in_dim(w_both, b, 0, keepdims=False)
     w_other = lax.dynamic_index_in_dim(w_both, 1 - b, 0, keepdims=False)
-    w_near = jnp.stack([w_same, flipped(w_other, "head", plane_bit)], 0)
+    w_first = flipped(w_other, "head", plane_bit)
+    pages_y, kv_own, w_first, q = lax.optimization_barrier((pages_y, kv_own, w_first, q))
+
+    kv_own = jnp.stack(kv_own, 0)
+    kv_c = flipped(kv_own, "head", 1)
+    pages_c = flipped(own_pages, "head", 1)
+    pages_cy = flipped(pages_y, "head", 1)
+    w_near = jnp.stack([w_same, w_first], 0)
+    w_far = flipped(w_near, "head", members)
     w_near_x = flipped(w_near, "grp", 1)
-    w_far = [flipped(w_same, "head", 2 * plane_bit), flipped(w_other, "head", 3 * plane_bit)]
-    pages_c = flipped(own_pages, "head", 1)
-    kv_c = flipped(kv_own, "head", 1)
-    (pages_y, kv_y), w_far = lax.optimization_barrier(((pages_y, kv_y), w_far))
-    pages_cy = flipped(pages_y, "head", 1)
-    kv_cy = flipped(kv_y, "head", 1)
-    w_far = jnp.stack(w_far, 0)
-    q, w_far = lax.optimization_barrier((q, w_far))
+    a = attend_pair(q, (page_a, page_b, pages_y, pages_c, pages_cy), (kv_own, kv_c))
+    got = flipped(a[1], "head", 1)
+    a, w_far, w_near_x = lax.optimization_barrier((a, w_far, w_near_x))
     w_far_x = flipped(w_far, "grp", 1)
     w_near_c = flipped(w_near, "head", 1)
-    a = attend_pair(
-        q, (page_a, page_b, pages_y, pages_c, pages_cy), (kv_own, kv_y, kv_c, kv_cy)
-    )
-    got = flipped(a[1], "head", 1)
-    a, w_near_x, w_far_x, w_near_c = lax.optimization_barrier((a, w_near_x, w_far_x, w_near_c))
     w_far_c = flipped(w_far, "head", 1)
     w_near_cx = flipped(w_near_x, "head", 1)
     w_far_cx = flipped(w_far_x, "head", 1)

time: 251 us -> 260 us (1.036)
  waiting for transfers between devices: 120 us -> 125 us
  starting transfers between devices: 38 us -> 34.2 us
  other arithmetic: 1.42 us -> 5.2 us
    ppermute x23 -> x21, waiting for transfers between devices: 72.5 us -> 77.6 us  [flipped(): return lax.ppermute(value, axis, pairs)]
    ppermute x23 -> x21, starting transfers between devices: 25 us -> 21.1 us  [flipped(): return lax.ppermute(value, axis, pairs)]
    unnamed x31 -> x48, local copies, waits for them, and re-layouts: 3.71 us -> 6.21 us
  transfers between devices with their start and end apart: 27 -> 25, of which waited for: 15 -> 14; matrix products, arithmetic and copies ran while one was open for 1% -> 2% of each run, Pallas kernels for 6% -> 6%
where the time goes in v8:
time: 260 us; the launch traced here: 259 us
  waiting for transfers between devices  125 us (48%)
  blocking collectives  52.6 us (20%)
  starting transfers between devices  34.2 us (13%)
  Pallas kernels  32 us (12%)
  local copies, waits for them, and re-layouts  10.1 us (4%)
  other arithmetic  5.2 us (2%)
    ppermute x21, waiting for transfers between devices, flipped(): return lax.ppermute(value, axis, pairs)  77.6 us
    all_to_all x1, blocking collectives, local(): lax.all_to_all(outgoing.reshape(n, slots // n, model), 'head', split_axis...  52.6 us
    all_to_all x1, waiting for transfers between devices, local(): lax.all_to_all(answered, 'head', split_axis=0, concat_axis=0, tiled=True)  47.3 us
    ppermute x21, starting transfers between devices, flipped(): return lax.ppermute(value, axis, pairs)  21.1 us
    pallas_call x1, Pallas kernels, attend_pair(): pl.pallas_call(functools.partial(attend_pair_kernel, block, chunk, width)...  15.7 us
    pallas_call x1, Pallas kernels, project_pair(): pl.pallas_call(project_pair_kernel, out_shape=[jax.ShapeDtypeStruct((rows...  6.83 us
    unnamed x48, local copies, waits for them, and re-layouts  6.21 us
    pallas_call x1, Pallas kernels, expert_pair(): pl.pallas_call(kernel, out_shape=jax.ShapeDtypeStruct((rows, model), BF16...  5.69 us
  transfers between devices with their start and end apart: 25, of which 14 were waited for; matrix products, arithmetic and copies ran while one was open for 2% of the time, Pallas kernels for 6%

profile of v8, /device:TPU:13, one launch (start us, length us, event | category | flops | bytes accessed | tf_op | source)
XLA Modules:
  0.0 259.3 jit_solution(11012098470181371615)
XLA Ops:
  0.0 2.6 %copy.29 = bf16[16,128,256]{2,1,0:T(8,128)(2,1)} copy(bf16[16,128,256]{2,0,1:T(8,128)(2,1)} %bitcast.64) | data formatting | bytes 2097152 | tf_op jit(solution)/shard_map/transpose | solution.py:560
  2.7 4.6 %all-to-all-start = ((bf16[8,2,128,256]{3,2,1,0:T(8,128)(2,1)}), bf16[8,2,128,256]{3,2,1,0:T(8,128)(2,1)S(1)}, u32[]{:S(2)}, u32[]{:S(2)}) async-start(bf16[8,2,128,256]{3,2,1,0:T(8,128)(2,1)} %bitcast.19), calls=%async_computation | async-start | bytes 2097152 | tf_op jit(solution)/shard_map/all_to_all | solution.py:562
  7.8 1.2 collective-permute-start.2
  9.0 3.3 %collective-permute-start = (bf16[256,512]{1,0:T(8,128)(2,1)}, bf16[256,512]{1,0:T(8,128)(2,1)S(1)}, u32[]{:S(2)}, u32[]{:S(2)}) collective-permute-start(bf16[256,512]{1,0:T(8,128)(2,1)} %bitcast.4), channel_id=1, source_target_pairs={{0,0},{1,1},{2,2},{3,3},{4,8},{5,9},{6,10},{7,11},{8,4},{9,5},{10,... | collective-permute-start | bytes 786440 | tf_op jit(solution)/shard_map/ppermute | solution.py:571
  12.4 13.2 %collective-permute-done.3 = bf16[2,4,16,1024]{3,2,1,0:T(8,128)(2,1)S(1)} collective-permute-done((bf16[2,4,16,1024]{3,2,1,0:T(8,128)(2,1)S(1)}, bf16[2,4,16,1024]{3,2,1,0:T(8,128)(2,1)S(1)}, u32[]{:S(2)}, u32[]{:S(2)}) %collective-permute-start.3) | collective-permute-done | bytes 262176 | tf_op jit(solution)/shard_map/ppermute | solution.py:543
  25.6 5.6 %collective-permute-done.2 = bf16[2,128,512]{2,1,0:T(8,128)(2,1)S(1)} collective-permute-done((bf16[2,128,512]{2,1,0:T(8,128)(2,1)S(1)}, bf16[2,128,512]{2,1,0:T(8,128)(2,1)S(1)}, u32[]{:S(2)}, u32[]{:S(2)}) %collective-permute-start.2) | collective-permute-done | bytes 262176 | tf_op jit(solution)/shard_map/ppermute | solution.py:543
  31.2 0.8 constant_dynamic-update-slice_fusion.1
  32.0 0.7 constant_dynamic-update-slice_fusion
  32.8 1.0 collective-permute-start.4
  33.8 1.7 fusion
  35.8 1.8 fusion.4
  37.6 1.2 collective-permute-start.5
  38.8 2.3 collective-permute-start.6
  41.1 1.0 collective-permute-done.8
  42.1 9.3 %collective-permute-done.5 = bf16[2,128,512]{2,1,0:T(8,128)(2,1)S(1)} collective-permute-done((bf16[2,128,512]{2,1,0:T(8,128)(2,1)S(1)}, bf16[2,128,512]{2,1,0:T(8,128)(2,1)S(1)}, u32[]{:S(2)}, u32[]{:S(2)}) %collective-permute-start.5) | collective-permute-done | bytes 262176 | tf_op jit(solution)/shard_map/ppermute | solution.py:543
  51.4 3.1 %collective-permute-done.6 = bf16[2,128,512]{2,1,0:T(8,128)(2,1)S(1)} collective-permute-done((bf16[2,128,512]{2,1,0:T(8,128)(2,1)}, bf16[2,128,512]{2,1,0:T(8,128)(2,1)S(1)}, u32[]{:S(2)}, u32[]{:S(2)}) %collective-permute-start.6) | collective-permute-done | bytes 262176 | tf_op jit(solution)/shard_map/ppermute | solution.py:543
  54.5 7.6 %collective-permute-done.7 = bf16[2,128,512]{2,1,0:T(8,128)(2,1)S(1)} collective-permute-done((bf16[2,128,512]{2,1,0:T(8,128)(2,1)S(1)}, bf16[2,128,512]{2,1,0:T(8,128)(2,1)S(1)}, u32[]{:S(2)}, u32[]{:S(2)}) %collective-permute-start.7) | collective-permute-done | bytes 262176 | tf_op jit(solution)/shard_map/ppermute | solution.py:543
  62.1 0.7 copy-done.16
  62.9 1.4 pad_maximum_fusion.kv_own
  64.2 2.7 %collective-permute-start.11 = (bf16[4,2,128,512]{3,2,1,0:T(8,128)(2,1)S(1)}, bf16[4,2,128,512]{3,2,1,0:T(8,128)(2,1)S(1)}, u32[]{:S(2)}, u32[]{:S(2)}) collective-permute-start(bf16[4,2,128,512]{3,2,1,0:T(8,128)(2,1)S(1)} %pad_maximum_fusion.kv_own), channel_id=1, source_target_pairs={{0,1},{1,0},{2,3},{3,2},{4,5},{5,4},{6,7},{7,6},{8,9},{9,8},{10,11... | collective-permute-start | bytes 3145736 | tf_op jit(solution)/shard_map/ppermute | solution.py:543
  67.0 0.4 collective-permute-start.10
  67.4 0.5 collective-permute-start.12
  67.9 1.2 collective-permute-start.13
  69.1 1.6 collective-permute-done.9.page_c
  70.7 1.0 copy-done.19
  71.7 15.7 %attend.1.a_ref = bf16[2,512,512]{2,1,0:T(8,128)(2,1)S(1)} custom-call(bf16[8,2,128,256]{3,2,1,0:T(8,128)(2,1)S(1)} %all-to-all-done.q_hbm, bf16[256,512]{1,0:T(8,128)(2,1)S(1)} %collective-permute-done.page_a, bf16[256,512]{1,0:T(8,128)(2,1)S(1)} %collective-permute-done.1.page_b, bf16[512,512]{1,0:T(8,128)(2,1)S(1)} %collective-permute-done.4.page_y, ...), custom_call_target="tpu_custom_call" | custom-call | flops 7516192768 | bytes 6291456 | tf_op jit(solution)/shard_map/attend/pallas_call | solution.py:259
  87.5 2.9 %collective-permute-done.12.refs_4_ = bf16[2,2,4,16,1024]{4,3,2,1,0:T(8,128)(2,1)S(1)} collective-permute-done((bf16[2,2,4,16,1024]{4,3,2,1,0:T(8,128)(2,1)S(1)}, bf16[2,2,4,16,1024]{4,3,2,1,0:T(8,128)(2,1)S(1)}, u32[]{:S(2)}, u32[]{:S(2)}) %collective-permute-start.12) | collective-permute-done | bytes 524320 | tf_op jit(solution)/shard_map/ppermute | solution.py:543
  90.4 1.2 collective-permute-start.18
  91.6 1.1 collective-permute-start.15
  92.8 0.6 collective-permute-start.16
  93.5 9.5 %collective-permute-done.18.refs_6_ = bf16[2,2,4,16,1024]{4,3,2,1,0:T(8,128)(2,1)S(1)} collective-permute-done((bf16[2,2,4,16,1024]{4,3,2,1,0:T(8,128)(2,1)S(1)}, bf16[2,2,4,16,1024]{4,3,2,1,0:T(8,128)(2,1)S(1)}, u32[]{:S(2)}, u32[]{:S(2)}) %collective-permute-start.18) | collective-permute-done | bytes 524320 | tf_op jit(solution)/shard_map/ppermute | solution.py:543
  103.0 1.7 collective-permute-start.19
  104.8 1.5 collective-permute-done.19.refs_7_
  106.3 0.8 copy-done.21
  107.1 6.8 %project.1 = (bf16[128,2048]{1,0:T(8,128)(2,1)S(1)}, bf16[128,2048]{1,0:T(8,128)(2,1)}, bf16[128,2048]{1,0:T(8,128)(2,1)}, bf16[128,2048]{1,0:T(8,128)(2,1)}) custom-call(bf16[2,512,512]{2,1,0:T(8,128)(2,1)} %copy-done.5, bf16[512,512]{1,0:T(8,128)(2,1)S(1)} %collective-permute-done.14.got_ref, bf16[2,2,4,16,1024]{4,3,2,1,0:T(8,128)(2,1)S(1)} %pad_maximum_fusion.1.refs_0_, ...), custom_call_target="tpu_custom_call" | custom-call | flops 2147483648 | bytes 7340032 | tf_op jit(solution)/shard_map/project/pallas_call | solution.py:327
  114.0 4.2 %collective-permute-start.20 = (bf16[128,2048]{1,0:T(8,128)(2,1)}, bf16[128,2048]{1,0:T(8,128)(2,1)S(1)}, u32[]{:S(2)}, u32[]{:S(2)}) collective-permute-start(bf16[128,2048]{1,0:T(8,128)(2,1)} %get-tuple-element.40), channel_id=1, source_target_pairs={{0,6},{1,7},{2,4},{3,5},{4,2},{5,3},{6,0},{7,1},{8,14},{9,15},{10,... | collective-permute-start | bytes 1572872 | tf_op jit(solution)/shard_map/ppermute | solution.py:543
  118.1 1.0 collective-permute-start.22
  119.9 10.5 %collective-permute-done.20 = bf16[128,2048]{1,0:T(8,128)(2,1)S(1)} collective-permute-done((bf16[128,2048]{1,0:T(8,128)(2,1)}, bf16[128,2048]{1,0:T(8,128)(2,1)S(1)}, u32[]{:S(2)}, u32[]{:S(2)}) %collective-permute-start.20) | collective-permute-done | bytes 524320 | tf_op jit(solution)/shard_map/ppermute | solution.py:543
  130.4 11.1 %collective-permute-done.21 = bf16[128,2048]{1,0:T(8,128)(2,1)S(1)} collective-permute-done((bf16[128,2048]{1,0:T(8,128)(2,1)}, bf16[128,2048]{1,0:T(8,128)(2,1)S(1)}, u32[]{:S(2)}, u32[]{:S(2)}) %collective-permute-start.21) | collective-permute-done | bytes 524320 | tf_op jit(solution)/shard_map/ppermute | solution.py:543
  141.5 0.6 collective-permute-done.22
  142.1 2.2 route.1
  144.3 52.6 %all_to_all.15 = bf16[16,32,2048]{2,1,0:T(8,128)(2,1)S(1)} all-to-all(bf16[16,32,2048]{2,1,0:T(8,128)(2,1)S(1)} %bitcast.51), channel_id=1, replica_groups=mesh['grp'=2,'head'=16] {'head'}, dimensions={0} | all-to-all | bytes 4194304 | tf_op jit(solution)/shard_map/all_to_all | solution.py:721
  196.9 5.7 %expert.1 = bf16[512,2048]{1,0:T(8,128)(2,1)S(1)} custom-call(bf16[512,2048]{1,0:T(8,128)(2,1)S(1)} %bitcast.53, bf16[2048,1024]{1,0:T(8,128)(2,1)} %bitcast.72, bf16[512,2048]{1,0:T(8,128)(2,1)} %bitcast.73), custom_call_target="tpu_custom_call" | custom-call | flops 3221225472 | bytes 10485760 | tf_op jit(solution)/shard_map/expert/pallas_call | solution.py:483
  202.6 1.3 copy-done.1
  203.9 5.1 %all-to-all-start.2 = ((bf16[16,32,2048]{2,1,0:T(8,128)(2,1)}), bf16[16,32,2048]{2,1,0:T(8,128)(2,1)S(1)}, u32[]{:S(2)}, u32[]{:S(2)}) async-start(bf16[16,32,2048]{2,1,0:T(8,128)(2,1)} %bitcast.52), calls=%async_computation.2 | async-start | bytes 4194304 | tf_op jit(solution)/shard_map/all_to_all | solution.py:734
  209.2 47.3 %all-to-all-done.2 = bf16[16,32,2048]{2,1,0:T(8,128)(2,1)S(1)} async-done(((bf16[16,32,2048]{2,1,0:T(8,128)(2,1)}), bf16[16,32,2048]{2,1,0:T(8,128)(2,1)S(1)}, u32[]{:S(2)}, u32[]{:S(2)}) %all-to-all-start.2) | async-done | bytes 2097184 | tf_op jit(solution)/shard_map/all_to_all | solution.py:734
  256.5 1.2 copy-done.3
  257.7 1.6 combine.1
  (75 shorter events, 2.0 us)
Async XLA Ops:
  0.0 7.3 %copy-start = (bf16[16,16,2048]{2,1,0:T(8,128)(2,1)S(1)}, bf16[16,16,2048]{2,1,0:T(8,128)(2,1)}, u32[]{:S(2)}) copy-start(bf16[16,16,2048]{2,1,0:T(8,128)(2,1)} %param.14) | copy-start | bytes 3145732
  2.7 5.1 %copy-start.11 = (bf16[128,1,2,512]{3,2,1,0:T(2,128)(2,1)S(1)}, bf16[128,1,2,512]{3,2,1,0:T(2,128)(2,1)}, u32[]{:S(2)}) copy-start(bf16[128,1,2,512]{3,2,1,0:T(2,128)(2,1)} %param.11) | copy-start | bytes 786436
  2.7 60.2 %all-to-all-start = ((bf16[8,2,128,256]{3,2,1,0:T(8,128)(2,1)}), bf16[8,2,128,256]{3,2,1,0:T(8,128)(2,1)S(1)}, u32[]{:S(2)}, u32[]{:S(2)}) async-start(bf16[8,2,128,256]{3,2,1,0:T(8,128)(2,1)} %bitcast.19), calls=%async_computation | async-start | bytes 2097152 | tf_op jit(solution)/shard_map/all_to_all | solution.py:562
  7.4 18.2 %collective-permute-start.3 = (bf16[2,4,16,1024]{3,2,1,0:T(8,128)(2,1)S(1)}, bf16[2,4,16,1024]{3,2,1,0:T(8,128)(2,1)S(1)}, u32[]{:S(2)}, u32[]{:S(2)}) collective-permute-start(bf16[2,4,16,1024]{3,2,1,0:T(8,128)(2,1)S(1)} %get-tuple-element.48), channel_id=1, source_target_pairs={{0,2},{1,3},{2,0},{3,1},{4,6},{5,7},{6,4},{7,5},{8,10},{9,11},{10,... | collective-permute-start | bytes 786440 | tf_op jit(solution)/shard_map/ppermute | solution.py:543
  7.8 24.2 %copy-start.7 = (bf16[128,1,2,512]{3,0,2,1:T(8,128)(2,1)}, bf16[128,1,2,512]{3,0,2,1:T(8,128)(2,1)S(1)}, u32[]{:S(2)}) copy-start(bf16[128,1,2,512]{3,0,2,1:T(8,128)(2,1)S(1)} %copy.34) | copy-start | bytes 786436
  7.8 23.4 %collective-permute-start.2 = (bf16[2,128,512]{2,1,0:T(8,128)(2,1)S(1)}, bf16[2,128,512]{2,1,0:T(8,128)(2,1)S(1)}, u32[]{:S(2)}, u32[]{:S(2)}) collective-permute-start(bf16[2,128,512]{2,1,0:T(8,128)(2,1)S(1)} %bitcast.62), channel_id=1, source_target_pairs={{0,2},{1,3},{2,0},{3,1},{4,6},{5,7},{6,4},{7,5},{8,10},{9,11},{10,... | collective-permute-start | bytes 786440 | tf_op jit(solution)/shard_map/ppermute | solution.py:543
  9.0 22.2 %collective-permute-start = (bf16[256,512]{1,0:T(8,128)(2,1)}, bf16[256,512]{1,0:T(8,128)(2,1)S(1)}, u32[]{:S(2)}, u32[]{:S(2)}) collective-permute-start(bf16[256,512]{1,0:T(8,128)(2,1)} %bitcast.4), channel_id=1, source_target_pairs={{0,0},{1,1},{2,2},{3,3},{4,8},{5,9},{6,10},{7,11},{8,4},{9,5},{10,... | collective-permute-start | bytes 786440 | tf_op jit(solution)/shard_map/ppermute | solution.py:571
  12.4 18.9 %collective-permute-start.1 = (bf16[256,512]{1,0:T(8,128)(2,1)}, bf16[256,512]{1,0:T(8,128)(2,1)S(1)}, u32[]{:S(2)}, u32[]{:S(2)}) collective-permute-start(bf16[256,512]{1,0:T(8,128)(2,1)} %bitcast.4), channel_id=1, source_target_pairs={{0,8},{1,9},{2,10},{3,11},{4,0},{5,1},{6,2},{7,3},{8,12},{9,13},{1... | collective-permute-start | bytes 786440 | tf_op jit(solution)/shard_map/ppermute | solution.py:571
  25.6 7.2 %copy-start.10 = (bf16[2,4,16,1024]{3,2,1,0:T(8,128)(2,1)}, bf16[2,4,16,1024]{3,2,1,0:T(8,128)(2,1)S(1)}, u32[]{:S(2)}) copy-start(bf16[2,4,16,1024]{3,2,1,0:T(8,128)(2,1)S(1)} %collective-permute-done.3) | copy-start | bytes 786436
  31.2 0.8 copy-start.9
  32.8 30.1 %collective-permute-start.4 = (bf16[512,512]{1,0:T(8,128)(2,1)}, bf16[512,512]{1,0:T(8,128)(2,1)S(1)}, u32[]{:S(2)}, u32[]{:S(2)}) collective-permute-start(bf16[512,512]{1,0:T(8,128)(2,1)} %constant_dynamic-update-slice_fusion), channel_id=1, source_target_pairs={{0,2},{1,3},{2,0},{3,1},{4,6},{5,7},{6,4},{7,5},{8,10},{9,11},{10,... | collective-permute-start | bytes 1572872 | tf_op jit(solution)/shard_map/ppermute | solution.py:543
  35.5 31.9 %copy-start.8 = (bf16[1,2,4,16,1024]{4,3,2,1,0:T(8,128)(2,1)S(1)}, bf16[1,2,4,16,1024]{4,3,2,1,0:T(8,128)(2,1)}, u32[]{:S(2)}) copy-start(bf16[1,2,4,16,1024]{4,3,2,1,0:T(8,128)(2,1)} %get-tuple-element.45) | copy-start | bytes 786436
  35.5 6.6 %collective-permute-start.8 = (bf16[2,4,16,1024]{3,2,1,0:T(8,128)(2,1)S(1)}, bf16[2,4,16,1024]{3,2,1,0:T(8,128)(2,1)S(1)}, u32[]{:S(2)}, u32[]{:S(2)}) collective-permute-start(bf16[2,4,16,1024]{3,2,1,0:T(8,128)(2,1)S(1)} %get-tuple-element.46), channel_id=1, source_target_pairs={{0,4},{1,5},{2,6},{3,7},{4,0},{5,1},{6,2},{7,3},{8,12},{9,13},{10,... | collective-permute-start | bytes 786440 | tf_op jit(solution)/shard_map/ppermute | solution.py:543
  37.6 13.8 %collective-permute-start.5 = (bf16[2,128,512]{2,1,0:T(8,128)(2,1)S(1)}, bf16[2,128,512]{2,1,0:T(8,128)(2,1)S(1)}, u32[]{:S(2)}, u32[]{:S(2)}) collective-permute-start(bf16[2,128,512]{2,1,0:T(8,128)(2,1)S(1)} %get-tuple-element.49), channel_id=1, source_target_pairs={{0,4},{1,5},{2,6},{3,7},{4,0},{5,1},{6,2},{7,3},{8,12},{9,13},{10,... | collective-permute-start | bytes 786440 | tf_op jit(solution)/shard_map/ppermute | solution.py:543
  38.8 15.8 %collective-permute-start.6 = (bf16[2,128,512]{2,1,0:T(8,128)(2,1)}, bf16[2,128,512]{2,1,0:T(8,128)(2,1)S(1)}, u32[]{:S(2)}, u32[]{:S(2)}) collective-permute-start(bf16[2,128,512]{2,1,0:T(8,128)(2,1)} %get-tuple-element.31), channel_id=1, source_target_pairs={{0,8},{1,9},{2,10},{3,11},{4,12},{5,13},{6,14},{7,15},{8,0},{9,1},... | collective-permute-start | bytes 786440 | tf_op jit(solution)/shard_map/ppermute | solution.py:543
  41.1 21.0 %collective-permute-start.7 = (bf16[2,128,512]{2,1,0:T(8,128)(2,1)S(1)}, bf16[2,128,512]{2,1,0:T(8,128)(2,1)S(1)}, u32[]{:S(2)}, u32[]{:S(2)}) collective-permute-start(bf16[2,128,512]{2,1,0:T(8,128)(2,1)S(1)} %get-tuple-element.49), channel_id=1, source_target_pairs={{0,12},{1,13},{2,14},{3,15},{4,8},{5,9},{6,10},{7,11},{8,4},{9,5},... | collective-permute-start | bytes 786440 | tf_op jit(solution)/shard_map/ppermute | solution.py:543
  42.1 20.0 %copy-start.12 = (bf16[2,4,16,1024]{3,2,1,0:T(8,128)(2,1)}, bf16[2,4,16,1024]{3,2,1,0:T(8,128)(2,1)S(1)}, u32[]{:S(2)}) copy-start(bf16[2,4,16,1024]{3,2,1,0:T(8,128)(2,1)S(1)} %collective-permute-done.8) | copy-start | bytes 786436
  51.4 10.7 %copy-start.14 = (bf16[2,128,512]{2,1,0:T(8,128)(2,1)}, bf16[2,128,512]{2,1,0:T(8,128)(2,1)S(1)}, u32[]{:S(2)}) copy-start(bf16[2,128,512]{2,1,0:T(8,128)(2,1)S(1)} %collective-permute-done.5) | copy-start | bytes 786436
  54.5 7.6 %copy-start.15 = (bf16[2,128,512]{2,1,0:T(8,128)(2,1)}, bf16[2,128,512]{2,1,0:T(8,128)(2,1)S(1)}, u32[]{:S(2)}) copy-start(bf16[2,128,512]{2,1,0:T(8,128)(2,1)S(1)} %collective-permute-done.6) | copy-start | bytes 786436
  62.1 0.7 copy-start.16
  62.8 4.5 %copy-start.13 = (bf16[2,4,16,1024]{3,2,1,0:T(8,128)(2,1)S(1)}, bf16[2,4,16,1024]{3,2,1,0:T(8,128)(2,1)}, u32[]{:S(2)}) copy-start(bf16[2,4,16,1024]{3,2,1,0:T(8,128)(2,1)} %copy-done.12) | copy-start | bytes 786436
  64.2 6.5 %collective-permute-start.11 = (bf16[4,2,128,512]{3,2,1,0:T(8,128)(2,1)S(1)}, bf16[4,2,128,512]{3,2,1,0:T(8,128)(2,1)S(1)}, u32[]{:S(2)}, u32[]{:S(2)}) collective-permute-start(bf16[4,2,128,512]{3,2,1,0:T(8,128)(2,1)S(1)} %pad_maximum_fusion.kv_own), channel_id=1, source_target_pairs={{0,1},{1,0},{2,3},{3,2},{4,5},{5,4},{6,7},{7,6},{8,9},{9,8},{10,11... | collective-permute-start | bytes 3145736 | tf_op jit(solution)/shard_map/ppermute | solution.py:543
  66.9 3.9 %collective-permute-start.9 = (bf16[512,512]{1,0:T(8,128)(2,1)}, bf16[512,512]{1,0:T(8,128)(2,1)S(1)}, u32[]{:S(2)}, u32[]{:S(2)}) collective-permute-start(bf16[512,512]{1,0:T(8,128)(2,1)} %constant_dynamic-update-slice_fusion), channel_id=1, source_target_pairs={{0,1},{1,0},{2,3},{3,2},{4,5},{5,4},{6,7},{7,6},{8,9},{9,8},{10,11... | collective-permute-start | bytes 1572872 | tf_op jit(solution)/shard_map/ppermute | solution.py:543
  67.0 3.8 %collective-permute-start.10 = (bf16[512,512]{1,0:T(8,128)(2,1)S(1)}, bf16[512,512]{1,0:T(8,128)(2,1)S(1)}, u32[]{:S(2)}, u32[]{:S(2)}) collective-permute-start(bf16[512,512]{1,0:T(8,128)(2,1)S(1)} %collective-permute-done.4.page_y), channel_id=1, source_target_pairs={{0,1},{1,0},{2,3},{3,2},{4,5},{5,4},{6,7},{7,6},{8,9},{9,8},{10,11... | collective-permute-start | bytes 1572872 | tf_op jit(solution)/shard_map/ppermute | solution.py:543
  67.4 23.0 %collective-permute-start.12 = (bf16[2,2,4,16,1024]{4,3,2,1,0:T(8,128)(2,1)S(1)}, bf16[2,2,4,16,1024]{4,3,2,1,0:T(8,128)(2,1)S(1)}, u32[]{:S(2)}, u32[]{:S(2)}) collective-permute-start(bf16[2,2,4,16,1024]{4,3,2,1,0:T(8,128)(2,1)S(1)} %pad_maximum_fusion.1.refs_0_), channel_id=1, source_target_pairs={{0,8},{1,9},{2,10},{3,11},{4,12},{5,13},{6,14},{7,15},{8,0},{9,1},... | collective-permute-start | bytes 1572872 | tf_op jit(solution)/shard_map/ppermute | solution.py:543
  67.9 22.5 %collective-permute-start.13 = (bf16[2,2,4,16,1024]{4,3,2,1,0:T(8,128)(2,1)S(1)}, bf16[2,2,4,16,1024]{4,3,2,1,0:T(8,128)(2,1)S(1)}, u32[]{:S(2)}, u32[]{:S(2)}) collective-permute-start(bf16[2,2,4,16,1024]{4,3,2,1,0:T(8,128)(2,1)S(1)} %pad_maximum_fusion.1.refs_0_), channel_id=1, source_target_pairs={{0,16},{16,0},{1,17},{17,1},{2,18},{18,2},{3,19},{19,3},{4,20},{20... | collective-permute-start | bytes 1572872 | tf_op jit(solution)/shard_map/ppermute | solution.py:543
  70.7 1.0 copy-start.19
  87.5 18.8 %copy-start.5 = (bf16[2,512,512]{2,1,0:T(8,128)(2,1)}, bf16[2,512,512]{2,1,0:T(8,128)(2,1)S(1)}, u32[]{:S(2)}) copy-start(bf16[2,512,512]{2,1,0:T(8,128)(2,1)S(1)} %attend.1.a_ref) | copy-start | bytes 3145732
  90.4 12.6 %collective-permute-start.18 = (bf16[2,2,4,16,1024]{4,3,2,1,0:T(8,128)(2,1)S(1)}, bf16[2,2,4,16,1024]{4,3,2,1,0:T(8,128)(2,1)S(1)}, u32[]{:S(2)}, u32[]{:S(2)}) collective-permute-start(bf16[2,2,4,16,1024]{4,3,2,1,0:T(8,128)(2,1)S(1)} %collective-permute-done.12.refs_4_), channel_id=1, source_target_pairs={{0,16},{16,0},{1,17},{17,1},{2,18},{18,2},{3,19},{19,3},{4,20},{20... | collective-permute-start | bytes 1572872 | tf_op jit(solution)/shard_map/ppermute | solution.py:543
  91.6 13.1 %collective-permute-start.15 = (bf16[2,2,4,16,1024]{4,3,2,1,0:T(8,128)(2,1)S(1)}, bf16[2,2,4,16,1024]{4,3,2,1,0:T(8,128)(2,1)S(1)}, u32[]{:S(2)}, u32[]{:S(2)}) collective-permute-start(bf16[2,2,4,16,1024]{4,3,2,1,0:T(8,128)(2,1)S(1)} %pad_maximum_fusion.1.refs_0_), channel_id=1, source_target_pairs={{0,1},{1,0},{2,3},{3,2},{4,5},{5,4},{6,7},{7,6},{8,9},{9,8},{10,11... | collective-permute-start | bytes 1572872 | tf_op jit(solution)/shard_map/ppermute | solution.py:543
  92.8 12.0 %collective-permute-start.17 = (bf16[2,2,4,16,1024]{4,3,2,1,0:T(8,128)(2,1)S(1)}, bf16[2,2,4,16,1024]{4,3,2,1,0:T(8,128)(2,1)S(1)}, u32[]{:S(2)}, u32[]{:S(2)}) collective-permute-start(bf16[2,2,4,16,1024]{4,3,2,1,0:T(8,128)(2,1)S(1)} %collective-permute-done.12.refs_4_), channel_id=1, source_target_pairs={{0,1},{1,0},{2,3},{3,2},{4,5},{5,4},{6,7},{7,6},{8,9},{9,8},{10,11... | collective-permute-start | bytes 1572872 | tf_op jit(solution)/shard_map/ppermute | solution.py:543
  92.8 26.3 %copy-start.17 = (s32[128,1,2]{0,2,1:T(2,128)S(1)}, s32[128,1,2]{0,2,1:T(2,128)}, u32[]{:S(2)}) copy-start(s32[128,1,2]{0,2,1:T(2,128)} %param.16) | copy-start | bytes 3076
  92.8 49.2 %copy-start.4 = (bf16[128,1,2048]{2,0,1:T(8,128)(2,1)S(1)}, bf16[128,1,2048]{2,0,1:T(8,128)(2,1)}, u32[]{:S(2)}) copy-start(bf16[128,1,2048]{2,0,1:T(8,128)(2,1)} %param.13) | copy-start | bytes 1572868
  92.8 49.2 %copy-start.6 = (f32[2048]{0:T(1024)S(1)}, f32[2048]{0:T(1024)}, u32[]{:S(2)}) copy-start(f32[2048]{0:T(1024)} %param.15) | copy-start | bytes 24580
  92.8 11.9 %collective-permute-start.16 = (bf16[2,2,4,16,1024]{4,3,2,1,0:T(8,128)(2,1)S(1)}, bf16[2,2,4,16,1024]{4,3,2,1,0:T(8,128)(2,1)S(1)}, u32[]{:S(2)}, u32[]{:S(2)}) collective-permute-start(bf16[2,2,4,16,1024]{4,3,2,1,0:T(8,128)(2,1)S(1)} %collective-permute-done.13.refs_2_), channel_id=1, source_target_pairs={{0,1},{1,0},{2,3},{3,2},{4,5},{5,4},{6,7},{7,6},{8,9},{9,8},{10,11... | collective-permute-start | bytes 1572872 | tf_op jit(solution)/shard_map/ppermute | solution.py:543
  93.4 11.4 %collective-permute-start.14 = (bf16[512,512]{1,0:T(8,128)(2,1)S(1)}, bf16[512,512]{1,0:T(8,128)(2,1)S(1)}, u32[]{:S(2)}, u32[]{:S(2)}) collective-permute-start(bf16[512,512]{1,0:T(8,128)(2,1)S(1)} %slice_bitcast_fusion), channel_id=1, source_target_pairs={{0,1},{1,0},{2,3},{3,2},{4,5},{5,4},{6,7},{7,6},{8,9},{9,8},{10,11... | collective-permute-start | bytes 1572872 | tf_op jit(solution)/shard_map/ppermute | solution.py:543
  103.0 3.3 %copy-start.20 = (bf16[2,2,4,16,1024]{4,3,2,1,0:T(8,128)(2,1)}, bf16[2,2,4,16,1024]{4,3,2,1,0:T(8,128)(2,1)S(1)}, u32[]{:S(2)}) copy-start(bf16[2,2,4,16,1024]{4,3,2,1,0:T(8,128)(2,1)S(1)} %collective-permute-done.18.refs_6_) | copy-start | bytes 1572868
  103.0 3.3 %collective-permute-start.19 = (bf16[2,2,4,16,1024]{4,3,2,1,0:T(8,128)(2,1)S(1)}, bf16[2,2,4,16,1024]{4,3,2,1,0:T(8,128)(2,1)S(1)}, u32[]{:S(2)}, u32[]{:S(2)}) collective-permute-start(bf16[2,2,4,16,1024]{4,3,2,1,0:T(8,128)(2,1)S(1)} %collective-permute-done.18.refs_6_), channel_id=1, source_target_pairs={{0,1},{1,0},{2,3},{3,2},{4,5},{5,4},{6,7},{7,6},{8,9},{9,8},{10,11... | collective-permute-start | bytes 1572872 | tf_op jit(solution)/shard_map/ppermute | solution.py:543
  106.3 0.8 copy-start.21
  114.0 16.4 %collective-permute-start.20 = (bf16[128,2048]{1,0:T(8,128)(2,1)}, bf16[128,2048]{1,0:T(8,128)(2,1)S(1)}, u32[]{:S(2)}, u32[]{:S(2)}) collective-permute-start(bf16[128,2048]{1,0:T(8,128)(2,1)} %get-tuple-element.40), channel_id=1, source_target_pairs={{0,6},{1,7},{2,4},{3,5},{4,2},{5,3},{6,0},{7,1},{8,14},{9,15},{10,... | collective-permute-start | bytes 1572872 | tf_op jit(solution)/shard_map/ppermute | solution.py:543
  118.1 23.4 %collective-permute-start.21 = (bf16[128,2048]{1,0:T(8,128)(2,1)}, bf16[128,2048]{1,0:T(8,128)(2,1)S(1)}, u32[]{:S(2)}, u32[]{:S(2)}) collective-permute-start(bf16[128,2048]{1,0:T(8,128)(2,1)} %get-tuple-element.41), channel_id=1, source_target_pairs={{0,4},{1,5},{2,6},{3,7},{4,0},{5,1},{6,2},{7,3},{8,12},{9,13},{10,... | collective-permute-start | bytes 1572872 | tf_op jit(solution)/shard_map/ppermute | solution.py:543
  118.1 23.9 %collective-permute-start.22 = (bf16[128,2048]{1,0:T(8,128)(2,1)}, bf16[128,2048]{1,0:T(8,128)(2,1)}, u32[]{:S(2)}, u32[]{:S(2)}) collective-permute-start(bf16[128,2048]{1,0:T(8,128)(2,1)} %get-tuple-element.42), channel_id=1, source_target_pairs={{0,2},{1,3},{2,0},{3,1},{4,6},{5,7},{6,4},{7,5},{8,10},{9,11},{10,... | collective-permute-start | bytes 1572872 | tf_op jit(solution)/shard_map/ppermute | solution.py:543
  144.3 52.6 %copy-start.2 = (f32[128,2048]{1,0:T(8,128)}, f32[128,2048]{1,0:T(8,128)S(1)}, u32[]{:S(2)}) copy-start(f32[128,2048]{1,0:T(8,128)S(1)} %get-tuple-element.44.stream_ref) | copy-start | bytes 3145732
  202.6 1.4 copy-start.1
  203.9 5.1 %copy-start.18 = (f32[128,1,2]{0,2,1:T(2,128)S(1)}, f32[128,1,2]{0,2,1:T(2,128)}, u32[]{:S(2)}) copy-start(f32[128,1,2]{0,2,1:T(2,128)} %param.17) | copy-start | bytes 3076
  203.9 52.5 %all-to-all-start.2 = ((bf16[16,32,2048]{2,1,0:T(8,128)(2,1)}), bf16[16,32,2048]{2,1,0:T(8,128)(2,1)S(1)}, u32[]{:S(2)}, u32[]{:S(2)}) async-start(bf16[16,32,2048]{2,1,0:T(8,128)(2,1)} %bitcast.52), calls=%async_computation.2 | async-start | bytes 4194304 | tf_op jit(solution)/shard_map/all_to_all | solution.py:734
  256.5 1.2 copy-start.3

commit v9 on v8

--- a/solution.py
+++ b/solution.py
@@ -155,6 +155,7 @@
     old = old_ref.shape[0]
     earlier_group = me // members > 0
     core = lax.rem(me, 2)
+    chip = jnp.bitwise_and(me // 2, members // 2 - 1)
     copies = []
 
     def bring(source, target, sem):
@@ -244,9 +245,8 @@
         for k in range(0, block, piece):
             member = (b * block + k) // piece
             side = jnp.bitwise_xor(core, member % 2)
-            o_ref[side, pl.ds((member // 2) * piece, piece), pl.ds(head * width, width)] = done[
-                k : k + piece
-            ]
+            start = pl.multiple_of(jnp.bitwise_xor(chip, member // 2) * piece, piece)
+            o_ref[side, pl.ds(start, piece), pl.ds(head * width, width)] = done[k : k + piece]
 
 
 def attend_pair(q, pages, kvs):
@@ -280,11 +280,10 @@
 
 
 def project_pair_kernel(a_ref, got_ref, *refs):
-    near, far, outs, (w_ref, all_ref, sems) = refs[:4], refs[4:8], refs[8:-3], refs[-3:]
+    near, far, outs, (w_ref, sems) = refs[:4], refs[4:8], refs[8:-2], refs[-2:]
     me = lax.axis_index("head")
     half = lax.axis_index("grp")
     core = lax.rem(me, 2)
-    chip = jnp.bitwise_and(me // 2, len(outs) - 1)
     steps, sides, heads, share, columns = near[0].shape
     width = w_ref.shape[1]
     copies = []
@@ -312,11 +311,9 @@
         head = jnp.bitwise_xor(core, 0 if mine else 1) * (heads // 2) + k % (heads // 2)
         part = jnp.dot(rows_of, w_ref[head], preferred_element_type=F32)
         acc = part if acc is None else acc + part
-    all_ref[...] = acc.astype(BF16)
     rows = outs[0].shape[0]
     for k, out in enumerate(outs):
-        start = pl.multiple_of(jnp.bitwise_xor(chip, k) * rows, rows)
-        out[...] = all_ref[pl.ds(start, rows), :]
+        out[...] = acc[k * rows : (k + 1) * rows].astype(BF16)
 
 
 def project_pair(a, got, near, far, parts):
@@ -331,7 +328,6 @@
         out_specs=[in_vmem()] * parts,
         scratch_shapes=[
             pltpu.VMEM((heads, width, model), BF16),
-            pltpu.VMEM((rows, model), BF16),
             pltpu.SemaphoreType.DMA((1,)),
         ],
         compiler_params=pltpu.CompilerParams(vmem_limit_bytes=HIGH_VMEM),
@@ -559,9 +555,6 @@
 
     query_slots = queries.reshape(local_rows, heads, width).transpose(1, 0, 2)
     query_slots = query_slots.reshape(members, heads // members, local_rows, width)
-    q = lax.all_to_all(
-        query_slots, "head", split_axis=0, concat_axis=0, tiled=True, axis_index_groups=group_sets
-    )
 
     def page_target(source, other):
         p, plane, rest = source // members, (source // plane_bit) % 2, source % plane_bit
@@ -581,8 +574,8 @@
     w_give = lax.dynamic_index_in_dim(w, 1 - y, 1, keepdims=False)
     w_got = flipped(w_give, "head", 2)
 
-    page_a, page_b, kv_beside, w_got = lax.optimization_barrier(
-        (page_a, page_b, kv_beside, w_got)
+    page_a, page_b, kv_beside, query_slots = lax.optimization_barrier(
+        (page_a, page_b, kv_beside, query_slots)
     )
     kv_both = jnp.stack([kv_heads, kv_beside], 1)
     kv_same = lax.dynamic_index_in_dim(kv_both, b, 0, keepdims=False)
@@ -592,6 +585,9 @@
         kv_own.append(flipped(kv_other if t % 2 else kv_same, "head", t * plane_bit))
     own_pages = jnp.concatenate([page_a, page_b], 0)
     pages_y = flipped(own_pages, "head", 2)
+    q = lax.all_to_all(
+        query_slots, "head", split_axis=0, concat_axis=0, tiled=True, axis_index_groups=group_sets
+    )
     w_both = jnp.stack([w_keep, w_got], 1)
     w_same = lax.dynamic_index_in_dim(w_both, b, 0, keepdims=False)
     w_other = lax.dynamic_index_in_dim(w_both, 1 - b, 0, keepdims=False)

time: 260 us -> 267 us (1.027)
  waiting for transfers between devices: 125 us -> 130 us
    ppermute x2, waiting for transfers between devices: 0.01 us -> 7.62 us  [parts_in_pairs(): lax.ppermute(cache[0], 'head', [(d, page_target(d, other)) for d in range...]
    unnamed x48 -> x44, local copies, waits for them, and re-layouts: 6.21 us -> 7.16 us
  transfers between devices with their start and end apart: 25 -> 25, of which waited for: 14 -> 15; matrix products, arithmetic and copies ran while one was open for 2% -> 3% of each run, Pallas kernels for 6% -> 6%
where the time goes in v9:
time: 267 us
  waiting for transfers between devices  130 us (49%)
  blocking collectives  52.6 us (20%)
  starting transfers between devices  34.9 us (13%)
  Pallas kernels  31.7 us (12%)
  local copies, waits for them, and re-layouts  11.6 us (4%)
  other arithmetic  5.2 us (2%)
    ppermute x21, waiting for transfers between devices, flipped(): return lax.ppermute(value, axis, pairs)  75.4 us
    all_to_all x1, blocking collectives, local(): lax.all_to_all(outgoing.reshape(n, slots // n, model), 'head', split_axis...  52.6 us
    all_to_all x1, waiting for transfers between devices, local(): lax.all_to_all(answered, 'head', split_axis=0, concat_axis=0, tiled=True)  47.3 us
    ppermute x21, starting transfers between devices, flipped(): return lax.ppermute(value, axis, pairs)  20.7 us
    pallas_call x1, Pallas kernels, attend_pair(): pl.pallas_call(functools.partial(attend_pair_kernel, block, chunk, width)...  15.7 us
    ppermute x2, waiting for transfers between devices, parts_in_pairs(): lax.ppermute(cache[0], 'head', [(d, page_target(d, other)) for d in range...  7.62 us
    unnamed x44, local copies, waits for them, and re-layouts  7.16 us
    pallas_call x1, Pallas kernels, project_pair(): pl.pallas_call(project_pair_kernel, out_shape=[jax.ShapeDtypeStruct((rows...  6.55 us
  transfers between devices with their start and end apart: 25, of which 15 were waited for; matrix products, arithmetic and copies ran while one was open for 3% of the time, Pallas kernels for 6%

profile of v9, /device:TPU:13, one launch (start us, length us, event | category | flops | bytes accessed | tf_op | source)
XLA Modules:
  0.0 266.5 jit_solution(1281387165030000757)
XLA Ops:
  0.0 1.1 copy.34
  1.4 3.2 %collective-permute-start = (bf16[256,512]{1,0:T(8,128)(2,1)}, bf16[256,512]{1,0:T(8,128)(2,1)S(1)}, u32[]{:S(2)}, u32[]{:S(2)}) collective-permute-start(bf16[256,512]{1,0:T(8,128)(2,1)} %bitcast.74), channel_id=1, source_target_pairs={{0,0},{1,1},{2,2},{3,3},{4,8},{5,9},{6,10},{7,11},{8,4},{9,5},{10,... | collective-permute-start | bytes 786440 | tf_op jit(solution)/shard_map/ppermute | solution.py:564
  4.6 2.6 copy.28
  7.2 1.1 collective-permute-done.2
  8.3 7.6 %collective-permute-done.page_a = bf16[256,512]{1,0:T(8,128)(2,1)S(1)} collective-permute-done((bf16[256,512]{1,0:T(8,128)(2,1)}, bf16[256,512]{1,0:T(8,128)(2,1)S(1)}, u32[]{:S(2)}, u32[]{:S(2)}) %collective-permute-start) | collective-permute-done | bytes 262176 | tf_op jit(solution)/shard_map/ppermute | solution.py:564
  16.0 5.8 %all-to-all-start = ((bf16[8,2,128,256]{3,2,1,0:T(8,128)(2,1)}), bf16[8,2,128,256]{3,2,1,0:T(8,128)(2,1)S(1)}, u32[]{:S(2)}, u32[]{:S(2)}) async-start(bf16[8,2,128,256]{3,2,1,0:T(8,128)(2,1)} %bitcast.61), calls=%async_computation | async-start | bytes 2097152 | tf_op jit(solution)/shard_map/all_to_all | solution.py:588
  21.8 0.8 dynamic-slice_bitcast_fusion
  22.8 0.7 constant_dynamic-update-slice_fusion.1
  23.5 0.7 constant_dynamic-update-slice_fusion
  24.2 1.2 collective-permute-start.3
  25.4 14.7 %collective-permute-done.7 = bf16[2,4,16,1024]{3,2,1,0:T(8,128)(2,1)} collective-permute-done((bf16[2,4,16,1024]{3,2,1,0:T(8,128)(2,1)}, bf16[2,4,16,1024]{3,2,1,0:T(8,128)(2,1)}, u32[]{:S(2)}, u32[]{:S(2)}) %collective-permute-start.7) | collective-permute-done | bytes 262176 | tf_op jit(solution)/shard_map/ppermute | solution.py:539
  40.1 1.7 fusion
  42.0 1.8 fusion.4
  43.9 1.2 collective-permute-start.4
  45.1 3.0 %collective-permute-start.5 = (bf16[2,128,512]{2,1,0:T(8,128)(2,1)}, bf16[2,128,512]{2,1,0:T(8,128)(2,1)S(1)}, u32[]{:S(2)}, u32[]{:S(2)}) collective-permute-start(bf16[2,128,512]{2,1,0:T(8,128)(2,1)} %get-tuple-element.31), channel_id=1, source_target_pairs={{0,8},{1,9},{2,10},{3,11},{4,12},{5,13},{6,14},{7,15},{8,0},{9,1},... | collective-permute-start | bytes 786440 | tf_op jit(solution)/shard_map/ppermute | solution.py:539
  48.1 0.5 collective-permute-done.8
  48.6 9.5 %collective-permute-done.4 = bf16[2,128,512]{2,1,0:T(8,128)(2,1)S(1)} collective-permute-done((bf16[2,128,512]{2,1,0:T(8,128)(2,1)S(1)}, bf16[2,128,512]{2,1,0:T(8,128)(2,1)S(1)}, u32[]{:S(2)}, u32[]{:S(2)}) %collective-permute-start.4) | collective-permute-done | bytes 262176 | tf_op jit(solution)/shard_map/ppermute | solution.py:539
  58.1 3.5 %collective-permute-done.5 = bf16[2,128,512]{2,1,0:T(8,128)(2,1)S(1)} collective-permute-done((bf16[2,128,512]{2,1,0:T(8,128)(2,1)}, bf16[2,128,512]{2,1,0:T(8,128)(2,1)S(1)}, u32[]{:S(2)}, u32[]{:S(2)}) %collective-permute-start.5) | collective-permute-done | bytes 262176 | tf_op jit(solution)/shard_map/ppermute | solution.py:539
  61.7 7.7 %collective-permute-done.6 = bf16[2,128,512]{2,1,0:T(8,128)(2,1)S(1)} collective-permute-done((bf16[2,128,512]{2,1,0:T(8,128)(2,1)S(1)}, bf16[2,128,512]{2,1,0:T(8,128)(2,1)S(1)}, u32[]{:S(2)}, u32[]{:S(2)}) %collective-permute-start.6) | collective-permute-done | bytes 262176 | tf_op jit(solution)/shard_map/ppermute | solution.py:539
  69.4 0.7 copy-done.14
  70.1 1.4 pad_maximum_fusion.kv_own
  71.4 2.4 collective-permute-start.11
  74.7 1.2 collective-permute-start.13
  75.9 1.8 collective-permute-done.9.page_c
  77.8 1.0 copy-done.17
  78.7 15.7 %attend.1.a_ref = bf16[2,512,512]{2,1,0:T(8,128)(2,1)S(1)} custom-call(bf16[8,2,128,256]{3,2,1,0:T(8,128)(2,1)S(1)} %all-to-all-done.q_hbm, bf16[256,512]{1,0:T(8,128)(2,1)S(1)} %collective-permute-done.page_a, bf16[256,512]{1,0:T(8,128)(2,1)S(1)} %collective-permute-done.1.page_b, bf16[512,512]{1,0:T(8,128)(2,1)S(1)} %collective-permute-done.3.page_y, ...), custom_call_target="tpu_custom_call" | custom-call | flops 7516192768 | bytes 6291456 | tf_op jit(solution)/shard_map/attend/pallas_call | solution.py:259
  94.5 2.7 %collective-permute-done.12.refs_4_ = bf16[2,2,4,16,1024]{4,3,2,1,0:T(8,128)(2,1)S(1)} collective-permute-done((bf16[2,2,4,16,1024]{4,3,2,1,0:T(8,128)(2,1)S(1)}, bf16[2,2,4,16,1024]{4,3,2,1,0:T(8,128)(2,1)S(1)}, u32[]{:S(2)}, u32[]{:S(2)}) %collective-permute-start.12) | collective-permute-done | bytes 524320 | tf_op jit(solution)/shard_map/ppermute | solution.py:539
  97.2 1.2 collective-permute-start.18
  98.4 1.1 collective-permute-start.15
  99.6 0.6 collective-permute-start.16
  100.3 9.5 %collective-permute-done.18.refs_6_ = bf16[2,2,4,16,1024]{4,3,2,1,0:T(8,128)(2,1)S(1)} collective-permute-done((bf16[2,2,4,16,1024]{4,3,2,1,0:T(8,128)(2,1)S(1)}, bf16[2,2,4,16,1024]{4,3,2,1,0:T(8,128)(2,1)S(1)}, u32[]{:S(2)}, u32[]{:S(2)}) %collective-permute-start.18) | collective-permute-done | bytes 524320 | tf_op jit(solution)/shard_map/ppermute | solution.py:539
  109.8 1.7 collective-permute-start.19
  111.6 1.5 collective-permute-done.19.refs_7_
  113.1 0.8 copy-done.19
  113.9 6.6 %project.1 = (bf16[128,2048]{1,0:T(8,128)(2,1)S(1)}, bf16[128,2048]{1,0:T(8,128)(2,1)}, bf16[128,2048]{1,0:T(8,128)(2,1)}, bf16[128,2048]{1,0:T(8,128)(2,1)}) custom-call(bf16[2,512,512]{2,1,0:T(8,128)(2,1)} %copy-done.5, bf16[512,512]{1,0:T(8,128)(2,1)S(1)} %collective-permute-done.14.got_ref, bf16[2,2,4,16,1024]{4,3,2,1,0:T(8,128)(2,1)S(1)} %pad_maximum_fusion.1.refs_0_, ...), custom_call_target="tpu_custom_call" | custom-call | flops 2147483648 | bytes 7340032 | tf_op jit(solution)/shard_map/project/pallas_call | solution.py:324
  120.5 4.9 %collective-permute-start.20 = (bf16[128,2048]{1,0:T(8,128)(2,1)}, bf16[128,2048]{1,0:T(8,128)(2,1)S(1)}, u32[]{:S(2)}, u32[]{:S(2)}) collective-permute-start(bf16[128,2048]{1,0:T(8,128)(2,1)} %get-tuple-element.40), channel_id=1, source_target_pairs={{0,6},{1,7},{2,4},{3,5},{4,2},{5,3},{6,0},{7,1},{8,14},{9,15},{10,... | collective-permute-start | bytes 1572872 | tf_op jit(solution)/shard_map/ppermute | solution.py:539
  125.4 0.5 collective-permute-start.22
  126.7 11.0 %collective-permute-done.20 = bf16[128,2048]{1,0:T(8,128)(2,1)S(1)} collective-permute-done((bf16[128,2048]{1,0:T(8,128)(2,1)}, bf16[128,2048]{1,0:T(8,128)(2,1)S(1)}, u32[]{:S(2)}, u32[]{:S(2)}) %collective-permute-start.20) | collective-permute-done | bytes 524320 | tf_op jit(solution)/shard_map/ppermute | solution.py:539
  137.7 10.6 %collective-permute-done.21 = bf16[128,2048]{1,0:T(8,128)(2,1)S(1)} collective-permute-done((bf16[128,2048]{1,0:T(8,128)(2,1)}, bf16[128,2048]{1,0:T(8,128)(2,1)S(1)}, u32[]{:S(2)}, u32[]{:S(2)}) %collective-permute-start.21) | collective-permute-done | bytes 524320 | tf_op jit(solution)/shard_map/ppermute | solution.py:539
  148.3 1.1 collective-permute-done.22
  149.4 2.2 route.1
  151.6 52.6 %all_to_all.15 = bf16[16,32,2048]{2,1,0:T(8,128)(2,1)S(1)} all-to-all(bf16[16,32,2048]{2,1,0:T(8,128)(2,1)S(1)} %bitcast.51), channel_id=1, replica_groups=mesh['grp'=2,'head'=16] {'head'}, dimensions={0} | all-to-all | bytes 4194304 | tf_op jit(solution)/shard_map/all_to_all | solution.py:717
  204.2 5.7 %expert.1 = bf16[512,2048]{1,0:T(8,128)(2,1)S(1)} custom-call(bf16[512,2048]{1,0:T(8,128)(2,1)S(1)} %bitcast.53, bf16[2048,1024]{1,0:T(8,128)(2,1)} %bitcast.72, bf16[512,2048]{1,0:T(8,128)(2,1)} %bitcast.73), custom_call_target="tpu_custom_call" | custom-call | flops 3221225472 | bytes 10485760 | tf_op jit(solution)/shard_map/expert/pallas_call | solution.py:479
  209.9 1.4 copy-done.1
  211.2 5.1 %all-to-all-start.2 = ((bf16[16,32,2048]{2,1,0:T(8,128)(2,1)}), bf16[16,32,2048]{2,1,0:T(8,128)(2,1)S(1)}, u32[]{:S(2)}, u32[]{:S(2)}) async-start(bf16[16,32,2048]{2,1,0:T(8,128)(2,1)} %bitcast.52), calls=%async_computation.2 | async-start | bytes 4194304 | tf_op jit(solution)/shard_map/all_to_all | solution.py:730
  216.4 47.3 %all-to-all-done.2 = bf16[16,32,2048]{2,1,0:T(8,128)(2,1)S(1)} async-done(((bf16[16,32,2048]{2,1,0:T(8,128)(2,1)}), bf16[16,32,2048]{2,1,0:T(8,128)(2,1)S(1)}, u32[]{:S(2)}, u32[]{:S(2)}) %all-to-all-start.2) | async-done | bytes 2097184 | tf_op jit(solution)/shard_map/all_to_all | solution.py:730
  263.7 1.2 copy-done.3
  265.0 1.6 combine.1
  (71 shorter events, 2.8 us)
Async XLA Ops:
  0.0 21.7 %copy-start = (bf16[16,16,2048]{2,1,0:T(8,128)(2,1)S(1)}, bf16[16,16,2048]{2,1,0:T(8,128)(2,1)}, u32[]{:S(2)}) copy-start(bf16[16,16,2048]{2,1,0:T(8,128)(2,1)} %param.14) | copy-start | bytes 3145732
  1.1 14.9 %copy-start.7 = (bf16[128,1,2,512]{3,0,2,1:T(8,128)(2,1)}, bf16[128,1,2,512]{3,0,2,1:T(8,128)(2,1)S(1)}, u32[]{:S(2)}) copy-start(bf16[128,1,2,512]{3,0,2,1:T(8,128)(2,1)S(1)} %copy.34) | copy-start | bytes 786436
  1.1 7.2 %collective-permute-start.2 = (bf16[2,128,512]{2,1,0:T(8,128)(2,1)S(1)}, bf16[2,128,512]{2,1,0:T(8,128)(2,1)S(1)}, u32[]{:S(2)}, u32[]{:S(2)}) collective-permute-start(bf16[2,128,512]{2,1,0:T(8,128)(2,1)S(1)} %bitcast.63), channel_id=1, source_target_pairs={{0,2},{1,3},{2,0},{3,1},{4,6},{5,7},{6,4},{7,5},{8,10},{9,11},{10,... | collective-permute-start | bytes 786440 | tf_op jit(solution)/shard_map/ppermute | solution.py:539
  1.4 14.6 %collective-permute-start = (bf16[256,512]{1,0:T(8,128)(2,1)}, bf16[256,512]{1,0:T(8,128)(2,1)S(1)}, u32[]{:S(2)}, u32[]{:S(2)}) collective-permute-start(bf16[256,512]{1,0:T(8,128)(2,1)} %bitcast.74), channel_id=1, source_target_pairs={{0,0},{1,1},{2,2},{3,3},{4,8},{5,9},{6,10},{7,11},{8,4},{9,5},{10,... | collective-permute-start | bytes 786440 | tf_op jit(solution)/shard_map/ppermute | solution.py:564
  4.6 11.4 %collective-permute-start.1 = (bf16[256,512]{1,0:T(8,128)(2,1)}, bf16[256,512]{1,0:T(8,128)(2,1)S(1)}, u32[]{:S(2)}, u32[]{:S(2)}) collective-permute-start(bf16[256,512]{1,0:T(8,128)(2,1)} %bitcast.75), channel_id=1, source_target_pairs={{0,8},{1,9},{2,10},{3,11},{4,0},{5,1},{6,2},{7,3},{8,12},{9,13},{1... | collective-permute-start | bytes 786440 | tf_op jit(solution)/shard_map/ppermute | solution.py:564
  8.3 7.6 %copy-start.9 = (bf16[2,128,512]{2,1,0:T(8,128)(2,1)}, bf16[2,128,512]{2,1,0:T(8,128)(2,1)S(1)}, u32[]{:S(2)}) copy-start(bf16[2,128,512]{2,1,0:T(8,128)(2,1)S(1)} %collective-permute-done.2) | copy-start | bytes 786436
  16.0 54.1 %all-to-all-start = ((bf16[8,2,128,256]{3,2,1,0:T(8,128)(2,1)}), bf16[8,2,128,256]{3,2,1,0:T(8,128)(2,1)S(1)}, u32[]{:S(2)}, u32[]{:S(2)}) async-start(bf16[8,2,128,256]{3,2,1,0:T(8,128)(2,1)} %bitcast.61), calls=%async_computation | async-start | bytes 2097152 | tf_op jit(solution)/shard_map/all_to_all | solution.py:588
  22.5 17.6 %collective-permute-start.7 = (bf16[2,4,16,1024]{3,2,1,0:T(8,128)(2,1)}, bf16[2,4,16,1024]{3,2,1,0:T(8,128)(2,1)}, u32[]{:S(2)}, u32[]{:S(2)}) collective-permute-start(bf16[2,4,16,1024]{3,2,1,0:T(8,128)(2,1)} %get-tuple-element.47), channel_id=1, source_target_pairs={{0,2},{1,3},{2,0},{3,1},{4,6},{5,7},{6,4},{7,5},{8,10},{9,11},{10,... | collective-permute-start | bytes 786440 | tf_op jit(solution)/shard_map/ppermute | solution.py:539
  24.2 45.8 %collective-permute-start.3 = (bf16[512,512]{1,0:T(8,128)(2,1)}, bf16[512,512]{1,0:T(8,128)(2,1)S(1)}, u32[]{:S(2)}, u32[]{:S(2)}) collective-permute-start(bf16[512,512]{1,0:T(8,128)(2,1)} %constant_dynamic-update-slice_fusion), channel_id=1, source_target_pairs={{0,2},{1,3},{2,0},{3,1},{4,6},{5,7},{6,4},{7,5},{8,10},{9,11},{10,... | collective-permute-start | bytes 1572872 | tf_op jit(solution)/shard_map/ppermute | solution.py:539
  41.8 32.6 %copy-start.8 = (bf16[1,2,4,16,1024]{4,3,2,1,0:T(8,128)(2,1)S(1)}, bf16[1,2,4,16,1024]{4,3,2,1,0:T(8,128)(2,1)}, u32[]{:S(2)}) copy-start(bf16[1,2,4,16,1024]{4,3,2,1,0:T(8,128)(2,1)} %get-tuple-element.45) | copy-start | bytes 786436
  41.8 6.8 %collective-permute-start.8 = (bf16[2,4,16,1024]{3,2,1,0:T(8,128)(2,1)S(1)}, bf16[2,4,16,1024]{3,2,1,0:T(8,128)(2,1)S(1)}, u32[]{:S(2)}, u32[]{:S(2)}) collective-permute-start(bf16[2,4,16,1024]{3,2,1,0:T(8,128)(2,1)S(1)} %get-tuple-element.46), channel_id=1, source_target_pairs={{0,4},{1,5},{2,6},{3,7},{4,0},{5,1},{6,2},{7,3},{8,12},{9,13},{10,... | collective-permute-start | bytes 786440 | tf_op jit(solution)/shard_map/ppermute | solution.py:539
  43.9 14.3 %collective-permute-start.4 = (bf16[2,128,512]{2,1,0:T(8,128)(2,1)S(1)}, bf16[2,128,512]{2,1,0:T(8,128)(2,1)S(1)}, u32[]{:S(2)}, u32[]{:S(2)}) collective-permute-start(bf16[2,128,512]{2,1,0:T(8,128)(2,1)S(1)} %get-tuple-element.49), channel_id=1, source_target_pairs={{0,4},{1,5},{2,6},{3,7},{4,0},{5,1},{6,2},{7,3},{8,12},{9,13},{10,... | collective-permute-start | bytes 786440 | tf_op jit(solution)/shard_map/ppermute | solution.py:539
  45.1 16.5 %collective-permute-start.5 = (bf16[2,128,512]{2,1,0:T(8,128)(2,1)}, bf16[2,128,512]{2,1,0:T(8,128)(2,1)S(1)}, u32[]{:S(2)}, u32[]{:S(2)}) collective-permute-start(bf16[2,128,512]{2,1,0:T(8,128)(2,1)} %get-tuple-element.31), channel_id=1, source_target_pairs={{0,8},{1,9},{2,10},{3,11},{4,12},{5,13},{6,14},{7,15},{8,0},{9,1},... | collective-permute-start | bytes 786440 | tf_op jit(solution)/shard_map/ppermute | solution.py:539
  48.1 21.3 %collective-permute-start.6 = (bf16[2,128,512]{2,1,0:T(8,128)(2,1)S(1)}, bf16[2,128,512]{2,1,0:T(8,128)(2,1)S(1)}, u32[]{:S(2)}, u32[]{:S(2)}) collective-permute-start(bf16[2,128,512]{2,1,0:T(8,128)(2,1)S(1)} %get-tuple-element.49), channel_id=1, source_target_pairs={{0,12},{1,13},{2,14},{3,15},{4,8},{5,9},{6,10},{7,11},{8,4},{9,5},... | collective-permute-start | bytes 786440 | tf_op jit(solution)/shard_map/ppermute | solution.py:539
  48.6 20.8 %copy-start.10 = (bf16[2,4,16,1024]{3,2,1,0:T(8,128)(2,1)}, bf16[2,4,16,1024]{3,2,1,0:T(8,128)(2,1)S(1)}, u32[]{:S(2)}) copy-start(bf16[2,4,16,1024]{3,2,1,0:T(8,128)(2,1)S(1)} %collective-permute-done.8) | copy-start | bytes 786436
  58.1 11.2 %copy-start.12 = (bf16[2,128,512]{2,1,0:T(8,128)(2,1)}, bf16[2,128,512]{2,1,0:T(8,128)(2,1)S(1)}, u32[]{:S(2)}) copy-start(bf16[2,128,512]{2,1,0:T(8,128)(2,1)S(1)} %collective-permute-done.4) | copy-start | bytes 786436
  61.7 7.7 %copy-start.13 = (bf16[2,128,512]{2,1,0:T(8,128)(2,1)}, bf16[2,128,512]{2,1,0:T(8,128)(2,1)S(1)}, u32[]{:S(2)}) copy-start(bf16[2,128,512]{2,1,0:T(8,128)(2,1)S(1)} %collective-permute-done.5) | copy-start | bytes 786436
  69.4 0.7 copy-start.14
  70.1 4.3 %copy-start.11 = (bf16[2,4,16,1024]{3,2,1,0:T(8,128)(2,1)S(1)}, bf16[2,4,16,1024]{3,2,1,0:T(8,128)(2,1)}, u32[]{:S(2)}) copy-start(bf16[2,4,16,1024]{3,2,1,0:T(8,128)(2,1)} %copy-done.10) | copy-start | bytes 786436
  71.4 6.3 %collective-permute-start.11 = (bf16[4,2,128,512]{3,2,1,0:T(8,128)(2,1)S(1)}, bf16[4,2,128,512]{3,2,1,0:T(8,128)(2,1)S(1)}, u32[]{:S(2)}, u32[]{:S(2)}) collective-permute-start(bf16[4,2,128,512]{3,2,1,0:T(8,128)(2,1)S(1)} %pad_maximum_fusion.kv_own), channel_id=1, source_target_pairs={{0,1},{1,0},{2,3},{3,2},{4,5},{5,4},{6,7},{7,6},{8,9},{9,8},{10,11... | collective-permute-start | bytes 3145736 | tf_op jit(solution)/shard_map/ppermute | solution.py:539
  73.9 3.9 %collective-permute-start.9 = (bf16[512,512]{1,0:T(8,128)(2,1)}, bf16[512,512]{1,0:T(8,128)(2,1)S(1)}, u32[]{:S(2)}, u32[]{:S(2)}) collective-permute-start(bf16[512,512]{1,0:T(8,128)(2,1)} %constant_dynamic-update-slice_fusion), channel_id=1, source_target_pairs={{0,1},{1,0},{2,3},{3,2},{4,5},{5,4},{6,7},{7,6},{8,9},{9,8},{10,11... | collective-permute-start | bytes 1572872 | tf_op jit(solution)/shard_map/ppermute | solution.py:539
  74.0 3.8 %collective-permute-start.10 = (bf16[512,512]{1,0:T(8,128)(2,1)S(1)}, bf16[512,512]{1,0:T(8,128)(2,1)S(1)}, u32[]{:S(2)}, u32[]{:S(2)}) collective-permute-start(bf16[512,512]{1,0:T(8,128)(2,1)S(1)} %collective-permute-done.3.page_y), channel_id=1, source_target_pairs={{0,1},{1,0},{2,3},{3,2},{4,5},{5,4},{6,7},{7,6},{8,9},{9,8},{10,11... | collective-permute-start | bytes 1572872 | tf_op jit(solution)/shard_map/ppermute | solution.py:539
  74.4 22.8 %collective-permute-start.12 = (bf16[2,2,4,16,1024]{4,3,2,1,0:T(8,128)(2,1)S(1)}, bf16[2,2,4,16,1024]{4,3,2,1,0:T(8,128)(2,1)S(1)}, u32[]{:S(2)}, u32[]{:S(2)}) collective-permute-start(bf16[2,2,4,16,1024]{4,3,2,1,0:T(8,128)(2,1)S(1)} %pad_maximum_fusion.1.refs_0_), channel_id=1, source_target_pairs={{0,8},{1,9},{2,10},{3,11},{4,12},{5,13},{6,14},{7,15},{8,0},{9,1},... | collective-permute-start | bytes 1572872 | tf_op jit(solution)/shard_map/ppermute | solution.py:539
  74.7 22.5 %collective-permute-start.13 = (bf16[2,2,4,16,1024]{4,3,2,1,0:T(8,128)(2,1)S(1)}, bf16[2,2,4,16,1024]{4,3,2,1,0:T(8,128)(2,1)S(1)}, u32[]{:S(2)}, u32[]{:S(2)}) collective-permute-start(bf16[2,2,4,16,1024]{4,3,2,1,0:T(8,128)(2,1)S(1)} %pad_maximum_fusion.1.refs_0_), channel_id=1, source_target_pairs={{0,16},{16,0},{1,17},{17,1},{2,18},{18,2},{3,19},{19,3},{4,20},{20... | collective-permute-start | bytes 1572872 | tf_op jit(solution)/shard_map/ppermute | solution.py:539
  77.7 1.0 copy-start.17
  94.5 18.6 %copy-start.5 = (bf16[2,512,512]{2,1,0:T(8,128)(2,1)}, bf16[2,512,512]{2,1,0:T(8,128)(2,1)S(1)}, u32[]{:S(2)}) copy-start(bf16[2,512,512]{2,1,0:T(8,128)(2,1)S(1)} %attend.1.a_ref) | copy-start | bytes 3145732
  97.2 12.6 %collective-permute-start.18 = (bf16[2,2,4,16,1024]{4,3,2,1,0:T(8,128)(2,1)S(1)}, bf16[2,2,4,16,1024]{4,3,2,1,0:T(8,128)(2,1)S(1)}, u32[]{:S(2)}, u32[]{:S(2)}) collective-permute-start(bf16[2,2,4,16,1024]{4,3,2,1,0:T(8,128)(2,1)S(1)} %collective-permute-done.12.refs_4_), channel_id=1, source_target_pairs={{0,16},{16,0},{1,17},{17,1},{2,18},{18,2},{3,19},{19,3},{4,20},{20... | collective-permute-start | bytes 1572872 | tf_op jit(solution)/shard_map/ppermute | solution.py:539
  98.4 13.1 %collective-permute-start.15 = (bf16[2,2,4,16,1024]{4,3,2,1,0:T(8,128)(2,1)S(1)}, bf16[2,2,4,16,1024]{4,3,2,1,0:T(8,128)(2,1)S(1)}, u32[]{:S(2)}, u32[]{:S(2)}) collective-permute-start(bf16[2,2,4,16,1024]{4,3,2,1,0:T(8,128)(2,1)S(1)} %pad_maximum_fusion.1.refs_0_), channel_id=1, source_target_pairs={{0,1},{1,0},{2,3},{3,2},{4,5},{5,4},{6,7},{7,6},{8,9},{9,8},{10,11... | collective-permute-start | bytes 1572872 | tf_op jit(solution)/shard_map/ppermute | solution.py:539
  99.6 12.0 %collective-permute-start.17 = (bf16[2,2,4,16,1024]{4,3,2,1,0:T(8,128)(2,1)S(1)}, bf16[2,2,4,16,1024]{4,3,2,1,0:T(8,128)(2,1)S(1)}, u32[]{:S(2)}, u32[]{:S(2)}) collective-permute-start(bf16[2,2,4,16,1024]{4,3,2,1,0:T(8,128)(2,1)S(1)} %collective-permute-done.12.refs_4_), channel_id=1, source_target_pairs={{0,1},{1,0},{2,3},{3,2},{4,5},{5,4},{6,7},{7,6},{8,9},{9,8},{10,11... | collective-permute-start | bytes 1572872 | tf_op jit(solution)/shard_map/ppermute | solution.py:539
  99.6 26.3 %copy-start.15 = (s32[128,1,2]{0,2,1:T(2,128)S(1)}, s32[128,1,2]{0,2,1:T(2,128)}, u32[]{:S(2)}) copy-start(s32[128,1,2]{0,2,1:T(2,128)} %param.16) | copy-start | bytes 3076
  99.6 49.8 %copy-start.4 = (bf16[128,1,2048]{2,0,1:T(8,128)(2,1)S(1)}, bf16[128,1,2048]{2,0,1:T(8,128)(2,1)}, u32[]{:S(2)}) copy-start(bf16[128,1,2048]{2,0,1:T(8,128)(2,1)} %param.13) | copy-start | bytes 1572868
  99.6 49.7 %copy-start.6 = (f32[2048]{0:T(1024)S(1)}, f32[2048]{0:T(1024)}, u32[]{:S(2)}) copy-start(f32[2048]{0:T(1024)} %param.15) | copy-start | bytes 24580
  99.6 11.9 %collective-permute-start.16 = (bf16[2,2,4,16,1024]{4,3,2,1,0:T(8,128)(2,1)S(1)}, bf16[2,2,4,16,1024]{4,3,2,1,0:T(8,128)(2,1)S(1)}, u32[]{:S(2)}, u32[]{:S(2)}) collective-permute-start(bf16[2,2,4,16,1024]{4,3,2,1,0:T(8,128)(2,1)S(1)} %collective-permute-done.13.refs_2_), channel_id=1, source_target_pairs={{0,1},{1,0},{2,3},{3,2},{4,5},{5,4},{6,7},{7,6},{8,9},{9,8},{10,11... | collective-permute-start | bytes 1572872 | tf_op jit(solution)/shard_map/ppermute | solution.py:539
  100.2 11.4 %collective-permute-start.14 = (bf16[512,512]{1,0:T(8,128)(2,1)S(1)}, bf16[512,512]{1,0:T(8,128)(2,1)S(1)}, u32[]{:S(2)}, u32[]{:S(2)}) collective-permute-start(bf16[512,512]{1,0:T(8,128)(2,1)S(1)} %slice_bitcast_fusion), channel_id=1, source_target_pairs={{0,1},{1,0},{2,3},{3,2},{4,5},{5,4},{6,7},{7,6},{8,9},{9,8},{10,11... | collective-permute-start | bytes 1572872 | tf_op jit(solution)/shard_map/ppermute | solution.py:539
  109.8 3.3 %copy-start.18 = (bf16[2,2,4,16,1024]{4,3,2,1,0:T(8,128)(2,1)}, bf16[2,2,4,16,1024]{4,3,2,1,0:T(8,128)(2,1)S(1)}, u32[]{:S(2)}) copy-start(bf16[2,2,4,16,1024]{4,3,2,1,0:T(8,128)(2,1)S(1)} %collective-permute-done.18.refs_6_) | copy-start | bytes 1572868
  109.8 3.3 %collective-permute-start.19 = (bf16[2,2,4,16,1024]{4,3,2,1,0:T(8,128)(2,1)S(1)}, bf16[2,2,4,16,1024]{4,3,2,1,0:T(8,128)(2,1)S(1)}, u32[]{:S(2)}, u32[]{:S(2)}) collective-permute-start(bf16[2,2,4,16,1024]{4,3,2,1,0:T(8,128)(2,1)S(1)} %collective-permute-done.18.refs_6_), channel_id=1, source_target_pairs={{0,1},{1,0},{2,3},{3,2},{4,5},{5,4},{6,7},{7,6},{8,9},{9,8},{10,11... | collective-permute-start | bytes 1572872 | tf_op jit(solution)/shard_map/ppermute | solution.py:539
  113.1 0.8 copy-start.19
  120.5 17.2 %collective-permute-start.20 = (bf16[128,2048]{1,0:T(8,128)(2,1)}, bf16[128,2048]{1,0:T(8,128)(2,1)S(1)}, u32[]{:S(2)}, u32[]{:S(2)}) collective-permute-start(bf16[128,2048]{1,0:T(8,128)(2,1)} %get-tuple-element.40), channel_id=1, source_target_pairs={{0,6},{1,7},{2,4},{3,5},{4,2},{5,3},{6,0},{7,1},{8,14},{9,15},{10,... | collective-permute-start | bytes 1572872 | tf_op jit(solution)/shard_map/ppermute | solution.py:539
  125.4 22.9 %collective-permute-start.21 = (bf16[128,2048]{1,0:T(8,128)(2,1)}, bf16[128,2048]{1,0:T(8,128)(2,1)S(1)}, u32[]{:S(2)}, u32[]{:S(2)}) collective-permute-start(bf16[128,2048]{1,0:T(8,128)(2,1)} %get-tuple-element.41), channel_id=1, source_target_pairs={{0,4},{1,5},{2,6},{3,7},{4,0},{5,1},{6,2},{7,3},{8,12},{9,13},{10,... | collective-permute-start | bytes 1572872 | tf_op jit(solution)/shard_map/ppermute | solution.py:539
  125.4 23.9 %collective-permute-start.22 = (bf16[128,2048]{1,0:T(8,128)(2,1)}, bf16[128,2048]{1,0:T(8,128)(2,1)}, u32[]{:S(2)}, u32[]{:S(2)}) collective-permute-start(bf16[128,2048]{1,0:T(8,128)(2,1)} %get-tuple-element.42), channel_id=1, source_target_pairs={{0,2},{1,3},{2,0},{3,1},{4,6},{5,7},{6,4},{7,5},{8,10},{9,11},{10,... | collective-permute-start | bytes 1572872 | tf_op jit(solution)/shard_map/ppermute | solution.py:539
  151.6 52.6 %copy-start.2 = (f32[128,2048]{1,0:T(8,128)}, f32[128,2048]{1,0:T(8,128)S(1)}, u32[]{:S(2)}) copy-start(f32[128,2048]{1,0:T(8,128)S(1)} %get-tuple-element.44.stream_ref) | copy-start | bytes 3145732
  209.9 1.4 copy-start.1
  211.2 5.1 %copy-start.16 = (f32[128,1,2]{0,2,1:T(2,128)S(1)}, f32[128,1,2]{0,2,1:T(2,128)}, u32[]{:S(2)}) copy-start(f32[128,1,2]{0,2,1:T(2,128)} %param.17) | copy-start | bytes 3076
  211.2 52.5 %all-to-all-start.2 = ((bf16[16,32,2048]{2,1,0:T(8,128)(2,1)}), bf16[16,32,2048]{2,1,0:T(8,128)(2,1)S(1)}, u32[]{:S(2)}, u32[]{:S(2)}) async-start(bf16[16,32,2048]{2,1,0:T(8,128)(2,1)} %bitcast.52), calls=%async_computation.2 | async-start | bytes 4194304 | tf_op jit(solution)/shard_map/all_to_all | solution.py:730
  263.7 1.2 copy-start.3

commit v10 on v9

--- a/solution.py
+++ b/solution.py
@@ -565,33 +565,38 @@
         for other in range(2)
     )
     kv_heads = new_kv.reshape(local_rows, pair_heads, 2 * width).transpose(1, 0, 2)
-    kv_beside = flipped(kv_heads, "head", 2)
+    kv_ordered = jnp.stack(
+        [
+            lax.dynamic_index_in_dim(kv_heads, b, 0, keepdims=False),
+            lax.dynamic_index_in_dim(kv_heads, 1 - b, 0, keepdims=False),
+        ],
+        0,
+    )
+    kv_beside = flipped(kv_ordered, "head", 2)
 
     columns = model // 2
     w = lax.dynamic_slice_in_dim(w_out, lax.axis_index("grp") * columns, columns, 2)
     w = w.reshape(2, 2, heads // 4, share, columns)
-    w_keep = lax.dynamic_index_in_dim(w, y, 1, keepdims=False)
-    w_give = lax.dynamic_index_in_dim(w, 1 - y, 1, keepdims=False)
-    w_got = flipped(w_give, "head", 2)
-
-    page_a, page_b, kv_beside, query_slots = lax.optimization_barrier(
-        (page_a, page_b, kv_beside, query_slots)
-    )
-    kv_both = jnp.stack([kv_heads, kv_beside], 1)
-    kv_same = lax.dynamic_index_in_dim(kv_both, b, 0, keepdims=False)
-    kv_other = lax.dynamic_index_in_dim(kv_both, 1 - b, 0, keepdims=False)
+    w = [lax.dynamic_index_in_dim(w, plane, 0, keepdims=False) for plane in (b, 1 - b)]
+    w_keep = [lax.dynamic_index_in_dim(part, y, 0, keepdims=False) for part in w]
+    w_give = [lax.dynamic_index_in_dim(part, 1 - y, 0, keepdims=False) for part in w]
+    w_got = flipped(jnp.stack(w_give, 0), "head", 2)
+
+    page_a, page_b, kv_beside, w_got, query_slots = lax.optimization_barrier(
+        (page_a, page_b, kv_beside, w_got, query_slots)
+    )
+    kv_same, kv_other = (jnp.stack([kv_ordered[k], kv_beside[k]], 0) for k in range(2))
     kv_own = [kv_same]
     for t in range(1, planes):
         kv_own.append(flipped(kv_other if t % 2 else kv_same, "head", t * plane_bit))
     own_pages = jnp.concatenate([page_a, page_b], 0)
     pages_y = flipped(own_pages, "head", 2)
+    w_same, w_other = (jnp.stack([w_keep[k], w_got[k]], 0) for k in range(2))
+    w_first = flipped(w_other, "head", plane_bit)
+    query_slots, w_first = lax.optimization_barrier((query_slots, w_first))
     q = lax.all_to_all(
         query_slots, "head", split_axis=0, concat_axis=0, tiled=True, axis_index_groups=group_sets
     )
-    w_both = jnp.stack([w_keep, w_got], 1)
-    w_same = lax.dynamic_index_in_dim(w_both, b, 0, keepdims=False)
-    w_other = lax.dynamic_index_in_dim(w_both, 1 - b, 0, keepdims=False)
-    w_first = flipped(w_other, "head", plane_bit)
     pages_y, kv_own, w_first, q = lax.optimization_barrier((pages_y, kv_own, w_first, q))
 
     kv_own = jnp.stack(kv_own, 0)

time: 267 us -> 260 us (0.974)
  waiting for transfers between devices: 130 us -> 127 us
    ppermute x2, waiting for transfers between devices: 7.62 us -> 3.44 us  [parts_in_pairs(): lax.ppermute(cache[0], 'head', [(d, page_target(d, other)) for d in range...]
    ppermute x21, starting transfers between devices: 20.7 us -> 17.1 us  [flipped(): return lax.ppermute(value, axis, pairs)]
    unnamed x44 -> x49, local copies, waits for them, and re-layouts: 7.16 us -> 6.6 us
  transfers between devices with their start and end apart: 25 -> 25, of which waited for: 15 -> 13; matrix products, arithmetic and copies ran while one was open for 3% -> 2% of each run, Pallas kernels for 6% -> 6%
where the time goes in v10:
time: 260 us; the launch traced here: 259 us
  waiting for transfers between devices  127 us (49%)
  blocking collectives  54.2 us (21%)
  starting transfers between devices  32.6 us (13%)
  Pallas kernels  31.7 us (12%)
  local copies, waits for them, and re-layouts  11.4 us (4%)
  other arithmetic  2.72 us (1%)
    ppermute x21, waiting for transfers between devices, flipped(): return lax.ppermute(value, axis, pairs)  75.8 us
    all_to_all x1, blocking collectives, local(): lax.all_to_all(outgoing.reshape(n, slots // n, model), 'head', split_axis...  54.2 us
    all_to_all x1, waiting for transfers between devices, local(): lax.all_to_all(answered, 'head', split_axis=0, concat_axis=0, tiled=True)  47.3 us
    ppermute x21, starting transfers between devices, flipped(): return lax.ppermute(value, axis, pairs)  17.1 us
    pallas_call x1, Pallas kernels, attend_pair(): pl.pallas_call(functools.partial(attend_pair_kernel, block, chunk, width)...  15.7 us
    all_to_all x1, starting transfers between devices, parts_in_pairs(): lax.all_to_all(query_slots, 'head', split_axis=0, concat_axis=0, tiled=Tr...  6.92 us
    unnamed x49, local copies, waits for them, and re-layouts  6.6 us
    pallas_call x1, Pallas kernels, project_pair(): pl.pallas_call(project_pair_kernel, out_shape=[jax.ShapeDtypeStruct((rows...  6.55 us
  transfers between devices with their start and end apart: 25, of which 13 were waited for; matrix products, arithmetic and copies ran while one was open for 2% of the time, Pallas kernels for 6%

profile of v10, /device:TPU:13, one launch (start us, length us, event | category | flops | bytes accessed | tf_op | source)
XLA Modules:
  0.0 259.4 jit_solution(14128597277355621217)
XLA Ops:
  0.0 1.2 copy-done
  1.3 0.7 dynamic-slice_bitcast_fusion
  2.3 0.5 constant_dynamic-slice_fusion.1
  2.9 1.3 collective-permute-start.2
  4.3 3.2 %collective-permute-start = (bf16[256,512]{1,0:T(8,128)(2,1)S(1)}, bf16[256,512]{1,0:T(8,128)(2,1)S(1)}, u32[]{:S(2)}, u32[]{:S(2)}) collective-permute-start(bf16[256,512]{1,0:T(8,128)(2,1)S(1)} %bitcast.66), channel_id=1, source_target_pairs={{0,0},{1,1},{2,2},{3,3},{4,8},{5,9},{6,10},{7,11},{8,4},{9,5},{10,... | collective-permute-start | bytes 786440 | tf_op jit(solution)/shard_map/ppermute | solution.py:564
  7.5 1.3 copy.29
  8.9 0.4 collective-permute-done.3
  9.3 5.6 %collective-permute-done.2 = bf16[2,128,512]{2,1,0:T(8,128)(2,1)S(1)} collective-permute-done((bf16[2,128,512]{2,1,0:T(8,128)(2,1)S(1)}, bf16[2,128,512]{2,1,0:T(8,128)(2,1)S(1)}, u32[]{:S(2)}, u32[]{:S(2)}) %collective-permute-start.2) | collective-permute-done | bytes 262176 | tf_op jit(solution)/shard_map/ppermute | solution.py:539
  14.9 3.4 %collective-permute-done.page_a = bf16[256,512]{1,0:T(8,128)(2,1)S(1)} collective-permute-done((bf16[256,512]{1,0:T(8,128)(2,1)S(1)}, bf16[256,512]{1,0:T(8,128)(2,1)S(1)}, u32[]{:S(2)}, u32[]{:S(2)}) %collective-permute-start) | collective-permute-done | bytes 262176 | tf_op jit(solution)/shard_map/ppermute | solution.py:564
  18.3 0.7 fusion
  19.1 5.6 %collective-permute-done.8 = bf16[2,4,16,1024]{3,2,1,0:T(8,128)(2,1)S(1)} collective-permute-done((bf16[2,4,16,1024]{3,2,1,0:T(8,128)(2,1)S(1)}, bf16[2,4,16,1024]{3,2,1,0:T(8,128)(2,1)S(1)}, u32[]{:S(2)}, u32[]{:S(2)}) %collective-permute-start.8) | collective-permute-done | bytes 262176 | tf_op jit(solution)/shard_map/ppermute | solution.py:539
  24.7 6.9 %all-to-all-start = ((bf16[8,2,128,256]{3,2,1,0:T(8,128)(2,1)}), bf16[8,2,128,256]{3,2,1,0:T(8,128)(2,1)S(1)}, u32[]{:S(2)}, u32[]{:S(2)}) async-start(bf16[8,2,128,256]{3,2,1,0:T(8,128)(2,1)} %bitcast.55), calls=%async_computation | async-start | bytes 2097152 | tf_op jit(solution)/shard_map/all_to_all | solution.py:597
  31.7 0.3 collective-permute-start.4
  32.1 1.0 fusion.1
  33.3 2.6 %collective-permute-start.7 = (bf16[2,128,512]{2,1,0:T(8,128)(2,1)S(1)}, bf16[2,128,512]{2,1,0:T(8,128)(2,1)S(1)}, u32[]{:S(2)}, u32[]{:S(2)}) collective-permute-start(bf16[2,128,512]{2,1,0:T(8,128)(2,1)S(1)} %pad_maximum_fusion.5), channel_id=1, source_target_pairs={{0,12},{1,13},{2,14},{3,15},{4,8},{5,9},{6,10},{7,11},{8,4},{9,5},... | collective-permute-start | bytes 786440 | tf_op jit(solution)/shard_map/ppermute | solution.py:539
  35.9 0.9 collective-permute-start.6
  36.8 23.2 %collective-permute-done.5 = bf16[2,128,512]{2,1,0:T(8,128)(2,1)S(1)} collective-permute-done((bf16[2,128,512]{2,1,0:T(8,128)(2,1)S(1)}, bf16[2,128,512]{2,1,0:T(8,128)(2,1)S(1)}, u32[]{:S(2)}, u32[]{:S(2)}) %collective-permute-start.5) | collective-permute-done | bytes 262176 | tf_op jit(solution)/shard_map/ppermute | solution.py:539
  60.0 3.2 %collective-permute-done.6 = bf16[2,128,512]{2,1,0:T(8,128)(2,1)S(1)} collective-permute-done((bf16[2,128,512]{2,1,0:T(8,128)(2,1)S(1)}, bf16[2,128,512]{2,1,0:T(8,128)(2,1)S(1)}, u32[]{:S(2)}, u32[]{:S(2)}) %collective-permute-start.6) | collective-permute-done | bytes 262176 | tf_op jit(solution)/shard_map/ppermute | solution.py:539
  63.2 0.7 copy-done.14
  63.9 1.3 pad_maximum_fusion.kv_own
  65.2 1.0 collective-permute-start.11
  66.3 0.4 collective-permute-start.10
  66.7 1.0 maximum_bitcast_fusion
  67.8 1.1 collective-permute-start.12
  68.9 1.2 collective-permute-start.13
  70.2 1.0 copy-done.19
  71.1 15.7 %attend.1.a_ref = bf16[2,512,512]{2,1,0:T(8,128)(2,1)S(1)} custom-call(bf16[8,2,128,256]{3,2,1,0:T(8,128)(2,1)S(1)} %all-to-all-done.q_hbm, bf16[256,512]{1,0:T(8,128)(2,1)S(1)} %collective-permute-done.page_a, bf16[256,512]{1,0:T(8,128)(2,1)S(1)} %collective-permute-done.1.page_b, bf16[512,512]{1,0:T(8,128)(2,1)S(1)} %collective-permute-done.4.page_y, ...), custom_call_target="tpu_custom_call" | custom-call | flops 7516192768 | bytes 6291456 | tf_op jit(solution)/shard_map/attend/pallas_call | solution.py:259
  86.9 3.9 %collective-permute-done.12.refs_4_ = bf16[2,2,4,16,1024]{4,3,2,1,0:T(8,128)(2,1)S(1)} collective-permute-done((bf16[2,2,4,16,1024]{4,3,2,1,0:T(8,128)(2,1)S(1)}, bf16[2,2,4,16,1024]{4,3,2,1,0:T(8,128)(2,1)S(1)}, u32[]{:S(2)}, u32[]{:S(2)}) %collective-permute-start.12) | collective-permute-done | bytes 524320 | tf_op jit(solution)/shard_map/ppermute | solution.py:539
  90.8 1.2 collective-permute-start.18
  92.0 0.7 collective-permute-start.15
  92.9 0.6 collective-permute-start.16
  93.5 10.3 %collective-permute-done.18.refs_6_ = bf16[2,2,4,16,1024]{4,3,2,1,0:T(8,128)(2,1)S(1)} collective-permute-done((bf16[2,2,4,16,1024]{4,3,2,1,0:T(8,128)(2,1)S(1)}, bf16[2,2,4,16,1024]{4,3,2,1,0:T(8,128)(2,1)S(1)}, u32[]{:S(2)}, u32[]{:S(2)}) %collective-permute-start.18) | collective-permute-done | bytes 524320 | tf_op jit(solution)/shard_map/ppermute | solution.py:539
  103.9 1.3 collective-permute-start.19
  105.2 1.5 collective-permute-done.19.refs_7_
  106.7 0.8 copy-done.21
  107.5 6.5 %project.1 = (bf16[128,2048]{1,0:T(8,128)(2,1)S(1)}, bf16[128,2048]{1,0:T(8,128)(2,1)}, bf16[128,2048]{1,0:T(8,128)(2,1)}, bf16[128,2048]{1,0:T(8,128)(2,1)}) custom-call(bf16[2,512,512]{2,1,0:T(8,128)(2,1)} %copy-done.5, bf16[512,512]{1,0:T(8,128)(2,1)S(1)} %collective-permute-done.14.got_ref, bf16[2,2,4,16,1024]{4,3,2,1,0:T(8,128)(2,1)S(1)} %pad_maximum_fusion.1.refs_0_, ...), custom_call_target="tpu_custom_call" | custom-call | flops 2147483648 | bytes 7340032 | tf_op jit(solution)/shard_map/project/pallas_call | solution.py:324
  114.1 2.5 collective-permute-start.20
  116.7 1.1 collective-permute-start.22
  118.6 10.1 %collective-permute-done.20 = bf16[128,2048]{1,0:T(8,128)(2,1)S(1)} collective-permute-done((bf16[128,2048]{1,0:T(8,128)(2,1)}, bf16[128,2048]{1,0:T(8,128)(2,1)S(1)}, u32[]{:S(2)}, u32[]{:S(2)}) %collective-permute-start.20) | collective-permute-done | bytes 524320 | tf_op jit(solution)/shard_map/ppermute | solution.py:539
  128.6 11.5 %collective-permute-done.21 = bf16[128,2048]{1,0:T(8,128)(2,1)S(1)} collective-permute-done((bf16[128,2048]{1,0:T(8,128)(2,1)}, bf16[128,2048]{1,0:T(8,128)(2,1)S(1)}, u32[]{:S(2)}, u32[]{:S(2)}) %collective-permute-start.21) | collective-permute-done | bytes 524320 | tf_op jit(solution)/shard_map/ppermute | solution.py:539
  140.5 2.2 route.1
  142.7 54.2 %all_to_all.15 = bf16[16,32,2048]{2,1,0:T(8,128)(2,1)S(1)} all-to-all(bf16[16,32,2048]{2,1,0:T(8,128)(2,1)S(1)} %bitcast.45), channel_id=1, replica_groups=mesh['grp'=2,'head'=16] {'head'}, dimensions={0} | all-to-all | bytes 4194304 | tf_op jit(solution)/shard_map/all_to_all | solution.py:722
  196.9 5.7 %expert.1 = bf16[512,2048]{1,0:T(8,128)(2,1)S(1)} custom-call(bf16[512,2048]{1,0:T(8,128)(2,1)S(1)} %bitcast.47, bf16[2048,1024]{1,0:T(8,128)(2,1)} %bitcast.64, bf16[512,2048]{1,0:T(8,128)(2,1)} %bitcast.65), custom_call_target="tpu_custom_call" | custom-call | flops 3221225472 | bytes 10485760 | tf_op jit(solution)/shard_map/expert/pallas_call | solution.py:479
  202.6 1.3 copy-done.1
  204.0 5.3 %all-to-all-start.2 = ((bf16[16,32,2048]{2,1,0:T(8,128)(2,1)}), bf16[16,32,2048]{2,1,0:T(8,128)(2,1)S(1)}, u32[]{:S(2)}, u32[]{:S(2)}) async-start(bf16[16,32,2048]{2,1,0:T(8,128)(2,1)} %bitcast.46), calls=%async_computation.2 | async-start | bytes 4194304 | tf_op jit(solution)/shard_map/all_to_all | solution.py:735
  209.3 47.3 %all-to-all-done.2 = bf16[16,32,2048]{2,1,0:T(8,128)(2,1)S(1)} async-done(((bf16[16,32,2048]{2,1,0:T(8,128)(2,1)}), bf16[16,32,2048]{2,1,0:T(8,128)(2,1)S(1)}, u32[]{:S(2)}, u32[]{:S(2)}) %all-to-all-start.2) | async-done | bytes 2097184 | tf_op jit(solution)/shard_map/all_to_all | solution.py:735
  256.6 1.2 copy-done.3
  257.8 1.6 combine.1
  (84 shorter events, 2.5 us)
Async XLA Ops:
  0.0 1.2 copy-start
  0.0 2.3 copy-start.7
  1.3 3.0 %copy-start.22 = (bf16[1,256,512]{2,1,0:T(8,128)(2,1)S(1)}, bf16[1,256,512]{2,1,0:T(8,128)(2,1)}, u32[]{:S(2)}) copy-start(bf16[1,256,512]{2,1,0:T(8,128)(2,1)} %param.12) | copy-start | bytes 786436
  1.3 6.2 %copy-start.8 = (bf16[128,1,16,256]{3,2,1,0:T(8,128)(2,1)S(1)}, bf16[128,1,16,256]{3,2,1,0:T(8,128)(2,1)}, u32[]{:S(2)}) copy-start(bf16[128,1,16,256]{3,2,1,0:T(8,128)(2,1)} %param.10) | copy-start | bytes 3145732
  2.0 7.2 %collective-permute-start.3 = (bf16[2,4,16,1024]{3,2,1,0:T(8,128)(2,1)S(1)}, bf16[2,4,16,1024]{3,2,1,0:T(8,128)(2,1)S(1)}, u32[]{:S(2)}, u32[]{:S(2)}) collective-permute-start(bf16[2,4,16,1024]{3,2,1,0:T(8,128)(2,1)S(1)} %pad_maximum_fusion.4), channel_id=1, source_target_pairs={{0,2},{1,3},{2,0},{3,1},{4,6},{5,7},{6,4},{7,5},{8,10},{9,11},{10,... | collective-permute-start | bytes 786440 | tf_op jit(solution)/shard_map/ppermute | solution.py:539
  2.9 11.9 %collective-permute-start.2 = (bf16[2,128,512]{2,1,0:T(8,128)(2,1)S(1)}, bf16[2,128,512]{2,1,0:T(8,128)(2,1)S(1)}, u32[]{:S(2)}, u32[]{:S(2)}) collective-permute-start(bf16[2,128,512]{2,1,0:T(8,128)(2,1)S(1)} %pad_maximum_fusion.3), channel_id=1, source_target_pairs={{0,2},{1,3},{2,0},{3,1},{4,6},{5,7},{6,4},{7,5},{8,10},{9,11},{10,... | collective-permute-start | bytes 786440 | tf_op jit(solution)/shard_map/ppermute | solution.py:539
  4.3 14.1 %collective-permute-start = (bf16[256,512]{1,0:T(8,128)(2,1)S(1)}, bf16[256,512]{1,0:T(8,128)(2,1)S(1)}, u32[]{:S(2)}, u32[]{:S(2)}) collective-permute-start(bf16[256,512]{1,0:T(8,128)(2,1)S(1)} %bitcast.66), channel_id=1, source_target_pairs={{0,0},{1,1},{2,2},{3,3},{4,8},{5,9},{6,10},{7,11},{8,4},{9,5},{10,... | collective-permute-start | bytes 786440 | tf_op jit(solution)/shard_map/ppermute | solution.py:564
  7.5 10.9 %collective-permute-start.1 = (bf16[256,512]{1,0:T(8,128)(2,1)S(1)}, bf16[256,512]{1,0:T(8,128)(2,1)S(1)}, u32[]{:S(2)}, u32[]{:S(2)}) collective-permute-start(bf16[256,512]{1,0:T(8,128)(2,1)S(1)} %bitcast.67), channel_id=1, source_target_pairs={{0,8},{1,9},{2,10},{3,11},{4,0},{5,1},{6,2},{7,3},{8,12},{9,13},{1... | collective-permute-start | bytes 786440 | tf_op jit(solution)/shard_map/ppermute | solution.py:564
  14.9 16.8 %copy-start.9 = (bf16[2,128,512]{2,1,0:T(8,128)(2,1)}, bf16[2,128,512]{2,1,0:T(8,128)(2,1)S(1)}, u32[]{:S(2)}) copy-start(bf16[2,128,512]{2,1,0:T(8,128)(2,1)S(1)} %collective-permute-done.2) | copy-start | bytes 786436
  19.0 5.7 %collective-permute-start.8 = (bf16[2,4,16,1024]{3,2,1,0:T(8,128)(2,1)S(1)}, bf16[2,4,16,1024]{3,2,1,0:T(8,128)(2,1)S(1)}, u32[]{:S(2)}, u32[]{:S(2)}) collective-permute-start(bf16[2,4,16,1024]{3,2,1,0:T(8,128)(2,1)S(1)} %pad_maximum_fusion.6), channel_id=1, source_target_pairs={{0,4},{1,5},{2,6},{3,7},{4,0},{5,1},{6,2},{7,3},{8,12},{9,13},{10,... | collective-permute-start | bytes 786440 | tf_op jit(solution)/shard_map/ppermute | solution.py:539
  24.7 7.0 %copy-start.10 = (bf16[2,4,16,1024]{3,2,1,0:T(8,128)(2,1)}, bf16[2,4,16,1024]{3,2,1,0:T(8,128)(2,1)S(1)}, u32[]{:S(2)}) copy-start(bf16[2,4,16,1024]{3,2,1,0:T(8,128)(2,1)S(1)} %collective-permute-done.8) | copy-start | bytes 786436
  24.7 39.2 %all-to-all-start = ((bf16[8,2,128,256]{3,2,1,0:T(8,128)(2,1)}), bf16[8,2,128,256]{3,2,1,0:T(8,128)(2,1)S(1)}, u32[]{:S(2)}, u32[]{:S(2)}) async-start(bf16[8,2,128,256]{3,2,1,0:T(8,128)(2,1)} %bitcast.55), calls=%async_computation | async-start | bytes 2097152 | tf_op jit(solution)/shard_map/all_to_all | solution.py:597
  31.7 31.4 %copy-start.15 = (bf16[512,512]{1,0:T(8,128)(2,1)}, bf16[512,512]{1,0:T(8,128)(2,1)S(1)}, u32[]{:S(2)}) copy-start(bf16[512,512]{1,0:T(8,128)(2,1)S(1)} %constant_dynamic-update-slice_fusion) | copy-start | bytes 1572868
  31.7 32.2 %collective-permute-start.4 = (bf16[512,512]{1,0:T(8,128)(2,1)S(1)}, bf16[512,512]{1,0:T(8,128)(2,1)S(1)}, u32[]{:S(2)}, u32[]{:S(2)}) collective-permute-start(bf16[512,512]{1,0:T(8,128)(2,1)S(1)} %constant_dynamic-update-slice_fusion), channel_id=1, source_target_pairs={{0,2},{1,3},{2,0},{3,1},{4,6},{5,7},{6,4},{7,5},{8,10},{9,11},{10,... | collective-permute-start | bytes 1572872 | tf_op jit(solution)/shard_map/ppermute | solution.py:539
  33.1 26.9 %collective-permute-start.5 = (bf16[2,128,512]{2,1,0:T(8,128)(2,1)S(1)}, bf16[2,128,512]{2,1,0:T(8,128)(2,1)S(1)}, u32[]{:S(2)}, u32[]{:S(2)}) collective-permute-start(bf16[2,128,512]{2,1,0:T(8,128)(2,1)S(1)} %pad_maximum_fusion.5), channel_id=1, source_target_pairs={{0,4},{1,5},{2,6},{3,7},{4,0},{5,1},{6,2},{7,3},{8,12},{9,13},{10,... | collective-permute-start | bytes 786440 | tf_op jit(solution)/shard_map/ppermute | solution.py:539
  33.3 26.7 %collective-permute-start.7 = (bf16[2,128,512]{2,1,0:T(8,128)(2,1)S(1)}, bf16[2,128,512]{2,1,0:T(8,128)(2,1)S(1)}, u32[]{:S(2)}, u32[]{:S(2)}) collective-permute-start(bf16[2,128,512]{2,1,0:T(8,128)(2,1)S(1)} %pad_maximum_fusion.5), channel_id=1, source_target_pairs={{0,12},{1,13},{2,14},{3,15},{4,8},{5,9},{6,10},{7,11},{8,4},{9,5},... | collective-permute-start | bytes 786440 | tf_op jit(solution)/shard_map/ppermute | solution.py:539
  35.9 27.2 %collective-permute-start.6 = (bf16[2,128,512]{2,1,0:T(8,128)(2,1)S(1)}, bf16[2,128,512]{2,1,0:T(8,128)(2,1)S(1)}, u32[]{:S(2)}, u32[]{:S(2)}) collective-permute-start(bf16[2,128,512]{2,1,0:T(8,128)(2,1)S(1)} %pad_maximum_fusion.2), channel_id=1, source_target_pairs={{0,8},{1,9},{2,10},{3,11},{4,12},{5,13},{6,14},{7,15},{8,0},{9,1},... | collective-permute-start | bytes 786440 | tf_op jit(solution)/shard_map/ppermute | solution.py:539
  60.0 3.2 %copy-start.12 = (bf16[2,128,512]{2,1,0:T(8,128)(2,1)}, bf16[2,128,512]{2,1,0:T(8,128)(2,1)S(1)}, u32[]{:S(2)}) copy-start(bf16[2,128,512]{2,1,0:T(8,128)(2,1)S(1)} %collective-permute-done.5) | copy-start | bytes 786436
  60.0 3.2 %copy-start.13 = (bf16[2,128,512]{2,1,0:T(8,128)(2,1)}, bf16[2,128,512]{2,1,0:T(8,128)(2,1)S(1)}, u32[]{:S(2)}) copy-start(bf16[2,128,512]{2,1,0:T(8,128)(2,1)S(1)} %collective-permute-done.7) | copy-start | bytes 786436
  63.2 0.7 copy-start.14
  63.9 2.3 copy-start.16
  63.9 3.8 %copy-start.11 = (bf16[2,4,16,1024]{3,2,1,0:T(8,128)(2,1)S(1)}, bf16[2,4,16,1024]{3,2,1,0:T(8,128)(2,1)}, u32[]{:S(2)}) copy-start(bf16[2,4,16,1024]{3,2,1,0:T(8,128)(2,1)} %copy-done.10) | copy-start | bytes 786436
  65.2 4.9 %collective-permute-start.11 = (bf16[4,2,128,512]{3,2,1,0:T(8,128)(2,1)S(1)}, bf16[4,2,128,512]{3,2,1,0:T(8,128)(2,1)S(1)}, u32[]{:S(2)}, u32[]{:S(2)}) collective-permute-start(bf16[4,2,128,512]{3,2,1,0:T(8,128)(2,1)S(1)} %pad_maximum_fusion.kv_own), channel_id=1, source_target_pairs={{0,1},{1,0},{2,3},{3,2},{4,5},{5,4},{6,7},{7,6},{8,9},{9,8},{10,11... | collective-permute-start | bytes 3145736 | tf_op jit(solution)/shard_map/ppermute | solution.py:539
  66.2 3.9 %collective-permute-start.9 = (bf16[512,512]{1,0:T(8,128)(2,1)S(1)}, bf16[512,512]{1,0:T(8,128)(2,1)S(1)}, u32[]{:S(2)}, u32[]{:S(2)}) collective-permute-start(bf16[512,512]{1,0:T(8,128)(2,1)S(1)} %copy-done.16), channel_id=1, source_target_pairs={{0,1},{1,0},{2,3},{3,2},{4,5},{5,4},{6,7},{7,6},{8,9},{9,8},{10,11... | collective-permute-start | bytes 1572872 | tf_op jit(solution)/shard_map/ppermute | solution.py:539
  66.3 3.8 %collective-permute-start.10 = (bf16[512,512]{1,0:T(8,128)(2,1)S(1)}, bf16[512,512]{1,0:T(8,128)(2,1)S(1)}, u32[]{:S(2)}, u32[]{:S(2)}) collective-permute-start(bf16[512,512]{1,0:T(8,128)(2,1)S(1)} %collective-permute-done.4.page_y), channel_id=1, source_target_pairs={{0,1},{1,0},{2,3},{3,2},{4,5},{5,4},{6,7},{7,6},{8,9},{9,8},{10,11... | collective-permute-start | bytes 1572872 | tf_op jit(solution)/shard_map/ppermute | solution.py:539
  67.8 23.0 %collective-permute-start.12 = (bf16[2,2,4,16,1024]{4,3,2,1,0:T(8,128)(2,1)S(1)}, bf16[2,2,4,16,1024]{4,3,2,1,0:T(8,128)(2,1)S(1)}, u32[]{:S(2)}, u32[]{:S(2)}) collective-permute-start(bf16[2,2,4,16,1024]{4,3,2,1,0:T(8,128)(2,1)S(1)} %pad_maximum_fusion.1.refs_0_), channel_id=1, source_target_pairs={{0,8},{1,9},{2,10},{3,11},{4,12},{5,13},{6,14},{7,15},{8,0},{9,1},... | collective-permute-start | bytes 1572872 | tf_op jit(solution)/shard_map/ppermute | solution.py:539
  68.9 21.9 %collective-permute-start.13 = (bf16[2,2,4,16,1024]{4,3,2,1,0:T(8,128)(2,1)S(1)}, bf16[2,2,4,16,1024]{4,3,2,1,0:T(8,128)(2,1)S(1)}, u32[]{:S(2)}, u32[]{:S(2)}) collective-permute-start(bf16[2,2,4,16,1024]{4,3,2,1,0:T(8,128)(2,1)S(1)} %pad_maximum_fusion.1.refs_0_), channel_id=1, source_target_pairs={{0,16},{16,0},{1,17},{17,1},{2,18},{18,2},{3,19},{19,3},{4,20},{20... | collective-permute-start | bytes 1572872 | tf_op jit(solution)/shard_map/ppermute | solution.py:539
  70.1 1.0 copy-start.19
  86.9 19.8 %copy-start.5 = (bf16[2,512,512]{2,1,0:T(8,128)(2,1)}, bf16[2,512,512]{2,1,0:T(8,128)(2,1)S(1)}, u32[]{:S(2)}) copy-start(bf16[2,512,512]{2,1,0:T(8,128)(2,1)S(1)} %attend.1.a_ref) | copy-start | bytes 3145732
  90.8 13.0 %collective-permute-start.18 = (bf16[2,2,4,16,1024]{4,3,2,1,0:T(8,128)(2,1)S(1)}, bf16[2,2,4,16,1024]{4,3,2,1,0:T(8,128)(2,1)S(1)}, u32[]{:S(2)}, u32[]{:S(2)}) collective-permute-start(bf16[2,2,4,16,1024]{4,3,2,1,0:T(8,128)(2,1)S(1)} %collective-permute-done.12.refs_4_), channel_id=1, source_target_pairs={{0,16},{16,0},{1,17},{17,1},{2,18},{18,2},{3,19},{19,3},{4,20},{20... | collective-permute-start | bytes 1572872 | tf_op jit(solution)/shard_map/ppermute | solution.py:539
  92.0 13.1 %collective-permute-start.15 = (bf16[2,2,4,16,1024]{4,3,2,1,0:T(8,128)(2,1)S(1)}, bf16[2,2,4,16,1024]{4,3,2,1,0:T(8,128)(2,1)S(1)}, u32[]{:S(2)}, u32[]{:S(2)}) collective-permute-start(bf16[2,2,4,16,1024]{4,3,2,1,0:T(8,128)(2,1)S(1)} %pad_maximum_fusion.1.refs_0_), channel_id=1, source_target_pairs={{0,1},{1,0},{2,3},{3,2},{4,5},{5,4},{6,7},{7,6},{8,9},{9,8},{10,11... | collective-permute-start | bytes 1572872 | tf_op jit(solution)/shard_map/ppermute | solution.py:539
  92.8 12.4 %collective-permute-start.17 = (bf16[2,2,4,16,1024]{4,3,2,1,0:T(8,128)(2,1)S(1)}, bf16[2,2,4,16,1024]{4,3,2,1,0:T(8,128)(2,1)S(1)}, u32[]{:S(2)}, u32[]{:S(2)}) collective-permute-start(bf16[2,2,4,16,1024]{4,3,2,1,0:T(8,128)(2,1)S(1)} %collective-permute-done.12.refs_4_), channel_id=1, source_target_pairs={{0,1},{1,0},{2,3},{3,2},{4,5},{5,4},{6,7},{7,6},{8,9},{9,8},{10,11... | collective-permute-start | bytes 1572872 | tf_op jit(solution)/shard_map/ppermute | solution.py:539
  92.8 25.0 %copy-start.17 = (s32[128,1,2]{0,2,1:T(2,128)S(1)}, s32[128,1,2]{0,2,1:T(2,128)}, u32[]{:S(2)}) copy-start(s32[128,1,2]{0,2,1:T(2,128)} %param.16) | copy-start | bytes 3076
  92.8 47.7 %copy-start.4 = (bf16[128,1,2048]{2,0,1:T(8,128)(2,1)S(1)}, bf16[128,1,2048]{2,0,1:T(8,128)(2,1)}, u32[]{:S(2)}) copy-start(bf16[128,1,2048]{2,0,1:T(8,128)(2,1)} %param.13) | copy-start | bytes 1572868
  92.8 47.7 %copy-start.6 = (f32[2048]{0:T(1024)S(1)}, f32[2048]{0:T(1024)}, u32[]{:S(2)}) copy-start(f32[2048]{0:T(1024)} %param.15) | copy-start | bytes 24580
  92.9 12.3 %collective-permute-start.16 = (bf16[2,2,4,16,1024]{4,3,2,1,0:T(8,128)(2,1)S(1)}, bf16[2,2,4,16,1024]{4,3,2,1,0:T(8,128)(2,1)S(1)}, u32[]{:S(2)}, u32[]{:S(2)}) collective-permute-start(bf16[2,2,4,16,1024]{4,3,2,1,0:T(8,128)(2,1)S(1)} %collective-permute-done.13.refs_2_), channel_id=1, source_target_pairs={{0,1},{1,0},{2,3},{3,2},{4,5},{5,4},{6,7},{7,6},{8,9},{9,8},{10,11... | collective-permute-start | bytes 1572872 | tf_op jit(solution)/shard_map/ppermute | solution.py:539
  93.4 11.7 %collective-permute-start.14 = (bf16[512,512]{1,0:T(8,128)(2,1)S(1)}, bf16[512,512]{1,0:T(8,128)(2,1)S(1)}, u32[]{:S(2)}, u32[]{:S(2)}) collective-permute-start(bf16[512,512]{1,0:T(8,128)(2,1)S(1)} %slice_bitcast_fusion), channel_id=1, source_target_pairs={{0,1},{1,0},{2,3},{3,2},{4,5},{5,4},{6,7},{7,6},{8,9},{9,8},{10,11... | collective-permute-start | bytes 1572872 | tf_op jit(solution)/shard_map/ppermute | solution.py:539
  103.9 2.9 %copy-start.20 = (bf16[2,2,4,16,1024]{4,3,2,1,0:T(8,128)(2,1)}, bf16[2,2,4,16,1024]{4,3,2,1,0:T(8,128)(2,1)S(1)}, u32[]{:S(2)}) copy-start(bf16[2,2,4,16,1024]{4,3,2,1,0:T(8,128)(2,1)S(1)} %collective-permute-done.18.refs_6_) | copy-start | bytes 1572868
  103.9 2.8 %collective-permute-start.19 = (bf16[2,2,4,16,1024]{4,3,2,1,0:T(8,128)(2,1)S(1)}, bf16[2,2,4,16,1024]{4,3,2,1,0:T(8,128)(2,1)S(1)}, u32[]{:S(2)}, u32[]{:S(2)}) collective-permute-start(bf16[2,2,4,16,1024]{4,3,2,1,0:T(8,128)(2,1)S(1)} %collective-permute-done.18.refs_6_), channel_id=1, source_target_pairs={{0,1},{1,0},{2,3},{3,2},{4,5},{5,4},{6,7},{7,6},{8,9},{9,8},{10,11... | collective-permute-start | bytes 1572872 | tf_op jit(solution)/shard_map/ppermute | solution.py:539
  106.7 0.8 copy-start.21
  114.1 14.6 %collective-permute-start.20 = (bf16[128,2048]{1,0:T(8,128)(2,1)}, bf16[128,2048]{1,0:T(8,128)(2,1)S(1)}, u32[]{:S(2)}, u32[]{:S(2)}) collective-permute-start(bf16[128,2048]{1,0:T(8,128)(2,1)} %get-tuple-element.46), channel_id=1, source_target_pairs={{0,6},{1,7},{2,4},{3,5},{4,2},{5,3},{6,0},{7,1},{8,14},{9,15},{10,... | collective-permute-start | bytes 1572872 | tf_op jit(solution)/shard_map/ppermute | solution.py:539
  116.6 23.6 %collective-permute-start.21 = (bf16[128,2048]{1,0:T(8,128)(2,1)}, bf16[128,2048]{1,0:T(8,128)(2,1)S(1)}, u32[]{:S(2)}, u32[]{:S(2)}) collective-permute-start(bf16[128,2048]{1,0:T(8,128)(2,1)} %get-tuple-element.47), channel_id=1, source_target_pairs={{0,4},{1,5},{2,6},{3,7},{4,0},{5,1},{6,2},{7,3},{8,12},{9,13},{10,... | collective-permute-start | bytes 1572872 | tf_op jit(solution)/shard_map/ppermute | solution.py:539
  116.7 23.9 %collective-permute-start.22 = (bf16[128,2048]{1,0:T(8,128)(2,1)}, bf16[128,2048]{1,0:T(8,128)(2,1)}, u32[]{:S(2)}, u32[]{:S(2)}) collective-permute-start(bf16[128,2048]{1,0:T(8,128)(2,1)} %get-tuple-element.48), channel_id=1, source_target_pairs={{0,2},{1,3},{2,0},{3,1},{4,6},{5,7},{6,4},{7,5},{8,10},{9,11},{10,... | collective-permute-start | bytes 1572872 | tf_op jit(solution)/shard_map/ppermute | solution.py:539
  142.7 54.2 %copy-start.2 = (f32[128,2048]{1,0:T(8,128)}, f32[128,2048]{1,0:T(8,128)S(1)}, u32[]{:S(2)}) copy-start(f32[128,2048]{1,0:T(8,128)S(1)} %get-tuple-element.50.stream_ref) | copy-start | bytes 3145732
  202.6 1.3 copy-start.1
  203.9 5.3 %copy-start.18 = (f32[128,1,2]{0,2,1:T(2,128)S(1)}, f32[128,1,2]{0,2,1:T(2,128)}, u32[]{:S(2)}) copy-start(f32[128,1,2]{0,2,1:T(2,128)} %param.17) | copy-start | bytes 3076
  204.0 52.7 %all-to-all-start.2 = ((bf16[16,32,2048]{2,1,0:T(8,128)(2,1)}), bf16[16,32,2048]{2,1,0:T(8,128)(2,1)S(1)}, u32[]{:S(2)}, u32[]{:S(2)}) async-start(bf16[16,32,2048]{2,1,0:T(8,128)(2,1)} %bitcast.46), calls=%async_computation.2 | async-start | bytes 4194304 | tf_op jit(solution)/shard_map/all_to_all | solution.py:735
  256.6 1.2 copy-start.3

commit v11 on v9

--- a/solution.py
+++ b/solution.py
@@ -133,13 +133,14 @@
     chunk,
     width,
     q_hbm,
-    page_a,
-    page_b,
+    page_own,
     page_y,
     page_c,
     page_cy,
     kv_own,
+    kv_y,
     kv_c,
+    kv_cy,
     o_ref,
     q_ref,
     old_ref,
@@ -151,7 +152,7 @@
     me = lax.axis_index("head")
     members, heads, piece, _ = q_hbm.shape
     length = members * piece
-    planes, sides = kv_own.shape[:2]
+    planes = kv_own.shape[0]
     old = old_ref.shape[0]
     earlier_group = me // members > 0
     core = lax.rem(me, 2)
@@ -167,19 +168,18 @@
         for head in range(heads):
             bring(q_hbm.at[member, head], q_ref.at[head, pl.ds(member * piece, piece)], 0)
     place = 0
-    for page in (page_a, page_b, page_y, page_c, page_cy):
+    for page in (page_own, page_y, page_c, page_cy):
         count = page.shape[0]
         bring(page, old_ref.at[pl.ds(place, count)], 1)
         place += count
-    for flip, pieces_of in ((0, kv_own), (1, kv_c)):
+    for flip, pieces_of in ((0, kv_own), (2, kv_y), (1, kv_c), (3, kv_cy)):
         for t in range(planes):
-            for u in range(sides):
-                number = jnp.bitwise_and(
-                    jnp.bitwise_xor(me, flip ^ (2 * u) ^ (t * (members // 2))), members - 1
-                )
-                start = pl.multiple_of(number * piece, piece)
-                area = 0 if t * (members // 2) >= members else length
-                bring(pieces_of.at[t, u], kv_ref.at[pl.ds(area + start, piece)], 2)
+            number = jnp.bitwise_and(
+                jnp.bitwise_xor(me, flip ^ (t * (members // 2))), members - 1
+            )
+            start = pl.multiple_of(number * piece, piece)
+            area = 0 if t * (members // 2) >= members else length
+            bring(pieces_of.at[t], kv_ref.at[pl.ds(area + start, piece)], 2)
     for copy in copies:
         copy.wait()
     scale = width**-0.5 * LOG2_E
@@ -555,6 +555,9 @@
 
     query_slots = queries.reshape(local_rows, heads, width).transpose(1, 0, 2)
     query_slots = query_slots.reshape(members, heads // members, local_rows, width)
+    q = lax.all_to_all(
+        query_slots, "head", split_axis=0, concat_axis=0, tiled=True, axis_index_groups=group_sets
+    )
 
     def page_target(source, other):
         p, plane, rest = source // members, (source // plane_bit) % 2, source % plane_bit
@@ -565,46 +568,45 @@
         for other in range(2)
     )
     kv_heads = new_kv.reshape(local_rows, pair_heads, 2 * width).transpose(1, 0, 2)
-    kv_beside = flipped(kv_heads, "head", 2)
-
+    kv_same = lax.dynamic_index_in_dim(kv_heads, b, 0, keepdims=False)
+    kv_other = lax.dynamic_index_in_dim(kv_heads, 1 - b, 0, keepdims=False)
     columns = model // 2
     w = lax.dynamic_slice_in_dim(w_out, lax.axis_index("grp") * columns, columns, 2)
     w = w.reshape(2, 2, heads // 4, share, columns)
     w_keep = lax.dynamic_index_in_dim(w, y, 1, keepdims=False)
     w_give = lax.dynamic_index_in_dim(w, 1 - y, 1, keepdims=False)
-    w_got = flipped(w_give, "head", 2)
-
-    page_a, page_b, kv_beside, query_slots = lax.optimization_barrier(
-        (page_a, page_b, kv_beside, query_slots)
-    )
-    kv_both = jnp.stack([kv_heads, kv_beside], 1)
-    kv_same = lax.dynamic_index_in_dim(kv_both, b, 0, keepdims=False)
-    kv_other = lax.dynamic_index_in_dim(kv_both, 1 - b, 0, keepdims=False)
     kv_own = [kv_same]
     for t in range(1, planes):
         kv_own.append(flipped(kv_other if t % 2 else kv_same, "head", t * plane_bit))
+
+    (page_a, page_b, kv_own), w_give = lax.optimization_barrier(
+        ((page_a, page_b, kv_own), w_give)
+    )
     own_pages = jnp.concatenate([page_a, page_b], 0)
+    kv_own = jnp.stack(kv_own, 0)
     pages_y = flipped(own_pages, "head", 2)
-    q = lax.all_to_all(
-        query_slots, "head", split_axis=0, concat_axis=0, tiled=True, axis_index_groups=group_sets
-    )
+    kv_y = flipped(kv_own, "head", 2)
+    w_got = flipped(w_give, "head", 2)
     w_both = jnp.stack([w_keep, w_got], 1)
     w_same = lax.dynamic_index_in_dim(w_both, b, 0, keepdims=False)
     w_other = lax.dynamic_index_in_dim(w_both, 1 - b, 0, keepdims=False)
     w_first = flipped(w_other, "head", plane_bit)
-    pages_y, kv_own, w_first, q = lax.optimization_barrier((pages_y, kv_own, w_first, q))
-
-    kv_own = jnp.stack(kv_own, 0)
+    w_far = [flipped(w_same, "head", 2 * plane_bit), flipped(w_other, "head", 3 * plane_bit)]
+    pages_y, kv_y, own_pages, kv_own, w_first = lax.optimization_barrier(
+        (pages_y, kv_y, own_pages, kv_own, w_first)
+    )
     kv_c = flipped(kv_own, "head", 1)
+    kv_cy = flipped(kv_y, "head", 1)
     pages_c = flipped(own_pages, "head", 1)
     pages_cy = flipped(pages_y, "head", 1)
     w_near = jnp.stack([w_same, w_first], 0)
-    w_far = flipped(w_near, "head", members)
     w_near_x = flipped(w_near, "grp", 1)
-    a = attend_pair(q, (page_a, page_b, pages_y, pages_c, pages_cy), (kv_own, kv_c))
+    w_far = jnp.stack(w_far, 0)
+    q, w_far = lax.optimization_barrier((q, w_far))
+    w_far_x = flipped(w_far, "grp", 1)
+    a = attend_pair(q, (own_pages, pages_y, pages_c, pages_cy), (kv_own, kv_y, kv_c, kv_cy))
     got = flipped(a[1], "head", 1)
-    a, w_far, w_near_x = lax.optimization_barrier((a, w_far, w_near_x))
-    w_far_x = flipped(w_far, "grp", 1)
+    a, w_near_x, w_far_x = lax.optimization_barrier((a, w_near_x, w_far_x))
     w_near_c = flipped(w_near, "head", 1)
     w_far_c = flipped(w_far, "head", 1)
     w_near_cx = flipped(w_near_x, "head", 1)

time: 267 us -> 260 us (0.974)
  waiting for transfers between devices: 130 us -> 139 us
  other arithmetic: 5.2 us -> 0.45 us
  starting transfers between devices: 34.9 us -> 30.2 us
  local copies, waits for them, and re-layouts: 11.6 us -> 7.45 us
    ppermute x21 -> x23, waiting for transfers between devices: 75.4 us -> 91.9 us  [flipped(): return lax.ppermute(value, axis, pairs)]
    ppermute x2, waiting for transfers between devices: 7.62 us -> 0.01 us  [parts_in_pairs(): lax.ppermute(cache[0], 'head', [(d, page_target(d, other)) for d in range...]
    ppermute x21 -> x23, starting transfers between devices: 20.7 us -> 16.8 us  [flipped(): return lax.ppermute(value, axis, pairs)]
    unnamed x44 -> x31, local copies, waits for them, and re-layouts: 7.16 us -> 3.71 us
  transfers between devices with their start and end apart: 25 -> 27, of which waited for: 15 -> 11; matrix products, arithmetic and copies ran while one was open for 3% -> 1% of each run, Pallas kernels for 6% -> 5%
where the time goes in v11:
time: 260 us; the launch traced here: 259 us
  waiting for transfers between devices  139 us (53%)
  blocking collectives  51.5 us (20%)
  starting transfers between devices  30.2 us (12%)
  Pallas kernels  29.9 us (12%)
  local copies, waits for them, and re-layouts  7.45 us (3%)
    ppermute x23, waiting for transfers between devices, flipped(): return lax.ppermute(value, axis, pairs)  91.9 us
    all_to_all x1, blocking collectives, local(): lax.all_to_all(outgoing.reshape(n, slots // n, model), 'head', split_axis...  51.5 us
    all_to_all x1, waiting for transfers between devices, local(): lax.all_to_all(answered, 'head', split_axis=0, concat_axis=0, tiled=True)  47.3 us
    ppermute x23, starting transfers between devices, flipped(): return lax.ppermute(value, axis, pairs)  16.8 us
    pallas_call x1, Pallas kernels, attend_pair(): pl.pallas_call(functools.partial(attend_pair_kernel, block, chunk, width)...  13.8 us
    pallas_call x1, Pallas kernels, project_pair(): pl.pallas_call(project_pair_kernel, out_shape=[jax.ShapeDtypeStruct((rows...  6.64 us
    pallas_call x1, Pallas kernels, expert_pair(): pl.pallas_call(kernel, out_shape=jax.ShapeDtypeStruct((rows, model), BF16...  5.69 us
    all_to_all x1, starting transfers between devices, local(): lax.all_to_all(answered, 'head', split_axis=0, concat_axis=0, tiled=True)  5.25 us
  transfers between devices with their start and end apart: 27, of which 11 were waited for; matrix products, arithmetic and copies ran while one was open for 1% of the time, Pallas kernels for 5%

profile of v11, /device:TPU:13, one launch (start us, length us, event | category | flops | bytes accessed | tf_op | source)
XLA Modules:
  0.0 259.2 jit_solution(18251659570811001254)
XLA Ops:
  0.0 2.7 %copy.27 = bf16[16,128,256]{2,1,0:T(8,128)(2,1)} copy(bf16[16,128,256]{2,0,1:T(8,128)(2,1)} %bitcast.56) | data formatting | bytes 2097152 | tf_op jit(solution)/shard_map/transpose | solution.py:556
  2.7 4.5 %all-to-all-start = ((bf16[8,2,128,256]{3,2,1,0:T(8,128)(2,1)}), bf16[8,2,128,256]{3,2,1,0:T(8,128)(2,1)}, u32[]{:S(2)}, u32[]{:S(2)}) async-start(bf16[8,2,128,256]{3,2,1,0:T(8,128)(2,1)} %bitcast.6), calls=%async_computation | async-start | bytes 2097152 | tf_op jit(solution)/shard_map/all_to_all | solution.py:558
  7.2 3.6 %collective-permute-start = (bf16[256,512]{1,0:T(8,128)(2,1)S(1)}, bf16[256,512]{1,0:T(8,128)(2,1)S(1)}, u32[]{:S(2)}, u32[]{:S(2)}) collective-permute-start(bf16[256,512]{1,0:T(8,128)(2,1)S(1)} %bitcast.72), channel_id=1, source_target_pairs={{0,0},{1,1},{2,2},{3,3},{4,8},{5,9},{6,10},{7,11},{8,4},{9,5},{10,... | collective-permute-start | bytes 786440 | tf_op jit(solution)/shard_map/ppermute | solution.py:567
  10.9 0.5 constant_dynamic-slice_fusion
  11.5 1.2 collective-permute-start.2
  12.7 1.5 collective-permute-start.4
  14.2 1.0 collective-permute-start.3
  15.4 14.4 %collective-permute-done.2 = bf16[128,512]{1,0:T(8,128)(2,1)S(1)} collective-permute-done((bf16[128,512]{1,0:T(8,128)(2,1)S(1)}, bf16[128,512]{1,0:T(8,128)(2,1)S(1)}, u32[]{:S(2)}, u32[]{:S(2)}) %collective-permute-start.2) | collective-permute-done | bytes 131104 | tf_op jit(solution)/shard_map/ppermute | solution.py:539
  29.8 6.3 %collective-permute-done.3 = bf16[128,512]{1,0:T(8,128)(2,1)S(1)} collective-permute-done((bf16[128,512]{1,0:T(8,128)(2,1)S(1)}, bf16[128,512]{1,0:T(8,128)(2,1)S(1)}, u32[]{:S(2)}, u32[]{:S(2)}) %collective-permute-start.3) | collective-permute-done | bytes 131104 | tf_op jit(solution)/shard_map/ppermute | solution.py:539
  36.2 0.3 collective-permute-start.9
  36.6 1.2 collective-permute-start.5
  37.8 0.3 collective-permute-start.8
  38.1 16.3 %collective-permute-done.5 = bf16[2,4,16,1024]{3,2,1,0:T(8,128)(2,1)S(1)} collective-permute-done((bf16[2,4,16,1024]{3,2,1,0:T(8,128)(2,1)S(1)}, bf16[2,4,16,1024]{3,2,1,0:T(8,128)(2,1)S(1)}, u32[]{:S(2)}, u32[]{:S(2)}) %collective-permute-start.5) | collective-permute-done | bytes 262176 | tf_op jit(solution)/shard_map/ppermute | solution.py:539
  54.5 0.1 collective-permute-start.10
  54.5 0.1 collective-permute-start.6
  54.6 11.1 %collective-permute-done.8.page_y = bf16[512,512]{1,0:T(8,128)(2,1)} collective-permute-done((bf16[512,512]{1,0:T(8,128)(2,1)S(1)}, bf16[512,512]{1,0:T(8,128)(2,1)}, u32[]{:S(2)}, u32[]{:S(2)}) %collective-permute-start.8) | collective-permute-done | bytes 524320 | tf_op jit(solution)/shard_map/ppermute | solution.py:539
  65.8 1.8 collective-permute-start.11
  67.6 0.5 collective-permute-start.13
  68.2 12.9 %collective-permute-done.7 = bf16[2,4,16,1024]{3,2,1,0:T(8,128)(2,1)S(1)} collective-permute-done((bf16[2,4,16,1024]{3,2,1,0:T(8,128)(2,1)S(1)}, bf16[2,4,16,1024]{3,2,1,0:T(8,128)(2,1)S(1)}, u32[]{:S(2)}, u32[]{:S(2)}) %collective-permute-start.7) | collective-permute-done | bytes 262176 | tf_op jit(solution)/shard_map/ppermute | solution.py:539
  81.1 1.2 collective-permute-start.15
  82.4 1.7 collective-permute-start.18
  84.1 0.3 collective-permute-start.16
  84.4 0.4 collective-permute-start.20
  84.7 13.8 %attend.1.a_ref = bf16[2,512,512]{2,1,0:T(8,128)(2,1)S(1)} custom-call(bf16[8,2,128,256]{3,2,1,0:T(8,128)(2,1)} %all-to-all-done.q_hbm, bf16[512,512]{1,0:T(8,128)(2,1)S(1)} %constant_dynamic-update-slice_fusion.page_own, bf16[512,512]{1,0:T(8,128)(2,1)} %collective-permute-done.8.page_y, bf16[512,512]{1,0:T(8,128)(2,1)} %collective-permute-done.11.page_c, ...), custom_call_target="tpu_custom_call" | custom-call | flops 7516192768 | bytes 6291456 | tf_op jit(solution)/shard_map/attend/pallas_call | solution.py:259
  98.6 0.2 collective-permute-start.17
  98.9 5.5 %collective-permute-done.16.refs_6_ = bf16[2,2,4,16,1024]{4,3,2,1,0:T(8,128)(2,1)S(1)} collective-permute-done((bf16[2,2,4,16,1024]{4,3,2,1,0:T(8,128)(2,1)S(1)}, bf16[2,2,4,16,1024]{4,3,2,1,0:T(8,128)(2,1)S(1)}, u32[]{:S(2)}, u32[]{:S(2)}) %collective-permute-start.16) | collective-permute-done | bytes 524320 | tf_op jit(solution)/shard_map/ppermute | solution.py:539
  104.4 2.3 collective-permute-start.19
  106.7 2.4 collective-permute-done.19.refs_3_
  109.1 0.8 copy-done.11
  109.9 6.6 %project.1 = (bf16[128,2048]{1,0:T(8,128)(2,1)S(1)}, bf16[128,2048]{1,0:T(8,128)(2,1)}, bf16[128,2048]{1,0:T(8,128)(2,1)}, bf16[128,2048]{1,0:T(8,128)(2,1)}) custom-call(bf16[2,512,512]{2,1,0:T(8,128)(2,1)} %copy-done.5, bf16[512,512]{1,0:T(8,128)(2,1)S(1)} %collective-permute-done.17.got_ref, bf16[2,2,4,16,1024]{4,3,2,1,0:T(8,128)(2,1)S(1)} %pad_maximum_fusion.2.refs_0_, ...), custom_call_target="tpu_custom_call" | custom-call | flops 2147483648 | bytes 7340032 | tf_op jit(solution)/shard_map/project/pallas_call | solution.py:324
  116.7 2.1 collective-permute-start.23
  118.7 0.5 collective-permute-start.24
  119.3 0.1 copy.21
  119.5 0.1 copy.23
  119.6 0.2 reduce_window_sum.11
  119.9 0.1 copy.26
  120.1 10.9 %collective-permute-done.22 = bf16[128,2048]{1,0:T(8,128)(2,1)S(1)} collective-permute-done((bf16[128,2048]{1,0:T(8,128)(2,1)}, bf16[128,2048]{1,0:T(8,128)(2,1)S(1)}, u32[]{:S(2)}, u32[]{:S(2)}) %collective-permute-start.22) | collective-permute-done | bytes 524320 | tf_op jit(solution)/shard_map/ppermute | solution.py:539
  130.9 11.1 %collective-permute-done.23 = bf16[128,2048]{1,0:T(8,128)(2,1)S(1)} collective-permute-done((bf16[128,2048]{1,0:T(8,128)(2,1)}, bf16[128,2048]{1,0:T(8,128)(2,1)S(1)}, u32[]{:S(2)}, u32[]{:S(2)}) %collective-permute-start.23) | collective-permute-done | bytes 524320 | tf_op jit(solution)/shard_map/ppermute | solution.py:539
  142.0 0.9 collective-permute-done.24
  142.9 2.2 route.1
  145.1 51.5 %all_to_all.15 = bf16[16,32,2048]{2,1,0:T(8,128)(2,1)S(1)} all-to-all(bf16[16,32,2048]{2,1,0:T(8,128)(2,1)S(1)} %bitcast.45), channel_id=1, replica_groups=mesh['grp'=2,'head'=16] {'head'}, dimensions={0} | all-to-all | bytes 4194304 | tf_op jit(solution)/shard_map/all_to_all | solution.py:719
  196.6 5.7 %expert.1 = bf16[512,2048]{1,0:T(8,128)(2,1)S(1)} custom-call(bf16[512,2048]{1,0:T(8,128)(2,1)S(1)} %bitcast.47, bf16[2048,1024]{1,0:T(8,128)(2,1)} %bitcast.70, bf16[512,2048]{1,0:T(8,128)(2,1)} %bitcast.71), custom_call_target="tpu_custom_call" | custom-call | flops 3221225472 | bytes 10485760 | tf_op jit(solution)/shard_map/expert/pallas_call | solution.py:479
  202.3 1.4 copy-done.1
  203.7 5.3 %all-to-all-start.2 = ((bf16[16,32,2048]{2,1,0:T(8,128)(2,1)}), bf16[16,32,2048]{2,1,0:T(8,128)(2,1)S(1)}, u32[]{:S(2)}, u32[]{:S(2)}) async-start(bf16[16,32,2048]{2,1,0:T(8,128)(2,1)} %bitcast.46), calls=%async_computation.2 | async-start | bytes 4194304 | tf_op jit(solution)/shard_map/all_to_all | solution.py:732
  208.9 0.1 copy.31
  209.1 47.3 %all-to-all-done.2 = bf16[16,32,2048]{2,1,0:T(8,128)(2,1)S(1)} async-done(((bf16[16,32,2048]{2,1,0:T(8,128)(2,1)}), bf16[16,32,2048]{2,1,0:T(8,128)(2,1)S(1)}, u32[]{:S(2)}, u32[]{:S(2)}) %all-to-all-start.2) | async-done | bytes 2097184 | tf_op jit(solution)/shard_map/all_to_all | solution.py:732
  256.4 1.2 copy-done.3
  257.6 1.6 combine.1
  (63 shorter events, 0.9 us)
Async XLA Ops:
  0.0 15.2 %copy-start = (bf16[16,16,2048]{2,1,0:T(8,128)(2,1)S(1)}, bf16[16,16,2048]{2,1,0:T(8,128)(2,1)}, u32[]{:S(2)}) copy-start(bf16[16,16,2048]{2,1,0:T(8,128)(2,1)} %param.14) | copy-start | bytes 3145732
  0.0 7.2 %copy-start.12 = (bf16[1,256,512]{2,1,0:T(8,128)(2,1)S(1)}, bf16[1,256,512]{2,1,0:T(8,128)(2,1)}, u32[]{:S(2)}) copy-start(bf16[1,256,512]{2,1,0:T(8,128)(2,1)} %param.12) | copy-start | bytes 786436
  0.0 10.9 %copy-start.7 = (bf16[128,1,2,512]{3,2,1,0:T(2,128)(2,1)S(1)}, bf16[128,1,2,512]{3,2,1,0:T(2,128)(2,1)}, u32[]{:S(2)}) copy-start(bf16[128,1,2,512]{3,2,1,0:T(2,128)(2,1)} %param.11) | copy-start | bytes 786436
  2.7 79.7 %all-to-all-start = ((bf16[8,2,128,256]{3,2,1,0:T(8,128)(2,1)}), bf16[8,2,128,256]{3,2,1,0:T(8,128)(2,1)}, u32[]{:S(2)}, u32[]{:S(2)}) async-start(bf16[8,2,128,256]{3,2,1,0:T(8,128)(2,1)} %bitcast.6), calls=%async_computation | async-start | bytes 2097152 | tf_op jit(solution)/shard_map/all_to_all | solution.py:558
  7.2 28.9 %collective-permute-start = (bf16[256,512]{1,0:T(8,128)(2,1)S(1)}, bf16[256,512]{1,0:T(8,128)(2,1)S(1)}, u32[]{:S(2)}, u32[]{:S(2)}) collective-permute-start(bf16[256,512]{1,0:T(8,128)(2,1)S(1)} %bitcast.72), channel_id=1, source_target_pairs={{0,0},{1,1},{2,2},{3,3},{4,8},{5,9},{6,10},{7,11},{8,4},{9,5},{10,... | collective-permute-start | bytes 786440 | tf_op jit(solution)/shard_map/ppermute | solution.py:567
  10.8 25.3 %collective-permute-start.1 = (bf16[256,512]{1,0:T(8,128)(2,1)S(1)}, bf16[256,512]{1,0:T(8,128)(2,1)S(1)}, u32[]{:S(2)}, u32[]{:S(2)}) collective-permute-start(bf16[256,512]{1,0:T(8,128)(2,1)S(1)} %bitcast.73), channel_id=1, source_target_pairs={{0,8},{1,9},{2,10},{3,11},{4,0},{5,1},{6,2},{7,3},{8,12},{9,13},{1... | collective-permute-start | bytes 786440 | tf_op jit(solution)/shard_map/ppermute | solution.py:567
  11.5 18.3 %collective-permute-start.2 = (bf16[128,512]{1,0:T(8,128)(2,1)S(1)}, bf16[128,512]{1,0:T(8,128)(2,1)S(1)}, u32[]{:S(2)}, u32[]{:S(2)}) collective-permute-start(bf16[128,512]{1,0:T(8,128)(2,1)S(1)} %bitcast.65), channel_id=1, source_target_pairs={{0,4},{1,5},{2,6},{3,7},{4,0},{5,1},{6,2},{7,3},{8,12},{9,13},{10,... | collective-permute-start | bytes 393224 | tf_op jit(solution)/shard_map/ppermute | solution.py:539
  12.7 23.4 %collective-permute-start.4 = (bf16[128,512]{1,0:T(8,128)(2,1)S(1)}, bf16[128,512]{1,0:T(8,128)(2,1)S(1)}, u32[]{:S(2)}, u32[]{:S(2)}) collective-permute-start(bf16[128,512]{1,0:T(8,128)(2,1)S(1)} %bitcast.66), channel_id=1, source_target_pairs={{0,12},{1,13},{2,14},{3,15},{4,8},{5,9},{6,10},{7,11},{8,4},{9,5},... | collective-permute-start | bytes 393224 | tf_op jit(solution)/shard_map/ppermute | solution.py:539
  14.2 21.9 %collective-permute-start.3 = (bf16[128,512]{1,0:T(8,128)(2,1)S(1)}, bf16[128,512]{1,0:T(8,128)(2,1)S(1)}, u32[]{:S(2)}, u32[]{:S(2)}) collective-permute-start(bf16[128,512]{1,0:T(8,128)(2,1)S(1)} %bitcast.59), channel_id=1, source_target_pairs={{0,8},{1,9},{2,10},{3,11},{4,12},{5,13},{6,14},{7,15},{8,0},{9,1},... | collective-permute-start | bytes 393224 | tf_op jit(solution)/shard_map/ppermute | solution.py:539
  36.2 18.4 %collective-permute-start.9 = (bf16[4,128,512]{2,1,0:T(8,128)(2,1)S(1)}, bf16[4,128,512]{2,1,0:T(8,128)(2,1)}, u32[]{:S(2)}, u32[]{:S(2)}) collective-permute-start(bf16[4,128,512]{2,1,0:T(8,128)(2,1)S(1)} %pad_maximum_fusion.1.kv_own), channel_id=1, source_target_pairs={{0,2},{1,3},{2,0},{3,1},{4,6},{5,7},{6,4},{7,5},{8,10},{9,11},{10,... | collective-permute-start | bytes 1572872 | tf_op jit(solution)/shard_map/ppermute | solution.py:539
  36.6 17.9 %collective-permute-start.5 = (bf16[2,4,16,1024]{3,2,1,0:T(8,128)(2,1)S(1)}, bf16[2,4,16,1024]{3,2,1,0:T(8,128)(2,1)S(1)}, u32[]{:S(2)}, u32[]{:S(2)}) collective-permute-start(bf16[2,4,16,1024]{3,2,1,0:T(8,128)(2,1)S(1)} %get-tuple-element.28), channel_id=1, source_target_pairs={{0,2},{1,3},{2,0},{3,1},{4,6},{5,7},{6,4},{7,5},{8,10},{9,11},{10,... | collective-permute-start | bytes 786440 | tf_op jit(solution)/shard_map/ppermute | solution.py:539
  37.8 28.0 %collective-permute-start.8 = (bf16[512,512]{1,0:T(8,128)(2,1)S(1)}, bf16[512,512]{1,0:T(8,128)(2,1)}, u32[]{:S(2)}, u32[]{:S(2)}) collective-permute-start(bf16[512,512]{1,0:T(8,128)(2,1)S(1)} %constant_dynamic-update-slice_fusion.page_own), channel_id=1, source_target_pairs={{0,2},{1,3},{2,0},{3,1},{4,6},{5,7},{6,4},{7,5},{8,10},{9,11},{10,... | collective-permute-start | bytes 1572872 | tf_op jit(solution)/shard_map/ppermute | solution.py:539
  54.5 11.3 %collective-permute-start.10 = (bf16[2,4,16,1024]{3,2,1,0:T(8,128)(2,1)S(1)}, bf16[2,4,16,1024]{3,2,1,0:T(8,128)(2,1)S(1)}, u32[]{:S(2)}, u32[]{:S(2)}) collective-permute-start(bf16[2,4,16,1024]{3,2,1,0:T(8,128)(2,1)S(1)} %get-tuple-element.52), channel_id=1, source_target_pairs={{0,4},{1,5},{2,6},{3,7},{4,0},{5,1},{6,2},{7,3},{8,12},{9,13},{10,... | collective-permute-start | bytes 786440 | tf_op jit(solution)/shard_map/ppermute | solution.py:539
  54.5 13.6 %collective-permute-start.6 = (bf16[2,4,16,1024]{3,2,1,0:T(8,128)(2,1)S(1)}, bf16[2,4,16,1024]{3,2,1,0:T(8,128)(2,1)S(1)}, u32[]{:S(2)}, u32[]{:S(2)}) collective-permute-start(bf16[2,4,16,1024]{3,2,1,0:T(8,128)(2,1)S(1)} %bitcast.57), channel_id=1, source_target_pairs={{0,8},{1,9},{2,10},{3,11},{4,12},{5,13},{6,14},{7,15},{8,0},{9,1},... | collective-permute-start | bytes 786440 | tf_op jit(solution)/shard_map/ppermute | solution.py:539
  65.8 16.6 %collective-permute-start.11 = (bf16[512,512]{1,0:T(8,128)(2,1)S(1)}, bf16[512,512]{1,0:T(8,128)(2,1)}, u32[]{:S(2)}, u32[]{:S(2)}) collective-permute-start(bf16[512,512]{1,0:T(8,128)(2,1)S(1)} %constant_dynamic-update-slice_fusion.page_own), channel_id=1, source_target_pairs={{0,1},{1,0},{2,3},{3,2},{4,5},{5,4},{6,7},{7,6},{8,9},{9,8},{10,11... | collective-permute-start | bytes 1572872 | tf_op jit(solution)/shard_map/ppermute | solution.py:539
  67.6 16.5 %collective-permute-start.12 = (bf16[512,512]{1,0:T(8,128)(2,1)}, bf16[512,512]{1,0:T(8,128)(2,1)}, u32[]{:S(2)}, u32[]{:S(2)}) collective-permute-start(bf16[512,512]{1,0:T(8,128)(2,1)} %collective-permute-done.8.page_y), channel_id=1, source_target_pairs={{0,1},{1,0},{2,3},{3,2},{4,5},{5,4},{6,7},{7,6},{8,9},{9,8},{10,11... | collective-permute-start | bytes 1572872 | tf_op jit(solution)/shard_map/ppermute | solution.py:539
  67.6 16.8 %collective-permute-start.13 = (bf16[4,128,512]{2,1,0:T(8,128)(2,1)S(1)}, bf16[4,128,512]{2,1,0:T(8,128)(2,1)}, u32[]{:S(2)}, u32[]{:S(2)}) collective-permute-start(bf16[4,128,512]{2,1,0:T(8,128)(2,1)S(1)} %pad_maximum_fusion.1.kv_own), channel_id=1, source_target_pairs={{0,1},{1,0},{2,3},{3,2},{4,5},{5,4},{6,7},{7,6},{8,9},{9,8},{10,11... | collective-permute-start | bytes 1572872 | tf_op jit(solution)/shard_map/ppermute | solution.py:539
  68.1 16.6 %collective-permute-start.14 = (bf16[4,128,512]{2,1,0:T(8,128)(2,1)}, bf16[4,128,512]{2,1,0:T(8,128)(2,1)}, u32[]{:S(2)}, u32[]{:S(2)}) collective-permute-start(bf16[4,128,512]{2,1,0:T(8,128)(2,1)} %collective-permute-done.9.kv_y), channel_id=1, source_target_pairs={{0,1},{1,0},{2,3},{3,2},{4,5},{5,4},{6,7},{7,6},{8,9},{9,8},{10,11... | collective-permute-start | bytes 1572872 | tf_op jit(solution)/shard_map/ppermute | solution.py:539
  68.1 13.0 %collective-permute-start.7 = (bf16[2,4,16,1024]{3,2,1,0:T(8,128)(2,1)S(1)}, bf16[2,4,16,1024]{3,2,1,0:T(8,128)(2,1)S(1)}, u32[]{:S(2)}, u32[]{:S(2)}) collective-permute-start(bf16[2,4,16,1024]{3,2,1,0:T(8,128)(2,1)S(1)} %get-tuple-element.52), channel_id=1, source_target_pairs={{0,12},{1,13},{2,14},{3,15},{4,8},{5,9},{6,10},{7,11},{8,4},{9,5},... | collective-permute-start | bytes 786440 | tf_op jit(solution)/shard_map/ppermute | solution.py:539
  81.1 17.8 %collective-permute-start.15 = (bf16[2,2,4,16,1024]{4,3,2,1,0:T(8,128)(2,1)S(1)}, bf16[2,2,4,16,1024]{4,3,2,1,0:T(8,128)(2,1)}, u32[]{:S(2)}, u32[]{:S(2)}) collective-permute-start(bf16[2,2,4,16,1024]{4,3,2,1,0:T(8,128)(2,1)S(1)} %pad_maximum_fusion.2.refs_0_), channel_id=1, source_target_pairs={{0,16},{16,0},{1,17},{17,1},{2,18},{18,2},{3,19},{19,3},{4,20},{20... | collective-permute-start | bytes 1572872 | tf_op jit(solution)/shard_map/ppermute | solution.py:539
  82.4 24.3 %collective-permute-start.18 = (bf16[2,2,4,16,1024]{4,3,2,1,0:T(8,128)(2,1)S(1)}, bf16[2,2,4,16,1024]{4,3,2,1,0:T(8,128)(2,1)S(1)}, u32[]{:S(2)}, u32[]{:S(2)}) collective-permute-start(bf16[2,2,4,16,1024]{4,3,2,1,0:T(8,128)(2,1)S(1)} %pad_maximum_fusion.2.refs_0_), channel_id=1, source_target_pairs={{0,1},{1,0},{2,3},{3,2},{4,5},{5,4},{6,7},{7,6},{8,9},{9,8},{10,11... | collective-permute-start | bytes 1572872 | tf_op jit(solution)/shard_map/ppermute | solution.py:539
  84.1 20.3 %collective-permute-start.16 = (bf16[2,2,4,16,1024]{4,3,2,1,0:T(8,128)(2,1)S(1)}, bf16[2,2,4,16,1024]{4,3,2,1,0:T(8,128)(2,1)S(1)}, u32[]{:S(2)}, u32[]{:S(2)}) collective-permute-start(bf16[2,2,4,16,1024]{4,3,2,1,0:T(8,128)(2,1)S(1)} %pad_maximum_fusion.refs_4_), channel_id=1, source_target_pairs={{0,16},{16,0},{1,17},{17,1},{2,18},{18,2},{3,19},{19,3},{4,20},{20... | collective-permute-start | bytes 1572872 | tf_op jit(solution)/shard_map/ppermute | solution.py:539
  84.4 22.3 %collective-permute-start.20 = (bf16[2,2,4,16,1024]{4,3,2,1,0:T(8,128)(2,1)S(1)}, bf16[2,2,4,16,1024]{4,3,2,1,0:T(8,128)(2,1)S(1)}, u32[]{:S(2)}, u32[]{:S(2)}) collective-permute-start(bf16[2,2,4,16,1024]{4,3,2,1,0:T(8,128)(2,1)S(1)} %pad_maximum_fusion.refs_4_), channel_id=1, source_target_pairs={{0,1},{1,0},{2,3},{3,2},{4,5},{5,4},{6,7},{7,6},{8,9},{9,8},{10,11... | collective-permute-start | bytes 1572872 | tf_op jit(solution)/shard_map/ppermute | solution.py:539
  98.6 10.6 %copy-start.5 = (bf16[2,512,512]{2,1,0:T(8,128)(2,1)}, bf16[2,512,512]{2,1,0:T(8,128)(2,1)S(1)}, u32[]{:S(2)}) copy-start(bf16[2,512,512]{2,1,0:T(8,128)(2,1)S(1)} %attend.1.a_ref) | copy-start | bytes 3145732
  98.6 20.7 %copy-start.8 = (s32[128,1,2]{0,2,1:T(2,128)S(1)}, s32[128,1,2]{0,2,1:T(2,128)}, u32[]{:S(2)}) copy-start(s32[128,1,2]{0,2,1:T(2,128)} %param.16) | copy-start | bytes 3076
  98.6 44.3 %copy-start.4 = (bf16[128,1,2048]{2,0,1:T(8,128)(2,1)S(1)}, bf16[128,1,2048]{2,0,1:T(8,128)(2,1)}, u32[]{:S(2)}) copy-start(bf16[128,1,2048]{2,0,1:T(8,128)(2,1)} %param.13) | copy-start | bytes 1572868
  98.6 44.3 %copy-start.6 = (f32[2048]{0:T(1024)S(1)}, f32[2048]{0:T(1024)}, u32[]{:S(2)}) copy-start(f32[2048]{0:T(1024)} %param.15) | copy-start | bytes 24580
  98.6 8.0 %collective-permute-start.17 = (bf16[512,512]{1,0:T(8,128)(2,1)S(1)}, bf16[512,512]{1,0:T(8,128)(2,1)S(1)}, u32[]{:S(2)}, u32[]{:S(2)}) collective-permute-start(bf16[512,512]{1,0:T(8,128)(2,1)S(1)} %slice_bitcast_fusion), channel_id=1, source_target_pairs={{0,1},{1,0},{2,3},{3,2},{4,5},{5,4},{6,7},{7,6},{8,9},{9,8},{10,11... | collective-permute-start | bytes 1572872 | tf_op jit(solution)/shard_map/ppermute | solution.py:539
  104.4 4.8 %copy-start.10 = (bf16[2,2,4,16,1024]{4,3,2,1,0:T(8,128)(2,1)}, bf16[2,2,4,16,1024]{4,3,2,1,0:T(8,128)(2,1)S(1)}, u32[]{:S(2)}) copy-start(bf16[2,2,4,16,1024]{4,3,2,1,0:T(8,128)(2,1)S(1)} %collective-permute-done.16.refs_6_) | copy-start | bytes 1572868
  104.4 4.7 %collective-permute-start.19 = (bf16[2,2,4,16,1024]{4,3,2,1,0:T(8,128)(2,1)}, bf16[2,2,4,16,1024]{4,3,2,1,0:T(8,128)(2,1)S(1)}, u32[]{:S(2)}, u32[]{:S(2)}) collective-permute-start(bf16[2,2,4,16,1024]{4,3,2,1,0:T(8,128)(2,1)} %collective-permute-done.15.refs_2_), channel_id=1, source_target_pairs={{0,1},{1,0},{2,3},{3,2},{4,5},{5,4},{6,7},{7,6},{8,9},{9,8},{10,11... | collective-permute-start | bytes 1572872 | tf_op jit(solution)/shard_map/ppermute | solution.py:539
  106.7 2.5 collective-permute-start.21
  109.1 0.8 copy-start.11
  116.6 14.3 %collective-permute-start.22 = (bf16[128,2048]{1,0:T(8,128)(2,1)}, bf16[128,2048]{1,0:T(8,128)(2,1)S(1)}, u32[]{:S(2)}, u32[]{:S(2)}) collective-permute-start(bf16[128,2048]{1,0:T(8,128)(2,1)} %get-tuple-element.46), channel_id=1, source_target_pairs={{0,6},{1,7},{2,4},{3,5},{4,2},{5,3},{6,0},{7,1},{8,14},{9,15},{10,... | collective-permute-start | bytes 1572872 | tf_op jit(solution)/shard_map/ppermute | solution.py:539
  116.7 25.3 %collective-permute-start.23 = (bf16[128,2048]{1,0:T(8,128)(2,1)}, bf16[128,2048]{1,0:T(8,128)(2,1)S(1)}, u32[]{:S(2)}, u32[]{:S(2)}) collective-permute-start(bf16[128,2048]{1,0:T(8,128)(2,1)} %get-tuple-element.47), channel_id=1, source_target_pairs={{0,4},{1,5},{2,6},{3,7},{4,0},{5,1},{6,2},{7,3},{8,12},{9,13},{10,... | collective-permute-start | bytes 1572872 | tf_op jit(solution)/shard_map/ppermute | solution.py:539
  118.7 24.2 %collective-permute-start.24 = (bf16[128,2048]{1,0:T(8,128)(2,1)}, bf16[128,2048]{1,0:T(8,128)(2,1)}, u32[]{:S(2)}, u32[]{:S(2)}) collective-permute-start(bf16[128,2048]{1,0:T(8,128)(2,1)} %get-tuple-element.48), channel_id=1, source_target_pairs={{0,2},{1,3},{2,0},{3,1},{4,6},{5,7},{6,4},{7,5},{8,10},{9,11},{10,... | collective-permute-start | bytes 1572872 | tf_op jit(solution)/shard_map/ppermute | solution.py:539
  145.1 51.5 %copy-start.2 = (f32[128,2048]{1,0:T(8,128)}, f32[128,2048]{1,0:T(8,128)S(1)}, u32[]{:S(2)}) copy-start(f32[128,2048]{1,0:T(8,128)S(1)} %get-tuple-element.50.stream_ref) | copy-start | bytes 3145732
  202.3 1.4 copy-start.1
  203.7 5.3 %copy-start.9 = (f32[128,1,2]{0,2,1:T(2,128)S(1)}, f32[128,1,2]{0,2,1:T(2,128)}, u32[]{:S(2)}) copy-start(f32[128,1,2]{0,2,1:T(2,128)} %param.17) | copy-start | bytes 3076
  203.7 52.7 %all-to-all-start.2 = ((bf16[16,32,2048]{2,1,0:T(8,128)(2,1)}), bf16[16,32,2048]{2,1,0:T(8,128)(2,1)S(1)}, u32[]{:S(2)}, u32[]{:S(2)}) async-start(bf16[16,32,2048]{2,1,0:T(8,128)(2,1)} %bitcast.46), calls=%async_computation.2 | async-start | bytes 4194304 | tf_op jit(solution)/shard_map/all_to_all | solution.py:732
  256.4 1.2 copy-start.3

commit v12 on v11

--- a/solution.py
+++ b/solution.py
@@ -133,7 +133,8 @@
     chunk,
     width,
     q_hbm,
-    page_own,
+    page_a,
+    page_b,
     page_y,
     page_c,
     page_cy,
@@ -168,7 +169,7 @@
         for head in range(heads):
             bring(q_hbm.at[member, head], q_ref.at[head, pl.ds(member * piece, piece)], 0)
     place = 0
-    for page in (page_own, page_y, page_c, page_cy):
+    for page in (page_a, page_b, page_y, page_c, page_cy):
         count = page.shape[0]
         bring(page, old_ref.at[pl.ds(place, count)], 1)
         place += count
@@ -280,27 +281,26 @@
 
 
 def project_pair_kernel(a_ref, got_ref, *refs):
-    near, far, outs, (w_ref, sems) = refs[:4], refs[4:8], refs[8:-2], refs[-2:]
+    given, outs, (w_ref, sems) = refs[:4], refs[4:-2], refs[-2:]
     me = lax.axis_index("head")
     half = lax.axis_index("grp")
     core = lax.rem(me, 2)
-    steps, sides, heads, share, columns = near[0].shape
+    planes, sides, heads, share, columns = given[0].shape
     width = w_ref.shape[1]
     copies = []
-    for first, given in ((0, near), (steps, far)):
-        for flip, x, pieces_of in zip((0, 1, 0, 1), (0, 0, 1, 1), given):
-            column = pl.multiple_of(jnp.bitwise_xor(half, x) * columns, columns)
-            for t in range(steps):
-                for u in range(sides):
-                    number = jnp.bitwise_xor(me, flip ^ (2 * u) ^ (4 * (first + t)))
-                    row = pl.multiple_of(number * share, share)
-                    copy = pltpu.make_async_copy(
-                        pieces_of.at[t, u],
-                        w_ref.at[:, pl.ds(row, share), pl.ds(column, columns)],
-                        sems.at[0],
-                    )
-                    copy.start()
-                    copies.append(copy)
+    for flip, x, pieces_of in zip((0, 1, 0, 1), (0, 0, 1, 1), given):
+        column = pl.multiple_of(jnp.bitwise_xor(half, x) * columns, columns)
+        for t in range(planes):
+            for u in range(sides):
+                number = jnp.bitwise_xor(me, flip ^ (2 * u) ^ (4 * t))
+                row = pl.multiple_of(number * share, share)
+                copy = pltpu.make_async_copy(
+                    pieces_of.at[t, u],
+                    w_ref.at[:, pl.ds(row, share), pl.ds(column, columns)],
+                    sems.at[0],
+                )
+                copy.start()
+                copies.append(copy)
     for copy in copies:
         copy.wait()
     acc = None
@@ -316,15 +316,15 @@
         out[...] = acc[k * rows : (k + 1) * rows].astype(BF16)
 
 
-def project_pair(a, got, near, far, parts):
-    _, _, heads, share, columns = near[0].shape
+def project_pair(a, got, given, parts):
+    _, _, heads, share, columns = given[0].shape
     rows = got.shape[0]
     width = 2 * got.shape[1] // heads
     model = 2 * columns
     return pl.pallas_call(
         project_pair_kernel,
         out_shape=[jax.ShapeDtypeStruct((rows // parts, model), BF16)] * parts,
-        in_specs=[in_vmem(), in_vmem()] + [in_hbm()] * 8,
+        in_specs=[in_vmem(), in_vmem()] + [in_hbm()] * 4,
         out_specs=[in_vmem()] * parts,
         scratch_shapes=[
             pltpu.VMEM((heads, width, model), BF16),
@@ -337,7 +337,7 @@
             transcendentals=0,
         ),
         name="project",
-    )(a, got, *near, *far)
+    )(a, got, *given)
 
 
 def project_kernel(a_ref, w_ref, o_ref):
@@ -534,12 +534,138 @@
     )(back, stream, slots_of, gates)
 
 
+def slot_matrix(slots_ref, slots, rows):
+    place = lax.broadcasted_iota(jnp.int32, (slots, rows), 0).astype(F32)
+    hit = place == slots_ref[0:1, :]
+    for k in range(1, slots_ref.shape[0]):
+        hit = hit | (place == slots_ref[k : k + 1, :])
+    return hit.astype(BF16)
+
+
+def by_copies(body, name, inputs, outputs, flops, bytes_accessed, transcendentals=0):
+    count = len(inputs)
+
+    def kernel(*refs):
+        ins, outs = refs[:count], refs[count : count + len(outputs)]
+        rest = refs[count + len(outputs) :]
+        in_vm, out_vm, sems = rest[:count], rest[count:-1], rest[-1]
+        copies = [
+            pltpu.make_async_copy(ins[k], in_vm[k], sems.at[k]) for k in range(count)
+        ]
+        for copy in copies:
+            copy.start()
+        body(lambda k: copies[k].wait(), in_vm, out_vm)
+        back = [
+            pltpu.make_async_copy(out_vm[k], outs[k], sems.at[count + k])
+            for k in range(len(outputs))
+        ]
+        for copy in back:
+            copy.start()
+        for copy in back:
+            copy.wait()
+
+    shapes = [jax.ShapeDtypeStruct(shape, dtype) for shape, dtype in outputs]
+    return pl.pallas_call(
+        kernel,
+        out_shape=shapes,
+        in_specs=[in_hbm()] * count,
+        out_specs=[in_hbm()] * len(outputs),
+        scratch_shapes=[pltpu.VMEM(x.shape, x.dtype) for x in inputs]
+        + [pltpu.VMEM(shape, dtype) for shape, dtype in outputs]
+        + [pltpu.SemaphoreType.DMA((count + len(outputs),))],
+        compiler_params=pltpu.CompilerParams(vmem_limit_bytes=HIGH_VMEM),
+        cost_estimate=pl.CostEstimate(
+            flops=flops, bytes_accessed=bytes_accessed, transcendentals=transcendentals
+        ),
+        name=name,
+    )(*inputs)
+
+
+def join_pair(parts, resid, gain):
+    rows, model = resid.shape
+    count = len(parts)
+
+    def body(wait, ins, outs):
+        wait(0)
+        total = ins[0][...].astype(F32)
+        for k in range(1, count):
+            wait(k)
+            total = total + ins[k][...].astype(F32)
+        wait(count)
+        stream = ins[count][...].astype(F32) + total
+        outs[0][...] = stream
+        normed = stream * lax.rsqrt(jnp.mean(stream * stream, 1, keepdims=True) + eps_norm)
+        wait(count + 1)
+        outs[1][...] = (normed * ins[count + 1][...]).astype(BF16)
+
+    return by_copies(
+        body,
+        "join",
+        list(parts) + [resid, gain],
+        [((rows, model), F32), ((rows, model), BF16)],
+        8 * rows * model,
+        2 * (count + 4) * rows * model,
+    )
+
+
+def spread(given, slots_of, slots, which):
+    rows, model = given.shape[-2:]
+
+    def body(wait, ins, outs):
+        wait(1)
+        matrix = slot_matrix(ins[1], slots, rows)
+        wait(0)
+        chosen = ins[0][...] if which is None else ins[0][which()]
+        outs[0][...] = jnp.dot(matrix, chosen, preferred_element_type=F32).astype(BF16)
+
+    return by_copies(
+        body,
+        "spread",
+        [given, slots_of],
+        [((slots, model), BF16)],
+        2 * slots * rows * model,
+        2 * (rows + slots) * model,
+    )[0]
+
+
+def gather(back, slots_of, gates, stream, partial, which):
+    slots, model = back.shape
+    rows, top = slots_of.shape
+    more = [] if stream is None else [stream, partial]
+
+    def body(wait, ins, outs):
+        back_ref, slots_ref, gates_ref = ins[:3]
+        for k in (1, 2, 0):
+            wait(k)
+        place = lax.broadcasted_iota(jnp.int32, (rows, slots), 1).astype(F32)
+        total = None
+        for k in range(top):
+            pick = (place == slots_ref[:, k : k + 1]).astype(BF16)
+            picked = jnp.dot(pick, back_ref[...], preferred_element_type=F32)
+            part = picked * gates_ref[:, k : k + 1]
+            total = part if total is None else total + part
+        if more:
+            wait(3)
+            wait(4)
+            total = ins[3][...] + (total + ins[4][which()].astype(F32))
+        outs[0][...] = total.astype(BF16)
+
+    return by_copies(
+        body,
+        "gather",
+        [back, slots_of, gates] + more,
+        [((rows, model), BF16)],
+        2 * top * slots * rows * model,
+        2 * (slots + 4 * rows) * model,
+    )[0]
+
+
 def flipped(value, axis, mask):
     pairs = [(source, source ^ mask) for source in range(lax.axis_size(axis))]
     return lax.ppermute(value, axis, pairs)
 
 
-def parts_in_pairs(queries, new_kv, cache, w_out):
+def parts_in_pairs(queries, new_kv, cache, w_out, other):
     n = lax.axis_size("head")
     local_rows, _, heads, width = queries.shape
     pair_heads = new_kv.shape[2]
@@ -570,56 +696,48 @@
     kv_heads = new_kv.reshape(local_rows, pair_heads, 2 * width).transpose(1, 0, 2)
     kv_same = lax.dynamic_index_in_dim(kv_heads, b, 0, keepdims=False)
     kv_other = lax.dynamic_index_in_dim(kv_heads, 1 - b, 0, keepdims=False)
+    kv_own = [kv_same]
+    for t in range(1, planes):
+        kv_own.append(flipped(kv_other if t % 2 else kv_same, "head", t * plane_bit))
+
     columns = model // 2
     w = lax.dynamic_slice_in_dim(w_out, lax.axis_index("grp") * columns, columns, 2)
     w = w.reshape(2, 2, heads // 4, share, columns)
     w_keep = lax.dynamic_index_in_dim(w, y, 1, keepdims=False)
     w_give = lax.dynamic_index_in_dim(w, 1 - y, 1, keepdims=False)
-    kv_own = [kv_same]
-    for t in range(1, planes):
-        kv_own.append(flipped(kv_other if t % 2 else kv_same, "head", t * plane_bit))
-
-    (page_a, page_b, kv_own), w_give = lax.optimization_barrier(
-        ((page_a, page_b, kv_own), w_give)
+    w_got = flipped(w_give, "head", 2)
+
+    (page_a, page_b, kv_own, q), w_got = lax.optimization_barrier(
+        ((page_a, page_b, kv_own, q), w_got)
     )
     own_pages = jnp.concatenate([page_a, page_b], 0)
     kv_own = jnp.stack(kv_own, 0)
     pages_y = flipped(own_pages, "head", 2)
     kv_y = flipped(kv_own, "head", 2)
-    w_got = flipped(w_give, "head", 2)
     w_both = jnp.stack([w_keep, w_got], 1)
     w_same = lax.dynamic_index_in_dim(w_both, b, 0, keepdims=False)
     w_other = lax.dynamic_index_in_dim(w_both, 1 - b, 0, keepdims=False)
-    w_first = flipped(w_other, "head", plane_bit)
-    w_far = [flipped(w_same, "head", 2 * plane_bit), flipped(w_other, "head", 3 * plane_bit)]
-    pages_y, kv_y, own_pages, kv_own, w_first = lax.optimization_barrier(
-        (pages_y, kv_y, own_pages, kv_own, w_first)
-    )
+    w_own = [w_same]
+    for t in range(1, planes):
+        w_own.append(flipped(w_other if t % 2 else w_same, "head", t * plane_bit))
+    pages_c = flipped(own_pages, "head", 1)
     kv_c = flipped(kv_own, "head", 1)
+    (pages_y, kv_y), w_own = lax.optimization_barrier(((pages_y, kv_y), w_own))
+    pages_cy = flipped(pages_y, "head", 1)
     kv_cy = flipped(kv_y, "head", 1)
-    pages_c = flipped(own_pages, "head", 1)
-    pages_cy = flipped(pages_y, "head", 1)
-    w_near = jnp.stack([w_same, w_first], 0)
-    w_near_x = flipped(w_near, "grp", 1)
-    w_far = jnp.stack(w_far, 0)
-    q, w_far = lax.optimization_barrier((q, w_far))
-    w_far_x = flipped(w_far, "grp", 1)
-    a = attend_pair(q, (own_pages, pages_y, pages_c, pages_cy), (kv_own, kv_y, kv_c, kv_cy))
+    w_own = jnp.stack(w_own, 0)
+    q, w_own = lax.optimization_barrier((q, w_own))
+    w_x = flipped(w_own, "grp", 1)
+    w_c = flipped(w_own, "head", 1)
+    a = attend_pair(
+        q, (page_a, page_b, pages_y, pages_c, pages_cy), (kv_own, kv_y, kv_c, kv_cy)
+    )
     got = flipped(a[1], "head", 1)
-    a, w_near_x, w_far_x = lax.optimization_barrier((a, w_near_x, w_far_x))
-    w_near_c = flipped(w_near, "head", 1)
-    w_far_c = flipped(w_far, "head", 1)
-    w_near_cx = flipped(w_near_x, "head", 1)
-    w_far_cx = flipped(w_far_x, "head", 1)
-    partial = project_pair(
-        a,
-        got,
-        (w_near, w_near_c, w_near_x, w_near_cx),
-        (w_far, w_far_c, w_far_x, w_far_cx),
-        members // 2,
-    )
+    a, w_x, w_c, other = lax.optimization_barrier((a, w_x, w_c, other))
+    w_cx = flipped(w_x, "head", 1)
+    partial = project_pair(a, got, (w_own, w_c, w_x, w_cx), members // 2)
     parts = [partial[0]] + [flipped(partial[k], "head", 2 * k) for k in (3, 2, 1)]
-    return [part[None] for part in parts]
+    return parts, other
 
 
 def parts_in_planes(queries, new_kv, cache, w_out):
@@ -683,6 +801,45 @@
     return [parts[:, k] for k in range(planes_of_seq)]
 
 
+def route_in_pairs(parts, resid, norm_gain, own, other, top, w_in, w_down, capacity, members):
+    n = lax.axis_size("head")
+    local_rows, seqs, model = resid.shape
+    me = lax.axis_index("head")
+    group_sets = [[g * members + m for m in range(members)] for g in range(n // members)]
+    couples = [[m, m + members] for m in range(members)]
+    group_slots = members * capacity
+
+    def around(value):
+        value = value.reshape(members, capacity, model)
+        value = lax.all_to_all(
+            value, "head", split_axis=0, concat_axis=0, tiled=True, axis_index_groups=group_sets
+        )
+        return value.reshape(group_slots, model)
+
+    def across(value):
+        return lax.all_gather(value, "head", axis=0, axis_index_groups=couples)
+
+    def other_group():
+        return 1 - lax.axis_index("head") // members
+
+    first = ((me // members) * group_slots).astype(F32)
+    slots_own, gates_own = own[:, :top] - first, own[:, top:]
+    slots_other, gates_other = other[:, :top] - first, other[:, top:]
+
+    stream, normed = join_pair(parts, resid.reshape(local_rows, model), norm_gain[None, :])
+    both = across(normed)
+    arrived_own = around(spread(normed, slots_own.T, group_slots, None))
+    both, arrived_own = lax.optimization_barrier((both, arrived_own))
+    answer_own = expert_pair(arrived_own, w_in, w_down)
+    out_other = spread(both, slots_other.T, group_slots, other_group)
+    answer_other = expert_pair(around(out_other), w_in, w_down)
+    partial = gather(around(answer_other), slots_other, gates_other, None, None, None)
+    partial, answer_own = lax.optimization_barrier((partial, answer_own))
+    sums = across(partial)
+    out = gather(around(answer_own), slots_own, gates_own, stream, sums, other_group)
+    return out.reshape(local_rows, seqs, model)
+
+
 def local(queries, new_kv, cache, resid, w_out, norm_gain, expert_ids, expert_gates, w_in, w_down):
     n = lax.axis_size("head")
     local_rows, seqs, heads, width = queries.shape
@@ -699,8 +856,6 @@
         and w_in.shape[0] == 1
         and w_out.shape[1] % 16 == 0
     )
-    plan = parts_in_pairs if in_pairs else parts_in_planes
-    parts = plan(queries, new_kv, cache, w_out)
 
     top = expert_ids.shape[2]
     experts = w_in.shape[0] * n
@@ -712,7 +867,14 @@
     before = jnp.cumsum(named, 0) - named
     slots_of = ids * capacity + jnp.sum(onehot * before[:, None, :], 2)
     slots = experts * capacity
-
+    if in_pairs:
+        own = jnp.concatenate([slots_of.astype(F32), gates], 1)
+        other = flipped(own, "head", members)
+        parts, other = parts_in_pairs(queries, new_kv, cache, w_out, other)
+        return route_in_pairs(
+            parts, resid, norm_gain, own, other, top, w_in[0], w_down[0], capacity, members
+        )
+    parts = parts_in_planes(queries, new_kv, cache, w_out)
     stream, outgoing = route(
         parts, resid.transpose(1, 0, 2), norm_gain[None, :], slots_of.T, slots
     )

time: 260 us -> 284 us (1.092); the launches traced: 259 us -> 279 us
  blocking collectives: 51.5 us -> 19 us
  between operations: 0.4 us -> 13.7 us
  local copies, waits for them, and re-layouts: 7.45 us -> 20.2 us
  starting transfers between devices: 30.2 us -> 42.4 us
  other arithmetic: 0.45 us -> 7.08 us
  Pallas kernels: 29.9 us -> 35.2 us
    all_gather x0 -> x2, waiting for transfers between devices: none -> 64.8 us  [across(): return lax.all_gather(value, 'head', axis=0, axis_index_groups=couples)]
    all_to_all x1 -> x3, waiting for transfers between devices: 47.3 us -> 7.49 us  [around(): lax.all_to_all(value, 'head', split_axis=0, concat_axis=0, tiled=True, ax...]
    all_to_all x1, blocking collectives: 51.5 us -> 19 us  [around(): lax.all_to_all(value, 'head', split_axis=0, concat_axis=0, tiled=True, ax...]
    ppermute x23 -> x21, waiting for transfers between devices: 91.9 us -> 67.5 us  [flipped(): return lax.ppermute(value, axis, pairs)]
    all_to_all x1 -> x3, starting transfers between devices: 5.25 us -> 16.4 us  [around(): lax.all_to_all(value, 'head', split_axis=0, concat_axis=0, tiled=True, ax...]
    unnamed x31 -> x63, local copies, waits for them, and re-layouts: 3.71 us -> 14.4 us
    pallas_call x2 -> x5, Pallas kernels: 3.77 us -> 7.43 us  [by_copies(): pl.pallas_call(kernel, out_shape=shapes, in_specs=[in_hbm()] * count, out...]
    pallas_call x1 -> x2, Pallas kernels: 5.69 us -> 7.9 us  [expert_pair(): pl.pallas_call(kernel, out_shape=jax.ShapeDtypeStruct((rows, model), BF16...]
  transfers between devices with their start and end apart: 27 -> 29, of which waited for: 11 -> 14; matrix products, arithmetic and copies ran while one was open for 1% -> 3% of each run, Pallas kernels for 5% -> 7%
where the time goes in v12:
time: 284 us; the launch traced here: 279 us
  waiting for transfers between devices  141 us (50%)
  starting transfers between devices  42.4 us (15%)
  Pallas kernels  35.2 us (12%)
  local copies, waits for them, and re-layouts  20.2 us (7%)
  blocking collectives  19 us (7%)
  between operations  13.7 us (5%)
  other arithmetic  7.08 us (2%)
    ppermute x21, waiting for transfers between devices, flipped(): return lax.ppermute(value, axis, pairs)  67.5 us
    all_gather x2, waiting for transfers between devices, across(): return lax.all_gather(value, 'head', axis=0, axis_index_groups=couples)  64.8 us
    all_to_all x1, blocking collectives, around(): lax.all_to_all(value, 'head', split_axis=0, concat_axis=0, tiled=True, ax...  19 us
    ppermute x21, starting transfers between devices, flipped(): return lax.ppermute(value, axis, pairs)  16.8 us
    all_to_all x3, starting transfers between devices, around(): lax.all_to_all(value, 'head', split_axis=0, concat_axis=0, tiled=True, ax...  16.4 us
    unnamed x63, local copies, waits for them, and re-layouts  14.4 us
    pallas_call x1, Pallas kernels, attend_pair(): pl.pallas_call(functools.partial(attend_pair_kernel, block, chunk, width)...  14.2 us
    pallas_call x2, Pallas kernels, expert_pair(): pl.pallas_call(kernel, out_shape=jax.ShapeDtypeStruct((rows, model), BF16...  7.9 us
  transfers between devices with their start and end apart: 29, of which 14 were waited for; matrix products, arithmetic and copies ran while one was open for 3% of the time, Pallas kernels for 7%

profile of v12, /device:TPU:13, one launch (start us, length us, event | category | flops | bytes accessed | tf_op | source)
XLA Modules:
  0.0 278.9 jit_solution(4098983643629694732)
XLA Ops:
  6.5 2.7 copy.35
  9.2 4.6 %all-to-all-start = ((bf16[8,2,128,256]{3,2,1,0:T(8,128)(2,1)}), bf16[8,2,128,256]{3,2,1,0:T(8,128)(2,1)S(1)}, u32[]{:S(2)}, u32[]{:S(2)}) async-start(bf16[8,2,128,256]{3,2,1,0:T(8,128)(2,1)} %bitcast.5), calls=%async_computation | async-start | bytes 2097152 | tf_op jit(solution)/shard_map/all_to_all | solution.py:684
  15.7 4.4 %collective-permute-start = (bf16[256,512]{1,0:T(8,128)(2,1)}, bf16[256,512]{1,0:T(8,128)(2,1)S(1)}, u32[]{:S(2)}, u32[]{:S(2)}) collective-permute-start(bf16[256,512]{1,0:T(8,128)(2,1)} %bitcast), channel_id=1, source_target_pairs={{0,0},{1,1},{2,2},{3,3},{4,8},{5,9},{6,10},{7,11},{8,4},{9,5},{10,... | collective-permute-start | bytes 786440 | tf_op jit(solution)/shard_map/ppermute | solution.py:693
  20.2 2.4 collective-permute-start.3
  22.6 8.3 %collective-permute-done.2 = bf16[128,512]{1,0:T(8,128)(2,1)S(1)} collective-permute-done((bf16[128,512]{1,0:T(8,128)(2,1)S(1)}, bf16[128,512]{1,0:T(8,128)(2,1)S(1)}, u32[]{:S(2)}, u32[]{:S(2)}) %collective-permute-start.2) | collective-permute-done | bytes 131104 | tf_op jit(solution)/shard_map/ppermute | solution.py:665
  31.9 7.8 %collective-permute-done.3 = bf16[128,512]{1,0:T(8,128)(2,1)S(1)} collective-permute-done((bf16[128,512]{1,0:T(8,128)(2,1)S(1)}, bf16[128,512]{1,0:T(8,128)(2,1)S(1)}, u32[]{:S(2)}, u32[]{:S(2)}) %collective-permute-start.3) | collective-permute-done | bytes 131104 | tf_op jit(solution)/shard_map/ppermute | solution.py:665
  39.7 6.0 %collective-permute-done.4 = bf16[128,512]{1,0:T(8,128)(2,1)S(1)} collective-permute-done((bf16[128,512]{1,0:T(8,128)(2,1)S(1)}, bf16[128,512]{1,0:T(8,128)(2,1)S(1)}, u32[]{:S(2)}, u32[]{:S(2)}) %collective-permute-start.4) | collective-permute-done | bytes 131104 | tf_op jit(solution)/shard_map/ppermute | solution.py:665
  46.4 2.1 fusion.1
  48.4 1.1 pad_maximum_fusion.1.kv_own
  51.3 1.2 collective-permute-start.6
  52.5 1.1 collective-permute-start.13
  53.8 7.5 %collective-permute-done.10 = bf16[2,4,16,1024]{3,2,1,0:T(8,128)(2,1)S(1)} collective-permute-done((bf16[2,4,16,1024]{3,2,1,0:T(8,128)(2,1)}, bf16[2,4,16,1024]{3,2,1,0:T(8,128)(2,1)S(1)}, u32[]{:S(2)}, u32[]{:S(2)}) %collective-permute-start.10) | collective-permute-done | bytes 262176 | tf_op jit(solution)/shard_map/ppermute | solution.py:665
  64.9 8.5 %collective-permute-done.9 = bf16[2,4,16,1024]{3,2,1,0:T(8,128)(2,1)} collective-permute-done((bf16[2,4,16,1024]{3,2,1,0:T(8,128)(2,1)S(1)}, bf16[2,4,16,1024]{3,2,1,0:T(8,128)(2,1)}, u32[]{:S(2)}, u32[]{:S(2)}) %collective-permute-start.9) | collective-permute-done | bytes 262176 | tf_op jit(solution)/shard_map/ppermute | solution.py:665
  73.8 1.4 collective-permute-start.12
  76.1 1.2 pad_maximum_fusion.refs_0_
  77.3 1.3 collective-permute-start.15
  80.4 2.3 collective-permute-start.17
  82.7 1.0 copy-done.14
  83.7 1.0 copy-done.16
  84.8 14.2 %attend.1.a_ref = bf16[2,512,512]{2,1,0:T(8,128)(2,1)S(1)} custom-call(bf16[8,2,128,256]{3,2,1,0:T(8,128)(2,1)} %copy-done.18, bf16[256,512]{1,0:T(8,128)(2,1)S(1)} %collective-permute-done.page_a, bf16[256,512]{1,0:T(8,128)(2,1)S(1)} %collective-permute-done.1.page_b, bf16[512,512]{1,0:T(8,128)(2,1)S(1)} %copy-done.16, ...), custom_call_target="tpu_custom_call" | custom-call | flops 7516192768 | bytes 6291456 | tf_op jit(solution)/shard_map/attend/pallas_call | solution.py:260
  99.0 2.6 collective-permute-done.15.refs_2_
  101.6 1.4 collective-permute-start.19
  103.1 2.9 %collective-permute-done.18.got_ref = bf16[512,512]{1,0:T(8,128)(2,1)S(1)} collective-permute-done((bf16[512,512]{1,0:T(8,128)(2,1)S(1)}, bf16[512,512]{1,0:T(8,128)(2,1)S(1)}, u32[]{:S(2)}, u32[]{:S(2)}) %collective-permute-start.18) | collective-permute-done | bytes 524320 | tf_op jit(solution)/shard_map/ppermute | solution.py:665
  106.0 1.0 copy-done.28
  107.0 5.7 %project.1 = (bf16[128,2048]{1,0:T(8,128)(2,1)S(1)}, bf16[128,2048]{1,0:T(8,128)(2,1)}, bf16[128,2048]{1,0:T(8,128)(2,1)}, bf16[128,2048]{1,0:T(8,128)(2,1)}) custom-call(bf16[2,512,512]{2,1,0:T(8,128)(2,1)S(1)} %attend.1.a_ref, bf16[512,512]{1,0:T(8,128)(2,1)S(1)} %collective-permute-done.18.got_ref, ...), custom_call_target="tpu_custom_call" | custom-call | flops 2147483648 | bytes 7340032 | tf_op jit(solution)/shard_map/project/pallas_call | solution.py:324
  113.2 1.1 collective-permute-start.21
  114.2 1.2 collective-permute-start.22
  115.5 11.6 %collective-permute-done.20.refs_1_ = bf16[128,2048]{1,0:T(8,128)(2,1)S(1)} collective-permute-done((bf16[128,2048]{1,0:T(8,128)(2,1)}, bf16[128,2048]{1,0:T(8,128)(2,1)S(1)}, u32[]{:S(2)}, u32[]{:S(2)}) %collective-permute-start.20) | collective-permute-done | bytes 524320 | tf_op jit(solution)/shard_map/ppermute | solution.py:665
  127.0 10.4 %collective-permute-done.21.refs_2_ = bf16[128,2048]{1,0:T(8,128)(2,1)S(1)} collective-permute-done((bf16[128,2048]{1,0:T(8,128)(2,1)}, bf16[128,2048]{1,0:T(8,128)(2,1)S(1)}, u32[]{:S(2)}, u32[]{:S(2)}) %collective-permute-start.21) | collective-permute-done | bytes 524320 | tf_op jit(solution)/shard_map/ppermute | solution.py:665
  137.5 1.6 collective-permute-done.22.refs_3_
  139.1 1.8 join.1
  141.7 1.0 copy-done.8
  142.7 1.0 copy-done.6
  144.3 1.0 copy-done.2
  145.3 5.0 %all-to-all-start.1 = ((bf16[8,32,2048]{2,1,0:T(8,128)(2,1)}), bf16[8,32,2048]{2,1,0:T(8,128)(2,1)}, u32[]{:S(2)}, u32[]{:S(2)}) async-start(bf16[8,32,2048]{2,1,0:T(8,128)(2,1)} %bitcast.52), calls=%async_computation.1 | async-start | bytes 2097152 | tf_op jit(solution)/shard_map/all_to_all | solution.py:814
  151.2 32.9 %all-gather.5.cloned.1.call-done = bf16[256,2048]{1,0:T(8,128)(2,1)} async-done(((bf16[128,2048]{1,0:T(8,128)(2,1)}), bf16[256,2048]{1,0:T(8,128)(2,1)}) %all-gather.5.cloned.1.call-update) | async-done | bytes 1048592 | tf_op jit(solution)/shard_map/all_gather | solution.py:820
  184.1 1.2 copy-done.7
  186.0 19.0 %all_to_all.25 = bf16[8,32,2048]{2,1,0:T(8,128)(2,1)S(1)} all-to-all(bf16[8,32,2048]{2,1,0:T(8,128)(2,1)S(1)} %bitcast.53), channel_id=1, replica_groups={{0,1,2,3,4,5,6,7},{8,9,10,11,12,13,14,15},{16,17,18,19,20,21,22,23},{24..., dimensions={0} | all-to-all | bytes 2097152 | tf_op jit(solution)/shard_map/all_to_all | solution.py:814
  205.0 3.8 %expert.2 = bf16[256,2048]{1,0:T(8,128)(2,1)S(1)} custom-call(bf16[256,2048]{1,0:T(8,128)(2,1)S(1)} %bitcast.57, bf16[2048,1024]{1,0:T(8,128)(2,1)} %bitcast.66, bf16[512,2048]{1,0:T(8,128)(2,1)S(1)} %bitcast.50), custom_call_target="tpu_custom_call" | custom-call | flops 1610612736 | bytes 8388608 | tf_op jit(solution)/shard_map/expert/pallas_call | solution.py:479
  209.8 6.0 %all-to-all-start.3 = ((bf16[8,32,2048]{2,1,0:T(8,128)(2,1)}), bf16[8,32,2048]{2,1,0:T(8,128)(2,1)}, u32[]{:S(2)}, u32[]{:S(2)}) async-start(bf16[8,32,2048]{2,1,0:T(8,128)(2,1)} %bitcast.56), calls=%async_computation.3 | async-start | bytes 2097152 | tf_op jit(solution)/shard_map/all_to_all | solution.py:814
  215.7 4.1 %expert.3 = bf16[256,2048]{1,0:T(8,128)(2,1)S(1)} custom-call(bf16[256,2048]{1,0:T(8,128)(2,1)} %bitcast.27.x_hbm, bf16[2048,1024]{1,0:T(8,128)(2,1)} %bitcast.67, bf16[512,2048]{1,0:T(8,128)(2,1)S(1)} %bitcast.51), custom_call_target="tpu_custom_call" | custom-call | flops 1610612736 | bytes 8388608 | tf_op jit(solution)/shard_map/expert/pallas_call | solution.py:479
  219.8 1.0 copy-done.3
  220.8 7.5 %all-to-all-done.3 = bf16[8,32,2048]{2,1,0:T(8,128)(2,1)} async-done(((bf16[8,32,2048]{2,1,0:T(8,128)(2,1)}), bf16[8,32,2048]{2,1,0:T(8,128)(2,1)}, u32[]{:S(2)}, u32[]{:S(2)}) %all-to-all-start.3) | async-done | bytes 1048608 | tf_op jit(solution)/shard_map/all_to_all | solution.py:814
  228.3 2.5 gather.2
  230.9 5.5 %all-to-all-start.4 = ((bf16[8,32,2048]{2,1,0:T(8,128)(2,1)}), bf16[8,32,2048]{2,1,0:T(8,128)(2,1)S(1)}, u32[]{:S(2)}, u32[]{:S(2)}) async-start(bf16[8,32,2048]{2,1,0:T(8,128)(2,1)} %bitcast.55), calls=%async_computation.4 | async-start | bytes 2097152 | tf_op jit(solution)/shard_map/all_to_all | solution.py:814
  237.1 31.9 %all-gather.7.cloned.1.call-done = bf16[256,2048]{1,0:T(8,128)(2,1)} async-done(((bf16[128,2048]{1,0:T(8,128)(2,1)}), bf16[256,2048]{1,0:T(8,128)(2,1)}) %all-gather.7.cloned.1.call-update) | async-done | bytes 1048592 | tf_op jit(solution)/shard_map/all_gather | solution.py:820
  269.0 1.2 copy-done.10
  270.2 1.9 gather.3
  (107 shorter events, 17.4 us)
Async XLA Ops:
  6.5 7.3 %copy-start = (bf16[16,16,2048]{2,1,0:T(8,128)(2,1)S(1)}, bf16[16,16,2048]{2,1,0:T(8,128)(2,1)}, u32[]{:S(2)}) copy-start(bf16[16,16,2048]{2,1,0:T(8,128)(2,1)} %param.14) | copy-start | bytes 3145732
  6.5 8.4 %copy-start.17 = (bf16[128,1,2,512]{3,2,1,0:T(2,128)(2,1)S(1)}, bf16[128,1,2,512]{3,2,1,0:T(2,128)(2,1)}, u32[]{:S(2)}) copy-start(bf16[128,1,2,512]{3,2,1,0:T(2,128)(2,1)} %param.11) | copy-start | bytes 786436
  9.2 52.7 %copy-start.25 = (s32[128,1,2]{0,2,1:T(2,128)S(1)}, s32[128,1,2]{0,2,1:T(2,128)}, u32[]{:S(2)}) copy-start(s32[128,1,2]{0,2,1:T(2,128)} %param.16) | copy-start | bytes 3076
  9.2 37.1 %all-to-all-start = ((bf16[8,2,128,256]{3,2,1,0:T(8,128)(2,1)}), bf16[8,2,128,256]{3,2,1,0:T(8,128)(2,1)S(1)}, u32[]{:S(2)}, u32[]{:S(2)}) async-start(bf16[8,2,128,256]{3,2,1,0:T(8,128)(2,1)} %bitcast.5), calls=%async_computation | async-start | bytes 2097152 | tf_op jit(solution)/shard_map/all_to_all | solution.py:684
  13.9 62.1 %copy-start.26 = (f32[128,1,2]{0,2,1:T(2,128)S(1)}, f32[128,1,2]{0,2,1:T(2,128)}, u32[]{:S(2)}) copy-start(f32[128,1,2]{0,2,1:T(2,128)} %param.17) | copy-start | bytes 3076
  14.7 30.9 %collective-permute-start.5 = (bf16[2,4,16,1024]{3,2,1,0:T(8,128)(2,1)}, bf16[2,4,16,1024]{3,2,1,0:T(8,128)(2,1)S(1)}, u32[]{:S(2)}, u32[]{:S(2)}) collective-permute-start(bf16[2,4,16,1024]{3,2,1,0:T(8,128)(2,1)} %get-tuple-element.70), channel_id=1, source_target_pairs={{0,2},{1,3},{2,0},{3,1},{4,6},{5,7},{6,4},{7,5},{8,10},{9,11},{10,... | collective-permute-start | bytes 786440 | tf_op jit(solution)/shard_map/ppermute | solution.py:665
  15.6 15.4 %collective-permute-start.2 = (bf16[128,512]{1,0:T(8,128)(2,1)S(1)}, bf16[128,512]{1,0:T(8,128)(2,1)S(1)}, u32[]{:S(2)}, u32[]{:S(2)}) collective-permute-start(bf16[128,512]{1,0:T(8,128)(2,1)S(1)} %bitcast.76), channel_id=1, source_target_pairs={{0,4},{1,5},{2,6},{3,7},{4,0},{5,1},{6,2},{7,3},{8,12},{9,13},{10,... | collective-permute-start | bytes 393224 | tf_op jit(solution)/shard_map/ppermute | solution.py:665
  15.7 29.9 %collective-permute-start = (bf16[256,512]{1,0:T(8,128)(2,1)}, bf16[256,512]{1,0:T(8,128)(2,1)S(1)}, u32[]{:S(2)}, u32[]{:S(2)}) collective-permute-start(bf16[256,512]{1,0:T(8,128)(2,1)} %bitcast), channel_id=1, source_target_pairs={{0,0},{1,1},{2,2},{3,3},{4,8},{5,9},{6,10},{7,11},{8,4},{9,5},{10,... | collective-permute-start | bytes 786440 | tf_op jit(solution)/shard_map/ppermute | solution.py:693
  20.1 26.2 %collective-permute-start.1 = (bf16[256,512]{1,0:T(8,128)(2,1)}, bf16[256,512]{1,0:T(8,128)(2,1)S(1)}, u32[]{:S(2)}, u32[]{:S(2)}) collective-permute-start(bf16[256,512]{1,0:T(8,128)(2,1)} %bitcast), channel_id=1, source_target_pairs={{0,8},{1,9},{2,10},{3,11},{4,0},{5,1},{6,2},{7,3},{8,12},{9,13},{1... | collective-permute-start | bytes 786440 | tf_op jit(solution)/shard_map/ppermute | solution.py:693
  20.2 19.5 %collective-permute-start.3 = (bf16[128,512]{1,0:T(8,128)(2,1)S(1)}, bf16[128,512]{1,0:T(8,128)(2,1)S(1)}, u32[]{:S(2)}, u32[]{:S(2)}) collective-permute-start(bf16[128,512]{1,0:T(8,128)(2,1)S(1)} %bitcast.72), channel_id=1, source_target_pairs={{0,8},{1,9},{2,10},{3,11},{4,12},{5,13},{6,14},{7,15},{8,0},{9,1},... | collective-permute-start | bytes 393224 | tf_op jit(solution)/shard_map/ppermute | solution.py:665
  31.0 17.5 %copy-start.22 = (bf16[128,512]{1,0:T(8,128)(2,1)}, bf16[128,512]{1,0:T(8,128)(2,1)S(1)}, u32[]{:S(2)}) copy-start(bf16[128,512]{1,0:T(8,128)(2,1)S(1)} %collective-permute-done.2) | copy-start | bytes 393220
  31.0 14.7 %collective-permute-start.4 = (bf16[128,512]{1,0:T(8,128)(2,1)S(1)}, bf16[128,512]{1,0:T(8,128)(2,1)S(1)}, u32[]{:S(2)}, u32[]{:S(2)}) collective-permute-start(bf16[128,512]{1,0:T(8,128)(2,1)S(1)} %bitcast.77), channel_id=1, source_target_pairs={{0,12},{1,13},{2,14},{3,15},{4,8},{5,9},{6,10},{7,11},{8,4},{9,5},... | collective-permute-start | bytes 393224 | tf_op jit(solution)/shard_map/ppermute | solution.py:665
  39.7 6.0 %copy-start.23 = (bf16[128,512]{1,0:T(8,128)(2,1)}, bf16[128,512]{1,0:T(8,128)(2,1)S(1)}, u32[]{:S(2)}) copy-start(bf16[128,512]{1,0:T(8,128)(2,1)S(1)} %collective-permute-done.3) | copy-start | bytes 393220
  46.3 2.1 copy-start.18
  48.4 12.8 %collective-permute-start.10 = (bf16[2,4,16,1024]{3,2,1,0:T(8,128)(2,1)}, bf16[2,4,16,1024]{3,2,1,0:T(8,128)(2,1)S(1)}, u32[]{:S(2)}, u32[]{:S(2)}) collective-permute-start(bf16[2,4,16,1024]{3,2,1,0:T(8,128)(2,1)} %get-tuple-element.67), channel_id=1, source_target_pairs={{0,12},{1,13},{2,14},{3,15},{4,8},{5,9},{6,10},{7,11},{8,4},{9,5},... | collective-permute-start | bytes 786440 | tf_op jit(solution)/shard_map/ppermute | solution.py:665
  49.5 23.9 %collective-permute-start.7 = (bf16[4,128,512]{2,1,0:T(8,128)(2,1)S(1)}, bf16[4,128,512]{2,1,0:T(8,128)(2,1)S(1)}, u32[]{:S(2)}, u32[]{:S(2)}) collective-permute-start(bf16[4,128,512]{2,1,0:T(8,128)(2,1)S(1)} %pad_maximum_fusion.1.kv_own), channel_id=1, source_target_pairs={{0,2},{1,3},{2,0},{3,1},{4,6},{5,7},{6,4},{7,5},{8,10},{9,11},{10,... | collective-permute-start | bytes 1572872 | tf_op jit(solution)/shard_map/ppermute | solution.py:665
  51.3 22.5 %collective-permute-start.6 = (bf16[512,512]{1,0:T(8,128)(2,1)}, bf16[512,512]{1,0:T(8,128)(2,1)S(1)}, u32[]{:S(2)}, u32[]{:S(2)}) collective-permute-start(bf16[512,512]{1,0:T(8,128)(2,1)} %constant_dynamic-update-slice_fusion), channel_id=1, source_target_pairs={{0,2},{1,3},{2,0},{3,1},{4,6},{5,7},{6,4},{7,5},{8,10},{9,11},{10,... | collective-permute-start | bytes 1572872 | tf_op jit(solution)/shard_map/ppermute | solution.py:665
  52.5 26.1 %collective-permute-start.13 = (bf16[4,128,512]{2,1,0:T(8,128)(2,1)S(1)}, bf16[4,128,512]{2,1,0:T(8,128)(2,1)}, u32[]{:S(2)}, u32[]{:S(2)}) collective-permute-start(bf16[4,128,512]{2,1,0:T(8,128)(2,1)S(1)} %pad_maximum_fusion.1.kv_own), channel_id=1, source_target_pairs={{0,1},{1,0},{2,3},{3,2},{4,5},{5,4},{6,7},{7,6},{8,9},{9,8},{10,11... | collective-permute-start | bytes 1572872 | tf_op jit(solution)/shard_map/ppermute | solution.py:665
  53.6 10.9 %collective-permute-start.8 = (bf16[2,4,16,1024]{3,2,1,0:T(8,128)(2,1)}, bf16[2,4,16,1024]{3,2,1,0:T(8,128)(2,1)}, u32[]{:S(2)}, u32[]{:S(2)}) collective-permute-start(bf16[2,4,16,1024]{3,2,1,0:T(8,128)(2,1)} %get-tuple-element.67), channel_id=1, source_target_pairs={{0,4},{1,5},{2,6},{3,7},{4,0},{5,1},{6,2},{7,3},{8,12},{9,13},{10,... | collective-permute-start | bytes 786440 | tf_op jit(solution)/shard_map/ppermute | solution.py:665
  62.0 11.5 %collective-permute-start.9 = (bf16[2,4,16,1024]{3,2,1,0:T(8,128)(2,1)S(1)}, bf16[2,4,16,1024]{3,2,1,0:T(8,128)(2,1)}, u32[]{:S(2)}, u32[]{:S(2)}) collective-permute-start(bf16[2,4,16,1024]{3,2,1,0:T(8,128)(2,1)S(1)} %get-tuple-element.43), channel_id=1, source_target_pairs={{0,8},{1,9},{2,10},{3,11},{4,12},{5,13},{6,14},{7,15},{8,0},{9,1},... | collective-permute-start | bytes 786440 | tf_op jit(solution)/shard_map/ppermute | solution.py:665
  64.5 15.9 %collective-permute-start.11 = (bf16[512,512]{1,0:T(8,128)(2,1)}, bf16[512,512]{1,0:T(8,128)(2,1)}, u32[]{:S(2)}, u32[]{:S(2)}) collective-permute-start(bf16[512,512]{1,0:T(8,128)(2,1)} %constant_dynamic-update-slice_fusion), channel_id=1, source_target_pairs={{0,1},{1,0},{2,3},{3,2},{4,5},{5,4},{6,7},{7,6},{8,9},{9,8},{10,11... | collective-permute-start | bytes 1572872 | tf_op jit(solution)/shard_map/ppermute | solution.py:665
  73.5 9.2 %copy-start.13 = (bf16[4,128,512]{2,1,0:T(8,128)(2,1)}, bf16[4,128,512]{2,1,0:T(8,128)(2,1)S(1)}, u32[]{:S(2)}) copy-start(bf16[4,128,512]{2,1,0:T(8,128)(2,1)S(1)} %collective-permute-done.7.kv_y) | copy-start | bytes 1572868
  73.8 8.9 %copy-start.15 = (bf16[512,512]{1,0:T(8,128)(2,1)}, bf16[512,512]{1,0:T(8,128)(2,1)S(1)}, u32[]{:S(2)}) copy-start(bf16[512,512]{1,0:T(8,128)(2,1)S(1)} %collective-permute-done.6.page_y) | copy-start | bytes 1572868
  73.8 8.9 %collective-permute-start.12 = (bf16[512,512]{1,0:T(8,128)(2,1)S(1)}, bf16[512,512]{1,0:T(8,128)(2,1)}, u32[]{:S(2)}, u32[]{:S(2)}) collective-permute-start(bf16[512,512]{1,0:T(8,128)(2,1)S(1)} %collective-permute-done.6.page_y), channel_id=1, source_target_pairs={{0,1},{1,0},{2,3},{3,2},{4,5},{5,4},{6,7},{7,6},{8,9},{9,8},{10,11... | collective-permute-start | bytes 1572872 | tf_op jit(solution)/shard_map/ppermute | solution.py:665
  75.2 7.5 %collective-permute-start.14 = (bf16[4,128,512]{2,1,0:T(8,128)(2,1)S(1)}, bf16[4,128,512]{2,1,0:T(8,128)(2,1)}, u32[]{:S(2)}, u32[]{:S(2)}) collective-permute-start(bf16[4,128,512]{2,1,0:T(8,128)(2,1)S(1)} %collective-permute-done.7.kv_y), channel_id=1, source_target_pairs={{0,1},{1,0},{2,3},{3,2},{4,5},{5,4},{6,7},{7,6},{8,9},{9,8},{10,11... | collective-permute-start | bytes 1572872 | tf_op jit(solution)/shard_map/ppermute | solution.py:665
  77.3 24.3 %collective-permute-start.15 = (bf16[4,2,4,16,1024]{4,3,2,1,0:T(8,128)(2,1)S(1)}, bf16[4,2,4,16,1024]{4,3,2,1,0:T(8,128)(2,1)S(1)}, u32[]{:S(2)}, u32[]{:S(2)}) collective-permute-start(bf16[4,2,4,16,1024]{4,3,2,1,0:T(8,128)(2,1)S(1)} %pad_maximum_fusion.refs_0_), channel_id=1, source_target_pairs={{0,16},{16,0},{1,17},{17,1},{2,18},{18,2},{3,19},{19,3},{4,20},{20... | collective-permute-start | bytes 3145736 | tf_op jit(solution)/shard_map/ppermute | solution.py:665
  78.6 23.0 %collective-permute-start.16 = (bf16[4,2,4,16,1024]{4,3,2,1,0:T(8,128)(2,1)S(1)}, bf16[4,2,4,16,1024]{4,3,2,1,0:T(8,128)(2,1)S(1)}, u32[]{:S(2)}, u32[]{:S(2)}) collective-permute-start(bf16[4,2,4,16,1024]{4,3,2,1,0:T(8,128)(2,1)S(1)} %pad_maximum_fusion.refs_0_), channel_id=1, source_target_pairs={{0,1},{1,0},{2,3},{3,2},{4,5},{5,4},{6,7},{7,6},{8,9},{9,8},{10,11... | collective-permute-start | bytes 3145736 | tf_op jit(solution)/shard_map/ppermute | solution.py:665
  80.4 18.6 %collective-permute-start.17 = (f32[128,4]{1,0:T(8,128)S(1)}, f32[128,4]{1,0:T(8,128)S(1)}, u32[]{:S(2)}, u32[]{:S(2)}) collective-permute-start(f32[128,4]{1,0:T(8,128)S(1)} %pad_maximum_fusion.2), channel_id=1, source_target_pairs={{0,8},{1,9},{2,10},{3,11},{4,12},{5,13},{6,14},{7,15},{8,0},{9,1},... | collective-permute-start | bytes 6152 | tf_op jit(solution)/shard_map/ppermute | solution.py:665
  82.7 1.0 copy-start.14
  83.7 1.0 copy-start.16
  101.6 4.4 %copy-start.27 = (bf16[4,2,4,16,1024]{4,3,2,1,0:T(8,128)(2,1)}, bf16[4,2,4,16,1024]{4,3,2,1,0:T(8,128)(2,1)S(1)}, u32[]{:S(2)}) copy-start(bf16[4,2,4,16,1024]{4,3,2,1,0:T(8,128)(2,1)S(1)} %collective-permute-done.15.refs_2_) | copy-start | bytes 3145732
  101.6 4.4 %collective-permute-start.19 = (bf16[4,2,4,16,1024]{4,3,2,1,0:T(8,128)(2,1)S(1)}, bf16[4,2,4,16,1024]{4,3,2,1,0:T(8,128)(2,1)S(1)}, u32[]{:S(2)}, u32[]{:S(2)}) collective-permute-start(bf16[4,2,4,16,1024]{4,3,2,1,0:T(8,128)(2,1)S(1)} %collective-permute-done.15.refs_2_), channel_id=1, source_target_pairs={{0,1},{1,0},{2,3},{3,2},{4,5},{5,4},{6,7},{7,6},{8,9},{9,8},{10,11... | collective-permute-start | bytes 3145736 | tf_op jit(solution)/shard_map/ppermute | solution.py:665
  103.0 36.0 %copy-start.11 = (bf16[128,1,2048]{2,0,1:T(8,128)(2,1)S(1)}, bf16[128,1,2048]{2,0,1:T(8,128)(2,1)}, u32[]{:S(2)}) copy-start(bf16[128,1,2048]{2,0,1:T(8,128)(2,1)} %param.13) | copy-start | bytes 1572868
  103.0 36.0 %copy-start.12 = (f32[2048]{0:T(1024)S(1)}, f32[2048]{0:T(1024)}, u32[]{:S(2)}) copy-start(f32[2048]{0:T(1024)} %param.15) | copy-start | bytes 24580
  103.0 3.0 %collective-permute-start.18 = (bf16[512,512]{1,0:T(8,128)(2,1)S(1)}, bf16[512,512]{1,0:T(8,128)(2,1)S(1)}, u32[]{:S(2)}, u32[]{:S(2)}) collective-permute-start(bf16[512,512]{1,0:T(8,128)(2,1)S(1)} %slice_bitcast_fusion), channel_id=1, source_target_pairs={{0,1},{1,0},{2,3},{3,2},{4,5},{5,4},{6,7},{7,6},{8,9},{9,8},{10,11... | collective-permute-start | bytes 1572872 | tf_op jit(solution)/shard_map/ppermute | solution.py:665
  112.7 14.4 %collective-permute-start.20 = (bf16[128,2048]{1,0:T(8,128)(2,1)}, bf16[128,2048]{1,0:T(8,128)(2,1)S(1)}, u32[]{:S(2)}, u32[]{:S(2)}) collective-permute-start(bf16[128,2048]{1,0:T(8,128)(2,1)} %get-tuple-element.55), channel_id=1, source_target_pairs={{0,6},{1,7},{2,4},{3,5},{4,2},{5,3},{6,0},{7,1},{8,14},{9,15},{10,... | collective-permute-start | bytes 1572872 | tf_op jit(solution)/shard_map/ppermute | solution.py:665
  113.2 24.3 %collective-permute-start.21 = (bf16[128,2048]{1,0:T(8,128)(2,1)}, bf16[128,2048]{1,0:T(8,128)(2,1)S(1)}, u32[]{:S(2)}, u32[]{:S(2)}) collective-permute-start(bf16[128,2048]{1,0:T(8,128)(2,1)} %get-tuple-element.56), channel_id=1, source_target_pairs={{0,4},{1,5},{2,6},{3,7},{4,0},{5,1},{6,2},{7,3},{8,12},{9,13},{10,... | collective-permute-start | bytes 1572872 | tf_op jit(solution)/shard_map/ppermute | solution.py:665
  114.2 24.8 %collective-permute-start.22 = (bf16[128,2048]{1,0:T(8,128)(2,1)}, bf16[128,2048]{1,0:T(8,128)(2,1)}, u32[]{:S(2)}, u32[]{:S(2)}) collective-permute-start(bf16[128,2048]{1,0:T(8,128)(2,1)} %get-tuple-element.57), channel_id=1, source_target_pairs={{0,2},{1,3},{2,0},{3,1},{4,6},{5,7},{6,4},{7,5},{8,10},{9,11},{10,... | collective-permute-start | bytes 1572872 | tf_op jit(solution)/shard_map/ppermute | solution.py:665
  142.7 1.0 copy-start.6
  143.7 61.2 %copy-start.1 = (bf16[1,512,2048]{2,1,0:T(8,128)(2,1)S(1)}, bf16[1,512,2048]{2,1,0:T(8,128)(2,1)}, u32[]{:S(2)}) copy-start(bf16[1,512,2048]{2,1,0:T(8,128)(2,1)} %param.19) | copy-start | bytes 6291460
  145.3 38.8 %all-to-all-start.1 = ((bf16[8,32,2048]{2,1,0:T(8,128)(2,1)}), bf16[8,32,2048]{2,1,0:T(8,128)(2,1)}, u32[]{:S(2)}, u32[]{:S(2)}) async-start(bf16[8,32,2048]{2,1,0:T(8,128)(2,1)} %bitcast.52), calls=%async_computation.1 | async-start | bytes 2097152 | tf_op jit(solution)/shard_map/all_to_all | solution.py:814
  150.3 33.8 %all-gather.5.cloned.1.call-start = ((), (), s32[]{:S(2)}) async-start(), calls=%async_computation.5 | async-start | bytes 1572864 | tf_op jit(solution)/shard_map/all_gather | solution.py:820
  184.1 1.2 copy-start.7
  209.8 18.5 %all-to-all-start.3 = ((bf16[8,32,2048]{2,1,0:T(8,128)(2,1)}), bf16[8,32,2048]{2,1,0:T(8,128)(2,1)}, u32[]{:S(2)}, u32[]{:S(2)}) async-start(bf16[8,32,2048]{2,1,0:T(8,128)(2,1)} %bitcast.56), calls=%async_computation.3 | async-start | bytes 2097152 | tf_op jit(solution)/shard_map/all_to_all | solution.py:814
  220.8 48.2 %copy-start.9 = (f32[128,2048]{1,0:T(8,128)S(1)}, f32[128,2048]{1,0:T(8,128)}, u32[]{:S(2)}) copy-start(f32[128,2048]{1,0:T(8,128)} %copy-done.8) | copy-start | bytes 3145732
  230.9 38.1 %all-to-all-start.4 = ((bf16[8,32,2048]{2,1,0:T(8,128)(2,1)}), bf16[8,32,2048]{2,1,0:T(8,128)(2,1)S(1)}, u32[]{:S(2)}, u32[]{:S(2)}) async-start(bf16[8,32,2048]{2,1,0:T(8,128)(2,1)} %bitcast.55), calls=%async_computation.4 | async-start | bytes 2097152 | tf_op jit(solution)/shard_map/all_to_all | solution.py:814
  236.4 32.6 %all-gather.7.cloned.1.call-start = ((), (), s32[]{:S(2)}) async-start(), calls=%async_computation.6 | async-start | bytes 1572864 | tf_op jit(solution)/shard_map/all_gather | solution.py:820
  269.0 1.2 copy-start.10
  (10 other events, 8.5 us)
Sparse Core Ops, SparseCore 0:
  152.7 31.3 all-gather.4
  238.7 30.2 all-gather.6

commit v13 on v11

--- a/solution.py
+++ b/solution.py
@@ -578,29 +578,28 @@
     kv_own = [kv_same]
     for t in range(1, planes):
         kv_own.append(flipped(kv_other if t % 2 else kv_same, "head", t * plane_bit))
-
-    (page_a, page_b, kv_own), w_give = lax.optimization_barrier(
-        ((page_a, page_b, kv_own), w_give)
+    w_got = flipped(w_give, "head", 2)
+
+    (page_a, page_b, kv_own, q), w_got = lax.optimization_barrier(
+        ((page_a, page_b, kv_own, q), w_got)
     )
     own_pages = jnp.concatenate([page_a, page_b], 0)
     kv_own = jnp.stack(kv_own, 0)
     pages_y = flipped(own_pages, "head", 2)
     kv_y = flipped(kv_own, "head", 2)
-    w_got = flipped(w_give, "head", 2)
     w_both = jnp.stack([w_keep, w_got], 1)
     w_same = lax.dynamic_index_in_dim(w_both, b, 0, keepdims=False)
     w_other = lax.dynamic_index_in_dim(w_both, 1 - b, 0, keepdims=False)
-    w_first = flipped(w_other, "head", plane_bit)
+    w_near = jnp.stack([w_same, flipped(w_other, "head", plane_bit)], 0)
+    w_near_x = flipped(w_near, "grp", 1)
     w_far = [flipped(w_same, "head", 2 * plane_bit), flipped(w_other, "head", 3 * plane_bit)]
-    pages_y, kv_y, own_pages, kv_own, w_first = lax.optimization_barrier(
-        (pages_y, kv_y, own_pages, kv_own, w_first)
+    pages_y, kv_y, own_pages, kv_own, w_near_x = lax.optimization_barrier(
+        (pages_y, kv_y, own_pages, kv_own, w_near_x)
     )
     kv_c = flipped(kv_own, "head", 1)
     kv_cy = flipped(kv_y, "head", 1)
     pages_c = flipped(own_pages, "head", 1)
     pages_cy = flipped(pages_y, "head", 1)
-    w_near = jnp.stack([w_same, w_first], 0)
-    w_near_x = flipped(w_near, "grp", 1)
     w_far = jnp.stack(w_far, 0)
     q, w_far = lax.optimization_barrier((q, w_far))
     w_far_x = flipped(w_far, "grp", 1)

time: 260 us -> 251 us (0.965)
  waiting for transfers between devices: 139 us -> 129 us
    ppermute x23, waiting for transfers between devices: 91.9 us -> 82.2 us  [flipped(): return lax.ppermute(value, axis, pairs)]
  transfers between devices with their start and end apart: 27 -> 27, of which waited for: 11 -> 14; matrix products, arithmetic and copies ran while one was open for 1% -> 1% of each run, Pallas kernels for 5% -> 6%
where the time goes in v13:
time: 251 us
  waiting for transfers between devices  129 us (51%)
  blocking collectives  51.4 us (20%)
  Pallas kernels  30.7 us (12%)
  starting transfers between devices  29.9 us (12%)
  local copies, waits for them, and re-layouts  7.34 us (3%)
    ppermute x23, waiting for transfers between devices, flipped(): return lax.ppermute(value, axis, pairs)  82.2 us
    all_to_all x1, blocking collectives, local(): lax.all_to_all(outgoing.reshape(n, slots // n, model), 'head', split_axis...  51.4 us
    all_to_all x1, waiting for transfers between devices, local(): lax.all_to_all(answered, 'head', split_axis=0, concat_axis=0, tiled=True)  47.3 us
    ppermute x23, starting transfers between devices, flipped(): return lax.ppermute(value, axis, pairs)  15.5 us
    pallas_call x1, Pallas kernels, attend_pair(): pl.pallas_call(functools.partial(attend_pair_kernel, block, chunk, width)...  14.5 us
    pallas_call x1, Pallas kernels, project_pair(): pl.pallas_call(project_pair_kernel, out_shape=[jax.ShapeDtypeStruct((rows...  6.77 us
    pallas_call x1, Pallas kernels, expert_pair(): pl.pallas_call(kernel, out_shape=jax.ShapeDtypeStruct((rows, model), BF16...  5.69 us
    all_to_all x1, starting transfers between devices, local(): lax.all_to_all(answered, 'head', split_axis=0, concat_axis=0, tiled=True)  5.25 us
  transfers between devices with their start and end apart: 27, of which 14 were waited for; matrix products, arithmetic and copies ran while one was open for 1% of the time, Pallas kernels for 6%

profile of v13, /device:TPU:13, one launch (start us, length us, event | category | flops | bytes accessed | tf_op | source)
XLA Modules:
  0.0 250.7 jit_solution(1549857054765693518)
XLA Ops:
  0.0 2.6 %copy.29 = bf16[16,128,256]{2,1,0:T(8,128)(2,1)} copy(bf16[16,128,256]{2,0,1:T(8,128)(2,1)} %bitcast.56) | data formatting | bytes 2097152 | tf_op jit(solution)/shard_map/transpose | solution.py:556
  2.6 4.6 %all-to-all-start = ((bf16[8,2,128,256]{3,2,1,0:T(8,128)(2,1)}), bf16[8,2,128,256]{3,2,1,0:T(8,128)(2,1)S(1)}, u32[]{:S(2)}, u32[]{:S(2)}) async-start(bf16[8,2,128,256]{3,2,1,0:T(8,128)(2,1)} %bitcast.9), calls=%async_computation | async-start | bytes 2097152 | tf_op jit(solution)/shard_map/all_to_all | solution.py:558
  7.4 0.3 collective-permute-start.5
  7.7 0.5 constant_dynamic-slice_fusion.2
  8.3 0.1 collective-permute-start.2
  8.5 4.4 %collective-permute-start = (bf16[256,512]{1,0:T(8,128)(2,1)}, bf16[256,512]{1,0:T(8,128)(2,1)S(1)}, u32[]{:S(2)}, u32[]{:S(2)}) collective-permute-start(bf16[256,512]{1,0:T(8,128)(2,1)} %bitcast.69), channel_id=1, source_target_pairs={{0,0},{1,1},{2,2},{3,3},{4,8},{5,9},{6,10},{7,11},{8,4},{9,5},{10,... | collective-permute-start | bytes 786440 | tf_op jit(solution)/shard_map/ppermute | solution.py:567
  13.0 2.4 collective-permute-start.3
  15.4 9.0 %collective-permute-done.2 = bf16[128,512]{1,0:T(8,128)(2,1)} collective-permute-done((bf16[128,512]{1,0:T(8,128)(2,1)S(1)}, bf16[128,512]{1,0:T(8,128)(2,1)}, u32[]{:S(2)}, u32[]{:S(2)}) %collective-permute-start.2) | collective-permute-done | bytes 131104 | tf_op jit(solution)/shard_map/ppermute | solution.py:539
  24.4 1.4 collective-permute-start.4
  25.8 7.4 %collective-permute-done.3 = bf16[128,512]{1,0:T(8,128)(2,1)} collective-permute-done((bf16[128,512]{1,0:T(8,128)(2,1)S(1)}, bf16[128,512]{1,0:T(8,128)(2,1)}, u32[]{:S(2)}, u32[]{:S(2)}) %collective-permute-start.3) | collective-permute-done | bytes 131104 | tf_op jit(solution)/shard_map/ppermute | solution.py:539
  33.2 6.0 %collective-permute-done.4 = bf16[128,512]{1,0:T(8,128)(2,1)} collective-permute-done((bf16[128,512]{1,0:T(8,128)(2,1)S(1)}, bf16[128,512]{1,0:T(8,128)(2,1)}, u32[]{:S(2)}, u32[]{:S(2)}) %collective-permute-start.4) | collective-permute-done | bytes 131104 | tf_op jit(solution)/shard_map/ppermute | solution.py:539
  39.2 0.7 copy-done.9
  40.0 1.1 pad_maximum_fusion.1.kv_own
  41.1 0.3 collective-permute-start.9
  41.5 1.2 collective-permute-start.8
  42.7 4.6 %collective-permute-done.10 = bf16[2,4,16,1024]{3,2,1,0:T(8,128)(2,1)S(1)} collective-permute-done((bf16[2,4,16,1024]{3,2,1,0:T(8,128)(2,1)S(1)}, bf16[2,4,16,1024]{3,2,1,0:T(8,128)(2,1)S(1)}, u32[]{:S(2)}, u32[]{:S(2)}) %collective-permute-start.10) | collective-permute-done | bytes 262176 | tf_op jit(solution)/shard_map/ppermute | solution.py:539
  47.4 1.3 collective-permute-start.11
  48.7 5.5 %collective-permute-done.9.kv_y = bf16[4,128,512]{2,1,0:T(8,128)(2,1)S(1)} collective-permute-done((bf16[4,128,512]{2,1,0:T(8,128)(2,1)S(1)}, bf16[4,128,512]{2,1,0:T(8,128)(2,1)S(1)}, u32[]{:S(2)}, u32[]{:S(2)}) %collective-permute-start.9) | collective-permute-done | bytes 524320 | tf_op jit(solution)/shard_map/ppermute | solution.py:539
  54.1 11.2 %collective-permute-done.8.page_y = bf16[512,512]{1,0:T(8,128)(2,1)S(1)} collective-permute-done((bf16[512,512]{1,0:T(8,128)(2,1)S(1)}, bf16[512,512]{1,0:T(8,128)(2,1)S(1)}, u32[]{:S(2)}, u32[]{:S(2)}) %collective-permute-start.8) | collective-permute-done | bytes 524320 | tf_op jit(solution)/shard_map/ppermute | solution.py:539
  65.4 1.3 collective-permute-start.12
  66.7 0.5 collective-permute-start.14
  67.3 13.0 %collective-permute-done.7 = bf16[2,4,16,1024]{3,2,1,0:T(8,128)(2,1)S(1)} collective-permute-done((bf16[2,4,16,1024]{3,2,1,0:T(8,128)(2,1)S(1)}, bf16[2,4,16,1024]{3,2,1,0:T(8,128)(2,1)S(1)}, u32[]{:S(2)}, u32[]{:S(2)}) %collective-permute-start.7) | collective-permute-done | bytes 262176 | tf_op jit(solution)/shard_map/ppermute | solution.py:539
  80.2 1.4 collective-permute-start.18
  81.6 1.3 collective-permute-start.16
  82.9 0.3 collective-permute-start.20
  83.2 14.5 %attend.1.a_ref = bf16[2,512,512]{2,1,0:T(8,128)(2,1)S(1)} custom-call(bf16[8,2,128,256]{3,2,1,0:T(8,128)(2,1)} %copy-done.8, bf16[512,512]{1,0:T(8,128)(2,1)S(1)} %constant_dynamic-update-slice_fusion.page_own, bf16[512,512]{1,0:T(8,128)(2,1)S(1)} %collective-permute-done.8.page_y, bf16[512,512]{1,0:T(8,128)(2,1)S(1)} %collective-permute-done.12.page_c, ...), custom_call_target="tpu_custom_call" | custom-call | flops 7516192768 | bytes 6291456 | tf_op jit(solution)/shard_map/attend/pallas_call | solution.py:259
  97.8 0.3 collective-permute-start.19
  98.1 0.3 collective-permute-start.21
  98.4 0.2 collective-permute-start.17
  98.6 1.2 collective-permute-done.19.refs_3_
  99.8 0.7 collective-permute-done.21.refs_7_
  100.6 0.7 collective-permute-done.17.got_ref
  101.4 6.8 %project.1 = (bf16[128,2048]{1,0:T(8,128)(2,1)S(1)}, bf16[128,2048]{1,0:T(8,128)(2,1)}, bf16[128,2048]{1,0:T(8,128)(2,1)}, bf16[128,2048]{1,0:T(8,128)(2,1)}) custom-call(bf16[2,512,512]{2,1,0:T(8,128)(2,1)} %copy-done.5, bf16[512,512]{1,0:T(8,128)(2,1)S(1)} %collective-permute-done.17.got_ref, bf16[2,2,4,16,1024]{4,3,2,1,0:T(8,128)(2,1)S(1)} %pad_maximum_fusion.2.refs_0_, ...), custom_call_target="tpu_custom_call" | custom-call | flops 2147483648 | bytes 7340032 | tf_op jit(solution)/shard_map/project/pallas_call | solution.py:324
  108.2 1.5 collective-permute-start.23
  109.7 1.2 collective-permute-start.24
  111.2 0.2 reduce_window_sum.11
  111.4 0.1 copy.26
  111.6 11.0 %collective-permute-done.22 = bf16[128,2048]{1,0:T(8,128)(2,1)S(1)} collective-permute-done((bf16[128,2048]{1,0:T(8,128)(2,1)}, bf16[128,2048]{1,0:T(8,128)(2,1)S(1)}, u32[]{:S(2)}, u32[]{:S(2)}) %collective-permute-start.22) | collective-permute-done | bytes 524320 | tf_op jit(solution)/shard_map/ppermute | solution.py:539
  122.7 10.4 %collective-permute-done.23 = bf16[128,2048]{1,0:T(8,128)(2,1)S(1)} collective-permute-done((bf16[128,2048]{1,0:T(8,128)(2,1)}, bf16[128,2048]{1,0:T(8,128)(2,1)S(1)}, u32[]{:S(2)}, u32[]{:S(2)}) %collective-permute-start.23) | collective-permute-done | bytes 524320 | tf_op jit(solution)/shard_map/ppermute | solution.py:539
  133.1 1.4 collective-permute-done.24
  134.5 2.2 route.1
  136.7 51.4 %all_to_all.15 = bf16[16,32,2048]{2,1,0:T(8,128)(2,1)S(1)} all-to-all(bf16[16,32,2048]{2,1,0:T(8,128)(2,1)S(1)} %bitcast.45), channel_id=1, replica_groups=mesh['grp'=2,'head'=16] {'head'}, dimensions={0} | all-to-all | bytes 4194304 | tf_op jit(solution)/shard_map/all_to_all | solution.py:718
  188.2 5.7 %expert.1 = bf16[512,2048]{1,0:T(8,128)(2,1)S(1)} custom-call(bf16[512,2048]{1,0:T(8,128)(2,1)S(1)} %bitcast.47, bf16[2048,1024]{1,0:T(8,128)(2,1)} %bitcast.67, bf16[512,2048]{1,0:T(8,128)(2,1)} %bitcast.68), custom_call_target="tpu_custom_call" | custom-call | flops 3221225472 | bytes 10485760 | tf_op jit(solution)/shard_map/expert/pallas_call | solution.py:479
  193.9 1.3 copy-done.1
  195.2 5.3 %all-to-all-start.2 = ((bf16[16,32,2048]{2,1,0:T(8,128)(2,1)}), bf16[16,32,2048]{2,1,0:T(8,128)(2,1)S(1)}, u32[]{:S(2)}, u32[]{:S(2)}) async-start(bf16[16,32,2048]{2,1,0:T(8,128)(2,1)} %bitcast.46), calls=%async_computation.2 | async-start | bytes 4194304 | tf_op jit(solution)/shard_map/all_to_all | solution.py:731
  200.6 47.3 %all-to-all-done.2 = bf16[16,32,2048]{2,1,0:T(8,128)(2,1)S(1)} async-done(((bf16[16,32,2048]{2,1,0:T(8,128)(2,1)}), bf16[16,32,2048]{2,1,0:T(8,128)(2,1)S(1)}, u32[]{:S(2)}, u32[]{:S(2)}) %all-to-all-start.2) | async-done | bytes 2097184 | tf_op jit(solution)/shard_map/all_to_all | solution.py:731
  247.9 1.2 copy-done.3
  249.1 1.6 combine.1
  (67 shorter events, 1.3 us)
Async XLA Ops:
  0.0 7.3 %copy-start = (bf16[16,16,2048]{2,1,0:T(8,128)(2,1)S(1)}, bf16[16,16,2048]{2,1,0:T(8,128)(2,1)}, u32[]{:S(2)}) copy-start(bf16[16,16,2048]{2,1,0:T(8,128)(2,1)} %param.14) | copy-start | bytes 3145732
  2.6 5.1 %copy-start.7 = (bf16[128,1,2,512]{3,2,1,0:T(2,128)(2,1)S(1)}, bf16[128,1,2,512]{3,2,1,0:T(2,128)(2,1)}, u32[]{:S(2)}) copy-start(bf16[128,1,2,512]{3,2,1,0:T(2,128)(2,1)} %param.11) | copy-start | bytes 786436
  2.6 36.5 %all-to-all-start = ((bf16[8,2,128,256]{3,2,1,0:T(8,128)(2,1)}), bf16[8,2,128,256]{3,2,1,0:T(8,128)(2,1)S(1)}, u32[]{:S(2)}, u32[]{:S(2)}) async-start(bf16[8,2,128,256]{3,2,1,0:T(8,128)(2,1)} %bitcast.9), calls=%async_computation | async-start | bytes 2097152 | tf_op jit(solution)/shard_map/all_to_all | solution.py:558
  7.4 31.8 %collective-permute-start.5 = (bf16[2,4,16,1024]{3,2,1,0:T(8,128)(2,1)S(1)}, bf16[2,4,16,1024]{3,2,1,0:T(8,128)(2,1)S(1)}, u32[]{:S(2)}, u32[]{:S(2)}) collective-permute-start(bf16[2,4,16,1024]{3,2,1,0:T(8,128)(2,1)S(1)} %get-tuple-element.56), channel_id=1, source_target_pairs={{0,2},{1,3},{2,0},{3,1},{4,6},{5,7},{6,4},{7,5},{8,10},{9,11},{10,... | collective-permute-start | bytes 786440 | tf_op jit(solution)/shard_map/ppermute | solution.py:539
  8.3 16.1 %collective-permute-start.2 = (bf16[128,512]{1,0:T(8,128)(2,1)S(1)}, bf16[128,512]{1,0:T(8,128)(2,1)}, u32[]{:S(2)}, u32[]{:S(2)}) collective-permute-start(bf16[128,512]{1,0:T(8,128)(2,1)S(1)} %bitcast.65), channel_id=1, source_target_pairs={{0,4},{1,5},{2,6},{3,7},{4,0},{5,1},{6,2},{7,3},{8,12},{9,13},{10,... | collective-permute-start | bytes 393224 | tf_op jit(solution)/shard_map/ppermute | solution.py:539
  8.5 30.7 %collective-permute-start = (bf16[256,512]{1,0:T(8,128)(2,1)}, bf16[256,512]{1,0:T(8,128)(2,1)S(1)}, u32[]{:S(2)}, u32[]{:S(2)}) collective-permute-start(bf16[256,512]{1,0:T(8,128)(2,1)} %bitcast.69), channel_id=1, source_target_pairs={{0,0},{1,1},{2,2},{3,3},{4,8},{5,9},{6,10},{7,11},{8,4},{9,5},{10,... | collective-permute-start | bytes 786440 | tf_op jit(solution)/shard_map/ppermute | solution.py:567
  12.9 26.3 %collective-permute-start.1 = (bf16[256,512]{1,0:T(8,128)(2,1)}, bf16[256,512]{1,0:T(8,128)(2,1)S(1)}, u32[]{:S(2)}, u32[]{:S(2)}) collective-permute-start(bf16[256,512]{1,0:T(8,128)(2,1)} %bitcast.70), channel_id=1, source_target_pairs={{0,8},{1,9},{2,10},{3,11},{4,0},{5,1},{6,2},{7,3},{8,12},{9,13},{1... | collective-permute-start | bytes 786440 | tf_op jit(solution)/shard_map/ppermute | solution.py:567
  13.0 20.2 %collective-permute-start.3 = (bf16[128,512]{1,0:T(8,128)(2,1)S(1)}, bf16[128,512]{1,0:T(8,128)(2,1)}, u32[]{:S(2)}, u32[]{:S(2)}) collective-permute-start(bf16[128,512]{1,0:T(8,128)(2,1)S(1)} %bitcast.59), channel_id=1, source_target_pairs={{0,8},{1,9},{2,10},{3,11},{4,12},{5,13},{6,14},{7,15},{8,0},{9,1},... | collective-permute-start | bytes 393224 | tf_op jit(solution)/shard_map/ppermute | solution.py:539
  24.4 14.8 %collective-permute-start.4 = (bf16[128,512]{1,0:T(8,128)(2,1)S(1)}, bf16[128,512]{1,0:T(8,128)(2,1)}, u32[]{:S(2)}, u32[]{:S(2)}) collective-permute-start(bf16[128,512]{1,0:T(8,128)(2,1)S(1)} %bitcast.66), channel_id=1, source_target_pairs={{0,12},{1,13},{2,14},{3,15},{4,8},{5,9},{6,10},{7,11},{8,4},{9,5},... | collective-permute-start | bytes 393224 | tf_op jit(solution)/shard_map/ppermute | solution.py:539
  39.1 0.7 copy-start.9
  39.2 8.2 %copy-start.8 = (bf16[8,2,128,256]{3,2,1,0:T(8,128)(2,1)}, bf16[8,2,128,256]{3,2,1,0:T(8,128)(2,1)S(1)}, u32[]{:S(2)}) copy-start(bf16[8,2,128,256]{3,2,1,0:T(8,128)(2,1)S(1)} %all-to-all-done.q_hbm) | copy-start | bytes 3145732
  39.8 1.6 copy-start.10
  39.9 7.4 %collective-permute-start.10 = (bf16[2,4,16,1024]{3,2,1,0:T(8,128)(2,1)S(1)}, bf16[2,4,16,1024]{3,2,1,0:T(8,128)(2,1)S(1)}, u32[]{:S(2)}, u32[]{:S(2)}) collective-permute-start(bf16[2,4,16,1024]{3,2,1,0:T(8,128)(2,1)S(1)} %get-tuple-element.54), channel_id=1, source_target_pairs={{0,4},{1,5},{2,6},{3,7},{4,0},{5,1},{6,2},{7,3},{8,12},{9,13},{10,... | collective-permute-start | bytes 786440 | tf_op jit(solution)/shard_map/ppermute | solution.py:539
  41.1 13.1 %collective-permute-start.9 = (bf16[4,128,512]{2,1,0:T(8,128)(2,1)S(1)}, bf16[4,128,512]{2,1,0:T(8,128)(2,1)S(1)}, u32[]{:S(2)}, u32[]{:S(2)}) collective-permute-start(bf16[4,128,512]{2,1,0:T(8,128)(2,1)S(1)} %pad_maximum_fusion.1.kv_own), channel_id=1, source_target_pairs={{0,2},{1,3},{2,0},{3,1},{4,6},{5,7},{6,4},{7,5},{8,10},{9,11},{10,... | collective-permute-start | bytes 1572872 | tf_op jit(solution)/shard_map/ppermute | solution.py:539
  41.5 23.9 %collective-permute-start.8 = (bf16[512,512]{1,0:T(8,128)(2,1)S(1)}, bf16[512,512]{1,0:T(8,128)(2,1)S(1)}, u32[]{:S(2)}, u32[]{:S(2)}) collective-permute-start(bf16[512,512]{1,0:T(8,128)(2,1)S(1)} %constant_dynamic-update-slice_fusion.page_own), channel_id=1, source_target_pairs={{0,2},{1,3},{2,0},{3,1},{4,6},{5,7},{6,4},{7,5},{8,10},{9,11},{10,... | collective-permute-start | bytes 1572872 | tf_op jit(solution)/shard_map/ppermute | solution.py:539
  47.4 18.0 %collective-permute-start.11 = (bf16[2,2,4,16,1024]{4,3,2,1,0:T(8,128)(2,1)S(1)}, bf16[2,2,4,16,1024]{4,3,2,1,0:T(8,128)(2,1)S(1)}, u32[]{:S(2)}, u32[]{:S(2)}) collective-permute-start(bf16[2,2,4,16,1024]{4,3,2,1,0:T(8,128)(2,1)S(1)} %pad_maximum_fusion.2.refs_0_), channel_id=1, source_target_pairs={{0,16},{16,0},{1,17},{17,1},{2,18},{18,2},{3,19},{19,3},{4,20},{20... | collective-permute-start | bytes 1572872 | tf_op jit(solution)/shard_map/ppermute | solution.py:539
  48.7 18.6 %collective-permute-start.6 = (bf16[2,4,16,1024]{3,2,1,0:T(8,128)(2,1)S(1)}, bf16[2,4,16,1024]{3,2,1,0:T(8,128)(2,1)S(1)}, u32[]{:S(2)}, u32[]{:S(2)}) collective-permute-start(bf16[2,4,16,1024]{3,2,1,0:T(8,128)(2,1)S(1)} %bitcast.57), channel_id=1, source_target_pairs={{0,8},{1,9},{2,10},{3,11},{4,12},{5,13},{6,14},{7,15},{8,0},{9,1},... | collective-permute-start | bytes 786440 | tf_op jit(solution)/shard_map/ppermute | solution.py:539
  65.4 16.3 %collective-permute-start.12 = (bf16[512,512]{1,0:T(8,128)(2,1)S(1)}, bf16[512,512]{1,0:T(8,128)(2,1)S(1)}, u32[]{:S(2)}, u32[]{:S(2)}) collective-permute-start(bf16[512,512]{1,0:T(8,128)(2,1)S(1)} %constant_dynamic-update-slice_fusion.page_own), channel_id=1, source_target_pairs={{0,1},{1,0},{2,3},{3,2},{4,5},{5,4},{6,7},{7,6},{8,9},{9,8},{10,11... | collective-permute-start | bytes 1572872 | tf_op jit(solution)/shard_map/ppermute | solution.py:539
  66.7 16.2 %collective-permute-start.13 = (bf16[512,512]{1,0:T(8,128)(2,1)S(1)}, bf16[512,512]{1,0:T(8,128)(2,1)S(1)}, u32[]{:S(2)}, u32[]{:S(2)}) collective-permute-start(bf16[512,512]{1,0:T(8,128)(2,1)S(1)} %collective-permute-done.8.page_y), channel_id=1, source_target_pairs={{0,1},{1,0},{2,3},{3,2},{4,5},{5,4},{6,7},{7,6},{8,9},{9,8},{10,11... | collective-permute-start | bytes 1572872 | tf_op jit(solution)/shard_map/ppermute | solution.py:539
  66.7 16.5 %collective-permute-start.14 = (bf16[4,128,512]{2,1,0:T(8,128)(2,1)S(1)}, bf16[4,128,512]{2,1,0:T(8,128)(2,1)S(1)}, u32[]{:S(2)}, u32[]{:S(2)}) collective-permute-start(bf16[4,128,512]{2,1,0:T(8,128)(2,1)S(1)} %pad_maximum_fusion.1.kv_own), channel_id=1, source_target_pairs={{0,1},{1,0},{2,3},{3,2},{4,5},{5,4},{6,7},{7,6},{8,9},{9,8},{10,11... | collective-permute-start | bytes 1572872 | tf_op jit(solution)/shard_map/ppermute | solution.py:539
  67.2 16.0 %collective-permute-start.15 = (bf16[4,128,512]{2,1,0:T(8,128)(2,1)S(1)}, bf16[4,128,512]{2,1,0:T(8,128)(2,1)S(1)}, u32[]{:S(2)}, u32[]{:S(2)}) collective-permute-start(bf16[4,128,512]{2,1,0:T(8,128)(2,1)S(1)} %collective-permute-done.9.kv_y), channel_id=1, source_target_pairs={{0,1},{1,0},{2,3},{3,2},{4,5},{5,4},{6,7},{7,6},{8,9},{9,8},{10,11... | collective-permute-start | bytes 1572872 | tf_op jit(solution)/shard_map/ppermute | solution.py:539
  67.2 13.0 %collective-permute-start.7 = (bf16[2,4,16,1024]{3,2,1,0:T(8,128)(2,1)S(1)}, bf16[2,4,16,1024]{3,2,1,0:T(8,128)(2,1)S(1)}, u32[]{:S(2)}, u32[]{:S(2)}) collective-permute-start(bf16[2,4,16,1024]{3,2,1,0:T(8,128)(2,1)S(1)} %get-tuple-element.54), channel_id=1, source_target_pairs={{0,12},{1,13},{2,14},{3,15},{4,8},{5,9},{6,10},{7,11},{8,4},{9,5},... | collective-permute-start | bytes 786440 | tf_op jit(solution)/shard_map/ppermute | solution.py:539
  80.2 18.4 %collective-permute-start.18 = (bf16[2,2,4,16,1024]{4,3,2,1,0:T(8,128)(2,1)S(1)}, bf16[2,2,4,16,1024]{4,3,2,1,0:T(8,128)(2,1)S(1)}, u32[]{:S(2)}, u32[]{:S(2)}) collective-permute-start(bf16[2,2,4,16,1024]{4,3,2,1,0:T(8,128)(2,1)S(1)} %pad_maximum_fusion.2.refs_0_), channel_id=1, source_target_pairs={{0,1},{1,0},{2,3},{3,2},{4,5},{5,4},{6,7},{7,6},{8,9},{9,8},{10,11... | collective-permute-start | bytes 1572872 | tf_op jit(solution)/shard_map/ppermute | solution.py:539
  81.6 16.2 %collective-permute-start.16 = (bf16[2,2,4,16,1024]{4,3,2,1,0:T(8,128)(2,1)S(1)}, bf16[2,2,4,16,1024]{4,3,2,1,0:T(8,128)(2,1)S(1)}, u32[]{:S(2)}, u32[]{:S(2)}) collective-permute-start(bf16[2,2,4,16,1024]{4,3,2,1,0:T(8,128)(2,1)S(1)} %pad_maximum_fusion.refs_4_), channel_id=1, source_target_pairs={{0,16},{16,0},{1,17},{17,1},{2,18},{18,2},{3,19},{19,3},{4,20},{20... | collective-permute-start | bytes 1572872 | tf_op jit(solution)/shard_map/ppermute | solution.py:539
  82.9 15.7 %collective-permute-start.20 = (bf16[2,2,4,16,1024]{4,3,2,1,0:T(8,128)(2,1)S(1)}, bf16[2,2,4,16,1024]{4,3,2,1,0:T(8,128)(2,1)S(1)}, u32[]{:S(2)}, u32[]{:S(2)}) collective-permute-start(bf16[2,2,4,16,1024]{4,3,2,1,0:T(8,128)(2,1)S(1)} %pad_maximum_fusion.refs_4_), channel_id=1, source_target_pairs={{0,1},{1,0},{2,3},{3,2},{4,5},{5,4},{6,7},{7,6},{8,9},{9,8},{10,11... | collective-permute-start | bytes 1572872 | tf_op jit(solution)/shard_map/ppermute | solution.py:539
  97.7 3.6 %copy-start.5 = (bf16[2,512,512]{2,1,0:T(8,128)(2,1)}, bf16[2,512,512]{2,1,0:T(8,128)(2,1)S(1)}, u32[]{:S(2)}) copy-start(bf16[2,512,512]{2,1,0:T(8,128)(2,1)S(1)} %attend.1.a_ref) | copy-start | bytes 3145732
  97.8 13.1 %copy-start.11 = (s32[128,1,2]{0,2,1:T(2,128)S(1)}, s32[128,1,2]{0,2,1:T(2,128)}, u32[]{:S(2)}) copy-start(s32[128,1,2]{0,2,1:T(2,128)} %param.16) | copy-start | bytes 3076
  97.8 36.7 %copy-start.4 = (bf16[128,1,2048]{2,0,1:T(8,128)(2,1)S(1)}, bf16[128,1,2048]{2,0,1:T(8,128)(2,1)}, u32[]{:S(2)}) copy-start(bf16[128,1,2048]{2,0,1:T(8,128)(2,1)} %param.13) | copy-start | bytes 1572868
  97.8 36.7 %copy-start.6 = (f32[2048]{0:T(1024)S(1)}, f32[2048]{0:T(1024)}, u32[]{:S(2)}) copy-start(f32[2048]{0:T(1024)} %param.15) | copy-start | bytes 24580
  97.8 3.5 %copy-start.13 = (bf16[2,2,4,16,1024]{4,3,2,1,0:T(8,128)(2,1)}, bf16[2,2,4,16,1024]{4,3,2,1,0:T(8,128)(2,1)S(1)}, u32[]{:S(2)}) copy-start(bf16[2,2,4,16,1024]{4,3,2,1,0:T(8,128)(2,1)S(1)} %collective-permute-done.16.refs_6_) | copy-start | bytes 1572868
  97.8 2.0 collective-permute-start.19
  98.1 2.4 collective-permute-start.21
  98.4 2.9 %collective-permute-start.17 = (bf16[512,512]{1,0:T(8,128)(2,1)S(1)}, bf16[512,512]{1,0:T(8,128)(2,1)S(1)}, u32[]{:S(2)}, u32[]{:S(2)}) collective-permute-start(bf16[512,512]{1,0:T(8,128)(2,1)S(1)} %slice_bitcast_fusion), channel_id=1, source_target_pairs={{0,1},{1,0},{2,3},{3,2},{4,5},{5,4},{6,7},{7,6},{8,9},{9,8},{10,11... | collective-permute-start | bytes 1572872 | tf_op jit(solution)/shard_map/ppermute | solution.py:539
  100.6 0.8 copy-start.14
  108.1 14.5 %collective-permute-start.22 = (bf16[128,2048]{1,0:T(8,128)(2,1)}, bf16[128,2048]{1,0:T(8,128)(2,1)S(1)}, u32[]{:S(2)}, u32[]{:S(2)}) collective-permute-start(bf16[128,2048]{1,0:T(8,128)(2,1)} %get-tuple-element.48), channel_id=1, source_target_pairs={{0,6},{1,7},{2,4},{3,5},{4,2},{5,3},{6,0},{7,1},{8,14},{9,15},{10,... | collective-permute-start | bytes 1572872 | tf_op jit(solution)/shard_map/ppermute | solution.py:539
  108.2 24.9 %collective-permute-start.23 = (bf16[128,2048]{1,0:T(8,128)(2,1)}, bf16[128,2048]{1,0:T(8,128)(2,1)S(1)}, u32[]{:S(2)}, u32[]{:S(2)}) collective-permute-start(bf16[128,2048]{1,0:T(8,128)(2,1)} %get-tuple-element.49), channel_id=1, source_target_pairs={{0,4},{1,5},{2,6},{3,7},{4,0},{5,1},{6,2},{7,3},{8,12},{9,13},{10,... | collective-permute-start | bytes 1572872 | tf_op jit(solution)/shard_map/ppermute | solution.py:539
  109.7 24.8 %collective-permute-start.24 = (bf16[128,2048]{1,0:T(8,128)(2,1)}, bf16[128,2048]{1,0:T(8,128)(2,1)}, u32[]{:S(2)}, u32[]{:S(2)}) collective-permute-start(bf16[128,2048]{1,0:T(8,128)(2,1)} %get-tuple-element.50), channel_id=1, source_target_pairs={{0,2},{1,3},{2,0},{3,1},{4,6},{5,7},{6,4},{7,5},{8,10},{9,11},{10,... | collective-permute-start | bytes 1572872 | tf_op jit(solution)/shard_map/ppermute | solution.py:539
  136.7 51.5 %copy-start.2 = (f32[128,2048]{1,0:T(8,128)}, f32[128,2048]{1,0:T(8,128)S(1)}, u32[]{:S(2)}) copy-start(f32[128,2048]{1,0:T(8,128)S(1)} %get-tuple-element.52.stream_ref) | copy-start | bytes 3145732
  193.9 1.4 copy-start.1
  195.2 5.3 %copy-start.12 = (f32[128,1,2]{0,2,1:T(2,128)S(1)}, f32[128,1,2]{0,2,1:T(2,128)}, u32[]{:S(2)}) copy-start(f32[128,1,2]{0,2,1:T(2,128)} %param.17) | copy-start | bytes 3076
  195.2 52.7 %all-to-all-start.2 = ((bf16[16,32,2048]{2,1,0:T(8,128)(2,1)}), bf16[16,32,2048]{2,1,0:T(8,128)(2,1)S(1)}, u32[]{:S(2)}, u32[]{:S(2)}) async-start(bf16[16,32,2048]{2,1,0:T(8,128)(2,1)} %bitcast.46), calls=%async_computation.2 | async-start | bytes 4194304 | tf_op jit(solution)/shard_map/all_to_all | solution.py:731
  247.9 1.2 copy-start.3

commit v14 on v13

--- a/solution.py
+++ b/solution.py
@@ -157,12 +157,12 @@
     earlier_group = me // members > 0
     core = lax.rem(me, 2)
     chip = jnp.bitwise_and(me // 2, members // 2 - 1)
-    copies = []
+    copies = [[], [], []]
 
     def bring(source, target, sem):
         copy = pltpu.make_async_copy(source, target, sems.at[sem])
         copy.start()
-        copies.append(copy)
+        copies[sem].append(copy)
 
     for member in range(members):
         for head in range(heads):
@@ -180,7 +180,7 @@
             start = pl.multiple_of(number * piece, piece)
             area = 0 if t * (members // 2) >= members else length
             bring(pieces_of.at[t], kv_ref.at[pl.ds(area + start, piece)], 2)
-    for copy in copies:
+    for copy in copies[0] + copies[1]:
         copy.wait()
     scale = width**-0.5 * LOG2_E
     scores = [s0, s1]
@@ -230,6 +230,10 @@
 
     running = None
     for part in pieces(0):
+        if part[0] == "past":
+            for copy in copies[2]:
+                copy.wait()
+            copies[2] = []
         running = make_scores(0, part, running)
     for unit, (head, b) in enumerate(units):
         top = jnp.max(running, 1, keepdims=True)
@@ -280,7 +284,7 @@
 
 
 def project_pair_kernel(a_ref, got_ref, *refs):
-    near, far, outs, (w_ref, sems) = refs[:4], refs[4:8], refs[8:-2], refs[-2:]
+    near, far, outs, (w_ref, all_ref, sems) = refs[:4], refs[4:8], refs[8:-3], refs[-3:]
     me = lax.axis_index("head")
     half = lax.axis_index("grp")
     core = lax.rem(me, 2)
@@ -301,19 +305,20 @@
                     )
                     copy.start()
                     copies.append(copy)
+    side = got_ref.shape[1]
+    for other, rows_of in enumerate((a_ref[0], got_ref[...])):
+        column = pl.multiple_of(jnp.bitwise_xor(core, other) * side, side)
+        all_ref[:, pl.ds(column, side)] = rows_of
     for copy in copies:
         copy.wait()
-    acc = None
-    for k in range(heads):
-        mine = k < heads // 2
-        at = pl.ds((k % (heads // 2)) * width, width)
-        rows_of = a_ref[0, :, at] if mine else got_ref[:, at]
-        head = jnp.bitwise_xor(core, 0 if mine else 1) * (heads // 2) + k % (heads // 2)
-        part = jnp.dot(rows_of, w_ref[head], preferred_element_type=F32)
-        acc = part if acc is None else acc + part
-    rows = outs[0].shape[0]
-    for k, out in enumerate(outs):
-        out[...] = acc[k * rows : (k + 1) * rows].astype(BF16)
+    rows, model = outs[0].shape
+    tile = min(512, model)
+    for column in range(0, model, tile):
+        at = pl.ds(column, tile)
+        w = w_ref[:, :, at].reshape(heads * width, tile)
+        product = jnp.dot(all_ref[...], w, preferred_element_type=F32).astype(BF16)
+        for k, out in enumerate(outs):
+            out[:, at] = product[k * rows : (k + 1) * rows]
 
 
 def project_pair(a, got, near, far, parts):
@@ -328,6 +333,7 @@
         out_specs=[in_vmem()] * parts,
         scratch_shapes=[
             pltpu.VMEM((heads, width, model), BF16),
+            pltpu.VMEM((rows, heads * width), BF16),
             pltpu.SemaphoreType.DMA((1,)),
         ],
         compiler_params=pltpu.CompilerParams(vmem_limit_bytes=HIGH_VMEM),
@@ -575,16 +581,15 @@
     w = w.reshape(2, 2, heads // 4, share, columns)
     w_keep = lax.dynamic_index_in_dim(w, y, 1, keepdims=False)
     w_give = lax.dynamic_index_in_dim(w, 1 - y, 1, keepdims=False)
-    kv_own = [kv_same]
-    for t in range(1, planes):
-        kv_own.append(flipped(kv_other if t % 2 else kv_same, "head", t * plane_bit))
+    kv_near = jnp.stack([kv_same, flipped(kv_other, "head", plane_bit)], 0)
+    kv_far = flipped(kv_near, "head", members)
     w_got = flipped(w_give, "head", 2)
 
-    (page_a, page_b, kv_own, q), w_got = lax.optimization_barrier(
-        ((page_a, page_b, kv_own, q), w_got)
+    (page_a, page_b, kv_far, q), w_got = lax.optimization_barrier(
+        ((page_a, page_b, kv_far, q), w_got)
     )
     own_pages = jnp.concatenate([page_a, page_b], 0)
-    kv_own = jnp.stack(kv_own, 0)
+    kv_own = jnp.concatenate([kv_near, kv_far], 0)
     pages_y = flipped(own_pages, "head", 2)
     kv_y = flipped(kv_own, "head", 2)
     w_both = jnp.stack([w_keep, w_got], 1)
@@ -592,7 +597,7 @@
     w_other = lax.dynamic_index_in_dim(w_both, 1 - b, 0, keepdims=False)
     w_near = jnp.stack([w_same, flipped(w_other, "head", plane_bit)], 0)
     w_near_x = flipped(w_near, "grp", 1)
-    w_far = [flipped(w_same, "head", 2 * plane_bit), flipped(w_other, "head", 3 * plane_bit)]
+    w_far = flipped(w_near, "head", members)
     pages_y, kv_y, own_pages, kv_own, w_near_x = lax.optimization_barrier(
         (pages_y, kv_y, own_pages, kv_own, w_near_x)
     )
@@ -600,7 +605,6 @@
     kv_cy = flipped(kv_y, "head", 1)
     pages_c = flipped(own_pages, "head", 1)
     pages_cy = flipped(pages_y, "head", 1)
-    w_far = jnp.stack(w_far, 0)
     q, w_far = lax.optimization_barrier((q, w_far))
     w_far_x = flipped(w_far, "grp", 1)
     a = attend_pair(q, (own_pages, pages_y, pages_c, pages_cy), (kv_own, kv_y, kv_c, kv_cy))

time: 251 us -> 247 us (0.984)
  waiting for transfers between devices: 129 us -> 120 us
  starting transfers between devices: 29.9 us -> 32.8 us
    ppermute x23 -> x21, waiting for transfers between devices: 82.2 us -> 72.5 us  [flipped(): return lax.ppermute(value, axis, pairs)]
    ppermute x23 -> x21, starting transfers between devices: 15.5 us -> 19.7 us  [flipped(): return lax.ppermute(value, axis, pairs)]
  transfers between devices with their start and end apart: 27 -> 25, of which waited for: 14 -> 12; matrix products, arithmetic and copies ran while one was open for 1% -> 2% of each run, Pallas kernels for 6% -> 6%
where the time goes in v14:
time: 247 us
  waiting for transfers between devices  120 us (49%)
  blocking collectives  53.1 us (21%)
  starting transfers between devices  32.8 us (13%)
  Pallas kernels  30.8 us (12%)
  local copies, waits for them, and re-layouts  8.25 us (3%)
    ppermute x21, waiting for transfers between devices, flipped(): return lax.ppermute(value, axis, pairs)  72.5 us
    all_to_all x1, blocking collectives, local(): lax.all_to_all(outgoing.reshape(n, slots // n, model), 'head', split_axis...  53.1 us
    all_to_all x1, waiting for transfers between devices, local(): lax.all_to_all(answered, 'head', split_axis=0, concat_axis=0, tiled=True)  47.3 us
    ppermute x21, starting transfers between devices, flipped(): return lax.ppermute(value, axis, pairs)  19.7 us
    pallas_call x1, Pallas kernels, attend_pair(): pl.pallas_call(functools.partial(attend_pair_kernel, block, chunk, width)...  14.8 us
    pallas_call x1, Pallas kernels, project_pair(): pl.pallas_call(project_pair_kernel, out_shape=[jax.ShapeDtypeStruct((rows...  6.54 us
    pallas_call x1, Pallas kernels, expert_pair(): pl.pallas_call(kernel, out_shape=jax.ShapeDtypeStruct((rows, model), BF16...  5.69 us
    all_to_all x1, starting transfers between devices, local(): lax.all_to_all(answered, 'head', split_axis=0, concat_axis=0, tiled=True)  5.26 us
  transfers between devices with their start and end apart: 25, of which 12 were waited for; matrix products, arithmetic and copies ran while one was open for 2% of the time, Pallas kernels for 6%

profile of v14, /device:TPU:13, one launch (start us, length us, event | category | flops | bytes accessed | tf_op | source)
XLA Modules:
  0.0 246.6 jit_solution(10086323421695735144)
XLA Ops:
  0.0 2.6 %copy.29 = bf16[16,128,256]{2,1,0:T(8,128)(2,1)} copy(bf16[16,128,256]{2,0,1:T(8,128)(2,1)} %bitcast.52) | data formatting | bytes 2097152 | tf_op jit(solution)/shard_map/transpose | solution.py:562
  2.6 4.5 %all-to-all-start = ((bf16[8,2,128,256]{3,2,1,0:T(8,128)(2,1)}), bf16[8,2,128,256]{3,2,1,0:T(8,128)(2,1)S(1)}, u32[]{:S(2)}, u32[]{:S(2)}) async-start(bf16[8,2,128,256]{3,2,1,0:T(8,128)(2,1)} %bitcast.10), calls=%async_computation | async-start | bytes 2097152 | tf_op jit(solution)/shard_map/all_to_all | solution.py:564
  7.2 3.3 %collective-permute-start = (bf16[256,512]{1,0:T(8,128)(2,1)}, bf16[256,512]{1,0:T(8,128)(2,1)S(1)}, u32[]{:S(2)}, u32[]{:S(2)}) collective-permute-start(bf16[256,512]{1,0:T(8,128)(2,1)} %bitcast.4), channel_id=1, source_target_pairs={{0,0},{1,1},{2,2},{3,3},{4,8},{5,9},{6,10},{7,11},{8,4},{9,5},{10,... | collective-permute-start | bytes 786440 | tf_op jit(solution)/shard_map/ppermute | solution.py:573
  10.6 0.5 constant_dynamic-slice_fusion.3
  11.2 0.7 copy.36
  11.8 1.2 collective-permute-start.2
  13.1 0.3 collective-permute-start.4
  13.5 14.7 %collective-permute-done.2 = bf16[128,512]{1,0:T(8,128)(2,1)S(1)} collective-permute-done((bf16[128,512]{1,0:T(8,128)(2,1)}, bf16[128,512]{1,0:T(8,128)(2,1)S(1)}, u32[]{:S(2)}, u32[]{:S(2)}) %collective-permute-start.2) | collective-permute-done | bytes 131104 | tf_op jit(solution)/shard_map/ppermute | solution.py:545
  28.2 2.3 collective-permute-start.3
  30.5 10.7 %collective-permute-done.3 = bf16[2,128,512]{2,1,0:T(8,128)(2,1)} collective-permute-done((bf16[2,128,512]{2,1,0:T(8,128)(2,1)S(1)}, bf16[2,128,512]{2,1,0:T(8,128)(2,1)}, u32[]{:S(2)}, u32[]{:S(2)}) %collective-permute-start.3) | collective-permute-done | bytes 262176 | tf_op jit(solution)/shard_map/ppermute | solution.py:545
  41.2 3.0 %collective-permute-start.5 = (bf16[2,4,16,1024]{3,2,1,0:T(8,128)(2,1)S(1)}, bf16[2,4,16,1024]{3,2,1,0:T(8,128)(2,1)S(1)}, u32[]{:S(2)}, u32[]{:S(2)}) collective-permute-start(bf16[2,4,16,1024]{3,2,1,0:T(8,128)(2,1)S(1)} %get-tuple-element.48), channel_id=1, source_target_pairs={{0,4},{1,5},{2,6},{3,7},{4,0},{5,1},{6,2},{7,3},{8,12},{9,13},{10,... | collective-permute-start | bytes 786440 | tf_op jit(solution)/shard_map/ppermute | solution.py:545
  44.2 1.0 pad_maximum_fusion.1.kv_own
  45.2 0.2 collective-permute-start.8
  45.5 1.0 constant_dynamic-update-slice_fusion.page_own
  46.4 1.4 collective-permute-start.7
  47.8 2.5 %collective-permute-done.5 = bf16[2,4,16,1024]{3,2,1,0:T(8,128)(2,1)S(1)} collective-permute-done((bf16[2,4,16,1024]{3,2,1,0:T(8,128)(2,1)S(1)}, bf16[2,4,16,1024]{3,2,1,0:T(8,128)(2,1)S(1)}, u32[]{:S(2)}, u32[]{:S(2)}) %collective-permute-start.5) | collective-permute-done | bytes 262176 | tf_op jit(solution)/shard_map/ppermute | solution.py:545
  50.4 1.3 collective-permute-start.9
  51.7 0.5 collective-permute-start.6
  52.2 5.7 %collective-permute-done.8.kv_y = bf16[4,128,512]{2,1,0:T(8,128)(2,1)S(1)} collective-permute-done((bf16[4,128,512]{2,1,0:T(8,128)(2,1)S(1)}, bf16[4,128,512]{2,1,0:T(8,128)(2,1)S(1)}, u32[]{:S(2)}, u32[]{:S(2)}) %collective-permute-start.8) | collective-permute-done | bytes 524320 | tf_op jit(solution)/shard_map/ppermute | solution.py:545
  57.9 11.2 %collective-permute-done.7.page_y = bf16[512,512]{1,0:T(8,128)(2,1)S(1)} collective-permute-done((bf16[512,512]{1,0:T(8,128)(2,1)S(1)}, bf16[512,512]{1,0:T(8,128)(2,1)S(1)}, u32[]{:S(2)}, u32[]{:S(2)}) %collective-permute-start.7) | collective-permute-done | bytes 524320 | tf_op jit(solution)/shard_map/ppermute | solution.py:545
  69.1 1.8 collective-permute-start.10
  70.9 0.5 collective-permute-start.12
  71.4 3.3 %collective-permute-done.6.refs_4_ = bf16[2,2,4,16,1024]{4,3,2,1,0:T(8,128)(2,1)S(1)} collective-permute-done((bf16[2,2,4,16,1024]{4,3,2,1,0:T(8,128)(2,1)S(1)}, bf16[2,2,4,16,1024]{4,3,2,1,0:T(8,128)(2,1)S(1)}, u32[]{:S(2)}, u32[]{:S(2)}) %collective-permute-start.6) | collective-permute-done | bytes 524320 | tf_op jit(solution)/shard_map/ppermute | solution.py:545
  74.7 0.9 collective-permute-start.16
  75.6 0.3 collective-permute-start.14
  75.8 0.3 collective-permute-start.18
  76.1 14.8 %attend.1.a_ref = bf16[2,512,512]{2,1,0:T(8,128)(2,1)S(1)} custom-call(bf16[8,2,128,256]{3,2,1,0:T(8,128)(2,1)} %copy-done.8, bf16[512,512]{1,0:T(8,128)(2,1)S(1)} %constant_dynamic-update-slice_fusion.page_own, bf16[512,512]{1,0:T(8,128)(2,1)S(1)} %collective-permute-done.7.page_y, bf16[512,512]{1,0:T(8,128)(2,1)S(1)} %collective-permute-done.10.page_c, ...), custom_call_target="tpu_custom_call" | custom-call | flops 7516192768 | bytes 6291456 | tf_op jit(solution)/shard_map/attend/pallas_call | solution.py:263
  91.1 0.3 collective-permute-start.17
  91.4 0.3 collective-permute-start.19
  91.7 0.2 collective-permute-start.15
  91.9 1.2 collective-permute-done.17.refs_3_
  93.1 0.7 collective-permute-done.19.refs_7_
  93.8 0.7 collective-permute-done.15.got_ref
  94.6 6.5 %project.1 = (bf16[128,2048]{1,0:T(8,128)(2,1)S(1)}, bf16[128,2048]{1,0:T(8,128)(2,1)}, bf16[128,2048]{1,0:T(8,128)(2,1)}, bf16[128,2048]{1,0:T(8,128)(2,1)}) custom-call(bf16[2,512,512]{2,1,0:T(8,128)(2,1)} %copy-done.5, bf16[512,512]{1,0:T(8,128)(2,1)S(1)} %collective-permute-done.15.got_ref, bf16[2,2,4,16,1024]{4,3,2,1,0:T(8,128)(2,1)S(1)} %pad_maximum_fusion.refs_0_, ...), custom_call_target="tpu_custom_call" | custom-call | flops 2147483648 | bytes 7340032 | tf_op jit(solution)/shard_map/project/pallas_call | solution.py:329
  101.1 3.5 %collective-permute-start.20 = (bf16[128,2048]{1,0:T(8,128)(2,1)}, bf16[128,2048]{1,0:T(8,128)(2,1)S(1)}, u32[]{:S(2)}, u32[]{:S(2)}) collective-permute-start(bf16[128,2048]{1,0:T(8,128)(2,1)} %get-tuple-element.42), channel_id=1, source_target_pairs={{0,6},{1,7},{2,4},{3,5},{4,2},{5,3},{6,0},{7,1},{8,14},{9,15},{10,... | collective-permute-start | bytes 1572872 | tf_op jit(solution)/shard_map/ppermute | solution.py:545
  104.6 0.4 collective-permute-start.21
  105.0 1.1 collective-permute-start.22
  106.4 0.2 reduce_window_sum.11
  106.9 10.2 %collective-permute-done.20 = bf16[128,2048]{1,0:T(8,128)(2,1)S(1)} collective-permute-done((bf16[128,2048]{1,0:T(8,128)(2,1)}, bf16[128,2048]{1,0:T(8,128)(2,1)S(1)}, u32[]{:S(2)}, u32[]{:S(2)}) %collective-permute-start.20) | collective-permute-done | bytes 524320 | tf_op jit(solution)/shard_map/ppermute | solution.py:545
  117.1 11.6 %collective-permute-done.21 = bf16[128,2048]{1,0:T(8,128)(2,1)S(1)} collective-permute-done((bf16[128,2048]{1,0:T(8,128)(2,1)}, bf16[128,2048]{1,0:T(8,128)(2,1)S(1)}, u32[]{:S(2)}, u32[]{:S(2)}) %collective-permute-start.21) | collective-permute-done | bytes 524320 | tf_op jit(solution)/shard_map/ppermute | solution.py:545
  128.7 2.2 route.1
  130.9 53.1 %all_to_all.15 = bf16[16,32,2048]{2,1,0:T(8,128)(2,1)S(1)} all-to-all(bf16[16,32,2048]{2,1,0:T(8,128)(2,1)S(1)} %bitcast.39), channel_id=1, replica_groups=mesh['grp'=2,'head'=16] {'head'}, dimensions={0} | all-to-all | bytes 4194304 | tf_op jit(solution)/shard_map/all_to_all | solution.py:722
  184.0 5.7 %expert.1 = bf16[512,2048]{1,0:T(8,128)(2,1)S(1)} custom-call(bf16[512,2048]{1,0:T(8,128)(2,1)S(1)} %bitcast.41, bf16[2048,1024]{1,0:T(8,128)(2,1)} %bitcast.58, bf16[512,2048]{1,0:T(8,128)(2,1)} %bitcast.59), custom_call_target="tpu_custom_call" | custom-call | flops 3221225472 | bytes 10485760 | tf_op jit(solution)/shard_map/expert/pallas_call | solution.py:485
  189.7 1.3 copy-done.1
  191.1 5.3 %all-to-all-start.2 = ((bf16[16,32,2048]{2,1,0:T(8,128)(2,1)}), bf16[16,32,2048]{2,1,0:T(8,128)(2,1)S(1)}, u32[]{:S(2)}, u32[]{:S(2)}) async-start(bf16[16,32,2048]{2,1,0:T(8,128)(2,1)} %bitcast.40), calls=%async_computation.2 | async-start | bytes 4194304 | tf_op jit(solution)/shard_map/all_to_all | solution.py:735
  196.4 47.3 %all-to-all-done.2 = bf16[16,32,2048]{2,1,0:T(8,128)(2,1)S(1)} async-done(((bf16[16,32,2048]{2,1,0:T(8,128)(2,1)}), bf16[16,32,2048]{2,1,0:T(8,128)(2,1)S(1)}, u32[]{:S(2)}, u32[]{:S(2)}) %all-to-all-start.2) | async-done | bytes 2097184 | tf_op jit(solution)/shard_map/all_to_all | solution.py:735
  243.7 1.2 copy-done.3
  245.0 1.6 combine.1
  (59 shorter events, 1.1 us)
Async XLA Ops:
  0.0 13.0 %copy-start = (bf16[16,16,2048]{2,1,0:T(8,128)(2,1)S(1)}, bf16[16,16,2048]{2,1,0:T(8,128)(2,1)}, u32[]{:S(2)}) copy-start(bf16[16,16,2048]{2,1,0:T(8,128)(2,1)} %param.14) | copy-start | bytes 3145732
  0.0 10.6 %copy-start.7 = (bf16[128,1,2,512]{3,2,1,0:T(2,128)(2,1)S(1)}, bf16[128,1,2,512]{3,2,1,0:T(2,128)(2,1)}, u32[]{:S(2)}) copy-start(bf16[128,1,2,512]{3,2,1,0:T(2,128)(2,1)} %param.11) | copy-start | bytes 786436
  2.6 38.5 %all-to-all-start = ((bf16[8,2,128,256]{3,2,1,0:T(8,128)(2,1)}), bf16[8,2,128,256]{3,2,1,0:T(8,128)(2,1)S(1)}, u32[]{:S(2)}, u32[]{:S(2)}) async-start(bf16[8,2,128,256]{3,2,1,0:T(8,128)(2,1)} %bitcast.10), calls=%async_computation | async-start | bytes 2097152 | tf_op jit(solution)/shard_map/all_to_all | solution.py:564
  7.2 23.3 %collective-permute-start = (bf16[256,512]{1,0:T(8,128)(2,1)}, bf16[256,512]{1,0:T(8,128)(2,1)S(1)}, u32[]{:S(2)}, u32[]{:S(2)}) collective-permute-start(bf16[256,512]{1,0:T(8,128)(2,1)} %bitcast.4), channel_id=1, source_target_pairs={{0,0},{1,1},{2,2},{3,3},{4,8},{5,9},{6,10},{7,11},{8,4},{9,5},{10,... | collective-permute-start | bytes 786440 | tf_op jit(solution)/shard_map/ppermute | solution.py:573
  10.5 20.0 %collective-permute-start.1 = (bf16[256,512]{1,0:T(8,128)(2,1)}, bf16[256,512]{1,0:T(8,128)(2,1)}, u32[]{:S(2)}, u32[]{:S(2)}) collective-permute-start(bf16[256,512]{1,0:T(8,128)(2,1)} %bitcast.4), channel_id=1, source_target_pairs={{0,8},{1,9},{2,10},{3,11},{4,0},{5,1},{6,2},{7,3},{8,12},{9,13},{1... | collective-permute-start | bytes 786440 | tf_op jit(solution)/shard_map/ppermute | solution.py:573
  11.8 16.4 %collective-permute-start.2 = (bf16[128,512]{1,0:T(8,128)(2,1)}, bf16[128,512]{1,0:T(8,128)(2,1)S(1)}, u32[]{:S(2)}, u32[]{:S(2)}) collective-permute-start(bf16[128,512]{1,0:T(8,128)(2,1)} %bitcast.36), channel_id=1, source_target_pairs={{0,4},{1,5},{2,6},{3,7},{4,0},{5,1},{6,2},{7,3},{8,12},{9,13},{10,... | collective-permute-start | bytes 393224 | tf_op jit(solution)/shard_map/ppermute | solution.py:545
  13.1 17.4 %collective-permute-start.4 = (bf16[2,4,16,1024]{3,2,1,0:T(8,128)(2,1)S(1)}, bf16[2,4,16,1024]{3,2,1,0:T(8,128)(2,1)S(1)}, u32[]{:S(2)}, u32[]{:S(2)}) collective-permute-start(bf16[2,4,16,1024]{3,2,1,0:T(8,128)(2,1)S(1)} %get-tuple-element.50), channel_id=1, source_target_pairs={{0,2},{1,3},{2,0},{3,1},{4,6},{5,7},{6,4},{7,5},{8,10},{9,11},{10,... | collective-permute-start | bytes 786440 | tf_op jit(solution)/shard_map/ppermute | solution.py:545
  28.2 13.0 %collective-permute-start.3 = (bf16[2,128,512]{2,1,0:T(8,128)(2,1)S(1)}, bf16[2,128,512]{2,1,0:T(8,128)(2,1)}, u32[]{:S(2)}, u32[]{:S(2)}) collective-permute-start(bf16[2,128,512]{2,1,0:T(8,128)(2,1)S(1)} %pad_maximum_fusion.2), channel_id=1, source_target_pairs={{0,8},{1,9},{2,10},{3,11},{4,12},{5,13},{6,14},{7,15},{8,0},{9,1},... | collective-permute-start | bytes 786440 | tf_op jit(solution)/shard_map/ppermute | solution.py:545
  41.2 9.2 %copy-start.8 = (bf16[8,2,128,256]{3,2,1,0:T(8,128)(2,1)}, bf16[8,2,128,256]{3,2,1,0:T(8,128)(2,1)S(1)}, u32[]{:S(2)}) copy-start(bf16[8,2,128,256]{3,2,1,0:T(8,128)(2,1)S(1)} %all-to-all-done.q_hbm) | copy-start | bytes 3145732
  41.2 9.1 %collective-permute-start.5 = (bf16[2,4,16,1024]{3,2,1,0:T(8,128)(2,1)S(1)}, bf16[2,4,16,1024]{3,2,1,0:T(8,128)(2,1)S(1)}, u32[]{:S(2)}, u32[]{:S(2)}) collective-permute-start(bf16[2,4,16,1024]{3,2,1,0:T(8,128)(2,1)S(1)} %get-tuple-element.48), channel_id=1, source_target_pairs={{0,4},{1,5},{2,6},{3,7},{4,0},{5,1},{6,2},{7,3},{8,12},{9,13},{10,... | collective-permute-start | bytes 786440 | tf_op jit(solution)/shard_map/ppermute | solution.py:545
  45.2 12.6 %collective-permute-start.8 = (bf16[4,128,512]{2,1,0:T(8,128)(2,1)S(1)}, bf16[4,128,512]{2,1,0:T(8,128)(2,1)S(1)}, u32[]{:S(2)}, u32[]{:S(2)}) collective-permute-start(bf16[4,128,512]{2,1,0:T(8,128)(2,1)S(1)} %pad_maximum_fusion.1.kv_own), channel_id=1, source_target_pairs={{0,2},{1,3},{2,0},{3,1},{4,6},{5,7},{6,4},{7,5},{8,10},{9,11},{10,... | collective-permute-start | bytes 1572872 | tf_op jit(solution)/shard_map/ppermute | solution.py:545
  46.4 22.7 %collective-permute-start.7 = (bf16[512,512]{1,0:T(8,128)(2,1)S(1)}, bf16[512,512]{1,0:T(8,128)(2,1)S(1)}, u32[]{:S(2)}, u32[]{:S(2)}) collective-permute-start(bf16[512,512]{1,0:T(8,128)(2,1)S(1)} %constant_dynamic-update-slice_fusion.page_own), channel_id=1, source_target_pairs={{0,2},{1,3},{2,0},{3,1},{4,6},{5,7},{6,4},{7,5},{8,10},{9,11},{10,... | collective-permute-start | bytes 1572872 | tf_op jit(solution)/shard_map/ppermute | solution.py:545
  50.4 18.7 %collective-permute-start.9 = (bf16[2,2,4,16,1024]{4,3,2,1,0:T(8,128)(2,1)S(1)}, bf16[2,2,4,16,1024]{4,3,2,1,0:T(8,128)(2,1)S(1)}, u32[]{:S(2)}, u32[]{:S(2)}) collective-permute-start(bf16[2,2,4,16,1024]{4,3,2,1,0:T(8,128)(2,1)S(1)} %pad_maximum_fusion.refs_0_), channel_id=1, source_target_pairs={{0,16},{16,0},{1,17},{17,1},{2,18},{18,2},{3,19},{19,3},{4,20},{20... | collective-permute-start | bytes 1572872 | tf_op jit(solution)/shard_map/ppermute | solution.py:545
  51.7 23.0 %collective-permute-start.6 = (bf16[2,2,4,16,1024]{4,3,2,1,0:T(8,128)(2,1)S(1)}, bf16[2,2,4,16,1024]{4,3,2,1,0:T(8,128)(2,1)S(1)}, u32[]{:S(2)}, u32[]{:S(2)}) collective-permute-start(bf16[2,2,4,16,1024]{4,3,2,1,0:T(8,128)(2,1)S(1)} %pad_maximum_fusion.refs_0_), channel_id=1, source_target_pairs={{0,8},{1,9},{2,10},{3,11},{4,12},{5,13},{6,14},{7,15},{8,0},{9,1},... | collective-permute-start | bytes 1572872 | tf_op jit(solution)/shard_map/ppermute | solution.py:545
  69.1 6.5 %collective-permute-start.10 = (bf16[512,512]{1,0:T(8,128)(2,1)S(1)}, bf16[512,512]{1,0:T(8,128)(2,1)S(1)}, u32[]{:S(2)}, u32[]{:S(2)}) collective-permute-start(bf16[512,512]{1,0:T(8,128)(2,1)S(1)} %constant_dynamic-update-slice_fusion.page_own), channel_id=1, source_target_pairs={{0,1},{1,0},{2,3},{3,2},{4,5},{5,4},{6,7},{7,6},{8,9},{9,8},{10,11... | collective-permute-start | bytes 1572872 | tf_op jit(solution)/shard_map/ppermute | solution.py:545
  70.9 5.0 %collective-permute-start.11 = (bf16[512,512]{1,0:T(8,128)(2,1)S(1)}, bf16[512,512]{1,0:T(8,128)(2,1)S(1)}, u32[]{:S(2)}, u32[]{:S(2)}) collective-permute-start(bf16[512,512]{1,0:T(8,128)(2,1)S(1)} %collective-permute-done.7.page_y), channel_id=1, source_target_pairs={{0,1},{1,0},{2,3},{3,2},{4,5},{5,4},{6,7},{7,6},{8,9},{9,8},{10,11... | collective-permute-start | bytes 1572872 | tf_op jit(solution)/shard_map/ppermute | solution.py:545
  70.9 5.2 %collective-permute-start.12 = (bf16[4,128,512]{2,1,0:T(8,128)(2,1)S(1)}, bf16[4,128,512]{2,1,0:T(8,128)(2,1)S(1)}, u32[]{:S(2)}, u32[]{:S(2)}) collective-permute-start(bf16[4,128,512]{2,1,0:T(8,128)(2,1)S(1)} %pad_maximum_fusion.1.kv_own), channel_id=1, source_target_pairs={{0,1},{1,0},{2,3},{3,2},{4,5},{5,4},{6,7},{7,6},{8,9},{9,8},{10,11... | collective-permute-start | bytes 1572872 | tf_op jit(solution)/shard_map/ppermute | solution.py:545
  71.4 4.7 %collective-permute-start.13 = (bf16[4,128,512]{2,1,0:T(8,128)(2,1)S(1)}, bf16[4,128,512]{2,1,0:T(8,128)(2,1)S(1)}, u32[]{:S(2)}, u32[]{:S(2)}) collective-permute-start(bf16[4,128,512]{2,1,0:T(8,128)(2,1)S(1)} %collective-permute-done.8.kv_y), channel_id=1, source_target_pairs={{0,1},{1,0},{2,3},{3,2},{4,5},{5,4},{6,7},{7,6},{8,9},{9,8},{10,11... | collective-permute-start | bytes 1572872 | tf_op jit(solution)/shard_map/ppermute | solution.py:545
  74.7 17.2 %collective-permute-start.16 = (bf16[2,2,4,16,1024]{4,3,2,1,0:T(8,128)(2,1)S(1)}, bf16[2,2,4,16,1024]{4,3,2,1,0:T(8,128)(2,1)S(1)}, u32[]{:S(2)}, u32[]{:S(2)}) collective-permute-start(bf16[2,2,4,16,1024]{4,3,2,1,0:T(8,128)(2,1)S(1)} %pad_maximum_fusion.refs_0_), channel_id=1, source_target_pairs={{0,1},{1,0},{2,3},{3,2},{4,5},{5,4},{6,7},{7,6},{8,9},{9,8},{10,11... | collective-permute-start | bytes 1572872 | tf_op jit(solution)/shard_map/ppermute | solution.py:545
  75.6 15.5 %collective-permute-start.14 = (bf16[2,2,4,16,1024]{4,3,2,1,0:T(8,128)(2,1)S(1)}, bf16[2,2,4,16,1024]{4,3,2,1,0:T(8,128)(2,1)S(1)}, u32[]{:S(2)}, u32[]{:S(2)}) collective-permute-start(bf16[2,2,4,16,1024]{4,3,2,1,0:T(8,128)(2,1)S(1)} %collective-permute-done.6.refs_4_), channel_id=1, source_target_pairs={{0,16},{16,0},{1,17},{17,1},{2,18},{18,2},{3,19},{19,3},{4,20},{20... | collective-permute-start | bytes 1572872 | tf_op jit(solution)/shard_map/ppermute | solution.py:545
  75.8 16.1 %collective-permute-start.18 = (bf16[2,2,4,16,1024]{4,3,2,1,0:T(8,128)(2,1)S(1)}, bf16[2,2,4,16,1024]{4,3,2,1,0:T(8,128)(2,1)S(1)}, u32[]{:S(2)}, u32[]{:S(2)}) collective-permute-start(bf16[2,2,4,16,1024]{4,3,2,1,0:T(8,128)(2,1)S(1)} %collective-permute-done.6.refs_4_), channel_id=1, source_target_pairs={{0,1},{1,0},{2,3},{3,2},{4,5},{5,4},{6,7},{7,6},{8,9},{9,8},{10,11... | collective-permute-start | bytes 1572872 | tf_op jit(solution)/shard_map/ppermute | solution.py:545
  91.0 3.6 %copy-start.5 = (bf16[2,512,512]{2,1,0:T(8,128)(2,1)}, bf16[2,512,512]{2,1,0:T(8,128)(2,1)S(1)}, u32[]{:S(2)}) copy-start(bf16[2,512,512]{2,1,0:T(8,128)(2,1)S(1)} %attend.1.a_ref) | copy-start | bytes 3145732
  91.0 15.1 %copy-start.9 = (s32[128,1,2]{0,2,1:T(2,128)S(1)}, s32[128,1,2]{0,2,1:T(2,128)}, u32[]{:S(2)}) copy-start(s32[128,1,2]{0,2,1:T(2,128)} %param.16) | copy-start | bytes 3076
  91.0 37.6 %copy-start.4 = (bf16[128,1,2048]{2,0,1:T(8,128)(2,1)S(1)}, bf16[128,1,2048]{2,0,1:T(8,128)(2,1)}, u32[]{:S(2)}) copy-start(bf16[128,1,2048]{2,0,1:T(8,128)(2,1)} %param.13) | copy-start | bytes 1572868
  91.1 37.6 %copy-start.6 = (f32[2048]{0:T(1024)S(1)}, f32[2048]{0:T(1024)}, u32[]{:S(2)}) copy-start(f32[2048]{0:T(1024)} %param.15) | copy-start | bytes 24580
  91.1 3.5 %copy-start.11 = (bf16[2,2,4,16,1024]{4,3,2,1,0:T(8,128)(2,1)}, bf16[2,2,4,16,1024]{4,3,2,1,0:T(8,128)(2,1)S(1)}, u32[]{:S(2)}) copy-start(bf16[2,2,4,16,1024]{4,3,2,1,0:T(8,128)(2,1)S(1)} %collective-permute-done.14.refs_6_) | copy-start | bytes 1572868
  91.1 2.0 collective-permute-start.17
  91.4 2.4 collective-permute-start.19
  91.7 2.9 %collective-permute-start.15 = (bf16[512,512]{1,0:T(8,128)(2,1)S(1)}, bf16[512,512]{1,0:T(8,128)(2,1)S(1)}, u32[]{:S(2)}, u32[]{:S(2)}) collective-permute-start(bf16[512,512]{1,0:T(8,128)(2,1)S(1)} %slice_bitcast_fusion), channel_id=1, source_target_pairs={{0,1},{1,0},{2,3},{3,2},{4,5},{5,4},{6,7},{7,6},{8,9},{9,8},{10,11... | collective-permute-start | bytes 1572872 | tf_op jit(solution)/shard_map/ppermute | solution.py:545
  93.8 0.8 copy-start.12
  101.1 15.9 %collective-permute-start.20 = (bf16[128,2048]{1,0:T(8,128)(2,1)}, bf16[128,2048]{1,0:T(8,128)(2,1)S(1)}, u32[]{:S(2)}, u32[]{:S(2)}) collective-permute-start(bf16[128,2048]{1,0:T(8,128)(2,1)} %get-tuple-element.42), channel_id=1, source_target_pairs={{0,6},{1,7},{2,4},{3,5},{4,2},{5,3},{6,0},{7,1},{8,14},{9,15},{10,... | collective-permute-start | bytes 1572872 | tf_op jit(solution)/shard_map/ppermute | solution.py:545
  104.6 24.0 %collective-permute-start.21 = (bf16[128,2048]{1,0:T(8,128)(2,1)}, bf16[128,2048]{1,0:T(8,128)(2,1)S(1)}, u32[]{:S(2)}, u32[]{:S(2)}) collective-permute-start(bf16[128,2048]{1,0:T(8,128)(2,1)} %get-tuple-element.43), channel_id=1, source_target_pairs={{0,4},{1,5},{2,6},{3,7},{4,0},{5,1},{6,2},{7,3},{8,12},{9,13},{10,... | collective-permute-start | bytes 1572872 | tf_op jit(solution)/shard_map/ppermute | solution.py:545
  105.0 23.7 %collective-permute-start.22 = (bf16[128,2048]{1,0:T(8,128)(2,1)}, bf16[128,2048]{1,0:T(8,128)(2,1)}, u32[]{:S(2)}, u32[]{:S(2)}) collective-permute-start(bf16[128,2048]{1,0:T(8,128)(2,1)} %get-tuple-element.44), channel_id=1, source_target_pairs={{0,2},{1,3},{2,0},{3,1},{4,6},{5,7},{6,4},{7,5},{8,10},{9,11},{10,... | collective-permute-start | bytes 1572872 | tf_op jit(solution)/shard_map/ppermute | solution.py:545
  130.9 53.1 %copy-start.2 = (f32[128,2048]{1,0:T(8,128)}, f32[128,2048]{1,0:T(8,128)S(1)}, u32[]{:S(2)}) copy-start(f32[128,2048]{1,0:T(8,128)S(1)} %get-tuple-element.46.stream_ref) | copy-start | bytes 3145732
  189.7 1.3 copy-start.1
  191.1 5.3 %copy-start.10 = (f32[128,1,2]{0,2,1:T(2,128)S(1)}, f32[128,1,2]{0,2,1:T(2,128)}, u32[]{:S(2)}) copy-start(f32[128,1,2]{0,2,1:T(2,128)} %param.17) | copy-start | bytes 3076
  191.1 52.7 %all-to-all-start.2 = ((bf16[16,32,2048]{2,1,0:T(8,128)(2,1)}), bf16[16,32,2048]{2,1,0:T(8,128)(2,1)S(1)}, u32[]{:S(2)}, u32[]{:S(2)}) async-start(bf16[16,32,2048]{2,1,0:T(8,128)(2,1)} %bitcast.40), calls=%async_computation.2 | async-start | bytes 4194304 | tf_op jit(solution)/shard_map/all_to_all | solution.py:735
  243.7 1.2 copy-start.3

commit v15 on v13

--- a/solution.py
+++ b/solution.py
@@ -157,20 +157,21 @@
     earlier_group = me // members > 0
     core = lax.rem(me, 2)
     chip = jnp.bitwise_and(me // 2, members // 2 - 1)
-    copies = []
+    copies = [[] for _ in range(6)]
 
     def bring(source, target, sem):
         copy = pltpu.make_async_copy(source, target, sems.at[sem])
         copy.start()
-        copies.append(copy)
+        copies[sem].append(copy)
 
     for member in range(members):
         for head in range(heads):
             bring(q_hbm.at[member, head], q_ref.at[head, pl.ds(member * piece, piece)], 0)
-    place = 0
-    for page in (page_own, page_y, page_c, page_cy):
+    place, places = 0, []
+    for sem, page in enumerate((page_own, page_y, page_c, page_cy)):
         count = page.shape[0]
-        bring(page, old_ref.at[pl.ds(place, count)], 1)
+        bring(page, old_ref.at[pl.ds(place, count)], 1 + sem)
+        places.append(place)
         place += count
     for flip, pieces_of in ((0, kv_own), (2, kv_y), (1, kv_c), (3, kv_cy)):
         for t in range(planes):
@@ -179,9 +180,13 @@
             )
             start = pl.multiple_of(number * piece, piece)
             area = 0 if t * (members // 2) >= members else length
-            bring(pieces_of.at[t], kv_ref.at[pl.ds(area + start, piece)], 2)
-    for copy in copies:
-        copy.wait()
+            bring(pieces_of.at[t], kv_ref.at[pl.ds(area + start, piece)], 5)
+    def arrive(sem):
+        for copy in copies[sem]:
+            copy.wait()
+        copies[sem] = []
+
+    arrive(0)
     scale = width**-0.5 * LOG2_E
     scores = [s0, s1]
     blocks = length // block
@@ -230,6 +235,12 @@
 
     running = None
     for part in pieces(0):
+        if part[0] != "old":
+            arrive(5)
+        else:
+            for sem, start in enumerate(places):
+                if start < part[1] + part[2]:
+                    arrive(1 + sem)
         running = make_scores(0, part, running)
     for unit, (head, b) in enumerate(units):
         top = jnp.max(running, 1, keepdims=True)
@@ -267,7 +278,7 @@
             pltpu.VMEM((2 * length, 2 * width), BF16),
             pltpu.VMEM((block, keys), F32),
             pltpu.VMEM((block, keys), F32),
-            pltpu.SemaphoreType.DMA((3,)),
+            pltpu.SemaphoreType.DMA((6,)),
         ],
         compiler_params=pltpu.CompilerParams(vmem_limit_bytes=HIGH_VMEM),
         cost_estimate=pl.CostEstimate(
@@ -279,41 +290,57 @@
     )(q, *pages, *kvs)
 
 
-def project_pair_kernel(a_ref, got_ref, *refs):
-    near, far, outs, (w_ref, sems) = refs[:4], refs[4:8], refs[8:-2], refs[-2:]
+def project_pair_kernel(a_hbm, got_hbm, *refs):
+    near, far, outs, (w_ref, all_ref, out_ref, sems) = refs[:4], refs[4:8], refs[8:-4], refs[-4:]
     me = lax.axis_index("head")
     half = lax.axis_index("grp")
     core = lax.rem(me, 2)
     steps, sides, heads, share, columns = near[0].shape
     width = w_ref.shape[1]
-    copies = []
-    for first, given in ((0, near), (steps, far)):
-        for flip, x, pieces_of in zip((0, 1, 0, 1), (0, 0, 1, 1), given):
-            column = pl.multiple_of(jnp.bitwise_xor(half, x) * columns, columns)
-            for t in range(steps):
-                for u in range(sides):
-                    number = jnp.bitwise_xor(me, flip ^ (2 * u) ^ (4 * (first + t)))
-                    row = pl.multiple_of(number * share, share)
-                    copy = pltpu.make_async_copy(
-                        pieces_of.at[t, u],
-                        w_ref.at[:, pl.ds(row, share), pl.ds(column, columns)],
-                        sems.at[0],
-                    )
-                    copy.start()
-                    copies.append(copy)
-    for copy in copies:
+    side = got_hbm.shape[1]
+    bring = [[], [], []]
+    for other, source in enumerate((a_hbm.at[0], got_hbm)):
+        at = pl.ds(pl.multiple_of(jnp.bitwise_xor(core, other) * side, side), side)
+        bring[2].append(pltpu.make_async_copy(source, all_ref.at[:, at], sems.at[2]))
+    for x in range(2):
+        column = pl.multiple_of(jnp.bitwise_xor(half, x) * columns, columns)
+        for first, given in ((0, near), (steps, far)):
+            for flip in range(2):
+                for t in range(steps):
+                    for u in range(sides):
+                        number = jnp.bitwise_xor(me, flip ^ (2 * u) ^ (4 * (first + t)))
+                        row = pl.multiple_of(number * share, share)
+                        bring[x].append(
+                            pltpu.make_async_copy(
+                                given[2 * x + flip].at[t, u],
+                                w_ref.at[:, pl.ds(row, share), pl.ds(column, columns)],
+                                sems.at[x],
+                            )
+                        )
+    for copies in (bring[2], bring[0], bring[1]):
+        for copy in copies:
+            copy.start()
+    for copy in bring[2]:
         copy.wait()
-    acc = None
-    for k in range(heads):
-        mine = k < heads // 2
-        at = pl.ds((k % (heads // 2)) * width, width)
-        rows_of = a_ref[0, :, at] if mine else got_ref[:, at]
-        head = jnp.bitwise_xor(core, 0 if mine else 1) * (heads // 2) + k % (heads // 2)
-        part = jnp.dot(rows_of, w_ref[head], preferred_element_type=F32)
-        acc = part if acc is None else acc + part
     rows = outs[0].shape[0]
-    for k, out in enumerate(outs):
-        out[...] = acc[k * rows : (k + 1) * rows].astype(BF16)
+    tile = min(512, columns)
+    back = []
+    for x in range(2):
+        for copy in bring[x]:
+            copy.wait()
+        for first in range(0, columns, tile):
+            column = jnp.bitwise_xor(half, x) * columns + first
+            at = pl.ds(pl.multiple_of(column, tile), tile)
+            w = w_ref[:, :, at].reshape(heads * width, tile)
+            out_ref[:, at] = jnp.dot(all_ref[...], w, preferred_element_type=F32).astype(BF16)
+            for k, out in enumerate(outs):
+                copy = pltpu.make_async_copy(
+                    out_ref.at[pl.ds(k * rows, rows), at], out.at[:, at], sems.at[3]
+                )
+                copy.start()
+                back.append(copy)
+    for copy in back:
+        copy.wait()
 
 
 def project_pair(a, got, near, far, parts):
@@ -323,12 +350,14 @@
     model = 2 * columns
     return pl.pallas_call(
         project_pair_kernel,
-        out_shape=[jax.ShapeDtypeStruct((rows // parts, model), BF16)] * parts,
-        in_specs=[in_vmem(), in_vmem()] + [in_hbm()] * 8,
-        out_specs=[in_vmem()] * parts,
+        out_shape=[pltpu.HBM((rows // parts, model), BF16)] * parts,
+        in_specs=[in_hbm()] * 10,
+        out_specs=[in_hbm()] * parts,
         scratch_shapes=[
             pltpu.VMEM((heads, width, model), BF16),
-            pltpu.SemaphoreType.DMA((1,)),
+            pltpu.VMEM((rows, heads * width), BF16),
+            pltpu.VMEM((rows, model), BF16),
+            pltpu.SemaphoreType.DMA((4,)),
         ],
         compiler_params=pltpu.CompilerParams(vmem_limit_bytes=HIGH_VMEM),
         cost_estimate=pl.CostEstimate(
@@ -478,7 +507,7 @@
 
     return pl.pallas_call(
         kernel,
-        out_shape=jax.ShapeDtypeStruct((rows, model), BF16),
+        out_shape=pltpu.HBM((rows, model), BF16),
         in_specs=[in_hbm()] * 3,
         out_specs=in_hbm(),
         scratch_shapes=[
@@ -498,18 +527,22 @@
     )(x, w_in, w_down)
 
 
-def combine_kernel(seqs, back_ref, stream_ref, slots_ref, gates_ref, o_ref):
+def combine_kernel(
+    seqs, back_ref, stream_hbm, slots_ref, gates_ref, o_ref, stream_ref, sem
+):
+    bring = pltpu.make_async_copy(stream_hbm, stream_ref, sem.at[0])
+    bring.start()
     slots = back_ref.shape[0]
     rows = stream_ref.shape[0]
     place = lax.broadcasted_iota(jnp.int32, (rows, slots), 1)
-    total = stream_ref[...]
     gathered = None
     for k in range(slots_ref.shape[1]):
         pick = (place == slots_ref[:, k : k + 1]).astype(BF16)
         picked = jnp.dot(pick, back_ref[...], preferred_element_type=F32)
         part = picked * gates_ref[:, k : k + 1]
         gathered = part if gathered is None else gathered + part
-    out = (total + gathered).astype(BF16)
+    bring.wait()
+    out = (stream_ref[...] + gathered).astype(BF16)
     local_rows = rows // seqs
     for seq in range(seqs):
         o_ref[seq] = out[seq * local_rows : (seq + 1) * local_rows]
@@ -522,8 +555,9 @@
     return pl.pallas_call(
         functools.partial(combine_kernel, seqs),
         out_shape=jax.ShapeDtypeStruct((seqs, rows // seqs, model), BF16),
-        in_specs=[in_vmem()] * 4,
+        in_specs=[in_vmem(), in_hbm(), in_vmem(), in_vmem()],
         out_specs=in_vmem(),
+        scratch_shapes=[pltpu.VMEM((rows, model), F32), pltpu.SemaphoreType.DMA((1,))],
         compiler_params=pltpu.CompilerParams(vmem_limit_bytes=HIGH_VMEM),
         cost_estimate=pl.CostEstimate(
             flops=2 * top * slots * rows * model,
@@ -592,7 +626,7 @@
     w_other = lax.dynamic_index_in_dim(w_both, 1 - b, 0, keepdims=False)
     w_near = jnp.stack([w_same, flipped(w_other, "head", plane_bit)], 0)
     w_near_x = flipped(w_near, "grp", 1)
-    w_far = [flipped(w_same, "head", 2 * plane_bit), flipped(w_other, "head", 3 * plane_bit)]
+    w_far = flipped(w_near, "head", members)
     pages_y, kv_y, own_pages, kv_own, w_near_x = lax.optimization_barrier(
         (pages_y, kv_y, own_pages, kv_own, w_near_x)
     )
@@ -600,7 +634,6 @@
     kv_cy = flipped(kv_y, "head", 1)
     pages_c = flipped(own_pages, "head", 1)
     pages_cy = flipped(pages_y, "head", 1)
-    w_far = jnp.stack(w_far, 0)
     q, w_far = lax.optimization_barrier((q, w_far))
     w_far_x = flipped(w_far, "grp", 1)
     a = attend_pair(q, (own_pages, pages_y, pages_c, pages_cy), (kv_own, kv_y, kv_c, kv_cy))

time: 251 us -> 241 us (0.960)
  waiting for transfers between devices: 129 us -> 119 us
    ppermute x23 -> x22, waiting for transfers between devices: 82.2 us -> 71.3 us  [flipped(): return lax.ppermute(value, axis, pairs)]
    ppermute x23 -> x22, starting transfers between devices: 15.5 us -> 15.8 us  [flipped(): return lax.ppermute(value, axis, pairs)]
  transfers between devices with their start and end apart: 27 -> 26, of which waited for: 14 -> 14; matrix products, arithmetic and copies ran while one was open for 1% -> 2% of each run, Pallas kernels for 6% -> 6%
where the time goes in v15:
time: 241 us
  waiting for transfers between devices  119 us (49%)
  blocking collectives  53.5 us (22%)
  starting transfers between devices  30 us (12%)
  Pallas kernels  29.6 us (12%)
  local copies, waits for them, and re-layouts  7.27 us (3%)
    ppermute x22, waiting for transfers between devices, flipped(): return lax.ppermute(value, axis, pairs)  71.3 us
    all_to_all x1, blocking collectives, local(): lax.all_to_all(outgoing.reshape(n, slots // n, model), 'head', split_axis...  53.5 us
    all_to_all x1, waiting for transfers between devices, local(): lax.all_to_all(answered, 'head', split_axis=0, concat_axis=0, tiled=True)  47.3 us
    ppermute x22, starting transfers between devices, flipped(): return lax.ppermute(value, axis, pairs)  15.8 us
    pallas_call x1, Pallas kernels, attend_pair(): pl.pallas_call(functools.partial(attend_pair_kernel, block, chunk, width)...  15.4 us
    pallas_call x1, Pallas kernels, expert_pair(): pl.pallas_call(kernel, out_shape=pltpu.HBM((rows, model), BF16), in_specs...  6.87 us
    all_to_all x1, starting transfers between devices, local(): lax.all_to_all(answered, 'head', split_axis=0, concat_axis=0, tiled=True)  5.13 us
  transfers between devices with their start and end apart: 26, of which 14 were waited for; matrix products, arithmetic and copies ran while one was open for 2% of the time, Pallas kernels for 6%

profile of v15, /device:TPU:13, one launch (start us, length us, event | category | flops | bytes accessed | tf_op | source)
XLA Modules:
  0.0 240.9 jit_solution(1812025598705134246)
XLA Ops:
  0.0 2.6 %copy.29 = bf16[16,128,256]{2,1,0:T(8,128)(2,1)} copy(bf16[16,128,256]{2,0,1:T(8,128)(2,1)} %bitcast.55) | data formatting | bytes 2097152 | tf_op jit(solution)/shard_map/transpose | solution.py:590
  2.6 4.6 %all-to-all-start = ((bf16[8,2,128,256]{3,2,1,0:T(8,128)(2,1)}), bf16[8,2,128,256]{3,2,1,0:T(8,128)(2,1)S(1)}, u32[]{:S(2)}, u32[]{:S(2)}) async-start(bf16[8,2,128,256]{3,2,1,0:T(8,128)(2,1)} %bitcast.9), calls=%async_computation | async-start | bytes 2097152 | tf_op jit(solution)/shard_map/all_to_all | solution.py:592
  7.4 0.3 collective-permute-start.5
  7.7 0.5 constant_dynamic-slice_fusion.2
  8.3 0.1 collective-permute-start.2
  8.5 4.4 %collective-permute-start = (bf16[256,512]{1,0:T(8,128)(2,1)}, bf16[256,512]{1,0:T(8,128)(2,1)S(1)}, u32[]{:S(2)}, u32[]{:S(2)}) collective-permute-start(bf16[256,512]{1,0:T(8,128)(2,1)} %bitcast.65), channel_id=1, source_target_pairs={{0,0},{1,1},{2,2},{3,3},{4,8},{5,9},{6,10},{7,11},{8,4},{9,5},{10,... | collective-permute-start | bytes 786440 | tf_op jit(solution)/shard_map/ppermute | solution.py:601
  13.0 2.4 collective-permute-start.3
  15.4 9.0 %collective-permute-done.2 = bf16[128,512]{1,0:T(8,128)(2,1)S(1)} collective-permute-done((bf16[128,512]{1,0:T(8,128)(2,1)S(1)}, bf16[128,512]{1,0:T(8,128)(2,1)S(1)}, u32[]{:S(2)}, u32[]{:S(2)}) %collective-permute-start.2) | collective-permute-done | bytes 131104 | tf_op jit(solution)/shard_map/ppermute | solution.py:573
  24.4 1.4 collective-permute-start.4
  25.8 7.4 %collective-permute-done.3 = bf16[128,512]{1,0:T(8,128)(2,1)} collective-permute-done((bf16[128,512]{1,0:T(8,128)(2,1)S(1)}, bf16[128,512]{1,0:T(8,128)(2,1)}, u32[]{:S(2)}, u32[]{:S(2)}) %collective-permute-start.3) | collective-permute-done | bytes 131104 | tf_op jit(solution)/shard_map/ppermute | solution.py:573
  33.2 6.0 %collective-permute-done.4 = bf16[128,512]{1,0:T(8,128)(2,1)} collective-permute-done((bf16[128,512]{1,0:T(8,128)(2,1)S(1)}, bf16[128,512]{1,0:T(8,128)(2,1)}, u32[]{:S(2)}, u32[]{:S(2)}) %collective-permute-start.4) | collective-permute-done | bytes 131104 | tf_op jit(solution)/shard_map/ppermute | solution.py:573
  39.3 1.3 pad_maximum_fusion.1.kv_own
  40.6 0.3 collective-permute-start.9
  41.0 1.0 constant_dynamic-update-slice_fusion.page_own
  41.9 1.2 collective-permute-start.8
  43.2 3.5 %collective-permute-done.6 = bf16[2,4,16,1024]{3,2,1,0:T(8,128)(2,1)S(1)} collective-permute-done((bf16[2,4,16,1024]{3,2,1,0:T(8,128)(2,1)S(1)}, bf16[2,4,16,1024]{3,2,1,0:T(8,128)(2,1)S(1)}, u32[]{:S(2)}, u32[]{:S(2)}) %collective-permute-start.6) | collective-permute-done | bytes 262176 | tf_op jit(solution)/shard_map/ppermute | solution.py:573
  46.7 1.3 collective-permute-start.10
  48.0 5.6 %collective-permute-done.9.kv_y = bf16[4,128,512]{2,1,0:T(8,128)(2,1)S(1)} collective-permute-done((bf16[4,128,512]{2,1,0:T(8,128)(2,1)S(1)}, bf16[4,128,512]{2,1,0:T(8,128)(2,1)S(1)}, u32[]{:S(2)}, u32[]{:S(2)}) %collective-permute-start.9) | collective-permute-done | bytes 524320 | tf_op jit(solution)/shard_map/ppermute | solution.py:573
  53.6 11.2 %collective-permute-done.8.page_y = bf16[512,512]{1,0:T(8,128)(2,1)S(1)} collective-permute-done((bf16[512,512]{1,0:T(8,128)(2,1)S(1)}, bf16[512,512]{1,0:T(8,128)(2,1)S(1)}, u32[]{:S(2)}, u32[]{:S(2)}) %collective-permute-start.8) | collective-permute-done | bytes 524320 | tf_op jit(solution)/shard_map/ppermute | solution.py:573
  64.9 1.3 collective-permute-start.11
  66.2 0.5 collective-permute-start.13
  66.7 4.0 %collective-permute-done.7.refs_4_ = bf16[2,2,4,16,1024]{4,3,2,1,0:T(8,128)(2,1)S(1)} collective-permute-done((bf16[2,2,4,16,1024]{4,3,2,1,0:T(8,128)(2,1)S(1)}, bf16[2,2,4,16,1024]{4,3,2,1,0:T(8,128)(2,1)S(1)}, u32[]{:S(2)}, u32[]{:S(2)}) %collective-permute-start.7) | collective-permute-done | bytes 524320 | tf_op jit(solution)/shard_map/ppermute | solution.py:573
  70.8 0.6 collective-permute-start.17
  71.4 0.3 collective-permute-start.15
  71.7 0.3 collective-permute-start.19
  72.0 15.4 %attend.1.a_hbm = bf16[2,512,512]{2,1,0:T(8,128)(2,1)S(1)} custom-call(bf16[8,2,128,256]{3,2,1,0:T(8,128)(2,1)} %copy-done.8, bf16[512,512]{1,0:T(8,128)(2,1)S(1)} %constant_dynamic-update-slice_fusion.page_own, bf16[512,512]{1,0:T(8,128)(2,1)S(1)} %collective-permute-done.8.page_y, bf16[512,512]{1,0:T(8,128)(2,1)S(1)} %collective-permute-done.11.page_c, ...), custom_call_target="tpu_custom_call" | custom-call | flops 7516192768 | bytes 6291456 | tf_op jit(solution)/shard_map/attend/pallas_call | solution.py:270
  87.5 0.3 collective-permute-start.18
  87.8 0.3 collective-permute-start.20
  88.0 0.2 collective-permute-start.16
  88.3 1.2 collective-permute-done.18.refs_3_
  89.4 0.7 collective-permute-done.20.refs_7_
  90.2 0.7 collective-permute-done.16.got_hbm
  90.9 4.4 %project.1 = (bf16[128,2048]{1,0:T(8,128)(2,1)}, bf16[128,2048]{1,0:T(8,128)(2,1)}, bf16[128,2048]{1,0:T(8,128)(2,1)}, bf16[128,2048]{1,0:T(8,128)(2,1)}) custom-call(bf16[2,512,512]{2,1,0:T(8,128)(2,1)S(1)} %attend.1.a_hbm, bf16[512,512]{1,0:T(8,128)(2,1)S(1)} %collective-permute-done.16.got_hbm, bf16[2,2,4,16,1024]{4,3,2,1,0:T(8,128)(2,1)S(1)} %pad_maximum_fusion.refs_0_, ...), custom_call_target="tpu_custom_call" | custom-call | flops 2147483648 | bytes 7340032 | tf_op jit(solution)/shard_map/project/pallas_call | solution.py:351
  95.3 3.5 %collective-permute-start.21 = (bf16[128,2048]{1,0:T(8,128)(2,1)}, bf16[128,2048]{1,0:T(8,128)(2,1)S(1)}, u32[]{:S(2)}, u32[]{:S(2)}) collective-permute-start(bf16[128,2048]{1,0:T(8,128)(2,1)} %get-tuple-element.48), channel_id=1, source_target_pairs={{0,6},{1,7},{2,4},{3,5},{4,2},{5,3},{6,0},{7,1},{8,14},{9,15},{10,... | collective-permute-start | bytes 1572872 | tf_op jit(solution)/shard_map/ppermute | solution.py:573
  98.9 1.1 collective-permute-start.23
  100.3 0.2 reduce_window_sum.11
  100.6 0.1 copy.26
  100.8 10.4 %collective-permute-done.21 = bf16[128,2048]{1,0:T(8,128)(2,1)S(1)} collective-permute-done((bf16[128,2048]{1,0:T(8,128)(2,1)}, bf16[128,2048]{1,0:T(8,128)(2,1)S(1)}, u32[]{:S(2)}, u32[]{:S(2)}) %collective-permute-start.21) | collective-permute-done | bytes 524320 | tf_op jit(solution)/shard_map/ppermute | solution.py:573
  111.2 11.2 %collective-permute-done.22 = bf16[128,2048]{1,0:T(8,128)(2,1)S(1)} collective-permute-done((bf16[128,2048]{1,0:T(8,128)(2,1)}, bf16[128,2048]{1,0:T(8,128)(2,1)S(1)}, u32[]{:S(2)}, u32[]{:S(2)}) %collective-permute-start.22) | collective-permute-done | bytes 524320 | tf_op jit(solution)/shard_map/ppermute | solution.py:573
  122.5 0.2 collective-permute-done.23
  122.7 1.0 copy-done.4
  123.7 1.1 route.1
  124.9 53.5 %all_to_all.15 = bf16[16,32,2048]{2,1,0:T(8,128)(2,1)S(1)} all-to-all(bf16[16,32,2048]{2,1,0:T(8,128)(2,1)S(1)} %bitcast.42), channel_id=1, replica_groups=mesh['grp'=2,'head'=16] {'head'}, dimensions={0} | all-to-all | bytes 4194304 | tf_op jit(solution)/shard_map/all_to_all | solution.py:751
  178.4 6.9 %expert.1 = bf16[512,2048]{1,0:T(8,128)(2,1)} custom-call(bf16[512,2048]{1,0:T(8,128)(2,1)S(1)} %bitcast.43, bf16[2048,1024]{1,0:T(8,128)(2,1)} %bitcast.64, bf16[512,2048]{1,0:T(8,128)(2,1)S(1)} %bitcast.52), custom_call_target="tpu_custom_call" | custom-call | flops 3221225472 | bytes 10485760 | tf_op jit(solution)/shard_map/expert/pallas_call | solution.py:508
  185.3 5.1 %all-to-all-start.2 = ((bf16[16,32,2048]{2,1,0:T(8,128)(2,1)}), bf16[16,32,2048]{2,1,0:T(8,128)(2,1)S(1)}, u32[]{:S(2)}, u32[]{:S(2)}) async-start(bf16[16,32,2048]{2,1,0:T(8,128)(2,1)} %bitcast.53), calls=%async_computation.2 | async-start | bytes 4194304 | tf_op jit(solution)/shard_map/all_to_all | solution.py:764
  190.5 47.3 %all-to-all-done.2 = bf16[16,32,2048]{2,1,0:T(8,128)(2,1)S(1)} async-done(((bf16[16,32,2048]{2,1,0:T(8,128)(2,1)}), bf16[16,32,2048]{2,1,0:T(8,128)(2,1)S(1)}, u32[]{:S(2)}, u32[]{:S(2)}) %all-to-all-start.2) | async-done | bytes 2097184 | tf_op jit(solution)/shard_map/all_to_all | solution.py:764
  237.8 1.2 copy-done.2
  239.0 1.7 combine.1
  (56 shorter events, 1.2 us)
Async XLA Ops:
  0.0 7.3 %copy-start = (bf16[16,16,2048]{2,1,0:T(8,128)(2,1)S(1)}, bf16[16,16,2048]{2,1,0:T(8,128)(2,1)}, u32[]{:S(2)}) copy-start(bf16[16,16,2048]{2,1,0:T(8,128)(2,1)} %param.14) | copy-start | bytes 3145732
  2.6 5.1 %copy-start.7 = (bf16[128,1,2,512]{3,2,1,0:T(2,128)(2,1)S(1)}, bf16[128,1,2,512]{3,2,1,0:T(2,128)(2,1)}, u32[]{:S(2)}) copy-start(bf16[128,1,2,512]{3,2,1,0:T(2,128)(2,1)} %param.11) | copy-start | bytes 786436
  2.6 36.5 %all-to-all-start = ((bf16[8,2,128,256]{3,2,1,0:T(8,128)(2,1)}), bf16[8,2,128,256]{3,2,1,0:T(8,128)(2,1)S(1)}, u32[]{:S(2)}, u32[]{:S(2)}) async-start(bf16[8,2,128,256]{3,2,1,0:T(8,128)(2,1)} %bitcast.9), calls=%async_computation | async-start | bytes 2097152 | tf_op jit(solution)/shard_map/all_to_all | solution.py:592
  7.4 31.7 %collective-permute-start.5 = (bf16[2,4,16,1024]{3,2,1,0:T(8,128)(2,1)S(1)}, bf16[2,4,16,1024]{3,2,1,0:T(8,128)(2,1)S(1)}, u32[]{:S(2)}, u32[]{:S(2)}) collective-permute-start(bf16[2,4,16,1024]{3,2,1,0:T(8,128)(2,1)S(1)} %get-tuple-element.56), channel_id=1, source_target_pairs={{0,2},{1,3},{2,0},{3,1},{4,6},{5,7},{6,4},{7,5},{8,10},{9,11},{10,... | collective-permute-start | bytes 786440 | tf_op jit(solution)/shard_map/ppermute | solution.py:573
  8.3 16.1 %collective-permute-start.2 = (bf16[128,512]{1,0:T(8,128)(2,1)S(1)}, bf16[128,512]{1,0:T(8,128)(2,1)S(1)}, u32[]{:S(2)}, u32[]{:S(2)}) collective-permute-start(bf16[128,512]{1,0:T(8,128)(2,1)S(1)} %bitcast.61), channel_id=1, source_target_pairs={{0,4},{1,5},{2,6},{3,7},{4,0},{5,1},{6,2},{7,3},{8,12},{9,13},{10,... | collective-permute-start | bytes 393224 | tf_op jit(solution)/shard_map/ppermute | solution.py:573
  8.5 30.7 %collective-permute-start = (bf16[256,512]{1,0:T(8,128)(2,1)}, bf16[256,512]{1,0:T(8,128)(2,1)S(1)}, u32[]{:S(2)}, u32[]{:S(2)}) collective-permute-start(bf16[256,512]{1,0:T(8,128)(2,1)} %bitcast.65), channel_id=1, source_target_pairs={{0,0},{1,1},{2,2},{3,3},{4,8},{5,9},{6,10},{7,11},{8,4},{9,5},{10,... | collective-permute-start | bytes 786440 | tf_op jit(solution)/shard_map/ppermute | solution.py:601
  12.9 26.3 %collective-permute-start.1 = (bf16[256,512]{1,0:T(8,128)(2,1)}, bf16[256,512]{1,0:T(8,128)(2,1)}, u32[]{:S(2)}, u32[]{:S(2)}) collective-permute-start(bf16[256,512]{1,0:T(8,128)(2,1)} %bitcast.66), channel_id=1, source_target_pairs={{0,8},{1,9},{2,10},{3,11},{4,0},{5,1},{6,2},{7,3},{8,12},{9,13},{1... | collective-permute-start | bytes 786440 | tf_op jit(solution)/shard_map/ppermute | solution.py:601
  13.0 20.2 %collective-permute-start.3 = (bf16[128,512]{1,0:T(8,128)(2,1)S(1)}, bf16[128,512]{1,0:T(8,128)(2,1)}, u32[]{:S(2)}, u32[]{:S(2)}) collective-permute-start(bf16[128,512]{1,0:T(8,128)(2,1)S(1)} %bitcast.57), channel_id=1, source_target_pairs={{0,8},{1,9},{2,10},{3,11},{4,12},{5,13},{6,14},{7,15},{8,0},{9,1},... | collective-permute-start | bytes 393224 | tf_op jit(solution)/shard_map/ppermute | solution.py:573
  24.4 14.8 %collective-permute-start.4 = (bf16[128,512]{1,0:T(8,128)(2,1)S(1)}, bf16[128,512]{1,0:T(8,128)(2,1)}, u32[]{:S(2)}, u32[]{:S(2)}) collective-permute-start(bf16[128,512]{1,0:T(8,128)(2,1)S(1)} %bitcast.62), channel_id=1, source_target_pairs={{0,12},{1,13},{2,14},{3,15},{4,8},{5,9},{6,10},{7,11},{8,4},{9,5},... | collective-permute-start | bytes 393224 | tf_op jit(solution)/shard_map/ppermute | solution.py:573
  39.2 7.6 %copy-start.8 = (bf16[8,2,128,256]{3,2,1,0:T(8,128)(2,1)}, bf16[8,2,128,256]{3,2,1,0:T(8,128)(2,1)S(1)}, u32[]{:S(2)}) copy-start(bf16[8,2,128,256]{3,2,1,0:T(8,128)(2,1)S(1)} %all-to-all-done.q_hbm) | copy-start | bytes 3145732
  39.2 7.4 %collective-permute-start.6 = (bf16[2,4,16,1024]{3,2,1,0:T(8,128)(2,1)S(1)}, bf16[2,4,16,1024]{3,2,1,0:T(8,128)(2,1)S(1)}, u32[]{:S(2)}, u32[]{:S(2)}) collective-permute-start(bf16[2,4,16,1024]{3,2,1,0:T(8,128)(2,1)S(1)} %get-tuple-element.54), channel_id=1, source_target_pairs={{0,4},{1,5},{2,6},{3,7},{4,0},{5,1},{6,2},{7,3},{8,12},{9,13},{10,... | collective-permute-start | bytes 786440 | tf_op jit(solution)/shard_map/ppermute | solution.py:573
  40.6 13.1 %collective-permute-start.9 = (bf16[4,128,512]{2,1,0:T(8,128)(2,1)S(1)}, bf16[4,128,512]{2,1,0:T(8,128)(2,1)S(1)}, u32[]{:S(2)}, u32[]{:S(2)}) collective-permute-start(bf16[4,128,512]{2,1,0:T(8,128)(2,1)S(1)} %pad_maximum_fusion.1.kv_own), channel_id=1, source_target_pairs={{0,2},{1,3},{2,0},{3,1},{4,6},{5,7},{6,4},{7,5},{8,10},{9,11},{10,... | collective-permute-start | bytes 1572872 | tf_op jit(solution)/shard_map/ppermute | solution.py:573
  41.9 23.0 %collective-permute-start.8 = (bf16[512,512]{1,0:T(8,128)(2,1)S(1)}, bf16[512,512]{1,0:T(8,128)(2,1)S(1)}, u32[]{:S(2)}, u32[]{:S(2)}) collective-permute-start(bf16[512,512]{1,0:T(8,128)(2,1)S(1)} %constant_dynamic-update-slice_fusion.page_own), channel_id=1, source_target_pairs={{0,2},{1,3},{2,0},{3,1},{4,6},{5,7},{6,4},{7,5},{8,10},{9,11},{10,... | collective-permute-start | bytes 1572872 | tf_op jit(solution)/shard_map/ppermute | solution.py:573
  46.7 18.1 %collective-permute-start.10 = (bf16[2,2,4,16,1024]{4,3,2,1,0:T(8,128)(2,1)S(1)}, bf16[2,2,4,16,1024]{4,3,2,1,0:T(8,128)(2,1)S(1)}, u32[]{:S(2)}, u32[]{:S(2)}) collective-permute-start(bf16[2,2,4,16,1024]{4,3,2,1,0:T(8,128)(2,1)S(1)} %pad_maximum_fusion.refs_0_), channel_id=1, source_target_pairs={{0,16},{16,0},{1,17},{17,1},{2,18},{18,2},{3,19},{19,3},{4,20},{20... | collective-permute-start | bytes 1572872 | tf_op jit(solution)/shard_map/ppermute | solution.py:573
  48.0 22.7 %collective-permute-start.7 = (bf16[2,2,4,16,1024]{4,3,2,1,0:T(8,128)(2,1)S(1)}, bf16[2,2,4,16,1024]{4,3,2,1,0:T(8,128)(2,1)S(1)}, u32[]{:S(2)}, u32[]{:S(2)}) collective-permute-start(bf16[2,2,4,16,1024]{4,3,2,1,0:T(8,128)(2,1)S(1)} %pad_maximum_fusion.refs_0_), channel_id=1, source_target_pairs={{0,8},{1,9},{2,10},{3,11},{4,12},{5,13},{6,14},{7,15},{8,0},{9,1},... | collective-permute-start | bytes 1572872 | tf_op jit(solution)/shard_map/ppermute | solution.py:573
  64.9 6.5 %collective-permute-start.11 = (bf16[512,512]{1,0:T(8,128)(2,1)S(1)}, bf16[512,512]{1,0:T(8,128)(2,1)S(1)}, u32[]{:S(2)}, u32[]{:S(2)}) collective-permute-start(bf16[512,512]{1,0:T(8,128)(2,1)S(1)} %constant_dynamic-update-slice_fusion.page_own), channel_id=1, source_target_pairs={{0,1},{1,0},{2,3},{3,2},{4,5},{5,4},{6,7},{7,6},{8,9},{9,8},{10,11... | collective-permute-start | bytes 1572872 | tf_op jit(solution)/shard_map/ppermute | solution.py:573
  66.2 5.4 %collective-permute-start.12 = (bf16[512,512]{1,0:T(8,128)(2,1)S(1)}, bf16[512,512]{1,0:T(8,128)(2,1)S(1)}, u32[]{:S(2)}, u32[]{:S(2)}) collective-permute-start(bf16[512,512]{1,0:T(8,128)(2,1)S(1)} %collective-permute-done.8.page_y), channel_id=1, source_target_pairs={{0,1},{1,0},{2,3},{3,2},{4,5},{5,4},{6,7},{7,6},{8,9},{9,8},{10,11... | collective-permute-start | bytes 1572872 | tf_op jit(solution)/shard_map/ppermute | solution.py:573
  66.2 5.7 %collective-permute-start.13 = (bf16[4,128,512]{2,1,0:T(8,128)(2,1)S(1)}, bf16[4,128,512]{2,1,0:T(8,128)(2,1)S(1)}, u32[]{:S(2)}, u32[]{:S(2)}) collective-permute-start(bf16[4,128,512]{2,1,0:T(8,128)(2,1)S(1)} %pad_maximum_fusion.1.kv_own), channel_id=1, source_target_pairs={{0,1},{1,0},{2,3},{3,2},{4,5},{5,4},{6,7},{7,6},{8,9},{9,8},{10,11... | collective-permute-start | bytes 1572872 | tf_op jit(solution)/shard_map/ppermute | solution.py:573
  66.7 5.2 %collective-permute-start.14 = (bf16[4,128,512]{2,1,0:T(8,128)(2,1)S(1)}, bf16[4,128,512]{2,1,0:T(8,128)(2,1)S(1)}, u32[]{:S(2)}, u32[]{:S(2)}) collective-permute-start(bf16[4,128,512]{2,1,0:T(8,128)(2,1)S(1)} %collective-permute-done.9.kv_y), channel_id=1, source_target_pairs={{0,1},{1,0},{2,3},{3,2},{4,5},{5,4},{6,7},{7,6},{8,9},{9,8},{10,11... | collective-permute-start | bytes 1572872 | tf_op jit(solution)/shard_map/ppermute | solution.py:573
  70.8 17.5 %collective-permute-start.17 = (bf16[2,2,4,16,1024]{4,3,2,1,0:T(8,128)(2,1)S(1)}, bf16[2,2,4,16,1024]{4,3,2,1,0:T(8,128)(2,1)S(1)}, u32[]{:S(2)}, u32[]{:S(2)}) collective-permute-start(bf16[2,2,4,16,1024]{4,3,2,1,0:T(8,128)(2,1)S(1)} %pad_maximum_fusion.refs_0_), channel_id=1, source_target_pairs={{0,1},{1,0},{2,3},{3,2},{4,5},{5,4},{6,7},{7,6},{8,9},{9,8},{10,11... | collective-permute-start | bytes 1572872 | tf_op jit(solution)/shard_map/ppermute | solution.py:573
  71.4 16.0 %collective-permute-start.15 = (bf16[2,2,4,16,1024]{4,3,2,1,0:T(8,128)(2,1)S(1)}, bf16[2,2,4,16,1024]{4,3,2,1,0:T(8,128)(2,1)S(1)}, u32[]{:S(2)}, u32[]{:S(2)}) collective-permute-start(bf16[2,2,4,16,1024]{4,3,2,1,0:T(8,128)(2,1)S(1)} %collective-permute-done.7.refs_4_), channel_id=1, source_target_pairs={{0,16},{16,0},{1,17},{17,1},{2,18},{18,2},{3,19},{19,3},{4,20},{20... | collective-permute-start | bytes 1572872 | tf_op jit(solution)/shard_map/ppermute | solution.py:573
  71.7 16.6 %collective-permute-start.19 = (bf16[2,2,4,16,1024]{4,3,2,1,0:T(8,128)(2,1)S(1)}, bf16[2,2,4,16,1024]{4,3,2,1,0:T(8,128)(2,1)S(1)}, u32[]{:S(2)}, u32[]{:S(2)}) collective-permute-start(bf16[2,2,4,16,1024]{4,3,2,1,0:T(8,128)(2,1)S(1)} %collective-permute-done.7.refs_4_), channel_id=1, source_target_pairs={{0,1},{1,0},{2,3},{3,2},{4,5},{5,4},{6,7},{7,6},{8,9},{9,8},{10,11... | collective-permute-start | bytes 1572872 | tf_op jit(solution)/shard_map/ppermute | solution.py:573
  87.4 12.6 %copy-start.9 = (s32[128,1,2]{0,2,1:T(2,128)S(1)}, s32[128,1,2]{0,2,1:T(2,128)}, u32[]{:S(2)}) copy-start(s32[128,1,2]{0,2,1:T(2,128)} %param.16) | copy-start | bytes 3076
  87.4 35.2 %copy-start.3 = (bf16[128,1,2048]{2,0,1:T(8,128)(2,1)S(1)}, bf16[128,1,2048]{2,0,1:T(8,128)(2,1)}, u32[]{:S(2)}) copy-start(bf16[128,1,2048]{2,0,1:T(8,128)(2,1)} %param.13) | copy-start | bytes 1572868
  87.4 35.2 %copy-start.5 = (f32[2048]{0:T(1024)S(1)}, f32[2048]{0:T(1024)}, u32[]{:S(2)}) copy-start(f32[2048]{0:T(1024)} %param.15) | copy-start | bytes 24580
  87.5 2.0 collective-permute-start.18
  87.8 2.4 %collective-permute-start.20 = (bf16[2,2,4,16,1024]{4,3,2,1,0:T(8,128)(2,1)S(1)}, bf16[2,2,4,16,1024]{4,3,2,1,0:T(8,128)(2,1)S(1)}, u32[]{:S(2)}, u32[]{:S(2)}) collective-permute-start(bf16[2,2,4,16,1024]{4,3,2,1,0:T(8,128)(2,1)S(1)} %collective-permute-done.15.refs_6_), channel_id=1, source_target_pairs={{0,1},{1,0},{2,3},{3,2},{4,5},{5,4},{6,7},{7,6},{8,9},{9,8},{10,11... | collective-permute-start | bytes 1572872 | tf_op jit(solution)/shard_map/ppermute | solution.py:573
  88.0 2.9 %collective-permute-start.16 = (bf16[512,512]{1,0:T(8,128)(2,1)S(1)}, bf16[512,512]{1,0:T(8,128)(2,1)S(1)}, u32[]{:S(2)}, u32[]{:S(2)}) collective-permute-start(bf16[512,512]{1,0:T(8,128)(2,1)S(1)} %slice_bitcast_fusion), channel_id=1, source_target_pairs={{0,1},{1,0},{2,3},{3,2},{4,5},{5,4},{6,7},{7,6},{8,9},{9,8},{10,11... | collective-permute-start | bytes 1572872 | tf_op jit(solution)/shard_map/ppermute | solution.py:573
  95.3 15.9 %collective-permute-start.21 = (bf16[128,2048]{1,0:T(8,128)(2,1)}, bf16[128,2048]{1,0:T(8,128)(2,1)S(1)}, u32[]{:S(2)}, u32[]{:S(2)}) collective-permute-start(bf16[128,2048]{1,0:T(8,128)(2,1)} %get-tuple-element.48), channel_id=1, source_target_pairs={{0,6},{1,7},{2,4},{3,5},{4,2},{5,3},{6,0},{7,1},{8,14},{9,15},{10,... | collective-permute-start | bytes 1572872 | tf_op jit(solution)/shard_map/ppermute | solution.py:573
  98.8 23.6 %collective-permute-start.22 = (bf16[128,2048]{1,0:T(8,128)(2,1)}, bf16[128,2048]{1,0:T(8,128)(2,1)S(1)}, u32[]{:S(2)}, u32[]{:S(2)}) collective-permute-start(bf16[128,2048]{1,0:T(8,128)(2,1)} %get-tuple-element.49), channel_id=1, source_target_pairs={{0,4},{1,5},{2,6},{3,7},{4,0},{5,1},{6,2},{7,3},{8,12},{9,13},{10,... | collective-permute-start | bytes 1572872 | tf_op jit(solution)/shard_map/ppermute | solution.py:573
  98.9 23.8 %collective-permute-start.23 = (bf16[128,2048]{1,0:T(8,128)(2,1)}, bf16[128,2048]{1,0:T(8,128)(2,1)S(1)}, u32[]{:S(2)}, u32[]{:S(2)}) collective-permute-start(bf16[128,2048]{1,0:T(8,128)(2,1)} %get-tuple-element.50), channel_id=1, source_target_pairs={{0,2},{1,3},{2,0},{3,1},{4,6},{5,7},{6,4},{7,5},{8,10},{9,11},{10,... | collective-permute-start | bytes 1572872 | tf_op jit(solution)/shard_map/ppermute | solution.py:573
  122.7 1.0 copy-start.4
  124.9 53.5 %copy-start.1 = (f32[128,2048]{1,0:T(8,128)}, f32[128,2048]{1,0:T(8,128)S(1)}, u32[]{:S(2)}) copy-start(f32[128,2048]{1,0:T(8,128)S(1)} %get-tuple-element.52.stream_hbm) | copy-start | bytes 3145732
  124.9 53.5 %copy-start.6 = (bf16[1,512,2048]{2,1,0:T(8,128)(2,1)S(1)}, bf16[1,512,2048]{2,1,0:T(8,128)(2,1)}, u32[]{:S(2)}) copy-start(bf16[1,512,2048]{2,1,0:T(8,128)(2,1)} %param.19) | copy-start | bytes 6291460
  185.2 5.1 %copy-start.10 = (f32[128,1,2]{0,2,1:T(2,128)S(1)}, f32[128,1,2]{0,2,1:T(2,128)}, u32[]{:S(2)}) copy-start(f32[128,1,2]{0,2,1:T(2,128)} %param.17) | copy-start | bytes 3076
  185.3 52.6 %all-to-all-start.2 = ((bf16[16,32,2048]{2,1,0:T(8,128)(2,1)}), bf16[16,32,2048]{2,1,0:T(8,128)(2,1)S(1)}, u32[]{:S(2)}, u32[]{:S(2)}) async-start(bf16[16,32,2048]{2,1,0:T(8,128)(2,1)} %bitcast.53), calls=%async_computation.2 | async-start | bytes 4194304 | tf_op jit(solution)/shard_map/all_to_all | solution.py:764
  237.8 1.2 copy-start.2

commit v16 on v15

--- a/solution.py
+++ b/solution.py
@@ -350,7 +350,8 @@
     model = 2 * columns
     return pl.pallas_call(
         project_pair_kernel,
-        out_shape=[pltpu.HBM((rows // parts, model), BF16)] * parts,
+        out_shape=[jax.ShapeDtypeStruct((rows // parts, model), BF16)]
+        + [pltpu.HBM((rows // parts, model), BF16)] * (parts - 1),
         in_specs=[in_hbm()] * 10,
         out_specs=[in_hbm()] * parts,
         scratch_shapes=[
@@ -406,7 +407,7 @@
 
 
 def route_kernel(resid_ref, gain_ref, slots_ref, *refs):
-    parts_refs, (stream_ref, out_ref) = refs[:-2], refs[-2:]
+    parts_refs, (stream_hbm, out_ref, stream_ref, sem) = refs[:-4], refs[-4:]
     seqs = resid_ref.shape[0]
     streams = []
     for seq in range(seqs):
@@ -417,6 +418,8 @@
         streams.append(stream + projected)
     stream = jnp.concatenate(streams, 0) if seqs > 1 else streams[0]
     stream_ref[...] = stream
+    back = pltpu.make_async_copy(stream_ref, stream_hbm, sem.at[0])
+    back.start()
     normed = stream * lax.rsqrt(jnp.mean(stream * stream, 1, keepdims=True) + eps_norm)
     normed = (normed * gain_ref[...]).astype(BF16)
     slots, rows = out_ref.shape[0], stream.shape[0]
@@ -425,6 +428,7 @@
     for k in range(1, slots_ref.shape[0]):
         hit = hit | (place == slots_ref[k : k + 1, :])
     out_ref[...] = jnp.dot(hit.astype(BF16), normed, preferred_element_type=F32).astype(BF16)
+    back.wait()
 
 
 def route(parts, resid, gain, slots_of, slots):
@@ -433,11 +437,12 @@
     return pl.pallas_call(
         route_kernel,
         out_shape=(
-            jax.ShapeDtypeStruct((rows, model), F32),
+            pltpu.HBM((rows, model), F32),
             jax.ShapeDtypeStruct((slots, model), BF16),
         ),
         in_specs=[in_vmem()] * (3 + len(parts)),
-        out_specs=(in_vmem(), in_vmem()),
+        out_specs=(in_hbm(), in_vmem()),
+        scratch_shapes=[pltpu.VMEM((rows, model), F32), pltpu.SemaphoreType.DMA((1,))],
         compiler_params=pltpu.CompilerParams(vmem_limit_bytes=HIGH_VMEM),
         cost_estimate=pl.CostEstimate(
             flops=2 * slots * rows * model,
@@ -477,33 +482,46 @@
 def expert_pair(x, w_in, w_down):
     rows, model = x.shape
     hidden_width = w_down.shape[0]
-    parts = 4
+    parts = 2
     depth = model // parts
+    tiles = 4
+    tile = model // tiles
 
     def kernel(x_hbm, in_hbm_ref, down_hbm, o_hbm, x_ref, in_ref, down_ref, o_ref, sems):
-        bring_x = pltpu.make_async_copy(x_hbm, x_ref, sems.at[parts])
-        bring_x.start()
-        bring_in = []
+        bring = []
         for k in range(parts):
             at = pl.ds(k * depth, depth)
-            bring_in.append(pltpu.make_async_copy(in_hbm_ref.at[at], in_ref.at[at], sems.at[k]))
-            bring_in[k].start()
-        bring_down = pltpu.make_async_copy(down_hbm, down_ref, sems.at[parts + 1])
-        bring_down.start()
-        bring_x.wait()
+            bring.append(
+                [
+                    pltpu.make_async_copy(x_hbm.at[:, at], x_ref.at[:, at], sems.at[2 * k]),
+                    pltpu.make_async_copy(in_hbm_ref.at[at], in_ref.at[at], sems.at[2 * k + 1]),
+                ]
+            )
+        bring.append([pltpu.make_async_copy(down_hbm, down_ref, sems.at[2 * parts])])
+        for copies in bring:
+            for copy in copies:
+                copy.start()
         inner = None
         for k in range(parts):
-            bring_in[k].wait()
+            for copy in bring[k]:
+                copy.wait()
             at = pl.ds(k * depth, depth)
             part = jnp.dot(x_ref[:, at], in_ref[at, :], preferred_element_type=F32)
             inner = part if inner is None else inner + part
         gate = inner[:, :hidden_width]
         hidden = (gate / (1.0 + jnp.exp(-gate)) * inner[:, hidden_width:]).astype(BF16)
-        bring_down.wait()
-        o_ref[...] = jnp.dot(hidden, down_ref[...], preferred_element_type=F32).astype(BF16)
-        back = pltpu.make_async_copy(o_ref, o_hbm, sems.at[parts + 2])
-        back.start()
-        back.wait()
+        bring[parts][0].wait()
+        back = []
+        for k in range(tiles):
+            at = pl.ds(k * tile, tile)
+            product = jnp.dot(hidden, down_ref[:, at], preferred_element_type=F32)
+            o_ref[:, at] = product.astype(BF16)
+            back.append(
+                pltpu.make_async_copy(o_ref.at[:, at], o_hbm.at[:, at], sems.at[2 * parts + 1])
+            )
+            back[k].start()
+        for copy in back:
+            copy.wait()
 
     return pl.pallas_call(
         kernel,
@@ -515,7 +533,7 @@
             pltpu.VMEM(w_in.shape, BF16),
             pltpu.VMEM(w_down.shape, BF16),
             pltpu.VMEM((rows, model), BF16),
-            pltpu.SemaphoreType.DMA((parts + 3,)),
+            pltpu.SemaphoreType.DMA((2 * parts + 2,)),
         ],
         compiler_params=pltpu.CompilerParams(vmem_limit_bytes=HIGH_VMEM),
         cost_estimate=pl.CostEstimate(
@@ -589,9 +607,6 @@
 
     query_slots = queries.reshape(local_rows, heads, width).transpose(1, 0, 2)
     query_slots = query_slots.reshape(members, heads // members, local_rows, width)
-    q = lax.all_to_all(
-        query_slots, "head", split_axis=0, concat_axis=0, tiled=True, axis_index_groups=group_sets
-    )
 
     def page_target(source, other):
         p, plane, rest = source // members, (source // plane_bit) % 2, source % plane_bit
@@ -609,26 +624,33 @@
     w = w.reshape(2, 2, heads // 4, share, columns)
     w_keep = lax.dynamic_index_in_dim(w, y, 1, keepdims=False)
     w_give = lax.dynamic_index_in_dim(w, 1 - y, 1, keepdims=False)
-    kv_own = [kv_same]
-    for t in range(1, planes):
-        kv_own.append(flipped(kv_other if t % 2 else kv_same, "head", t * plane_bit))
     w_got = flipped(w_give, "head", 2)
-
-    (page_a, page_b, kv_own, q), w_got = lax.optimization_barrier(
-        ((page_a, page_b, kv_own, q), w_got)
+    kv_last, w_got = lax.optimization_barrier((kv_other, w_got))
+    kv_own = [
+        kv_same,
+        flipped(kv_other, "head", plane_bit),
+        flipped(kv_same, "head", 2 * plane_bit),
+        flipped(kv_last, "head", 3 * plane_bit),
+    ]
+
+    page_a, page_b, kv_own, w_got, query_slots = lax.optimization_barrier(
+        (page_a, page_b, kv_own, w_got, query_slots)
     )
     own_pages = jnp.concatenate([page_a, page_b], 0)
     kv_own = jnp.stack(kv_own, 0)
     pages_y = flipped(own_pages, "head", 2)
     kv_y = flipped(kv_own, "head", 2)
+    q = lax.all_to_all(
+        query_slots, "head", split_axis=0, concat_axis=0, tiled=True, axis_index_groups=group_sets
+    )
     w_both = jnp.stack([w_keep, w_got], 1)
     w_same = lax.dynamic_index_in_dim(w_both, b, 0, keepdims=False)
     w_other = lax.dynamic_index_in_dim(w_both, 1 - b, 0, keepdims=False)
     w_near = jnp.stack([w_same, flipped(w_other, "head", plane_bit)], 0)
     w_near_x = flipped(w_near, "grp", 1)
     w_far = flipped(w_near, "head", members)
-    pages_y, kv_y, own_pages, kv_own, w_near_x = lax.optimization_barrier(
-        (pages_y, kv_y, own_pages, kv_own, w_near_x)
+    pages_y, kv_y, own_pages, kv_own, w_near_x, q = lax.optimization_barrier(
+        (pages_y, kv_y, own_pages, kv_own, w_near_x, q)
     )
     kv_c = flipped(kv_own, "head", 1)
     kv_cy = flipped(kv_y, "head", 1)

time: 241 us -> 250 us (1.037)
  waiting for transfers between devices: 119 us -> 123 us
  starting transfers between devices: 30 us -> 33.1 us
    ppermute x22, waiting for transfers between devices: 71.3 us -> 76 us  [flipped(): return lax.ppermute(value, axis, pairs)]
    all_to_all x1, starting transfers between devices: 4.64 us -> 7.75 us  [parts_in_pairs(): lax.all_to_all(query_slots, 'head', split_axis=0, concat_axis=0, tiled=Tr...]
  transfers between devices with their start and end apart: 26 -> 26, of which waited for: 14 -> 15; matrix products, arithmetic and copies ran while one was open for 2% -> 2% of each run, Pallas kernels for 6% -> 6%
where the time goes in v16:
time: 250 us
  waiting for transfers between devices  123 us (49%)
  blocking collectives  54.5 us (22%)
  starting transfers between devices  33.1 us (13%)
  Pallas kernels  31 us (12%)
  local copies, waits for them, and re-layouts  6.09 us (2%)
    ppermute x22, waiting for transfers between devices, flipped(): return lax.ppermute(value, axis, pairs)  76 us
    all_to_all x1, blocking collectives, local(): lax.all_to_all(outgoing.reshape(n, slots // n, model), 'head', split_axis...  54.5 us
    all_to_all x1, waiting for transfers between devices, local(): lax.all_to_all(answered, 'head', split_axis=0, concat_axis=0, tiled=True)  47.3 us
    ppermute x22, starting transfers between devices, flipped(): return lax.ppermute(value, axis, pairs)  17 us
    pallas_call x1, Pallas kernels, attend_pair(): pl.pallas_call(functools.partial(attend_pair_kernel, block, chunk, width)...  14.7 us
    all_to_all x1, starting transfers between devices, parts_in_pairs(): lax.all_to_all(query_slots, 'head', split_axis=0, concat_axis=0, tiled=Tr...  7.75 us
    pallas_call x1, Pallas kernels, expert_pair(): pl.pallas_call(kernel, out_shape=pltpu.HBM((rows, model), BF16), in_specs...  7.09 us
    all_to_all x1, starting transfers between devices, local(): lax.all_to_all(answered, 'head', split_axis=0, concat_axis=0, tiled=True)  5.14 us
  transfers between devices with their start and end apart: 26, of which 15 were waited for; matrix products, arithmetic and copies ran while one was open for 2% of the time, Pallas kernels for 6%

profile of v16, /device:TPU:13, one launch (start us, length us, event | category | flops | bytes accessed | tf_op | source)
XLA Modules:
  0.0 249.9 jit_solution(8756099614531457484)
XLA Ops:
  0.1 1.2 copy-done
  1.3 0.3 collective-permute-start.4
  1.6 3.2 %collective-permute-start = (bf16[256,512]{1,0:T(8,128)(2,1)}, bf16[256,512]{1,0:T(8,128)(2,1)S(1)}, u32[]{:S(2)}, u32[]{:S(2)}) collective-permute-start(bf16[256,512]{1,0:T(8,128)(2,1)} %bitcast.4), channel_id=1, source_target_pairs={{0,0},{1,1},{2,2},{3,3},{4,8},{5,9},{6,10},{7,11},{8,4},{9,5},{10,... | collective-permute-start | bytes 786440 | tf_op jit(solution)/shard_map/ppermute | solution.py:616
  4.9 0.5 constant_dynamic-slice_fusion.2
  5.5 1.3 collective-permute-start.2
  6.9 1.1 collective-permute-start.3
  8.0 0.6 collective-permute-done.4
  8.6 1.3 collective-permute-start.5
  9.9 1.3 copy.29
  11.2 3.4 %collective-permute-done.2 = bf16[128,512]{1,0:T(8,128)(2,1)S(1)} collective-permute-done((bf16[128,512]{1,0:T(8,128)(2,1)S(1)}, bf16[128,512]{1,0:T(8,128)(2,1)S(1)}, u32[]{:S(2)}, u32[]{:S(2)}) %collective-permute-start.2) | collective-permute-done | bytes 131104 | tf_op jit(solution)/shard_map/ppermute | solution.py:591
  14.5 9.3 %collective-permute-done.3 = bf16[128,512]{1,0:T(8,128)(2,1)S(1)} collective-permute-done((bf16[128,512]{1,0:T(8,128)(2,1)S(1)}, bf16[128,512]{1,0:T(8,128)(2,1)S(1)}, u32[]{:S(2)}, u32[]{:S(2)}) %collective-permute-start.3) | collective-permute-done | bytes 131104 | tf_op jit(solution)/shard_map/ppermute | solution.py:591
  23.9 3.2 %collective-permute-done.5 = bf16[128,512]{1,0:T(8,128)(2,1)S(1)} collective-permute-done((bf16[128,512]{1,0:T(8,128)(2,1)S(1)}, bf16[128,512]{1,0:T(8,128)(2,1)S(1)}, u32[]{:S(2)}, u32[]{:S(2)}) %collective-permute-start.5) | collective-permute-done | bytes 131104 | tf_op jit(solution)/shard_map/ppermute | solution.py:591
  27.1 7.7 %all-to-all-start = ((bf16[8,2,128,256]{3,2,1,0:T(8,128)(2,1)}), bf16[8,2,128,256]{3,2,1,0:T(8,128)(2,1)}, u32[]{:S(2)}, u32[]{:S(2)}) async-start(bf16[8,2,128,256]{3,2,1,0:T(8,128)(2,1)} %bitcast.11), calls=%async_computation | async-start | bytes 2097152 | tf_op jit(solution)/shard_map/all_to_all | solution.py:643
  34.9 0.3 collective-permute-start.8
  35.3 1.0 pad_maximum_fusion.kv_own
  36.4 1.0 constant_dynamic-update-slice_fusion.page_own
  37.4 1.5 collective-permute-start.6
  38.8 14.2 %collective-permute-done.8 = bf16[2,4,16,1024]{3,2,1,0:T(8,128)(2,1)S(1)} collective-permute-done((bf16[2,4,16,1024]{3,2,1,0:T(8,128)(2,1)S(1)}, bf16[2,4,16,1024]{3,2,1,0:T(8,128)(2,1)S(1)}, u32[]{:S(2)}, u32[]{:S(2)}) %collective-permute-start.8) | collective-permute-done | bytes 262176 | tf_op jit(solution)/shard_map/ppermute | solution.py:591
  53.1 1.3 collective-permute-start.9
  54.4 2.0 collective-permute-start.10
  56.4 2.5 collective-permute-done.7.kv_y
  58.9 11.2 %collective-permute-done.6.page_y = bf16[512,512]{1,0:T(8,128)(2,1)} collective-permute-done((bf16[512,512]{1,0:T(8,128)(2,1)S(1)}, bf16[512,512]{1,0:T(8,128)(2,1)}, u32[]{:S(2)}, u32[]{:S(2)}) %collective-permute-start.6) | collective-permute-done | bytes 524320 | tf_op jit(solution)/shard_map/ppermute | solution.py:591
  70.1 0.7 collective-permute-start.11
  70.9 0.4 collective-permute-start.13
  71.4 6.9 %collective-permute-done.10.refs_4_ = bf16[2,2,4,16,1024]{4,3,2,1,0:T(8,128)(2,1)} collective-permute-done((bf16[2,2,4,16,1024]{4,3,2,1,0:T(8,128)(2,1)S(1)}, bf16[2,2,4,16,1024]{4,3,2,1,0:T(8,128)(2,1)}, u32[]{:S(2)}, u32[]{:S(2)}) %collective-permute-start.10) | collective-permute-done | bytes 524320 | tf_op jit(solution)/shard_map/ppermute | solution.py:591
  78.3 1.5 collective-permute-start.17
  79.8 0.3 collective-permute-start.15
  80.1 0.3 collective-permute-start.19
  80.4 14.7 %attend.1.a_hbm = bf16[2,512,512]{2,1,0:T(8,128)(2,1)S(1)} custom-call(bf16[8,2,128,256]{3,2,1,0:T(8,128)(2,1)} %all-to-all-done.q_hbm, bf16[512,512]{1,0:T(8,128)(2,1)S(1)} %constant_dynamic-update-slice_fusion.page_own, bf16[512,512]{1,0:T(8,128)(2,1)} %collective-permute-done.6.page_y, bf16[512,512]{1,0:T(8,128)(2,1)S(1)} %collective-permute-done.11.page_c, ...), custom_call_target="tpu_custom_call" | custom-call | flops 7516192768 | bytes 6291456 | tf_op jit(solution)/shard_map/attend/pallas_call | solution.py:270
  95.2 0.3 collective-permute-start.18
  95.5 0.3 collective-permute-start.20
  95.8 0.2 collective-permute-start.16
  96.0 1.2 collective-permute-done.18.refs_3_
  97.2 0.7 collective-permute-done.20.refs_7_
  97.9 0.7 collective-permute-done.16.got_hbm
  98.7 5.1 %project.1 = (bf16[128,2048]{1,0:T(8,128)(2,1)S(1)}, bf16[128,2048]{1,0:T(8,128)(2,1)}, bf16[128,2048]{1,0:T(8,128)(2,1)}, bf16[128,2048]{1,0:T(8,128)(2,1)}) custom-call(bf16[2,512,512]{2,1,0:T(8,128)(2,1)} %copy-done.3, bf16[512,512]{1,0:T(8,128)(2,1)S(1)} %collective-permute-done.16.got_hbm, bf16[2,2,4,16,1024]{4,3,2,1,0:T(8,128)(2,1)S(1)} %pad_maximum_fusion.1.refs_0_, ...), custom_call_target="tpu_custom_call" | custom-call | flops 2147483648 | bytes 7340032 | tf_op jit(solution)/shard_map/project/pallas_call | solution.py:351
  103.7 2.4 collective-permute-start.21
  106.2 1.1 collective-permute-start.23
  108.1 10.1 %collective-permute-done.21 = bf16[128,2048]{1,0:T(8,128)(2,1)S(1)} collective-permute-done((bf16[128,2048]{1,0:T(8,128)(2,1)}, bf16[128,2048]{1,0:T(8,128)(2,1)S(1)}, u32[]{:S(2)}, u32[]{:S(2)}) %collective-permute-start.21) | collective-permute-done | bytes 524320 | tf_op jit(solution)/shard_map/ppermute | solution.py:591
  118.3 11.7 %collective-permute-done.22 = bf16[128,2048]{1,0:T(8,128)(2,1)S(1)} collective-permute-done((bf16[128,2048]{1,0:T(8,128)(2,1)}, bf16[128,2048]{1,0:T(8,128)(2,1)S(1)}, u32[]{:S(2)}, u32[]{:S(2)}) %collective-permute-start.22) | collective-permute-done | bytes 524320 | tf_op jit(solution)/shard_map/ppermute | solution.py:591
  129.9 0.2 collective-permute-done.23
  130.1 2.4 route.1
  132.5 54.5 %all_to_all.15 = bf16[16,32,2048]{2,1,0:T(8,128)(2,1)S(1)} all-to-all(bf16[16,32,2048]{2,1,0:T(8,128)(2,1)S(1)} %bitcast.42), channel_id=1, replica_groups=mesh['grp'=2,'head'=16] {'head'}, dimensions={0} | all-to-all | bytes 4194304 | tf_op jit(solution)/shard_map/all_to_all | solution.py:773
  187.1 7.1 %expert.1 = bf16[512,2048]{1,0:T(8,128)(2,1)} custom-call(bf16[512,2048]{1,0:T(8,128)(2,1)S(1)} %bitcast.43, bf16[2048,1024]{1,0:T(8,128)(2,1)} %bitcast.65, bf16[512,2048]{1,0:T(8,128)(2,1)S(1)} %bitcast.51), custom_call_target="tpu_custom_call" | custom-call | flops 3221225472 | bytes 10485760 | tf_op jit(solution)/shard_map/expert/pallas_call | solution.py:526
  194.2 5.1 %all-to-all-start.2 = ((bf16[16,32,2048]{2,1,0:T(8,128)(2,1)}), bf16[16,32,2048]{2,1,0:T(8,128)(2,1)S(1)}, u32[]{:S(2)}, u32[]{:S(2)}) async-start(bf16[16,32,2048]{2,1,0:T(8,128)(2,1)} %bitcast.52), calls=%async_computation.2 | async-start | bytes 4194304 | tf_op jit(solution)/shard_map/all_to_all | solution.py:786
  199.4 47.3 %all-to-all-done.2 = bf16[16,32,2048]{2,1,0:T(8,128)(2,1)S(1)} async-done(((bf16[16,32,2048]{2,1,0:T(8,128)(2,1)}), bf16[16,32,2048]{2,1,0:T(8,128)(2,1)S(1)}, u32[]{:S(2)}, u32[]{:S(2)}) %all-to-all-start.2) | async-done | bytes 2097184 | tf_op jit(solution)/shard_map/all_to_all | solution.py:786
  246.7 1.2 copy-done.1
  247.9 1.7 combine.1
  (60 shorter events, 1.6 us)
Async XLA Ops:
  0.0 1.2 copy-start
  0.0 4.9 %copy-start.6 = (bf16[128,1,2,512]{3,2,1,0:T(2,128)(2,1)S(1)}, bf16[128,1,2,512]{3,2,1,0:T(2,128)(2,1)}, u32[]{:S(2)}) copy-start(bf16[128,1,2,512]{3,2,1,0:T(2,128)(2,1)} %param.11) | copy-start | bytes 786436
  0.0 9.9 %copy-start.7 = (bf16[128,1,16,256]{3,2,1,0:T(8,128)(2,1)S(1)}, bf16[128,1,16,256]{3,2,1,0:T(8,128)(2,1)}, u32[]{:S(2)}) copy-start(bf16[128,1,16,256]{3,2,1,0:T(8,128)(2,1)} %param.10) | copy-start | bytes 3145732
  1.3 7.2 %collective-permute-start.4 = (bf16[2,4,16,1024]{3,2,1,0:T(8,128)(2,1)S(1)}, bf16[2,4,16,1024]{3,2,1,0:T(8,128)(2,1)S(1)}, u32[]{:S(2)}, u32[]{:S(2)}) collective-permute-start(bf16[2,4,16,1024]{3,2,1,0:T(8,128)(2,1)S(1)} %get-tuple-element.62), channel_id=1, source_target_pairs={{0,2},{1,3},{2,0},{3,1},{4,6},{5,7},{6,4},{7,5},{8,10},{9,11},{10,... | collective-permute-start | bytes 786440 | tf_op jit(solution)/shard_map/ppermute | solution.py:591
  1.6 22.3 %collective-permute-start = (bf16[256,512]{1,0:T(8,128)(2,1)}, bf16[256,512]{1,0:T(8,128)(2,1)S(1)}, u32[]{:S(2)}, u32[]{:S(2)}) collective-permute-start(bf16[256,512]{1,0:T(8,128)(2,1)} %bitcast.4), channel_id=1, source_target_pairs={{0,0},{1,1},{2,2},{3,3},{4,8},{5,9},{6,10},{7,11},{8,4},{9,5},{10,... | collective-permute-start | bytes 786440 | tf_op jit(solution)/shard_map/ppermute | solution.py:616
  4.8 19.1 %collective-permute-start.1 = (bf16[256,512]{1,0:T(8,128)(2,1)}, bf16[256,512]{1,0:T(8,128)(2,1)}, u32[]{:S(2)}, u32[]{:S(2)}) collective-permute-start(bf16[256,512]{1,0:T(8,128)(2,1)} %bitcast.4), channel_id=1, source_target_pairs={{0,8},{1,9},{2,10},{3,11},{4,0},{5,1},{6,2},{7,3},{8,12},{9,13},{1... | collective-permute-start | bytes 786440 | tf_op jit(solution)/shard_map/ppermute | solution.py:616
  5.5 9.0 %collective-permute-start.2 = (bf16[128,512]{1,0:T(8,128)(2,1)S(1)}, bf16[128,512]{1,0:T(8,128)(2,1)S(1)}, u32[]{:S(2)}, u32[]{:S(2)}) collective-permute-start(bf16[128,512]{1,0:T(8,128)(2,1)S(1)} %bitcast.60), channel_id=1, source_target_pairs={{0,4},{1,5},{2,6},{3,7},{4,0},{5,1},{6,2},{7,3},{8,12},{9,13},{10,... | collective-permute-start | bytes 393224 | tf_op jit(solution)/shard_map/ppermute | solution.py:591
  6.9 17.0 %collective-permute-start.3 = (bf16[128,512]{1,0:T(8,128)(2,1)S(1)}, bf16[128,512]{1,0:T(8,128)(2,1)S(1)}, u32[]{:S(2)}, u32[]{:S(2)}) collective-permute-start(bf16[128,512]{1,0:T(8,128)(2,1)S(1)} %bitcast.56), channel_id=1, source_target_pairs={{0,8},{1,9},{2,10},{3,11},{4,12},{5,13},{6,14},{7,15},{8,0},{9,1},... | collective-permute-start | bytes 393224 | tf_op jit(solution)/shard_map/ppermute | solution.py:591
  8.6 18.6 %collective-permute-start.5 = (bf16[128,512]{1,0:T(8,128)(2,1)S(1)}, bf16[128,512]{1,0:T(8,128)(2,1)S(1)}, u32[]{:S(2)}, u32[]{:S(2)}) collective-permute-start(bf16[128,512]{1,0:T(8,128)(2,1)S(1)} %bitcast.61), channel_id=1, source_target_pairs={{0,12},{1,13},{2,14},{3,15},{4,8},{5,9},{6,10},{7,11},{8,4},{9,5},... | collective-permute-start | bytes 393224 | tf_op jit(solution)/shard_map/ppermute | solution.py:591
  14.5 20.7 %copy-start.8 = (bf16[128,512]{1,0:T(8,128)(2,1)}, bf16[128,512]{1,0:T(8,128)(2,1)S(1)}, u32[]{:S(2)}) copy-start(bf16[128,512]{1,0:T(8,128)(2,1)S(1)} %collective-permute-done.2) | copy-start | bytes 393220
  23.9 3.2 %copy-start.9 = (bf16[128,512]{1,0:T(8,128)(2,1)}, bf16[128,512]{1,0:T(8,128)(2,1)S(1)}, u32[]{:S(2)}) copy-start(bf16[128,512]{1,0:T(8,128)(2,1)S(1)} %collective-permute-done.3) | copy-start | bytes 393220
  27.1 8.1 %copy-start.10 = (bf16[128,512]{1,0:T(8,128)(2,1)S(1)}, bf16[128,512]{1,0:T(8,128)(2,1)}, u32[]{:S(2)}) copy-start(bf16[128,512]{1,0:T(8,128)(2,1)} %copy-done.9) | copy-start | bytes 393220
  27.1 43.0 %all-to-all-start = ((bf16[8,2,128,256]{3,2,1,0:T(8,128)(2,1)}), bf16[8,2,128,256]{3,2,1,0:T(8,128)(2,1)}, u32[]{:S(2)}, u32[]{:S(2)}) async-start(bf16[8,2,128,256]{3,2,1,0:T(8,128)(2,1)} %bitcast.11), calls=%async_computation | async-start | bytes 2097152 | tf_op jit(solution)/shard_map/all_to_all | solution.py:643
  34.9 18.1 %collective-permute-start.8 = (bf16[2,4,16,1024]{3,2,1,0:T(8,128)(2,1)S(1)}, bf16[2,4,16,1024]{3,2,1,0:T(8,128)(2,1)S(1)}, u32[]{:S(2)}, u32[]{:S(2)}) collective-permute-start(bf16[2,4,16,1024]{3,2,1,0:T(8,128)(2,1)S(1)} %get-tuple-element.60), channel_id=1, source_target_pairs={{0,4},{1,5},{2,6},{3,7},{4,0},{5,1},{6,2},{7,3},{8,12},{9,13},{10,... | collective-permute-start | bytes 786440 | tf_op jit(solution)/shard_map/ppermute | solution.py:591
  36.2 22.7 %collective-permute-start.7 = (bf16[4,128,512]{2,1,0:T(8,128)(2,1)S(1)}, bf16[4,128,512]{2,1,0:T(8,128)(2,1)}, u32[]{:S(2)}, u32[]{:S(2)}) collective-permute-start(bf16[4,128,512]{2,1,0:T(8,128)(2,1)S(1)} %pad_maximum_fusion.kv_own), channel_id=1, source_target_pairs={{0,2},{1,3},{2,0},{3,1},{4,6},{5,7},{6,4},{7,5},{8,10},{9,11},{10,... | collective-permute-start | bytes 1572872 | tf_op jit(solution)/shard_map/ppermute | solution.py:591
  37.4 32.8 %collective-permute-start.6 = (bf16[512,512]{1,0:T(8,128)(2,1)S(1)}, bf16[512,512]{1,0:T(8,128)(2,1)}, u32[]{:S(2)}, u32[]{:S(2)}) collective-permute-start(bf16[512,512]{1,0:T(8,128)(2,1)S(1)} %constant_dynamic-update-slice_fusion.page_own), channel_id=1, source_target_pairs={{0,2},{1,3},{2,0},{3,1},{4,6},{5,7},{6,4},{7,5},{8,10},{9,11},{10,... | collective-permute-start | bytes 1572872 | tf_op jit(solution)/shard_map/ppermute | solution.py:591
  53.1 17.0 %collective-permute-start.9 = (bf16[2,2,4,16,1024]{4,3,2,1,0:T(8,128)(2,1)S(1)}, bf16[2,2,4,16,1024]{4,3,2,1,0:T(8,128)(2,1)S(1)}, u32[]{:S(2)}, u32[]{:S(2)}) collective-permute-start(bf16[2,2,4,16,1024]{4,3,2,1,0:T(8,128)(2,1)S(1)} %pad_maximum_fusion.1.refs_0_), channel_id=1, source_target_pairs={{0,16},{16,0},{1,17},{17,1},{2,18},{18,2},{3,19},{19,3},{4,20},{20... | collective-permute-start | bytes 1572872 | tf_op jit(solution)/shard_map/ppermute | solution.py:591
  54.4 23.9 %collective-permute-start.10 = (bf16[2,2,4,16,1024]{4,3,2,1,0:T(8,128)(2,1)S(1)}, bf16[2,2,4,16,1024]{4,3,2,1,0:T(8,128)(2,1)}, u32[]{:S(2)}, u32[]{:S(2)}) collective-permute-start(bf16[2,2,4,16,1024]{4,3,2,1,0:T(8,128)(2,1)S(1)} %pad_maximum_fusion.1.refs_0_), channel_id=1, source_target_pairs={{0,8},{1,9},{2,10},{3,11},{4,12},{5,13},{6,14},{7,15},{8,0},{9,1},... | collective-permute-start | bytes 1572872 | tf_op jit(solution)/shard_map/ppermute | solution.py:591
  70.1 9.7 %collective-permute-start.11 = (bf16[512,512]{1,0:T(8,128)(2,1)S(1)}, bf16[512,512]{1,0:T(8,128)(2,1)S(1)}, u32[]{:S(2)}, u32[]{:S(2)}) collective-permute-start(bf16[512,512]{1,0:T(8,128)(2,1)S(1)} %constant_dynamic-update-slice_fusion.page_own), channel_id=1, source_target_pairs={{0,1},{1,0},{2,3},{3,2},{4,5},{5,4},{6,7},{7,6},{8,9},{9,8},{10,11... | collective-permute-start | bytes 1572872 | tf_op jit(solution)/shard_map/ppermute | solution.py:591
  70.8 9.3 %collective-permute-start.12 = (bf16[512,512]{1,0:T(8,128)(2,1)}, bf16[512,512]{1,0:T(8,128)(2,1)S(1)}, u32[]{:S(2)}, u32[]{:S(2)}) collective-permute-start(bf16[512,512]{1,0:T(8,128)(2,1)} %collective-permute-done.6.page_y), channel_id=1, source_target_pairs={{0,1},{1,0},{2,3},{3,2},{4,5},{5,4},{6,7},{7,6},{8,9},{9,8},{10,11... | collective-permute-start | bytes 1572872 | tf_op jit(solution)/shard_map/ppermute | solution.py:591
  70.9 9.5 %collective-permute-start.13 = (bf16[4,128,512]{2,1,0:T(8,128)(2,1)S(1)}, bf16[4,128,512]{2,1,0:T(8,128)(2,1)S(1)}, u32[]{:S(2)}, u32[]{:S(2)}) collective-permute-start(bf16[4,128,512]{2,1,0:T(8,128)(2,1)S(1)} %pad_maximum_fusion.kv_own), channel_id=1, source_target_pairs={{0,1},{1,0},{2,3},{3,2},{4,5},{5,4},{6,7},{7,6},{8,9},{9,8},{10,11... | collective-permute-start | bytes 1572872 | tf_op jit(solution)/shard_map/ppermute | solution.py:591
  71.3 9.0 %collective-permute-start.14 = (bf16[4,128,512]{2,1,0:T(8,128)(2,1)}, bf16[4,128,512]{2,1,0:T(8,128)(2,1)S(1)}, u32[]{:S(2)}, u32[]{:S(2)}) collective-permute-start(bf16[4,128,512]{2,1,0:T(8,128)(2,1)} %collective-permute-done.7.kv_y), channel_id=1, source_target_pairs={{0,1},{1,0},{2,3},{3,2},{4,5},{5,4},{6,7},{7,6},{8,9},{9,8},{10,11... | collective-permute-start | bytes 1572872 | tf_op jit(solution)/shard_map/ppermute | solution.py:591
  78.3 17.7 %collective-permute-start.17 = (bf16[2,2,4,16,1024]{4,3,2,1,0:T(8,128)(2,1)S(1)}, bf16[2,2,4,16,1024]{4,3,2,1,0:T(8,128)(2,1)S(1)}, u32[]{:S(2)}, u32[]{:S(2)}) collective-permute-start(bf16[2,2,4,16,1024]{4,3,2,1,0:T(8,128)(2,1)S(1)} %pad_maximum_fusion.1.refs_0_), channel_id=1, source_target_pairs={{0,1},{1,0},{2,3},{3,2},{4,5},{5,4},{6,7},{7,6},{8,9},{9,8},{10,11... | collective-permute-start | bytes 1572872 | tf_op jit(solution)/shard_map/ppermute | solution.py:591
  79.8 15.4 %collective-permute-start.15 = (bf16[2,2,4,16,1024]{4,3,2,1,0:T(8,128)(2,1)}, bf16[2,2,4,16,1024]{4,3,2,1,0:T(8,128)(2,1)S(1)}, u32[]{:S(2)}, u32[]{:S(2)}) collective-permute-start(bf16[2,2,4,16,1024]{4,3,2,1,0:T(8,128)(2,1)} %collective-permute-done.10.refs_4_), channel_id=1, source_target_pairs={{0,16},{16,0},{1,17},{17,1},{2,18},{18,2},{3,19},{19,3},{4,20},{20... | collective-permute-start | bytes 1572872 | tf_op jit(solution)/shard_map/ppermute | solution.py:591
  80.1 15.9 %collective-permute-start.19 = (bf16[2,2,4,16,1024]{4,3,2,1,0:T(8,128)(2,1)}, bf16[2,2,4,16,1024]{4,3,2,1,0:T(8,128)(2,1)S(1)}, u32[]{:S(2)}, u32[]{:S(2)}) collective-permute-start(bf16[2,2,4,16,1024]{4,3,2,1,0:T(8,128)(2,1)} %collective-permute-done.10.refs_4_), channel_id=1, source_target_pairs={{0,1},{1,0},{2,3},{3,2},{4,5},{5,4},{6,7},{7,6},{8,9},{9,8},{10,11... | collective-permute-start | bytes 1572872 | tf_op jit(solution)/shard_map/ppermute | solution.py:591
  95.1 3.6 %copy-start.3 = (bf16[2,512,512]{2,1,0:T(8,128)(2,1)}, bf16[2,512,512]{2,1,0:T(8,128)(2,1)S(1)}, u32[]{:S(2)}) copy-start(bf16[2,512,512]{2,1,0:T(8,128)(2,1)S(1)} %attend.1.a_hbm) | copy-start | bytes 3145732
  95.1 12.2 %copy-start.11 = (s32[128,1,2]{0,2,1:T(2,128)S(1)}, s32[128,1,2]{0,2,1:T(2,128)}, u32[]{:S(2)}) copy-start(s32[128,1,2]{0,2,1:T(2,128)} %param.16) | copy-start | bytes 3076
  95.1 35.0 %copy-start.2 = (bf16[128,1,2048]{2,0,1:T(8,128)(2,1)S(1)}, bf16[128,1,2048]{2,0,1:T(8,128)(2,1)}, u32[]{:S(2)}) copy-start(bf16[128,1,2048]{2,0,1:T(8,128)(2,1)} %param.13) | copy-start | bytes 1572868
  95.2 35.0 %copy-start.4 = (f32[2048]{0:T(1024)S(1)}, f32[2048]{0:T(1024)}, u32[]{:S(2)}) copy-start(f32[2048]{0:T(1024)} %param.15) | copy-start | bytes 24580
  95.2 2.0 collective-permute-start.18
  95.5 2.4 collective-permute-start.20
  95.8 2.9 %collective-permute-start.16 = (bf16[512,512]{1,0:T(8,128)(2,1)S(1)}, bf16[512,512]{1,0:T(8,128)(2,1)S(1)}, u32[]{:S(2)}, u32[]{:S(2)}) collective-permute-start(bf16[512,512]{1,0:T(8,128)(2,1)S(1)} %slice_bitcast_fusion), channel_id=1, source_target_pairs={{0,1},{1,0},{2,3},{3,2},{4,5},{5,4},{6,7},{7,6},{8,9},{9,8},{10,11... | collective-permute-start | bytes 1572872 | tf_op jit(solution)/shard_map/ppermute | solution.py:591
  103.7 14.5 %collective-permute-start.21 = (bf16[128,2048]{1,0:T(8,128)(2,1)}, bf16[128,2048]{1,0:T(8,128)(2,1)S(1)}, u32[]{:S(2)}, u32[]{:S(2)}) collective-permute-start(bf16[128,2048]{1,0:T(8,128)(2,1)} %get-tuple-element.54), channel_id=1, source_target_pairs={{0,6},{1,7},{2,4},{3,5},{4,2},{5,3},{6,0},{7,1},{8,14},{9,15},{10,... | collective-permute-start | bytes 1572872 | tf_op jit(solution)/shard_map/ppermute | solution.py:591
  106.2 23.8 %collective-permute-start.22 = (bf16[128,2048]{1,0:T(8,128)(2,1)}, bf16[128,2048]{1,0:T(8,128)(2,1)S(1)}, u32[]{:S(2)}, u32[]{:S(2)}) collective-permute-start(bf16[128,2048]{1,0:T(8,128)(2,1)} %get-tuple-element.55), channel_id=1, source_target_pairs={{0,4},{1,5},{2,6},{3,7},{4,0},{5,1},{6,2},{7,3},{8,12},{9,13},{10,... | collective-permute-start | bytes 1572872 | tf_op jit(solution)/shard_map/ppermute | solution.py:591
  106.2 23.9 %collective-permute-start.23 = (bf16[128,2048]{1,0:T(8,128)(2,1)}, bf16[128,2048]{1,0:T(8,128)(2,1)}, u32[]{:S(2)}, u32[]{:S(2)}) collective-permute-start(bf16[128,2048]{1,0:T(8,128)(2,1)} %get-tuple-element.56), channel_id=1, source_target_pairs={{0,2},{1,3},{2,0},{3,1},{4,6},{5,7},{6,4},{7,5},{8,10},{9,11},{10,... | collective-permute-start | bytes 1572872 | tf_op jit(solution)/shard_map/ppermute | solution.py:591
  132.5 54.5 %copy-start.5 = (bf16[1,512,2048]{2,1,0:T(8,128)(2,1)S(1)}, bf16[1,512,2048]{2,1,0:T(8,128)(2,1)}, u32[]{:S(2)}) copy-start(bf16[1,512,2048]{2,1,0:T(8,128)(2,1)} %param.19) | copy-start | bytes 6291460
  194.1 5.2 %copy-start.12 = (f32[128,1,2]{0,2,1:T(2,128)S(1)}, f32[128,1,2]{0,2,1:T(2,128)}, u32[]{:S(2)}) copy-start(f32[128,1,2]{0,2,1:T(2,128)} %param.17) | copy-start | bytes 3076
  194.2 52.6 %all-to-all-start.2 = ((bf16[16,32,2048]{2,1,0:T(8,128)(2,1)}), bf16[16,32,2048]{2,1,0:T(8,128)(2,1)S(1)}, u32[]{:S(2)}, u32[]{:S(2)}) async-start(bf16[16,32,2048]{2,1,0:T(8,128)(2,1)} %bitcast.52), calls=%async_computation.2 | async-start | bytes 4194304 | tf_op jit(solution)/shard_map/all_to_all | solution.py:786
  246.7 1.2 copy-start.1

commit v17 on v15

--- a/solution.py
+++ b/solution.py
@@ -350,7 +350,8 @@
     model = 2 * columns
     return pl.pallas_call(
         project_pair_kernel,
-        out_shape=[pltpu.HBM((rows // parts, model), BF16)] * parts,
+        out_shape=[jax.ShapeDtypeStruct((rows // parts, model), BF16)]
+        + [pltpu.HBM((rows // parts, model), BF16)] * (parts - 1),
         in_specs=[in_hbm()] * 10,
         out_specs=[in_hbm()] * parts,
         scratch_shapes=[
@@ -406,7 +407,7 @@
 
 
 def route_kernel(resid_ref, gain_ref, slots_ref, *refs):
-    parts_refs, (stream_ref, out_ref) = refs[:-2], refs[-2:]
+    parts_refs, (stream_hbm, out_ref, stream_ref, sem) = refs[:-4], refs[-4:]
     seqs = resid_ref.shape[0]
     streams = []
     for seq in range(seqs):
@@ -417,6 +418,8 @@
         streams.append(stream + projected)
     stream = jnp.concatenate(streams, 0) if seqs > 1 else streams[0]
     stream_ref[...] = stream
+    back = pltpu.make_async_copy(stream_ref, stream_hbm, sem.at[0])
+    back.start()
     normed = stream * lax.rsqrt(jnp.mean(stream * stream, 1, keepdims=True) + eps_norm)
     normed = (normed * gain_ref[...]).astype(BF16)
     slots, rows = out_ref.shape[0], stream.shape[0]
@@ -425,6 +428,7 @@
     for k in range(1, slots_ref.shape[0]):
         hit = hit | (place == slots_ref[k : k + 1, :])
     out_ref[...] = jnp.dot(hit.astype(BF16), normed, preferred_element_type=F32).astype(BF16)
+    back.wait()
 
 
 def route(parts, resid, gain, slots_of, slots):
@@ -433,11 +437,12 @@
     return pl.pallas_call(
         route_kernel,
         out_shape=(
-            jax.ShapeDtypeStruct((rows, model), F32),
+            pltpu.HBM((rows, model), F32),
             jax.ShapeDtypeStruct((slots, model), BF16),
         ),
         in_specs=[in_vmem()] * (3 + len(parts)),
-        out_specs=(in_vmem(), in_vmem()),
+        out_specs=(in_hbm(), in_vmem()),
+        scratch_shapes=[pltpu.VMEM((rows, model), F32), pltpu.SemaphoreType.DMA((1,))],
         compiler_params=pltpu.CompilerParams(vmem_limit_bytes=HIGH_VMEM),
         cost_estimate=pl.CostEstimate(
             flops=2 * slots * rows * model,
@@ -589,9 +594,6 @@
 
     query_slots = queries.reshape(local_rows, heads, width).transpose(1, 0, 2)
     query_slots = query_slots.reshape(members, heads // members, local_rows, width)
-    q = lax.all_to_all(
-        query_slots, "head", split_axis=0, concat_axis=0, tiled=True, axis_index_groups=group_sets
-    )
 
     def page_target(source, other):
         p, plane, rest = source // members, (source // plane_bit) % 2, source % plane_bit
@@ -609,22 +611,30 @@
     w = w.reshape(2, 2, heads // 4, share, columns)
     w_keep = lax.dynamic_index_in_dim(w, y, 1, keepdims=False)
     w_give = lax.dynamic_index_in_dim(w, 1 - y, 1, keepdims=False)
-    kv_own = [kv_same]
-    for t in range(1, planes):
-        kv_own.append(flipped(kv_other if t % 2 else kv_same, "head", t * plane_bit))
     w_got = flipped(w_give, "head", 2)
-
-    (page_a, page_b, kv_own, q), w_got = lax.optimization_barrier(
-        ((page_a, page_b, kv_own, q), w_got)
+    kv_last, query_slots, w_got = lax.optimization_barrier((kv_other, query_slots, w_got))
+    kv_own = [
+        kv_same,
+        flipped(kv_other, "head", plane_bit),
+        flipped(kv_same, "head", 2 * plane_bit),
+        flipped(kv_last, "head", 3 * plane_bit),
+    ]
+    q = lax.all_to_all(
+        query_slots, "head", split_axis=0, concat_axis=0, tiled=True, axis_index_groups=group_sets
+    )
+    w_both = jnp.stack([w_keep, w_got], 1)
+    w_same = lax.dynamic_index_in_dim(w_both, b, 0, keepdims=False)
+    w_other = lax.dynamic_index_in_dim(w_both, 1 - b, 0, keepdims=False)
+    w_first = flipped(w_other, "head", plane_bit)
+
+    page_a, page_b, kv_own, w_first, q = lax.optimization_barrier(
+        (page_a, page_b, kv_own, w_first, q)
     )
     own_pages = jnp.concatenate([page_a, page_b], 0)
     kv_own = jnp.stack(kv_own, 0)
     pages_y = flipped(own_pages, "head", 2)
     kv_y = flipped(kv_own, "head", 2)
-    w_both = jnp.stack([w_keep, w_got], 1)
-    w_same = lax.dynamic_index_in_dim(w_both, b, 0, keepdims=False)
-    w_other = lax.dynamic_index_in_dim(w_both, 1 - b, 0, keepdims=False)
-    w_near = jnp.stack([w_same, flipped(w_other, "head", plane_bit)], 0)
+    w_near = jnp.stack([w_same, w_first], 0)
     w_near_x = flipped(w_near, "grp", 1)
     w_far = flipped(w_near, "head", members)
     pages_y, kv_y, own_pages, kv_own, w_near_x = lax.optimization_barrier(

time: 241 us -> 247 us (1.025)
  starting transfers between devices: 30 us -> 34.4 us
    ppermute x22, starting transfers between devices: 15.8 us -> 19.7 us  [flipped(): return lax.ppermute(value, axis, pairs)]
  transfers between devices with their start and end apart: 26 -> 26, of which waited for: 14 -> 13; matrix products, arithmetic and copies ran while one was open for 2% -> 2% of each run, Pallas kernels for 6% -> 6%
where the time goes in v17:
time: 247 us
  waiting for transfers between devices  119 us (48%)
  blocking collectives  54 us (22%)
  starting transfers between devices  34.4 us (14%)
  Pallas kernels  31.2 us (13%)
  local copies, waits for them, and re-layouts  6.09 us (2%)
    ppermute x22, waiting for transfers between devices, flipped(): return lax.ppermute(value, axis, pairs)  71.7 us
    all_to_all x1, blocking collectives, local(): lax.all_to_all(outgoing.reshape(n, slots // n, model), 'head', split_axis...  54 us
    all_to_all x1, waiting for transfers between devices, local(): lax.all_to_all(answered, 'head', split_axis=0, concat_axis=0, tiled=True)  47.3 us
    ppermute x22, starting transfers between devices, flipped(): return lax.ppermute(value, axis, pairs)  19.7 us
    pallas_call x1, Pallas kernels, attend_pair(): pl.pallas_call(functools.partial(attend_pair_kernel, block, chunk, width)...  15.4 us
    pallas_call x1, Pallas kernels, expert_pair(): pl.pallas_call(kernel, out_shape=pltpu.HBM((rows, model), BF16), in_specs...  6.87 us
    all_to_all x1, starting transfers between devices, parts_in_pairs(): lax.all_to_all(query_slots, 'head', split_axis=0, concat_axis=0, tiled=Tr...  5.39 us
    all_to_all x1, starting transfers between devices, local(): lax.all_to_all(answered, 'head', split_axis=0, concat_axis=0, tiled=True)  5.13 us
  transfers between devices with their start and end apart: 26, of which 13 were waited for; matrix products, arithmetic and copies ran while one was open for 2% of the time, Pallas kernels for 6%

profile of v17, /device:TPU:13, one launch (start us, length us, event | category | flops | bytes accessed | tf_op | source)
XLA Modules:
  0.0 246.7 jit_solution(17015967578559009083)
XLA Ops:
  0.1 1.2 copy-done
  1.3 0.3 collective-permute-start.4
  1.6 0.5 constant_dynamic-slice_fusion.2
  2.2 1.3 copy.29
  3.5 5.0 %collective-permute-done.4 = bf16[2,4,16,1024]{3,2,1,0:T(8,128)(2,1)S(1)} collective-permute-done((bf16[2,4,16,1024]{3,2,1,0:T(8,128)(2,1)S(1)}, bf16[2,4,16,1024]{3,2,1,0:T(8,128)(2,1)S(1)}, u32[]{:S(2)}, u32[]{:S(2)}) %collective-permute-start.4) | collective-permute-done | bytes 262176 | tf_op jit(solution)/shard_map/ppermute | solution.py:578
  8.6 5.4 %all-to-all-start = ((bf16[8,2,128,256]{3,2,1,0:T(8,128)(2,1)}), bf16[8,2,128,256]{3,2,1,0:T(8,128)(2,1)S(1)}, u32[]{:S(2)}, u32[]{:S(2)}) async-start(bf16[8,2,128,256]{3,2,1,0:T(8,128)(2,1)} %bitcast.9), calls=%async_computation | async-start | bytes 2097152 | tf_op jit(solution)/shard_map/all_to_all | solution.py:622
  14.0 0.3 collective-permute-start.2
  14.2 4.2 %collective-permute-start = (bf16[256,512]{1,0:T(8,128)(2,1)}, bf16[256,512]{1,0:T(8,128)(2,1)S(1)}, u32[]{:S(2)}, u32[]{:S(2)}) collective-permute-start(bf16[256,512]{1,0:T(8,128)(2,1)} %bitcast.4), channel_id=1, source_target_pairs={{0,0},{1,1},{2,2},{3,3},{4,8},{5,9},{6,10},{7,11},{8,4},{9,5},{10,... | collective-permute-start | bytes 786440 | tf_op jit(solution)/shard_map/ppermute | solution.py:603
  18.6 1.2 collective-permute-start.6
  19.8 1.3 collective-permute-start.3
  21.1 10.0 %collective-permute-done.2 = bf16[128,512]{1,0:T(8,128)(2,1)} collective-permute-done((bf16[128,512]{1,0:T(8,128)(2,1)S(1)}, bf16[128,512]{1,0:T(8,128)(2,1)}, u32[]{:S(2)}, u32[]{:S(2)}) %collective-permute-start.2) | collective-permute-done | bytes 131104 | tf_op jit(solution)/shard_map/ppermute | solution.py:578
  31.1 1.4 collective-permute-start.5
  32.5 12.9 %collective-permute-done.3 = bf16[128,512]{1,0:T(8,128)(2,1)S(1)} collective-permute-done((bf16[128,512]{1,0:T(8,128)(2,1)S(1)}, bf16[128,512]{1,0:T(8,128)(2,1)S(1)}, u32[]{:S(2)}, u32[]{:S(2)}) %collective-permute-start.3) | collective-permute-done | bytes 131104 | tf_op jit(solution)/shard_map/ppermute | solution.py:578
  45.4 1.1 pad_maximum_fusion.1.kv_own
  46.5 0.3 collective-permute-start.9
  46.9 1.0 constant_dynamic-update-slice_fusion.page_own
  47.9 1.2 collective-permute-start.8
  49.2 1.3 collective-permute-start.10
  50.5 2.8 %collective-permute-start.7 = (bf16[2,2,4,16,1024]{4,3,2,1,0:T(8,128)(2,1)S(1)}, bf16[2,2,4,16,1024]{4,3,2,1,0:T(8,128)(2,1)S(1)}, u32[]{:S(2)}, u32[]{:S(2)}) collective-permute-start(bf16[2,2,4,16,1024]{4,3,2,1,0:T(8,128)(2,1)S(1)} %pad_maximum_fusion.refs_0_), channel_id=1, source_target_pairs={{0,8},{1,9},{2,10},{3,11},{4,12},{5,13},{6,14},{7,15},{8,0},{9,1},... | collective-permute-start | bytes 1572872 | tf_op jit(solution)/shard_map/ppermute | solution.py:578
  53.2 5.5 %collective-permute-done.9.kv_y = bf16[4,128,512]{2,1,0:T(8,128)(2,1)S(1)} collective-permute-done((bf16[4,128,512]{2,1,0:T(8,128)(2,1)S(1)}, bf16[4,128,512]{2,1,0:T(8,128)(2,1)S(1)}, u32[]{:S(2)}, u32[]{:S(2)}) %collective-permute-start.9) | collective-permute-done | bytes 524320 | tf_op jit(solution)/shard_map/ppermute | solution.py:578
  58.7 11.2 %collective-permute-done.8.page_y = bf16[512,512]{1,0:T(8,128)(2,1)S(1)} collective-permute-done((bf16[512,512]{1,0:T(8,128)(2,1)S(1)}, bf16[512,512]{1,0:T(8,128)(2,1)S(1)}, u32[]{:S(2)}, u32[]{:S(2)}) %collective-permute-start.8) | collective-permute-done | bytes 524320 | tf_op jit(solution)/shard_map/ppermute | solution.py:578
  69.9 2.3 collective-permute-start.11
  72.2 0.5 collective-permute-start.13
  72.7 2.4 collective-permute-done.7.refs_4_
  75.1 1.5 collective-permute-start.17
  76.6 0.3 collective-permute-start.15
  76.9 0.3 collective-permute-start.19
  77.2 15.4 %attend.1.a_hbm = bf16[2,512,512]{2,1,0:T(8,128)(2,1)S(1)} custom-call(bf16[8,2,128,256]{3,2,1,0:T(8,128)(2,1)} %copy-done.8, bf16[512,512]{1,0:T(8,128)(2,1)S(1)} %constant_dynamic-update-slice_fusion.page_own, bf16[512,512]{1,0:T(8,128)(2,1)S(1)} %collective-permute-done.8.page_y, bf16[512,512]{1,0:T(8,128)(2,1)S(1)} %collective-permute-done.11.page_c, ...), custom_call_target="tpu_custom_call" | custom-call | flops 7516192768 | bytes 6291456 | tf_op jit(solution)/shard_map/attend/pallas_call | solution.py:270
  92.7 0.3 collective-permute-start.18
  93.0 0.3 collective-permute-start.20
  93.2 0.2 collective-permute-start.16
  93.5 1.2 collective-permute-done.18.refs_3_
  94.6 0.7 collective-permute-done.20.refs_7_
  95.4 0.7 collective-permute-done.16.got_hbm
  96.2 4.8 %project.1 = (bf16[128,2048]{1,0:T(8,128)(2,1)S(1)}, bf16[128,2048]{1,0:T(8,128)(2,1)}, bf16[128,2048]{1,0:T(8,128)(2,1)}, bf16[128,2048]{1,0:T(8,128)(2,1)}) custom-call(bf16[2,512,512]{2,1,0:T(8,128)(2,1)} %copy-done.3, bf16[512,512]{1,0:T(8,128)(2,1)S(1)} %collective-permute-done.16.got_hbm, bf16[2,2,4,16,1024]{4,3,2,1,0:T(8,128)(2,1)S(1)} %pad_maximum_fusion.refs_0_, ...), custom_call_target="tpu_custom_call" | custom-call | flops 2147483648 | bytes 7340032 | tf_op jit(solution)/shard_map/project/pallas_call | solution.py:351
  100.9 2.8 %collective-permute-start.21 = (bf16[128,2048]{1,0:T(8,128)(2,1)}, bf16[128,2048]{1,0:T(8,128)(2,1)S(1)}, u32[]{:S(2)}, u32[]{:S(2)}) collective-permute-start(bf16[128,2048]{1,0:T(8,128)(2,1)} %get-tuple-element.54), channel_id=1, source_target_pairs={{0,6},{1,7},{2,4},{3,5},{4,2},{5,3},{6,0},{7,1},{8,14},{9,15},{10,... | collective-permute-start | bytes 1572872 | tf_op jit(solution)/shard_map/ppermute | solution.py:578
  103.8 1.1 collective-permute-start.23
  105.2 0.2 reduce_window_sum.11
  105.7 10.3 %collective-permute-done.21 = bf16[128,2048]{1,0:T(8,128)(2,1)S(1)} collective-permute-done((bf16[128,2048]{1,0:T(8,128)(2,1)}, bf16[128,2048]{1,0:T(8,128)(2,1)S(1)}, u32[]{:S(2)}, u32[]{:S(2)}) %collective-permute-start.21) | collective-permute-done | bytes 524320 | tf_op jit(solution)/shard_map/ppermute | solution.py:578
  116.0 11.3 %collective-permute-done.22 = bf16[128,2048]{1,0:T(8,128)(2,1)S(1)} collective-permute-done((bf16[128,2048]{1,0:T(8,128)(2,1)}, bf16[128,2048]{1,0:T(8,128)(2,1)S(1)}, u32[]{:S(2)}, u32[]{:S(2)}) %collective-permute-start.22) | collective-permute-done | bytes 524320 | tf_op jit(solution)/shard_map/ppermute | solution.py:578
  127.3 0.4 collective-permute-done.23
  127.7 2.4 route.1
  130.1 54.0 %all_to_all.15 = bf16[16,32,2048]{2,1,0:T(8,128)(2,1)S(1)} all-to-all(bf16[16,32,2048]{2,1,0:T(8,128)(2,1)S(1)} %bitcast.42), channel_id=1, replica_groups=mesh['grp'=2,'head'=16] {'head'}, dimensions={0} | all-to-all | bytes 4194304 | tf_op jit(solution)/shard_map/all_to_all | solution.py:761
  184.1 6.9 %expert.1 = bf16[512,2048]{1,0:T(8,128)(2,1)} custom-call(bf16[512,2048]{1,0:T(8,128)(2,1)S(1)} %bitcast.43, bf16[2048,1024]{1,0:T(8,128)(2,1)} %bitcast.64, bf16[512,2048]{1,0:T(8,128)(2,1)S(1)} %bitcast.51), custom_call_target="tpu_custom_call" | custom-call | flops 3221225472 | bytes 10485760 | tf_op jit(solution)/shard_map/expert/pallas_call | solution.py:513
  191.0 5.1 %all-to-all-start.2 = ((bf16[16,32,2048]{2,1,0:T(8,128)(2,1)}), bf16[16,32,2048]{2,1,0:T(8,128)(2,1)S(1)}, u32[]{:S(2)}, u32[]{:S(2)}) async-start(bf16[16,32,2048]{2,1,0:T(8,128)(2,1)} %bitcast.52), calls=%async_computation.2 | async-start | bytes 4194304 | tf_op jit(solution)/shard_map/all_to_all | solution.py:774
  196.3 47.3 %all-to-all-done.2 = bf16[16,32,2048]{2,1,0:T(8,128)(2,1)S(1)} async-done(((bf16[16,32,2048]{2,1,0:T(8,128)(2,1)}), bf16[16,32,2048]{2,1,0:T(8,128)(2,1)S(1)}, u32[]{:S(2)}, u32[]{:S(2)}) %all-to-all-start.2) | async-done | bytes 2097184 | tf_op jit(solution)/shard_map/all_to_all | solution.py:774
  243.6 1.2 copy-done.1
  244.8 1.7 combine.1
  (56 shorter events, 1.2 us)
Async XLA Ops:
  0.0 1.2 copy-start
  0.0 1.6 copy-start.6
  0.0 2.2 copy-start.7
  1.3 7.2 %collective-permute-start.4 = (bf16[2,4,16,1024]{3,2,1,0:T(8,128)(2,1)S(1)}, bf16[2,4,16,1024]{3,2,1,0:T(8,128)(2,1)S(1)}, u32[]{:S(2)}, u32[]{:S(2)}) collective-permute-start(bf16[2,4,16,1024]{3,2,1,0:T(8,128)(2,1)S(1)} %get-tuple-element.62), channel_id=1, source_target_pairs={{0,2},{1,3},{2,0},{3,1},{4,6},{5,7},{6,4},{7,5},{8,10},{9,11},{10,... | collective-permute-start | bytes 786440 | tf_op jit(solution)/shard_map/ppermute | solution.py:578
  8.6 36.8 %all-to-all-start = ((bf16[8,2,128,256]{3,2,1,0:T(8,128)(2,1)}), bf16[8,2,128,256]{3,2,1,0:T(8,128)(2,1)S(1)}, u32[]{:S(2)}, u32[]{:S(2)}) async-start(bf16[8,2,128,256]{3,2,1,0:T(8,128)(2,1)} %bitcast.9), calls=%async_computation | async-start | bytes 2097152 | tf_op jit(solution)/shard_map/all_to_all | solution.py:622
  14.0 17.1 %collective-permute-start.2 = (bf16[128,512]{1,0:T(8,128)(2,1)S(1)}, bf16[128,512]{1,0:T(8,128)(2,1)}, u32[]{:S(2)}, u32[]{:S(2)}) collective-permute-start(bf16[128,512]{1,0:T(8,128)(2,1)S(1)} %bitcast.60), channel_id=1, source_target_pairs={{0,4},{1,5},{2,6},{3,7},{4,0},{5,1},{6,2},{7,3},{8,12},{9,13},{10,... | collective-permute-start | bytes 393224 | tf_op jit(solution)/shard_map/ppermute | solution.py:578
  14.2 31.1 %collective-permute-start = (bf16[256,512]{1,0:T(8,128)(2,1)}, bf16[256,512]{1,0:T(8,128)(2,1)S(1)}, u32[]{:S(2)}, u32[]{:S(2)}) collective-permute-start(bf16[256,512]{1,0:T(8,128)(2,1)} %bitcast.4), channel_id=1, source_target_pairs={{0,0},{1,1},{2,2},{3,3},{4,8},{5,9},{6,10},{7,11},{8,4},{9,5},{10,... | collective-permute-start | bytes 786440 | tf_op jit(solution)/shard_map/ppermute | solution.py:603
  18.5 26.9 %collective-permute-start.1 = (bf16[256,512]{1,0:T(8,128)(2,1)}, bf16[256,512]{1,0:T(8,128)(2,1)}, u32[]{:S(2)}, u32[]{:S(2)}) collective-permute-start(bf16[256,512]{1,0:T(8,128)(2,1)} %bitcast.4), channel_id=1, source_target_pairs={{0,8},{1,9},{2,10},{3,11},{4,0},{5,1},{6,2},{7,3},{8,12},{9,13},{1... | collective-permute-start | bytes 786440 | tf_op jit(solution)/shard_map/ppermute | solution.py:603
  18.6 26.8 %collective-permute-start.6 = (bf16[2,4,16,1024]{3,2,1,0:T(8,128)(2,1)S(1)}, bf16[2,4,16,1024]{3,2,1,0:T(8,128)(2,1)S(1)}, u32[]{:S(2)}, u32[]{:S(2)}) collective-permute-start(bf16[2,4,16,1024]{3,2,1,0:T(8,128)(2,1)S(1)} %get-tuple-element.60), channel_id=1, source_target_pairs={{0,4},{1,5},{2,6},{3,7},{4,0},{5,1},{6,2},{7,3},{8,12},{9,13},{10,... | collective-permute-start | bytes 786440 | tf_op jit(solution)/shard_map/ppermute | solution.py:578
  19.8 25.5 %collective-permute-start.3 = (bf16[128,512]{1,0:T(8,128)(2,1)S(1)}, bf16[128,512]{1,0:T(8,128)(2,1)S(1)}, u32[]{:S(2)}, u32[]{:S(2)}) collective-permute-start(bf16[128,512]{1,0:T(8,128)(2,1)S(1)} %bitcast.56), channel_id=1, source_target_pairs={{0,8},{1,9},{2,10},{3,11},{4,12},{5,13},{6,14},{7,15},{8,0},{9,1},... | collective-permute-start | bytes 393224 | tf_op jit(solution)/shard_map/ppermute | solution.py:578
  31.1 14.3 %collective-permute-start.5 = (bf16[128,512]{1,0:T(8,128)(2,1)S(1)}, bf16[128,512]{1,0:T(8,128)(2,1)S(1)}, u32[]{:S(2)}, u32[]{:S(2)}) collective-permute-start(bf16[128,512]{1,0:T(8,128)(2,1)S(1)} %bitcast.61), channel_id=1, source_target_pairs={{0,12},{1,13},{2,14},{3,15},{4,8},{5,9},{6,10},{7,11},{8,4},{9,5},... | collective-permute-start | bytes 393224 | tf_op jit(solution)/shard_map/ppermute | solution.py:578
  45.4 3.8 %copy-start.8 = (bf16[8,2,128,256]{3,2,1,0:T(8,128)(2,1)}, bf16[8,2,128,256]{3,2,1,0:T(8,128)(2,1)S(1)}, u32[]{:S(2)}) copy-start(bf16[8,2,128,256]{3,2,1,0:T(8,128)(2,1)S(1)} %all-to-all-done.q_hbm) | copy-start | bytes 3145732
  46.5 12.1 %collective-permute-start.9 = (bf16[4,128,512]{2,1,0:T(8,128)(2,1)S(1)}, bf16[4,128,512]{2,1,0:T(8,128)(2,1)S(1)}, u32[]{:S(2)}, u32[]{:S(2)}) collective-permute-start(bf16[4,128,512]{2,1,0:T(8,128)(2,1)S(1)} %pad_maximum_fusion.1.kv_own), channel_id=1, source_target_pairs={{0,2},{1,3},{2,0},{3,1},{4,6},{5,7},{6,4},{7,5},{8,10},{9,11},{10,... | collective-permute-start | bytes 1572872 | tf_op jit(solution)/shard_map/ppermute | solution.py:578
  47.9 22.0 %collective-permute-start.8 = (bf16[512,512]{1,0:T(8,128)(2,1)S(1)}, bf16[512,512]{1,0:T(8,128)(2,1)S(1)}, u32[]{:S(2)}, u32[]{:S(2)}) collective-permute-start(bf16[512,512]{1,0:T(8,128)(2,1)S(1)} %constant_dynamic-update-slice_fusion.page_own), channel_id=1, source_target_pairs={{0,2},{1,3},{2,0},{3,1},{4,6},{5,7},{6,4},{7,5},{8,10},{9,11},{10,... | collective-permute-start | bytes 1572872 | tf_op jit(solution)/shard_map/ppermute | solution.py:578
  49.2 20.7 %collective-permute-start.10 = (bf16[2,2,4,16,1024]{4,3,2,1,0:T(8,128)(2,1)S(1)}, bf16[2,2,4,16,1024]{4,3,2,1,0:T(8,128)(2,1)S(1)}, u32[]{:S(2)}, u32[]{:S(2)}) collective-permute-start(bf16[2,2,4,16,1024]{4,3,2,1,0:T(8,128)(2,1)S(1)} %pad_maximum_fusion.refs_0_), channel_id=1, source_target_pairs={{0,16},{16,0},{1,17},{17,1},{2,18},{18,2},{3,19},{19,3},{4,20},{20... | collective-permute-start | bytes 1572872 | tf_op jit(solution)/shard_map/ppermute | solution.py:578
  50.5 24.7 %collective-permute-start.7 = (bf16[2,2,4,16,1024]{4,3,2,1,0:T(8,128)(2,1)S(1)}, bf16[2,2,4,16,1024]{4,3,2,1,0:T(8,128)(2,1)S(1)}, u32[]{:S(2)}, u32[]{:S(2)}) collective-permute-start(bf16[2,2,4,16,1024]{4,3,2,1,0:T(8,128)(2,1)S(1)} %pad_maximum_fusion.refs_0_), channel_id=1, source_target_pairs={{0,8},{1,9},{2,10},{3,11},{4,12},{5,13},{6,14},{7,15},{8,0},{9,1},... | collective-permute-start | bytes 1572872 | tf_op jit(solution)/shard_map/ppermute | solution.py:578
  69.9 6.7 %collective-permute-start.11 = (bf16[512,512]{1,0:T(8,128)(2,1)S(1)}, bf16[512,512]{1,0:T(8,128)(2,1)S(1)}, u32[]{:S(2)}, u32[]{:S(2)}) collective-permute-start(bf16[512,512]{1,0:T(8,128)(2,1)S(1)} %constant_dynamic-update-slice_fusion.page_own), channel_id=1, source_target_pairs={{0,1},{1,0},{2,3},{3,2},{4,5},{5,4},{6,7},{7,6},{8,9},{9,8},{10,11... | collective-permute-start | bytes 1572872 | tf_op jit(solution)/shard_map/ppermute | solution.py:578
  72.2 4.7 %collective-permute-start.12 = (bf16[512,512]{1,0:T(8,128)(2,1)S(1)}, bf16[512,512]{1,0:T(8,128)(2,1)S(1)}, u32[]{:S(2)}, u32[]{:S(2)}) collective-permute-start(bf16[512,512]{1,0:T(8,128)(2,1)S(1)} %collective-permute-done.8.page_y), channel_id=1, source_target_pairs={{0,1},{1,0},{2,3},{3,2},{4,5},{5,4},{6,7},{7,6},{8,9},{9,8},{10,11... | collective-permute-start | bytes 1572872 | tf_op jit(solution)/shard_map/ppermute | solution.py:578
  72.2 5.0 %collective-permute-start.13 = (bf16[4,128,512]{2,1,0:T(8,128)(2,1)S(1)}, bf16[4,128,512]{2,1,0:T(8,128)(2,1)S(1)}, u32[]{:S(2)}, u32[]{:S(2)}) collective-permute-start(bf16[4,128,512]{2,1,0:T(8,128)(2,1)S(1)} %pad_maximum_fusion.1.kv_own), channel_id=1, source_target_pairs={{0,1},{1,0},{2,3},{3,2},{4,5},{5,4},{6,7},{7,6},{8,9},{9,8},{10,11... | collective-permute-start | bytes 1572872 | tf_op jit(solution)/shard_map/ppermute | solution.py:578
  72.7 4.5 %collective-permute-start.14 = (bf16[4,128,512]{2,1,0:T(8,128)(2,1)S(1)}, bf16[4,128,512]{2,1,0:T(8,128)(2,1)S(1)}, u32[]{:S(2)}, u32[]{:S(2)}) collective-permute-start(bf16[4,128,512]{2,1,0:T(8,128)(2,1)S(1)} %collective-permute-done.9.kv_y), channel_id=1, source_target_pairs={{0,1},{1,0},{2,3},{3,2},{4,5},{5,4},{6,7},{7,6},{8,9},{9,8},{10,11... | collective-permute-start | bytes 1572872 | tf_op jit(solution)/shard_map/ppermute | solution.py:578
  75.1 18.3 %collective-permute-start.17 = (bf16[2,2,4,16,1024]{4,3,2,1,0:T(8,128)(2,1)S(1)}, bf16[2,2,4,16,1024]{4,3,2,1,0:T(8,128)(2,1)S(1)}, u32[]{:S(2)}, u32[]{:S(2)}) collective-permute-start(bf16[2,2,4,16,1024]{4,3,2,1,0:T(8,128)(2,1)S(1)} %pad_maximum_fusion.refs_0_), channel_id=1, source_target_pairs={{0,1},{1,0},{2,3},{3,2},{4,5},{5,4},{6,7},{7,6},{8,9},{9,8},{10,11... | collective-permute-start | bytes 1572872 | tf_op jit(solution)/shard_map/ppermute | solution.py:578
  76.6 16.1 %collective-permute-start.15 = (bf16[2,2,4,16,1024]{4,3,2,1,0:T(8,128)(2,1)S(1)}, bf16[2,2,4,16,1024]{4,3,2,1,0:T(8,128)(2,1)S(1)}, u32[]{:S(2)}, u32[]{:S(2)}) collective-permute-start(bf16[2,2,4,16,1024]{4,3,2,1,0:T(8,128)(2,1)S(1)} %collective-permute-done.7.refs_4_), channel_id=1, source_target_pairs={{0,16},{16,0},{1,17},{17,1},{2,18},{18,2},{3,19},{19,3},{4,20},{20... | collective-permute-start | bytes 1572872 | tf_op jit(solution)/shard_map/ppermute | solution.py:578
  76.9 16.6 %collective-permute-start.19 = (bf16[2,2,4,16,1024]{4,3,2,1,0:T(8,128)(2,1)S(1)}, bf16[2,2,4,16,1024]{4,3,2,1,0:T(8,128)(2,1)S(1)}, u32[]{:S(2)}, u32[]{:S(2)}) collective-permute-start(bf16[2,2,4,16,1024]{4,3,2,1,0:T(8,128)(2,1)S(1)} %collective-permute-done.7.refs_4_), channel_id=1, source_target_pairs={{0,1},{1,0},{2,3},{3,2},{4,5},{5,4},{6,7},{7,6},{8,9},{9,8},{10,11... | collective-permute-start | bytes 1572872 | tf_op jit(solution)/shard_map/ppermute | solution.py:578
  92.6 3.6 %copy-start.3 = (bf16[2,512,512]{2,1,0:T(8,128)(2,1)}, bf16[2,512,512]{2,1,0:T(8,128)(2,1)S(1)}, u32[]{:S(2)}) copy-start(bf16[2,512,512]{2,1,0:T(8,128)(2,1)S(1)} %attend.1.a_hbm) | copy-start | bytes 3145732
  92.6 12.3 %copy-start.9 = (s32[128,1,2]{0,2,1:T(2,128)S(1)}, s32[128,1,2]{0,2,1:T(2,128)}, u32[]{:S(2)}) copy-start(s32[128,1,2]{0,2,1:T(2,128)} %param.16) | copy-start | bytes 3076
  92.6 35.0 %copy-start.2 = (bf16[128,1,2048]{2,0,1:T(8,128)(2,1)S(1)}, bf16[128,1,2048]{2,0,1:T(8,128)(2,1)}, u32[]{:S(2)}) copy-start(bf16[128,1,2048]{2,0,1:T(8,128)(2,1)} %param.13) | copy-start | bytes 1572868
  92.6 35.0 %copy-start.4 = (f32[2048]{0:T(1024)S(1)}, f32[2048]{0:T(1024)}, u32[]{:S(2)}) copy-start(f32[2048]{0:T(1024)} %param.15) | copy-start | bytes 24580
  92.7 2.0 collective-permute-start.18
  93.0 2.4 collective-permute-start.20
  93.2 2.9 %collective-permute-start.16 = (bf16[512,512]{1,0:T(8,128)(2,1)S(1)}, bf16[512,512]{1,0:T(8,128)(2,1)S(1)}, u32[]{:S(2)}, u32[]{:S(2)}) collective-permute-start(bf16[512,512]{1,0:T(8,128)(2,1)S(1)} %slice_bitcast_fusion), channel_id=1, source_target_pairs={{0,1},{1,0},{2,3},{3,2},{4,5},{5,4},{6,7},{7,6},{8,9},{9,8},{10,11... | collective-permute-start | bytes 1572872 | tf_op jit(solution)/shard_map/ppermute | solution.py:578
  100.9 15.0 %collective-permute-start.21 = (bf16[128,2048]{1,0:T(8,128)(2,1)}, bf16[128,2048]{1,0:T(8,128)(2,1)S(1)}, u32[]{:S(2)}, u32[]{:S(2)}) collective-permute-start(bf16[128,2048]{1,0:T(8,128)(2,1)} %get-tuple-element.54), channel_id=1, source_target_pairs={{0,6},{1,7},{2,4},{3,5},{4,2},{5,3},{6,0},{7,1},{8,14},{9,15},{10,... | collective-permute-start | bytes 1572872 | tf_op jit(solution)/shard_map/ppermute | solution.py:578
  103.7 23.6 %collective-permute-start.22 = (bf16[128,2048]{1,0:T(8,128)(2,1)}, bf16[128,2048]{1,0:T(8,128)(2,1)S(1)}, u32[]{:S(2)}, u32[]{:S(2)}) collective-permute-start(bf16[128,2048]{1,0:T(8,128)(2,1)} %get-tuple-element.55), channel_id=1, source_target_pairs={{0,4},{1,5},{2,6},{3,7},{4,0},{5,1},{6,2},{7,3},{8,12},{9,13},{10,... | collective-permute-start | bytes 1572872 | tf_op jit(solution)/shard_map/ppermute | solution.py:578
  103.8 23.9 %collective-permute-start.23 = (bf16[128,2048]{1,0:T(8,128)(2,1)}, bf16[128,2048]{1,0:T(8,128)(2,1)}, u32[]{:S(2)}, u32[]{:S(2)}) collective-permute-start(bf16[128,2048]{1,0:T(8,128)(2,1)} %get-tuple-element.56), channel_id=1, source_target_pairs={{0,2},{1,3},{2,0},{3,1},{4,6},{5,7},{6,4},{7,5},{8,10},{9,11},{10,... | collective-permute-start | bytes 1572872 | tf_op jit(solution)/shard_map/ppermute | solution.py:578
  130.1 54.0 %copy-start.5 = (bf16[1,512,2048]{2,1,0:T(8,128)(2,1)S(1)}, bf16[1,512,2048]{2,1,0:T(8,128)(2,1)}, u32[]{:S(2)}) copy-start(bf16[1,512,2048]{2,1,0:T(8,128)(2,1)} %param.19) | copy-start | bytes 6291460
  191.0 5.1 %copy-start.10 = (f32[128,1,2]{0,2,1:T(2,128)S(1)}, f32[128,1,2]{0,2,1:T(2,128)}, u32[]{:S(2)}) copy-start(f32[128,1,2]{0,2,1:T(2,128)} %param.17) | copy-start | bytes 3076
  191.0 52.6 %all-to-all-start.2 = ((bf16[16,32,2048]{2,1,0:T(8,128)(2,1)}), bf16[16,32,2048]{2,1,0:T(8,128)(2,1)S(1)}, u32[]{:S(2)}, u32[]{:S(2)}) async-start(bf16[16,32,2048]{2,1,0:T(8,128)(2,1)} %bitcast.52), calls=%async_computation.2 | async-start | bytes 4194304 | tf_op jit(solution)/shard_map/all_to_all | solution.py:774
  243.6 1.2 copy-start.1

commit v18 on v17

--- a/solution.py
+++ b/solution.py
@@ -612,13 +612,9 @@
     w_keep = lax.dynamic_index_in_dim(w, y, 1, keepdims=False)
     w_give = lax.dynamic_index_in_dim(w, 1 - y, 1, keepdims=False)
     w_got = flipped(w_give, "head", 2)
-    kv_last, query_slots, w_got = lax.optimization_barrier((kv_other, query_slots, w_got))
-    kv_own = [
-        kv_same,
-        flipped(kv_other, "head", plane_bit),
-        flipped(kv_same, "head", 2 * plane_bit),
-        flipped(kv_last, "head", 3 * plane_bit),
-    ]
+    kv_own = [kv_same]
+    for t in range(1, planes):
+        kv_own.append(flipped(kv_other if t % 2 else kv_same, "head", t * plane_bit))
     q = lax.all_to_all(
         query_slots, "head", split_axis=0, concat_axis=0, tiled=True, axis_index_groups=group_sets
     )
@@ -627,10 +623,8 @@
     w_other = lax.dynamic_index_in_dim(w_both, 1 - b, 0, keepdims=False)
     w_first = flipped(w_other, "head", plane_bit)
 
-    page_a, page_b, kv_own, w_first, q = lax.optimization_barrier(
-        (page_a, page_b, kv_own, w_first, q)
-    )
     own_pages = jnp.concatenate([page_a, page_b], 0)
+    own_pages, kv_own, w_first, q = lax.optimization_barrier((own_pages, kv_own, w_first, q))
     kv_own = jnp.stack(kv_own, 0)
     pages_y = flipped(own_pages, "head", 2)
     kv_y = flipped(kv_own, "head", 2)

time: 247 us -> 243 us (0.984)
  waiting for transfers between devices: 119 us -> 115 us
    ppermute x22, waiting for transfers between devices: 71.7 us -> 67.3 us  [flipped(): return lax.ppermute(value, axis, pairs)]
  transfers between devices with their start and end apart: 26 -> 26, of which waited for: 13 -> 14; matrix products, arithmetic and copies ran while one was open for 2% -> 1% of each run, Pallas kernels for 6% -> 6%
where the time goes in v18:
time: 243 us; the launch traced here: 242 us
  waiting for transfers between devices  115 us (47%)
  blocking collectives  54.3 us (22%)
  starting transfers between devices  32.8 us (13%)
  Pallas kernels  31.2 us (13%)
  local copies, waits for them, and re-layouts  5.24 us (2%)
  other arithmetic  3.61 us (1%)
    ppermute x22, waiting for transfers between devices, flipped(): return lax.ppermute(value, axis, pairs)  67.3 us
    all_to_all x1, blocking collectives, local(): lax.all_to_all(outgoing.reshape(n, slots // n, model), 'head', split_axis...  54.3 us
    all_to_all x1, waiting for transfers between devices, local(): lax.all_to_all(answered, 'head', split_axis=0, concat_axis=0, tiled=True)  47.3 us
    ppermute x22, starting transfers between devices, flipped(): return lax.ppermute(value, axis, pairs)  20 us
    pallas_call x1, Pallas kernels, attend_pair(): pl.pallas_call(functools.partial(attend_pair_kernel, block, chunk, width)...  15.4 us
    pallas_call x1, Pallas kernels, expert_pair(): pl.pallas_call(kernel, out_shape=pltpu.HBM((rows, model), BF16), in_specs...  6.88 us
    all_to_all x1, starting transfers between devices, local(): lax.all_to_all(answered, 'head', split_axis=0, concat_axis=0, tiled=True)  5.14 us
  transfers between devices with their start and end apart: 26, of which 14 were waited for; matrix products, arithmetic and copies ran while one was open for 1% of the time, Pallas kernels for 6%

profile of v18, /device:TPU:13, one launch (start us, length us, event | category | flops | bytes accessed | tf_op | source)
XLA Modules:
  0.0 242.2 jit_solution(11122471057407073329)
XLA Ops:
  0.0 2.6 %copy.29 = bf16[16,128,256]{2,1,0:T(8,128)(2,1)} copy(bf16[16,128,256]{2,0,1:T(8,128)(2,1)} %bitcast.54) | data formatting | bytes 2097152 | tf_op jit(solution)/shard_map/transpose | solution.py:595
  2.6 4.5 %all-to-all-start = ((bf16[8,2,128,256]{3,2,1,0:T(8,128)(2,1)}), bf16[8,2,128,256]{3,2,1,0:T(8,128)(2,1)S(1)}, u32[]{:S(2)}, u32[]{:S(2)}) async-start(bf16[8,2,128,256]{3,2,1,0:T(8,128)(2,1)} %bitcast.13), calls=%async_computation | async-start | bytes 2097152 | tf_op jit(solution)/shard_map/all_to_all | solution.py:618
  7.3 0.3 collective-permute-start.5
  7.6 3.1 %collective-permute-start = (bf16[256,512]{1,0:T(8,128)(2,1)}, bf16[256,512]{1,0:T(8,128)(2,1)S(1)}, u32[]{:S(2)}, u32[]{:S(2)}) collective-permute-start(bf16[256,512]{1,0:T(8,128)(2,1)} %bitcast.63), channel_id=1, source_target_pairs={{0,0},{1,1},{2,2},{3,3},{4,8},{5,9},{6,10},{7,11},{8,4},{9,5},{10,... | collective-permute-start | bytes 786440 | tf_op jit(solution)/shard_map/ppermute | solution.py:603
  10.8 14.7 %collective-permute-done.5 = bf16[2,4,16,1024]{3,2,1,0:T(8,128)(2,1)S(1)} collective-permute-done((bf16[2,4,16,1024]{3,2,1,0:T(8,128)(2,1)S(1)}, bf16[2,4,16,1024]{3,2,1,0:T(8,128)(2,1)S(1)}, u32[]{:S(2)}, u32[]{:S(2)}) %collective-permute-start.5) | collective-permute-done | bytes 262176 | tf_op jit(solution)/shard_map/ppermute | solution.py:578
  25.6 0.2 collective-permute-start.6
  25.9 0.5 constant_dynamic-slice_fusion.2
  26.4 1.4 collective-permute-start.2
  27.8 2.4 collective-permute-start.3
  30.2 1.0 pad_maximum_fusion.page_own
  31.2 5.5 %collective-permute-done.2 = bf16[128,512]{1,0:T(8,128)(2,1)S(1)} collective-permute-done((bf16[128,512]{1,0:T(8,128)(2,1)S(1)}, bf16[128,512]{1,0:T(8,128)(2,1)S(1)}, u32[]{:S(2)}, u32[]{:S(2)}) %collective-permute-start.2) | collective-permute-done | bytes 131104 | tf_op jit(solution)/shard_map/ppermute | solution.py:578
  36.7 3.1 %collective-permute-done.3 = bf16[128,512]{1,0:T(8,128)(2,1)} collective-permute-done((bf16[128,512]{1,0:T(8,128)(2,1)S(1)}, bf16[128,512]{1,0:T(8,128)(2,1)}, u32[]{:S(2)}, u32[]{:S(2)}) %collective-permute-start.3) | collective-permute-done | bytes 131104 | tf_op jit(solution)/shard_map/ppermute | solution.py:578
  39.8 1.3 pad_maximum_fusion.2.kv_own
  41.2 0.6 collective-permute-start.9
  41.8 1.0 pad_maximum_fusion.1.refs_0_
  42.8 1.3 collective-permute-start.10
  44.1 0.9 collective-permute-start.8
  45.0 3.8 %collective-permute-start.7 = (bf16[2,2,4,16,1024]{4,3,2,1,0:T(8,128)(2,1)S(1)}, bf16[2,2,4,16,1024]{4,3,2,1,0:T(8,128)(2,1)S(1)}, u32[]{:S(2)}, u32[]{:S(2)}) collective-permute-start(bf16[2,2,4,16,1024]{4,3,2,1,0:T(8,128)(2,1)S(1)} %pad_maximum_fusion.1.refs_0_), channel_id=1, source_target_pairs={{0,8},{1,9},{2,10},{3,11},{4,12},{5,13},{6,14},{7,15},{8,0},{9,1},... | collective-permute-start | bytes 1572872 | tf_op jit(solution)/shard_map/ppermute | solution.py:578
  48.8 3.3 %collective-permute-done.9.kv_y = bf16[4,128,512]{2,1,0:T(8,128)(2,1)S(1)} collective-permute-done((bf16[4,128,512]{2,1,0:T(8,128)(2,1)S(1)}, bf16[4,128,512]{2,1,0:T(8,128)(2,1)S(1)}, u32[]{:S(2)}, u32[]{:S(2)}) %collective-permute-start.9) | collective-permute-done | bytes 524320 | tf_op jit(solution)/shard_map/ppermute | solution.py:578
  52.1 0.7 collective-permute-done.10.refs_2_
  52.9 10.5 %collective-permute-done.8.page_y = bf16[512,512]{1,0:T(8,128)(2,1)S(1)} collective-permute-done((bf16[512,512]{1,0:T(8,128)(2,1)S(1)}, bf16[512,512]{1,0:T(8,128)(2,1)S(1)}, u32[]{:S(2)}, u32[]{:S(2)}) %collective-permute-start.8) | collective-permute-done | bytes 524320 | tf_op jit(solution)/shard_map/ppermute | solution.py:578
  63.4 3.5 %collective-permute-start.11 = (bf16[512,512]{1,0:T(8,128)(2,1)S(1)}, bf16[512,512]{1,0:T(8,128)(2,1)S(1)}, u32[]{:S(2)}, u32[]{:S(2)}) collective-permute-start(bf16[512,512]{1,0:T(8,128)(2,1)S(1)} %pad_maximum_fusion.page_own), channel_id=1, source_target_pairs={{0,1},{1,0},{2,3},{3,2},{4,5},{5,4},{6,7},{7,6},{8,9},{9,8},{10,11... | collective-permute-start | bytes 1572872 | tf_op jit(solution)/shard_map/ppermute | solution.py:578
  66.8 0.5 collective-permute-start.13
  67.3 4.2 %collective-permute-done.7.refs_4_ = bf16[2,2,4,16,1024]{4,3,2,1,0:T(8,128)(2,1)S(1)} collective-permute-done((bf16[2,2,4,16,1024]{4,3,2,1,0:T(8,128)(2,1)S(1)}, bf16[2,2,4,16,1024]{4,3,2,1,0:T(8,128)(2,1)S(1)}, u32[]{:S(2)}, u32[]{:S(2)}) %collective-permute-start.7) | collective-permute-done | bytes 524320 | tf_op jit(solution)/shard_map/ppermute | solution.py:578
  71.6 0.5 collective-permute-start.17
  72.1 0.3 collective-permute-start.15
  72.3 0.3 collective-permute-start.19
  72.6 15.4 %attend.1.a_hbm = bf16[2,512,512]{2,1,0:T(8,128)(2,1)S(1)} custom-call(bf16[8,2,128,256]{3,2,1,0:T(8,128)(2,1)} %copy-done.7, bf16[512,512]{1,0:T(8,128)(2,1)S(1)} %pad_maximum_fusion.page_own, bf16[512,512]{1,0:T(8,128)(2,1)S(1)} %collective-permute-done.8.page_y, bf16[512,512]{1,0:T(8,128)(2,1)S(1)} %collective-permute-done.11.page_c, ...), custom_call_target="tpu_custom_call" | custom-call | flops 7516192768 | bytes 6291456 | tf_op jit(solution)/shard_map/attend/pallas_call | solution.py:270
  88.1 0.3 collective-permute-start.18
  88.4 0.3 collective-permute-start.20
  88.7 0.2 collective-permute-start.16
  88.9 1.2 collective-permute-done.18.refs_3_
  90.1 0.7 collective-permute-done.20.refs_7_
  90.9 0.7 collective-permute-done.16.got_hbm
  91.6 4.8 %project.1 = (bf16[128,2048]{1,0:T(8,128)(2,1)S(1)}, bf16[128,2048]{1,0:T(8,128)(2,1)}, bf16[128,2048]{1,0:T(8,128)(2,1)}, bf16[128,2048]{1,0:T(8,128)(2,1)}) custom-call(bf16[2,512,512]{2,1,0:T(8,128)(2,1)} %copy-done.3, bf16[512,512]{1,0:T(8,128)(2,1)S(1)} %collective-permute-done.16.got_hbm, bf16[2,2,4,16,1024]{4,3,2,1,0:T(8,128)(2,1)S(1)} %pad_maximum_fusion.1.refs_0_, ...), custom_call_target="tpu_custom_call" | custom-call | flops 2147483648 | bytes 7340032 | tf_op jit(solution)/shard_map/project/pallas_call | solution.py:351
  96.4 2.6 %collective-permute-start.21 = (bf16[128,2048]{1,0:T(8,128)(2,1)}, bf16[128,2048]{1,0:T(8,128)(2,1)S(1)}, u32[]{:S(2)}, u32[]{:S(2)}) collective-permute-start(bf16[128,2048]{1,0:T(8,128)(2,1)} %get-tuple-element.46), channel_id=1, source_target_pairs={{0,6},{1,7},{2,4},{3,5},{4,2},{5,3},{6,0},{7,1},{8,14},{9,15},{10,... | collective-permute-start | bytes 1572872 | tf_op jit(solution)/shard_map/ppermute | solution.py:578
  99.0 0.7 collective-permute-start.23
  100.0 0.2 reduce_window_sum.11
  100.5 10.8 %collective-permute-done.21 = bf16[128,2048]{1,0:T(8,128)(2,1)S(1)} collective-permute-done((bf16[128,2048]{1,0:T(8,128)(2,1)}, bf16[128,2048]{1,0:T(8,128)(2,1)S(1)}, u32[]{:S(2)}, u32[]{:S(2)}) %collective-permute-start.21) | collective-permute-done | bytes 524320 | tf_op jit(solution)/shard_map/ppermute | solution.py:578
  111.2 10.9 %collective-permute-done.22 = bf16[128,2048]{1,0:T(8,128)(2,1)S(1)} collective-permute-done((bf16[128,2048]{1,0:T(8,128)(2,1)}, bf16[128,2048]{1,0:T(8,128)(2,1)S(1)}, u32[]{:S(2)}, u32[]{:S(2)}) %collective-permute-start.22) | collective-permute-done | bytes 524320 | tf_op jit(solution)/shard_map/ppermute | solution.py:578
  122.2 0.8 collective-permute-done.23
  122.9 2.4 route.1
  125.4 54.3 %all_to_all.15 = bf16[16,32,2048]{2,1,0:T(8,128)(2,1)S(1)} all-to-all(bf16[16,32,2048]{2,1,0:T(8,128)(2,1)S(1)} %bitcast.42), channel_id=1, replica_groups=mesh['grp'=2,'head'=16] {'head'}, dimensions={0} | all-to-all | bytes 4194304 | tf_op jit(solution)/shard_map/all_to_all | solution.py:755
  179.6 6.9 %expert.1 = bf16[512,2048]{1,0:T(8,128)(2,1)} custom-call(bf16[512,2048]{1,0:T(8,128)(2,1)S(1)} %bitcast.43, bf16[2048,1024]{1,0:T(8,128)(2,1)} %bitcast.62, bf16[512,2048]{1,0:T(8,128)(2,1)S(1)} %bitcast.51), custom_call_target="tpu_custom_call" | custom-call | flops 3221225472 | bytes 10485760 | tf_op jit(solution)/shard_map/expert/pallas_call | solution.py:513
  186.5 5.1 %all-to-all-start.2 = ((bf16[16,32,2048]{2,1,0:T(8,128)(2,1)}), bf16[16,32,2048]{2,1,0:T(8,128)(2,1)S(1)}, u32[]{:S(2)}, u32[]{:S(2)}) async-start(bf16[16,32,2048]{2,1,0:T(8,128)(2,1)} %bitcast.52), calls=%async_computation.2 | async-start | bytes 4194304 | tf_op jit(solution)/shard_map/all_to_all | solution.py:768
  191.8 47.3 %all-to-all-done.2 = bf16[16,32,2048]{2,1,0:T(8,128)(2,1)S(1)} async-done(((bf16[16,32,2048]{2,1,0:T(8,128)(2,1)}), bf16[16,32,2048]{2,1,0:T(8,128)(2,1)S(1)}, u32[]{:S(2)}, u32[]{:S(2)}) %all-to-all-start.2) | async-done | bytes 2097184 | tf_op jit(solution)/shard_map/all_to_all | solution.py:768
  239.1 1.2 copy-done.1
  240.3 1.7 combine.1
  (53 shorter events, 1.1 us)
Async XLA Ops:
  0.0 7.2 %copy-start = (bf16[16,16,2048]{2,1,0:T(8,128)(2,1)S(1)}, bf16[16,16,2048]{2,1,0:T(8,128)(2,1)}, u32[]{:S(2)}) copy-start(bf16[16,16,2048]{2,1,0:T(8,128)(2,1)} %param.14) | copy-start | bytes 3145732
  2.6 37.2 %all-to-all-start = ((bf16[8,2,128,256]{3,2,1,0:T(8,128)(2,1)}), bf16[8,2,128,256]{3,2,1,0:T(8,128)(2,1)S(1)}, u32[]{:S(2)}, u32[]{:S(2)}) async-start(bf16[8,2,128,256]{3,2,1,0:T(8,128)(2,1)} %bitcast.13), calls=%async_computation | async-start | bytes 2097152 | tf_op jit(solution)/shard_map/all_to_all | solution.py:618
  7.2 18.7 %copy-start.6 = (bf16[128,1,2,512]{3,2,1,0:T(2,128)(2,1)S(1)}, bf16[128,1,2,512]{3,2,1,0:T(2,128)(2,1)}, u32[]{:S(2)}) copy-start(bf16[128,1,2,512]{3,2,1,0:T(2,128)(2,1)} %param.11) | copy-start | bytes 786436
  7.3 18.3 %collective-permute-start.5 = (bf16[2,4,16,1024]{3,2,1,0:T(8,128)(2,1)S(1)}, bf16[2,4,16,1024]{3,2,1,0:T(8,128)(2,1)S(1)}, u32[]{:S(2)}, u32[]{:S(2)}) collective-permute-start(bf16[2,4,16,1024]{3,2,1,0:T(8,128)(2,1)S(1)} %get-tuple-element.53), channel_id=1, source_target_pairs={{0,2},{1,3},{2,0},{3,1},{4,6},{5,7},{6,4},{7,5},{8,10},{9,11},{10,... | collective-permute-start | bytes 786440 | tf_op jit(solution)/shard_map/ppermute | solution.py:578
  7.6 22.6 %collective-permute-start = (bf16[256,512]{1,0:T(8,128)(2,1)}, bf16[256,512]{1,0:T(8,128)(2,1)S(1)}, u32[]{:S(2)}, u32[]{:S(2)}) collective-permute-start(bf16[256,512]{1,0:T(8,128)(2,1)} %bitcast.63), channel_id=1, source_target_pairs={{0,0},{1,1},{2,2},{3,3},{4,8},{5,9},{6,10},{7,11},{8,4},{9,5},{10,... | collective-permute-start | bytes 786440 | tf_op jit(solution)/shard_map/ppermute | solution.py:603
  10.7 19.5 %collective-permute-start.1 = (bf16[256,512]{1,0:T(8,128)(2,1)}, bf16[256,512]{1,0:T(8,128)(2,1)}, u32[]{:S(2)}, u32[]{:S(2)}) collective-permute-start(bf16[256,512]{1,0:T(8,128)(2,1)} %bitcast.64), channel_id=1, source_target_pairs={{0,8},{1,9},{2,10},{3,11},{4,0},{5,1},{6,2},{7,3},{8,12},{9,13},{1... | collective-permute-start | bytes 786440 | tf_op jit(solution)/shard_map/ppermute | solution.py:603
  25.6 14.2 %collective-permute-start.6 = (bf16[2,4,16,1024]{3,2,1,0:T(8,128)(2,1)S(1)}, bf16[2,4,16,1024]{3,2,1,0:T(8,128)(2,1)}, u32[]{:S(2)}, u32[]{:S(2)}) collective-permute-start(bf16[2,4,16,1024]{3,2,1,0:T(8,128)(2,1)S(1)} %get-tuple-element.52), channel_id=1, source_target_pairs={{0,4},{1,5},{2,6},{3,7},{4,0},{5,1},{6,2},{7,3},{8,12},{9,13},{10,... | collective-permute-start | bytes 786440 | tf_op jit(solution)/shard_map/ppermute | solution.py:578
  26.4 10.2 %collective-permute-start.2 = (bf16[128,512]{1,0:T(8,128)(2,1)S(1)}, bf16[128,512]{1,0:T(8,128)(2,1)S(1)}, u32[]{:S(2)}, u32[]{:S(2)}) collective-permute-start(bf16[128,512]{1,0:T(8,128)(2,1)S(1)} %bitcast.59), channel_id=1, source_target_pairs={{0,4},{1,5},{2,6},{3,7},{4,0},{5,1},{6,2},{7,3},{8,12},{9,13},{10,... | collective-permute-start | bytes 393224 | tf_op jit(solution)/shard_map/ppermute | solution.py:578
  27.8 12.0 %collective-permute-start.3 = (bf16[128,512]{1,0:T(8,128)(2,1)S(1)}, bf16[128,512]{1,0:T(8,128)(2,1)}, u32[]{:S(2)}, u32[]{:S(2)}) collective-permute-start(bf16[128,512]{1,0:T(8,128)(2,1)S(1)} %bitcast.56), channel_id=1, source_target_pairs={{0,8},{1,9},{2,10},{3,11},{4,12},{5,13},{6,14},{7,15},{8,0},{9,1},... | collective-permute-start | bytes 393224 | tf_op jit(solution)/shard_map/ppermute | solution.py:578
  30.2 9.6 %collective-permute-start.4 = (bf16[128,512]{1,0:T(8,128)(2,1)S(1)}, bf16[128,512]{1,0:T(8,128)(2,1)}, u32[]{:S(2)}, u32[]{:S(2)}) collective-permute-start(bf16[128,512]{1,0:T(8,128)(2,1)S(1)} %bitcast.60), channel_id=1, source_target_pairs={{0,12},{1,13},{2,14},{3,15},{4,8},{5,9},{6,10},{7,11},{8,4},{9,5},... | collective-permute-start | bytes 393224 | tf_op jit(solution)/shard_map/ppermute | solution.py:578
  39.8 4.2 %copy-start.7 = (bf16[8,2,128,256]{3,2,1,0:T(8,128)(2,1)}, bf16[8,2,128,256]{3,2,1,0:T(8,128)(2,1)S(1)}, u32[]{:S(2)}) copy-start(bf16[8,2,128,256]{3,2,1,0:T(8,128)(2,1)S(1)} %all-to-all-done.q_hbm) | copy-start | bytes 3145732
  41.2 10.9 %collective-permute-start.9 = (bf16[4,128,512]{2,1,0:T(8,128)(2,1)S(1)}, bf16[4,128,512]{2,1,0:T(8,128)(2,1)S(1)}, u32[]{:S(2)}, u32[]{:S(2)}) collective-permute-start(bf16[4,128,512]{2,1,0:T(8,128)(2,1)S(1)} %pad_maximum_fusion.2.kv_own), channel_id=1, source_target_pairs={{0,2},{1,3},{2,0},{3,1},{4,6},{5,7},{6,4},{7,5},{8,10},{9,11},{10,... | collective-permute-start | bytes 1572872 | tf_op jit(solution)/shard_map/ppermute | solution.py:578
  42.8 10.1 %collective-permute-start.10 = (bf16[2,2,4,16,1024]{4,3,2,1,0:T(8,128)(2,1)S(1)}, bf16[2,2,4,16,1024]{4,3,2,1,0:T(8,128)(2,1)S(1)}, u32[]{:S(2)}, u32[]{:S(2)}) collective-permute-start(bf16[2,2,4,16,1024]{4,3,2,1,0:T(8,128)(2,1)S(1)} %pad_maximum_fusion.1.refs_0_), channel_id=1, source_target_pairs={{0,16},{16,0},{1,17},{17,1},{2,18},{18,2},{3,19},{19,3},{4,20},{20... | collective-permute-start | bytes 1572872 | tf_op jit(solution)/shard_map/ppermute | solution.py:578
  44.1 19.3 %collective-permute-start.8 = (bf16[512,512]{1,0:T(8,128)(2,1)S(1)}, bf16[512,512]{1,0:T(8,128)(2,1)S(1)}, u32[]{:S(2)}, u32[]{:S(2)}) collective-permute-start(bf16[512,512]{1,0:T(8,128)(2,1)S(1)} %pad_maximum_fusion.page_own), channel_id=1, source_target_pairs={{0,2},{1,3},{2,0},{3,1},{4,6},{5,7},{6,4},{7,5},{8,10},{9,11},{10,... | collective-permute-start | bytes 1572872 | tf_op jit(solution)/shard_map/ppermute | solution.py:578
  45.0 26.6 %collective-permute-start.7 = (bf16[2,2,4,16,1024]{4,3,2,1,0:T(8,128)(2,1)S(1)}, bf16[2,2,4,16,1024]{4,3,2,1,0:T(8,128)(2,1)S(1)}, u32[]{:S(2)}, u32[]{:S(2)}) collective-permute-start(bf16[2,2,4,16,1024]{4,3,2,1,0:T(8,128)(2,1)S(1)} %pad_maximum_fusion.1.refs_0_), channel_id=1, source_target_pairs={{0,8},{1,9},{2,10},{3,11},{4,12},{5,13},{6,14},{7,15},{8,0},{9,1},... | collective-permute-start | bytes 1572872 | tf_op jit(solution)/shard_map/ppermute | solution.py:578
  63.4 8.7 %collective-permute-start.11 = (bf16[512,512]{1,0:T(8,128)(2,1)S(1)}, bf16[512,512]{1,0:T(8,128)(2,1)S(1)}, u32[]{:S(2)}, u32[]{:S(2)}) collective-permute-start(bf16[512,512]{1,0:T(8,128)(2,1)S(1)} %pad_maximum_fusion.page_own), channel_id=1, source_target_pairs={{0,1},{1,0},{2,3},{3,2},{4,5},{5,4},{6,7},{7,6},{8,9},{9,8},{10,11... | collective-permute-start | bytes 1572872 | tf_op jit(solution)/shard_map/ppermute | solution.py:578
  66.8 5.5 %collective-permute-start.12 = (bf16[512,512]{1,0:T(8,128)(2,1)S(1)}, bf16[512,512]{1,0:T(8,128)(2,1)S(1)}, u32[]{:S(2)}, u32[]{:S(2)}) collective-permute-start(bf16[512,512]{1,0:T(8,128)(2,1)S(1)} %collective-permute-done.8.page_y), channel_id=1, source_target_pairs={{0,1},{1,0},{2,3},{3,2},{4,5},{5,4},{6,7},{7,6},{8,9},{9,8},{10,11... | collective-permute-start | bytes 1572872 | tf_op jit(solution)/shard_map/ppermute | solution.py:578
  66.8 5.8 %collective-permute-start.13 = (bf16[4,128,512]{2,1,0:T(8,128)(2,1)S(1)}, bf16[4,128,512]{2,1,0:T(8,128)(2,1)S(1)}, u32[]{:S(2)}, u32[]{:S(2)}) collective-permute-start(bf16[4,128,512]{2,1,0:T(8,128)(2,1)S(1)} %pad_maximum_fusion.2.kv_own), channel_id=1, source_target_pairs={{0,1},{1,0},{2,3},{3,2},{4,5},{5,4},{6,7},{7,6},{8,9},{9,8},{10,11... | collective-permute-start | bytes 1572872 | tf_op jit(solution)/shard_map/ppermute | solution.py:578
  67.3 5.3 %collective-permute-start.14 = (bf16[4,128,512]{2,1,0:T(8,128)(2,1)S(1)}, bf16[4,128,512]{2,1,0:T(8,128)(2,1)S(1)}, u32[]{:S(2)}, u32[]{:S(2)}) collective-permute-start(bf16[4,128,512]{2,1,0:T(8,128)(2,1)S(1)} %collective-permute-done.9.kv_y), channel_id=1, source_target_pairs={{0,1},{1,0},{2,3},{3,2},{4,5},{5,4},{6,7},{7,6},{8,9},{9,8},{10,11... | collective-permute-start | bytes 1572872 | tf_op jit(solution)/shard_map/ppermute | solution.py:578
  71.6 17.4 %collective-permute-start.17 = (bf16[2,2,4,16,1024]{4,3,2,1,0:T(8,128)(2,1)S(1)}, bf16[2,2,4,16,1024]{4,3,2,1,0:T(8,128)(2,1)S(1)}, u32[]{:S(2)}, u32[]{:S(2)}) collective-permute-start(bf16[2,2,4,16,1024]{4,3,2,1,0:T(8,128)(2,1)S(1)} %pad_maximum_fusion.1.refs_0_), channel_id=1, source_target_pairs={{0,1},{1,0},{2,3},{3,2},{4,5},{5,4},{6,7},{7,6},{8,9},{9,8},{10,11... | collective-permute-start | bytes 1572872 | tf_op jit(solution)/shard_map/ppermute | solution.py:578
  72.1 16.1 %collective-permute-start.15 = (bf16[2,2,4,16,1024]{4,3,2,1,0:T(8,128)(2,1)S(1)}, bf16[2,2,4,16,1024]{4,3,2,1,0:T(8,128)(2,1)S(1)}, u32[]{:S(2)}, u32[]{:S(2)}) collective-permute-start(bf16[2,2,4,16,1024]{4,3,2,1,0:T(8,128)(2,1)S(1)} %collective-permute-done.7.refs_4_), channel_id=1, source_target_pairs={{0,16},{16,0},{1,17},{17,1},{2,18},{18,2},{3,19},{19,3},{4,20},{20... | collective-permute-start | bytes 1572872 | tf_op jit(solution)/shard_map/ppermute | solution.py:578
  72.3 16.6 %collective-permute-start.19 = (bf16[2,2,4,16,1024]{4,3,2,1,0:T(8,128)(2,1)S(1)}, bf16[2,2,4,16,1024]{4,3,2,1,0:T(8,128)(2,1)S(1)}, u32[]{:S(2)}, u32[]{:S(2)}) collective-permute-start(bf16[2,2,4,16,1024]{4,3,2,1,0:T(8,128)(2,1)S(1)} %collective-permute-done.7.refs_4_), channel_id=1, source_target_pairs={{0,1},{1,0},{2,3},{3,2},{4,5},{5,4},{6,7},{7,6},{8,9},{9,8},{10,11... | collective-permute-start | bytes 1572872 | tf_op jit(solution)/shard_map/ppermute | solution.py:578
  88.0 3.6 %copy-start.3 = (bf16[2,512,512]{2,1,0:T(8,128)(2,1)}, bf16[2,512,512]{2,1,0:T(8,128)(2,1)S(1)}, u32[]{:S(2)}) copy-start(bf16[2,512,512]{2,1,0:T(8,128)(2,1)S(1)} %attend.1.a_hbm) | copy-start | bytes 3145732
  88.1 11.6 %copy-start.8 = (s32[128,1,2]{0,2,1:T(2,128)S(1)}, s32[128,1,2]{0,2,1:T(2,128)}, u32[]{:S(2)}) copy-start(s32[128,1,2]{0,2,1:T(2,128)} %param.16) | copy-start | bytes 3076
  88.1 34.8 %copy-start.2 = (bf16[128,1,2048]{2,0,1:T(8,128)(2,1)S(1)}, bf16[128,1,2048]{2,0,1:T(8,128)(2,1)}, u32[]{:S(2)}) copy-start(bf16[128,1,2048]{2,0,1:T(8,128)(2,1)} %param.13) | copy-start | bytes 1572868
  88.1 34.8 %copy-start.4 = (f32[2048]{0:T(1024)S(1)}, f32[2048]{0:T(1024)}, u32[]{:S(2)}) copy-start(f32[2048]{0:T(1024)} %param.15) | copy-start | bytes 24580
  88.1 2.0 collective-permute-start.18
  88.4 2.4 %collective-permute-start.20 = (bf16[2,2,4,16,1024]{4,3,2,1,0:T(8,128)(2,1)S(1)}, bf16[2,2,4,16,1024]{4,3,2,1,0:T(8,128)(2,1)S(1)}, u32[]{:S(2)}, u32[]{:S(2)}) collective-permute-start(bf16[2,2,4,16,1024]{4,3,2,1,0:T(8,128)(2,1)S(1)} %collective-permute-done.15.refs_6_), channel_id=1, source_target_pairs={{0,1},{1,0},{2,3},{3,2},{4,5},{5,4},{6,7},{7,6},{8,9},{9,8},{10,11... | collective-permute-start | bytes 1572872 | tf_op jit(solution)/shard_map/ppermute | solution.py:578
  88.7 2.9 %collective-permute-start.16 = (bf16[512,512]{1,0:T(8,128)(2,1)S(1)}, bf16[512,512]{1,0:T(8,128)(2,1)S(1)}, u32[]{:S(2)}, u32[]{:S(2)}) collective-permute-start(bf16[512,512]{1,0:T(8,128)(2,1)S(1)} %slice_bitcast_fusion), channel_id=1, source_target_pairs={{0,1},{1,0},{2,3},{3,2},{4,5},{5,4},{6,7},{7,6},{8,9},{9,8},{10,11... | collective-permute-start | bytes 1572872 | tf_op jit(solution)/shard_map/ppermute | solution.py:578
  96.4 14.8 %collective-permute-start.21 = (bf16[128,2048]{1,0:T(8,128)(2,1)}, bf16[128,2048]{1,0:T(8,128)(2,1)S(1)}, u32[]{:S(2)}, u32[]{:S(2)}) collective-permute-start(bf16[128,2048]{1,0:T(8,128)(2,1)} %get-tuple-element.46), channel_id=1, source_target_pairs={{0,6},{1,7},{2,4},{3,5},{4,2},{5,3},{6,0},{7,1},{8,14},{9,15},{10,... | collective-permute-start | bytes 1572872 | tf_op jit(solution)/shard_map/ppermute | solution.py:578
  99.0 23.2 %collective-permute-start.22 = (bf16[128,2048]{1,0:T(8,128)(2,1)}, bf16[128,2048]{1,0:T(8,128)(2,1)S(1)}, u32[]{:S(2)}, u32[]{:S(2)}) collective-permute-start(bf16[128,2048]{1,0:T(8,128)(2,1)} %get-tuple-element.47), channel_id=1, source_target_pairs={{0,4},{1,5},{2,6},{3,7},{4,0},{5,1},{6,2},{7,3},{8,12},{9,13},{10,... | collective-permute-start | bytes 1572872 | tf_op jit(solution)/shard_map/ppermute | solution.py:578
  99.0 23.9 %collective-permute-start.23 = (bf16[128,2048]{1,0:T(8,128)(2,1)}, bf16[128,2048]{1,0:T(8,128)(2,1)}, u32[]{:S(2)}, u32[]{:S(2)}) collective-permute-start(bf16[128,2048]{1,0:T(8,128)(2,1)} %get-tuple-element.48), channel_id=1, source_target_pairs={{0,2},{1,3},{2,0},{3,1},{4,6},{5,7},{6,4},{7,5},{8,10},{9,11},{10,... | collective-permute-start | bytes 1572872 | tf_op jit(solution)/shard_map/ppermute | solution.py:578
  125.3 54.3 %copy-start.5 = (bf16[1,512,2048]{2,1,0:T(8,128)(2,1)S(1)}, bf16[1,512,2048]{2,1,0:T(8,128)(2,1)}, u32[]{:S(2)}) copy-start(bf16[1,512,2048]{2,1,0:T(8,128)(2,1)} %param.19) | copy-start | bytes 6291460
  186.5 5.2 %copy-start.9 = (f32[128,1,2]{0,2,1:T(2,128)S(1)}, f32[128,1,2]{0,2,1:T(2,128)}, u32[]{:S(2)}) copy-start(f32[128,1,2]{0,2,1:T(2,128)} %param.17) | copy-start | bytes 3076
  186.5 52.6 %all-to-all-start.2 = ((bf16[16,32,2048]{2,1,0:T(8,128)(2,1)}), bf16[16,32,2048]{2,1,0:T(8,128)(2,1)S(1)}, u32[]{:S(2)}, u32[]{:S(2)}) async-start(bf16[16,32,2048]{2,1,0:T(8,128)(2,1)} %bitcast.52), calls=%async_computation.2 | async-start | bytes 4194304 | tf_op jit(solution)/shard_map/all_to_all | solution.py:768
  239.1 1.2 copy-start.1

commit v19 on v15

--- a/solution.py
+++ b/solution.py
@@ -614,17 +614,18 @@
         kv_own.append(flipped(kv_other if t % 2 else kv_same, "head", t * plane_bit))
     w_got = flipped(w_give, "head", 2)
 
-    (page_a, page_b, kv_own, q), w_got = lax.optimization_barrier(
-        ((page_a, page_b, kv_own, q), w_got)
-    )
+    kv_own[1], kv_own[2], w_got = lax.optimization_barrier((kv_own[1], kv_own[2], w_got))
+    w_both = jnp.stack([w_keep, w_got], 1)
+    w_same = lax.dynamic_index_in_dim(w_both, b, 0, keepdims=False)
+    w_other = lax.dynamic_index_in_dim(w_both, 1 - b, 0, keepdims=False)
+    w_first = flipped(w_other, "head", plane_bit)
+
     own_pages = jnp.concatenate([page_a, page_b], 0)
+    own_pages, kv_own, w_first, q = lax.optimization_barrier((own_pages, kv_own, w_first, q))
     kv_own = jnp.stack(kv_own, 0)
     pages_y = flipped(own_pages, "head", 2)
     kv_y = flipped(kv_own, "head", 2)
-    w_both = jnp.stack([w_keep, w_got], 1)
-    w_same = lax.dynamic_index_in_dim(w_both, b, 0, keepdims=False)
-    w_other = lax.dynamic_index_in_dim(w_both, 1 - b, 0, keepdims=False)
-    w_near = jnp.stack([w_same, flipped(w_other, "head", plane_bit)], 0)
+    w_near = jnp.stack([w_same, w_first], 0)
     w_near_x = flipped(w_near, "grp", 1)
     w_far = flipped(w_near, "head", members)
     pages_y, kv_y, own_pages, kv_own, w_near_x = lax.optimization_barrier(

time: 241 us -> 239 us (level)
  waiting for transfers between devices: 119 us -> 112 us
  starting transfers between devices: 30 us -> 35.5 us
    ppermute x22, waiting for transfers between devices: 71.3 us -> 60.1 us  [flipped(): return lax.ppermute(value, axis, pairs)]
    ppermute x22, starting transfers between devices: 15.8 us -> 22.8 us  [flipped(): return lax.ppermute(value, axis, pairs)]
    ppermute x2, waiting for transfers between devices: 0.01 us -> 4.78 us  [parts_in_pairs(): lax.ppermute(cache[0], 'head', [(d, page_target(d, other)) for d in range...]
  transfers between devices with their start and end apart: 26 -> 26, of which waited for: 14 -> 15; matrix products, arithmetic and copies ran while one was open for 2% -> 1% of each run, Pallas kernels for 6% -> 6%
where the time goes in v19:
time: 239 us; the launch traced here: 238 us
  waiting for transfers between devices  112 us (47%)
  blocking collectives  52.9 us (22%)
  starting transfers between devices  35.5 us (15%)
  Pallas kernels  29.5 us (12%)
  local copies, waits for them, and re-layouts  6.28 us (3%)
    ppermute x22, waiting for transfers between devices, flipped(): return lax.ppermute(value, axis, pairs)  60.1 us
    all_to_all x1, blocking collectives, local(): lax.all_to_all(outgoing.reshape(n, slots // n, model), 'head', split_axis...  52.9 us
    all_to_all x1, waiting for transfers between devices, local(): lax.all_to_all(answered, 'head', split_axis=0, concat_axis=0, tiled=True)  47.3 us
    ppermute x22, starting transfers between devices, flipped(): return lax.ppermute(value, axis, pairs)  22.8 us
    pallas_call x1, Pallas kernels, attend_pair(): pl.pallas_call(functools.partial(attend_pair_kernel, block, chunk, width)...  15.4 us
    pallas_call x1, Pallas kernels, expert_pair(): pl.pallas_call(kernel, out_shape=pltpu.HBM((rows, model), BF16), in_specs...  6.87 us
    all_to_all x1, starting transfers between devices, local(): lax.all_to_all(answered, 'head', split_axis=0, concat_axis=0, tiled=True)  5.13 us
    ppermute x2, waiting for transfers between devices, parts_in_pairs(): lax.ppermute(cache[0], 'head', [(d, page_target(d, other)) for d in range...  4.78 us
  transfers between devices with their start and end apart: 26, of which 15 were waited for; matrix products, arithmetic and copies ran while one was open for 1% of the time, Pallas kernels for 6%

profile of v19, /device:TPU:13, one launch (start us, length us, event | category | flops | bytes accessed | tf_op | source)
XLA Modules:
  0.0 238.3 jit_solution(8129931312715127613)
XLA Ops:
  0.0 2.6 %copy.29 = bf16[16,128,256]{2,1,0:T(8,128)(2,1)} copy(bf16[16,128,256]{2,0,1:T(8,128)(2,1)} %bitcast.55) | data formatting | bytes 2097152 | tf_op jit(solution)/shard_map/transpose | solution.py:590
  2.6 4.6 %all-to-all-start = ((bf16[8,2,128,256]{3,2,1,0:T(8,128)(2,1)}), bf16[8,2,128,256]{3,2,1,0:T(8,128)(2,1)S(1)}, u32[]{:S(2)}, u32[]{:S(2)}) async-start(bf16[8,2,128,256]{3,2,1,0:T(8,128)(2,1)} %bitcast.13), calls=%async_computation | async-start | bytes 2097152 | tf_op jit(solution)/shard_map/all_to_all | solution.py:592
  7.4 0.3 collective-permute-start.4
  7.7 0.5 constant_dynamic-slice_fusion.2
  8.3 0.1 collective-permute-start.2
  8.5 2.4 collective-permute-start.3
  10.9 2.2 collective-permute-start
  13.0 0.8 collective-permute-start.1
  13.8 10.6 %collective-permute-done.2 = bf16[128,512]{1,0:T(8,128)(2,1)S(1)} collective-permute-done((bf16[128,512]{1,0:T(8,128)(2,1)S(1)}, bf16[128,512]{1,0:T(8,128)(2,1)S(1)}, u32[]{:S(2)}, u32[]{:S(2)}) %collective-permute-start.2) | collective-permute-done | bytes 131104 | tf_op jit(solution)/shard_map/ppermute | solution.py:573
  24.4 3.0 %collective-permute-done.3 = bf16[128,512]{1,0:T(8,128)(2,1)S(1)} collective-permute-done((bf16[128,512]{1,0:T(8,128)(2,1)S(1)}, bf16[128,512]{1,0:T(8,128)(2,1)S(1)}, u32[]{:S(2)}, u32[]{:S(2)}) %collective-permute-start.3) | collective-permute-done | bytes 131104 | tf_op jit(solution)/shard_map/ppermute | solution.py:573
  27.6 0.7 collective-permute-start.5
  28.3 4.8 %collective-permute-done.1 = bf16[256,512]{1,0:T(8,128)(2,1)S(1)} collective-permute-done((bf16[256,512]{1,0:T(8,128)(2,1)}, bf16[256,512]{1,0:T(8,128)(2,1)S(1)}, u32[]{:S(2)}, u32[]{:S(2)}) %collective-permute-start.1) | collective-permute-done | bytes 262176 | tf_op jit(solution)/shard_map/ppermute | solution.py:601
  33.1 3.2 %collective-permute-done.5 = bf16[128,512]{1,0:T(8,128)(2,1)} collective-permute-done((bf16[128,512]{1,0:T(8,128)(2,1)S(1)}, bf16[128,512]{1,0:T(8,128)(2,1)}, u32[]{:S(2)}, u32[]{:S(2)}) %collective-permute-start.5) | collective-permute-done | bytes 131104 | tf_op jit(solution)/shard_map/ppermute | solution.py:573
  36.5 1.1 pad_maximum_fusion.2.kv_own
  37.6 0.2 collective-permute-start.9
  37.8 1.3 collective-permute-start.10
  39.1 1.3 collective-permute-start.8
  40.4 5.0 %collective-permute-start.7 = (bf16[2,2,4,16,1024]{4,3,2,1,0:T(8,128)(2,1)S(1)}, bf16[2,2,4,16,1024]{4,3,2,1,0:T(8,128)(2,1)S(1)}, u32[]{:S(2)}, u32[]{:S(2)}) collective-permute-start(bf16[2,2,4,16,1024]{4,3,2,1,0:T(8,128)(2,1)S(1)} %pad_maximum_fusion.1.refs_0_), channel_id=1, source_target_pairs={{0,8},{1,9},{2,10},{3,11},{4,12},{5,13},{6,14},{7,15},{8,0},{9,1},... | collective-permute-start | bytes 1572872 | tf_op jit(solution)/shard_map/ppermute | solution.py:573
  45.4 4.0 %collective-permute-done.9.kv_y = bf16[4,128,512]{2,1,0:T(8,128)(2,1)S(1)} collective-permute-done((bf16[4,128,512]{2,1,0:T(8,128)(2,1)S(1)}, bf16[4,128,512]{2,1,0:T(8,128)(2,1)S(1)}, u32[]{:S(2)}, u32[]{:S(2)}) %collective-permute-start.9) | collective-permute-done | bytes 524320 | tf_op jit(solution)/shard_map/ppermute | solution.py:573
  49.4 11.2 %collective-permute-done.8.page_y = bf16[512,512]{1,0:T(8,128)(2,1)S(1)} collective-permute-done((bf16[512,512]{1,0:T(8,128)(2,1)S(1)}, bf16[512,512]{1,0:T(8,128)(2,1)S(1)}, u32[]{:S(2)}, u32[]{:S(2)}) %collective-permute-start.8) | collective-permute-done | bytes 524320 | tf_op jit(solution)/shard_map/ppermute | solution.py:573
  60.6 2.6 %collective-permute-start.11 = (bf16[512,512]{1,0:T(8,128)(2,1)S(1)}, bf16[512,512]{1,0:T(8,128)(2,1)S(1)}, u32[]{:S(2)}, u32[]{:S(2)}) collective-permute-start(bf16[512,512]{1,0:T(8,128)(2,1)S(1)} %pad_maximum_fusion.page_own), channel_id=1, source_target_pairs={{0,1},{1,0},{2,3},{3,2},{4,5},{5,4},{6,7},{7,6},{8,9},{9,8},{10,11... | collective-permute-start | bytes 1572872 | tf_op jit(solution)/shard_map/ppermute | solution.py:573
  63.2 0.5 collective-permute-start.13
  63.7 3.5 %collective-permute-done.7.refs_4_ = bf16[2,2,4,16,1024]{4,3,2,1,0:T(8,128)(2,1)S(1)} collective-permute-done((bf16[2,2,4,16,1024]{4,3,2,1,0:T(8,128)(2,1)S(1)}, bf16[2,2,4,16,1024]{4,3,2,1,0:T(8,128)(2,1)S(1)}, u32[]{:S(2)}, u32[]{:S(2)}) %collective-permute-start.7) | collective-permute-done | bytes 524320 | tf_op jit(solution)/shard_map/ppermute | solution.py:573
  67.2 1.6 collective-permute-start.17
  68.8 0.3 collective-permute-start.15
  69.1 0.3 collective-permute-start.19
  69.4 15.4 %attend.1.a_hbm = bf16[2,512,512]{2,1,0:T(8,128)(2,1)S(1)} custom-call(bf16[8,2,128,256]{3,2,1,0:T(8,128)(2,1)} %copy-done.8, bf16[512,512]{1,0:T(8,128)(2,1)S(1)} %pad_maximum_fusion.page_own, bf16[512,512]{1,0:T(8,128)(2,1)S(1)} %collective-permute-done.8.page_y, bf16[512,512]{1,0:T(8,128)(2,1)S(1)} %collective-permute-done.11.page_c, ...), custom_call_target="tpu_custom_call" | custom-call | flops 7516192768 | bytes 6291456 | tf_op jit(solution)/shard_map/attend/pallas_call | solution.py:270
  84.9 0.3 collective-permute-start.18
  85.2 0.3 collective-permute-start.20
  85.4 0.2 collective-permute-start.16
  85.7 1.2 collective-permute-done.18.refs_3_
  86.8 0.7 collective-permute-done.20.refs_7_
  87.6 0.7 collective-permute-done.16.got_hbm
  88.3 4.4 %project.1 = (bf16[128,2048]{1,0:T(8,128)(2,1)}, bf16[128,2048]{1,0:T(8,128)(2,1)}, bf16[128,2048]{1,0:T(8,128)(2,1)}, bf16[128,2048]{1,0:T(8,128)(2,1)}) custom-call(bf16[2,512,512]{2,1,0:T(8,128)(2,1)S(1)} %attend.1.a_hbm, bf16[512,512]{1,0:T(8,128)(2,1)S(1)} %collective-permute-done.16.got_hbm, ...), custom_call_target="tpu_custom_call" | custom-call | flops 2147483648 | bytes 7340032 | tf_op jit(solution)/shard_map/project/pallas_call | solution.py:351
  92.7 4.0 %collective-permute-start.21 = (bf16[128,2048]{1,0:T(8,128)(2,1)}, bf16[128,2048]{1,0:T(8,128)(2,1)S(1)}, u32[]{:S(2)}, u32[]{:S(2)}) collective-permute-start(bf16[128,2048]{1,0:T(8,128)(2,1)} %get-tuple-element.52), channel_id=1, source_target_pairs={{0,6},{1,7},{2,4},{3,5},{4,2},{5,3},{6,0},{7,1},{8,14},{9,15},{10,... | collective-permute-start | bytes 1572872 | tf_op jit(solution)/shard_map/ppermute | solution.py:573
  96.8 1.1 collective-permute-start.23
  98.3 0.2 reduce_window_sum.11
  98.7 10.3 %collective-permute-done.21 = bf16[128,2048]{1,0:T(8,128)(2,1)S(1)} collective-permute-done((bf16[128,2048]{1,0:T(8,128)(2,1)}, bf16[128,2048]{1,0:T(8,128)(2,1)S(1)}, u32[]{:S(2)}, u32[]{:S(2)}) %collective-permute-start.21) | collective-permute-done | bytes 524320 | tf_op jit(solution)/shard_map/ppermute | solution.py:573
  109.0 11.2 %collective-permute-done.22 = bf16[128,2048]{1,0:T(8,128)(2,1)S(1)} collective-permute-done((bf16[128,2048]{1,0:T(8,128)(2,1)}, bf16[128,2048]{1,0:T(8,128)(2,1)S(1)}, u32[]{:S(2)}, u32[]{:S(2)}) %collective-permute-start.22) | collective-permute-done | bytes 524320 | tf_op jit(solution)/shard_map/ppermute | solution.py:573
  120.2 0.4 collective-permute-done.23
  120.6 1.0 copy-done.4
  121.7 1.1 route.1
  122.8 52.9 %all_to_all.15 = bf16[16,32,2048]{2,1,0:T(8,128)(2,1)S(1)} all-to-all(bf16[16,32,2048]{2,1,0:T(8,128)(2,1)S(1)} %bitcast.42), channel_id=1, replica_groups=mesh['grp'=2,'head'=16] {'head'}, dimensions={0} | all-to-all | bytes 4194304 | tf_op jit(solution)/shard_map/all_to_all | solution.py:752
  175.8 6.9 %expert.1 = bf16[512,2048]{1,0:T(8,128)(2,1)} custom-call(bf16[512,2048]{1,0:T(8,128)(2,1)S(1)} %bitcast.43, bf16[2048,1024]{1,0:T(8,128)(2,1)} %bitcast.65, bf16[512,2048]{1,0:T(8,128)(2,1)S(1)} %bitcast.52), custom_call_target="tpu_custom_call" | custom-call | flops 3221225472 | bytes 10485760 | tf_op jit(solution)/shard_map/expert/pallas_call | solution.py:508
  182.7 5.1 %all-to-all-start.2 = ((bf16[16,32,2048]{2,1,0:T(8,128)(2,1)}), bf16[16,32,2048]{2,1,0:T(8,128)(2,1)S(1)}, u32[]{:S(2)}, u32[]{:S(2)}) async-start(bf16[16,32,2048]{2,1,0:T(8,128)(2,1)} %bitcast.53), calls=%async_computation.2 | async-start | bytes 4194304 | tf_op jit(solution)/shard_map/all_to_all | solution.py:765
  187.9 47.3 %all-to-all-done.2 = bf16[16,32,2048]{2,1,0:T(8,128)(2,1)S(1)} async-done(((bf16[16,32,2048]{2,1,0:T(8,128)(2,1)}), bf16[16,32,2048]{2,1,0:T(8,128)(2,1)S(1)}, u32[]{:S(2)}, u32[]{:S(2)}) %all-to-all-start.2) | async-done | bytes 2097184 | tf_op jit(solution)/shard_map/all_to_all | solution.py:765
  235.2 1.2 copy-done.2
  236.4 1.7 combine.1
  (55 shorter events, 1.3 us)
Async XLA Ops:
  0.0 7.3 %copy-start = (bf16[16,16,2048]{2,1,0:T(8,128)(2,1)S(1)}, bf16[16,16,2048]{2,1,0:T(8,128)(2,1)}, u32[]{:S(2)}) copy-start(bf16[16,16,2048]{2,1,0:T(8,128)(2,1)} %param.14) | copy-start | bytes 3145732
  2.6 5.1 %copy-start.7 = (bf16[128,1,2,512]{3,2,1,0:T(2,128)(2,1)S(1)}, bf16[128,1,2,512]{3,2,1,0:T(2,128)(2,1)}, u32[]{:S(2)}) copy-start(bf16[128,1,2,512]{3,2,1,0:T(2,128)(2,1)} %param.11) | copy-start | bytes 786436
  2.6 33.8 %all-to-all-start = ((bf16[8,2,128,256]{3,2,1,0:T(8,128)(2,1)}), bf16[8,2,128,256]{3,2,1,0:T(8,128)(2,1)S(1)}, u32[]{:S(2)}, u32[]{:S(2)}) async-start(bf16[8,2,128,256]{3,2,1,0:T(8,128)(2,1)} %bitcast.13), calls=%async_computation | async-start | bytes 2097152 | tf_op jit(solution)/shard_map/all_to_all | solution.py:592
  7.4 20.0 %collective-permute-start.4 = (bf16[2,4,16,1024]{3,2,1,0:T(8,128)(2,1)S(1)}, bf16[2,4,16,1024]{3,2,1,0:T(8,128)(2,1)S(1)}, u32[]{:S(2)}, u32[]{:S(2)}) collective-permute-start(bf16[2,4,16,1024]{3,2,1,0:T(8,128)(2,1)S(1)} %get-tuple-element.60), channel_id=1, source_target_pairs={{0,2},{1,3},{2,0},{3,1},{4,6},{5,7},{6,4},{7,5},{8,10},{9,11},{10,... | collective-permute-start | bytes 786440 | tf_op jit(solution)/shard_map/ppermute | solution.py:573
  8.3 16.1 %collective-permute-start.2 = (bf16[128,512]{1,0:T(8,128)(2,1)S(1)}, bf16[128,512]{1,0:T(8,128)(2,1)S(1)}, u32[]{:S(2)}, u32[]{:S(2)}) collective-permute-start(bf16[128,512]{1,0:T(8,128)(2,1)S(1)} %bitcast.61), channel_id=1, source_target_pairs={{0,4},{1,5},{2,6},{3,7},{4,0},{5,1},{6,2},{7,3},{8,12},{9,13},{10,... | collective-permute-start | bytes 393224 | tf_op jit(solution)/shard_map/ppermute | solution.py:573
  8.5 18.9 %collective-permute-start.3 = (bf16[128,512]{1,0:T(8,128)(2,1)S(1)}, bf16[128,512]{1,0:T(8,128)(2,1)S(1)}, u32[]{:S(2)}, u32[]{:S(2)}) collective-permute-start(bf16[128,512]{1,0:T(8,128)(2,1)S(1)} %bitcast.57), channel_id=1, source_target_pairs={{0,8},{1,9},{2,10},{3,11},{4,12},{5,13},{6,14},{7,15},{8,0},{9,1},... | collective-permute-start | bytes 393224 | tf_op jit(solution)/shard_map/ppermute | solution.py:573
  10.9 17.4 %collective-permute-start = (bf16[256,512]{1,0:T(8,128)(2,1)}, bf16[256,512]{1,0:T(8,128)(2,1)S(1)}, u32[]{:S(2)}, u32[]{:S(2)}) collective-permute-start(bf16[256,512]{1,0:T(8,128)(2,1)} %bitcast.66), channel_id=1, source_target_pairs={{0,0},{1,1},{2,2},{3,3},{4,8},{5,9},{6,10},{7,11},{8,4},{9,5},{10,... | collective-permute-start | bytes 786440 | tf_op jit(solution)/shard_map/ppermute | solution.py:601
  13.0 20.0 %collective-permute-start.1 = (bf16[256,512]{1,0:T(8,128)(2,1)}, bf16[256,512]{1,0:T(8,128)(2,1)S(1)}, u32[]{:S(2)}, u32[]{:S(2)}) collective-permute-start(bf16[256,512]{1,0:T(8,128)(2,1)} %bitcast.67), channel_id=1, source_target_pairs={{0,8},{1,9},{2,10},{3,11},{4,0},{5,1},{6,2},{7,3},{8,12},{9,13},{1... | collective-permute-start | bytes 786440 | tf_op jit(solution)/shard_map/ppermute | solution.py:601
  27.5 9.0 %collective-permute-start.6 = (bf16[2,4,16,1024]{3,2,1,0:T(8,128)(2,1)S(1)}, bf16[2,4,16,1024]{3,2,1,0:T(8,128)(2,1)S(1)}, u32[]{:S(2)}, u32[]{:S(2)}) collective-permute-start(bf16[2,4,16,1024]{3,2,1,0:T(8,128)(2,1)S(1)} %get-tuple-element.58), channel_id=1, source_target_pairs={{0,4},{1,5},{2,6},{3,7},{4,0},{5,1},{6,2},{7,3},{8,12},{9,13},{10,... | collective-permute-start | bytes 786440 | tf_op jit(solution)/shard_map/ppermute | solution.py:573
  27.6 8.8 %collective-permute-start.5 = (bf16[128,512]{1,0:T(8,128)(2,1)S(1)}, bf16[128,512]{1,0:T(8,128)(2,1)}, u32[]{:S(2)}, u32[]{:S(2)}) collective-permute-start(bf16[128,512]{1,0:T(8,128)(2,1)S(1)} %bitcast.62), channel_id=1, source_target_pairs={{0,12},{1,13},{2,14},{3,15},{4,8},{5,9},{6,10},{7,11},{8,4},{9,5},... | collective-permute-start | bytes 393224 | tf_op jit(solution)/shard_map/ppermute | solution.py:573
  36.5 1.3 copy-start.8
  37.6 11.8 %collective-permute-start.9 = (bf16[4,128,512]{2,1,0:T(8,128)(2,1)S(1)}, bf16[4,128,512]{2,1,0:T(8,128)(2,1)S(1)}, u32[]{:S(2)}, u32[]{:S(2)}) collective-permute-start(bf16[4,128,512]{2,1,0:T(8,128)(2,1)S(1)} %pad_maximum_fusion.2.kv_own), channel_id=1, source_target_pairs={{0,2},{1,3},{2,0},{3,1},{4,6},{5,7},{6,4},{7,5},{8,10},{9,11},{10,... | collective-permute-start | bytes 1572872 | tf_op jit(solution)/shard_map/ppermute | solution.py:573
  37.8 11.6 %collective-permute-start.10 = (bf16[2,2,4,16,1024]{4,3,2,1,0:T(8,128)(2,1)S(1)}, bf16[2,2,4,16,1024]{4,3,2,1,0:T(8,128)(2,1)S(1)}, u32[]{:S(2)}, u32[]{:S(2)}) collective-permute-start(bf16[2,2,4,16,1024]{4,3,2,1,0:T(8,128)(2,1)S(1)} %pad_maximum_fusion.1.refs_0_), channel_id=1, source_target_pairs={{0,16},{16,0},{1,17},{17,1},{2,18},{18,2},{3,19},{19,3},{4,20},{20... | collective-permute-start | bytes 1572872 | tf_op jit(solution)/shard_map/ppermute | solution.py:573
  39.1 21.5 %collective-permute-start.8 = (bf16[512,512]{1,0:T(8,128)(2,1)S(1)}, bf16[512,512]{1,0:T(8,128)(2,1)S(1)}, u32[]{:S(2)}, u32[]{:S(2)}) collective-permute-start(bf16[512,512]{1,0:T(8,128)(2,1)S(1)} %pad_maximum_fusion.page_own), channel_id=1, source_target_pairs={{0,2},{1,3},{2,0},{3,1},{4,6},{5,7},{6,4},{7,5},{8,10},{9,11},{10,... | collective-permute-start | bytes 1572872 | tf_op jit(solution)/shard_map/ppermute | solution.py:573
  40.4 26.8 %collective-permute-start.7 = (bf16[2,2,4,16,1024]{4,3,2,1,0:T(8,128)(2,1)S(1)}, bf16[2,2,4,16,1024]{4,3,2,1,0:T(8,128)(2,1)S(1)}, u32[]{:S(2)}, u32[]{:S(2)}) collective-permute-start(bf16[2,2,4,16,1024]{4,3,2,1,0:T(8,128)(2,1)S(1)} %pad_maximum_fusion.1.refs_0_), channel_id=1, source_target_pairs={{0,8},{1,9},{2,10},{3,11},{4,12},{5,13},{6,14},{7,15},{8,0},{9,1},... | collective-permute-start | bytes 1572872 | tf_op jit(solution)/shard_map/ppermute | solution.py:573
  60.6 8.2 %collective-permute-start.11 = (bf16[512,512]{1,0:T(8,128)(2,1)S(1)}, bf16[512,512]{1,0:T(8,128)(2,1)S(1)}, u32[]{:S(2)}, u32[]{:S(2)}) collective-permute-start(bf16[512,512]{1,0:T(8,128)(2,1)S(1)} %pad_maximum_fusion.page_own), channel_id=1, source_target_pairs={{0,1},{1,0},{2,3},{3,2},{4,5},{5,4},{6,7},{7,6},{8,9},{9,8},{10,11... | collective-permute-start | bytes 1572872 | tf_op jit(solution)/shard_map/ppermute | solution.py:573
  63.2 5.9 %collective-permute-start.12 = (bf16[512,512]{1,0:T(8,128)(2,1)S(1)}, bf16[512,512]{1,0:T(8,128)(2,1)S(1)}, u32[]{:S(2)}, u32[]{:S(2)}) collective-permute-start(bf16[512,512]{1,0:T(8,128)(2,1)S(1)} %collective-permute-done.8.page_y), channel_id=1, source_target_pairs={{0,1},{1,0},{2,3},{3,2},{4,5},{5,4},{6,7},{7,6},{8,9},{9,8},{10,11... | collective-permute-start | bytes 1572872 | tf_op jit(solution)/shard_map/ppermute | solution.py:573
  63.2 6.1 %collective-permute-start.13 = (bf16[4,128,512]{2,1,0:T(8,128)(2,1)S(1)}, bf16[4,128,512]{2,1,0:T(8,128)(2,1)S(1)}, u32[]{:S(2)}, u32[]{:S(2)}) collective-permute-start(bf16[4,128,512]{2,1,0:T(8,128)(2,1)S(1)} %pad_maximum_fusion.2.kv_own), channel_id=1, source_target_pairs={{0,1},{1,0},{2,3},{3,2},{4,5},{5,4},{6,7},{7,6},{8,9},{9,8},{10,11... | collective-permute-start | bytes 1572872 | tf_op jit(solution)/shard_map/ppermute | solution.py:573
  63.7 5.6 %collective-permute-start.14 = (bf16[4,128,512]{2,1,0:T(8,128)(2,1)S(1)}, bf16[4,128,512]{2,1,0:T(8,128)(2,1)S(1)}, u32[]{:S(2)}, u32[]{:S(2)}) collective-permute-start(bf16[4,128,512]{2,1,0:T(8,128)(2,1)S(1)} %collective-permute-done.9.kv_y), channel_id=1, source_target_pairs={{0,1},{1,0},{2,3},{3,2},{4,5},{5,4},{6,7},{7,6},{8,9},{9,8},{10,11... | collective-permute-start | bytes 1572872 | tf_op jit(solution)/shard_map/ppermute | solution.py:573
  67.2 18.5 %collective-permute-start.17 = (bf16[2,2,4,16,1024]{4,3,2,1,0:T(8,128)(2,1)S(1)}, bf16[2,2,4,16,1024]{4,3,2,1,0:T(8,128)(2,1)S(1)}, u32[]{:S(2)}, u32[]{:S(2)}) collective-permute-start(bf16[2,2,4,16,1024]{4,3,2,1,0:T(8,128)(2,1)S(1)} %pad_maximum_fusion.1.refs_0_), channel_id=1, source_target_pairs={{0,1},{1,0},{2,3},{3,2},{4,5},{5,4},{6,7},{7,6},{8,9},{9,8},{10,11... | collective-permute-start | bytes 1572872 | tf_op jit(solution)/shard_map/ppermute | solution.py:573
  68.8 16.0 %collective-permute-start.15 = (bf16[2,2,4,16,1024]{4,3,2,1,0:T(8,128)(2,1)S(1)}, bf16[2,2,4,16,1024]{4,3,2,1,0:T(8,128)(2,1)S(1)}, u32[]{:S(2)}, u32[]{:S(2)}) collective-permute-start(bf16[2,2,4,16,1024]{4,3,2,1,0:T(8,128)(2,1)S(1)} %collective-permute-done.7.refs_4_), channel_id=1, source_target_pairs={{0,16},{16,0},{1,17},{17,1},{2,18},{18,2},{3,19},{19,3},{4,20},{20... | collective-permute-start | bytes 1572872 | tf_op jit(solution)/shard_map/ppermute | solution.py:573
  69.1 16.6 %collective-permute-start.19 = (bf16[2,2,4,16,1024]{4,3,2,1,0:T(8,128)(2,1)S(1)}, bf16[2,2,4,16,1024]{4,3,2,1,0:T(8,128)(2,1)S(1)}, u32[]{:S(2)}, u32[]{:S(2)}) collective-permute-start(bf16[2,2,4,16,1024]{4,3,2,1,0:T(8,128)(2,1)S(1)} %collective-permute-done.7.refs_4_), channel_id=1, source_target_pairs={{0,1},{1,0},{2,3},{3,2},{4,5},{5,4},{6,7},{7,6},{8,9},{9,8},{10,11... | collective-permute-start | bytes 1572872 | tf_op jit(solution)/shard_map/ppermute | solution.py:573
  84.8 13.1 %copy-start.9 = (s32[128,1,2]{0,2,1:T(2,128)S(1)}, s32[128,1,2]{0,2,1:T(2,128)}, u32[]{:S(2)}) copy-start(s32[128,1,2]{0,2,1:T(2,128)} %param.16) | copy-start | bytes 3076
  84.8 35.8 %copy-start.3 = (bf16[128,1,2048]{2,0,1:T(8,128)(2,1)S(1)}, bf16[128,1,2048]{2,0,1:T(8,128)(2,1)}, u32[]{:S(2)}) copy-start(bf16[128,1,2048]{2,0,1:T(8,128)(2,1)} %param.13) | copy-start | bytes 1572868
  84.8 35.8 %copy-start.5 = (f32[2048]{0:T(1024)S(1)}, f32[2048]{0:T(1024)}, u32[]{:S(2)}) copy-start(f32[2048]{0:T(1024)} %param.15) | copy-start | bytes 24580
  84.9 2.0 collective-permute-start.18
  85.2 2.4 %collective-permute-start.20 = (bf16[2,2,4,16,1024]{4,3,2,1,0:T(8,128)(2,1)S(1)}, bf16[2,2,4,16,1024]{4,3,2,1,0:T(8,128)(2,1)S(1)}, u32[]{:S(2)}, u32[]{:S(2)}) collective-permute-start(bf16[2,2,4,16,1024]{4,3,2,1,0:T(8,128)(2,1)S(1)} %collective-permute-done.15.refs_6_), channel_id=1, source_target_pairs={{0,1},{1,0},{2,3},{3,2},{4,5},{5,4},{6,7},{7,6},{8,9},{9,8},{10,11... | collective-permute-start | bytes 1572872 | tf_op jit(solution)/shard_map/ppermute | solution.py:573
  85.4 2.9 %collective-permute-start.16 = (bf16[512,512]{1,0:T(8,128)(2,1)S(1)}, bf16[512,512]{1,0:T(8,128)(2,1)S(1)}, u32[]{:S(2)}, u32[]{:S(2)}) collective-permute-start(bf16[512,512]{1,0:T(8,128)(2,1)S(1)} %slice_bitcast_fusion), channel_id=1, source_target_pairs={{0,1},{1,0},{2,3},{3,2},{4,5},{5,4},{6,7},{7,6},{8,9},{9,8},{10,11... | collective-permute-start | bytes 1572872 | tf_op jit(solution)/shard_map/ppermute | solution.py:573
  92.7 16.3 %collective-permute-start.21 = (bf16[128,2048]{1,0:T(8,128)(2,1)}, bf16[128,2048]{1,0:T(8,128)(2,1)S(1)}, u32[]{:S(2)}, u32[]{:S(2)}) collective-permute-start(bf16[128,2048]{1,0:T(8,128)(2,1)} %get-tuple-element.52), channel_id=1, source_target_pairs={{0,6},{1,7},{2,4},{3,5},{4,2},{5,3},{6,0},{7,1},{8,14},{9,15},{10,... | collective-permute-start | bytes 1572872 | tf_op jit(solution)/shard_map/ppermute | solution.py:573
  96.8 23.5 %collective-permute-start.22 = (bf16[128,2048]{1,0:T(8,128)(2,1)}, bf16[128,2048]{1,0:T(8,128)(2,1)S(1)}, u32[]{:S(2)}, u32[]{:S(2)}) collective-permute-start(bf16[128,2048]{1,0:T(8,128)(2,1)} %get-tuple-element.53), channel_id=1, source_target_pairs={{0,4},{1,5},{2,6},{3,7},{4,0},{5,1},{6,2},{7,3},{8,12},{9,13},{10,... | collective-permute-start | bytes 1572872 | tf_op jit(solution)/shard_map/ppermute | solution.py:573
  96.8 23.8 %collective-permute-start.23 = (bf16[128,2048]{1,0:T(8,128)(2,1)}, bf16[128,2048]{1,0:T(8,128)(2,1)S(1)}, u32[]{:S(2)}, u32[]{:S(2)}) collective-permute-start(bf16[128,2048]{1,0:T(8,128)(2,1)} %get-tuple-element.54), channel_id=1, source_target_pairs={{0,2},{1,3},{2,0},{3,1},{4,6},{5,7},{6,4},{7,5},{8,10},{9,11},{10,... | collective-permute-start | bytes 1572872 | tf_op jit(solution)/shard_map/ppermute | solution.py:573
  120.6 1.0 copy-start.4
  122.8 53.0 %copy-start.1 = (f32[128,2048]{1,0:T(8,128)}, f32[128,2048]{1,0:T(8,128)S(1)}, u32[]{:S(2)}) copy-start(f32[128,2048]{1,0:T(8,128)S(1)} %get-tuple-element.56.stream_hbm) | copy-start | bytes 3145732
  122.8 52.9 %copy-start.6 = (bf16[1,512,2048]{2,1,0:T(8,128)(2,1)S(1)}, bf16[1,512,2048]{2,1,0:T(8,128)(2,1)}, u32[]{:S(2)}) copy-start(bf16[1,512,2048]{2,1,0:T(8,128)(2,1)} %param.19) | copy-start | bytes 6291460
  182.6 5.1 %copy-start.10 = (f32[128,1,2]{0,2,1:T(2,128)S(1)}, f32[128,1,2]{0,2,1:T(2,128)}, u32[]{:S(2)}) copy-start(f32[128,1,2]{0,2,1:T(2,128)} %param.17) | copy-start | bytes 3076
  182.7 52.6 %all-to-all-start.2 = ((bf16[16,32,2048]{2,1,0:T(8,128)(2,1)}), bf16[16,32,2048]{2,1,0:T(8,128)(2,1)S(1)}, u32[]{:S(2)}, u32[]{:S(2)}) async-start(bf16[16,32,2048]{2,1,0:T(8,128)(2,1)} %bitcast.53), calls=%async_computation.2 | async-start | bytes 4194304 | tf_op jit(solution)/shard_map/all_to_all | solution.py:765
  235.2 1.2 copy-start.2

commit v20 on v19

--- a/solution.py
+++ b/solution.py
@@ -157,21 +157,20 @@
     earlier_group = me // members > 0
     core = lax.rem(me, 2)
     chip = jnp.bitwise_and(me // 2, members // 2 - 1)
-    copies = [[] for _ in range(6)]
+    copies = []
 
     def bring(source, target, sem):
         copy = pltpu.make_async_copy(source, target, sems.at[sem])
         copy.start()
-        copies[sem].append(copy)
+        copies.append(copy)
 
     for member in range(members):
         for head in range(heads):
             bring(q_hbm.at[member, head], q_ref.at[head, pl.ds(member * piece, piece)], 0)
-    place, places = 0, []
-    for sem, page in enumerate((page_own, page_y, page_c, page_cy)):
+    place = 0
+    for page in (page_own, page_y, page_c, page_cy):
         count = page.shape[0]
-        bring(page, old_ref.at[pl.ds(place, count)], 1 + sem)
-        places.append(place)
+        bring(page, old_ref.at[pl.ds(place, count)], 1)
         place += count
     for flip, pieces_of in ((0, kv_own), (2, kv_y), (1, kv_c), (3, kv_cy)):
         for t in range(planes):
@@ -180,13 +179,9 @@
             )
             start = pl.multiple_of(number * piece, piece)
             area = 0 if t * (members // 2) >= members else length
-            bring(pieces_of.at[t], kv_ref.at[pl.ds(area + start, piece)], 5)
-    def arrive(sem):
-        for copy in copies[sem]:
-            copy.wait()
-        copies[sem] = []
-
-    arrive(0)
+            bring(pieces_of.at[t], kv_ref.at[pl.ds(area + start, piece)], 2)
+    for copy in copies:
+        copy.wait()
     scale = width**-0.5 * LOG2_E
     scores = [s0, s1]
     blocks = length // block
@@ -235,12 +230,6 @@
 
     running = None
     for part in pieces(0):
-        if part[0] != "old":
-            arrive(5)
-        else:
-            for sem, start in enumerate(places):
-                if start < part[1] + part[2]:
-                    arrive(1 + sem)
         running = make_scores(0, part, running)
     for unit, (head, b) in enumerate(units):
         top = jnp.max(running, 1, keepdims=True)
@@ -278,7 +267,7 @@
             pltpu.VMEM((2 * length, 2 * width), BF16),
             pltpu.VMEM((block, keys), F32),
             pltpu.VMEM((block, keys), F32),
-            pltpu.SemaphoreType.DMA((6,)),
+            pltpu.SemaphoreType.DMA((3,)),
         ],
         compiler_params=pltpu.CompilerParams(vmem_limit_bytes=HIGH_VMEM),
         cost_estimate=pl.CostEstimate(

time: 239 us -> 238 us (level)
  no operation moved by 1% of the time
where the time goes in v20:
time: 238 us
  waiting for transfers between devices  112 us (47%)
  blocking collectives  52.9 us (22%)
  starting transfers between devices  35.5 us (15%)
  Pallas kernels  28.9 us (12%)
  local copies, waits for them, and re-layouts  6.28 us (3%)
    ppermute x22, waiting for transfers between devices, flipped(): return lax.ppermute(value, axis, pairs)  60.1 us
    all_to_all x1, blocking collectives, local(): lax.all_to_all(outgoing.reshape(n, slots // n, model), 'head', split_axis...  52.9 us
    all_to_all x1, waiting for transfers between devices, local(): lax.all_to_all(answered, 'head', split_axis=0, concat_axis=0, tiled=True)  47.3 us
    ppermute x22, starting transfers between devices, flipped(): return lax.ppermute(value, axis, pairs)  22.7 us
    pallas_call x1, Pallas kernels, attend_pair(): pl.pallas_call(functools.partial(attend_pair_kernel, block, chunk, width)...  14.5 us
    pallas_call x1, Pallas kernels, expert_pair(): pl.pallas_call(kernel, out_shape=pltpu.HBM((rows, model), BF16), in_specs...  6.87 us
    all_to_all x1, starting transfers between devices, local(): lax.all_to_all(answered, 'head', split_axis=0, concat_axis=0, tiled=True)  5.14 us
    ppermute x2, waiting for transfers between devices, parts_in_pairs(): lax.ppermute(cache[0], 'head', [(d, page_target(d, other)) for d in range...  4.78 us
  transfers between devices with their start and end apart: 26, of which 15 were waited for; matrix products, arithmetic and copies ran while one was open for 1% of the time, Pallas kernels for 6%

profile of v20, /device:TPU:13, one launch (start us, length us, event | category | flops | bytes accessed | tf_op | source)
XLA Modules:
  0.0 237.7 jit_solution(18421078089848086806)
XLA Ops:
  0.0 2.6 %copy.29 = bf16[16,128,256]{2,1,0:T(8,128)(2,1)} copy(bf16[16,128,256]{2,0,1:T(8,128)(2,1)} %bitcast.55) | data formatting | bytes 2097152 | tf_op jit(solution)/shard_map/transpose | solution.py:579
  2.6 4.6 %all-to-all-start = ((bf16[8,2,128,256]{3,2,1,0:T(8,128)(2,1)}), bf16[8,2,128,256]{3,2,1,0:T(8,128)(2,1)S(1)}, u32[]{:S(2)}, u32[]{:S(2)}) async-start(bf16[8,2,128,256]{3,2,1,0:T(8,128)(2,1)} %bitcast.13), calls=%async_computation | async-start | bytes 2097152 | tf_op jit(solution)/shard_map/all_to_all | solution.py:581
  7.4 0.3 collective-permute-start.4
  7.7 0.5 constant_dynamic-slice_fusion.2
  8.3 0.1 collective-permute-start.2
  8.5 2.4 collective-permute-start.3
  10.9 2.2 collective-permute-start
  13.0 0.8 collective-permute-start.1
  13.8 10.6 %collective-permute-done.2 = bf16[128,512]{1,0:T(8,128)(2,1)S(1)} collective-permute-done((bf16[128,512]{1,0:T(8,128)(2,1)S(1)}, bf16[128,512]{1,0:T(8,128)(2,1)S(1)}, u32[]{:S(2)}, u32[]{:S(2)}) %collective-permute-start.2) | collective-permute-done | bytes 131104 | tf_op jit(solution)/shard_map/ppermute | solution.py:562
  24.4 3.0 %collective-permute-done.3 = bf16[128,512]{1,0:T(8,128)(2,1)S(1)} collective-permute-done((bf16[128,512]{1,0:T(8,128)(2,1)S(1)}, bf16[128,512]{1,0:T(8,128)(2,1)S(1)}, u32[]{:S(2)}, u32[]{:S(2)}) %collective-permute-start.3) | collective-permute-done | bytes 131104 | tf_op jit(solution)/shard_map/ppermute | solution.py:562
  27.6 0.7 collective-permute-start.5
  28.3 4.8 %collective-permute-done.1 = bf16[256,512]{1,0:T(8,128)(2,1)S(1)} collective-permute-done((bf16[256,512]{1,0:T(8,128)(2,1)}, bf16[256,512]{1,0:T(8,128)(2,1)S(1)}, u32[]{:S(2)}, u32[]{:S(2)}) %collective-permute-start.1) | collective-permute-done | bytes 262176 | tf_op jit(solution)/shard_map/ppermute | solution.py:590
  33.1 3.2 %collective-permute-done.5 = bf16[128,512]{1,0:T(8,128)(2,1)} collective-permute-done((bf16[128,512]{1,0:T(8,128)(2,1)S(1)}, bf16[128,512]{1,0:T(8,128)(2,1)}, u32[]{:S(2)}, u32[]{:S(2)}) %collective-permute-start.5) | collective-permute-done | bytes 131104 | tf_op jit(solution)/shard_map/ppermute | solution.py:562
  36.5 1.1 pad_maximum_fusion.2.kv_own
  37.6 0.2 collective-permute-start.9
  37.8 1.3 collective-permute-start.10
  39.1 1.3 collective-permute-start.8
  40.4 5.0 %collective-permute-start.7 = (bf16[2,2,4,16,1024]{4,3,2,1,0:T(8,128)(2,1)S(1)}, bf16[2,2,4,16,1024]{4,3,2,1,0:T(8,128)(2,1)S(1)}, u32[]{:S(2)}, u32[]{:S(2)}) collective-permute-start(bf16[2,2,4,16,1024]{4,3,2,1,0:T(8,128)(2,1)S(1)} %pad_maximum_fusion.1.refs_0_), channel_id=1, source_target_pairs={{0,8},{1,9},{2,10},{3,11},{4,12},{5,13},{6,14},{7,15},{8,0},{9,1},... | collective-permute-start | bytes 1572872 | tf_op jit(solution)/shard_map/ppermute | solution.py:562
  45.4 4.0 %collective-permute-done.9.kv_y = bf16[4,128,512]{2,1,0:T(8,128)(2,1)S(1)} collective-permute-done((bf16[4,128,512]{2,1,0:T(8,128)(2,1)S(1)}, bf16[4,128,512]{2,1,0:T(8,128)(2,1)S(1)}, u32[]{:S(2)}, u32[]{:S(2)}) %collective-permute-start.9) | collective-permute-done | bytes 524320 | tf_op jit(solution)/shard_map/ppermute | solution.py:562
  49.4 11.2 %collective-permute-done.8.page_y = bf16[512,512]{1,0:T(8,128)(2,1)S(1)} collective-permute-done((bf16[512,512]{1,0:T(8,128)(2,1)S(1)}, bf16[512,512]{1,0:T(8,128)(2,1)S(1)}, u32[]{:S(2)}, u32[]{:S(2)}) %collective-permute-start.8) | collective-permute-done | bytes 524320 | tf_op jit(solution)/shard_map/ppermute | solution.py:562
  60.6 2.6 %collective-permute-start.11 = (bf16[512,512]{1,0:T(8,128)(2,1)S(1)}, bf16[512,512]{1,0:T(8,128)(2,1)S(1)}, u32[]{:S(2)}, u32[]{:S(2)}) collective-permute-start(bf16[512,512]{1,0:T(8,128)(2,1)S(1)} %pad_maximum_fusion.page_own), channel_id=1, source_target_pairs={{0,1},{1,0},{2,3},{3,2},{4,5},{5,4},{6,7},{7,6},{8,9},{9,8},{10,11... | collective-permute-start | bytes 1572872 | tf_op jit(solution)/shard_map/ppermute | solution.py:562
  63.2 0.5 collective-permute-start.13
  63.7 3.5 %collective-permute-done.7.refs_4_ = bf16[2,2,4,16,1024]{4,3,2,1,0:T(8,128)(2,1)S(1)} collective-permute-done((bf16[2,2,4,16,1024]{4,3,2,1,0:T(8,128)(2,1)S(1)}, bf16[2,2,4,16,1024]{4,3,2,1,0:T(8,128)(2,1)S(1)}, u32[]{:S(2)}, u32[]{:S(2)}) %collective-permute-start.7) | collective-permute-done | bytes 524320 | tf_op jit(solution)/shard_map/ppermute | solution.py:562
  67.2 1.6 collective-permute-start.17
  68.8 0.3 collective-permute-start.15
  69.1 0.3 collective-permute-start.19
  69.4 14.5 %attend.1.a_hbm = bf16[2,512,512]{2,1,0:T(8,128)(2,1)S(1)} custom-call(bf16[8,2,128,256]{3,2,1,0:T(8,128)(2,1)} %copy-done.8, bf16[512,512]{1,0:T(8,128)(2,1)S(1)} %pad_maximum_fusion.page_own, bf16[512,512]{1,0:T(8,128)(2,1)S(1)} %collective-permute-done.8.page_y, bf16[512,512]{1,0:T(8,128)(2,1)S(1)} %collective-permute-done.11.page_c, ...), custom_call_target="tpu_custom_call" | custom-call | flops 7516192768 | bytes 6291456 | tf_op jit(solution)/shard_map/attend/pallas_call | solution.py:259
  84.0 0.3 collective-permute-start.18
  84.2 0.3 collective-permute-start.20
  84.5 0.2 collective-permute-start.16
  84.8 1.2 collective-permute-done.18.refs_3_
  85.9 0.7 collective-permute-done.20.refs_7_
  86.7 0.7 collective-permute-done.16.got_hbm
  87.4 4.6 %project.1 = (bf16[128,2048]{1,0:T(8,128)(2,1)}, bf16[128,2048]{1,0:T(8,128)(2,1)}, bf16[128,2048]{1,0:T(8,128)(2,1)}, bf16[128,2048]{1,0:T(8,128)(2,1)}) custom-call(bf16[2,512,512]{2,1,0:T(8,128)(2,1)S(1)} %attend.1.a_hbm, bf16[512,512]{1,0:T(8,128)(2,1)S(1)} %collective-permute-done.16.got_hbm, ...), custom_call_target="tpu_custom_call" | custom-call | flops 2147483648 | bytes 7340032 | tf_op jit(solution)/shard_map/project/pallas_call | solution.py:340
  92.0 4.0 %collective-permute-start.21 = (bf16[128,2048]{1,0:T(8,128)(2,1)}, bf16[128,2048]{1,0:T(8,128)(2,1)S(1)}, u32[]{:S(2)}, u32[]{:S(2)}) collective-permute-start(bf16[128,2048]{1,0:T(8,128)(2,1)} %get-tuple-element.52), channel_id=1, source_target_pairs={{0,6},{1,7},{2,4},{3,5},{4,2},{5,3},{6,0},{7,1},{8,14},{9,15},{10,... | collective-permute-start | bytes 1572872 | tf_op jit(solution)/shard_map/ppermute | solution.py:562
  96.1 1.1 collective-permute-start.23
  97.6 0.2 reduce_window_sum.11
  98.0 10.3 %collective-permute-done.21 = bf16[128,2048]{1,0:T(8,128)(2,1)S(1)} collective-permute-done((bf16[128,2048]{1,0:T(8,128)(2,1)}, bf16[128,2048]{1,0:T(8,128)(2,1)S(1)}, u32[]{:S(2)}, u32[]{:S(2)}) %collective-permute-start.21) | collective-permute-done | bytes 524320 | tf_op jit(solution)/shard_map/ppermute | solution.py:562
  108.3 11.2 %collective-permute-done.22 = bf16[128,2048]{1,0:T(8,128)(2,1)S(1)} collective-permute-done((bf16[128,2048]{1,0:T(8,128)(2,1)}, bf16[128,2048]{1,0:T(8,128)(2,1)S(1)}, u32[]{:S(2)}, u32[]{:S(2)}) %collective-permute-start.22) | collective-permute-done | bytes 524320 | tf_op jit(solution)/shard_map/ppermute | solution.py:562
  119.6 0.3 collective-permute-done.23
  119.9 1.0 copy-done.4
  120.9 1.2 route.1
  122.1 52.9 %all_to_all.15 = bf16[16,32,2048]{2,1,0:T(8,128)(2,1)S(1)} all-to-all(bf16[16,32,2048]{2,1,0:T(8,128)(2,1)S(1)} %bitcast.42), channel_id=1, replica_groups=mesh['grp'=2,'head'=16] {'head'}, dimensions={0} | all-to-all | bytes 4194304 | tf_op jit(solution)/shard_map/all_to_all | solution.py:741
  175.1 6.9 %expert.1 = bf16[512,2048]{1,0:T(8,128)(2,1)} custom-call(bf16[512,2048]{1,0:T(8,128)(2,1)S(1)} %bitcast.43, bf16[2048,1024]{1,0:T(8,128)(2,1)} %bitcast.65, bf16[512,2048]{1,0:T(8,128)(2,1)S(1)} %bitcast.52), custom_call_target="tpu_custom_call" | custom-call | flops 3221225472 | bytes 10485760 | tf_op jit(solution)/shard_map/expert/pallas_call | solution.py:497
  182.0 5.1 %all-to-all-start.2 = ((bf16[16,32,2048]{2,1,0:T(8,128)(2,1)}), bf16[16,32,2048]{2,1,0:T(8,128)(2,1)S(1)}, u32[]{:S(2)}, u32[]{:S(2)}) async-start(bf16[16,32,2048]{2,1,0:T(8,128)(2,1)} %bitcast.53), calls=%async_computation.2 | async-start | bytes 4194304 | tf_op jit(solution)/shard_map/all_to_all | solution.py:754
  187.2 47.3 %all-to-all-done.2 = bf16[16,32,2048]{2,1,0:T(8,128)(2,1)S(1)} async-done(((bf16[16,32,2048]{2,1,0:T(8,128)(2,1)}), bf16[16,32,2048]{2,1,0:T(8,128)(2,1)S(1)}, u32[]{:S(2)}, u32[]{:S(2)}) %all-to-all-start.2) | async-done | bytes 2097184 | tf_op jit(solution)/shard_map/all_to_all | solution.py:754
  234.5 1.2 copy-done.2
  235.8 1.7 combine.1
  (55 shorter events, 1.4 us)
Async XLA Ops:
  0.0 7.3 %copy-start = (bf16[16,16,2048]{2,1,0:T(8,128)(2,1)S(1)}, bf16[16,16,2048]{2,1,0:T(8,128)(2,1)}, u32[]{:S(2)}) copy-start(bf16[16,16,2048]{2,1,0:T(8,128)(2,1)} %param.14) | copy-start | bytes 3145732
  2.6 5.1 %copy-start.7 = (bf16[128,1,2,512]{3,2,1,0:T(2,128)(2,1)S(1)}, bf16[128,1,2,512]{3,2,1,0:T(2,128)(2,1)}, u32[]{:S(2)}) copy-start(bf16[128,1,2,512]{3,2,1,0:T(2,128)(2,1)} %param.11) | copy-start | bytes 786436
  2.6 33.8 %all-to-all-start = ((bf16[8,2,128,256]{3,2,1,0:T(8,128)(2,1)}), bf16[8,2,128,256]{3,2,1,0:T(8,128)(2,1)S(1)}, u32[]{:S(2)}, u32[]{:S(2)}) async-start(bf16[8,2,128,256]{3,2,1,0:T(8,128)(2,1)} %bitcast.13), calls=%async_computation | async-start | bytes 2097152 | tf_op jit(solution)/shard_map/all_to_all | solution.py:581
  7.4 20.0 %collective-permute-start.4 = (bf16[2,4,16,1024]{3,2,1,0:T(8,128)(2,1)S(1)}, bf16[2,4,16,1024]{3,2,1,0:T(8,128)(2,1)S(1)}, u32[]{:S(2)}, u32[]{:S(2)}) collective-permute-start(bf16[2,4,16,1024]{3,2,1,0:T(8,128)(2,1)S(1)} %get-tuple-element.60), channel_id=1, source_target_pairs={{0,2},{1,3},{2,0},{3,1},{4,6},{5,7},{6,4},{7,5},{8,10},{9,11},{10,... | collective-permute-start | bytes 786440 | tf_op jit(solution)/shard_map/ppermute | solution.py:562
  8.3 16.1 %collective-permute-start.2 = (bf16[128,512]{1,0:T(8,128)(2,1)S(1)}, bf16[128,512]{1,0:T(8,128)(2,1)S(1)}, u32[]{:S(2)}, u32[]{:S(2)}) collective-permute-start(bf16[128,512]{1,0:T(8,128)(2,1)S(1)} %bitcast.61), channel_id=1, source_target_pairs={{0,4},{1,5},{2,6},{3,7},{4,0},{5,1},{6,2},{7,3},{8,12},{9,13},{10,... | collective-permute-start | bytes 393224 | tf_op jit(solution)/shard_map/ppermute | solution.py:562
  8.5 18.9 %collective-permute-start.3 = (bf16[128,512]{1,0:T(8,128)(2,1)S(1)}, bf16[128,512]{1,0:T(8,128)(2,1)S(1)}, u32[]{:S(2)}, u32[]{:S(2)}) collective-permute-start(bf16[128,512]{1,0:T(8,128)(2,1)S(1)} %bitcast.57), channel_id=1, source_target_pairs={{0,8},{1,9},{2,10},{3,11},{4,12},{5,13},{6,14},{7,15},{8,0},{9,1},... | collective-permute-start | bytes 393224 | tf_op jit(solution)/shard_map/ppermute | solution.py:562
  10.9 17.4 %collective-permute-start = (bf16[256,512]{1,0:T(8,128)(2,1)}, bf16[256,512]{1,0:T(8,128)(2,1)S(1)}, u32[]{:S(2)}, u32[]{:S(2)}) collective-permute-start(bf16[256,512]{1,0:T(8,128)(2,1)} %bitcast.66), channel_id=1, source_target_pairs={{0,0},{1,1},{2,2},{3,3},{4,8},{5,9},{6,10},{7,11},{8,4},{9,5},{10,... | collective-permute-start | bytes 786440 | tf_op jit(solution)/shard_map/ppermute | solution.py:590
  13.0 20.0 %collective-permute-start.1 = (bf16[256,512]{1,0:T(8,128)(2,1)}, bf16[256,512]{1,0:T(8,128)(2,1)S(1)}, u32[]{:S(2)}, u32[]{:S(2)}) collective-permute-start(bf16[256,512]{1,0:T(8,128)(2,1)} %bitcast.67), channel_id=1, source_target_pairs={{0,8},{1,9},{2,10},{3,11},{4,0},{5,1},{6,2},{7,3},{8,12},{9,13},{1... | collective-permute-start | bytes 786440 | tf_op jit(solution)/shard_map/ppermute | solution.py:590
  27.5 9.0 %collective-permute-start.6 = (bf16[2,4,16,1024]{3,2,1,0:T(8,128)(2,1)S(1)}, bf16[2,4,16,1024]{3,2,1,0:T(8,128)(2,1)S(1)}, u32[]{:S(2)}, u32[]{:S(2)}) collective-permute-start(bf16[2,4,16,1024]{3,2,1,0:T(8,128)(2,1)S(1)} %get-tuple-element.58), channel_id=1, source_target_pairs={{0,4},{1,5},{2,6},{3,7},{4,0},{5,1},{6,2},{7,3},{8,12},{9,13},{10,... | collective-permute-start | bytes 786440 | tf_op jit(solution)/shard_map/ppermute | solution.py:562
  27.6 8.8 %collective-permute-start.5 = (bf16[128,512]{1,0:T(8,128)(2,1)S(1)}, bf16[128,512]{1,0:T(8,128)(2,1)}, u32[]{:S(2)}, u32[]{:S(2)}) collective-permute-start(bf16[128,512]{1,0:T(8,128)(2,1)S(1)} %bitcast.62), channel_id=1, source_target_pairs={{0,12},{1,13},{2,14},{3,15},{4,8},{5,9},{6,10},{7,11},{8,4},{9,5},... | collective-permute-start | bytes 393224 | tf_op jit(solution)/shard_map/ppermute | solution.py:562
  36.5 1.3 copy-start.8
  37.6 11.8 %collective-permute-start.9 = (bf16[4,128,512]{2,1,0:T(8,128)(2,1)S(1)}, bf16[4,128,512]{2,1,0:T(8,128)(2,1)S(1)}, u32[]{:S(2)}, u32[]{:S(2)}) collective-permute-start(bf16[4,128,512]{2,1,0:T(8,128)(2,1)S(1)} %pad_maximum_fusion.2.kv_own), channel_id=1, source_target_pairs={{0,2},{1,3},{2,0},{3,1},{4,6},{5,7},{6,4},{7,5},{8,10},{9,11},{10,... | collective-permute-start | bytes 1572872 | tf_op jit(solution)/shard_map/ppermute | solution.py:562
  37.8 11.6 %collective-permute-start.10 = (bf16[2,2,4,16,1024]{4,3,2,1,0:T(8,128)(2,1)S(1)}, bf16[2,2,4,16,1024]{4,3,2,1,0:T(8,128)(2,1)S(1)}, u32[]{:S(2)}, u32[]{:S(2)}) collective-permute-start(bf16[2,2,4,16,1024]{4,3,2,1,0:T(8,128)(2,1)S(1)} %pad_maximum_fusion.1.refs_0_), channel_id=1, source_target_pairs={{0,16},{16,0},{1,17},{17,1},{2,18},{18,2},{3,19},{19,3},{4,20},{20... | collective-permute-start | bytes 1572872 | tf_op jit(solution)/shard_map/ppermute | solution.py:562
  39.1 21.5 %collective-permute-start.8 = (bf16[512,512]{1,0:T(8,128)(2,1)S(1)}, bf16[512,512]{1,0:T(8,128)(2,1)S(1)}, u32[]{:S(2)}, u32[]{:S(2)}) collective-permute-start(bf16[512,512]{1,0:T(8,128)(2,1)S(1)} %pad_maximum_fusion.page_own), channel_id=1, source_target_pairs={{0,2},{1,3},{2,0},{3,1},{4,6},{5,7},{6,4},{7,5},{8,10},{9,11},{10,... | collective-permute-start | bytes 1572872 | tf_op jit(solution)/shard_map/ppermute | solution.py:562
  40.4 26.8 %collective-permute-start.7 = (bf16[2,2,4,16,1024]{4,3,2,1,0:T(8,128)(2,1)S(1)}, bf16[2,2,4,16,1024]{4,3,2,1,0:T(8,128)(2,1)S(1)}, u32[]{:S(2)}, u32[]{:S(2)}) collective-permute-start(bf16[2,2,4,16,1024]{4,3,2,1,0:T(8,128)(2,1)S(1)} %pad_maximum_fusion.1.refs_0_), channel_id=1, source_target_pairs={{0,8},{1,9},{2,10},{3,11},{4,12},{5,13},{6,14},{7,15},{8,0},{9,1},... | collective-permute-start | bytes 1572872 | tf_op jit(solution)/shard_map/ppermute | solution.py:562
  60.6 8.2 %collective-permute-start.11 = (bf16[512,512]{1,0:T(8,128)(2,1)S(1)}, bf16[512,512]{1,0:T(8,128)(2,1)S(1)}, u32[]{:S(2)}, u32[]{:S(2)}) collective-permute-start(bf16[512,512]{1,0:T(8,128)(2,1)S(1)} %pad_maximum_fusion.page_own), channel_id=1, source_target_pairs={{0,1},{1,0},{2,3},{3,2},{4,5},{5,4},{6,7},{7,6},{8,9},{9,8},{10,11... | collective-permute-start | bytes 1572872 | tf_op jit(solution)/shard_map/ppermute | solution.py:562
  63.2 5.9 %collective-permute-start.12 = (bf16[512,512]{1,0:T(8,128)(2,1)S(1)}, bf16[512,512]{1,0:T(8,128)(2,1)S(1)}, u32[]{:S(2)}, u32[]{:S(2)}) collective-permute-start(bf16[512,512]{1,0:T(8,128)(2,1)S(1)} %collective-permute-done.8.page_y), channel_id=1, source_target_pairs={{0,1},{1,0},{2,3},{3,2},{4,5},{5,4},{6,7},{7,6},{8,9},{9,8},{10,11... | collective-permute-start | bytes 1572872 | tf_op jit(solution)/shard_map/ppermute | solution.py:562
  63.2 6.1 %collective-permute-start.13 = (bf16[4,128,512]{2,1,0:T(8,128)(2,1)S(1)}, bf16[4,128,512]{2,1,0:T(8,128)(2,1)S(1)}, u32[]{:S(2)}, u32[]{:S(2)}) collective-permute-start(bf16[4,128,512]{2,1,0:T(8,128)(2,1)S(1)} %pad_maximum_fusion.2.kv_own), channel_id=1, source_target_pairs={{0,1},{1,0},{2,3},{3,2},{4,5},{5,4},{6,7},{7,6},{8,9},{9,8},{10,11... | collective-permute-start | bytes 1572872 | tf_op jit(solution)/shard_map/ppermute | solution.py:562
  63.7 5.6 %collective-permute-start.14 = (bf16[4,128,512]{2,1,0:T(8,128)(2,1)S(1)}, bf16[4,128,512]{2,1,0:T(8,128)(2,1)S(1)}, u32[]{:S(2)}, u32[]{:S(2)}) collective-permute-start(bf16[4,128,512]{2,1,0:T(8,128)(2,1)S(1)} %collective-permute-done.9.kv_y), channel_id=1, source_target_pairs={{0,1},{1,0},{2,3},{3,2},{4,5},{5,4},{6,7},{7,6},{8,9},{9,8},{10,11... | collective-permute-start | bytes 1572872 | tf_op jit(solution)/shard_map/ppermute | solution.py:562
  67.2 17.6 %collective-permute-start.17 = (bf16[2,2,4,16,1024]{4,3,2,1,0:T(8,128)(2,1)S(1)}, bf16[2,2,4,16,1024]{4,3,2,1,0:T(8,128)(2,1)S(1)}, u32[]{:S(2)}, u32[]{:S(2)}) collective-permute-start(bf16[2,2,4,16,1024]{4,3,2,1,0:T(8,128)(2,1)S(1)} %pad_maximum_fusion.1.refs_0_), channel_id=1, source_target_pairs={{0,1},{1,0},{2,3},{3,2},{4,5},{5,4},{6,7},{7,6},{8,9},{9,8},{10,11... | collective-permute-start | bytes 1572872 | tf_op jit(solution)/shard_map/ppermute | solution.py:562
  68.8 15.1 %collective-permute-start.15 = (bf16[2,2,4,16,1024]{4,3,2,1,0:T(8,128)(2,1)S(1)}, bf16[2,2,4,16,1024]{4,3,2,1,0:T(8,128)(2,1)S(1)}, u32[]{:S(2)}, u32[]{:S(2)}) collective-permute-start(bf16[2,2,4,16,1024]{4,3,2,1,0:T(8,128)(2,1)S(1)} %collective-permute-done.7.refs_4_), channel_id=1, source_target_pairs={{0,16},{16,0},{1,17},{17,1},{2,18},{18,2},{3,19},{19,3},{4,20},{20... | collective-permute-start | bytes 1572872 | tf_op jit(solution)/shard_map/ppermute | solution.py:562
  69.1 15.7 %collective-permute-start.19 = (bf16[2,2,4,16,1024]{4,3,2,1,0:T(8,128)(2,1)S(1)}, bf16[2,2,4,16,1024]{4,3,2,1,0:T(8,128)(2,1)S(1)}, u32[]{:S(2)}, u32[]{:S(2)}) collective-permute-start(bf16[2,2,4,16,1024]{4,3,2,1,0:T(8,128)(2,1)S(1)} %collective-permute-done.7.refs_4_), channel_id=1, source_target_pairs={{0,1},{1,0},{2,3},{3,2},{4,5},{5,4},{6,7},{7,6},{8,9},{9,8},{10,11... | collective-permute-start | bytes 1572872 | tf_op jit(solution)/shard_map/ppermute | solution.py:562
  83.9 13.4 %copy-start.9 = (s32[128,1,2]{0,2,1:T(2,128)S(1)}, s32[128,1,2]{0,2,1:T(2,128)}, u32[]{:S(2)}) copy-start(s32[128,1,2]{0,2,1:T(2,128)} %param.16) | copy-start | bytes 3076
  83.9 36.0 %copy-start.3 = (bf16[128,1,2048]{2,0,1:T(8,128)(2,1)S(1)}, bf16[128,1,2048]{2,0,1:T(8,128)(2,1)}, u32[]{:S(2)}) copy-start(bf16[128,1,2048]{2,0,1:T(8,128)(2,1)} %param.13) | copy-start | bytes 1572868
  83.9 36.0 %copy-start.5 = (f32[2048]{0:T(1024)S(1)}, f32[2048]{0:T(1024)}, u32[]{:S(2)}) copy-start(f32[2048]{0:T(1024)} %param.15) | copy-start | bytes 24580
  84.0 2.0 collective-permute-start.18
  84.2 2.4 %collective-permute-start.20 = (bf16[2,2,4,16,1024]{4,3,2,1,0:T(8,128)(2,1)S(1)}, bf16[2,2,4,16,1024]{4,3,2,1,0:T(8,128)(2,1)S(1)}, u32[]{:S(2)}, u32[]{:S(2)}) collective-permute-start(bf16[2,2,4,16,1024]{4,3,2,1,0:T(8,128)(2,1)S(1)} %collective-permute-done.15.refs_6_), channel_id=1, source_target_pairs={{0,1},{1,0},{2,3},{3,2},{4,5},{5,4},{6,7},{7,6},{8,9},{9,8},{10,11... | collective-permute-start | bytes 1572872 | tf_op jit(solution)/shard_map/ppermute | solution.py:562
  84.5 2.9 %collective-permute-start.16 = (bf16[512,512]{1,0:T(8,128)(2,1)S(1)}, bf16[512,512]{1,0:T(8,128)(2,1)S(1)}, u32[]{:S(2)}, u32[]{:S(2)}) collective-permute-start(bf16[512,512]{1,0:T(8,128)(2,1)S(1)} %slice_bitcast_fusion), channel_id=1, source_target_pairs={{0,1},{1,0},{2,3},{3,2},{4,5},{5,4},{6,7},{7,6},{8,9},{9,8},{10,11... | collective-permute-start | bytes 1572872 | tf_op jit(solution)/shard_map/ppermute | solution.py:562
  92.0 16.3 %collective-permute-start.21 = (bf16[128,2048]{1,0:T(8,128)(2,1)}, bf16[128,2048]{1,0:T(8,128)(2,1)S(1)}, u32[]{:S(2)}, u32[]{:S(2)}) collective-permute-start(bf16[128,2048]{1,0:T(8,128)(2,1)} %get-tuple-element.52), channel_id=1, source_target_pairs={{0,6},{1,7},{2,4},{3,5},{4,2},{5,3},{6,0},{7,1},{8,14},{9,15},{10,... | collective-permute-start | bytes 1572872 | tf_op jit(solution)/shard_map/ppermute | solution.py:562
  96.1 23.5 %collective-permute-start.22 = (bf16[128,2048]{1,0:T(8,128)(2,1)}, bf16[128,2048]{1,0:T(8,128)(2,1)S(1)}, u32[]{:S(2)}, u32[]{:S(2)}) collective-permute-start(bf16[128,2048]{1,0:T(8,128)(2,1)} %get-tuple-element.53), channel_id=1, source_target_pairs={{0,4},{1,5},{2,6},{3,7},{4,0},{5,1},{6,2},{7,3},{8,12},{9,13},{10,... | collective-permute-start | bytes 1572872 | tf_op jit(solution)/shard_map/ppermute | solution.py:562
  96.1 23.7 %collective-permute-start.23 = (bf16[128,2048]{1,0:T(8,128)(2,1)}, bf16[128,2048]{1,0:T(8,128)(2,1)S(1)}, u32[]{:S(2)}, u32[]{:S(2)}) collective-permute-start(bf16[128,2048]{1,0:T(8,128)(2,1)} %get-tuple-element.54), channel_id=1, source_target_pairs={{0,2},{1,3},{2,0},{3,1},{4,6},{5,7},{6,4},{7,5},{8,10},{9,11},{10,... | collective-permute-start | bytes 1572872 | tf_op jit(solution)/shard_map/ppermute | solution.py:562
  119.9 1.0 copy-start.4
  122.1 53.0 %copy-start.1 = (f32[128,2048]{1,0:T(8,128)}, f32[128,2048]{1,0:T(8,128)S(1)}, u32[]{:S(2)}) copy-start(f32[128,2048]{1,0:T(8,128)S(1)} %get-tuple-element.56.stream_hbm) | copy-start | bytes 3145732
  122.1 53.0 %copy-start.6 = (bf16[1,512,2048]{2,1,0:T(8,128)(2,1)S(1)}, bf16[1,512,2048]{2,1,0:T(8,128)(2,1)}, u32[]{:S(2)}) copy-start(bf16[1,512,2048]{2,1,0:T(8,128)(2,1)} %param.19) | copy-start | bytes 6291460
  182.0 5.2 %copy-start.10 = (f32[128,1,2]{0,2,1:T(2,128)S(1)}, f32[128,1,2]{0,2,1:T(2,128)}, u32[]{:S(2)}) copy-start(f32[128,1,2]{0,2,1:T(2,128)} %param.17) | copy-start | bytes 3076
  182.0 52.6 %all-to-all-start.2 = ((bf16[16,32,2048]{2,1,0:T(8,128)(2,1)}), bf16[16,32,2048]{2,1,0:T(8,128)(2,1)S(1)}, u32[]{:S(2)}, u32[]{:S(2)}) async-start(bf16[16,32,2048]{2,1,0:T(8,128)(2,1)} %bitcast.53), calls=%async_computation.2 | async-start | bytes 4194304 | tf_op jit(solution)/shard_map/all_to_all | solution.py:754
  234.5 1.2 copy-start.2

commit v21 on v20

--- a/solution.py
+++ b/solution.py
@@ -578,9 +578,6 @@
 
     query_slots = queries.reshape(local_rows, heads, width).transpose(1, 0, 2)
     query_slots = query_slots.reshape(members, heads // members, local_rows, width)
-    q = lax.all_to_all(
-        query_slots, "head", split_axis=0, concat_axis=0, tiled=True, axis_index_groups=group_sets
-    )
 
     def page_target(source, other):
         p, plane, rest = source // members, (source // plane_bit) % 2, source % plane_bit
@@ -603,14 +600,19 @@
         kv_own.append(flipped(kv_other if t % 2 else kv_same, "head", t * plane_bit))
     w_got = flipped(w_give, "head", 2)
 
-    kv_own[1], kv_own[2], w_got = lax.optimization_barrier((kv_own[1], kv_own[2], w_got))
+    kv_own[1], kv_own[2], w_got, query_slots = lax.optimization_barrier(
+        (kv_own[1], kv_own[2], w_got, query_slots)
+    )
+    q = lax.all_to_all(
+        query_slots, "head", split_axis=0, concat_axis=0, tiled=True, axis_index_groups=group_sets
+    )
     w_both = jnp.stack([w_keep, w_got], 1)
     w_same = lax.dynamic_index_in_dim(w_both, b, 0, keepdims=False)
     w_other = lax.dynamic_index_in_dim(w_both, 1 - b, 0, keepdims=False)
     w_first = flipped(w_other, "head", plane_bit)
 
     own_pages = jnp.concatenate([page_a, page_b], 0)
-    own_pages, kv_own, w_first, q = lax.optimization_barrier((own_pages, kv_own, w_first, q))
+    own_pages, kv_own, w_first = lax.optimization_barrier((own_pages, kv_own, w_first))
     kv_own = jnp.stack(kv_own, 0)
     pages_y = flipped(own_pages, "head", 2)
     kv_y = flipped(kv_own, "head", 2)

time: 238 us -> 244 us (1.025)
  starting transfers between devices: 35.5 us -> 39.8 us
  blocking collectives: 52.9 us -> 55.6 us
    ppermute x22, waiting for transfers between devices: 60.1 us -> 51.3 us  [flipped(): return lax.ppermute(value, axis, pairs)]
    ppermute x2, waiting for transfers between devices: 4.78 us -> 13 us  [parts_in_pairs(): lax.ppermute(cache[0], 'head', [(d, page_target(d, other)) for d in range...]
    all_to_all x1, starting transfers between devices: 4.64 us -> 8.67 us  [parts_in_pairs(): lax.all_to_all(query_slots, 'head', split_axis=0, concat_axis=0, tiled=Tr...]
    all_to_all x1, blocking collectives: 52.9 us -> 55.6 us  [local(): lax.all_to_all(outgoing.reshape(n, slots // n, model), 'head', split_axis...]
  transfers between devices with their start and end apart: 26 -> 26, of which waited for: 15 -> 15; matrix products, arithmetic and copies ran while one was open for 1% -> 2% of each run, Pallas kernels for 6% -> 6%
where the time goes in v21:
time: 244 us
  waiting for transfers between devices  112 us (46%)
  blocking collectives  55.6 us (23%)
  starting transfers between devices  39.8 us (16%)
  Pallas kernels  28.7 us (12%)
  local copies, waits for them, and re-layouts  6.13 us (3%)
    all_to_all x1, blocking collectives, local(): lax.all_to_all(outgoing.reshape(n, slots // n, model), 'head', split_axis...  55.6 us
    ppermute x22, waiting for transfers between devices, flipped(): return lax.ppermute(value, axis, pairs)  51.3 us
    all_to_all x1, waiting for transfers between devices, local(): lax.all_to_all(answered, 'head', split_axis=0, concat_axis=0, tiled=True)  47.3 us
    ppermute x22, starting transfers between devices, flipped(): return lax.ppermute(value, axis, pairs)  24 us
    pallas_call x1, Pallas kernels, attend_pair(): pl.pallas_call(functools.partial(attend_pair_kernel, block, chunk, width)...  13.8 us
    ppermute x2, waiting for transfers between devices, parts_in_pairs(): lax.ppermute(cache[0], 'head', [(d, page_target(d, other)) for d in range...  13 us
    all_to_all x1, starting transfers between devices, parts_in_pairs(): lax.all_to_all(query_slots, 'head', split_axis=0, concat_axis=0, tiled=Tr...  8.67 us
    pallas_call x1, Pallas kernels, expert_pair(): pl.pallas_call(kernel, out_shape=pltpu.HBM((rows, model), BF16), in_specs...  6.88 us
  transfers between devices with their start and end apart: 26, of which 15 were waited for; matrix products, arithmetic and copies ran while one was open for 2% of the time, Pallas kernels for 6%

profile of v21, /device:TPU:13, one launch (start us, length us, event | category | flops | bytes accessed | tf_op | source)
XLA Modules:
  0.0 243.6 jit_solution(1033005485396988235)
XLA Ops:
  0.1 1.2 copy-done
  1.3 0.3 collective-permute-start.2
  1.6 0.5 constant_dynamic-slice_fusion.2
  2.3 2.5 %collective-permute-start.1 = (bf16[128,512]{1,0:T(8,128)(2,1)S(1)}, bf16[128,512]{1,0:T(8,128)(2,1)S(1)}, u32[]{:S(2)}, u32[]{:S(2)}) collective-permute-start(bf16[128,512]{1,0:T(8,128)(2,1)S(1)} %bitcast.57), channel_id=1, source_target_pairs={{0,8},{1,9},{2,10},{3,11},{4,12},{5,13},{6,14},{7,15},{8,0},{9,1},... | collective-permute-start | bytes 393224 | tf_op jit(solution)/shard_map/ppermute | solution.py:562
  4.8 1.3 copy.29
  6.2 0.2 collective-permute-done
  6.4 3.5 %collective-permute-done.1 = bf16[128,512]{1,0:T(8,128)(2,1)S(1)} collective-permute-done((bf16[128,512]{1,0:T(8,128)(2,1)S(1)}, bf16[128,512]{1,0:T(8,128)(2,1)S(1)}, u32[]{:S(2)}, u32[]{:S(2)}) %collective-permute-start.1) | collective-permute-done | bytes 131104 | tf_op jit(solution)/shard_map/ppermute | solution.py:562
  9.9 8.7 %all-to-all-start = ((bf16[8,2,128,256]{3,2,1,0:T(8,128)(2,1)}), bf16[8,2,128,256]{3,2,1,0:T(8,128)(2,1)}, u32[]{:S(2)}, u32[]{:S(2)}) async-start(bf16[8,2,128,256]{3,2,1,0:T(8,128)(2,1)} %bitcast.10), calls=%async_computation | async-start | bytes 2097152 | tf_op jit(solution)/shard_map/all_to_all | solution.py:606
  18.5 1.9 collective-permute-start.3
  20.6 2.7 %collective-permute-start.6 = (bf16[2,4,16,1024]{3,2,1,0:T(8,128)(2,1)S(1)}, bf16[2,4,16,1024]{3,2,1,0:T(8,128)(2,1)S(1)}, u32[]{:S(2)}, u32[]{:S(2)}) collective-permute-start(bf16[2,4,16,1024]{3,2,1,0:T(8,128)(2,1)S(1)} %get-tuple-element.58), channel_id=1, source_target_pairs={{0,4},{1,5},{2,6},{3,7},{4,0},{5,1},{6,2},{7,3},{8,12},{9,13},{10,... | collective-permute-start | bytes 786440 | tf_op jit(solution)/shard_map/ppermute | solution.py:562
  23.3 4.8 %collective-permute-done.3 = bf16[256,512]{1,0:T(8,128)(2,1)S(1)} collective-permute-done((bf16[256,512]{1,0:T(8,128)(2,1)S(1)}, bf16[256,512]{1,0:T(8,128)(2,1)S(1)}, u32[]{:S(2)}, u32[]{:S(2)}) %collective-permute-start.3) | collective-permute-done | bytes 262176 | tf_op jit(solution)/shard_map/ppermute | solution.py:587
  28.0 8.2 %collective-permute-done.4 = bf16[256,512]{1,0:T(8,128)(2,1)S(1)} collective-permute-done((bf16[256,512]{1,0:T(8,128)(2,1)S(1)}, bf16[256,512]{1,0:T(8,128)(2,1)S(1)}, u32[]{:S(2)}, u32[]{:S(2)}) %collective-permute-start.4) | collective-permute-done | bytes 262176 | tf_op jit(solution)/shard_map/ppermute | solution.py:587
  36.3 5.9 %collective-permute-done.6 = bf16[2,4,16,1024]{3,2,1,0:T(8,128)(2,1)S(1)} collective-permute-done((bf16[2,4,16,1024]{3,2,1,0:T(8,128)(2,1)S(1)}, bf16[2,4,16,1024]{3,2,1,0:T(8,128)(2,1)S(1)}, u32[]{:S(2)}, u32[]{:S(2)}) %collective-permute-start.6) | collective-permute-done | bytes 262176 | tf_op jit(solution)/shard_map/ppermute | solution.py:562
  42.2 1.0 pad_maximum_fusion.2.kv_own
  43.2 0.4 collective-permute-start.9
  43.7 1.3 collective-permute-start.10
  44.9 1.1 collective-permute-start.8
  46.0 4.9 %collective-permute-start.7 = (bf16[2,2,4,16,1024]{4,3,2,1,0:T(8,128)(2,1)S(1)}, bf16[2,2,4,16,1024]{4,3,2,1,0:T(8,128)(2,1)}, u32[]{:S(2)}, u32[]{:S(2)}) collective-permute-start(bf16[2,2,4,16,1024]{4,3,2,1,0:T(8,128)(2,1)S(1)} %pad_maximum_fusion.1.refs_0_), channel_id=1, source_target_pairs={{0,8},{1,9},{2,10},{3,11},{4,12},{5,13},{6,14},{7,15},{8,0},{9,1},... | collective-permute-start | bytes 1572872 | tf_op jit(solution)/shard_map/ppermute | solution.py:562
  50.9 3.1 %collective-permute-done.9.kv_y = bf16[4,128,512]{2,1,0:T(8,128)(2,1)} collective-permute-done((bf16[4,128,512]{2,1,0:T(8,128)(2,1)S(1)}, bf16[4,128,512]{2,1,0:T(8,128)(2,1)}, u32[]{:S(2)}, u32[]{:S(2)}) %collective-permute-start.9) | collective-permute-done | bytes 524320 | tf_op jit(solution)/shard_map/ppermute | solution.py:562
  54.1 0.3 collective-permute-done.10.refs_2_
  54.4 10.9 %collective-permute-done.8.page_y = bf16[512,512]{1,0:T(8,128)(2,1)} collective-permute-done((bf16[512,512]{1,0:T(8,128)(2,1)S(1)}, bf16[512,512]{1,0:T(8,128)(2,1)}, u32[]{:S(2)}, u32[]{:S(2)}) %collective-permute-start.8) | collective-permute-done | bytes 524320 | tf_op jit(solution)/shard_map/ppermute | solution.py:562
  65.3 3.6 %collective-permute-start.11 = (bf16[512,512]{1,0:T(8,128)(2,1)S(1)}, bf16[512,512]{1,0:T(8,128)(2,1)}, u32[]{:S(2)}, u32[]{:S(2)}) collective-permute-start(bf16[512,512]{1,0:T(8,128)(2,1)S(1)} %pad_maximum_fusion.page_own), channel_id=1, source_target_pairs={{0,1},{1,0},{2,3},{3,2},{4,5},{5,4},{6,7},{7,6},{8,9},{9,8},{10,11... | collective-permute-start | bytes 1572872 | tf_op jit(solution)/shard_map/ppermute | solution.py:562
  68.9 0.5 collective-permute-start.13
  69.5 2.9 %collective-permute-done.7.refs_4_ = bf16[2,2,4,16,1024]{4,3,2,1,0:T(8,128)(2,1)} collective-permute-done((bf16[2,2,4,16,1024]{4,3,2,1,0:T(8,128)(2,1)S(1)}, bf16[2,2,4,16,1024]{4,3,2,1,0:T(8,128)(2,1)}, u32[]{:S(2)}, u32[]{:S(2)}) %collective-permute-start.7) | collective-permute-done | bytes 524320 | tf_op jit(solution)/shard_map/ppermute | solution.py:562
  72.3 0.5 collective-permute-start.17
  72.8 0.3 collective-permute-start.15
  73.1 0.4 collective-permute-start.19
  73.4 13.8 %attend.1.a_hbm = bf16[2,512,512]{2,1,0:T(8,128)(2,1)S(1)} custom-call(bf16[8,2,128,256]{3,2,1,0:T(8,128)(2,1)} %all-to-all-done.q_hbm, bf16[512,512]{1,0:T(8,128)(2,1)S(1)} %pad_maximum_fusion.page_own, bf16[512,512]{1,0:T(8,128)(2,1)} %collective-permute-done.8.page_y, bf16[512,512]{1,0:T(8,128)(2,1)} %collective-permute-done.11.page_c, ...), custom_call_target="tpu_custom_call" | custom-call | flops 7516192768 | bytes 6291456 | tf_op jit(solution)/shard_map/attend/pallas_call | solution.py:259
  87.4 0.2 collective-permute-start.16
  87.6 0.4 collective-permute-start.18
  88.1 1.2 collective-permute-done.16.got_hbm
  89.4 0.7 collective-permute-done.18.refs_3_
  90.1 0.7 collective-permute-done.20.refs_7_
  90.8 5.1 %project.1 = (bf16[128,2048]{1,0:T(8,128)(2,1)}, bf16[128,2048]{1,0:T(8,128)(2,1)}, bf16[128,2048]{1,0:T(8,128)(2,1)}, bf16[128,2048]{1,0:T(8,128)(2,1)}) custom-call(bf16[2,512,512]{2,1,0:T(8,128)(2,1)S(1)} %attend.1.a_hbm, bf16[512,512]{1,0:T(8,128)(2,1)S(1)} %collective-permute-done.16.got_hbm, ...), custom_call_target="tpu_custom_call" | custom-call | flops 2147483648 | bytes 7340032 | tf_op jit(solution)/shard_map/project/pallas_call | solution.py:340
  96.0 3.3 %collective-permute-start.21 = (bf16[128,2048]{1,0:T(8,128)(2,1)}, bf16[128,2048]{1,0:T(8,128)(2,1)S(1)}, u32[]{:S(2)}, u32[]{:S(2)}) collective-permute-start(bf16[128,2048]{1,0:T(8,128)(2,1)} %get-tuple-element.52), channel_id=1, source_target_pairs={{0,6},{1,7},{2,4},{3,5},{4,2},{5,3},{6,0},{7,1},{8,14},{9,15},{10,... | collective-permute-start | bytes 1572872 | tf_op jit(solution)/shard_map/ppermute | solution.py:562
  99.3 0.3 collective-permute-start.22
  99.6 1.1 collective-permute-start.23
  101.0 0.2 reduce_window_sum.11
  101.5 10.2 %collective-permute-done.21 = bf16[128,2048]{1,0:T(8,128)(2,1)S(1)} collective-permute-done((bf16[128,2048]{1,0:T(8,128)(2,1)}, bf16[128,2048]{1,0:T(8,128)(2,1)S(1)}, u32[]{:S(2)}, u32[]{:S(2)}) %collective-permute-start.21) | collective-permute-done | bytes 524320 | tf_op jit(solution)/shard_map/ppermute | solution.py:562
  111.7 11.6 %collective-permute-done.22 = bf16[128,2048]{1,0:T(8,128)(2,1)S(1)} collective-permute-done((bf16[128,2048]{1,0:T(8,128)(2,1)}, bf16[128,2048]{1,0:T(8,128)(2,1)S(1)}, u32[]{:S(2)}, u32[]{:S(2)}) %collective-permute-start.22) | collective-permute-done | bytes 524320 | tf_op jit(solution)/shard_map/ppermute | solution.py:562
  123.3 1.0 copy-done.4
  124.3 1.1 route.1
  125.5 55.6 %all_to_all.15 = bf16[16,32,2048]{2,1,0:T(8,128)(2,1)S(1)} all-to-all(bf16[16,32,2048]{2,1,0:T(8,128)(2,1)S(1)} %bitcast.42), channel_id=1, replica_groups=mesh['grp'=2,'head'=16] {'head'}, dimensions={0} | all-to-all | bytes 4194304 | tf_op jit(solution)/shard_map/all_to_all | solution.py:743
  181.0 6.9 %expert.1 = bf16[512,2048]{1,0:T(8,128)(2,1)} custom-call(bf16[512,2048]{1,0:T(8,128)(2,1)S(1)} %bitcast.43, bf16[2048,1024]{1,0:T(8,128)(2,1)} %bitcast.66, bf16[512,2048]{1,0:T(8,128)(2,1)S(1)} %bitcast.52), custom_call_target="tpu_custom_call" | custom-call | flops 3221225472 | bytes 10485760 | tf_op jit(solution)/shard_map/expert/pallas_call | solution.py:497
  187.9 5.1 %all-to-all-start.2 = ((bf16[16,32,2048]{2,1,0:T(8,128)(2,1)}), bf16[16,32,2048]{2,1,0:T(8,128)(2,1)S(1)}, u32[]{:S(2)}, u32[]{:S(2)}) async-start(bf16[16,32,2048]{2,1,0:T(8,128)(2,1)} %bitcast.53), calls=%async_computation.2 | async-start | bytes 4194304 | tf_op jit(solution)/shard_map/all_to_all | solution.py:756
  193.2 47.3 %all-to-all-done.2 = bf16[16,32,2048]{2,1,0:T(8,128)(2,1)S(1)} async-done(((bf16[16,32,2048]{2,1,0:T(8,128)(2,1)}), bf16[16,32,2048]{2,1,0:T(8,128)(2,1)S(1)}, u32[]{:S(2)}, u32[]{:S(2)}) %all-to-all-start.2) | async-done | bytes 2097184 | tf_op jit(solution)/shard_map/all_to_all | solution.py:756
  240.5 1.2 copy-done.2
  241.7 1.7 combine.1
  (59 shorter events, 1.4 us)
Async XLA Ops:
  0.0 1.2 copy-start
  0.0 1.6 copy-start.7
  0.0 4.8 %copy-start.8 = (bf16[128,1,16,256]{3,2,1,0:T(8,128)(2,1)S(1)}, bf16[128,1,16,256]{3,2,1,0:T(8,128)(2,1)}, u32[]{:S(2)}) copy-start(bf16[128,1,16,256]{3,2,1,0:T(8,128)(2,1)} %param.10) | copy-start | bytes 3145732
  1.3 8.5 %collective-permute-start.2 = (bf16[2,4,16,1024]{3,2,1,0:T(8,128)(2,1)S(1)}, bf16[2,4,16,1024]{3,2,1,0:T(8,128)(2,1)S(1)}, u32[]{:S(2)}, u32[]{:S(2)}) collective-permute-start(bf16[2,4,16,1024]{3,2,1,0:T(8,128)(2,1)S(1)} %get-tuple-element.60), channel_id=1, source_target_pairs={{0,2},{1,3},{2,0},{3,1},{4,6},{5,7},{6,4},{7,5},{8,10},{9,11},{10,... | collective-permute-start | bytes 786440 | tf_op jit(solution)/shard_map/ppermute | solution.py:562
  2.2 4.2 %collective-permute-start = (bf16[128,512]{1,0:T(8,128)(2,1)S(1)}, bf16[128,512]{1,0:T(8,128)(2,1)S(1)}, u32[]{:S(2)}, u32[]{:S(2)}) collective-permute-start(bf16[128,512]{1,0:T(8,128)(2,1)S(1)} %bitcast.61), channel_id=1, source_target_pairs={{0,4},{1,5},{2,6},{3,7},{4,0},{5,1},{6,2},{7,3},{8,12},{9,13},{10,... | collective-permute-start | bytes 393224 | tf_op jit(solution)/shard_map/ppermute | solution.py:562
  2.3 7.5 %collective-permute-start.1 = (bf16[128,512]{1,0:T(8,128)(2,1)S(1)}, bf16[128,512]{1,0:T(8,128)(2,1)S(1)}, u32[]{:S(2)}, u32[]{:S(2)}) collective-permute-start(bf16[128,512]{1,0:T(8,128)(2,1)S(1)} %bitcast.57), channel_id=1, source_target_pairs={{0,8},{1,9},{2,10},{3,11},{4,12},{5,13},{6,14},{7,15},{8,0},{9,1},... | collective-permute-start | bytes 393224 | tf_op jit(solution)/shard_map/ppermute | solution.py:562
  6.1 12.4 %copy-start.12 = (bf16[1,256,512]{2,1,0:T(8,128)(2,1)S(1)}, bf16[1,256,512]{2,1,0:T(8,128)(2,1)}, u32[]{:S(2)}) copy-start(bf16[1,256,512]{2,1,0:T(8,128)(2,1)} %param.12) | copy-start | bytes 786436
  9.8 18.2 %copy-start.9 = (bf16[128,512]{1,0:T(8,128)(2,1)}, bf16[128,512]{1,0:T(8,128)(2,1)S(1)}, u32[]{:S(2)}) copy-start(bf16[128,512]{1,0:T(8,128)(2,1)S(1)} %collective-permute-done.1) | copy-start | bytes 393220
  9.9 63.0 %all-to-all-start = ((bf16[8,2,128,256]{3,2,1,0:T(8,128)(2,1)}), bf16[8,2,128,256]{3,2,1,0:T(8,128)(2,1)}, u32[]{:S(2)}, u32[]{:S(2)}) async-start(bf16[8,2,128,256]{3,2,1,0:T(8,128)(2,1)} %bitcast.10), calls=%async_computation | async-start | bytes 2097152 | tf_op jit(solution)/shard_map/all_to_all | solution.py:606
  18.5 9.5 %collective-permute-start.3 = (bf16[256,512]{1,0:T(8,128)(2,1)S(1)}, bf16[256,512]{1,0:T(8,128)(2,1)S(1)}, u32[]{:S(2)}, u32[]{:S(2)}) collective-permute-start(bf16[256,512]{1,0:T(8,128)(2,1)S(1)} %bitcast.67), channel_id=1, source_target_pairs={{0,0},{1,1},{2,2},{3,3},{4,8},{5,9},{6,10},{7,11},{8,4},{9,5},{10,... | collective-permute-start | bytes 786440 | tf_op jit(solution)/shard_map/ppermute | solution.py:587
  20.4 15.8 %collective-permute-start.4 = (bf16[256,512]{1,0:T(8,128)(2,1)S(1)}, bf16[256,512]{1,0:T(8,128)(2,1)S(1)}, u32[]{:S(2)}, u32[]{:S(2)}) collective-permute-start(bf16[256,512]{1,0:T(8,128)(2,1)S(1)} %bitcast.68), channel_id=1, source_target_pairs={{0,8},{1,9},{2,10},{3,11},{4,0},{5,1},{6,2},{7,3},{8,12},{9,13},{1... | collective-permute-start | bytes 786440 | tf_op jit(solution)/shard_map/ppermute | solution.py:587
  20.6 21.7 %collective-permute-start.6 = (bf16[2,4,16,1024]{3,2,1,0:T(8,128)(2,1)S(1)}, bf16[2,4,16,1024]{3,2,1,0:T(8,128)(2,1)S(1)}, u32[]{:S(2)}, u32[]{:S(2)}) collective-permute-start(bf16[2,4,16,1024]{3,2,1,0:T(8,128)(2,1)S(1)} %get-tuple-element.58), channel_id=1, source_target_pairs={{0,4},{1,5},{2,6},{3,7},{4,0},{5,1},{6,2},{7,3},{8,12},{9,13},{10,... | collective-permute-start | bytes 786440 | tf_op jit(solution)/shard_map/ppermute | solution.py:562
  23.2 13.1 %collective-permute-start.5 = (bf16[128,512]{1,0:T(8,128)(2,1)S(1)}, bf16[128,512]{1,0:T(8,128)(2,1)S(1)}, u32[]{:S(2)}, u32[]{:S(2)}) collective-permute-start(bf16[128,512]{1,0:T(8,128)(2,1)S(1)} %bitcast.62), channel_id=1, source_target_pairs={{0,12},{1,13},{2,14},{3,15},{4,8},{5,9},{6,10},{7,11},{8,4},{9,5},... | collective-permute-start | bytes 393224 | tf_op jit(solution)/shard_map/ppermute | solution.py:562
  43.2 10.9 %collective-permute-start.9 = (bf16[4,128,512]{2,1,0:T(8,128)(2,1)S(1)}, bf16[4,128,512]{2,1,0:T(8,128)(2,1)}, u32[]{:S(2)}, u32[]{:S(2)}) collective-permute-start(bf16[4,128,512]{2,1,0:T(8,128)(2,1)S(1)} %pad_maximum_fusion.2.kv_own), channel_id=1, source_target_pairs={{0,2},{1,3},{2,0},{3,1},{4,6},{5,7},{6,4},{7,5},{8,10},{9,11},{10,... | collective-permute-start | bytes 1572872 | tf_op jit(solution)/shard_map/ppermute | solution.py:562
  43.7 10.7 %collective-permute-start.10 = (bf16[2,2,4,16,1024]{4,3,2,1,0:T(8,128)(2,1)S(1)}, bf16[2,2,4,16,1024]{4,3,2,1,0:T(8,128)(2,1)S(1)}, u32[]{:S(2)}, u32[]{:S(2)}) collective-permute-start(bf16[2,2,4,16,1024]{4,3,2,1,0:T(8,128)(2,1)S(1)} %pad_maximum_fusion.1.refs_0_), channel_id=1, source_target_pairs={{0,16},{16,0},{1,17},{17,1},{2,18},{18,2},{3,19},{19,3},{4,20},{20... | collective-permute-start | bytes 1572872 | tf_op jit(solution)/shard_map/ppermute | solution.py:562
  44.9 20.3 %collective-permute-start.8 = (bf16[512,512]{1,0:T(8,128)(2,1)S(1)}, bf16[512,512]{1,0:T(8,128)(2,1)}, u32[]{:S(2)}, u32[]{:S(2)}) collective-permute-start(bf16[512,512]{1,0:T(8,128)(2,1)S(1)} %pad_maximum_fusion.page_own), channel_id=1, source_target_pairs={{0,2},{1,3},{2,0},{3,1},{4,6},{5,7},{6,4},{7,5},{8,10},{9,11},{10,... | collective-permute-start | bytes 1572872 | tf_op jit(solution)/shard_map/ppermute | solution.py:562
  46.0 26.3 %collective-permute-start.7 = (bf16[2,2,4,16,1024]{4,3,2,1,0:T(8,128)(2,1)S(1)}, bf16[2,2,4,16,1024]{4,3,2,1,0:T(8,128)(2,1)}, u32[]{:S(2)}, u32[]{:S(2)}) collective-permute-start(bf16[2,2,4,16,1024]{4,3,2,1,0:T(8,128)(2,1)S(1)} %pad_maximum_fusion.1.refs_0_), channel_id=1, source_target_pairs={{0,8},{1,9},{2,10},{3,11},{4,12},{5,13},{6,14},{7,15},{8,0},{9,1},... | collective-permute-start | bytes 1572872 | tf_op jit(solution)/shard_map/ppermute | solution.py:562
  65.3 7.5 %collective-permute-start.11 = (bf16[512,512]{1,0:T(8,128)(2,1)S(1)}, bf16[512,512]{1,0:T(8,128)(2,1)}, u32[]{:S(2)}, u32[]{:S(2)}) collective-permute-start(bf16[512,512]{1,0:T(8,128)(2,1)S(1)} %pad_maximum_fusion.page_own), channel_id=1, source_target_pairs={{0,1},{1,0},{2,3},{3,2},{4,5},{5,4},{6,7},{7,6},{8,9},{9,8},{10,11... | collective-permute-start | bytes 1572872 | tf_op jit(solution)/shard_map/ppermute | solution.py:562
  68.9 4.1 %collective-permute-start.12 = (bf16[512,512]{1,0:T(8,128)(2,1)}, bf16[512,512]{1,0:T(8,128)(2,1)}, u32[]{:S(2)}, u32[]{:S(2)}) collective-permute-start(bf16[512,512]{1,0:T(8,128)(2,1)} %collective-permute-done.8.page_y), channel_id=1, source_target_pairs={{0,1},{1,0},{2,3},{3,2},{4,5},{5,4},{6,7},{7,6},{8,9},{9,8},{10,11... | collective-permute-start | bytes 1572872 | tf_op jit(solution)/shard_map/ppermute | solution.py:562
  68.9 4.5 %collective-permute-start.13 = (bf16[4,128,512]{2,1,0:T(8,128)(2,1)S(1)}, bf16[4,128,512]{2,1,0:T(8,128)(2,1)}, u32[]{:S(2)}, u32[]{:S(2)}) collective-permute-start(bf16[4,128,512]{2,1,0:T(8,128)(2,1)S(1)} %pad_maximum_fusion.2.kv_own), channel_id=1, source_target_pairs={{0,1},{1,0},{2,3},{3,2},{4,5},{5,4},{6,7},{7,6},{8,9},{9,8},{10,11... | collective-permute-start | bytes 1572872 | tf_op jit(solution)/shard_map/ppermute | solution.py:562
  69.5 4.0 %collective-permute-start.14 = (bf16[4,128,512]{2,1,0:T(8,128)(2,1)}, bf16[4,128,512]{2,1,0:T(8,128)(2,1)}, u32[]{:S(2)}, u32[]{:S(2)}) collective-permute-start(bf16[4,128,512]{2,1,0:T(8,128)(2,1)} %collective-permute-done.9.kv_y), channel_id=1, source_target_pairs={{0,1},{1,0},{2,3},{3,2},{4,5},{5,4},{6,7},{7,6},{8,9},{9,8},{10,11... | collective-permute-start | bytes 1572872 | tf_op jit(solution)/shard_map/ppermute | solution.py:562
  72.3 15.8 %collective-permute-start.17 = (bf16[2,2,4,16,1024]{4,3,2,1,0:T(8,128)(2,1)S(1)}, bf16[2,2,4,16,1024]{4,3,2,1,0:T(8,128)(2,1)}, u32[]{:S(2)}, u32[]{:S(2)}) collective-permute-start(bf16[2,2,4,16,1024]{4,3,2,1,0:T(8,128)(2,1)S(1)} %pad_maximum_fusion.1.refs_0_), channel_id=1, source_target_pairs={{0,1},{1,0},{2,3},{3,2},{4,5},{5,4},{6,7},{7,6},{8,9},{9,8},{10,11... | collective-permute-start | bytes 1572872 | tf_op jit(solution)/shard_map/ppermute | solution.py:562
  72.8 14.8 %collective-permute-start.15 = (bf16[2,2,4,16,1024]{4,3,2,1,0:T(8,128)(2,1)}, bf16[2,2,4,16,1024]{4,3,2,1,0:T(8,128)(2,1)S(1)}, u32[]{:S(2)}, u32[]{:S(2)}) collective-permute-start(bf16[2,2,4,16,1024]{4,3,2,1,0:T(8,128)(2,1)} %collective-permute-done.7.refs_4_), channel_id=1, source_target_pairs={{0,16},{16,0},{1,17},{17,1},{2,18},{18,2},{3,19},{19,3},{4,20},{20... | collective-permute-start | bytes 1572872 | tf_op jit(solution)/shard_map/ppermute | solution.py:562
  73.1 16.3 %collective-permute-start.19 = (bf16[2,2,4,16,1024]{4,3,2,1,0:T(8,128)(2,1)}, bf16[2,2,4,16,1024]{4,3,2,1,0:T(8,128)(2,1)S(1)}, u32[]{:S(2)}, u32[]{:S(2)}) collective-permute-start(bf16[2,2,4,16,1024]{4,3,2,1,0:T(8,128)(2,1)} %collective-permute-done.7.refs_4_), channel_id=1, source_target_pairs={{0,1},{1,0},{2,3},{3,2},{4,5},{5,4},{6,7},{7,6},{8,9},{9,8},{10,11... | collective-permute-start | bytes 1572872 | tf_op jit(solution)/shard_map/ppermute | solution.py:562
  87.3 13.4 %copy-start.10 = (s32[128,1,2]{0,2,1:T(2,128)S(1)}, s32[128,1,2]{0,2,1:T(2,128)}, u32[]{:S(2)}) copy-start(s32[128,1,2]{0,2,1:T(2,128)} %param.16) | copy-start | bytes 3076
  87.3 35.9 %copy-start.3 = (bf16[128,1,2048]{2,0,1:T(8,128)(2,1)S(1)}, bf16[128,1,2048]{2,0,1:T(8,128)(2,1)}, u32[]{:S(2)}) copy-start(bf16[128,1,2048]{2,0,1:T(8,128)(2,1)} %param.13) | copy-start | bytes 1572868
  87.4 35.9 %copy-start.5 = (f32[2048]{0:T(1024)S(1)}, f32[2048]{0:T(1024)}, u32[]{:S(2)}) copy-start(f32[2048]{0:T(1024)} %param.15) | copy-start | bytes 24580
  87.4 2.0 collective-permute-start.16
  87.6 2.5 %collective-permute-start.18 = (bf16[2,2,4,16,1024]{4,3,2,1,0:T(8,128)(2,1)S(1)}, bf16[2,2,4,16,1024]{4,3,2,1,0:T(8,128)(2,1)S(1)}, u32[]{:S(2)}, u32[]{:S(2)}) collective-permute-start(bf16[2,2,4,16,1024]{4,3,2,1,0:T(8,128)(2,1)S(1)} %collective-permute-done.10.refs_2_), channel_id=1, source_target_pairs={{0,1},{1,0},{2,3},{3,2},{4,5},{5,4},{6,7},{7,6},{8,9},{9,8},{10,11... | collective-permute-start | bytes 1572872 | tf_op jit(solution)/shard_map/ppermute | solution.py:562
  88.0 2.9 %collective-permute-start.20 = (bf16[2,2,4,16,1024]{4,3,2,1,0:T(8,128)(2,1)S(1)}, bf16[2,2,4,16,1024]{4,3,2,1,0:T(8,128)(2,1)S(1)}, u32[]{:S(2)}, u32[]{:S(2)}) collective-permute-start(bf16[2,2,4,16,1024]{4,3,2,1,0:T(8,128)(2,1)S(1)} %collective-permute-done.15.refs_6_), channel_id=1, source_target_pairs={{0,1},{1,0},{2,3},{3,2},{4,5},{5,4},{6,7},{7,6},{8,9},{9,8},{10,11... | collective-permute-start | bytes 1572872 | tf_op jit(solution)/shard_map/ppermute | solution.py:562
  96.0 15.7 %collective-permute-start.21 = (bf16[128,2048]{1,0:T(8,128)(2,1)}, bf16[128,2048]{1,0:T(8,128)(2,1)S(1)}, u32[]{:S(2)}, u32[]{:S(2)}) collective-permute-start(bf16[128,2048]{1,0:T(8,128)(2,1)} %get-tuple-element.52), channel_id=1, source_target_pairs={{0,6},{1,7},{2,4},{3,5},{4,2},{5,3},{6,0},{7,1},{8,14},{9,15},{10,... | collective-permute-start | bytes 1572872 | tf_op jit(solution)/shard_map/ppermute | solution.py:562
  99.3 24.0 %collective-permute-start.22 = (bf16[128,2048]{1,0:T(8,128)(2,1)}, bf16[128,2048]{1,0:T(8,128)(2,1)S(1)}, u32[]{:S(2)}, u32[]{:S(2)}) collective-permute-start(bf16[128,2048]{1,0:T(8,128)(2,1)} %get-tuple-element.53), channel_id=1, source_target_pairs={{0,4},{1,5},{2,6},{3,7},{4,0},{5,1},{6,2},{7,3},{8,12},{9,13},{10,... | collective-permute-start | bytes 1572872 | tf_op jit(solution)/shard_map/ppermute | solution.py:562
  99.6 23.6 %collective-permute-start.23 = (bf16[128,2048]{1,0:T(8,128)(2,1)}, bf16[128,2048]{1,0:T(8,128)(2,1)S(1)}, u32[]{:S(2)}, u32[]{:S(2)}) collective-permute-start(bf16[128,2048]{1,0:T(8,128)(2,1)} %get-tuple-element.54), channel_id=1, source_target_pairs={{0,2},{1,3},{2,0},{3,1},{4,6},{5,7},{6,4},{7,5},{8,10},{9,11},{10,... | collective-permute-start | bytes 1572872 | tf_op jit(solution)/shard_map/ppermute | solution.py:562
  123.3 1.0 copy-start.4
  125.5 55.6 %copy-start.1 = (f32[128,2048]{1,0:T(8,128)}, f32[128,2048]{1,0:T(8,128)S(1)}, u32[]{:S(2)}) copy-start(f32[128,2048]{1,0:T(8,128)S(1)} %get-tuple-element.56.stream_hbm) | copy-start | bytes 3145732
  125.5 55.6 %copy-start.6 = (bf16[1,512,2048]{2,1,0:T(8,128)(2,1)S(1)}, bf16[1,512,2048]{2,1,0:T(8,128)(2,1)}, u32[]{:S(2)}) copy-start(bf16[1,512,2048]{2,1,0:T(8,128)(2,1)} %param.19) | copy-start | bytes 6291460
  187.9 5.1 %copy-start.11 = (f32[128,1,2]{0,2,1:T(2,128)S(1)}, f32[128,1,2]{0,2,1:T(2,128)}, u32[]{:S(2)}) copy-start(f32[128,1,2]{0,2,1:T(2,128)} %param.17) | copy-start | bytes 3076
  187.9 52.6 %all-to-all-start.2 = ((bf16[16,32,2048]{2,1,0:T(8,128)(2,1)}), bf16[16,32,2048]{2,1,0:T(8,128)(2,1)S(1)}, u32[]{:S(2)}, u32[]{:S(2)}) async-start(bf16[16,32,2048]{2,1,0:T(8,128)(2,1)} %bitcast.53), calls=%async_computation.2 | async-start | bytes 4194304 | tf_op jit(solution)/shard_map/all_to_all | solution.py:756
  240.5 1.2 copy-start.2
